TPU v7x, 32 devices: a whole 2x2x4 slice. The times are simulated.
32 devices in a mesh: dp: 2 (over x), expert: 16 (over z, y, core).
Axes of the slice: x: 2, y: 2, z: 4, core: 2. Of those that a mesh axis runs over, the one named last changes fastest.
Arguments:
- hidden_in: bfloat16 [48, 4096], P('dp'), may hold values from -6 to 6
- norm_gain: float32 [4096], replicated, may hold values from 0.1 to 1.9
- route_ids: int32 [48, 8], P('dp'), may hold values from 0 to 15, all different within a row; in each aligned block of 24 rows (0 to 23, 24 to 47, ...) at most 24 rows name the same one
- route_gates: float32 [48, 8], P('dp'), may hold values from 0.05 to 0.5
- w_gate: bfloat16 [16, 4096, 1536], P('expert', None, 'dp'), may hold values from -0.09375 to 0.09375
- w_up: bfloat16 [16, 4096, 1536], P('expert', None, 'dp'), may hold values from -0.09375 to 0.09375
- w_down: bfloat16 [16, 1536, 4096], P('expert', 'dp'), may hold values from -0.15625 to 0.15625
- context: bfloat16 [48, 2048], P('dp', 'expert'), may hold values from -6 to 6
- w_out: bfloat16 [2048, 4096], P('expert'), may hold values from -0.125 to 0.125
- grad_out: bfloat16 [48, 4096], P('dp'), may hold values from -6 to 6
Outputs:
- output: bfloat16 [48, 4096], P('dp')
- d_hidden: bfloat16 [48, 4096], P('dp')
- d_context: bfloat16 [48, 2048], P('dp', 'expert')
- d_w_out: bfloat16 [2048, 4096], P('expert', 'dp')
Inputs may be any that keep to these rules, and one draw needn't show every extreme that they name: `route_ids`: each token names 8 different experts. Among the 24 tokens of one index of dp no expert is named by more than 24 of them, and in every draw some expert is named by exactly 24.
All inputs are finite; a program needn't handle non-finite values.
Results may differ from a plain program's by a relative error of at most 0.013.
Values may be sent and summed in bfloat16 or wider, within the bound.
No kernel may reach another device: no remote copies, remote signals or barrier semaphores. Data moves between devices by JAX's collectives and lax.ppermute only.
A program may use at most 64 MiB of HBM per device.

v0:
```python
import jax
import jax.numpy as jnp
from jax import lax
from jax.sharding import PartitionSpec as P

EPSILON = 1e-06
EXACT = lax.Precision.HIGHEST


def expert_terms(rows_in, rows_grad, w_gate, w_up, w_down):
    pre_gate = jnp.einsum("cgd,gdf->cgf", rows_in, w_gate, preferred_element_type=jnp.float32)
    pre_up = jnp.einsum("cgd,gdf->cgf", rows_in, w_up, preferred_element_type=jnp.float32)
    sig = jax.nn.sigmoid(pre_gate)
    act = (pre_gate * sig * pre_up).astype(jnp.bfloat16)
    out_term = jnp.einsum("cgf,gfd->cgd", act, w_down, preferred_element_type=jnp.float32)
    back_act = jnp.einsum("cgd,gfd->cgf", rows_grad, w_down, preferred_element_type=jnp.float32)
    grad_gate = (back_act * pre_up * sig * (1.0 + pre_gate * (1.0 - sig))).astype(jnp.bfloat16)
    grad_up = (back_act * pre_gate * sig).astype(jnp.bfloat16)
    back_term = jnp.einsum("cgf,gdf->cgd", grad_gate, w_gate, preferred_element_type=jnp.float32)
    back_term = back_term + jnp.einsum(
        "cgf,gdf->cgd", grad_up, w_up, preferred_element_type=jnp.float32
    )
    return jnp.stack([out_term, back_term], axis=1)


def per_device(
    hidden_in, norm_gain, route_ids, route_gates, w_gate, w_up, w_down, context, w_out, grad_out
):
    tok_rows = hidden_in.shape[0]
    top_count = route_ids.shape[1]
    local_count = w_gate.shape[0]
    experts_all = local_count * lax.axis_size("expert")
    most_rows = min(tok_rows, max(2, 3 * tok_rows * top_count // experts_all))
    hidden32 = hidden_in.astype(jnp.float32)
    scale_inv = lax.rsqrt(jnp.mean(hidden32 * hidden32, axis=1, keepdims=True) + EPSILON)
    unit_rows = hidden32 * scale_inv
    normed = (unit_rows * norm_gain).astype(jnp.bfloat16)
    first_id = lax.axis_index("expert") * local_count
    local_ids = first_id + jnp.arange(local_count, dtype=jnp.int32)
    matches = route_ids[None, :, :] == local_ids[:, None, None]
    chosen = jnp.any(matches, axis=2)
    gate_sel = jnp.sum(jnp.where(matches, route_gates[None, :, :], jnp.float32(0.0)), axis=2)
    rank_rows = jnp.cumsum(chosen.astype(jnp.int32), axis=1) - 1
    places = jnp.where(chosen, rank_rows, -1)
    slot_index = jnp.arange(most_rows, dtype=jnp.int32)
    picker = (places[:, None, :] == slot_index[None, :, None]).astype(jnp.float32)
    picker_half = picker.astype(jnp.bfloat16)
    rows_in = jnp.einsum(
        "gst,td->sgd", picker_half, normed, preferred_element_type=jnp.float32
    ).astype(jnp.bfloat16)
    gate_slot = jnp.einsum("gst,gt->sg", picker, gate_sel, precision=EXACT)
    grad_slot = jnp.einsum("gst,td->sgd", picker_half, grad_out, preferred_element_type=jnp.float32)
    rows_grad = (gate_slot[:, :, None] * grad_slot).astype(jnp.bfloat16)
    all_in, all_grad = (
        lax.all_gather(rows_in, "dp", axis=0, tiled=True),
        lax.all_gather(rows_grad, "dp", axis=0, tiled=True),
    )
    summed = lax.psum_scatter(
        expert_terms(all_in, all_grad, w_gate, w_up, w_down).astype(jnp.bfloat16),
        "dp",
        scatter_dimension=0,
        tiled=True,
    ).astype(jnp.float32)
    weighted = picker * jnp.transpose(gate_slot)[:, :, None]
    moe_part = jnp.einsum("gst,sgd->td", weighted, summed[:, 0], precision=EXACT)
    back_part = jnp.einsum("gst,sgd->td", picker, summed[:, 1], precision=EXACT)
    moe_sum, normed_grad = lax.psum((moe_part, back_part), "expert")
    output = (hidden32 + moe_sum).astype(jnp.bfloat16)
    scaled = normed_grad * norm_gain
    centre = jnp.mean(scaled * unit_rows, axis=1, keepdims=True)
    d_hidden = (grad_out.astype(jnp.float32) + scale_inv * (scaled - unit_rows * centre)).astype(
        jnp.bfloat16
    )
    d_context = lax.dot_general(
        d_hidden, w_out, (((1,), (1,)), ((), ())), preferred_element_type=jnp.float32
    ).astype(jnp.bfloat16)
    grad_term = lax.dot_general(
        context, d_hidden, (((0,), (0,)), ((), ())), preferred_element_type=jnp.float32
    )
    w_grad = lax.psum_scatter(grad_term.astype(jnp.bfloat16), "dp", scatter_dimension=1, tiled=True)
    return (output, d_hidden, d_context, w_grad)


def solution(mesh):
    return jax.shard_map(
        per_device,
        mesh=mesh,
        in_specs=(
            P("dp", None),
            P(),
            P("dp", None),
            P("dp", None),
            P("expert", None, "dp"),
            P("expert", None, "dp"),
            P("expert", "dp", None),
            P("dp", "expert"),
            P("expert", None),
            P("dp", None),
        ),
        out_specs=(P("dp", None), P("dp", None), P("dp", "expert"), P("expert", "dp")),
        check_vma=False,
    )
```

profile of v0, /device:TPU:0, one launch (start us, length us, event | category | flops | bytes accessed | tf_op | source)
XLA Modules:
  0.0 190.4 jit_solution(17105007094588930449)
XLA Ops:
  7.2 0.0 copy-start
  7.2 0.0 reduce-scatter.7.cloned.1.call-start
  7.2 0.8 select_reduce_fusion
  8.1 0.1 copy.18
  8.2 0.1 add_reduce_fusion
  8.3 0.1 convolution_bitcast_fusion.1
  8.4 1.3 fusion.31
  9.7 8.6 %all_gather.7 = bf16[48,1,4096]{2,0,1:T(8,128)(2,1)S(1)} all-gather(bf16[24,1,4096]{2,0,1:T(8,128)(2,1)S(1)} %fusion.31), channel_id=1, replica_groups=mesh['dp'=2,'expert'=16] {'dp'}, dimensions={0}, use_global_device_ids=true | all-gather | bytes 589824 | tf_op jit(solution)/shard_map/all_gather | solution.py:56
  18.4 1.1 fusion.50
  19.4 1.2 fusion.30
  20.6 6.8 %all_gather.6 = bf16[48,1,4096]{2,0,1:T(8,128)(2,1)S(1)} all-gather(bf16[24,1,4096]{2,0,1:T(8,128)(2,1)S(1)} %fusion.30), channel_id=1, replica_groups=mesh['dp'=2,'expert'=16] {'dp'}, dimensions={0}, use_global_device_ids=true | all-gather | bytes 589824 | tf_op jit(solution)/shard_map/all_gather | solution.py:55
  27.4 4.1 %fusion.32 = f32[48,1,768]{2,0,1:T(8,128)S(1)} fusion(bf16[1,4096,768]{2,1,0:T(8,128)(2,1)} %param.14, bf16[48,1,4096]{2,0,1:T(8,128)(2,1)S(1)} %all_gather.6), kind=kOutput, calls=%fused_computation.25 | convolution fusion | flops 301989888 | bytes 6832128 | tf_op jit(solution)/shard_map/cgd,gdf->cgf/dot_general | solution.py:11
  31.5 0.0 copy-done.1
  31.5 1.1 fusion.35
  32.6 0.0 copy-done.2
  32.7 0.0 slice-start
  32.7 2.0 %fusion.38 = f32[48,1,768]{2,0,1:T(8,128)S(1)} fusion(bf16[1,768,4096]{2,1,0:T(8,128)(2,1)S(1)} %copy-done.2, bf16[48,1,4096]{2,0,1:T(8,128)(2,1)S(1)} %all_gather.7), kind=kOutput, calls=%fused_computation.27 | convolution fusion | flops 301989888 | bytes 6832128 | tf_op jit(solution)/shard_map/cgd,gfd->cgf/dot_general | solution.py:16
  34.7 0.0 slice-start.1
  34.7 1.9 %fusion.4 = f32[48,4096]{1,0:T(8,128)S(1)} fusion(bf16[1,4096,768]{2,1,0:T(8,128)(2,1)S(1)} %copy-done.1, f32[48,1,768]{2,0,1:T(8,128)S(1)} %fusion.38, f32[48,1,768]{2,0,1:T(8,128)S(1)} %fusion.32), kind=kOutput, calls=%fused_computation.4 | convolution fusion | flops 302211072 | bytes 7372800 | tf_op jit(solution)/shard_map/cgf,gdf->cgd/dot_general | solution.py:20
  36.6 1.2 fusion.22
  37.8 0.0 slice-done
  37.8 1.9 %fusion.25 = bf16[48,1,1,4096]{3,0,2,1:T(8,128)(2,1)S(1)} fusion(f32[48,4096]{1,0:T(8,128)S(1)} %fusion.4, bf16[1,4096,768]{2,1,0:T(8,128)(2,1)S(1)} %bitcast.126, f32[48,1,768]{2,0,1:T(8,128)S(1)} %fusion.32, f32[48,1,768]{2,0,1:T(8,128)S(1)} %fusion.38, f32[48,1,768]{2,0,1:T(8,128)S(1)} %fusion.35), kind=kOutput, calls=%fused_computation.18 | convolution fusion | flops 302751744 | bytes 7913472 | tf_op jit(solution)/shard_map/cgf,gdf->cgd/dot_general | solution.py:19
  39.8 0.0 copy-start.3
  39.8 0.0 copy-start.6
  39.8 0.0 copy-start.5
  39.8 0.0 copy-start.7
  39.8 0.1 maximum_bitcast_fusion
  39.9 0.9 copy.25
  40.8 0.0 reduce-scatter.7.cloned.1.call-update
  40.9 0.0 all-reduce.3.cloned.1.call-start
  40.9 0.1 compare_select_fusion
  41.0 18.6 %reduce-scatter.7.cloned.1.call-done = bf16[24,8192]{1,0:T(8,128)(2,1)} async-done(((bf16[48,8192]{1,0:T(8,128)(2,1)}), bf16[24,8192]{1,0:T(8,128)(2,1)}) %reduce-scatter.7.cloned.1.call-update) | async-done | bytes 393232
  59.7 2.2 %reshape.311 = bf16[24,2,1,4096]{3,2,1,0:T(2,128)(2,1)S(1)} reshape(bf16[24,8192]{1,0:T(8,128)(2,1)} %reduce-scatter.7.cloned.1.call-done) | data formatting | bytes 786432
  61.9 0.9 fusion.71
  62.8 1.1 fusion.56
  63.9 1.3 fusion.57
  65.2 0.0 all-reduce.3.cloned.1.call-update
  65.2 0.0 reduce-scatter.5.cloned.1.call-start
  65.3 92.4 %all-reduce.3.cloned.1.call-done = (f32[24,4096]{1,0:T(8,128)}, f32[24,4096]{1,0:T(8,128)}) async-done(((f32[24,4096]{1,0:T(8,128)}, f32[24,4096]{1,0:T(8,128)}), (f32[24,4096]{1,0:T(8,128)}, f32[24,4096]{1,0:T(8,128)})) %all-reduce.3.cloned.1.call-update) | async-done | bytes 786448 | tf_op jit(solution)/shard_map/psum | solution.py:67
  157.7 0.0 copy-done.6
  157.7 1.2 fusion.45
  158.9 0.0 copy-done.5
  158.9 2.0 %fusion.49 = (bf16[24,4096]{1,0:T(8,128)(2,1)S(1)}, bf16[24,4096]{1,0:T(8,128)(2,1)}) fusion(bf16[24,4096]{1,0:T(8,128)(2,1)S(1)} %copy-done.3, bf16[24,4096]{1,0:T(8,128)(2,1)S(1)} %copy-done.5, f32[24,4096]{1,0:T(8,128)} %get-tuple-element.17, f32[24]{0:T(128)S(1)} %broadcast_multiply_fusion, f32[4096]{0:T(1024)S(1)} %copy-done.6, ...), kind=kLoop, calls=%fused_computation.42 | loop fusion | flops 1081344 | bytes 1589440 | tf_op jit(solution)/shard_map/convert_element_type | solution.py:71
  160.9 1.5 fusion.12
  162.3 0.0 reduce-scatter.5.cloned.1.call-update
  162.4 1.0 convolution_convert_fusion.2
  163.4 18.4 %reduce-scatter.5.cloned.1.call-done = bf16[128,2048]{0,1:T(8,128)(2,1)} async-done(((bf16[128,4096]{0,1:T(8,128)(2,1)}), bf16[128,2048]{0,1:T(8,128)(2,1)}) %reduce-scatter.5.cloned.1.call-update) | async-done | bytes 524304 | tf_op jit(solution)/shard_map/reduce_scatter | solution.py:80
  181.8 2.0 %copy.19 = bf16[128,2048]{1,0:T(8,128)(2,1)} copy(bf16[128,2048]{0,1:T(8,128)(2,1)} %reduce-scatter.5.cloned.1.call-done) | data formatting | bytes 1048576
  (15 shorter events, 0.1 us)
Async XLA Ops:
  7.2 155.2 %copy-start = (bf16[128,4096]{1,0:T(8,128)(2,1)S(1)}, bf16[128,4096]{1,0:T(8,128)(2,1)}, u32[]{:S(2)}) copy-start(bf16[128,4096]{1,0:T(8,128)(2,1)} %param.18) | copy-start | bytes 3145732
  7.2 52.5 %reduce-scatter.7.cloned.1.call-start = ((), (), s32[]{:S(2)}) async-start(), calls=%async_computation.3 | async-start | bytes 1179648
  8.2 23.3 %copy-start.1 = (bf16[1,4096,768]{2,1,0:T(8,128)(2,1)S(1)}, bf16[1,4096,768]{2,1,0:T(8,128)(2,1)}, u32[]{:S(2)}) copy-start(bf16[1,4096,768]{2,1,0:T(8,128)(2,1)} %param.15) | copy-start | bytes 18874372
  27.4 5.2 %copy-start.2 = (bf16[1,768,4096]{2,1,0:T(8,128)(2,1)S(1)}, bf16[1,768,4096]{2,1,0:T(8,128)(2,1)}, u32[]{:S(2)}) copy-start(bf16[1,768,4096]{2,1,0:T(8,128)(2,1)} %param.16) | copy-start | bytes 18874372
  32.7 5.1 %slice-start = ((s8[6291456]{0:T(1024)(128)(4,1)}), s8[4194304]{0:T(1024)(128)(4,1)S(1)}, s32[]{:S(2)}) async-start(s8[6291456]{0:T(1024)(128)(4,1)} %bitcast.125), calls=%async_computation.5 | async-start | bytes 8388608
  34.7 3.1 %slice-start.1 = ((s8[6291456]{0:T(1024)(128)(4,1)}), s8[2097152]{0:T(1024)(128)(4,1)S(1)}, s32[]{:S(2)}) async-start(s8[6291456]{0:T(1024)(128)(4,1)} %bitcast.125), calls=%async_computation.6 | async-start | bytes 4194304
  39.8 117.9 %copy-start.3 = (bf16[24,4096]{1,0:T(8,128)(2,1)S(1)}, bf16[24,4096]{1,0:T(8,128)(2,1)}, u32[]{:S(2)}) copy-start(bf16[24,4096]{1,0:T(8,128)(2,1)} %param.10) | copy-start | bytes 589828
  39.8 117.9 %copy-start.6 = (f32[4096]{0:T(1024)S(1)}, f32[4096]{0:T(1024)}, u32[]{:S(2)}) copy-start(f32[4096]{0:T(1024)} %param.11) | copy-start | bytes 49156
  39.8 119.1 %copy-start.5 = (bf16[24,4096]{1,0:T(8,128)(2,1)S(1)}, bf16[24,4096]{1,0:T(8,128)(2,1)}, u32[]{:S(2)}) copy-start(bf16[24,4096]{1,0:T(8,128)(2,1)} %param.19) | copy-start | bytes 589828
  39.8 121.0 %copy-start.7 = (bf16[24,128]{1,0:T(8,128)(2,1)S(1)}, bf16[24,128]{1,0:T(8,128)(2,1)}, u32[]{:S(2)}) copy-start(bf16[24,128]{1,0:T(8,128)(2,1)} %param.17) | copy-start | bytes 18436
  40.9 116.8 %all-reduce.3.cloned.1.call-start = ((), (), s32[]{:S(2)}) async-start(), calls=%async_computation.4 | async-start | bytes 1572864 | tf_op jit(solution)/shard_map/psum | solution.py:67
  65.2 116.6 %reduce-scatter.5.cloned.1.call-start = ((), (), s32[]{:S(2)}) async-start(), calls=%async_computation.2 | async-start | bytes 1572864 | tf_op jit(solution)/shard_map/reduce_scatter | solution.py:80
  160.9 23.0 %copy-start.4 = (bf16[24,4096]{1,0:T(8,128)(2,1)}, bf16[24,4096]{1,0:T(8,128)(2,1)S(1)}, u32[]{:S(2)}) copy-start(bf16[24,4096]{1,0:T(8,128)(2,1)S(1)} %get-tuple-element.22) | copy-start | bytes 589828
Sparse Core Ops, SparseCore 0:
  41.0 18.6 reduce-scatter.6
  65.4 92.2 all-reduce.2
  162.5 19.2 reduce-scatter.4
where the time goes:
time: 191 us; the launch traced here: 190 us
  waiting for transfers between devices  129 us (68%)
  matrix products  19.7 us (10%)
  blocking collectives  15.4 us (8%)
  between operations  14 us (7%)
  local copies, waits for them, and re-layouts  6.29 us (3%)
  other arithmetic  5.43 us (3%)
    psum x1, waiting for transfers between devices, per_device(): moe_sum, normed_grad = lax.psum((moe_part, back_part), 'expert')  92.4 us
    unnamed x4, waiting for transfers between devices  18.7 us
    reduce_scatter x1, waiting for transfers between devices, per_device(): lax.psum_scatter(grad_term.astype(jnp.bfloat16), 'dp', scatter_dimension=...  18.4 us
    all_gather x1, blocking collectives, per_device(): lax.all_gather(rows_grad, 'dp', axis=0, tiled=True)  8.63 us
    all_gather x1, blocking collectives, per_device(): lax.all_gather(rows_in, 'dp', axis=0, tiled=True)  6.76 us
    unnamed x23, local copies, waits for them, and re-layouts  5.3 us
    dot_general x1, matrix products, expert_terms(): jnp.einsum('cgd,gdf->cgf', rows_in, w_gate, preferred_element_type=jnp.fl...  4.07 us
  transfers between devices with their start and end apart: 3, of which 3 were waited for; matrix products, arithmetic and copies ran while one was open for 1% of the time, Pallas kernels for 0%

commit v1 on v0

v1 whole, which is shorter than its diff:
```python
import jax
import jax.numpy as jnp
from jax import lax
from jax.sharding import PartitionSpec as P

EPSILON = 1e-06
F32 = jnp.float32
BF16 = jnp.bfloat16


def from_ahead(value, step, count):
    return lax.ppermute(value, "dp", [((i + step) % count, i) for i in range(count)])


def blocks_of(value, count):
    return jnp.stack([value] + [from_ahead(value, k, count) for k in range(1, count)])


def reduce_all(part, n_dp, n_e):
    rows, width = part.shape[0] // n_dp, part.shape[1] // n_e
    shares = part.reshape(n_dp, rows, n_e, width).transpose(0, 2, 1, 3).reshape(n_dp * n_e, rows, width)
    arrived = lax.all_to_all(shares, ("dp", "expert"), 0, 0, tiled=True)
    total = jnp.sum(arrived.astype(F32), axis=0).astype(BF16)
    spread = lax.all_gather(total, "expert", axis=0, tiled=False)
    return spread.transpose(1, 0, 2).reshape(rows, part.shape[1])


def per_device(
    hidden_in, norm_gain, route_ids, route_gates, w_gate, w_up, w_down, context, w_out, grad_out
):
    n_dp, n_e = lax.axis_size("dp"), lax.axis_size("expert")
    me = lax.axis_index("dp")
    rows, width = hidden_in.shape
    expert = lax.axis_index("expert")
    gate_own = jnp.sum(jnp.where(route_ids == expert, route_gates, 0.0), axis=1, keepdims=True)
    order = lambda blocks: jnp.roll(blocks, me, axis=0).reshape((n_dp * rows,) + blocks.shape[2:])
    hidden = order(blocks_of(hidden_in, n_dp)).astype(F32)
    grads = order(blocks_of(grad_out, n_dp)).astype(F32)
    gates = order(blocks_of(gate_own, n_dp))
    contexts = blocks_of(context, n_dp).reshape(n_dp * rows, -1)

    scale_inv = lax.rsqrt(jnp.mean(hidden * hidden, axis=1, keepdims=True) + EPSILON)
    normed = (hidden * scale_inv * norm_gain).astype(BF16)
    rows_grad = (gates * grads).astype(BF16)
    dot = lambda a, b, dims: lax.dot_general(a, b, (dims, ((), ())), preferred_element_type=F32)
    wg, wu, wd = w_gate[0], w_up[0], w_down[0]
    pre_gate = dot(normed, wg, ((1,), (0,)))
    pre_up = dot(normed, wu, ((1,), (0,)))
    back_act = dot(rows_grad, wd, ((1,), (1,)))
    sig = jax.nn.sigmoid(pre_gate)
    grad_gate = (back_act * pre_up * sig * (1.0 + pre_gate * (1.0 - sig))).astype(BF16)
    grad_up = (back_act * pre_gate * sig).astype(BF16)
    in_part = dot(grad_gate, wg, ((1,), (1,))) + dot(grad_up, wu, ((1,), (1,)))
    normed_grad = reduce_all(in_part.astype(BF16), n_dp, n_e).astype(F32)
    act = (pre_gate * sig * pre_up).astype(BF16)
    out_part = gates * dot(act, wd, ((1,), (0,)))
    moe_sum = reduce_all(out_part.astype(BF16), n_dp, n_e).astype(F32)

    own = hidden_in.astype(F32)
    own_scale = lax.rsqrt(jnp.mean(own * own, axis=1, keepdims=True) + EPSILON)
    unit_rows = own * own_scale
    output = (own + moe_sum).astype(BF16)
    scaled = normed_grad * norm_gain
    centre = jnp.mean(scaled * unit_rows, axis=1, keepdims=True)
    d_hidden = (grad_out.astype(F32) + own_scale * (scaled - unit_rows * centre)).astype(BF16)
    d_context = dot(d_hidden, w_out, ((1,), (1,))).astype(BF16)
    part = width // n_dp
    columns = lambda k: lax.dynamic_slice_in_dim(d_hidden, ((me + k) % n_dp) * part, part, 1)
    pieces = [columns(0)]
    for k in range(1, n_dp):
        pieces.append(from_ahead(columns(n_dp - k), k, n_dp))
    d_w_out = dot(contexts, jnp.concatenate(pieces, axis=0), ((0,), (0,))).astype(BF16)
    return (output, d_hidden, d_context, d_w_out)


def solution(mesh):
    return jax.shard_map(
        per_device,
        mesh=mesh,
        in_specs=(
            P("dp", None),
            P(),
            P("dp", None),
            P("dp", None),
            P("expert", None, "dp"),
            P("expert", None, "dp"),
            P("expert", "dp", None),
            P("dp", "expert"),
            P("expert", None),
            P("dp", None),
        ),
        out_specs=(P("dp", None), P("dp", None), P("dp", "expert"), P("expert", "dp")),
        check_vma=False,
    )
```

time: 191 us -> 102 us (0.53)
  waiting for transfers between devices: 129 us -> 17.1 us
  blocking collectives: 15.4 us -> 42.4 us
  starting transfers between devices: 0.12 us -> 15.3 us
  between operations: 14 us -> 0.91 us
  local copies, waits for them, and re-layouts: 6.29 us -> 2.63 us
  matrix products: 19.7 us -> 17.2 us
    psum x1 -> x0, waiting for transfers between devices: 92.4 us -> none  [per_device(): moe_sum, normed_grad = lax.psum((moe_part, back_part), 'expert')]
    all_gather x2, blocking collectives: 15.4 us -> 42.4 us  [reduce_all(): spread = lax.all_gather(total, 'expert', axis=0, tiled=False)]
    unnamed x4 -> x0, waiting for transfers between devices: 18.7 us -> none
    reduce_scatter x1 -> x0, waiting for transfers between devices: 18.4 us -> none  [per_device(): lax.psum_scatter(grad_term.astype(jnp.bfloat16), 'dp', scatter_dimension=...]
    ppermute x0 -> x5, waiting for transfers between devices: none -> 9.22 us  [from_ahead(): lax.ppermute(value, 'dp', [((i + step) % count, i) for i in range(count)])]
    all_to_all x0 -> x2, starting transfers between devices: none -> 8.69 us  [reduce_all(): arrived = lax.all_to_all(shares, ('dp', 'expert'), 0, 0, tiled=True)]
    all_to_all x0 -> x2, waiting for transfers between devices: none -> 7.87 us  [reduce_all(): arrived = lax.all_to_all(shares, ('dp', 'expert'), 0, 0, tiled=True)]
    ppermute x0 -> x5, starting transfers between devices: none -> 6.65 us  [from_ahead(): lax.ppermute(value, 'dp', [((i + step) % count, i) for i in range(count)])]
  transfers between devices with their start and end apart: 3 -> 7, of which waited for: 3 -> 3; matrix products, arithmetic and copies ran while one was open for 1% -> 23% of each run, Pallas kernels for 0% -> 0%
where the time goes in v1:
time: 102 us; the launch traced here: 101 us
  blocking collectives  42.4 us (42%)
  matrix products  17.2 us (17%)
  waiting for transfers between devices  17.1 us (17%)
  starting transfers between devices  15.3 us (15%)
  other arithmetic  5.69 us (6%)
  local copies, waits for them, and re-layouts  2.63 us (3%)
    all_gather x2, blocking collectives, reduce_all(): spread = lax.all_gather(total, 'expert', axis=0, tiled=False)  42.4 us
    dot_general x8, matrix products, per_device(): lax.dot_general(a, b, (dims, ((), ())), preferred_element_type=F32)  17.2 us
    ppermute x5, waiting for transfers between devices, from_ahead(): lax.ppermute(value, 'dp', [((i + step) % count, i) for i in range(count)])  9.22 us
    all_to_all x2, starting transfers between devices, reduce_all(): arrived = lax.all_to_all(shares, ('dp', 'expert'), 0, 0, tiled=True)  8.69 us
    all_to_all x2, waiting for transfers between devices, reduce_all(): arrived = lax.all_to_all(shares, ('dp', 'expert'), 0, 0, tiled=True)  7.87 us
    ppermute x5, starting transfers between devices, from_ahead(): lax.ppermute(value, 'dp', [((i + step) % count, i) for i in range(count)])  6.65 us
  transfers between devices with their start and end apart: 7, of which 3 were waited for; matrix products, arithmetic and copies ran while one was open for 23% of the time, Pallas kernels for 0%

profile of v1, /device:TPU:0, one launch (start us, length us, event | category | flops | bytes accessed | tf_op | source)
XLA Modules:
  0.0 101.2 jit_solution(1581101945019791968)
XLA Ops:
  0.6 0.0 copy-start
  0.6 3.0 %collective-permute-start.1 = (bf16[24,4096]{1,0:T(8,128)(2,1)}, bf16[24,4096]{1,0:T(8,128)(2,1)S(1)}, u32[]{:S(2)}, u32[]{:S(2)}) collective-permute-start(bf16[24,4096]{1,0:T(8,128)(2,1)} %param.12), channel_id=1, source_target_pairs={{16,0},{0,16},{17,1},{1,17},{18,2},{2,18},{19,3},{3,19},{20,4},{4,... | collective-permute-start | bytes 589832 | tf_op jit(solution)/shard_map/ppermute | solution.py:12
  3.7 0.1 collective-permute-start.2
  3.7 0.7 select_reduce_fusion
  4.5 2.0 %collective-permute-start = (f32[24,1]{0,1:T(1,128)S(1)}, f32[24,1]{0,1:T(1,128)S(1)}, u32[]{:S(2)}, u32[]{:S(2)}) collective-permute-start(f32[24,1]{0,1:T(1,128)S(1)} %bitcast.89), channel_id=1, source_target_pairs={{16,0},{0,16},{17,1},{1,17},{18,2},{2,18},{19,3},{3,19},{20,4},{4,... | collective-permute-start | bytes 296 | tf_op jit(solution)/shard_map/ppermute | solution.py:12
  6.5 0.1 collective-permute-start.3
  6.5 6.6 %collective-permute-done = f32[24,1]{0,1:T(1,128)S(1)} collective-permute-done((f32[24,1]{0,1:T(1,128)S(1)}, f32[24,1]{0,1:T(1,128)S(1)}, u32[]{:S(2)}, u32[]{:S(2)}) %collective-permute-start) | collective-permute-done | bytes 128 | tf_op jit(solution)/shard_map/ppermute | solution.py:12
  13.1 0.5 broadcast.77
  13.6 0.8 fusion.56
  14.5 0.0 collective-permute-done.1
  14.5 0.0 collective-permute-done.2
  14.5 1.8 %fusion.24 = (f32[2,24]{1,0:T(2,128)S(1)}, bf16[2,24,4096]{2,1,0:T(8,128)(2,1)S(1)}, bf16[2,24,4096]{2,1,0:T(8,128)(2,1)S(1)}) fusion(s32[]{:T(128)S(6)} %select_n.40, bf16[1,24,4096]{2,1,0:T(8,128)(2,1)S(1)} %bitcast.83, bf16[1,24,4096]{2,1,0:T(8,128)(2,1)} %bitcast.73, bf16[1,24,4096]{2,1,0:T(8,128)(2,1)S(1)} %bitcast.84, ...), kind=kLoop, calls=%fused_computation.20 | loop fusion | flops 2359248 | bytes 1573252 | tf_op jit(solution)/shard_map/reduce_sum | solution.py:42
  16.3 0.9 fusion.26
  17.1 0.0 copy-start.2
  17.2 4.1 %fusion.10 = f32[48,768]{1,0:T(8,128)S(1)} fusion(bf16[48,4096]{1,0:T(8,128)(2,1)S(1)} %bitcast.71, bf16[1,4096,768]{2,1,0:T(8,128)(2,1)} %param.16), kind=kOutput, calls=%fused_computation.10 | convolution fusion | flops 301989888 | bytes 6832128 | tf_op jit(solution)/shard_map/dot_general | solution.py:45
  21.2 0.0 copy-done.1
  21.3 0.0 slice-start
  21.3 1.1 %fusion.6 = f32[48,768]{1,0:T(8,128)S(1)} fusion(bf16[48,4096]{1,0:T(8,128)(2,1)S(1)} %bitcast.72, bf16[1,4096,768]{2,1,0:T(8,128)(2,1)S(1)} %copy-done.1), kind=kOutput, calls=%fused_computation.6 | convolution fusion | flops 301989888 | bytes 6832128 | tf_op jit(solution)/shard_map/dot_general | solution.py:45
  22.4 0.0 copy-done.2
  22.4 0.0 slice-start.1
  22.4 2.0 %fusion = f32[48,768]{1,0:T(8,128)S(1)} fusion(bf16[48,4096]{1,0:T(8,128)(2,1)S(1)} %bitcast.79, bf16[1,768,4096]{2,1,0:T(8,128)(2,1)S(1)} %copy-done.2), kind=kOutput, calls=%fused_computation | convolution fusion | flops 301989888 | bytes 6832128 | tf_op jit(solution)/shard_map/dot_general | solution.py:45
  24.5 1.9 %fusion.4 = f32[48,4096]{1,0:T(8,128)S(1)} fusion(bf16[1,4096,768]{2,1,0:T(8,128)(2,1)S(1)} %copy-done.1, f32[48,768]{1,0:T(8,128)S(1)} %fusion, f32[48,768]{1,0:T(8,128)S(1)} %fusion.10), kind=kOutput, calls=%fused_computation.4 | convolution fusion | flops 302211072 | bytes 7372800 | tf_op jit(solution)/shard_map/dot_general | solution.py:45
  26.4 0.0 slice-done
  26.4 0.0 copy-start.3
  26.4 1.9 %fusion.21 = bf16[48,4096]{1,0:T(8,128)(2,1)S(1)} fusion(f32[48,4096]{1,0:T(8,128)S(1)} %fusion.4, bf16[1,4096,768]{2,1,0:T(8,128)(2,1)S(1)} %bitcast.68, f32[48,768]{1,0:T(8,128)S(1)} %fusion.10, f32[48,768]{1,0:T(8,128)S(1)} %fusion, f32[48,768]{1,0:T(8,128)S(1)} %fusion.6), kind=kOutput, calls=%fused_computation.15 | convolution fusion | flops 302751744 | bytes 7913472 | tf_op jit(solution)/shard_map/dot_general | solution.py:45
  28.4 0.0 copy-start.7
  28.4 0.1 copy.23
  28.5 0.9 copy.18
  29.3 6.1 %all-to-all-start.1 = ((bf16[32,24,256]{2,1,0:T(8,128)(2,1)}), bf16[32,24,256]{2,1,0:T(8,128)(2,1)S(1)}, u32[]{:S(2)}, u32[]{:S(2)}) async-start(bf16[32,24,256]{2,1,0:T(8,128)(2,1)} %bitcast.18), calls=%async_computation.1 | async-start | bytes 786432 | tf_op jit(solution)/shard_map/all_to_all | solution.py:22
  35.4 0.2 fusion.35
  35.6 0.1 mul.111
  35.7 4.0 %fusion.18 = bf16[48,4096]{1,0:T(8,128)(2,1)S(1)} fusion(bf16[1,768,4096]{2,1,0:T(8,128)(2,1)} %param.18, f32[48]{0:T(128)S(1)} %mul.111, f32[48,768]{1,0:T(8,128)S(1)} %fusion.6, f32[48,768]{1,0:T(8,128)S(1)} %fusion.10), kind=kOutput, calls=%fused_computation.14 | convolution fusion | flops 302604288 | bytes 6979776 | tf_op jit(solution)/shard_map/dot_general | solution.py:45
  39.7 0.1 copy.22
  39.8 0.9 copy.16
  40.7 7.9 %all-to-all-done.1 = bf16[32,24,256]{2,1,0:T(8,128)(2,1)S(1)} async-done(((bf16[32,24,256]{2,1,0:T(8,128)(2,1)}), bf16[32,24,256]{2,1,0:T(8,128)(2,1)S(1)}, u32[]{:S(2)}, u32[]{:S(2)}) %all-to-all-start.1) | async-done | bytes 393248 | tf_op jit(solution)/shard_map/all_to_all | solution.py:22
  48.5 2.6 %all-to-all-start = ((bf16[32,24,256]{2,1,0:T(8,128)(2,1)}), bf16[32,24,256]{2,1,0:T(8,128)(2,1)S(1)}, u32[]{:S(2)}, u32[]{:S(2)}) async-start(bf16[32,24,256]{2,1,0:T(8,128)(2,1)} %bitcast.10), calls=%async_computation | async-start | bytes 786432 | tf_op jit(solution)/shard_map/all_to_all | solution.py:22
  51.1 0.0 collective-permute-done.3
  51.2 0.1 reduce_sum.64
  51.2 22.8 %all-gather.1 = bf16[384,256]{1,0:T(8,128)(2,1)S(1)} all-gather(bf16[24,256]{1,0:T(8,128)(2,1)S(1)} %reduce_sum.64), channel_id=3, replica_groups=mesh['dp'=2,'expert'=16] {'expert'}, dimensions={0}, use_global_device_ids=true | all-gather | bytes 208896 | tf_op jit(solution)/shard_map/all_gather | solution.py:24
  74.2 0.2 fusion.29
  74.4 0.0 all-to-all-done
  74.4 0.1 reduce_sum.62
  74.5 19.6 %all-gather = bf16[384,256]{1,0:T(8,128)(2,1)S(1)} all-gather(bf16[24,256]{1,0:T(8,128)(2,1)S(1)} %reduce_sum.62), channel_id=2, replica_groups=mesh['dp'=2,'expert'=16] {'expert'}, dimensions={0}, use_global_device_ids=true | all-gather | bytes 208896 | tf_op jit(solution)/shard_map/all_gather | solution.py:24
  94.1 0.8 fusion.33
  95.0 1.5 %collective-permute-start.4 = (bf16[24,2048]{1,0:T(8,128)(2,1)S(1)}, bf16[24,2048]{1,0:T(8,128)(2,1)S(1)}, u32[]{:S(2)}, u32[]{:S(2)}) collective-permute-start(bf16[24,2048]{1,0:T(8,128)(2,1)S(1)} %get-tuple-element.10), channel_id=1, source_target_pairs={{16,0},{0,16},{17,1},{1,17},{18,2},{2,18},{19,3},{3,19},{20,4},{4,... | collective-permute-start | bytes 294920 | tf_op jit(solution)/shard_map/ppermute | solution.py:12
  96.5 1.0 convolution_convert_fusion.1
  97.5 2.6 %collective-permute-done.4 = bf16[24,2048]{1,0:T(8,128)(2,1)S(1)} collective-permute-done((bf16[24,2048]{1,0:T(8,128)(2,1)S(1)}, bf16[24,2048]{1,0:T(8,128)(2,1)S(1)}, u32[]{:S(2)}, u32[]{:S(2)}) %collective-permute-start.4) | collective-permute-done | bytes 98336 | tf_op jit(solution)/shard_map/ppermute | solution.py:12
  100.1 1.1 %convolution_convert_fusion = bf16[128,2048]{1,0:T(8,128)(2,1)} fusion(bf16[48,128]{1,0:T(8,128)(2,1)S(1)} %bitcast.85, bf16[24,2048]{1,0:T(8,128)(2,1)S(1)} %collective-permute-done.4, bf16[24,2048]{1,0:T(8,128)(2,1)S(1)} %get-tuple-element.9), kind=kOutput, calls=%fused_computation.16 | convolution fusion | flops 25821184 | bytes 733184 | tf_op jit(solution)/shard_map/dot_general | solution.py:45
  (21 shorter events, 0.2 us)
Async XLA Ops:
  0.6 95.9 %copy-start = (bf16[128,4096]{1,0:T(8,128)(2,1)S(1)}, bf16[128,4096]{1,0:T(8,128)(2,1)}, u32[]{:S(2)}) copy-start(bf16[128,4096]{1,0:T(8,128)(2,1)} %param.20) | copy-start | bytes 3145732
  0.6 13.8 %collective-permute-start.1 = (bf16[24,4096]{1,0:T(8,128)(2,1)}, bf16[24,4096]{1,0:T(8,128)(2,1)S(1)}, u32[]{:S(2)}, u32[]{:S(2)}) collective-permute-start(bf16[24,4096]{1,0:T(8,128)(2,1)} %param.12), channel_id=1, source_target_pairs={{16,0},{0,16},{17,1},{1,17},{18,2},{2,18},{19,3},{3,19},{20,4},{4,... | collective-permute-start | bytes 589832 | tf_op jit(solution)/shard_map/ppermute | solution.py:12
  3.7 10.8 %collective-permute-start.2 = (bf16[24,4096]{1,0:T(8,128)(2,1)}, bf16[24,4096]{1,0:T(8,128)(2,1)S(1)}, u32[]{:S(2)}, u32[]{:S(2)}) collective-permute-start(bf16[24,4096]{1,0:T(8,128)(2,1)} %param.21), channel_id=1, source_target_pairs={{16,0},{0,16},{17,1},{1,17},{18,2},{2,18},{19,3},{3,19},{20,4},{4,... | collective-permute-start | bytes 589832 | tf_op jit(solution)/shard_map/ppermute | solution.py:12
  4.5 8.7 %collective-permute-start = (f32[24,1]{0,1:T(1,128)S(1)}, f32[24,1]{0,1:T(1,128)S(1)}, u32[]{:S(2)}, u32[]{:S(2)}) collective-permute-start(f32[24,1]{0,1:T(1,128)S(1)} %bitcast.89), channel_id=1, source_target_pairs={{16,0},{0,16},{17,1},{1,17},{18,2},{2,18},{19,3},{3,19},{20,4},{4,... | collective-permute-start | bytes 296 | tf_op jit(solution)/shard_map/ppermute | solution.py:12
  6.5 44.7 %collective-permute-start.3 = (bf16[24,128]{1,0:T(8,128)(2,1)}, bf16[24,128]{1,0:T(8,128)(2,1)S(1)}, u32[]{:S(2)}, u32[]{:S(2)}) collective-permute-start(bf16[24,128]{1,0:T(8,128)(2,1)} %param.19), channel_id=1, source_target_pairs={{16,0},{0,16},{17,1},{1,17},{18,2},{2,18},{19,3},{3,19},{20,4},{4,... | collective-permute-start | bytes 18440 | tf_op jit(solution)/shard_map/ppermute | solution.py:12
  13.6 7.6 %copy-start.1 = (bf16[1,4096,768]{2,1,0:T(8,128)(2,1)S(1)}, bf16[1,4096,768]{2,1,0:T(8,128)(2,1)}, u32[]{:S(2)}) copy-start(bf16[1,4096,768]{2,1,0:T(8,128)(2,1)} %param.17) | copy-start | bytes 18874372
  17.1 5.3 %copy-start.2 = (bf16[1,768,4096]{2,1,0:T(8,128)(2,1)S(1)}, bf16[1,768,4096]{2,1,0:T(8,128)(2,1)}, u32[]{:S(2)}) copy-start(bf16[1,768,4096]{2,1,0:T(8,128)(2,1)} %param.18) | copy-start | bytes 18874372
  21.3 5.1 %slice-start = ((s8[6291456]{0:T(1024)(128)(4,1)}), s8[4194304]{0:T(1024)(128)(4,1)S(1)}, s32[]{:S(2)}) async-start(s8[6291456]{0:T(1024)(128)(4,1)} %bitcast.67), calls=%async_computation.2 | async-start | bytes 8388608
  22.4 4.0 %slice-start.1 = ((s8[6291456]{0:T(1024)(128)(4,1)}), s8[2097152]{0:T(1024)(128)(4,1)S(1)}, s32[]{:S(2)}) async-start(s8[6291456]{0:T(1024)(128)(4,1)} %bitcast.67), calls=%async_computation.3 | async-start | bytes 4194304
  26.4 9.0 %copy-start.3 = (bf16[24,4096]{1,0:T(8,128)(2,1)S(1)}, bf16[24,4096]{1,0:T(8,128)(2,1)}, u32[]{:S(2)}) copy-start(bf16[24,4096]{1,0:T(8,128)(2,1)} %param.12) | copy-start | bytes 589828
  28.4 22.8 %copy-start.7 = (bf16[24,128]{1,0:T(8,128)(2,1)S(1)}, bf16[24,128]{1,0:T(8,128)(2,1)}, u32[]{:S(2)}) copy-start(bf16[24,128]{1,0:T(8,128)(2,1)} %param.19) | copy-start | bytes 18436
  29.3 44.8 %copy-start.6 = (f32[4096]{0:T(1024)S(1)}, f32[4096]{0:T(1024)}, u32[]{:S(2)}) copy-start(f32[4096]{0:T(1024)} %param.13) | copy-start | bytes 49156
  29.3 19.2 %all-to-all-start.1 = ((bf16[32,24,256]{2,1,0:T(8,128)(2,1)}), bf16[32,24,256]{2,1,0:T(8,128)(2,1)S(1)}, u32[]{:S(2)}, u32[]{:S(2)}) async-start(bf16[32,24,256]{2,1,0:T(8,128)(2,1)} %bitcast.18), calls=%async_computation.1 | async-start | bytes 786432 | tf_op jit(solution)/shard_map/all_to_all | solution.py:22
  35.7 58.4 %copy-start.5 = (bf16[24,4096]{1,0:T(8,128)(2,1)S(1)}, bf16[24,4096]{1,0:T(8,128)(2,1)}, u32[]{:S(2)}) copy-start(bf16[24,4096]{1,0:T(8,128)(2,1)} %param.21) | copy-start | bytes 589828
  48.5 25.9 %all-to-all-start = ((bf16[32,24,256]{2,1,0:T(8,128)(2,1)}), bf16[32,24,256]{2,1,0:T(8,128)(2,1)S(1)}, u32[]{:S(2)}, u32[]{:S(2)}) async-start(bf16[32,24,256]{2,1,0:T(8,128)(2,1)} %bitcast.10), calls=%async_computation | async-start | bytes 786432 | tf_op jit(solution)/shard_map/all_to_all | solution.py:22
  95.0 6.2 %copy-start.4 = (bf16[24,4096]{1,0:T(8,128)(2,1)}, bf16[24,4096]{1,0:T(8,128)(2,1)S(1)}, u32[]{:S(2)}) copy-start(bf16[24,4096]{1,0:T(8,128)(2,1)S(1)} %get-tuple-element.11) | copy-start | bytes 589828
  95.0 5.1 %collective-permute-start.4 = (bf16[24,2048]{1,0:T(8,128)(2,1)S(1)}, bf16[24,2048]{1,0:T(8,128)(2,1)S(1)}, u32[]{:S(2)}, u32[]{:S(2)}) collective-permute-start(bf16[24,2048]{1,0:T(8,128)(2,1)S(1)} %get-tuple-element.10), channel_id=1, source_target_pairs={{16,0},{0,16},{17,1},{1,17},{18,2},{2,18},{19,3},{3,19},{20,4},{4,... | collective-permute-start | bytes 294920 | tf_op jit(solution)/shard_map/ppermute | solution.py:12

commit v2 on v1

v2 whole, which is shorter than its diff:
```python
import jax
import jax.numpy as jnp
from jax import lax
from jax.sharding import PartitionSpec as P

EPSILON = 1e-06
F32 = jnp.float32
BF16 = jnp.bfloat16


def from_ahead(value, step, count):
    return lax.ppermute(value, "dp", [((i + step) % count, i) for i in range(count)])


def blocks_of(value, count):
    return jnp.stack([value] + [from_ahead(value, k, count) for k in range(1, count)])


def plane_sum(part, n_dp, n_lo):
    rows, width = part.shape[0] // n_dp, part.shape[1] // n_lo
    shares = part.reshape(n_dp, rows, n_lo, width).transpose(0, 2, 1, 3).reshape(n_dp * n_lo, rows, width)
    arrived = lax.all_to_all(shares, ("dp", "lo"), 0, 0, tiled=True)
    return jnp.sum(arrived.astype(F32), axis=0).astype(BF16)


def copies_sum(chunk, n_hi):
    arrived = lax.all_to_all(jnp.broadcast_to(chunk, (n_hi,) + chunk.shape), "hi", 0, 0, tiled=True)
    return jnp.sum(arrived.astype(F32), axis=0).astype(BF16)


def spread(chunk, axes, count, n_lo):
    rows, width = chunk.shape
    arrived = lax.all_to_all(jnp.broadcast_to(chunk, (count,) + chunk.shape), axes, 0, 0, tiled=True)
    blocks = arrived.reshape(count // n_lo, n_lo, rows, width).transpose(0, 2, 1, 3)
    return blocks.reshape(count // n_lo * rows, n_lo * width)


def per_device(
    hidden_in, norm_gain, route_ids, route_gates, w_gate, w_up, w_down, context, w_out, grad_out
):
    n_dp, n_hi, n_lo = (lax.axis_size(name) for name in ("dp", "hi", "lo"))
    me = lax.axis_index("dp")
    rows, width = hidden_in.shape
    expert = lax.axis_index("hi") * n_lo + lax.axis_index("lo")
    gate_own = jnp.sum(jnp.where(route_ids == expert, route_gates, 0.0), axis=1, keepdims=True)
    order = lambda blocks: jnp.roll(blocks, me, axis=0).reshape((n_dp * rows,) + blocks.shape[2:])
    hidden = order(blocks_of(hidden_in, n_dp)).astype(F32)
    grads = order(blocks_of(grad_out, n_dp)).astype(F32)
    gates = order(blocks_of(gate_own, n_dp))
    contexts = order(blocks_of(context, n_dp))

    scale_inv = lax.rsqrt(jnp.mean(hidden * hidden, axis=1, keepdims=True) + EPSILON)
    normed = (hidden * scale_inv * norm_gain).astype(BF16)
    rows_grad = (gates * grads).astype(BF16)
    dot = lambda a, b, dims: lax.dot_general(a, b, (dims, ((), ())), preferred_element_type=F32)
    wg, wu, wd = w_gate[0], w_up[0], w_down[0]
    pre_gate = dot(normed, wg, ((1,), (0,)))
    pre_up = dot(normed, wu, ((1,), (0,)))
    sig = jax.nn.sigmoid(pre_gate)
    act = (pre_gate * sig * pre_up).astype(BF16)
    out_part = (gates * dot(act, wd, ((1,), (0,)))).astype(BF16)
    out_plane = plane_sum(out_part, n_dp, n_lo)
    back_act = dot(rows_grad, wd, ((1,), (1,)))
    grad_gate = (back_act * pre_up * sig * (1.0 + pre_gate * (1.0 - sig))).astype(BF16)
    grad_up = (back_act * pre_gate * sig).astype(BF16)
    in_part = dot(grad_gate, wg, ((1,), (1,))) + dot(grad_up, wu, ((1,), (1,)))
    out_sum = copies_sum(out_plane, n_hi)
    in_plane = plane_sum(in_part.astype(BF16), n_dp, n_lo)
    moe_sum = spread(out_sum, "lo", n_lo, n_lo).astype(F32)
    in_sum = copies_sum(in_plane, n_hi)
    normed_grad = spread(in_sum, ("dp", "lo"), n_dp * n_lo, n_lo).astype(F32)

    output = (hidden_in.astype(F32) + moe_sum).astype(BF16)
    unit_rows = hidden * scale_inv
    scaled = normed_grad * norm_gain
    centre = jnp.mean(scaled * unit_rows, axis=1, keepdims=True)
    d_hidden = (grads + scale_inv * (scaled - unit_rows * centre)).astype(BF16)
    mine = lax.dynamic_slice_in_dim(d_hidden, me * rows, rows, 0)
    d_context = dot(mine, w_out, ((1,), (1,))).astype(BF16)
    part = width // n_dp
    columns = lax.dynamic_slice_in_dim(d_hidden, me * part, part, 1)
    d_w_out = dot(contexts, columns, ((0,), (0,))).astype(BF16)
    return (output, mine, d_context, d_w_out)


def low_count(n_dp, n_e):
    low = 1
    while n_e % (2 * low) == 0 and 2 * low * n_dp <= 2 * (n_e // (2 * low)):
        low = 2 * low
    return low


def solution(mesh):
    n_dp, n_e = mesh.shape["dp"], mesh.shape["expert"]
    low = low_count(n_dp, n_e)
    mesh = jax.sharding.Mesh(mesh.devices.reshape(n_dp, n_e // low, low), ("dp", "hi", "lo"))
    expert = ("hi", "lo")
    return jax.shard_map(
        per_device,
        mesh=mesh,
        in_specs=(
            P("dp", None),
            P(),
            P("dp", None),
            P("dp", None),
            P(expert, None, "dp"),
            P(expert, None, "dp"),
            P(expert, "dp", None),
            P("dp", expert),
            P(expert, None),
            P("dp", None),
        ),
        out_specs=(P("dp", None), P("dp", None), P("dp", expert), P(expert, "dp")),
        check_vma=False,
    )
```

time: 102 us -> 102 us (level)
  blocking collectives: 42.4 us -> 0 us
  waiting for transfers between devices: 17.1 us -> 32.9 us
  starting transfers between devices: 15.3 us -> 30.1 us
  local copies, waits for them, and re-layouts: 2.63 us -> 8.52 us
  matrix products: 17.2 us -> 20.9 us
  other arithmetic: 5.69 us -> 8.17 us
    all_gather x2 -> x0, blocking collectives: 42.4 us -> none  [reduce_all(): spread = lax.all_gather(total, 'expert', axis=0, tiled=False)]
    all_to_all x2 -> x6, waiting for transfers between devices: 7.87 us -> 27.5 us  [the longest x2 13.4 us: copies_sum(): lax.all_to_all(jnp.broadcast_to(chunk, (n_hi,) + chunk.shape), 'hi', 0, 0...]
    all_to_all x2 -> x6, starting transfers between devices: 8.69 us -> 23.5 us  [the longest x2 8.48 us: plane_sum(): arrived = lax.all_to_all(shares, ('dp', 'lo'), 0, 0, tiled=True)]
    ppermute x5 -> x4, waiting for transfers between devices: 9.22 us -> 5.41 us  [from_ahead(): lax.ppermute(value, 'dp', [((i + step) % count, i) for i in range(count)])]
    dot_general x8, matrix products: 17.2 us -> 20.9 us  [per_device(): lax.dot_general(a, b, (dims, ((), ())), preferred_element_type=F32)]
    broadcast_in_dim x0 -> x4, local copies, waits for them, and re-layouts: none -> 2.87 us  [the longest x2 1.48 us: spread(): jnp.broadcast_to(chunk, (count,) + chunk.shape)]
    convert_element_type x1 -> x5, other arithmetic: 0.85 us -> 3.61 us  [the longest x1 1.66 us: per_device(): output = (hidden_in.astype(F32) + moe_sum).astype(BF16)]
    reshape x2 -> x4, local copies, waits for them, and re-layouts: 1.73 us -> 3.31 us  [plane_sum(): part.reshape(n_dp, rows, n_lo, width).transpose(0, 2, 1, 3)]
  transfers between devices with their start and end apart: 7 -> 10, of which waited for: 3 -> 7; matrix products, arithmetic and copies ran while one was open for 23% -> 30% of each run, Pallas kernels for 0% -> 0%
where the time goes in v2:
time: 102 us; the launch traced here: 101 us
  waiting for transfers between devices  32.9 us (32%)
  starting transfers between devices  30.1 us (30%)
  matrix products  20.9 us (20%)
  local copies, waits for them, and re-layouts  8.52 us (8%)
  other arithmetic  8.17 us (8%)
    dot_general x8, matrix products, per_device(): lax.dot_general(a, b, (dims, ((), ())), preferred_element_type=F32)  20.9 us
    all_to_all x2, waiting for transfers between devices, copies_sum(): lax.all_to_all(jnp.broadcast_to(chunk, (n_hi,) + chunk.shape), 'hi', 0, 0...  13.4 us
    all_to_all x2, starting transfers between devices, plane_sum(): arrived = lax.all_to_all(shares, ('dp', 'lo'), 0, 0, tiled=True)  8.48 us
    all_to_all x2, starting transfers between devices, copies_sum(): lax.all_to_all(jnp.broadcast_to(chunk, (n_hi,) + chunk.shape), 'hi', 0, 0...  8.24 us
    all_to_all x2, waiting for transfers between devices, plane_sum(): arrived = lax.all_to_all(shares, ('dp', 'lo'), 0, 0, tiled=True)  7.43 us
    all_to_all x2, starting transfers between devices, spread(): lax.all_to_all(jnp.broadcast_to(chunk, (count,) + chunk.shape), axes, 0,...  6.82 us
    all_to_all x2, waiting for transfers between devices, spread(): lax.all_to_all(jnp.broadcast_to(chunk, (count,) + chunk.shape), axes, 0,...  6.66 us
    ppermute x4, starting transfers between devices, from_ahead(): lax.ppermute(value, 'dp', [((i + step) % count, i) for i in range(count)])  6.57 us
  transfers between devices with their start and end apart: 10, of which 7 were waited for; matrix products, arithmetic and copies ran while one was open for 30% of the time, Pallas kernels for 0%

profile of v2, /device:TPU:0, one launch (start us, length us, event | category | flops | bytes accessed | tf_op | source)
XLA Modules:
  0.0 101.5 jit_solution(2627450801742985060)
XLA Ops:
  0.6 3.0 %collective-permute-start.1 = (bf16[24,4096]{1,0:T(8,128)(2,1)}, bf16[24,4096]{1,0:T(8,128)(2,1)S(1)}, u32[]{:S(2)}, u32[]{:S(2)}) collective-permute-start(bf16[24,4096]{1,0:T(8,128)(2,1)} %param.12), channel_id=1, source_target_pairs={{16,0},{0,16},{17,1},{1,17},{18,2},{2,18},{19,3},{3,19},{20,4},{4,... | collective-permute-start | bytes 589832 | tf_op jit(solution)/shard_map/ppermute | solution.py:12
  3.7 0.7 select_reduce_fusion
  4.4 0.1 collective-permute-start
  4.5 1.9 %collective-permute-start.2 = (bf16[24,4096]{1,0:T(8,128)(2,1)}, bf16[24,4096]{1,0:T(8,128)(2,1)}, u32[]{:S(2)}, u32[]{:S(2)}) collective-permute-start(bf16[24,4096]{1,0:T(8,128)(2,1)} %param.21), channel_id=1, source_target_pairs={{16,0},{0,16},{17,1},{1,17},{18,2},{2,18},{19,3},{3,19},{20,4},{4,... | collective-permute-start | bytes 589832 | tf_op jit(solution)/shard_map/ppermute | solution.py:12
  6.5 3.2 %collective-permute-done = f32[24,1]{0,1:T(1,128)S(1)} collective-permute-done((f32[24,1]{0,1:T(1,128)S(1)}, f32[24,1]{0,1:T(1,128)S(1)}, u32[]{:S(2)}, u32[]{:S(2)}) %collective-permute-start) | collective-permute-done | bytes 128 | tf_op jit(solution)/shard_map/ppermute | solution.py:12
  9.7 0.5 broadcast.76
  10.2 0.7 fusion.56
  10.9 0.1 mul.128
  10.9 1.5 %multiply_reduce_fusion = (f32[2,24]{1,0:T(2,128)S(1)}, f32[2,24,4096]{2,1,0:T(8,128)S(1)}) fusion(s32[]{:T(128)S(6)} %select_n.38, bf16[1,24,4096]{2,1,0:T(8,128)(2,1)S(1)} %bitcast.104, bf16[1,24,4096]{2,1,0:T(8,128)(2,1)} %bitcast.102), kind=kLoop, calls=%fused_computation.40 | loop fusion | flops 1179600 | bytes 1179844 | tf_op jit(solution)/shard_map/reduce_sum | solution.py:52
  12.4 1.2 %multiply_convert_fusion.1 = bf16[2,24,4096]{2,1,0:T(8,128)(2,1)S(1)} fusion(f32[2,24,4096]{2,1,0:T(8,128)S(1)} %get-tuple-element.8, f32[4096]{0:T(1024)} %param.13, f32[2,24]{1,0:T(2,128)S(1)} %add_rsqrt_fusion), kind=kLoop, calls=%fused_computation.39 | loop fusion | flops 589824 | bytes 1196224 | tf_op jit(solution)/shard_map/convert_element_type | solution.py:53
  13.7 4.1 %fusion.10 = f32[48,768]{1,0:T(8,128)S(1)} fusion(bf16[48,4096]{1,0:T(8,128)(2,1)S(1)} %bitcast.94, bf16[1,4096,768]{2,1,0:T(8,128)(2,1)} %param.16), kind=kOutput, calls=%fused_computation.10 | convolution fusion | flops 301989888 | bytes 6832128 | tf_op jit(solution)/shard_map/dot_general | solution.py:55
  17.8 1.1 %fusion.6 = f32[48,768]{1,0:T(8,128)S(1)} fusion(bf16[48,4096]{1,0:T(8,128)(2,1)S(1)} %bitcast.95, bf16[1,4096,768]{2,1,0:T(8,128)(2,1)S(1)} %copy-done.1), kind=kOutput, calls=%fused_computation.6 | convolution fusion | flops 301989888 | bytes 6832128 | tf_op jit(solution)/shard_map/dot_general | solution.py:55
  18.9 1.2 %fusion.18 = bf16[48,4096]{1,0:T(8,128)(2,1)S(1)} fusion(bf16[1,768,4096]{2,1,0:T(8,128)(2,1)S(1)} %copy-done.2, f32[48]{0:T(128)S(1)} %mul.128, f32[48,768]{1,0:T(8,128)S(1)} %fusion.6, f32[48,768]{1,0:T(8,128)S(1)} %fusion.10), kind=kOutput, calls=%fused_computation.14 | convolution fusion | flops 302604288 | bytes 6979776 | tf_op jit(solution)/shard_map/dot_general | solution.py:55
  20.1 0.3 reshape.112
  20.4 0.9 copy.29
  21.3 4.3 %all-to-all-start = ((bf16[8,24,1024]{2,1,0:T(8,128)(2,1)}), bf16[8,24,1024]{2,1,0:T(8,128)(2,1)S(1)}, u32[]{:S(2)}, u32[]{:S(2)}) async-start(bf16[8,24,1024]{2,1,0:T(8,128)(2,1)} %bitcast.10), calls=%async_computation | async-start | bytes 786432 | tf_op jit(solution)/shard_map/all_to_all | solution.py:22
  25.6 1.5 %multiply_convert_fusion = (bf16[2,24,4096]{2,1,0:T(8,128)(2,1)S(1)}, f32[2,24,4096]{2,1,0:T(8,128)S(1)}) fusion(f32[2,24]{1,0:T(2,128)S(1)} %bitcast.108, s32[]{:T(128)S(6)} %select_n.38, bf16[1,24,4096]{2,1,0:T(8,128)(2,1)} %bitcast.14, bf16[1,24,4096]{2,1,0:T(8,128)(2,1)S(1)} %bitcast.103), kind=kLoop, calls=%fused_computation.38 | loop fusion | flops 1179648 | bytes 1573060 | tf_op jit(solution)/shard_map/convert_element_type | solution.py:54
  27.2 4.9 %fusion = f32[48,768]{1,0:T(8,128)S(1)} fusion(bf16[48,4096]{1,0:T(8,128)(2,1)S(1)} %bitcast.101, bf16[1,768,4096]{2,1,0:T(8,128)(2,1)} %param.18), kind=kOutput, calls=%fused_computation | convolution fusion | flops 301989888 | bytes 6832128 | tf_op jit(solution)/shard_map/dot_general | solution.py:55
  32.1 4.7 %fusion.4 = f32[48,4096]{1,0:T(8,128)S(1)} fusion(bf16[1,4096,768]{2,1,0:T(8,128)(2,1)} %param.17, f32[48,768]{1,0:T(8,128)S(1)} %fusion, f32[48,768]{1,0:T(8,128)S(1)} %fusion.10), kind=kOutput, calls=%fused_computation.4 | convolution fusion | flops 302211072 | bytes 7372800 | tf_op jit(solution)/shard_map/dot_general | solution.py:55
  36.9 2.7 %fusion.21 = bf16[48,4096]{1,0:T(8,128)(2,1)} fusion(f32[48,4096]{1,0:T(8,128)S(1)} %fusion.4, bf16[1,4096,768]{2,1,0:T(8,128)(2,1)S(1)} %bitcast.91, f32[48,768]{1,0:T(8,128)S(1)} %fusion.10, f32[48,768]{1,0:T(8,128)S(1)} %fusion, f32[48,768]{1,0:T(8,128)S(1)} %fusion.6), kind=kOutput, calls=%fused_computation.15 | convolution fusion | flops 302751744 | bytes 7913472 | tf_op jit(solution)/shard_map/dot_general | solution.py:55
  39.6 1.3 %reshape.114 = bf16[2,24,4,1024]{3,2,1,0:T(4,128)(2,1)S(1)} reshape(bf16[48,4096]{1,0:T(8,128)(2,1)} %fusion.21) | data formatting | bytes 786432 | tf_op jit(solution)/shard_map/reshape | solution.py:21
  40.9 0.9 copy.31
  41.8 4.2 %all-to-all-start.3 = ((bf16[8,24,1024]{2,1,0:T(8,128)(2,1)}), bf16[8,24,1024]{2,1,0:T(8,128)(2,1)S(1)}, u32[]{:S(2)}, u32[]{:S(2)}) async-start(bf16[8,24,1024]{2,1,0:T(8,128)(2,1)} %bitcast.98), calls=%async_computation.3 | async-start | bytes 786432 | tf_op jit(solution)/shard_map/all_to_all | solution.py:22
  46.0 7.4 %all-to-all-done.3 = bf16[8,24,1024]{2,1,0:T(8,128)(2,1)S(1)} async-done(((bf16[8,24,1024]{2,1,0:T(8,128)(2,1)}), bf16[8,24,1024]{2,1,0:T(8,128)(2,1)S(1)}, u32[]{:S(2)}, u32[]{:S(2)}) %all-to-all-start.3) | async-done | bytes 393248 | tf_op jit(solution)/shard_map/all_to_all | solution.py:22
  53.4 0.7 broadcast_in_dim.25
  54.1 4.9 %all-to-all-start.1 = ((bf16[4,24,1024]{2,1,0:T(8,128)(2,1)}), bf16[4,24,1024]{2,1,0:T(8,128)(2,1)S(1)}, u32[]{:S(2)}, u32[]{:S(2)}) async-start(bf16[4,24,1024]{2,1,0:T(8,128)(2,1)} %broadcast_in_dim.25), calls=%async_computation.1 | async-start | bytes 393216 | tf_op jit(solution)/shard_map/all_to_all | solution.py:27
  59.1 7.2 %all-to-all-done.1 = bf16[4,24,1024]{2,1,0:T(8,128)(2,1)S(1)} async-done(((bf16[4,24,1024]{2,1,0:T(8,128)(2,1)}), bf16[4,24,1024]{2,1,0:T(8,128)(2,1)S(1)}, u32[]{:S(2)}, u32[]{:S(2)}) %all-to-all-start.1) | async-done | bytes 196640 | tf_op jit(solution)/shard_map/all_to_all | solution.py:27
  66.3 0.7 broadcast_in_dim.27
  67.0 3.4 %all-to-all-start.4 = ((bf16[4,24,1024]{2,1,0:T(8,128)(2,1)}), bf16[4,24,1024]{2,1,0:T(8,128)(2,1)S(1)}, u32[]{:S(2)}, u32[]{:S(2)}) async-start(bf16[4,24,1024]{2,1,0:T(8,128)(2,1)} %broadcast_in_dim.27), calls=%async_computation.4 | async-start | bytes 393216 | tf_op jit(solution)/shard_map/all_to_all | solution.py:27
  70.4 6.2 %all-to-all-done.4 = bf16[4,24,1024]{2,1,0:T(8,128)(2,1)S(1)} async-done(((bf16[4,24,1024]{2,1,0:T(8,128)(2,1)}), bf16[4,24,1024]{2,1,0:T(8,128)(2,1)S(1)}, u32[]{:S(2)}, u32[]{:S(2)}) %all-to-all-start.4) | async-done | bytes 196640 | tf_op jit(solution)/shard_map/all_to_all | solution.py:27
  76.6 0.7 broadcast_in_dim.26
  77.3 3.4 %all-to-all-start.2 = ((bf16[4,24,1024]{2,1,0:T(8,128)(2,1)}), bf16[4,24,1024]{2,1,0:T(8,128)(2,1)S(1)}, u32[]{:S(2)}, u32[]{:S(2)}) async-start(bf16[4,24,1024]{2,1,0:T(8,128)(2,1)} %broadcast_in_dim.26), calls=%async_computation.2 | async-start | bytes 393216 | tf_op jit(solution)/shard_map/all_to_all | solution.py:33
  80.7 1.5 %collective-permute-start.3 = (bf16[24,128]{1,0:T(8,128)(2,1)S(1)}, bf16[24,128]{1,0:T(8,128)(2,1)S(1)}, u32[]{:S(2)}, u32[]{:S(2)}) collective-permute-start(bf16[24,128]{1,0:T(8,128)(2,1)S(1)} %copy-done.6), channel_id=1, source_target_pairs={{16,0},{0,16},{17,1},{1,17},{18,2},{2,18},{19,3},{3,19},{20,4},{4,... | collective-permute-start | bytes 18440 | tf_op jit(solution)/shard_map/ppermute | solution.py:12
  82.2 2.2 %collective-permute-done.3 = bf16[24,128]{1,0:T(8,128)(2,1)S(1)} collective-permute-done((bf16[24,128]{1,0:T(8,128)(2,1)S(1)}, bf16[24,128]{1,0:T(8,128)(2,1)S(1)}, u32[]{:S(2)}, u32[]{:S(2)}) %collective-permute-start.3) | collective-permute-done | bytes 6176 | tf_op jit(solution)/shard_map/ppermute | solution.py:12
  84.5 1.5 %all-to-all-done.2 = bf16[4,24,1024]{2,1,0:T(8,128)(2,1)S(1)} async-done(((bf16[4,24,1024]{2,1,0:T(8,128)(2,1)}), bf16[4,24,1024]{2,1,0:T(8,128)(2,1)S(1)}, u32[]{:S(2)}, u32[]{:S(2)}) %all-to-all-start.2) | async-done | bytes 196640 | tf_op jit(solution)/shard_map/all_to_all | solution.py:33
  86.0 0.8 broadcast_in_dim.28
  86.8 3.5 %all-to-all-start.5 = ((bf16[8,24,1024]{2,1,0:T(8,128)(2,1)}), bf16[8,24,1024]{2,1,0:T(8,128)(2,1)S(1)}, u32[]{:S(2)}, u32[]{:S(2)}) async-start(bf16[8,24,1024]{2,1,0:T(8,128)(2,1)} %broadcast_in_dim.28), calls=%async_computation.5 | async-start | bytes 786432 | tf_op jit(solution)/shard_map/all_to_all | solution.py:33
  90.2 0.3 copy.30
  90.5 0.2 copy.35
  90.8 1.7 %add_convert_fusion = bf16[24,4096]{1,0:T(8,128)(2,1)} fusion(f32[24,4096]{1,0:T(8,128)S(1)} %bitcast.100, bf16[24,4096]{1,0:T(8,128)(2,1)} %param.12), kind=kLoop, calls=%fused_computation.50 | loop fusion | flops 294912 | bytes 786432 | tf_op jit(solution)/shard_map/convert_element_type | solution.py:73
  92.4 5.2 %all-to-all-done.5 = bf16[8,24,1024]{2,1,0:T(8,128)(2,1)S(1)} async-done(((bf16[8,24,1024]{2,1,0:T(8,128)(2,1)}), bf16[8,24,1024]{2,1,0:T(8,128)(2,1)S(1)}, u32[]{:S(2)}, u32[]{:S(2)}) %all-to-all-start.5) | async-done | bytes 393248 | tf_op jit(solution)/shard_map/all_to_all | solution.py:33
  97.6 0.2 fusion.26
  97.9 0.1 convert_bitcast_fusion
  98.0 0.5 copy.32
  98.6 0.5 copy.36
  99.0 0.3 fusion.31
  99.4 1.0 convolution_convert_fusion.1
  100.4 1.1 %convolution_convert_fusion = bf16[128,2048]{1,0:T(8,128)(2,1)} fusion(bf16[48,128]{1,0:T(8,128)(2,1)S(1)} %bitcast.105, bf16[48,4096]{1,0:T(8,128)(2,1)S(1)} %fusion.31, s32[]{:T(128)S(6)} %select_n.40), kind=kOutput, calls=%fused_computation.16 | convolution fusion | flops 25427968 | bytes 733188 | tf_op jit(solution)/shard_map/dot_general | solution.py:55
  (34 shorter events, 0.5 us)
Async XLA Ops:
  0.6 98.7 %copy-start = (bf16[128,4096]{1,0:T(8,128)(2,1)S(1)}, bf16[128,4096]{1,0:T(8,128)(2,1)}, u32[]{:S(2)}) copy-start(bf16[128,4096]{1,0:T(8,128)(2,1)} %param.20) | copy-start | bytes 3145732
  0.6 10.3 %collective-permute-start.1 = (bf16[24,4096]{1,0:T(8,128)(2,1)}, bf16[24,4096]{1,0:T(8,128)(2,1)S(1)}, u32[]{:S(2)}, u32[]{:S(2)}) collective-permute-start(bf16[24,4096]{1,0:T(8,128)(2,1)} %param.12), channel_id=1, source_target_pairs={{16,0},{0,16},{17,1},{1,17},{18,2},{2,18},{19,3},{3,19},{20,4},{4,... | collective-permute-start | bytes 589832 | tf_op jit(solution)/shard_map/ppermute | solution.py:12
  4.4 5.3 %collective-permute-start = (f32[24,1]{0,1:T(1,128)S(1)}, f32[24,1]{0,1:T(1,128)S(1)}, u32[]{:S(2)}, u32[]{:S(2)}) collective-permute-start(f32[24,1]{0,1:T(1,128)S(1)} %bitcast.109), channel_id=1, source_target_pairs={{16,0},{0,16},{17,1},{1,17},{18,2},{2,18},{19,3},{3,19},{20,4},{4,... | collective-permute-start | bytes 296 | tf_op jit(solution)/shard_map/ppermute | solution.py:12
  4.5 21.1 %collective-permute-start.2 = (bf16[24,4096]{1,0:T(8,128)(2,1)}, bf16[24,4096]{1,0:T(8,128)(2,1)}, u32[]{:S(2)}, u32[]{:S(2)}) collective-permute-start(bf16[24,4096]{1,0:T(8,128)(2,1)} %param.21), channel_id=1, source_target_pairs={{16,0},{0,16},{17,1},{1,17},{18,2},{2,18},{19,3},{3,19},{20,4},{4,... | collective-permute-start | bytes 589832 | tf_op jit(solution)/shard_map/ppermute | solution.py:12
  10.9 6.8 %copy-start.1 = (bf16[1,4096,768]{2,1,0:T(8,128)(2,1)S(1)}, bf16[1,4096,768]{2,1,0:T(8,128)(2,1)}, u32[]{:S(2)}) copy-start(bf16[1,4096,768]{2,1,0:T(8,128)(2,1)} %param.17) | copy-start | bytes 18874372
  13.7 5.3 %copy-start.2 = (bf16[1,768,4096]{2,1,0:T(8,128)(2,1)S(1)}, bf16[1,768,4096]{2,1,0:T(8,128)(2,1)}, u32[]{:S(2)}) copy-start(bf16[1,768,4096]{2,1,0:T(8,128)(2,1)} %param.18) | copy-start | bytes 18874372
  18.9 6.7 %copy-start.4 = (bf16[24,4096]{1,0:T(8,128)(2,1)S(1)}, bf16[24,4096]{1,0:T(8,128)(2,1)}, u32[]{:S(2)}) copy-start(bf16[24,4096]{1,0:T(8,128)(2,1)} %param.21) | copy-start | bytes 589828
  21.3 20.5 %all-to-all-start = ((bf16[8,24,1024]{2,1,0:T(8,128)(2,1)}), bf16[8,24,1024]{2,1,0:T(8,128)(2,1)S(1)}, u32[]{:S(2)}, u32[]{:S(2)}) async-start(bf16[8,24,1024]{2,1,0:T(8,128)(2,1)} %bitcast.10), calls=%async_computation | async-start | bytes 786432 | tf_op jit(solution)/shard_map/all_to_all | solution.py:22
  25.6 11.2 %slice-start = ((s8[6291456]{0:T(1024)(128)(4,1)}), s8[4194304]{0:T(1024)(128)(4,1)S(1)}, s32[]{:S(2)}) async-start(s8[6291456]{0:T(1024)(128)(4,1)} %bitcast.90), calls=%async_computation.6 | async-start | bytes 8388608
  27.2 9.7 %slice-start.1 = ((s8[6291456]{0:T(1024)(128)(4,1)}), s8[2097152]{0:T(1024)(128)(4,1)S(1)}, s32[]{:S(2)}) async-start(s8[6291456]{0:T(1024)(128)(4,1)} %bitcast.90), calls=%async_computation.7 | async-start | bytes 4194304
  36.9 43.8 %copy-start.6 = (bf16[24,128]{1,0:T(8,128)(2,1)S(1)}, bf16[24,128]{1,0:T(8,128)(2,1)}, u32[]{:S(2)}) copy-start(bf16[24,128]{1,0:T(8,128)(2,1)} %param.19) | copy-start | bytes 18436
  36.9 45.3 %copy-start.5 = (f32[4096]{0:T(1024)S(1)}, f32[4096]{0:T(1024)}, u32[]{:S(2)}) copy-start(f32[4096]{0:T(1024)} %param.13) | copy-start | bytes 49156
  41.8 11.7 %all-to-all-start.3 = ((bf16[8,24,1024]{2,1,0:T(8,128)(2,1)}), bf16[8,24,1024]{2,1,0:T(8,128)(2,1)S(1)}, u32[]{:S(2)}, u32[]{:S(2)}) async-start(bf16[8,24,1024]{2,1,0:T(8,128)(2,1)} %bitcast.98), calls=%async_computation.3 | async-start | bytes 786432 | tf_op jit(solution)/shard_map/all_to_all | solution.py:22
  54.1 12.2 %all-to-all-start.1 = ((bf16[4,24,1024]{2,1,0:T(8,128)(2,1)}), bf16[4,24,1024]{2,1,0:T(8,128)(2,1)S(1)}, u32[]{:S(2)}, u32[]{:S(2)}) async-start(bf16[4,24,1024]{2,1,0:T(8,128)(2,1)} %broadcast_in_dim.25), calls=%async_computation.1 | async-start | bytes 393216 | tf_op jit(solution)/shard_map/all_to_all | solution.py:27
  67.0 9.6 %all-to-all-start.4 = ((bf16[4,24,1024]{2,1,0:T(8,128)(2,1)}), bf16[4,24,1024]{2,1,0:T(8,128)(2,1)S(1)}, u32[]{:S(2)}, u32[]{:S(2)}) async-start(bf16[4,24,1024]{2,1,0:T(8,128)(2,1)} %broadcast_in_dim.27), calls=%async_computation.4 | async-start | bytes 393216 | tf_op jit(solution)/shard_map/all_to_all | solution.py:27
  77.3 8.7 %all-to-all-start.2 = ((bf16[4,24,1024]{2,1,0:T(8,128)(2,1)}), bf16[4,24,1024]{2,1,0:T(8,128)(2,1)S(1)}, u32[]{:S(2)}, u32[]{:S(2)}) async-start(bf16[4,24,1024]{2,1,0:T(8,128)(2,1)} %broadcast_in_dim.26), calls=%async_computation.2 | async-start | bytes 393216 | tf_op jit(solution)/shard_map/all_to_all | solution.py:33
  80.7 3.7 %collective-permute-start.3 = (bf16[24,128]{1,0:T(8,128)(2,1)S(1)}, bf16[24,128]{1,0:T(8,128)(2,1)S(1)}, u32[]{:S(2)}, u32[]{:S(2)}) collective-permute-start(bf16[24,128]{1,0:T(8,128)(2,1)S(1)} %copy-done.6), channel_id=1, source_target_pairs={{16,0},{0,16},{17,1},{1,17},{18,2},{2,18},{19,3},{3,19},{20,4},{4,... | collective-permute-start | bytes 18440 | tf_op jit(solution)/shard_map/ppermute | solution.py:12
  86.8 10.9 %all-to-all-start.5 = ((bf16[8,24,1024]{2,1,0:T(8,128)(2,1)}), bf16[8,24,1024]{2,1,0:T(8,128)(2,1)S(1)}, u32[]{:S(2)}, u32[]{:S(2)}) async-start(bf16[8,24,1024]{2,1,0:T(8,128)(2,1)} %broadcast_in_dim.28), calls=%async_computation.5 | async-start | bytes 786432 | tf_op jit(solution)/shard_map/all_to_all | solution.py:33
  99.4 2.1 %copy-start.3 = (bf16[24,4096]{1,0:T(8,128)(2,1)}, bf16[24,4096]{1,0:T(8,128)(2,1)S(1)}, u32[]{:S(2)}) copy-start(bf16[24,4096]{1,0:T(8,128)(2,1)S(1)} %constant_dynamic-slice_fusion.3) | copy-start | bytes 589828

commit v3 on v1

v3 whole, which is shorter than its diff:
```python
import functools

import jax
import jax.numpy as jnp
from jax import lax
from jax.experimental import pallas as pl
from jax.experimental.pallas import tpu as pltpu
from jax.sharding import PartitionSpec as P

EPSILON = 1e-06
F32 = jnp.float32
BF16 = jnp.bfloat16
STEP = 256
VMEM_LIMIT = 40 * 1024 * 1024


def dot(a, b, dims):
    return lax.dot_general(a, b, (dims, ((), ())), preferred_element_type=F32)


def place(step, count):
    return pl.multiple_of(step * count, count)


def rows_of(refs, columns):
    return jnp.concatenate([ref[:, columns].astype(F32) for ref in refs], axis=0)


def own_columns(ids, i, j, width):
    return ((ids[1] ^ j) * 2 + (ids[2] ^ i)) * width


def store_blocks(out_ref, j, columns, value, count):
    rows = value.shape[0] // count
    for k in range(count):
        out_ref[j, k, :, columns] = value[k * rows : (k + 1) * rows].astype(BF16)


def forward_kernel(n_dp, ids, *refs):
    hid, gates = refs[:n_dp], refs[n_dp : 2 * n_dp]
    gain, w_gate, w_up, w_down, pre_gate, pre_up, send, keep, normed, act = refs[2 * n_dp :]
    total = hid[0].shape[0] * n_dp
    width = hid[0].shape[1]
    chunk = send.shape[3]

    def squares(step, held):
        value = rows_of(hid, pl.ds(place(step, 512), 512))
        return held + jnp.sum(value * value, axis=1, keepdims=True)

    sums = lax.fori_loop(0, width // 512, squares, jnp.zeros((total, 1), F32))
    scale = lax.rsqrt(sums / width + EPSILON)

    def norm(step, carry):
        columns = pl.ds(place(step, 512), 512)
        normed[:, columns] = (rows_of(hid, columns) * scale * gain[:, columns]).astype(BF16)
        return carry

    lax.fori_loop(0, width // 512, norm, 0)

    def hidden_units(step, carry):
        columns = pl.ds(place(step, STEP), STEP)
        gate_part = dot(normed[...], w_gate[:, columns], ((1,), (0,)))
        up_part = dot(normed[...], w_up[:, columns], ((1,), (0,)))
        pre_gate[:, columns] = gate_part
        pre_up[:, columns] = up_part
        act[:, columns] = (gate_part * jax.nn.sigmoid(gate_part) * up_part).astype(BF16)
        return carry

    lax.fori_loop(0, w_gate.shape[1] // STEP, hidden_units, 0)
    weight = jnp.concatenate([gate[:, :1] for gate in gates], axis=0)
    for i, target in ((1, send), (0, keep)):
        for j in range(2):
            first = own_columns(ids, i, j, chunk)

            def outward(step, carry):
                columns = pl.ds(pl.multiple_of(first + step * STEP, STEP), STEP)
                part = weight * dot(act[...], w_down[:, columns], ((1,), (0,)))
                store_blocks(target, j, pl.ds(place(step, STEP), STEP), part, n_dp)
                return carry

            lax.fori_loop(0, chunk // STEP, outward, 0)


def inward_part(ids, i, n_dp, grad_gate, grad_up, w_gate, w_up, target):
    chunk = target.shape[3]
    for j in range(2):
        first = own_columns(ids, i, j, chunk)

        def inward(step, carry):
            columns = pl.ds(pl.multiple_of(first + step * STEP, STEP), STEP)
            part = dot(grad_gate[...], w_gate[columns, :], ((1,), (1,)))
            part = part + dot(grad_up[...], w_up[columns, :], ((1,), (1,)))
            store_blocks(target, j, pl.ds(place(step, STEP), STEP), part, n_dp)
            return carry

        lax.fori_loop(0, chunk // STEP, inward, 0)


def backward_kernel(n_dp, ids, *refs):
    grads, gates = refs[:n_dp], refs[n_dp : 2 * n_dp]
    pre_gate, pre_up, w_gate, w_up, w_down, grad_gate, grad_up, send, weighted = refs[2 * n_dp :]
    weight = jnp.concatenate([gate[:, :1] for gate in gates], axis=0)

    def weigh(step, carry):
        columns = pl.ds(place(step, 512), 512)
        weighted[:, columns] = (weight * rows_of(grads, columns)).astype(BF16)
        return carry

    lax.fori_loop(0, weighted.shape[1] // 512, weigh, 0)

    def hidden_units(step, carry):
        columns = pl.ds(place(step, STEP), STEP)
        back = dot(weighted[...], w_down[columns, :], ((1,), (1,)))
        gate_part, up_part = pre_gate[:, columns], pre_up[:, columns]
        sig = jax.nn.sigmoid(gate_part)
        grad_gate[:, columns] = (back * up_part * sig * (1.0 + gate_part * (1.0 - sig))).astype(BF16)
        grad_up[:, columns] = (back * gate_part * sig).astype(BF16)
        return carry

    lax.fori_loop(0, w_down.shape[0] // STEP, hidden_units, 0)
    inward_part(ids, 1, n_dp, grad_gate, grad_up, w_gate, w_up, send)


def keep_kernel(n_dp, ids, grad_gate, grad_up, w_gate, w_up, keep):
    inward_part(ids, 0, n_dp, grad_gate, grad_up, w_gate, w_up, keep)


def finish_kernel(n_dp, ids, *refs):
    hid, grads, contexts = refs[:n_dp], refs[n_dp : 2 * n_dp], refs[2 * n_dp : 3 * n_dp]
    gain, w_out, back_own, back_other, moe_own, moe_other = refs[3 * n_dp : 3 * n_dp + 6]
    output, d_hidden, d_context, d_w_out, summed, d_all = refs[3 * n_dp + 6 :]
    rows, width = hid[0].shape
    chunk = back_own.shape[3]
    for i, (back, moe) in enumerate(((back_own, moe_own), (back_other, moe_other))):
        for j in range(2):
            columns = pl.ds(pl.multiple_of(own_columns(ids, i, j, chunk), chunk), chunk)
            for k in range(n_dp):
                summed[k * rows : (k + 1) * rows, columns] = back[k, j].astype(F32) * gain[:, columns]
            output[:, columns] = (hid[0][:, columns].astype(F32) + moe[j].astype(F32)).astype(BF16)

    def sums(step, held):
        columns = pl.ds(place(step, 512), 512)
        value = rows_of(hid, columns)
        return (
            held[0] + jnp.sum(value * value, axis=1, keepdims=True),
            held[1] + jnp.sum(value * summed[:, columns], axis=1, keepdims=True),
        )

    zeros = jnp.zeros((rows * n_dp, 1), F32)
    squares, products = lax.fori_loop(0, width // 512, sums, (zeros, zeros))
    scale = lax.rsqrt(squares / width + EPSILON)
    centre = scale * products / width

    def total(step, carry):
        columns = pl.ds(place(step, 512), 512)
        unit_rows = rows_of(hid, columns) * scale
        value = rows_of(grads, columns) + scale * (summed[:, columns] - unit_rows * centre)
        d_all[:, columns] = value.astype(BF16)
        d_hidden[:, columns] = value[:rows].astype(BF16)
        return carry

    lax.fori_loop(0, width // 512, total, 0)
    d_context[...] = dot(d_hidden[...], w_out[...], ((1,), (1,))).astype(BF16)
    part = width // n_dp
    turned = jnp.concatenate([ref[...].astype(F32) for ref in contexts], axis=0).T.astype(BF16)
    step_width = min(part, 512)

    def product(step, carry):
        columns = pl.ds(pl.multiple_of(ids[0] * part + step * step_width, step_width), step_width)
        d_w_out[:, pl.ds(place(step, step_width), step_width)] = dot(
            turned, d_all[:, columns], ((1,), (0,))
        ).astype(BF16)
        return carry

    lax.fori_loop(0, part // step_width, product, 0)


def run(kernel, n_dp, ids, operands, outs, scratch, flops, name):
    held = [pltpu.with_memory_space_constraint(value, pltpu.VMEM) for value in operands]
    return pl.pallas_call(
        functools.partial(kernel, n_dp),
        out_shape=[pltpu.VMEM(shape, kind) for shape, kind in outs],
        in_specs=[pl.BlockSpec(memory_space=pltpu.SMEM)]
        + [pl.BlockSpec(memory_space=pltpu.VMEM)] * len(held),
        out_specs=[pl.BlockSpec(memory_space=pltpu.VMEM)] * len(outs),
        scratch_shapes=[pltpu.VMEM(shape, kind) for shape, kind in scratch],
        compiler_params=pltpu.CompilerParams(vmem_limit_bytes=VMEM_LIMIT),
        cost_estimate=pl.CostEstimate(flops=flops, bytes_accessed=flops // 96, transcendentals=0),
        name=name,
    )(ids, *held)


def per_device(
    hidden_in, norm_gain, route_ids, route_gates, w_gate, w_up, w_down, context, w_out, grad_out
):
    n_dp, n_hi = lax.axis_size("dp"), lax.axis_size("hi")
    me, hi, y, c = (lax.axis_index(name) for name in ("dp", "hi", "y", "c"))
    rows, width = hidden_in.shape
    all_rows, units, chunk = n_dp * rows, w_gate.shape[2], width // 4
    ids = jnp.stack([me, y, c]).astype(jnp.int32)

    def swap(value, axes, turn):
        sizes = [lax.axis_size(name) for name in axes]
        count = 1
        for size in sizes:
            count *= size
        return lax.ppermute(value, axes, [(i, i ^ turn) for i in range(count)])

    def all_blocks(value):
        return [value] + [swap(value, ("dp",), k) for k in range(1, n_dp)]

    hid = all_blocks(hidden_in)
    expert = (hi * 2 + y) * 2 + c
    gate_own = jnp.sum(jnp.where(route_ids == expert, route_gates, 0.0), axis=1, keepdims=True)
    small = all_blocks(
        jnp.concatenate([context.astype(F32), jnp.broadcast_to(gate_own, (rows, 128))], axis=1)
    )
    contexts = [value[:, : context.shape[1]] for value in small]
    gates = [value[:, context.shape[1] :] for value in small]
    grads = all_blocks(grad_out)
    gain = norm_gain.reshape(1, width)
    wg, wu, wd = w_gate[0], w_up[0], w_down[0]
    product = 2 * all_rows * width * units
    shares = ((2, n_dp, rows, chunk), BF16)

    def plane_share(send, keep):
        half = keep + swap(send, ("c",), 1)
        total = half[0, 0].astype(F32)
        pieces = [swap(half[t % 2, t // 2], ("dp", "y"), t) for t in range(1, 2 * n_dp)]
        for piece in pieces:
            total = total + piece.astype(F32)
        return total.astype(BF16)

    def column_sum(value):
        pieces = [swap(value, ("hi",), t) for t in range(1, n_hi)]
        total = value.astype(F32)
        for piece in pieces:
            total = total + piece.astype(F32)
        return total.astype(BF16)

    pre_gate, pre_up, out_send, out_keep = run(
        forward_kernel, n_dp, ids, hid + gates + [gain, wg, wu, wd],
        [((all_rows, units), F32), ((all_rows, units), F32), shares, shares],
        [((all_rows, width), BF16), ((all_rows, units), BF16)], 3 * product, "forward",
    )
    out_share = plane_share(out_send, out_keep)
    grad_gate, grad_up, in_send = run(
        backward_kernel, n_dp, ids, grads + gates + [pre_gate, pre_up, wg, wu, wd],
        [((all_rows, units), BF16), ((all_rows, units), BF16), shares],
        [((all_rows, width), BF16)], 2 * product, "backward",
    )
    (in_keep,) = run(
        keep_kernel, n_dp, ids, [grad_gate, grad_up, wg, wu], [shares], [], product, "backward_keep"
    )
    out_total = column_sum(out_share)
    in_share = plane_share(in_send, in_keep)
    moe_own = jnp.stack([out_total, swap(out_total, ("y",), 1)])
    in_total = column_sum(in_share)
    moe_other = swap(moe_own, ("c",), 1)
    pieces = [in_total] + [swap(in_total, ("dp", "y"), t) for t in range(1, 2 * n_dp)]
    back_own = jnp.stack(pieces).reshape(n_dp, 2, rows, chunk)
    back_other = swap(back_own, ("c",), 1)
    heads = context.shape[1]
    return run(
        finish_kernel, n_dp, ids,
        hid + grads + contexts + [gain, w_out, back_own, back_other, moe_own, moe_other],
        [((rows, width), BF16), ((rows, width), BF16), ((rows, heads), BF16), ((heads, width // n_dp), BF16)],
        [((all_rows, width), F32), ((all_rows, width), BF16)], product // 4, "finish",
    )


def solution(mesh):
    n_dp, n_e = mesh.shape["dp"], mesh.shape["expert"]
    names = ("dp", "hi", "y", "c")
    mesh = jax.sharding.Mesh(mesh.devices.reshape(n_dp, n_e // 4, 2, 2), names)
    expert = names[1:]
    return jax.shard_map(
        per_device,
        mesh=mesh,
        in_specs=(
            P("dp", None),
            P(),
            P("dp", None),
            P("dp", None),
            P(expert, None, "dp"),
            P(expert, None, "dp"),
            P(expert, "dp", None),
            P("dp", expert),
            P(expert, None),
            P("dp", None),
        ),
        out_specs=(P("dp", None), P("dp", None), P("dp", expert), P(expert, "dp")),
        check_vma=False,
    )
```

time: 102 us -> 87.1 us (0.85)
  blocking collectives: 42.4 us -> 0 us
  local copies, waits for them, and re-layouts: 2.63 us -> 26.8 us
  Pallas kernels: 0 us -> 20 us
  matrix products: 17.2 us -> 0 us
  starting transfers between devices: 15.3 us -> 26.8 us
  waiting for transfers between devices: 17.1 us -> 9.81 us
  other arithmetic: 5.69 us -> 2.26 us
    all_gather x2 -> x0, blocking collectives: 42.4 us -> none  [reduce_all(): spread = lax.all_gather(total, 'expert', axis=0, tiled=False)]
    unnamed x22 -> x32, local copies, waits for them, and re-layouts: 0.23 us -> 26.7 us
    ppermute x5 -> x23, starting transfers between devices: 6.65 us -> 26.8 us  [swap(): return lax.ppermute(value, axes, [(i, i ^ turn) for i in range(count)])]
    pallas_call x0 -> x4, Pallas kernels: none -> 20 us  [run(): pl.pallas_call(functools.partial(kernel, n_dp), out_shape=[pltpu.VMEM(sha...]
    dot_general x8 -> x0, matrix products: 17.2 us -> none  [per_device(): lax.dot_general(a, b, (dims, ((), ())), preferred_element_type=F32)]
    all_to_all x2 -> x0, starting transfers between devices: 8.69 us -> none  [reduce_all(): arrived = lax.all_to_all(shares, ('dp', 'expert'), 0, 0, tiled=True)]
    all_to_all x2 -> x0, waiting for transfers between devices: 7.87 us -> none  [reduce_all(): arrived = lax.all_to_all(shares, ('dp', 'expert'), 0, 0, tiled=True)]
    reduce_sum x5 -> x0, other arithmetic: 2.33 us -> none  [the longest x1 1.78 us: per_device(): jnp.mean(hidden * hidden, axis=1, keepdims=True) + EPSILON]
  transfers between devices with their start and end apart: 7 -> 23, of which waited for: 3 -> 7; matrix products, arithmetic and copies ran while one was open for 23% -> 1% of each run, Pallas kernels for 0% -> 13%
where the time goes in v3:
time: 87.1 us; the launch traced here: 86.5 us
  local copies, waits for them, and re-layouts  26.8 us (31%)
  starting transfers between devices  26.8 us (31%)
  Pallas kernels  20 us (23%)
  waiting for transfers between devices  9.81 us (11%)
  other arithmetic  2.26 us (3%)
    ppermute x23, starting transfers between devices, swap(): return lax.ppermute(value, axes, [(i, i ^ turn) for i in range(count)])  26.8 us
    unnamed x32, local copies, waits for them, and re-layouts  26.7 us
    pallas_call x4, Pallas kernels, run(): pl.pallas_call(functools.partial(kernel, n_dp), out_shape=[pltpu.VMEM(sha...  20 us
    ppermute x23, waiting for transfers between devices, swap(): return lax.ppermute(value, axes, [(i, i ^ turn) for i in range(count)])  9.81 us
  transfers between devices with their start and end apart: 23, of which 7 were waited for; matrix products, arithmetic and copies ran while one was open for 1% of the time, Pallas kernels for 13%

profile of v3, /device:TPU:0, one launch (start us, length us, event | category | flops | bytes accessed | tf_op | source)
XLA Modules:
  0.0 86.5 jit_solution(6151940017617488129)
XLA Ops:
  0.6 0.7 convert_element_type.69.refs_4_
  1.3 0.7 select_reduce_fusion
  2.1 0.1 broadcast_in_dim.11.refs_2_
  2.1 2.9 %collective-permute-start.2 = (f32[24,256]{1,0:T(8,128)S(1)}, f32[24,256]{1,0:T(8,128)S(1)}, u32[]{:S(2)}, u32[]{:S(2)}) collective-permute-start(f32[24,256]{1,0:T(8,128)S(1)} %pad_maximum_fusion.2), channel_id=1, source_target_pairs={{0,16},{16,0},{1,17},{17,1},{2,18},{18,2},{3,19},{19,3},{4,20},{20... | collective-permute-start | bytes 73736 | tf_op jit(solution)/shard_map/ppermute | solution.py:207
  5.1 0.1 collective-permute-start
  5.2 1.9 %collective-permute-start.1 = (bf16[24,4096]{1,0:T(8,128)(2,1)}, bf16[24,4096]{1,0:T(8,128)(2,1)S(1)}, u32[]{:S(2)}, u32[]{:S(2)}) collective-permute-start(bf16[24,4096]{1,0:T(8,128)(2,1)} %refs_2_.1), channel_id=1, source_target_pairs={{0,16},{16,0},{1,17},{17,1},{2,18},{18,2},{3,19},{19,3},{4,20},{20... | collective-permute-start | bytes 589832 | tf_op jit(solution)/shard_map/ppermute | solution.py:207
  7.1 0.6 pad_add_fusion.ids
  7.7 5.4 %collective-permute-done.refs_1_ = bf16[24,4096]{1,0:T(8,128)(2,1)S(1)} collective-permute-done((bf16[24,4096]{1,0:T(8,128)(2,1)}, bf16[24,4096]{1,0:T(8,128)(2,1)S(1)}, u32[]{:S(2)}, u32[]{:S(2)}) %collective-permute-start) | collective-permute-done | bytes 196640 | tf_op jit(solution)/shard_map/ppermute | solution.py:207
  13.1 2.8 %copy-done = bf16[1,4096,768]{2,1,0:T(8,128)(2,1)S(1)} copy-done((bf16[1,4096,768]{2,1,0:T(8,128)(2,1)S(1)}, bf16[1,4096,768]{2,1,0:T(8,128)(2,1)}, u32[]{:S(2)}) %copy-start) | copy-done | bytes 6291480
  15.9 2.8 %copy-done.3 = bf16[1,4096,768]{2,1,0:T(8,128)(2,1)S(1)} copy-done((bf16[1,4096,768]{2,1,0:T(8,128)(2,1)S(1)}, bf16[1,4096,768]{2,1,0:T(8,128)(2,1)}, u32[]{:S(2)}) %copy-start.3) | copy-done | bytes 6291480
  18.7 2.8 %copy-done.6 = bf16[1,768,4096]{2,1,0:T(8,128)(2,1)S(1)} copy-done((bf16[1,768,4096]{2,1,0:T(8,128)(2,1)S(1)}, bf16[1,768,4096]{2,1,0:T(8,128)(2,1)}, u32[]{:S(2)}) %copy-start.6) | copy-done | bytes 6291480
  21.5 0.9 %copy-done.9 = bf16[24,4096]{1,0:T(8,128)(2,1)S(1)} copy-done((bf16[24,4096]{1,0:T(8,128)(2,1)S(1)}, bf16[24,4096]{1,0:T(8,128)(2,1)}, u32[]{:S(2)}) %copy-start.9) | copy-done | bytes 196632
  22.4 0.7 copy-done.12
  23.1 7.5 %forward.1 = (f32[48,768]{1,0:T(8,128)S(1)}, f32[48,768]{1,0:T(8,128)S(1)}, bf16[2,2,24,1024]{3,2,1,0:T(8,128)(2,1)S(1)}, bf16[2,2,24,1024]{3,2,1,0:T(8,128)(2,1)S(1)}) custom-call(s32[3]{0:T(128)} %pad_add_fusion.ids, bf16[24,4096]{1,0:T(8,128)(2,1)S(1)} %copy-done.9, bf16[24,4096]{1,0:T(8,128)(2,1)S(1)} %collective-permute-done.refs_1_, ...), custom_call_target="tpu_custom_call" | custom-call | flops 905969664 | bytes 9437184 | tf_op jit(solution)/shard_map/forward/pallas_call | solution.py:180
  30.7 2.8 %copy-done.1 = bf16[1,4096,768]{2,1,0:T(8,128)(2,1)S(1)} copy-done((bf16[1,4096,768]{2,1,0:T(8,128)(2,1)S(1)}, bf16[1,4096,768]{2,1,0:T(8,128)(2,1)}, u32[]{:S(2)}) %copy-start.1) | copy-done | bytes 6291480
  33.4 2.8 %copy-done.4 = bf16[1,4096,768]{2,1,0:T(8,128)(2,1)S(1)} copy-done((bf16[1,4096,768]{2,1,0:T(8,128)(2,1)S(1)}, bf16[1,4096,768]{2,1,0:T(8,128)(2,1)}, u32[]{:S(2)}) %copy-start.4) | copy-done | bytes 6291480
  36.2 2.8 %copy-done.7 = bf16[1,768,4096]{2,1,0:T(8,128)(2,1)S(1)} copy-done((bf16[1,768,4096]{2,1,0:T(8,128)(2,1)S(1)}, bf16[1,768,4096]{2,1,0:T(8,128)(2,1)}, u32[]{:S(2)}) %copy-start.7) | copy-done | bytes 6291480
  39.0 6.4 %backward.1 = (bf16[48,768]{1,0:T(8,128)(2,1)S(1)}, bf16[48,768]{1,0:T(8,128)(2,1)S(1)}, bf16[2,2,24,1024]{3,2,1,0:T(8,128)(2,1)S(1)}) custom-call(s32[3]{0:T(128)} %pad_add_fusion.ids, bf16[24,4096]{1,0:T(8,128)(2,1)S(1)} %copy-done.11, bf16[24,4096]{1,0:T(8,128)(2,1)S(1)} %collective-permute-done.1.refs_1_.refs_3_, ...), custom_call_target="tpu_custom_call" | custom-call | flops 603979776 | bytes 6291456 | tf_op jit(solution)/shard_map/backward/pallas_call | solution.py:180
  45.5 0.5 collective-permute-start.14
  46.0 2.8 %copy-done.2 = bf16[1,4096,768]{2,1,0:T(8,128)(2,1)S(1)} copy-done((bf16[1,4096,768]{2,1,0:T(8,128)(2,1)S(1)}, bf16[1,4096,768]{2,1,0:T(8,128)(2,1)}, u32[]{:S(2)}) %copy-start.2) | copy-done | bytes 6291480
  48.8 2.8 %copy-done.5 = bf16[1,4096,768]{2,1,0:T(8,128)(2,1)S(1)} copy-done((bf16[1,4096,768]{2,1,0:T(8,128)(2,1)S(1)}, bf16[1,4096,768]{2,1,0:T(8,128)(2,1)}, u32[]{:S(2)}) %copy-start.5) | copy-done | bytes 6291480
  51.6 3.4 %backward_keep.1 = bf16[2,2,24,1024]{3,2,1,0:T(8,128)(2,1)S(1)} custom-call(s32[3]{0:T(128)S(1)} %copy-done.13, bf16[48,768]{1,0:T(8,128)(2,1)S(1)} %get-tuple-element.13.grad_gate, bf16[48,768]{1,0:T(8,128)(2,1)S(1)} %get-tuple-element.14.grad_up, bf16[4096,768]{1,0:T(8,128)(2,1)S(1)} %bitcast.38, bf16[4096,768]{1,0:T(8,128)(2,1)S(1)} %bitcast.41), custom_call_target="tpu_custom_call" | custom-call | flops 301989888 | bytes 3145728 | tf_op jit(solution)/shard_map/backward_keep/pallas_call | solution.py:180
  55.1 1.6 %collective-permute-start.4 = (bf16[24,1024]{1,0:T(8,128)(2,1)S(1)}, bf16[24,1024]{1,0:T(8,128)(2,1)S(1)}, u32[]{:S(2)}, u32[]{:S(2)}) collective-permute-start(bf16[24,1024]{1,0:T(8,128)(2,1)S(1)} %get-tuple-element.21), channel_id=1, source_target_pairs={{0,2},{2,0},{16,18},{18,16},{1,3},{3,1},{17,19},{19,17},{4,6},{6,4... | collective-permute-start | bytes 147464 | tf_op jit(solution)/shard_map/ppermute | solution.py:207
  56.7 0.2 collective-permute-start.6
  56.8 1.8 %collective-permute-start.5 = (bf16[24,1024]{1,0:T(8,128)(2,1)S(1)}, bf16[24,1024]{1,0:T(8,128)(2,1)S(1)}, u32[]{:S(2)}, u32[]{:S(2)}) collective-permute-start(bf16[24,1024]{1,0:T(8,128)(2,1)S(1)} %get-tuple-element.23), channel_id=1, source_target_pairs={{0,16},{2,18},{16,0},{18,2},{1,17},{3,19},{17,1},{19,3},{4,20},{6,... | collective-permute-start | bytes 147464 | tf_op jit(solution)/shard_map/ppermute | solution.py:207
  58.7 1.6 %collective-permute-start.15 = (bf16[24,1024]{1,0:T(8,128)(2,1)S(1)}, bf16[24,1024]{1,0:T(8,128)(2,1)S(1)}, u32[]{:S(2)}, u32[]{:S(2)}) collective-permute-start(bf16[24,1024]{1,0:T(8,128)(2,1)S(1)} %get-tuple-element.18), channel_id=1, source_target_pairs={{0,2},{2,0},{16,18},{18,16},{1,3},{3,1},{17,19},{19,17},{4,6},{6,4... | collective-permute-start | bytes 147464 | tf_op jit(solution)/shard_map/ppermute | solution.py:207
  60.3 0.2 collective-permute-start.17
  60.5 1.8 %collective-permute-start.16 = (bf16[24,1024]{1,0:T(8,128)(2,1)S(1)}, bf16[24,1024]{1,0:T(8,128)(2,1)S(1)}, u32[]{:S(2)}, u32[]{:S(2)}) collective-permute-start(bf16[24,1024]{1,0:T(8,128)(2,1)S(1)} %get-tuple-element.20), channel_id=1, source_target_pairs={{0,16},{2,18},{16,0},{18,2},{1,17},{3,19},{17,1},{19,3},{4,20},{6,... | collective-permute-start | bytes 147464 | tf_op jit(solution)/shard_map/ppermute | solution.py:207
  62.3 3.7 %collective-permute-start.9 = (bf16[24,1024]{1,0:T(8,128)(2,1)S(1)}, bf16[24,1024]{1,0:T(8,128)(2,1)S(1)}, u32[]{:S(2)}, u32[]{:S(2)}) collective-permute-start(bf16[24,1024]{1,0:T(8,128)(2,1)S(1)} %fusion.5), channel_id=1, source_target_pairs={{0,12},{4,8},{8,4},{12,0},{1,13},{5,9},{9,5},{13,1},{2,14},{6,10},... | collective-permute-start | bytes 147464 | tf_op jit(solution)/shard_map/ppermute | solution.py:207
  66.0 0.8 collective-permute-start.7
  66.8 3.7 %collective-permute-start.20 = (bf16[24,1024]{1,0:T(8,128)(2,1)S(1)}, bf16[24,1024]{1,0:T(8,128)(2,1)S(1)}, u32[]{:S(2)}, u32[]{:S(2)}) collective-permute-start(bf16[24,1024]{1,0:T(8,128)(2,1)S(1)} %fusion.2), channel_id=1, source_target_pairs={{0,12},{4,8},{8,4},{12,0},{1,13},{5,9},{9,5},{13,1},{2,14},{6,10},... | collective-permute-start | bytes 147464 | tf_op jit(solution)/shard_map/ppermute | solution.py:207
  70.5 0.8 collective-permute-start.18
  71.2 0.4 collective-permute-done.8
  71.7 2.0 %collective-permute-start.12 = (bf16[24,1024]{1,0:T(8,128)(2,1)S(1)}, bf16[24,1024]{1,0:T(8,128)(2,1)S(1)}, u32[]{:S(2)}, u32[]{:S(2)}) collective-permute-start(bf16[24,1024]{1,0:T(8,128)(2,1)S(1)} %add_convert_fusion.1), channel_id=1, source_target_pairs={{0,18},{2,16},{16,2},{18,0},{1,19},{3,17},{17,3},{19,1},{4,22},{6,... | collective-permute-start | bytes 147464 | tf_op jit(solution)/shard_map/ppermute | solution.py:207
  73.7 1.0 %collective-permute-start.11 = (bf16[24,1024]{1,0:T(8,128)(2,1)S(1)}, bf16[24,1024]{1,0:T(8,128)(2,1)S(1)}, u32[]{:S(2)}, u32[]{:S(2)}) collective-permute-start(bf16[24,1024]{1,0:T(8,128)(2,1)S(1)} %add_convert_fusion.1), channel_id=1, source_target_pairs={{0,16},{2,18},{16,0},{18,2},{1,17},{3,19},{17,1},{19,3},{4,20},{6,... | collective-permute-start | bytes 147464 | tf_op jit(solution)/shard_map/ppermute | solution.py:207
  74.8 0.5 collective-permute-start.10
  75.3 0.2 collective-permute-done.19
  75.5 1.6 %collective-permute-start.21 = (bf16[24,1024]{1,0:T(8,128)(2,1)S(1)}, bf16[24,1024]{1,0:T(8,128)(2,1)S(1)}, u32[]{:S(2)}, u32[]{:S(2)}) collective-permute-start(bf16[24,1024]{1,0:T(8,128)(2,1)S(1)} %add_convert_fusion), channel_id=1, source_target_pairs={{0,2},{2,0},{1,3},{3,1},{4,6},{6,4},{5,7},{7,5},{8,10},{10,8},{9,1... | collective-permute-start | bytes 147464 | tf_op jit(solution)/shard_map/ppermute | solution.py:207
  77.1 0.7 collective-permute-done.11
  77.8 1.1 %collective-permute-done.10 = bf16[24,1024]{1,0:T(8,128)(2,1)S(1)} collective-permute-done((bf16[24,1024]{1,0:T(8,128)(2,1)S(1)}, bf16[24,1024]{1,0:T(8,128)(2,1)S(1)}, u32[]{:S(2)}, u32[]{:S(2)}) %collective-permute-start.10) | collective-permute-done | bytes 49184 | tf_op jit(solution)/shard_map/ppermute | solution.py:207
  79.0 0.7 collective-permute-done.21
  79.7 0.1 collective-permute-start.22
  79.7 1.3 %collective-permute-done.22.refs_11_ = bf16[2,24,1024]{2,1,0:T(8,128)(2,1)S(1)} collective-permute-done((bf16[2,24,1024]{2,1,0:T(8,128)(2,1)S(1)}, bf16[2,24,1024]{2,1,0:T(8,128)(2,1)S(1)}, u32[]{:S(2)}, u32[]{:S(2)}) %collective-permute-start.22) | collective-permute-done | bytes 98336 | tf_op jit(solution)/shard_map/ppermute | solution.py:207
  81.0 2.7 %finish.1 = (bf16[24,4096]{1,0:T(8,128)(2,1)S(1)}, bf16[24,4096]{1,0:T(8,128)(2,1)S(1)}, bf16[24,128]{1,0:T(8,128)(2,1)S(1)}, bf16[128,2048]{1,0:T(8,128)(2,1)S(1)}) custom-call(s32[3]{0:T(128)S(1)} %copy-done.13, bf16[24,4096]{1,0:T(8,128)(2,1)S(1)} %copy-done.10, bf16[24,4096]{1,0:T(8,128)(2,1)S(1)} %collective-permute-done.refs_1_, ...), custom_call_target="tpu_custom_call" | custom-call | flops 75497472 | bytes 786432 | tf_op jit(solution)/shard_map/finish/pallas_call | solution.py:180
  83.8 0.7 copy.14
  84.5 0.6 copy.16
  85.1 0.7 copy.15
  85.7 0.8 copy.17
  (50 shorter events, 0.5 us)
Async XLA Ops:
  2.1 5.6 %collective-permute-start.2 = (f32[24,256]{1,0:T(8,128)S(1)}, f32[24,256]{1,0:T(8,128)S(1)}, u32[]{:S(2)}, u32[]{:S(2)}) collective-permute-start(f32[24,256]{1,0:T(8,128)S(1)} %pad_maximum_fusion.2), channel_id=1, source_target_pairs={{0,16},{16,0},{1,17},{17,1},{2,18},{18,2},{3,19},{19,3},{4,20},{20... | collective-permute-start | bytes 73736 | tf_op jit(solution)/shard_map/ppermute | solution.py:207
  5.1 8.0 %collective-permute-start = (bf16[24,4096]{1,0:T(8,128)(2,1)}, bf16[24,4096]{1,0:T(8,128)(2,1)S(1)}, u32[]{:S(2)}, u32[]{:S(2)}) collective-permute-start(bf16[24,4096]{1,0:T(8,128)(2,1)} %refs_0_.5), channel_id=1, source_target_pairs={{0,16},{16,0},{1,17},{17,1},{2,18},{18,2},{3,19},{19,3},{4,20},{20... | collective-permute-start | bytes 589832 | tf_op jit(solution)/shard_map/ppermute | solution.py:207
  5.2 25.5 %collective-permute-start.1 = (bf16[24,4096]{1,0:T(8,128)(2,1)}, bf16[24,4096]{1,0:T(8,128)(2,1)S(1)}, u32[]{:S(2)}, u32[]{:S(2)}) collective-permute-start(bf16[24,4096]{1,0:T(8,128)(2,1)} %refs_2_.1), channel_id=1, source_target_pairs={{0,16},{16,0},{1,17},{17,1},{2,18},{18,2},{3,19},{19,3},{4,20},{20... | collective-permute-start | bytes 589832 | tf_op jit(solution)/shard_map/ppermute | solution.py:207
  13.1 2.8 %copy-start = (bf16[1,4096,768]{2,1,0:T(8,128)(2,1)S(1)}, bf16[1,4096,768]{2,1,0:T(8,128)(2,1)}, u32[]{:S(2)}) copy-start(bf16[1,4096,768]{2,1,0:T(8,128)(2,1)} %param.14) | copy-start | bytes 18874372
  15.9 2.8 %copy-start.3 = (bf16[1,4096,768]{2,1,0:T(8,128)(2,1)S(1)}, bf16[1,4096,768]{2,1,0:T(8,128)(2,1)}, u32[]{:S(2)}) copy-start(bf16[1,4096,768]{2,1,0:T(8,128)(2,1)} %param.15) | copy-start | bytes 18874372
  18.7 2.8 %copy-start.6 = (bf16[1,768,4096]{2,1,0:T(8,128)(2,1)S(1)}, bf16[1,768,4096]{2,1,0:T(8,128)(2,1)}, u32[]{:S(2)}) copy-start(bf16[1,768,4096]{2,1,0:T(8,128)(2,1)} %param.16) | copy-start | bytes 18874372
  21.5 0.9 %copy-start.9 = (bf16[24,4096]{1,0:T(8,128)(2,1)S(1)}, bf16[24,4096]{1,0:T(8,128)(2,1)}, u32[]{:S(2)}) copy-start(bf16[24,4096]{1,0:T(8,128)(2,1)} %refs_0_.5) | copy-start | bytes 589828
  22.4 0.7 copy-start.12
  23.1 7.5 %copy-start.11 = (bf16[24,4096]{1,0:T(8,128)(2,1)S(1)}, bf16[24,4096]{1,0:T(8,128)(2,1)}, u32[]{:S(2)}) copy-start(bf16[24,4096]{1,0:T(8,128)(2,1)} %refs_2_.1) | copy-start | bytes 589828
  30.6 2.8 %copy-start.1 = (bf16[1,4096,768]{2,1,0:T(8,128)(2,1)S(1)}, bf16[1,4096,768]{2,1,0:T(8,128)(2,1)}, u32[]{:S(2)}) copy-start(bf16[1,4096,768]{2,1,0:T(8,128)(2,1)} %param.14) | copy-start | bytes 18874372
  33.4 2.8 %copy-start.4 = (bf16[1,4096,768]{2,1,0:T(8,128)(2,1)S(1)}, bf16[1,4096,768]{2,1,0:T(8,128)(2,1)}, u32[]{:S(2)}) copy-start(bf16[1,4096,768]{2,1,0:T(8,128)(2,1)} %param.15) | copy-start | bytes 18874372
  36.2 2.8 %copy-start.7 = (bf16[1,768,4096]{2,1,0:T(8,128)(2,1)S(1)}, bf16[1,768,4096]{2,1,0:T(8,128)(2,1)}, u32[]{:S(2)}) copy-start(bf16[1,768,4096]{2,1,0:T(8,128)(2,1)} %param.16) | copy-start | bytes 18874372
  39.0 7.0 %copy-start.13 = (s32[3]{0:T(128)S(1)}, s32[3]{0:T(128)}, u32[]{:S(2)}) copy-start(s32[3]{0:T(128)} %pad_add_fusion.ids) | copy-start | bytes 40
  45.5 9.5 %collective-permute-start.3 = (bf16[2,2,24,1024]{3,2,1,0:T(8,128)(2,1)S(1)}, bf16[2,2,24,1024]{3,2,1,0:T(8,128)(2,1)S(1)}, u32[]{:S(2)}, u32[]{:S(2)}) collective-permute-start(bf16[2,2,24,1024]{3,2,1,0:T(8,128)(2,1)S(1)} %get-tuple-element.15), channel_id=1, source_target_pairs={{0,1},{1,0},{2,3},{3,2},{4,5},{5,4},{6,7},{7,6},{8,9},{9,8},{10,11... | collective-permute-start | bytes 589832 | tf_op jit(solution)/shard_map/ppermute | solution.py:207
  45.5 13.1 %collective-permute-start.14 = (bf16[2,2,24,1024]{3,2,1,0:T(8,128)(2,1)S(1)}, bf16[2,2,24,1024]{3,2,1,0:T(8,128)(2,1)S(1)}, u32[]{:S(2)}, u32[]{:S(2)}) collective-permute-start(bf16[2,2,24,1024]{3,2,1,0:T(8,128)(2,1)S(1)} %get-tuple-element.17), channel_id=1, source_target_pairs={{0,1},{1,0},{2,3},{3,2},{4,5},{5,4},{6,7},{7,6},{8,9},{9,8},{10,11... | collective-permute-start | bytes 589832 | tf_op jit(solution)/shard_map/ppermute | solution.py:207
  46.0 2.8 %copy-start.2 = (bf16[1,4096,768]{2,1,0:T(8,128)(2,1)S(1)}, bf16[1,4096,768]{2,1,0:T(8,128)(2,1)}, u32[]{:S(2)}) copy-start(bf16[1,4096,768]{2,1,0:T(8,128)(2,1)} %param.14) | copy-start | bytes 18874372
  48.8 2.8 %copy-start.5 = (bf16[1,4096,768]{2,1,0:T(8,128)(2,1)S(1)}, bf16[1,4096,768]{2,1,0:T(8,128)(2,1)}, u32[]{:S(2)}) copy-start(bf16[1,4096,768]{2,1,0:T(8,128)(2,1)} %param.15) | copy-start | bytes 18874372
  51.6 29.4 %copy-start.8 = (bf16[128,4096]{1,0:T(8,128)(2,1)S(1)}, bf16[128,4096]{1,0:T(8,128)(2,1)}, u32[]{:S(2)}) copy-start(bf16[128,4096]{1,0:T(8,128)(2,1)} %refs_7_.1) | copy-start | bytes 3145732
  51.6 29.4 %copy-start.10 = (bf16[24,4096]{1,0:T(8,128)(2,1)S(1)}, bf16[24,4096]{1,0:T(8,128)(2,1)}, u32[]{:S(2)}) copy-start(bf16[24,4096]{1,0:T(8,128)(2,1)} %refs_0_.5) | copy-start | bytes 589828
  55.1 5.4 %collective-permute-start.4 = (bf16[24,1024]{1,0:T(8,128)(2,1)S(1)}, bf16[24,1024]{1,0:T(8,128)(2,1)S(1)}, u32[]{:S(2)}, u32[]{:S(2)}) collective-permute-start(bf16[24,1024]{1,0:T(8,128)(2,1)S(1)} %get-tuple-element.21), channel_id=1, source_target_pairs={{0,2},{2,0},{16,18},{18,16},{1,3},{3,1},{17,19},{19,17},{4,6},{6,4... | collective-permute-start | bytes 147464 | tf_op jit(solution)/shard_map/ppermute | solution.py:207
  56.7 5.6 %collective-permute-start.6 = (bf16[24,1024]{1,0:T(8,128)(2,1)S(1)}, bf16[24,1024]{1,0:T(8,128)(2,1)S(1)}, u32[]{:S(2)}, u32[]{:S(2)}) collective-permute-start(bf16[24,1024]{1,0:T(8,128)(2,1)S(1)} %get-tuple-element.22), channel_id=1, source_target_pairs={{0,18},{2,16},{16,2},{18,0},{1,19},{3,17},{17,3},{19,1},{4,22},{6,... | collective-permute-start | bytes 147464 | tf_op jit(solution)/shard_map/ppermute | solution.py:207
  56.8 5.4 %collective-permute-start.5 = (bf16[24,1024]{1,0:T(8,128)(2,1)S(1)}, bf16[24,1024]{1,0:T(8,128)(2,1)S(1)}, u32[]{:S(2)}, u32[]{:S(2)}) collective-permute-start(bf16[24,1024]{1,0:T(8,128)(2,1)S(1)} %get-tuple-element.23), channel_id=1, source_target_pairs={{0,16},{2,18},{16,0},{18,2},{1,17},{3,19},{17,1},{19,3},{4,20},{6,... | collective-permute-start | bytes 147464 | tf_op jit(solution)/shard_map/ppermute | solution.py:207
  58.7 7.3 %collective-permute-start.15 = (bf16[24,1024]{1,0:T(8,128)(2,1)S(1)}, bf16[24,1024]{1,0:T(8,128)(2,1)S(1)}, u32[]{:S(2)}, u32[]{:S(2)}) collective-permute-start(bf16[24,1024]{1,0:T(8,128)(2,1)S(1)} %get-tuple-element.18), channel_id=1, source_target_pairs={{0,2},{2,0},{16,18},{18,16},{1,3},{3,1},{17,19},{19,17},{4,6},{6,4... | collective-permute-start | bytes 147464 | tf_op jit(solution)/shard_map/ppermute | solution.py:207
  60.3 6.5 %collective-permute-start.17 = (bf16[24,1024]{1,0:T(8,128)(2,1)S(1)}, bf16[24,1024]{1,0:T(8,128)(2,1)S(1)}, u32[]{:S(2)}, u32[]{:S(2)}) collective-permute-start(bf16[24,1024]{1,0:T(8,128)(2,1)S(1)} %get-tuple-element.19), channel_id=1, source_target_pairs={{0,18},{2,16},{16,2},{18,0},{1,19},{3,17},{17,3},{19,1},{4,22},{6,... | collective-permute-start | bytes 147464 | tf_op jit(solution)/shard_map/ppermute | solution.py:207
  60.5 6.3 %collective-permute-start.16 = (bf16[24,1024]{1,0:T(8,128)(2,1)S(1)}, bf16[24,1024]{1,0:T(8,128)(2,1)S(1)}, u32[]{:S(2)}, u32[]{:S(2)}) collective-permute-start(bf16[24,1024]{1,0:T(8,128)(2,1)S(1)} %get-tuple-element.20), channel_id=1, source_target_pairs={{0,16},{2,18},{16,0},{18,2},{1,17},{3,19},{17,1},{19,3},{4,20},{6,... | collective-permute-start | bytes 147464 | tf_op jit(solution)/shard_map/ppermute | solution.py:207
  62.3 8.2 %collective-permute-start.9 = (bf16[24,1024]{1,0:T(8,128)(2,1)S(1)}, bf16[24,1024]{1,0:T(8,128)(2,1)S(1)}, u32[]{:S(2)}, u32[]{:S(2)}) collective-permute-start(bf16[24,1024]{1,0:T(8,128)(2,1)S(1)} %fusion.5), channel_id=1, source_target_pairs={{0,12},{4,8},{8,4},{12,0},{1,13},{5,9},{9,5},{13,1},{2,14},{6,10},... | collective-permute-start | bytes 147464 | tf_op jit(solution)/shard_map/ppermute | solution.py:207
  66.0 5.7 %collective-permute-start.8 = (bf16[24,1024]{1,0:T(8,128)(2,1)S(1)}, bf16[24,1024]{1,0:T(8,128)(2,1)S(1)}, u32[]{:S(2)}, u32[]{:S(2)}) collective-permute-start(bf16[24,1024]{1,0:T(8,128)(2,1)S(1)} %fusion.5), channel_id=1, source_target_pairs={{0,8},{4,12},{8,0},{12,4},{1,9},{5,13},{9,1},{13,5},{2,10},{6,14},... | collective-permute-start | bytes 147464 | tf_op jit(solution)/shard_map/ppermute | solution.py:207
  66.0 5.7 %collective-permute-start.7 = (bf16[24,1024]{1,0:T(8,128)(2,1)S(1)}, bf16[24,1024]{1,0:T(8,128)(2,1)S(1)}, u32[]{:S(2)}, u32[]{:S(2)}) collective-permute-start(bf16[24,1024]{1,0:T(8,128)(2,1)S(1)} %fusion.5), channel_id=1, source_target_pairs={{0,4},{4,0},{8,12},{12,8},{1,5},{5,1},{9,13},{13,9},{2,6},{6,2},{1... | collective-permute-start | bytes 147464 | tf_op jit(solution)/shard_map/ppermute | solution.py:207
  66.8 8.0 %collective-permute-start.20 = (bf16[24,1024]{1,0:T(8,128)(2,1)S(1)}, bf16[24,1024]{1,0:T(8,128)(2,1)S(1)}, u32[]{:S(2)}, u32[]{:S(2)}) collective-permute-start(bf16[24,1024]{1,0:T(8,128)(2,1)S(1)} %fusion.2), channel_id=1, source_target_pairs={{0,12},{4,8},{8,4},{12,0},{1,13},{5,9},{9,5},{13,1},{2,14},{6,10},... | collective-permute-start | bytes 147464 | tf_op jit(solution)/shard_map/ppermute | solution.py:207
  70.5 5.0 %collective-permute-start.19 = (bf16[24,1024]{1,0:T(8,128)(2,1)S(1)}, bf16[24,1024]{1,0:T(8,128)(2,1)S(1)}, u32[]{:S(2)}, u32[]{:S(2)}) collective-permute-start(bf16[24,1024]{1,0:T(8,128)(2,1)S(1)} %fusion.2), channel_id=1, source_target_pairs={{0,8},{4,12},{8,0},{12,4},{1,9},{5,13},{9,1},{13,5},{2,10},{6,14},... | collective-permute-start | bytes 147464 | tf_op jit(solution)/shard_map/ppermute | solution.py:207
  70.5 5.0 %collective-permute-start.18 = (bf16[24,1024]{1,0:T(8,128)(2,1)S(1)}, bf16[24,1024]{1,0:T(8,128)(2,1)S(1)}, u32[]{:S(2)}, u32[]{:S(2)}) collective-permute-start(bf16[24,1024]{1,0:T(8,128)(2,1)S(1)} %fusion.2), channel_id=1, source_target_pairs={{0,4},{4,0},{8,12},{12,8},{1,5},{5,1},{9,13},{13,9},{2,6},{6,2},{1... | collective-permute-start | bytes 147464 | tf_op jit(solution)/shard_map/ppermute | solution.py:207
  71.7 5.4 %collective-permute-start.12 = (bf16[24,1024]{1,0:T(8,128)(2,1)S(1)}, bf16[24,1024]{1,0:T(8,128)(2,1)S(1)}, u32[]{:S(2)}, u32[]{:S(2)}) collective-permute-start(bf16[24,1024]{1,0:T(8,128)(2,1)S(1)} %add_convert_fusion.1), channel_id=1, source_target_pairs={{0,18},{2,16},{16,2},{18,0},{1,19},{3,17},{17,3},{19,1},{4,22},{6,... | collective-permute-start | bytes 147464 | tf_op jit(solution)/shard_map/ppermute | solution.py:207
  73.7 4.1 %collective-permute-start.11 = (bf16[24,1024]{1,0:T(8,128)(2,1)S(1)}, bf16[24,1024]{1,0:T(8,128)(2,1)S(1)}, u32[]{:S(2)}, u32[]{:S(2)}) collective-permute-start(bf16[24,1024]{1,0:T(8,128)(2,1)S(1)} %add_convert_fusion.1), channel_id=1, source_target_pairs={{0,16},{2,18},{16,0},{18,2},{1,17},{3,19},{17,1},{19,3},{4,20},{6,... | collective-permute-start | bytes 147464 | tf_op jit(solution)/shard_map/ppermute | solution.py:207
  74.8 4.1 %collective-permute-start.10 = (bf16[24,1024]{1,0:T(8,128)(2,1)S(1)}, bf16[24,1024]{1,0:T(8,128)(2,1)S(1)}, u32[]{:S(2)}, u32[]{:S(2)}) collective-permute-start(bf16[24,1024]{1,0:T(8,128)(2,1)S(1)} %add_convert_fusion.1), channel_id=1, source_target_pairs={{0,2},{2,0},{16,18},{18,16},{1,3},{3,1},{17,19},{19,17},{4,6},{6,4... | collective-permute-start | bytes 147464 | tf_op jit(solution)/shard_map/ppermute | solution.py:207
  75.5 4.2 %collective-permute-start.21 = (bf16[24,1024]{1,0:T(8,128)(2,1)S(1)}, bf16[24,1024]{1,0:T(8,128)(2,1)S(1)}, u32[]{:S(2)}, u32[]{:S(2)}) collective-permute-start(bf16[24,1024]{1,0:T(8,128)(2,1)S(1)} %add_convert_fusion), channel_id=1, source_target_pairs={{0,2},{2,0},{1,3},{3,1},{4,6},{6,4},{5,7},{7,5},{8,10},{10,8},{9,1... | collective-permute-start | bytes 147464 | tf_op jit(solution)/shard_map/ppermute | solution.py:207
  78.9 2.1 %collective-permute-start.13 = (bf16[2,2,24,1024]{3,2,1,0:T(8,128)(2,1)S(1)}, bf16[2,2,24,1024]{3,2,1,0:T(8,128)(2,1)S(1)}, u32[]{:S(2)}, u32[]{:S(2)}) collective-permute-start(bf16[2,2,24,1024]{3,2,1,0:T(8,128)(2,1)S(1)} %bitcast.44), channel_id=1, source_target_pairs={{0,1},{1,0},{2,3},{3,2},{4,5},{5,4},{6,7},{7,6},{8,9},{9,8},{10,11... | collective-permute-start | bytes 589832 | tf_op jit(solution)/shard_map/ppermute | solution.py:207
  79.7 1.4 %collective-permute-start.22 = (bf16[2,24,1024]{2,1,0:T(8,128)(2,1)S(1)}, bf16[2,24,1024]{2,1,0:T(8,128)(2,1)S(1)}, u32[]{:S(2)}, u32[]{:S(2)}) collective-permute-start(bf16[2,24,1024]{2,1,0:T(8,128)(2,1)S(1)} %pad_maximum_fusion.1.refs_10_), channel_id=1, source_target_pairs={{0,1},{1,0},{2,3},{3,2},{4,5},{5,4},{6,7},{7,6},{8,9},{9,8},{10,11... | collective-permute-start | bytes 294920 | tf_op jit(solution)/shard_map/ppermute | solution.py:207

commit v4 on v3

v4 whole, which is shorter than its diff:
```python
import functools

import jax
import jax.numpy as jnp
from jax import lax
from jax.experimental import pallas as pl
from jax.experimental.pallas import tpu as pltpu
from jax.sharding import PartitionSpec as P

EPSILON = 1e-06
F32 = jnp.float32
BF16 = jnp.bfloat16
STEP = 256
LANES = 128
LOAD_PIECES = 4
FEW_ROWS = 64
VMEM_LIMIT = 12 * 1024 * 1024


def dot(a, b, dims):
    return lax.dot_general(a, b, (dims, ((), ())), preferred_element_type=F32)


def place(step, count):
    return pl.multiple_of(step * count, count)


def rows_of(refs, columns):
    return jnp.concatenate([ref[:, columns].astype(F32) for ref in refs], axis=0)


def own_columns(ids, i, j, width):
    return ((ids[1] ^ j) * 2 + (ids[2] ^ i)) * width


def store_blocks(out_ref, j, columns, value, count):
    rows = value.shape[0] // count
    for k in range(count):
        out_ref[j, k, :, columns] = value[k * rows : (k + 1) * rows].astype(BF16)


def load_kernel(n_dp, ids, w_gate, w_up, hid, grads, gain, named, weights, context, *refs):
    sources = (w_gate, w_up, hid, grads, gain)
    targets, small, named_held, weights_held, context_held, sems = (
        refs[:5], refs[5], refs[6], refs[7], refs[8], refs[9]
    )
    small_copies = [
        pltpu.make_async_copy(source, target, sems.at[n])
        for n, (source, target) in enumerate(
            ((named, named_held), (weights, weights_held), (context, context_held))
        )
    ]
    for copy in small_copies:
        copy.start()
    copies = []
    for source, target in zip(sources, targets):
        pieces = LOAD_PIECES if source.shape[0] % (LOAD_PIECES * 16) == 0 else 1
        part = source.shape[0] // pieces
        for p in range(pieces):
            block = pl.ds(p * part, part)
            where = (source.at[block], target.at[block]) if pieces > 1 else (source, target)
            copies.append(pltpu.make_async_copy(*where, sems.at[len(copies) + 3]))
    for copy in copies:
        copy.start()
    for copy in small_copies:
        copy.wait()
    rows = context_held.shape[0]
    row = jnp.sum(jnp.where(named_held[...] == ids[3], weights_held[...], 0.0), axis=0, keepdims=True)
    square = (rows, rows)
    diagonal = lax.broadcasted_iota(jnp.int32, square, 0) == lax.broadcasted_iota(jnp.int32, square, 1)
    gate = jnp.sum(jnp.where(diagonal, row, 0.0), axis=1, keepdims=True)
    heads = context_held.shape[1]
    small[:, :heads] = context_held[...].astype(F32)
    small[:, heads:] = jnp.broadcast_to(gate, (rows, LANES))
    for copy in copies:
        copy.wait()


def loop(count, body, unroll):
    if unroll:
        for step in range(count):
            body(step)
    else:
        def carried(step, carry):
            body(step)
            return carry

        lax.fori_loop(0, count, carried, 0)


def gates_of(smalls):
    return jnp.concatenate([small[:, small.shape[1] - LANES : small.shape[1] - LANES + 1] for small in smalls], axis=0)


def hidden_kernel(n_dp, ids, *refs):
    hid = refs[:n_dp]
    gain, w_gate, w_up, down_source, pre_gate, pre_up, act, w_down, normed, sem = refs[n_dp:]
    down_copy = pltpu.make_async_copy(down_source, w_down, sem)
    down_copy.start()
    total = hid[0].shape[0] * n_dp
    width = hid[0].shape[1]
    few = total <= FEW_ROWS
    sums = jnp.zeros((total, 1), F32)
    for step in range(width // 512):
        value = rows_of(hid, pl.ds(step * 512, 512))
        sums = sums + jnp.sum(value * value, axis=1, keepdims=True)
    scale = lax.rsqrt(sums / width + EPSILON)

    def norm(step):
        columns = pl.ds(place(step, 512), 512)
        normed[:, columns] = (rows_of(hid, columns) * scale * gain[:, columns]).astype(BF16)

    loop(width // 512, norm, few)

    def hidden_units(step):
        columns = pl.ds(place(step, STEP), STEP)
        gate_part = dot(normed[...], w_gate[:, columns], ((1,), (0,)))
        up_part = dot(normed[...], w_up[:, columns], ((1,), (0,)))
        pre_gate[:, columns] = gate_part
        pre_up[:, columns] = up_part
        act[:, columns] = (gate_part * jax.nn.sigmoid(gate_part) * up_part).astype(BF16)

    loop(w_gate.shape[1] // STEP, hidden_units, few)
    down_copy.wait()


def outward_kernel(n_dp, ids, *refs):
    smalls = refs[:n_dp]
    act, w_down, send, keep = refs[n_dp:]
    weight = gates_of(smalls)
    chunk = send.shape[3]
    few = act.shape[0] <= FEW_ROWS
    for i, target in ((1, send), (0, keep)):
        for j in range(2):
            first = own_columns(ids, i, j, chunk)

            def outward(step):
                columns = pl.ds(pl.multiple_of(first + step * STEP, STEP), STEP)
                part = weight * dot(act[...], w_down[:, columns], ((1,), (0,)))
                store_blocks(target, j, pl.ds(place(step, STEP), STEP), part, n_dp)

            loop(chunk // STEP, outward, few)


def inward_part(ids, i, n_dp, grad_gate, grad_up, w_gate, w_up, target):
    chunk = target.shape[3]
    few = grad_gate.shape[0] <= FEW_ROWS
    for j in range(2):
        first = own_columns(ids, i, j, chunk)

        def inward(step):
            columns = pl.ds(pl.multiple_of(first + step * STEP, STEP), STEP)
            part = dot(grad_gate[...], w_gate[columns, :], ((1,), (1,)))
            part = part + dot(grad_up[...], w_up[columns, :], ((1,), (1,)))
            store_blocks(target, j, pl.ds(place(step, STEP), STEP), part, n_dp)

        loop(chunk // STEP, inward, few)


def backward_kernel(n_dp, ids, *refs):
    grads, smalls = refs[:n_dp], refs[n_dp : 2 * n_dp]
    pre_gate, pre_up, w_gate, w_up, w_down, grad_gate, grad_up, send, weighted = refs[2 * n_dp :]
    weight = gates_of(smalls)
    few = weighted.shape[0] <= FEW_ROWS

    def weigh(step):
        columns = pl.ds(place(step, 512), 512)
        weighted[:, columns] = (weight * rows_of(grads, columns)).astype(BF16)

    loop(weighted.shape[1] // 512, weigh, few)

    def hidden_units(step):
        columns = pl.ds(place(step, STEP), STEP)
        back = dot(weighted[...], w_down[columns, :], ((1,), (1,)))
        gate_part, up_part = pre_gate[:, columns], pre_up[:, columns]
        sig = jax.nn.sigmoid(gate_part)
        grad_gate[:, columns] = (back * up_part * sig * (1.0 + gate_part * (1.0 - sig))).astype(BF16)
        grad_up[:, columns] = (back * gate_part * sig).astype(BF16)

    loop(w_down.shape[0] // STEP, hidden_units, few)
    inward_part(ids, 1, n_dp, grad_gate, grad_up, w_gate, w_up, send)


def keep_kernel(n_dp, ids, grad_gate, grad_up, w_gate, w_up, keep):
    inward_part(ids, 0, n_dp, grad_gate, grad_up, w_gate, w_up, keep)


def finish_kernel(n_dp, ids, *refs):
    hid, grads, smalls = refs[:n_dp], refs[n_dp : 2 * n_dp], refs[2 * n_dp : 3 * n_dp]
    gain, w_out, back_own, back_other, moe_own, moe_other = refs[3 * n_dp : 3 * n_dp + 6]
    output, d_hidden, d_context, d_w_out, summed, d_all = refs[3 * n_dp + 6 :]
    rows, width = hid[0].shape
    chunk = back_own.shape[3]
    for i, (back, moe) in enumerate(((back_own, moe_own), (back_other, moe_other))):
        for j in range(2):
            columns = pl.ds(pl.multiple_of(own_columns(ids, i, j, chunk), chunk), chunk)
            for k in range(n_dp):
                summed[k * rows : (k + 1) * rows, columns] = back[k, j].astype(F32) * gain[:, columns]
            output[:, columns] = (hid[0][:, columns].astype(F32) + moe[j].astype(F32)).astype(BF16)

    few = rows * n_dp <= FEW_ROWS
    squares = jnp.zeros((rows * n_dp, 1), F32)
    products = squares
    for step in range(width // 512):
        columns = pl.ds(step * 512, 512)
        value = rows_of(hid, columns)
        squares = squares + jnp.sum(value * value, axis=1, keepdims=True)
        products = products + jnp.sum(value * summed[:, columns], axis=1, keepdims=True)
    scale = lax.rsqrt(squares / width + EPSILON)
    centre = scale * products / width

    def total(step):
        columns = pl.ds(place(step, 512), 512)
        unit_rows = rows_of(hid, columns) * scale
        value = rows_of(grads, columns) + scale * (summed[:, columns] - unit_rows * centre)
        d_all[:, columns] = value.astype(BF16)
        d_hidden[:, columns] = value[:rows].astype(BF16)

    loop(width // 512, total, few)
    d_context[...] = dot(d_hidden[...], w_out[...], ((1,), (1,))).astype(BF16)
    part = width // n_dp
    heads = d_context.shape[1]
    turned = jnp.concatenate([small[:, :heads] for small in smalls], axis=0).T.astype(BF16)
    step_width = min(part, 512)

    def product(step):
        columns = pl.ds(pl.multiple_of(ids[0] * part + step * step_width, step_width), step_width)
        d_w_out[:, pl.ds(place(step, step_width), step_width)] = dot(
            turned, d_all[:, columns], ((1,), (0,))
        ).astype(BF16)

    loop(part // step_width, product, few)


def run(kernel, n_dp, ids, operands, outs, scratch, cost, name, far=(), out_space=pltpu.VMEM):
    spaces = [pltpu.HBM if n in far else pltpu.VMEM for n in range(len(operands))]
    held = [pltpu.with_memory_space_constraint(value, space) for value, space in zip(operands, spaces)]
    kinds = [
        pltpu.VMEM(shape, kind) if out_space is pltpu.VMEM else jax.ShapeDtypeStruct(shape, kind)
        for shape, kind in outs
    ]
    return pl.pallas_call(
        functools.partial(kernel, n_dp),
        out_shape=kinds,
        in_specs=[pl.BlockSpec(memory_space=pltpu.SMEM)]
        + [pl.BlockSpec(memory_space=space) for space in spaces],
        out_specs=[pl.BlockSpec(memory_space=pltpu.VMEM)] * len(outs),
        scratch_shapes=scratch,
        compiler_params=pltpu.CompilerParams(vmem_limit_bytes=VMEM_LIMIT),
        cost_estimate=pl.CostEstimate(flops=0, bytes_accessed=cost, transcendentals=0),
        name=name,
    )(ids, *held)


def per_device(
    hidden_in, norm_gain, route_ids, route_gates, w_gate, w_up, w_down, context, w_out, grad_out
):
    n_dp, n_hi = lax.axis_size("dp"), lax.axis_size("hi")
    me, hi, y, c = (lax.axis_index(name) for name in ("dp", "hi", "y", "c"))
    rows, width = hidden_in.shape
    top, heads = route_ids.shape[1], context.shape[1]
    all_rows, units, chunk = n_dp * rows, w_gate.shape[2], width // 4
    expert = (hi * 2 + y) * 2 + c
    ids = jnp.stack([me, y, c, expert]).astype(jnp.int32)

    def swap(value, axes, turn):
        sizes = [lax.axis_size(name) for name in axes]
        count = 1
        for size in sizes:
            count *= size
        return lax.ppermute(value, axes, [(i, i ^ turn) for i in range(count)])

    def all_blocks(value, own=None):
        own = value if own is None else own
        return [own] + [swap(value, ("dp",), k) for k in range(1, n_dp)]

    weights = 2 * width * units
    shares = ((2, n_dp, rows, chunk), BF16)
    wg, wu, hid_own, grads_own, gain, small_own = run(
        load_kernel, n_dp, ids,
        [w_gate[0], w_up[0], hidden_in, grad_out, norm_gain.reshape(1, width), route_ids.T, route_gates.T, context],
        [((width, units), BF16), ((width, units), BF16), ((rows, width), BF16), ((rows, width), BF16),
         ((1, width), F32), ((rows, heads + LANES), F32)],
        [pltpu.VMEM((top, rows), jnp.int32), pltpu.VMEM((top, rows), F32), pltpu.VMEM((rows, heads), BF16),
         pltpu.SemaphoreType.DMA((2 * LOAD_PIECES + 6,))],
        2 * weights, "load", far=range(8),
    )
    hid = all_blocks(hidden_in, hid_own)
    smalls = all_blocks(small_own)
    grads = all_blocks(grad_out, grads_own)

    def plane_halves(send, keep):
        return keep + swap(send, ("c",), 1)

    def plane_share(halves):
        totals = [half[0, 0].astype(F32) for half in halves]
        for t in range(1, 2 * n_dp):
            piece = swap(jnp.stack([half[t % 2, t // 2] for half in halves]), ("dp", "y"), t)
            totals = [total + piece[n].astype(F32) for n, total in enumerate(totals)]
        return [total.astype(BF16) for total in totals]

    def column_sum(value):
        pieces = [swap(value, ("hi",), t) for t in range(1, n_hi)]
        total = value.astype(F32)
        for piece in pieces:
            total = total + piece.astype(F32)
        return total.astype(BF16)

    pre_gate, pre_up, act, wd = run(
        hidden_kernel, n_dp, ids, hid + [gain, wg, wu, w_down[0]],
        [((all_rows, units), F32), ((all_rows, units), F32), ((all_rows, units), BF16), ((units, width), BF16)],
        [pltpu.VMEM((all_rows, width), BF16), pltpu.SemaphoreType.DMA], 2 * weights, "hidden", far=(n_dp + 3,),
    )
    out_send, out_keep = run(
        outward_kernel, n_dp, ids, smalls + [act, wd], [shares, shares], [], weights, "outward"
    )
    out_half = plane_halves(out_send, out_keep)
    grad_gate, grad_up, in_send = run(
        backward_kernel, n_dp, ids, grads + smalls + [pre_gate, pre_up, wg, wu, wd],
        [((all_rows, units), BF16), ((all_rows, units), BF16), shares],
        [pltpu.VMEM((all_rows, width), BF16)], 2 * weights, "backward",
    )
    (in_keep,) = run(
        keep_kernel, n_dp, ids, [grad_gate, grad_up, wg, wu], [shares], [], weights, "backward_keep"
    )
    in_half = plane_halves(in_send, in_keep)
    in_share, out_share = plane_share([in_half, out_half])
    in_total, out_total = column_sum(in_share), column_sum(out_share)
    pieces = [in_total] + [swap(in_total, ("dp", "y"), t) for t in range(1, 2 * n_dp)]
    back_own = jnp.stack(pieces).reshape(n_dp, 2, rows, chunk)
    back_other = swap(back_own, ("c",), 1)
    moe_own = jnp.stack([out_total, swap(out_total, ("y",), 1)])
    moe_other = swap(moe_own, ("c",), 1)
    return run(
        finish_kernel, n_dp, ids,
        hid + grads + smalls + [gain, w_out, back_own, back_other, moe_own, moe_other],
        [((rows, width), BF16), ((rows, width), BF16), ((rows, heads), BF16), ((heads, width // n_dp), BF16)],
        [pltpu.VMEM((all_rows, width), F32), pltpu.VMEM((all_rows, width), BF16)],
        weights, "finish", out_space=None,
    )


def solution(mesh):
    n_dp, n_e = mesh.shape["dp"], mesh.shape["expert"]
    names = ("dp", "hi", "y", "c")
    mesh = jax.sharding.Mesh(mesh.devices.reshape(n_dp, n_e // 4, 2, 2), names)
    expert = names[1:]
    return jax.shard_map(
        per_device,
        mesh=mesh,
        in_specs=(
            P("dp", None),
            P(),
            P("dp", None),
            P("dp", None),
            P(expert, None, "dp"),
            P(expert, None, "dp"),
            P(expert, "dp", None),
            P("dp", expert),
            P(expert, None),
            P("dp", None),
        ),
        out_specs=(P("dp", None), P("dp", None), P("dp", expert), P(expert, "dp")),
        check_vma=False,
    )
```

time: 87.1 us -> 55.5 us (0.64)
  local copies, waits for them, and re-layouts: 26.8 us -> 0.03 us
  starting transfers between devices: 26.8 us -> 24.5 us
  other arithmetic: 2.26 us -> 0.36 us
    unnamed x32 -> x2, local copies, waits for them, and re-layouts: 26.7 us -> 0.01 us
    ppermute x23 -> x20, starting transfers between devices: 26.8 us -> 24.5 us  [swap(): return lax.ppermute(value, axes, [(i, i ^ turn) for i in range(count)])]
    ppermute x23 -> x20, waiting for transfers between devices: 9.81 us -> 9.47 us  [swap(): return lax.ppermute(value, axes, [(i, i ^ turn) for i in range(count)])]
    pallas_call x4 -> x6, Pallas kernels: 20 us -> 20.1 us  [run(): pl.pallas_call(functools.partial(kernel, n_dp), out_shape=kinds, in_specs...]
  transfers between devices with their start and end apart: 23 -> 20, of which waited for: 7 -> 8; matrix products, arithmetic and copies ran while one was open for 1% -> 0% of each run, Pallas kernels for 13% -> 23%
where the time goes in v4:
time: 55.5 us; the launch traced here: 55.3 us
  starting transfers between devices  24.5 us (44%)
  Pallas kernels  20.1 us (36%)
  waiting for transfers between devices  9.47 us (17%)
  between operations  0.81 us (1%)
    ppermute x20, starting transfers between devices, swap(): return lax.ppermute(value, axes, [(i, i ^ turn) for i in range(count)])  24.5 us
    pallas_call x6, Pallas kernels, run(): pl.pallas_call(functools.partial(kernel, n_dp), out_shape=kinds, in_specs...  20.1 us
    ppermute x20, waiting for transfers between devices, swap(): return lax.ppermute(value, axes, [(i, i ^ turn) for i in range(count)])  9.47 us
  transfers between devices with their start and end apart: 20, of which 8 were waited for; matrix products, arithmetic and copies ran while one was open for 0% of the time, Pallas kernels for 23%

profile of v4, /device:TPU:0, one launch (start us, length us, event | category | flops | bytes accessed | tf_op | source)
XLA Modules:
  0.0 55.3 jit_solution(1467204535762611771)
XLA Ops:
  0.6 3.0 %collective-permute-start = (bf16[24,4096]{1,0:T(8,128)(2,1)}, bf16[24,4096]{1,0:T(8,128)(2,1)S(1)}, u32[]{:S(2)}, u32[]{:S(2)}) collective-permute-start(bf16[24,4096]{1,0:T(8,128)(2,1)} %hid.1), channel_id=1, source_target_pairs={{0,16},{16,0},{1,17},{17,1},{2,18},{18,2},{3,19},{19,3},{4,20},{20... | collective-permute-start | bytes 589832 | tf_op jit(solution)/shard_map/ppermute | solution.py:271
  3.6 0.1 collective-permute-start.1
  3.7 0.1 pad_add_fusion.ids
  3.8 5.4 %load.1 = (bf16[4096,768]{1,0:T(8,128)(2,1)S(1)}, bf16[4096,768]{1,0:T(8,128)(2,1)S(1)}, bf16[24,4096]{1,0:T(8,128)(2,1)S(1)}, bf16[24,4096]{1,0:T(8,128)(2,1)S(...) custom-call(s32[4]{0:T(128)S(1)} %pad_add_fusion.ids, bf16[4096,768]{1,0:T(8,128)(2,1)} %bitcast.71, ...), custom_call_target="tpu_custom_call" | custom-call | bytes 12582912 | tf_op jit(solution)/shard_map/load/pallas_call | solution.py:242
  9.2 2.0 %collective-permute-start.2 = (f32[24,256]{1,0:T(8,128)S(1)}, f32[24,256]{1,0:T(8,128)S(1)}, u32[]{:S(2)}, u32[]{:S(2)}) collective-permute-start(f32[24,256]{1,0:T(8,128)S(1)} %get-tuple-element.21.refs_2_.refs_0_.refs_4_), channel_id=1, source_target_pairs={{0,16},{16,0},{1,17},{17,1},{2,18},{18,2},{3,19},{19,3},{4,20},{20... | collective-permute-start | bytes 73736 | tf_op jit(solution)/shard_map/ppermute | solution.py:271
  11.2 0.0 collective-permute-done.refs_1_
  11.2 3.3 %hidden.1 = (f32[48,768]{1,0:T(8,128)S(1)}, f32[48,768]{1,0:T(8,128)S(1)}, bf16[48,768]{1,0:T(8,128)(2,1)S(1)}, bf16[768,4096]{1,0:T(8,128)(2,1)S(1)}) custom-call(s32[4]{0:T(128)S(1)} %pad_add_fusion.ids, bf16[24,4096]{1,0:T(8,128)(2,1)S(1)} %get-tuple-element.19.refs_0_, bf16[24,4096]{1,0:T(8,128)(2,1)S(1)} %collective-permute-done.refs_1_, ...), custom_call_target="tpu_custom_call" | custom-call | bytes 12582912 | tf_op jit(solution)/shard_map/hidden/pallas_call | solution.py:242
  14.5 0.0 collective-permute-done.2.refs_3_.refs_1_.refs_5_
  14.5 0.0 collective-permute-done.1.refs_1_.refs_3_
  14.5 4.9 %backward.1 = (bf16[48,768]{1,0:T(8,128)(2,1)S(1)}, bf16[48,768]{1,0:T(8,128)(2,1)S(1)}, bf16[2,2,24,1024]{3,2,1,0:T(8,128)(2,1)S(1)}) custom-call(s32[4]{0:T(128)S(1)} %pad_add_fusion.ids, bf16[24,4096]{1,0:T(8,128)(2,1)S(1)} %get-tuple-element.20.refs_0_.refs_2_, bf16[24,4096]{1,0:T(8,128)(2,1)S(1)} %collective-permute-done.1.refs_1_.refs_3_, ...), custom_call_target="tpu_custom_call" | custom-call | bytes 12582912 | tf_op jit(solution)/shard_map/backward/pallas_call | solution.py:242
  19.4 0.1 collective-permute-start.3
  19.5 1.8 %outward.1 = (bf16[2,2,24,1024]{3,2,1,0:T(8,128)(2,1)S(1)}, bf16[2,2,24,1024]{3,2,1,0:T(8,128)(2,1)S(1)}) custom-call(s32[4]{0:T(128)S(1)} %pad_add_fusion.ids, f32[24,256]{1,0:T(8,128)S(1)} %get-tuple-element.21.refs_2_.refs_0_.refs_4_, f32[24,256]{1,0:T(8,128)S(1)} %collective-permute-done.2.refs_3_.refs_1_.refs_5_, ...), custom_call_target="tpu_custom_call" | custom-call | bytes 6291456 | tf_op jit(solution)/shard_map/outward/pallas_call | solution.py:242
  21.3 0.6 %collective-permute-start.4 = (bf16[2,2,24,1024]{3,2,1,0:T(8,128)(2,1)S(1)}, bf16[2,2,24,1024]{3,2,1,0:T(8,128)(2,1)S(1)}, u32[]{:S(2)}, u32[]{:S(2)}) collective-permute-start(bf16[2,2,24,1024]{3,2,1,0:T(8,128)(2,1)S(1)} %get-tuple-element.33), channel_id=1, source_target_pairs={{0,1},{1,0},{2,3},{3,2},{4,5},{5,4},{6,7},{7,6},{8,9},{9,8},{10,11... | collective-permute-start | bytes 589832 | tf_op jit(solution)/shard_map/ppermute | solution.py:271
  21.8 2.5 %backward_keep.1 = bf16[2,2,24,1024]{3,2,1,0:T(8,128)(2,1)S(1)} custom-call(s32[4]{0:T(128)S(1)} %pad_add_fusion.ids, bf16[48,768]{1,0:T(8,128)(2,1)S(1)} %get-tuple-element.28.grad_gate, bf16[48,768]{1,0:T(8,128)(2,1)S(1)} %get-tuple-element.29.grad_up, bf16[4096,768]{1,0:T(8,128)(2,1)S(1)} %get-tuple-element.23.refs_3_.refs_6_.w_gate, ...), custom_call_target="tpu_custom_call" | custom-call | bytes 6291456 | tf_op jit(solution)/shard_map/backward_keep/pallas_call | solution.py:242
  24.4 0.0 collective-permute-done.3
  24.4 0.1 add.50
  24.4 0.0 collective-permute-done.4
  24.5 0.1 add.51
  24.6 1.6 %collective-permute-start.5 = (bf16[2,24,1024]{2,1,0:T(8,128)(2,1)S(1)}, bf16[2,24,1024]{2,1,0:T(8,128)(2,1)S(1)}, u32[]{:S(2)}, u32[]{:S(2)}) collective-permute-start(bf16[2,24,1024]{2,1,0:T(8,128)(2,1)S(1)} %pad_maximum_fusion.1), channel_id=1, source_target_pairs={{0,2},{2,0},{16,18},{18,16},{1,3},{3,1},{17,19},{19,17},{4,6},{6,4... | collective-permute-start | bytes 294920 | tf_op jit(solution)/shard_map/ppermute | solution.py:271
  26.2 0.8 %collective-permute-start.6 = (bf16[2,24,1024]{2,1,0:T(8,128)(2,1)S(1)}, bf16[2,24,1024]{2,1,0:T(8,128)(2,1)S(1)}, u32[]{:S(2)}, u32[]{:S(2)}) collective-permute-start(bf16[2,24,1024]{2,1,0:T(8,128)(2,1)S(1)} %pad_maximum_fusion.2), channel_id=1, source_target_pairs={{0,16},{2,18},{16,0},{18,2},{1,17},{3,19},{17,1},{19,3},{4,20},{6,... | collective-permute-start | bytes 294920 | tf_op jit(solution)/shard_map/ppermute | solution.py:271
  26.9 1.3 %collective-permute-start.7 = (bf16[2,24,1024]{2,1,0:T(8,128)(2,1)S(1)}, bf16[2,24,1024]{2,1,0:T(8,128)(2,1)S(1)}, u32[]{:S(2)}, u32[]{:S(2)}) collective-permute-start(bf16[2,24,1024]{2,1,0:T(8,128)(2,1)S(1)} %pad_maximum_fusion.3), channel_id=1, source_target_pairs={{0,18},{2,16},{16,2},{18,0},{1,19},{3,17},{17,3},{19,1},{4,22},{6,... | collective-permute-start | bytes 294920 | tf_op jit(solution)/shard_map/ppermute | solution.py:271
  28.3 1.1 %collective-permute-done.5 = bf16[2,24,1024]{2,1,0:T(8,128)(2,1)S(1)} collective-permute-done((bf16[2,24,1024]{2,1,0:T(8,128)(2,1)S(1)}, bf16[2,24,1024]{2,1,0:T(8,128)(2,1)S(1)}, u32[]{:S(2)}, u32[]{:S(2)}) %collective-permute-start.5) | collective-permute-done | bytes 98336 | tf_op jit(solution)/shard_map/ppermute | solution.py:271
  29.3 2.4 %collective-permute-done.6 = bf16[2,24,1024]{2,1,0:T(8,128)(2,1)S(1)} collective-permute-done((bf16[2,24,1024]{2,1,0:T(8,128)(2,1)S(1)}, bf16[2,24,1024]{2,1,0:T(8,128)(2,1)S(1)}, u32[]{:S(2)}, u32[]{:S(2)}) %collective-permute-start.6) | collective-permute-done | bytes 98336 | tf_op jit(solution)/shard_map/ppermute | solution.py:271
  31.7 1.2 %collective-permute-done.7 = bf16[2,24,1024]{2,1,0:T(8,128)(2,1)S(1)} collective-permute-done((bf16[2,24,1024]{2,1,0:T(8,128)(2,1)S(1)}, bf16[2,24,1024]{2,1,0:T(8,128)(2,1)S(1)}, u32[]{:S(2)}, u32[]{:S(2)}) %collective-permute-start.7) | collective-permute-done | bytes 98336 | tf_op jit(solution)/shard_map/ppermute | solution.py:271
  32.9 0.1 fusion
  32.9 3.7 %collective-permute-start.10 = (bf16[24,1024]{1,0:T(8,128)(2,1)S(1)}, bf16[24,1024]{1,0:T(8,128)(2,1)S(1)}, u32[]{:S(2)}, u32[]{:S(2)}) collective-permute-start(bf16[24,1024]{1,0:T(8,128)(2,1)S(1)} %get-tuple-element.35), channel_id=1, source_target_pairs={{0,12},{4,8},{8,4},{12,0},{1,13},{5,9},{9,5},{13,1},{2,14},{6,10},... | collective-permute-start | bytes 147464 | tf_op jit(solution)/shard_map/ppermute | solution.py:271
  36.6 0.0 collective-permute-start.8
  36.6 0.8 %collective-permute-start.9 = (bf16[24,1024]{1,0:T(8,128)(2,1)S(1)}, bf16[24,1024]{1,0:T(8,128)(2,1)S(1)}, u32[]{:S(2)}, u32[]{:S(2)}) collective-permute-start(bf16[24,1024]{1,0:T(8,128)(2,1)S(1)} %get-tuple-element.35), channel_id=1, source_target_pairs={{0,8},{4,12},{8,0},{12,4},{1,9},{5,13},{9,1},{13,5},{2,10},{6,14},... | collective-permute-start | bytes 147464 | tf_op jit(solution)/shard_map/ppermute | solution.py:271
  37.4 1.2 %collective-permute-start.15 = (bf16[24,1024]{1,0:T(8,128)(2,1)S(1)}, bf16[24,1024]{1,0:T(8,128)(2,1)S(1)}, u32[]{:S(2)}, u32[]{:S(2)}) collective-permute-start(bf16[24,1024]{1,0:T(8,128)(2,1)S(1)} %get-tuple-element.34), channel_id=1, source_target_pairs={{0,4},{4,0},{8,12},{12,8},{1,5},{5,1},{9,13},{13,9},{2,6},{6,2},{1... | collective-permute-start | bytes 147464 | tf_op jit(solution)/shard_map/ppermute | solution.py:271
  38.6 2.9 %collective-permute-start.16 = (bf16[24,1024]{1,0:T(8,128)(2,1)S(1)}, bf16[24,1024]{1,0:T(8,128)(2,1)S(1)}, u32[]{:S(2)}, u32[]{:S(2)}) collective-permute-start(bf16[24,1024]{1,0:T(8,128)(2,1)S(1)} %get-tuple-element.34), channel_id=1, source_target_pairs={{0,8},{4,12},{8,0},{12,4},{1,9},{5,13},{9,1},{13,5},{2,10},{6,14},... | collective-permute-start | bytes 147464 | tf_op jit(solution)/shard_map/ppermute | solution.py:271
  41.6 0.0 collective-permute-done.10
  41.6 1.4 %collective-permute-start.17 = (bf16[24,1024]{1,0:T(8,128)(2,1)S(1)}, bf16[24,1024]{1,0:T(8,128)(2,1)S(1)}, u32[]{:S(2)}, u32[]{:S(2)}) collective-permute-start(bf16[24,1024]{1,0:T(8,128)(2,1)S(1)} %get-tuple-element.34), channel_id=1, source_target_pairs={{0,12},{4,8},{8,4},{12,0},{1,13},{5,9},{9,5},{13,1},{2,14},{6,10},... | collective-permute-start | bytes 147464 | tf_op jit(solution)/shard_map/ppermute | solution.py:271
  43.0 0.0 collective-permute-done.8
  43.0 0.2 collective-permute-done.9
  43.2 0.8 %collective-permute-start.11 = (bf16[24,1024]{1,0:T(8,128)(2,1)S(1)}, bf16[24,1024]{1,0:T(8,128)(2,1)S(1)}, u32[]{:S(2)}, u32[]{:S(2)}) collective-permute-start(bf16[24,1024]{1,0:T(8,128)(2,1)S(1)} %add_convert_fusion.1), channel_id=1, source_target_pairs={{0,2},{2,0},{16,18},{18,16},{1,3},{3,1},{17,19},{19,17},{4,6},{6,4... | collective-permute-start | bytes 147464 | tf_op jit(solution)/shard_map/ppermute | solution.py:271
  44.0 0.8 %collective-permute-start.12 = (bf16[24,1024]{1,0:T(8,128)(2,1)S(1)}, bf16[24,1024]{1,0:T(8,128)(2,1)S(1)}, u32[]{:S(2)}, u32[]{:S(2)}) collective-permute-start(bf16[24,1024]{1,0:T(8,128)(2,1)S(1)} %add_convert_fusion.1), channel_id=1, source_target_pairs={{0,16},{2,18},{16,0},{18,2},{1,17},{3,19},{17,1},{19,3},{4,20},{6,... | collective-permute-start | bytes 147464 | tf_op jit(solution)/shard_map/ppermute | solution.py:271
  44.8 2.0 %collective-permute-start.13 = (bf16[24,1024]{1,0:T(8,128)(2,1)S(1)}, bf16[24,1024]{1,0:T(8,128)(2,1)S(1)}, u32[]{:S(2)}, u32[]{:S(2)}) collective-permute-start(bf16[24,1024]{1,0:T(8,128)(2,1)S(1)} %add_convert_fusion.1), channel_id=1, source_target_pairs={{0,18},{2,16},{16,2},{18,0},{1,19},{3,17},{17,3},{19,1},{4,22},{6,... | collective-permute-start | bytes 147464 | tf_op jit(solution)/shard_map/ppermute | solution.py:271
  46.8 0.7 %collective-permute-done.17 = bf16[24,1024]{1,0:T(8,128)(2,1)S(1)} collective-permute-done((bf16[24,1024]{1,0:T(8,128)(2,1)S(1)}, bf16[24,1024]{1,0:T(8,128)(2,1)S(1)}, u32[]{:S(2)}, u32[]{:S(2)}) %collective-permute-start.17) | collective-permute-done | bytes 49184 | tf_op jit(solution)/shard_map/ppermute | solution.py:271
  47.5 1.4 %collective-permute-start.18 = (bf16[24,1024]{1,0:T(8,128)(2,1)S(1)}, bf16[24,1024]{1,0:T(8,128)(2,1)S(1)}, u32[]{:S(2)}, u32[]{:S(2)}) collective-permute-start(bf16[24,1024]{1,0:T(8,128)(2,1)S(1)} %add_convert_fusion), channel_id=1, source_target_pairs={{0,2},{2,0},{1,3},{3,1},{4,6},{6,4},{5,7},{7,5},{8,10},{10,8},{9,1... | collective-permute-start | bytes 147464 | tf_op jit(solution)/shard_map/ppermute | solution.py:271
  48.9 0.0 collective-permute-done.11
  48.9 0.0 collective-permute-done.12
  48.9 0.9 %collective-permute-done.13 = bf16[24,1024]{1,0:T(8,128)(2,1)S(1)} collective-permute-done((bf16[24,1024]{1,0:T(8,128)(2,1)S(1)}, bf16[24,1024]{1,0:T(8,128)(2,1)S(1)}, u32[]{:S(2)}, u32[]{:S(2)}) %collective-permute-start.13) | collective-permute-done | bytes 49184 | tf_op jit(solution)/shard_map/ppermute | solution.py:271
  49.8 0.1 collective-permute-start.14
  49.9 1.7 %collective-permute-done.18 = bf16[24,1024]{1,0:T(8,128)(2,1)S(1)} collective-permute-done((bf16[24,1024]{1,0:T(8,128)(2,1)S(1)}, bf16[24,1024]{1,0:T(8,128)(2,1)S(1)}, u32[]{:S(2)}, u32[]{:S(2)}) %collective-permute-start.18) | collective-permute-done | bytes 49184 | tf_op jit(solution)/shard_map/ppermute | solution.py:271
  51.7 0.1 collective-permute-start.19
  51.7 1.3 %collective-permute-done.19.refs_11_ = bf16[2,24,1024]{2,1,0:T(8,128)(2,1)S(1)} collective-permute-done((bf16[2,24,1024]{2,1,0:T(8,128)(2,1)S(1)}, bf16[2,24,1024]{2,1,0:T(8,128)(2,1)S(1)}, u32[]{:S(2)}, u32[]{:S(2)}) %collective-permute-start.19) | collective-permute-done | bytes 98336 | tf_op jit(solution)/shard_map/ppermute | solution.py:271
  53.0 0.0 collective-permute-done.14.refs_9_
  53.0 2.3 %finish.1 = (bf16[24,4096]{1,0:T(8,128)(2,1)}, bf16[24,4096]{1,0:T(8,128)(2,1)}, bf16[24,128]{1,0:T(8,128)(2,1)}, bf16[128,2048]{1,0:T(8,128)(2,1)}) custom-call(s32[4]{0:T(128)S(1)} %pad_add_fusion.ids, bf16[24,4096]{1,0:T(8,128)(2,1)S(1)} %get-tuple-element.19.refs_0_, bf16[24,4096]{1,0:T(8,128)(2,1)S(1)} %collective-permute-done.refs_1_, ...), custom_call_target="tpu_custom_call" | custom-call | bytes 6291456 | tf_op jit(solution)/shard_map/finish/pallas_call | solution.py:242
  (13 shorter events, 0.2 us)
Async XLA Ops:
  0.6 10.5 %collective-permute-start = (bf16[24,4096]{1,0:T(8,128)(2,1)}, bf16[24,4096]{1,0:T(8,128)(2,1)S(1)}, u32[]{:S(2)}, u32[]{:S(2)}) collective-permute-start(bf16[24,4096]{1,0:T(8,128)(2,1)} %hid.1), channel_id=1, source_target_pairs={{0,16},{16,0},{1,17},{17,1},{2,18},{18,2},{3,19},{19,3},{4,20},{20... | collective-permute-start | bytes 589832 | tf_op jit(solution)/shard_map/ppermute | solution.py:271
  3.6 10.9 %collective-permute-start.1 = (bf16[24,4096]{1,0:T(8,128)(2,1)}, bf16[24,4096]{1,0:T(8,128)(2,1)S(1)}, u32[]{:S(2)}, u32[]{:S(2)}) collective-permute-start(bf16[24,4096]{1,0:T(8,128)(2,1)} %grads.1), channel_id=1, source_target_pairs={{0,16},{16,0},{1,17},{17,1},{2,18},{18,2},{3,19},{19,3},{4,20},{20... | collective-permute-start | bytes 589832 | tf_op jit(solution)/shard_map/ppermute | solution.py:271
  9.2 5.4 %collective-permute-start.2 = (f32[24,256]{1,0:T(8,128)S(1)}, f32[24,256]{1,0:T(8,128)S(1)}, u32[]{:S(2)}, u32[]{:S(2)}) collective-permute-start(f32[24,256]{1,0:T(8,128)S(1)} %get-tuple-element.21.refs_2_.refs_0_.refs_4_), channel_id=1, source_target_pairs={{0,16},{16,0},{1,17},{17,1},{2,18},{18,2},{3,19},{19,3},{4,20},{20... | collective-permute-start | bytes 73736 | tf_op jit(solution)/shard_map/ppermute | solution.py:271
  19.4 5.0 %collective-permute-start.3 = (bf16[2,2,24,1024]{3,2,1,0:T(8,128)(2,1)S(1)}, bf16[2,2,24,1024]{3,2,1,0:T(8,128)(2,1)S(1)}, u32[]{:S(2)}, u32[]{:S(2)}) collective-permute-start(bf16[2,2,24,1024]{3,2,1,0:T(8,128)(2,1)S(1)} %get-tuple-element.30), channel_id=1, source_target_pairs={{0,1},{1,0},{2,3},{3,2},{4,5},{5,4},{6,7},{7,6},{8,9},{9,8},{10,11... | collective-permute-start | bytes 589832 | tf_op jit(solution)/shard_map/ppermute | solution.py:271
  21.3 3.2 %collective-permute-start.4 = (bf16[2,2,24,1024]{3,2,1,0:T(8,128)(2,1)S(1)}, bf16[2,2,24,1024]{3,2,1,0:T(8,128)(2,1)S(1)}, u32[]{:S(2)}, u32[]{:S(2)}) collective-permute-start(bf16[2,2,24,1024]{3,2,1,0:T(8,128)(2,1)S(1)} %get-tuple-element.33), channel_id=1, source_target_pairs={{0,1},{1,0},{2,3},{3,2},{4,5},{5,4},{6,7},{7,6},{8,9},{9,8},{10,11... | collective-permute-start | bytes 589832 | tf_op jit(solution)/shard_map/ppermute | solution.py:271
  21.8 31.2 %copy-start = (bf16[128,4096]{1,0:T(8,128)(2,1)S(1)}, bf16[128,4096]{1,0:T(8,128)(2,1)}, u32[]{:S(2)}) copy-start(bf16[128,4096]{1,0:T(8,128)(2,1)} %refs_7_.1) | copy-start | bytes 3145732
  24.6 4.8 %collective-permute-start.5 = (bf16[2,24,1024]{2,1,0:T(8,128)(2,1)S(1)}, bf16[2,24,1024]{2,1,0:T(8,128)(2,1)S(1)}, u32[]{:S(2)}, u32[]{:S(2)}) collective-permute-start(bf16[2,24,1024]{2,1,0:T(8,128)(2,1)S(1)} %pad_maximum_fusion.1), channel_id=1, source_target_pairs={{0,2},{2,0},{16,18},{18,16},{1,3},{3,1},{17,19},{19,17},{4,6},{6,4... | collective-permute-start | bytes 294920 | tf_op jit(solution)/shard_map/ppermute | solution.py:271
  26.2 5.6 %collective-permute-start.6 = (bf16[2,24,1024]{2,1,0:T(8,128)(2,1)S(1)}, bf16[2,24,1024]{2,1,0:T(8,128)(2,1)S(1)}, u32[]{:S(2)}, u32[]{:S(2)}) collective-permute-start(bf16[2,24,1024]{2,1,0:T(8,128)(2,1)S(1)} %pad_maximum_fusion.2), channel_id=1, source_target_pairs={{0,16},{2,18},{16,0},{18,2},{1,17},{3,19},{17,1},{19,3},{4,20},{6,... | collective-permute-start | bytes 294920 | tf_op jit(solution)/shard_map/ppermute | solution.py:271
  26.9 6.0 %collective-permute-start.7 = (bf16[2,24,1024]{2,1,0:T(8,128)(2,1)S(1)}, bf16[2,24,1024]{2,1,0:T(8,128)(2,1)S(1)}, u32[]{:S(2)}, u32[]{:S(2)}) collective-permute-start(bf16[2,24,1024]{2,1,0:T(8,128)(2,1)S(1)} %pad_maximum_fusion.3), channel_id=1, source_target_pairs={{0,18},{2,16},{16,2},{18,0},{1,19},{3,17},{17,3},{19,1},{4,22},{6,... | collective-permute-start | bytes 294920 | tf_op jit(solution)/shard_map/ppermute | solution.py:271
  32.9 8.6 %collective-permute-start.10 = (bf16[24,1024]{1,0:T(8,128)(2,1)S(1)}, bf16[24,1024]{1,0:T(8,128)(2,1)S(1)}, u32[]{:S(2)}, u32[]{:S(2)}) collective-permute-start(bf16[24,1024]{1,0:T(8,128)(2,1)S(1)} %get-tuple-element.35), channel_id=1, source_target_pairs={{0,12},{4,8},{8,4},{12,0},{1,13},{5,9},{9,5},{13,1},{2,14},{6,10},... | collective-permute-start | bytes 147464 | tf_op jit(solution)/shard_map/ppermute | solution.py:271
  36.6 6.3 %collective-permute-start.8 = (bf16[24,1024]{1,0:T(8,128)(2,1)S(1)}, bf16[24,1024]{1,0:T(8,128)(2,1)S(1)}, u32[]{:S(2)}, u32[]{:S(2)}) collective-permute-start(bf16[24,1024]{1,0:T(8,128)(2,1)S(1)} %get-tuple-element.35), channel_id=1, source_target_pairs={{0,4},{4,0},{8,12},{12,8},{1,5},{5,1},{9,13},{13,9},{2,6},{6,2},{1... | collective-permute-start | bytes 147464 | tf_op jit(solution)/shard_map/ppermute | solution.py:271
  36.6 6.6 %collective-permute-start.9 = (bf16[24,1024]{1,0:T(8,128)(2,1)S(1)}, bf16[24,1024]{1,0:T(8,128)(2,1)S(1)}, u32[]{:S(2)}, u32[]{:S(2)}) collective-permute-start(bf16[24,1024]{1,0:T(8,128)(2,1)S(1)} %get-tuple-element.35), channel_id=1, source_target_pairs={{0,8},{4,12},{8,0},{12,4},{1,9},{5,13},{9,1},{13,5},{2,10},{6,14},... | collective-permute-start | bytes 147464 | tf_op jit(solution)/shard_map/ppermute | solution.py:271
  37.4 7.4 %collective-permute-start.15 = (bf16[24,1024]{1,0:T(8,128)(2,1)S(1)}, bf16[24,1024]{1,0:T(8,128)(2,1)S(1)}, u32[]{:S(2)}, u32[]{:S(2)}) collective-permute-start(bf16[24,1024]{1,0:T(8,128)(2,1)S(1)} %get-tuple-element.34), channel_id=1, source_target_pairs={{0,4},{4,0},{8,12},{12,8},{1,5},{5,1},{9,13},{13,9},{2,6},{6,2},{1... | collective-permute-start | bytes 147464 | tf_op jit(solution)/shard_map/ppermute | solution.py:271
  38.6 8.1 %collective-permute-start.16 = (bf16[24,1024]{1,0:T(8,128)(2,1)S(1)}, bf16[24,1024]{1,0:T(8,128)(2,1)S(1)}, u32[]{:S(2)}, u32[]{:S(2)}) collective-permute-start(bf16[24,1024]{1,0:T(8,128)(2,1)S(1)} %get-tuple-element.34), channel_id=1, source_target_pairs={{0,8},{4,12},{8,0},{12,4},{1,9},{5,13},{9,1},{13,5},{2,10},{6,14},... | collective-permute-start | bytes 147464 | tf_op jit(solution)/shard_map/ppermute | solution.py:271
  41.6 5.9 %collective-permute-start.17 = (bf16[24,1024]{1,0:T(8,128)(2,1)S(1)}, bf16[24,1024]{1,0:T(8,128)(2,1)S(1)}, u32[]{:S(2)}, u32[]{:S(2)}) collective-permute-start(bf16[24,1024]{1,0:T(8,128)(2,1)S(1)} %get-tuple-element.34), channel_id=1, source_target_pairs={{0,12},{4,8},{8,4},{12,0},{1,13},{5,9},{9,5},{13,1},{2,14},{6,10},... | collective-permute-start | bytes 147464 | tf_op jit(solution)/shard_map/ppermute | solution.py:271
  43.2 5.7 %collective-permute-start.11 = (bf16[24,1024]{1,0:T(8,128)(2,1)S(1)}, bf16[24,1024]{1,0:T(8,128)(2,1)S(1)}, u32[]{:S(2)}, u32[]{:S(2)}) collective-permute-start(bf16[24,1024]{1,0:T(8,128)(2,1)S(1)} %add_convert_fusion.1), channel_id=1, source_target_pairs={{0,2},{2,0},{16,18},{18,16},{1,3},{3,1},{17,19},{19,17},{4,6},{6,4... | collective-permute-start | bytes 147464 | tf_op jit(solution)/shard_map/ppermute | solution.py:271
  44.0 4.9 %collective-permute-start.12 = (bf16[24,1024]{1,0:T(8,128)(2,1)S(1)}, bf16[24,1024]{1,0:T(8,128)(2,1)S(1)}, u32[]{:S(2)}, u32[]{:S(2)}) collective-permute-start(bf16[24,1024]{1,0:T(8,128)(2,1)S(1)} %add_convert_fusion.1), channel_id=1, source_target_pairs={{0,16},{2,18},{16,0},{18,2},{1,17},{3,19},{17,1},{19,3},{4,20},{6,... | collective-permute-start | bytes 147464 | tf_op jit(solution)/shard_map/ppermute | solution.py:271
  44.8 5.0 %collective-permute-start.13 = (bf16[24,1024]{1,0:T(8,128)(2,1)S(1)}, bf16[24,1024]{1,0:T(8,128)(2,1)S(1)}, u32[]{:S(2)}, u32[]{:S(2)}) collective-permute-start(bf16[24,1024]{1,0:T(8,128)(2,1)S(1)} %add_convert_fusion.1), channel_id=1, source_target_pairs={{0,18},{2,16},{16,2},{18,0},{1,19},{3,17},{17,3},{19,1},{4,22},{6,... | collective-permute-start | bytes 147464 | tf_op jit(solution)/shard_map/ppermute | solution.py:271
  47.5 4.2 %collective-permute-start.18 = (bf16[24,1024]{1,0:T(8,128)(2,1)S(1)}, bf16[24,1024]{1,0:T(8,128)(2,1)S(1)}, u32[]{:S(2)}, u32[]{:S(2)}) collective-permute-start(bf16[24,1024]{1,0:T(8,128)(2,1)S(1)} %add_convert_fusion), channel_id=1, source_target_pairs={{0,2},{2,0},{1,3},{3,1},{4,6},{6,4},{5,7},{7,5},{8,10},{10,8},{9,1... | collective-permute-start | bytes 147464 | tf_op jit(solution)/shard_map/ppermute | solution.py:271
  49.8 3.2 %collective-permute-start.14 = (bf16[2,2,24,1024]{3,2,1,0:T(8,128)(2,1)S(1)}, bf16[2,2,24,1024]{3,2,1,0:T(8,128)(2,1)S(1)}, u32[]{:S(2)}, u32[]{:S(2)}) collective-permute-start(bf16[2,2,24,1024]{3,2,1,0:T(8,128)(2,1)S(1)} %bitcast.69), channel_id=1, source_target_pairs={{0,1},{1,0},{2,3},{3,2},{4,5},{5,4},{6,7},{7,6},{8,9},{9,8},{10,11... | collective-permute-start | bytes 589832 | tf_op jit(solution)/shard_map/ppermute | solution.py:271
  51.7 1.4 %collective-permute-start.19 = (bf16[2,24,1024]{2,1,0:T(8,128)(2,1)S(1)}, bf16[2,24,1024]{2,1,0:T(8,128)(2,1)S(1)}, u32[]{:S(2)}, u32[]{:S(2)}) collective-permute-start(bf16[2,24,1024]{2,1,0:T(8,128)(2,1)S(1)} %pad_maximum_fusion.4.refs_10_), channel_id=1, source_target_pairs={{0,1},{1,0},{2,3},{3,2},{4,5},{5,4},{6,7},{7,6},{8,9},{9,8},{10,11... | collective-permute-start | bytes 294920 | tf_op jit(solution)/shard_map/ppermute | solution.py:271

commit v5 on v4

--- a/solution.py
+++ b/solution.py
@@ -12,7 +12,7 @@
 BF16 = jnp.bfloat16
 STEP = 256
 LANES = 128
-LOAD_PIECES = 4
+LOAD_PIECES = 8
 FEW_ROWS = 64
 VMEM_LIMIT = 12 * 1024 * 1024
 
@@ -36,7 +36,7 @@
 def store_blocks(out_ref, j, columns, value, count):
     rows = value.shape[0] // count
     for k in range(count):
-        out_ref[j, k, :, columns] = value[k * rows : (k + 1) * rows].astype(BF16)
+        out_ref[k, j, :, columns] = value[k * rows : (k + 1) * rows].astype(BF16)
 
 
 def load_kernel(n_dp, ids, w_gate, w_up, hid, grads, gain, named, weights, context, *refs):
@@ -126,7 +126,7 @@
 
 def outward_kernel(n_dp, ids, *refs):
     smalls = refs[:n_dp]
-    act, w_down, send, keep = refs[n_dp:]
+    act, w_down, send, keep = refs[2 * n_dp :]
     weight = gates_of(smalls)
     chunk = send.shape[3]
     few = act.shape[0] <= FEW_ROWS
@@ -159,44 +159,47 @@
 
 def backward_kernel(n_dp, ids, *refs):
     grads, smalls = refs[:n_dp], refs[n_dp : 2 * n_dp]
-    pre_gate, pre_up, w_gate, w_up, w_down, grad_gate, grad_up, send, weighted = refs[2 * n_dp :]
+    pre_gate, pre_up, w_down, waiting, grad_gate, grad_up, passed, rows_grad = refs[2 * n_dp :]
+    passed[...] = waiting[...]
     weight = gates_of(smalls)
-    few = weighted.shape[0] <= FEW_ROWS
+    few = rows_grad.shape[0] <= FEW_ROWS
 
     def weigh(step):
         columns = pl.ds(place(step, 512), 512)
-        weighted[:, columns] = (weight * rows_of(grads, columns)).astype(BF16)
-
-    loop(weighted.shape[1] // 512, weigh, few)
+        rows_grad[:, columns] = (weight * rows_of(grads, columns)).astype(BF16)
+
+    loop(rows_grad.shape[1] // 512, weigh, few)
 
     def hidden_units(step):
         columns = pl.ds(place(step, STEP), STEP)
-        back = dot(weighted[...], w_down[columns, :], ((1,), (1,)))
+        back = dot(rows_grad[...], w_down[columns, :], ((1,), (1,)))
         gate_part, up_part = pre_gate[:, columns], pre_up[:, columns]
         sig = jax.nn.sigmoid(gate_part)
         grad_gate[:, columns] = (back * up_part * sig * (1.0 + gate_part * (1.0 - sig))).astype(BF16)
         grad_up[:, columns] = (back * gate_part * sig).astype(BF16)
 
     loop(w_down.shape[0] // STEP, hidden_units, few)
-    inward_part(ids, 1, n_dp, grad_gate, grad_up, w_gate, w_up, send)
-
-
-def keep_kernel(n_dp, ids, grad_gate, grad_up, w_gate, w_up, keep):
-    inward_part(ids, 0, n_dp, grad_gate, grad_up, w_gate, w_up, keep)
+
+
+def inward_kernel(i, n_dp, ids, grad_gate, grad_up, w_gate, w_up, waiting, target, passed):
+    passed[...] = waiting[...]
+    inward_part(ids, i, n_dp, grad_gate, grad_up, w_gate, w_up, target)
 
 
 def finish_kernel(n_dp, ids, *refs):
     hid, grads, smalls = refs[:n_dp], refs[n_dp : 2 * n_dp], refs[2 * n_dp : 3 * n_dp]
-    gain, w_out, back_own, back_other, moe_own, moe_other = refs[3 * n_dp : 3 * n_dp + 6]
-    output, d_hidden, d_context, d_w_out, summed, d_all = refs[3 * n_dp + 6 :]
+    back, moe = refs[3 * n_dp : 7 * n_dp], refs[7 * n_dp : 7 * n_dp + 4]
+    gain, w_out, output, d_hidden, d_context, d_w_out, summed, d_all = refs[7 * n_dp + 4 :]
     rows, width = hid[0].shape
-    chunk = back_own.shape[3]
-    for i, (back, moe) in enumerate(((back_own, moe_own), (back_other, moe_other))):
+    chunk = moe[0].shape[1]
+    for i in range(2):
         for j in range(2):
             columns = pl.ds(pl.multiple_of(own_columns(ids, i, j, chunk), chunk), chunk)
             for k in range(n_dp):
-                summed[k * rows : (k + 1) * rows, columns] = back[k, j].astype(F32) * gain[:, columns]
-            output[:, columns] = (hid[0][:, columns].astype(F32) + moe[j].astype(F32)).astype(BF16)
+                piece = back[(i * n_dp + k) * 2 + j]
+                summed[k * rows : (k + 1) * rows, columns] = piece[...].astype(F32) * gain[:, columns]
+            piece = moe[i * 2 + j]
+            output[:, columns] = (hid[0][:, columns].astype(F32) + piece[...].astype(F32)).astype(BF16)
 
     few = rows * n_dp <= FEW_ROWS
     squares = jnp.zeros((rows * n_dp, 1), F32)
@@ -275,7 +278,7 @@
         return [own] + [swap(value, ("dp",), k) for k in range(1, n_dp)]
 
     weights = 2 * width * units
-    shares = ((2, n_dp, rows, chunk), BF16)
+    shares = ((n_dp, 2, rows, chunk), BF16)
     wg, wu, hid_own, grads_own, gain, small_own = run(
         load_kernel, n_dp, ids,
         [w_gate[0], w_up[0], hidden_in, grad_out, norm_gain.reshape(1, width), route_ids.T, route_gates.T, context],
@@ -289,20 +292,12 @@
     smalls = all_blocks(small_own)
     grads = all_blocks(grad_out, grads_own)
 
-    def plane_halves(send, keep):
-        return keep + swap(send, ("c",), 1)
-
-    def plane_share(halves):
-        totals = [half[0, 0].astype(F32) for half in halves]
-        for t in range(1, 2 * n_dp):
-            piece = swap(jnp.stack([half[t % 2, t // 2] for half in halves]), ("dp", "y"), t)
-            totals = [total + piece[n].astype(F32) for n, total in enumerate(totals)]
-        return [total.astype(BF16) for total in totals]
-
-    def column_sum(value):
-        pieces = [swap(value, ("hi",), t) for t in range(1, n_hi)]
-        total = value.astype(F32)
-        for piece in pieces:
+    def add(one, other):
+        return (one.astype(F32) + other.astype(F32)).astype(BF16)
+
+    def total_of(pieces):
+        total = pieces[0].astype(F32)
+        for piece in pieces[1:]:
             total = total + piece.astype(F32)
         return total.astype(BF16)
 
@@ -312,28 +307,43 @@
         [pltpu.VMEM((all_rows, width), BF16), pltpu.SemaphoreType.DMA], 2 * weights, "hidden", far=(n_dp + 3,),
     )
     out_send, out_keep = run(
-        outward_kernel, n_dp, ids, smalls + [act, wd], [shares, shares], [], weights, "outward"
-    )
-    out_half = plane_halves(out_send, out_keep)
-    grad_gate, grad_up, in_send = run(
-        backward_kernel, n_dp, ids, grads + smalls + [pre_gate, pre_up, wg, wu, wd],
+        outward_kernel, n_dp, ids, smalls + grads + [act, wd], [shares, shares], [], weights, "outward"
+    )
+    out_other = swap(out_send, ("c",), 1)
+    grad_gate, grad_up, out_keep = run(
+        backward_kernel, n_dp, ids, grads + smalls + [pre_gate, pre_up, wd, out_keep],
         [((all_rows, units), BF16), ((all_rows, units), BF16), shares],
-        [pltpu.VMEM((all_rows, width), BF16)], 2 * weights, "backward",
-    )
-    (in_keep,) = run(
-        keep_kernel, n_dp, ids, [grad_gate, grad_up, wg, wu], [shares], [], weights, "backward_keep"
-    )
-    in_half = plane_halves(in_send, in_keep)
-    in_share, out_share = plane_share([in_half, out_half])
-    in_total, out_total = column_sum(in_share), column_sum(out_share)
-    pieces = [in_total] + [swap(in_total, ("dp", "y"), t) for t in range(1, 2 * n_dp)]
-    back_own = jnp.stack(pieces).reshape(n_dp, 2, rows, chunk)
-    back_other = swap(back_own, ("c",), 1)
-    moe_own = jnp.stack([out_total, swap(out_total, ("y",), 1)])
-    moe_other = swap(moe_own, ("c",), 1)
+        [pltpu.VMEM((all_rows, width), BF16)], weights, "backward",
+    )
+    out_half = add(out_keep, out_other)
+    out_blocks = [swap(out_half[k], ("dp",), k) for k in range(1, n_dp)]
+    in_send, out_block = run(
+        functools.partial(inward_kernel, 1), n_dp, ids, [grad_gate, grad_up, wg, wu, out_half[0]],
+        [shares, (shares[0][1:], BF16)], [], weights, "inward_send",
+    )
+    in_other = swap(in_send, ("c",), 1)
+    out_block = total_of([out_block] + out_blocks)
+    out_other = swap(out_block[1], ("y",), 1)
+    in_keep, out_share = run(
+        functools.partial(inward_kernel, 0), n_dp, ids, [grad_gate, grad_up, wg, wu, out_block[0]],
+        [shares, (shares[0][2:], BF16)], [], weights, "inward_keep",
+    )
+    out_total = add(out_share, out_other)
+    in_half = add(in_keep, in_other)
+    turns = [t for t in range(2 * n_dp - 1, 0, -1)]
+    in_share = total_of([in_half[0, 0]] + [swap(in_half[t // 2, t % 2], ("dp", "y"), t) for t in turns])
+    in_total = total_of([in_share] + [swap(in_share, ("hi",), t) for t in range(n_hi - 1, 0, -1)])
+    turn = 1
+    while turn < n_hi:
+        out_total = add(out_total, swap(out_total, ("hi",), turn))
+        turn = 2 * turn
+    spread = {t: swap(in_total, ("dp", "y"), t) for t in turns}
+    back = [in_total] + [spread[t] for t in range(1, 2 * n_dp)]
+    moe = [out_total, swap(out_total, ("y",), 1)]
+    back = back + [swap(piece, ("c",), 1) for piece in back]
+    moe = moe + [swap(piece, ("c",), 1) for piece in moe]
     return run(
-        finish_kernel, n_dp, ids,
-        hid + grads + smalls + [gain, w_out, back_own, back_other, moe_own, moe_other],
+        finish_kernel, n_dp, ids, hid + grads + smalls + back + moe + [gain, w_out],
         [((rows, width), BF16), ((rows, width), BF16), ((rows, heads), BF16), ((heads, width // n_dp), BF16)],
         [pltpu.VMEM((all_rows, width), F32), pltpu.VMEM((all_rows, width), BF16)],
         weights, "finish", out_space=None,

time: 55.5 us -> 56.5 us (1.018)
  starting transfers between devices: 24.5 us -> 25.5 us
    ppermute x20 -> x25, starting transfers between devices: 24.5 us -> 25.5 us  [swap(): return lax.ppermute(value, axes, [(i, i ^ turn) for i in range(count)])]
    pallas_call x6 -> x7, Pallas kernels: 20.1 us -> 20.4 us  [run(): pl.pallas_call(functools.partial(kernel, n_dp), out_shape=kinds, in_specs...]
    ppermute x20 -> x25, waiting for transfers between devices: 9.47 us -> 9.24 us  [swap(): return lax.ppermute(value, axes, [(i, i ^ turn) for i in range(count)])]
  transfers between devices with their start and end apart: 20 -> 25, of which waited for: 8 -> 7; matrix products, arithmetic and copies ran while one was open for 0% -> 0% of each run, Pallas kernels for 23% -> 29%
where the time goes in v5:
time: 56.5 us; the launch traced here: 56.3 us
  starting transfers between devices  25.5 us (45%)
  Pallas kernels  20.4 us (36%)
  waiting for transfers between devices  9.24 us (16%)
  between operations  0.82 us (1%)
    ppermute x25, starting transfers between devices, swap(): return lax.ppermute(value, axes, [(i, i ^ turn) for i in range(count)])  25.5 us
    pallas_call x7, Pallas kernels, run(): pl.pallas_call(functools.partial(kernel, n_dp), out_shape=kinds, in_specs...  20.4 us
    ppermute x25, waiting for transfers between devices, swap(): return lax.ppermute(value, axes, [(i, i ^ turn) for i in range(count)])  9.24 us
  transfers between devices with their start and end apart: 25, of which 7 were waited for; matrix products, arithmetic and copies ran while one was open for 0% of the time, Pallas kernels for 29%

profile of v5, /device:TPU:0, one launch (start us, length us, event | category | flops | bytes accessed | tf_op | source)
XLA Modules:
  0.0 56.3 jit_solution(7916027289526353357)
XLA Ops:
  0.6 3.0 %collective-permute-start = (bf16[24,4096]{1,0:T(8,128)(2,1)}, bf16[24,4096]{1,0:T(8,128)(2,1)S(1)}, u32[]{:S(2)}, u32[]{:S(2)}) collective-permute-start(bf16[24,4096]{1,0:T(8,128)(2,1)} %hid.1), channel_id=1, source_target_pairs={{0,16},{16,0},{1,17},{17,1},{2,18},{18,2},{3,19},{19,3},{4,20},{20... | collective-permute-start | bytes 589832 | tf_op jit(solution)/shard_map/ppermute | solution.py:274
  3.6 0.1 collective-permute-start.1
  3.7 0.1 pad_add_fusion.ids
  3.8 5.4 %load.1 = (bf16[4096,768]{1,0:T(8,128)(2,1)S(1)}, bf16[4096,768]{1,0:T(8,128)(2,1)S(1)}, bf16[24,4096]{1,0:T(8,128)(2,1)S(1)}, bf16[24,4096]{1,0:T(8,128)(2,1)S(...) custom-call(s32[4]{0:T(128)S(1)} %pad_add_fusion.ids, bf16[4096,768]{1,0:T(8,128)(2,1)} %bitcast.29, ...), custom_call_target="tpu_custom_call" | custom-call | bytes 12582912 | tf_op jit(solution)/shard_map/load/pallas_call | solution.py:245
  9.2 2.0 %collective-permute-start.2 = (f32[24,256]{1,0:T(8,128)S(1)}, f32[24,256]{1,0:T(8,128)S(1)}, u32[]{:S(2)}, u32[]{:S(2)}) collective-permute-start(f32[24,256]{1,0:T(8,128)S(1)} %get-tuple-element.25.refs_0_.refs_2_.refs_4_), channel_id=1, source_target_pairs={{0,16},{16,0},{1,17},{17,1},{2,18},{18,2},{3,19},{19,3},{4,20},{20... | collective-permute-start | bytes 73736 | tf_op jit(solution)/shard_map/ppermute | solution.py:274
  11.2 3.3 %hidden.1 = (f32[48,768]{1,0:T(8,128)S(1)}, f32[48,768]{1,0:T(8,128)S(1)}, bf16[48,768]{1,0:T(8,128)(2,1)S(1)}, bf16[768,4096]{1,0:T(8,128)(2,1)S(1)}) custom-call(s32[4]{0:T(128)S(1)} %pad_add_fusion.ids, bf16[24,4096]{1,0:T(8,128)(2,1)S(1)} %get-tuple-element.23.refs_0_, bf16[24,4096]{1,0:T(8,128)(2,1)S(1)} %collective-permute-done.refs_1_, ...), custom_call_target="tpu_custom_call" | custom-call | bytes 12582912 | tf_op jit(solution)/shard_map/hidden/pallas_call | solution.py:245
  14.6 0.0 collective-permute-done.2.refs_1_.refs_3_.refs_5_
  14.6 1.8 %outward.1 = (bf16[2,2,24,1024]{3,2,1,0:T(8,128)(2,1)S(1)}, bf16[2,2,24,1024]{3,2,1,0:T(8,128)(2,1)S(1)}) custom-call(s32[4]{0:T(128)S(1)} %pad_add_fusion.ids, f32[24,256]{1,0:T(8,128)S(1)} %get-tuple-element.25.refs_0_.refs_2_.refs_4_, f32[24,256]{1,0:T(8,128)S(1)} %collective-permute-done.2.refs_1_.refs_3_.refs_5_, ...), custom_call_target="tpu_custom_call" | custom-call | bytes 6291456 | tf_op jit(solution)/shard_map/outward/pallas_call | solution.py:245
  16.4 0.1 collective-permute-start.3
  16.5 2.6 %backward.1 = (bf16[48,768]{1,0:T(8,128)(2,1)S(1)}, bf16[48,768]{1,0:T(8,128)(2,1)S(1)}, bf16[2,2,24,1024]{3,2,1,0:T(8,128)(2,1)S(1)}) custom-call(s32[4]{0:T(128)S(1)} %pad_add_fusion.ids, bf16[24,4096]{1,0:T(8,128)(2,1)S(1)} %get-tuple-element.24.refs_2_.refs_0_, bf16[24,4096]{1,0:T(8,128)(2,1)S(1)} %collective-permute-done.1.refs_3_.refs_1_, ...), custom_call_target="tpu_custom_call" | custom-call | bytes 6291456 | tf_op jit(solution)/shard_map/backward/pallas_call | solution.py:245
  19.1 0.1 add_convert_fusion.1
  19.2 0.7 %collective-permute-start.4 = (bf16[2,24,1024]{2,1,0:T(8,128)(2,1)S(1)}, bf16[2,24,1024]{2,1,0:T(8,128)(2,1)S(1)}, u32[]{:S(2)}, u32[]{:S(2)}) collective-permute-start(bf16[2,24,1024]{2,1,0:T(8,128)(2,1)S(1)} %get-tuple-element.45), channel_id=1, source_target_pairs={{0,16},{16,0},{1,17},{17,1},{2,18},{18,2},{3,19},{19,3},{4,20},{20... | collective-permute-start | bytes 294920 | tf_op jit(solution)/shard_map/ppermute | solution.py:274
  19.9 2.5 %inward_send.1 = (bf16[2,2,24,1024]{3,2,1,0:T(8,128)(2,1)S(1)}, bf16[2,24,1024]{2,1,0:T(8,128)(2,1)S(1)}) custom-call(s32[4]{0:T(128)S(1)} %pad_add_fusion.ids, bf16[48,768]{1,0:T(8,128)(2,1)S(1)} %get-tuple-element.34.grad_gate, bf16[48,768]{1,0:T(8,128)(2,1)S(1)} %get-tuple-element.35.grad_up, bf16[4096,768]{1,0:T(8,128)(2,1)S(1)} %get-tuple-element.27.refs_3_.w_gate, ...), custom_call_target="tpu_custom_call" | custom-call | bytes 6291456 | tf_op jit(solution)/shard_map/inward_send/pallas_call | solution.py:245
  22.4 2.1 %collective-permute-done.4 = bf16[2,24,1024]{2,1,0:T(8,128)(2,1)S(1)} collective-permute-done((bf16[2,24,1024]{2,1,0:T(8,128)(2,1)S(1)}, bf16[2,24,1024]{2,1,0:T(8,128)(2,1)S(1)}, u32[]{:S(2)}, u32[]{:S(2)}) %collective-permute-start.4) | collective-permute-done | bytes 98336 | tf_op jit(solution)/shard_map/ppermute | solution.py:274
  24.5 1.6 %collective-permute-start.19 = (bf16[24,1024]{1,0:T(8,128)(2,1)S(1)}, bf16[24,1024]{1,0:T(8,128)(2,1)S(1)}, u32[]{:S(2)}, u32[]{:S(2)}) collective-permute-start(bf16[24,1024]{1,0:T(8,128)(2,1)S(1)} %get-tuple-element.47), channel_id=1, source_target_pairs={{0,2},{2,0},{1,3},{3,1},{4,6},{6,4},{5,7},{7,5},{8,10},{10,8},{9,1... | collective-permute-start | bytes 147464 | tf_op jit(solution)/shard_map/ppermute | solution.py:274
  26.1 2.5 %inward_keep.1 = (bf16[2,2,24,1024]{3,2,1,0:T(8,128)(2,1)S(1)}, bf16[24,1024]{1,0:T(8,128)(2,1)S(1)}) custom-call(s32[4]{0:T(128)S(1)} %pad_add_fusion.ids, bf16[48,768]{1,0:T(8,128)(2,1)S(1)} %get-tuple-element.34.grad_gate, bf16[48,768]{1,0:T(8,128)(2,1)S(1)} %get-tuple-element.35.grad_up, bf16[4096,768]{1,0:T(8,128)(2,1)S(1)} %get-tuple-element.27.refs_3_.w_gate, ...), custom_call_target="tpu_custom_call" | custom-call | bytes 6291456 | tf_op jit(solution)/shard_map/inward_keep/pallas_call | solution.py:245
  28.6 0.0 collective-permute-done.19
  28.7 1.6 %collective-permute-start.20 = (bf16[24,1024]{1,0:T(8,128)(2,1)S(1)}, bf16[24,1024]{1,0:T(8,128)(2,1)S(1)}, u32[]{:S(2)}, u32[]{:S(2)}) collective-permute-start(bf16[24,1024]{1,0:T(8,128)(2,1)S(1)} %add_convert_fusion.5), channel_id=1, source_target_pairs={{0,4},{4,0},{8,12},{12,8},{1,5},{5,1},{9,13},{13,9},{2,6},{6,2},{1... | collective-permute-start | bytes 147464 | tf_op jit(solution)/shard_map/ppermute | solution.py:274
  30.3 0.1 add_convert_fusion
  30.4 1.6 %collective-permute-start.6 = (bf16[24,1024]{1,0:T(8,128)(2,1)S(1)}, bf16[24,1024]{1,0:T(8,128)(2,1)S(1)}, u32[]{:S(2)}, u32[]{:S(2)}) collective-permute-start(bf16[24,1024]{1,0:T(8,128)(2,1)S(1)} %get-tuple-element.42), channel_id=1, source_target_pairs={{0,18},{2,16},{16,2},{18,0},{1,19},{3,17},{17,3},{19,1},{4,22},{6,... | collective-permute-start | bytes 147464 | tf_op jit(solution)/shard_map/ppermute | solution.py:274
  32.0 0.5 collective-permute-start.8
  32.5 1.4 %collective-permute-start.7 = (bf16[24,1024]{1,0:T(8,128)(2,1)S(1)}, bf16[24,1024]{1,0:T(8,128)(2,1)S(1)}, u32[]{:S(2)}, u32[]{:S(2)}) collective-permute-start(bf16[24,1024]{1,0:T(8,128)(2,1)S(1)} %get-tuple-element.44), channel_id=1, source_target_pairs={{0,16},{2,18},{16,0},{18,2},{1,17},{3,19},{17,1},{19,3},{4,20},{6,... | collective-permute-start | bytes 147464 | tf_op jit(solution)/shard_map/ppermute | solution.py:274
  33.9 0.0 collective-permute-done.20
  34.0 2.7 %collective-permute-start.21 = (bf16[24,1024]{1,0:T(8,128)(2,1)S(1)}, bf16[24,1024]{1,0:T(8,128)(2,1)S(1)}, u32[]{:S(2)}, u32[]{:S(2)}) collective-permute-start(bf16[24,1024]{1,0:T(8,128)(2,1)S(1)} %add_convert_fusion.4), channel_id=1, source_target_pairs={{0,8},{4,12},{8,0},{12,4},{1,9},{5,13},{9,1},{13,5},{2,10},{6,14},... | collective-permute-start | bytes 147464 | tf_op jit(solution)/shard_map/ppermute | solution.py:274
  36.6 0.0 collective-permute-done.6
  36.6 0.0 collective-permute-done.8
  36.6 0.0 collective-permute-done.7
  36.7 0.5 collective-permute-start.11
  37.2 2.5 %collective-permute-start.10 = (bf16[24,1024]{1,0:T(8,128)(2,1)S(1)}, bf16[24,1024]{1,0:T(8,128)(2,1)S(1)}, u32[]{:S(2)}, u32[]{:S(2)}) collective-permute-start(bf16[24,1024]{1,0:T(8,128)(2,1)S(1)} %fusion.2), channel_id=1, source_target_pairs={{0,8},{4,12},{8,0},{12,4},{1,9},{5,13},{9,1},{13,5},{2,10},{6,14},... | collective-permute-start | bytes 147464 | tf_op jit(solution)/shard_map/ppermute | solution.py:274
  39.8 1.4 %collective-permute-start.9 = (bf16[24,1024]{1,0:T(8,128)(2,1)S(1)}, bf16[24,1024]{1,0:T(8,128)(2,1)S(1)}, u32[]{:S(2)}, u32[]{:S(2)}) collective-permute-start(bf16[24,1024]{1,0:T(8,128)(2,1)S(1)} %fusion.2), channel_id=1, source_target_pairs={{0,12},{4,8},{8,4},{12,0},{1,13},{5,9},{9,5},{13,1},{2,14},{6,10},... | collective-permute-start | bytes 147464 | tf_op jit(solution)/shard_map/ppermute | solution.py:274
  41.1 0.0 collective-permute-done.21
  41.1 0.1 collective-permute-start.23
  41.2 1.6 %collective-permute-start.22 = (bf16[24,1024]{1,0:T(8,128)(2,1)S(1)}, bf16[24,1024]{1,0:T(8,128)(2,1)S(1)}, u32[]{:S(2)}, u32[]{:S(2)}) collective-permute-start(bf16[24,1024]{1,0:T(8,128)(2,1)S(1)} %add_convert_fusion.3.refs_14_), channel_id=1, source_target_pairs={{0,2},{2,0},{1,3},{3,1},{4,6},{6,4},{5,7},{7,5},{8,10},{10,8},{9,1... | collective-permute-start | bytes 147464 | tf_op jit(solution)/shard_map/ppermute | solution.py:274
  42.8 0.0 collective-permute-done.11
  42.8 0.0 collective-permute-done.10
  42.8 2.8 %collective-permute-done.9 = bf16[24,1024]{1,0:T(8,128)(2,1)S(1)} collective-permute-done((bf16[24,1024]{1,0:T(8,128)(2,1)S(1)}, bf16[24,1024]{1,0:T(8,128)(2,1)S(1)}, u32[]{:S(2)}, u32[]{:S(2)}) %collective-permute-start.9) | collective-permute-done | bytes 49184 | tf_op jit(solution)/shard_map/ppermute | solution.py:274
  45.7 2.4 %collective-permute-start.14 = (bf16[24,1024]{1,0:T(8,128)(2,1)S(1)}, bf16[24,1024]{1,0:T(8,128)(2,1)S(1)}, u32[]{:S(2)}, u32[]{:S(2)}) collective-permute-start(bf16[24,1024]{1,0:T(8,128)(2,1)S(1)} %add_convert_fusion.6.refs_6_), channel_id=1, source_target_pairs={{0,18},{2,16},{16,2},{18,0},{1,19},{3,17},{17,3},{19,1},{4,22},{6,... | collective-permute-start | bytes 147464 | tf_op jit(solution)/shard_map/ppermute | solution.py:274
  48.1 0.6 %collective-permute-start.13 = (bf16[24,1024]{1,0:T(8,128)(2,1)S(1)}, bf16[24,1024]{1,0:T(8,128)(2,1)S(1)}, u32[]{:S(2)}, u32[]{:S(2)}) collective-permute-start(bf16[24,1024]{1,0:T(8,128)(2,1)S(1)} %add_convert_fusion.6.refs_6_), channel_id=1, source_target_pairs={{0,16},{2,18},{16,0},{18,2},{1,17},{3,19},{17,1},{19,3},{4,20},{6,... | collective-permute-start | bytes 147464 | tf_op jit(solution)/shard_map/ppermute | solution.py:274
  48.7 0.5 collective-permute-start.12
  49.2 0.0 collective-permute-done.23.refs_16_
  49.2 0.0 collective-permute-start.15
  49.2 0.5 collective-permute-start.24
  49.7 1.0 %collective-permute-done.14.refs_9_ = bf16[24,1024]{1,0:T(8,128)(2,1)S(1)} collective-permute-done((bf16[24,1024]{1,0:T(8,128)(2,1)S(1)}, bf16[24,1024]{1,0:T(8,128)(2,1)S(1)}, u32[]{:S(2)}, u32[]{:S(2)}) %collective-permute-start.14) | collective-permute-done | bytes 49184 | tf_op jit(solution)/shard_map/ppermute | solution.py:274
  50.7 1.5 %collective-permute-done.13.refs_8_ = bf16[24,1024]{1,0:T(8,128)(2,1)S(1)} collective-permute-done((bf16[24,1024]{1,0:T(8,128)(2,1)S(1)}, bf16[24,1024]{1,0:T(8,128)(2,1)S(1)}, u32[]{:S(2)}, u32[]{:S(2)}) %collective-permute-start.13) | collective-permute-done | bytes 49184 | tf_op jit(solution)/shard_map/ppermute | solution.py:274
  52.2 0.6 %collective-permute-done.12.refs_7_ = bf16[24,1024]{1,0:T(8,128)(2,1)S(1)} collective-permute-done((bf16[24,1024]{1,0:T(8,128)(2,1)S(1)}, bf16[24,1024]{1,0:T(8,128)(2,1)S(1)}, u32[]{:S(2)}, u32[]{:S(2)}) %collective-permute-start.12) | collective-permute-done | bytes 49184 | tf_op jit(solution)/shard_map/ppermute | solution.py:274
  52.8 0.6 %collective-permute-done.17.refs_12_ = bf16[24,1024]{1,0:T(8,128)(2,1)S(1)} collective-permute-done((bf16[24,1024]{1,0:T(8,128)(2,1)S(1)}, bf16[24,1024]{1,0:T(8,128)(2,1)S(1)}, u32[]{:S(2)}, u32[]{:S(2)}) %collective-permute-start.17) | collective-permute-done | bytes 49184 | tf_op jit(solution)/shard_map/ppermute | solution.py:274
  53.4 0.6 %collective-permute-done.16.refs_11_ = bf16[24,1024]{1,0:T(8,128)(2,1)S(1)} collective-permute-done((bf16[24,1024]{1,0:T(8,128)(2,1)S(1)}, bf16[24,1024]{1,0:T(8,128)(2,1)S(1)}, u32[]{:S(2)}, u32[]{:S(2)}) %collective-permute-start.16) | collective-permute-done | bytes 49184 | tf_op jit(solution)/shard_map/ppermute | solution.py:274
  54.0 2.3 %finish.1 = (bf16[24,4096]{1,0:T(8,128)(2,1)}, bf16[24,4096]{1,0:T(8,128)(2,1)}, bf16[24,128]{1,0:T(8,128)(2,1)}, bf16[128,2048]{1,0:T(8,128)(2,1)}) custom-call(s32[4]{0:T(128)S(1)} %pad_add_fusion.ids, bf16[24,4096]{1,0:T(8,128)(2,1)S(1)} %get-tuple-element.23.refs_0_, bf16[24,4096]{1,0:T(8,128)(2,1)S(1)} %collective-permute-done.refs_1_, ...), custom_call_target="tpu_custom_call" | custom-call | bytes 6291456 | tf_op jit(solution)/shard_map/finish/pallas_call | solution.py:245
  (23 shorter events, 0.2 us)
Async XLA Ops:
  0.6 10.6 %collective-permute-start = (bf16[24,4096]{1,0:T(8,128)(2,1)}, bf16[24,4096]{1,0:T(8,128)(2,1)S(1)}, u32[]{:S(2)}, u32[]{:S(2)}) collective-permute-start(bf16[24,4096]{1,0:T(8,128)(2,1)} %hid.1), channel_id=1, source_target_pairs={{0,16},{16,0},{1,17},{17,1},{2,18},{18,2},{3,19},{19,3},{4,20},{20... | collective-permute-start | bytes 589832 | tf_op jit(solution)/shard_map/ppermute | solution.py:274
  3.6 11.0 %collective-permute-start.1 = (bf16[24,4096]{1,0:T(8,128)(2,1)}, bf16[24,4096]{1,0:T(8,128)(2,1)S(1)}, u32[]{:S(2)}, u32[]{:S(2)}) collective-permute-start(bf16[24,4096]{1,0:T(8,128)(2,1)} %grads.1), channel_id=1, source_target_pairs={{0,16},{16,0},{1,17},{17,1},{2,18},{18,2},{3,19},{19,3},{4,20},{20... | collective-permute-start | bytes 589832 | tf_op jit(solution)/shard_map/ppermute | solution.py:274
  9.2 5.4 %collective-permute-start.2 = (f32[24,256]{1,0:T(8,128)S(1)}, f32[24,256]{1,0:T(8,128)S(1)}, u32[]{:S(2)}, u32[]{:S(2)}) collective-permute-start(f32[24,256]{1,0:T(8,128)S(1)} %get-tuple-element.25.refs_0_.refs_2_.refs_4_), channel_id=1, source_target_pairs={{0,16},{16,0},{1,17},{17,1},{2,18},{18,2},{3,19},{19,3},{4,20},{20... | collective-permute-start | bytes 73736 | tf_op jit(solution)/shard_map/ppermute | solution.py:274
  16.4 2.7 %collective-permute-start.3 = (bf16[2,2,24,1024]{3,2,1,0:T(8,128)(2,1)S(1)}, bf16[2,2,24,1024]{3,2,1,0:T(8,128)(2,1)S(1)}, u32[]{:S(2)}, u32[]{:S(2)}) collective-permute-start(bf16[2,2,24,1024]{3,2,1,0:T(8,128)(2,1)S(1)} %get-tuple-element.37), channel_id=1, source_target_pairs={{0,1},{1,0},{2,3},{3,2},{4,5},{5,4},{6,7},{7,6},{8,9},{9,8},{10,11... | collective-permute-start | bytes 589832 | tf_op jit(solution)/shard_map/ppermute | solution.py:274
  19.2 5.3 %collective-permute-start.4 = (bf16[2,24,1024]{2,1,0:T(8,128)(2,1)S(1)}, bf16[2,24,1024]{2,1,0:T(8,128)(2,1)S(1)}, u32[]{:S(2)}, u32[]{:S(2)}) collective-permute-start(bf16[2,24,1024]{2,1,0:T(8,128)(2,1)S(1)} %get-tuple-element.45), channel_id=1, source_target_pairs={{0,16},{16,0},{1,17},{17,1},{2,18},{18,2},{3,19},{19,3},{4,20},{20... | collective-permute-start | bytes 294920 | tf_op jit(solution)/shard_map/ppermute | solution.py:274
  24.5 4.2 %collective-permute-start.19 = (bf16[24,1024]{1,0:T(8,128)(2,1)S(1)}, bf16[24,1024]{1,0:T(8,128)(2,1)S(1)}, u32[]{:S(2)}, u32[]{:S(2)}) collective-permute-start(bf16[24,1024]{1,0:T(8,128)(2,1)S(1)} %get-tuple-element.47), channel_id=1, source_target_pairs={{0,2},{2,0},{1,3},{3,1},{4,6},{6,4},{5,7},{7,5},{8,10},{10,8},{9,1... | collective-permute-start | bytes 147464 | tf_op jit(solution)/shard_map/ppermute | solution.py:274
  26.1 4.2 %collective-permute-start.5 = (bf16[2,2,24,1024]{3,2,1,0:T(8,128)(2,1)S(1)}, bf16[2,2,24,1024]{3,2,1,0:T(8,128)(2,1)S(1)}, u32[]{:S(2)}, u32[]{:S(2)}) collective-permute-start(bf16[2,2,24,1024]{3,2,1,0:T(8,128)(2,1)S(1)} %get-tuple-element.40), channel_id=1, source_target_pairs={{0,1},{1,0},{2,3},{3,2},{4,5},{5,4},{6,7},{7,6},{8,9},{9,8},{10,11... | collective-permute-start | bytes 589832 | tf_op jit(solution)/shard_map/ppermute | solution.py:274
  26.1 28.0 %copy-start = (bf16[128,4096]{1,0:T(8,128)(2,1)S(1)}, bf16[128,4096]{1,0:T(8,128)(2,1)}, u32[]{:S(2)}) copy-start(bf16[128,4096]{1,0:T(8,128)(2,1)} %refs_19_.1) | copy-start | bytes 3145732
  28.7 5.3 %collective-permute-start.20 = (bf16[24,1024]{1,0:T(8,128)(2,1)S(1)}, bf16[24,1024]{1,0:T(8,128)(2,1)S(1)}, u32[]{:S(2)}, u32[]{:S(2)}) collective-permute-start(bf16[24,1024]{1,0:T(8,128)(2,1)S(1)} %add_convert_fusion.5), channel_id=1, source_target_pairs={{0,4},{4,0},{8,12},{12,8},{1,5},{5,1},{9,13},{13,9},{2,6},{6,2},{1... | collective-permute-start | bytes 147464 | tf_op jit(solution)/shard_map/ppermute | solution.py:274
  30.4 6.2 %collective-permute-start.6 = (bf16[24,1024]{1,0:T(8,128)(2,1)S(1)}, bf16[24,1024]{1,0:T(8,128)(2,1)S(1)}, u32[]{:S(2)}, u32[]{:S(2)}) collective-permute-start(bf16[24,1024]{1,0:T(8,128)(2,1)S(1)} %get-tuple-element.42), channel_id=1, source_target_pairs={{0,18},{2,16},{16,2},{18,0},{1,19},{3,17},{17,3},{19,1},{4,22},{6,... | collective-permute-start | bytes 147464 | tf_op jit(solution)/shard_map/ppermute | solution.py:274
  32.0 4.6 %collective-permute-start.8 = (bf16[24,1024]{1,0:T(8,128)(2,1)S(1)}, bf16[24,1024]{1,0:T(8,128)(2,1)S(1)}, u32[]{:S(2)}, u32[]{:S(2)}) collective-permute-start(bf16[24,1024]{1,0:T(8,128)(2,1)S(1)} %get-tuple-element.43), channel_id=1, source_target_pairs={{0,2},{2,0},{16,18},{18,16},{1,3},{3,1},{17,19},{19,17},{4,6},{6,4... | collective-permute-start | bytes 147464 | tf_op jit(solution)/shard_map/ppermute | solution.py:274
  32.5 4.1 %collective-permute-start.7 = (bf16[24,1024]{1,0:T(8,128)(2,1)S(1)}, bf16[24,1024]{1,0:T(8,128)(2,1)S(1)}, u32[]{:S(2)}, u32[]{:S(2)}) collective-permute-start(bf16[24,1024]{1,0:T(8,128)(2,1)S(1)} %get-tuple-element.44), channel_id=1, source_target_pairs={{0,16},{2,18},{16,0},{18,2},{1,17},{3,19},{17,1},{19,3},{4,20},{6,... | collective-permute-start | bytes 147464 | tf_op jit(solution)/shard_map/ppermute | solution.py:274
  34.0 7.2 %collective-permute-start.21 = (bf16[24,1024]{1,0:T(8,128)(2,1)S(1)}, bf16[24,1024]{1,0:T(8,128)(2,1)S(1)}, u32[]{:S(2)}, u32[]{:S(2)}) collective-permute-start(bf16[24,1024]{1,0:T(8,128)(2,1)S(1)} %add_convert_fusion.4), channel_id=1, source_target_pairs={{0,8},{4,12},{8,0},{12,4},{1,9},{5,13},{9,1},{13,5},{2,10},{6,14},... | collective-permute-start | bytes 147464 | tf_op jit(solution)/shard_map/ppermute | solution.py:274
  36.7 6.1 %collective-permute-start.11 = (bf16[24,1024]{1,0:T(8,128)(2,1)S(1)}, bf16[24,1024]{1,0:T(8,128)(2,1)S(1)}, u32[]{:S(2)}, u32[]{:S(2)}) collective-permute-start(bf16[24,1024]{1,0:T(8,128)(2,1)S(1)} %fusion.2), channel_id=1, source_target_pairs={{0,4},{4,0},{8,12},{12,8},{1,5},{5,1},{9,13},{13,9},{2,6},{6,2},{1... | collective-permute-start | bytes 147464 | tf_op jit(solution)/shard_map/ppermute | solution.py:274
  37.2 5.6 %collective-permute-start.10 = (bf16[24,1024]{1,0:T(8,128)(2,1)S(1)}, bf16[24,1024]{1,0:T(8,128)(2,1)S(1)}, u32[]{:S(2)}, u32[]{:S(2)}) collective-permute-start(bf16[24,1024]{1,0:T(8,128)(2,1)S(1)} %fusion.2), channel_id=1, source_target_pairs={{0,8},{4,12},{8,0},{12,4},{1,9},{5,13},{9,1},{13,5},{2,10},{6,14},... | collective-permute-start | bytes 147464 | tf_op jit(solution)/shard_map/ppermute | solution.py:274
  39.8 5.9 %collective-permute-start.9 = (bf16[24,1024]{1,0:T(8,128)(2,1)S(1)}, bf16[24,1024]{1,0:T(8,128)(2,1)S(1)}, u32[]{:S(2)}, u32[]{:S(2)}) collective-permute-start(bf16[24,1024]{1,0:T(8,128)(2,1)S(1)} %fusion.2), channel_id=1, source_target_pairs={{0,12},{4,8},{8,4},{12,0},{1,13},{5,9},{9,5},{13,1},{2,14},{6,10},... | collective-permute-start | bytes 147464 | tf_op jit(solution)/shard_map/ppermute | solution.py:274
  41.1 8.1 %collective-permute-start.23 = (bf16[24,1024]{1,0:T(8,128)(2,1)S(1)}, bf16[24,1024]{1,0:T(8,128)(2,1)S(1)}, u32[]{:S(2)}, u32[]{:S(2)}) collective-permute-start(bf16[24,1024]{1,0:T(8,128)(2,1)S(1)} %add_convert_fusion.3.refs_14_), channel_id=1, source_target_pairs={{0,1},{1,0},{2,3},{3,2},{4,5},{5,4},{6,7},{7,6},{8,9},{9,8},{10,11... | collective-permute-start | bytes 147464 | tf_op jit(solution)/shard_map/ppermute | solution.py:274
  41.2 8.0 %collective-permute-start.22 = (bf16[24,1024]{1,0:T(8,128)(2,1)S(1)}, bf16[24,1024]{1,0:T(8,128)(2,1)S(1)}, u32[]{:S(2)}, u32[]{:S(2)}) collective-permute-start(bf16[24,1024]{1,0:T(8,128)(2,1)S(1)} %add_convert_fusion.3.refs_14_), channel_id=1, source_target_pairs={{0,2},{2,0},{1,3},{3,1},{4,6},{6,4},{5,7},{7,5},{8,10},{10,8},{9,1... | collective-permute-start | bytes 147464 | tf_op jit(solution)/shard_map/ppermute | solution.py:274
  45.7 5.1 %collective-permute-start.14 = (bf16[24,1024]{1,0:T(8,128)(2,1)S(1)}, bf16[24,1024]{1,0:T(8,128)(2,1)S(1)}, u32[]{:S(2)}, u32[]{:S(2)}) collective-permute-start(bf16[24,1024]{1,0:T(8,128)(2,1)S(1)} %add_convert_fusion.6.refs_6_), channel_id=1, source_target_pairs={{0,18},{2,16},{16,2},{18,0},{1,19},{3,17},{17,3},{19,1},{4,22},{6,... | collective-permute-start | bytes 147464 | tf_op jit(solution)/shard_map/ppermute | solution.py:274
  48.1 4.1 %collective-permute-start.13 = (bf16[24,1024]{1,0:T(8,128)(2,1)S(1)}, bf16[24,1024]{1,0:T(8,128)(2,1)S(1)}, u32[]{:S(2)}, u32[]{:S(2)}) collective-permute-start(bf16[24,1024]{1,0:T(8,128)(2,1)S(1)} %add_convert_fusion.6.refs_6_), channel_id=1, source_target_pairs={{0,16},{2,18},{16,0},{18,2},{1,17},{3,19},{17,1},{19,3},{4,20},{6,... | collective-permute-start | bytes 147464 | tf_op jit(solution)/shard_map/ppermute | solution.py:274
  48.7 4.1 %collective-permute-start.12 = (bf16[24,1024]{1,0:T(8,128)(2,1)S(1)}, bf16[24,1024]{1,0:T(8,128)(2,1)S(1)}, u32[]{:S(2)}, u32[]{:S(2)}) collective-permute-start(bf16[24,1024]{1,0:T(8,128)(2,1)S(1)} %add_convert_fusion.6.refs_6_), channel_id=1, source_target_pairs={{0,2},{2,0},{16,18},{18,16},{1,3},{3,1},{17,19},{19,17},{4,6},{6,4... | collective-permute-start | bytes 147464 | tf_op jit(solution)/shard_map/ppermute | solution.py:274
  49.2 3.6 %collective-permute-start.15 = (bf16[24,1024]{1,0:T(8,128)(2,1)S(1)}, bf16[24,1024]{1,0:T(8,128)(2,1)S(1)}, u32[]{:S(2)}, u32[]{:S(2)}) collective-permute-start(bf16[24,1024]{1,0:T(8,128)(2,1)S(1)} %add_convert_fusion.6.refs_6_), channel_id=1, source_target_pairs={{0,1},{1,0},{2,3},{3,2},{4,5},{5,4},{6,7},{7,6},{8,9},{9,8},{10,11... | collective-permute-start | bytes 147464 | tf_op jit(solution)/shard_map/ppermute | solution.py:274
  49.2 3.6 %collective-permute-start.24 = (bf16[24,1024]{1,0:T(8,128)(2,1)S(1)}, bf16[24,1024]{1,0:T(8,128)(2,1)S(1)}, u32[]{:S(2)}, u32[]{:S(2)}) collective-permute-start(bf16[24,1024]{1,0:T(8,128)(2,1)S(1)} %collective-permute-done.22.refs_15_), channel_id=1, source_target_pairs={{0,1},{1,0},{2,3},{3,2},{4,5},{5,4},{6,7},{7,6},{8,9},{9,8},{10,11... | collective-permute-start | bytes 147464 | tf_op jit(solution)/shard_map/ppermute | solution.py:274
  50.7 2.1 %collective-permute-start.18 = (bf16[24,1024]{1,0:T(8,128)(2,1)S(1)}, bf16[24,1024]{1,0:T(8,128)(2,1)S(1)}, u32[]{:S(2)}, u32[]{:S(2)}) collective-permute-start(bf16[24,1024]{1,0:T(8,128)(2,1)S(1)} %collective-permute-done.14.refs_9_), channel_id=1, source_target_pairs={{0,1},{1,0},{2,3},{3,2},{4,5},{5,4},{6,7},{7,6},{8,9},{9,8},{10,11... | collective-permute-start | bytes 147464 | tf_op jit(solution)/shard_map/ppermute | solution.py:274
  52.2 1.2 %collective-permute-start.17 = (bf16[24,1024]{1,0:T(8,128)(2,1)S(1)}, bf16[24,1024]{1,0:T(8,128)(2,1)S(1)}, u32[]{:S(2)}, u32[]{:S(2)}) collective-permute-start(bf16[24,1024]{1,0:T(8,128)(2,1)S(1)} %collective-permute-done.13.refs_8_), channel_id=1, source_target_pairs={{0,1},{1,0},{2,3},{3,2},{4,5},{5,4},{6,7},{7,6},{8,9},{9,8},{10,11... | collective-permute-start | bytes 147464 | tf_op jit(solution)/shard_map/ppermute | solution.py:274
  52.8 1.2 %collective-permute-start.16 = (bf16[24,1024]{1,0:T(8,128)(2,1)S(1)}, bf16[24,1024]{1,0:T(8,128)(2,1)S(1)}, u32[]{:S(2)}, u32[]{:S(2)}) collective-permute-start(bf16[24,1024]{1,0:T(8,128)(2,1)S(1)} %collective-permute-done.12.refs_7_), channel_id=1, source_target_pairs={{0,1},{1,0},{2,3},{3,2},{4,5},{5,4},{6,7},{7,6},{8,9},{9,8},{10,11... | collective-permute-start | bytes 147464 | tf_op jit(solution)/shard_map/ppermute | solution.py:274

commit v6 on v5

--- a/solution.py
+++ b/solution.py
@@ -29,14 +29,11 @@
     return jnp.concatenate([ref[:, columns].astype(F32) for ref in refs], axis=0)
 
 
-def own_columns(ids, i, j, width):
-    return ((ids[1] ^ j) * 2 + (ids[2] ^ i)) * width
-
-
-def store_blocks(out_ref, j, columns, value, count):
+def store_blocks(place_of, columns, value, count):
     rows = value.shape[0] // count
     for k in range(count):
-        out_ref[k, j, :, columns] = value[k * rows : (k + 1) * rows].astype(BF16)
+        ref, lead = place_of(k)
+        ref[(*lead, slice(None), columns)] = value[k * rows : (k + 1) * rows].astype(BF16)
 
 
 def load_kernel(n_dp, ids, w_gate, w_up, hid, grads, gain, named, weights, context, *refs):
@@ -126,35 +123,38 @@
 
 def outward_kernel(n_dp, ids, *refs):
     smalls = refs[:n_dp]
-    act, w_down, send, keep = refs[2 * n_dp :]
+    act, w_down, target = refs[2 * n_dp :]
     weight = gates_of(smalls)
-    chunk = send.shape[3]
+    chunk = target.shape[3]
     few = act.shape[0] <= FEW_ROWS
-    for i, target in ((1, send), (0, keep)):
-        for j in range(2):
-            first = own_columns(ids, i, j, chunk)
-
-            def outward(step):
-                columns = pl.ds(pl.multiple_of(first + step * STEP, STEP), STEP)
-                part = weight * dot(act[...], w_down[:, columns], ((1,), (0,)))
-                store_blocks(target, j, pl.ds(place(step, STEP), STEP), part, n_dp)
-
-            loop(chunk // STEP, outward, few)
-
-
-def inward_part(ids, i, n_dp, grad_gate, grad_up, w_gate, w_up, target):
-    chunk = target.shape[3]
+    for j in range(2):
+        first = (ids[1] ^ j) * chunk
+
+        def outward(step):
+            columns = pl.ds(pl.multiple_of(first + step * STEP, STEP), STEP)
+            part = weight * dot(act[...], w_down[:, columns], ((1,), (0,)))
+            store_blocks(lambda k: (target, (k, j)), pl.ds(place(step, STEP), STEP), part, n_dp)
+
+        loop(chunk // STEP, outward, few)
+
+
+def inward_last_kernel(n_dp, ids, grad_gate, grad_up, w_gate, w_up, waiting, earlier, target, passed):
+    passed[...] = waiting[...]
+    inward_kernel(0, n_dp, ids, grad_gate, grad_up, w_gate, w_up, target)
+
+
+def inward_kernel(j, n_dp, ids, grad_gate, grad_up, w_gate, w_up, target):
+    chunk = target.shape[2]
     few = grad_gate.shape[0] <= FEW_ROWS
-    for j in range(2):
-        first = own_columns(ids, i, j, chunk)
-
-        def inward(step):
-            columns = pl.ds(pl.multiple_of(first + step * STEP, STEP), STEP)
-            part = dot(grad_gate[...], w_gate[columns, :], ((1,), (1,)))
-            part = part + dot(grad_up[...], w_up[columns, :], ((1,), (1,)))
-            store_blocks(target, j, pl.ds(place(step, STEP), STEP), part, n_dp)
-
-        loop(chunk // STEP, inward, few)
+    first = (ids[1] ^ j) * chunk
+
+    def inward(step):
+        columns = pl.ds(pl.multiple_of(first + step * STEP, STEP), STEP)
+        part = dot(grad_gate[...], w_gate[columns, :], ((1,), (1,)))
+        part = part + dot(grad_up[...], w_up[columns, :], ((1,), (1,)))
+        store_blocks(lambda k: (target, (k,)), pl.ds(place(step, STEP), STEP), part, n_dp)
+
+    loop(chunk // STEP, inward, few)
 
 
 def backward_kernel(n_dp, ids, *refs):
@@ -181,25 +181,21 @@
     loop(w_down.shape[0] // STEP, hidden_units, few)
 
 
-def inward_kernel(i, n_dp, ids, grad_gate, grad_up, w_gate, w_up, waiting, target, passed):
-    passed[...] = waiting[...]
-    inward_part(ids, i, n_dp, grad_gate, grad_up, w_gate, w_up, target)
-
-
 def finish_kernel(n_dp, ids, *refs):
     hid, grads, smalls = refs[:n_dp], refs[n_dp : 2 * n_dp], refs[2 * n_dp : 3 * n_dp]
     back, moe = refs[3 * n_dp : 7 * n_dp], refs[7 * n_dp : 7 * n_dp + 4]
     gain, w_out, output, d_hidden, d_context, d_w_out, summed, d_all = refs[7 * n_dp + 4 :]
     rows, width = hid[0].shape
     chunk = moe[0].shape[1]
-    for i in range(2):
-        for j in range(2):
-            columns = pl.ds(pl.multiple_of(own_columns(ids, i, j, chunk), chunk), chunk)
-            for k in range(n_dp):
-                piece = back[(i * n_dp + k) * 2 + j]
-                summed[k * rows : (k + 1) * rows, columns] = piece[...].astype(F32) * gain[:, columns]
-            piece = moe[i * 2 + j]
-            output[:, columns] = (hid[0][:, columns].astype(F32) + piece[...].astype(F32)).astype(BF16)
+    first_core = ids[2] == 0
+    for j in range(2):
+        columns = pl.ds(pl.multiple_of((ids[1] ^ j) * chunk, chunk), chunk)
+        for k in range(n_dp):
+            here, there = back[k * 2 + j], back[(n_dp + k) * 2 + j]
+            piece = jnp.where(first_core, here[...].astype(F32), there[...].astype(F32))
+            summed[k * rows : (k + 1) * rows, columns] = piece * gain[:, columns]
+        piece = jnp.where(first_core, moe[2 + j][...].astype(F32), moe[j][...].astype(F32))
+        output[:, columns] = (hid[0][:, columns].astype(F32) + piece).astype(BF16)
 
     few = rows * n_dp <= FEW_ROWS
     squares = jnp.zeros((rows * n_dp, 1), F32)
@@ -262,23 +258,28 @@
     me, hi, y, c = (lax.axis_index(name) for name in ("dp", "hi", "y", "c"))
     rows, width = hidden_in.shape
     top, heads = route_ids.shape[1], context.shape[1]
-    all_rows, units, chunk = n_dp * rows, w_gate.shape[2], width // 4
+    all_rows, units, chunk = n_dp * rows, w_gate.shape[2], width // 2
     expert = (hi * 2 + y) * 2 + c
     ids = jnp.stack([me, y, c, expert]).astype(jnp.int32)
 
-    def swap(value, axes, turn):
-        sizes = [lax.axis_size(name) for name in axes]
+    def swap(value, axes, turn, core=None):
         count = 1
-        for size in sizes:
-            count *= size
-        return lax.ppermute(value, axes, [(i, i ^ turn) for i in range(count)])
+        for name in axes:
+            count *= lax.axis_size(name)
+        if core is None:
+            return lax.ppermute(value, axes, [(i, i ^ turn) for i in range(count)])
+        pairs = [(2 * i + core, 2 * (i ^ turn) + core) for i in range(count)]
+        return lax.ppermute(value, axes + ("c",), pairs)
+
+    def hand_over(value, core):
+        return lax.ppermute(value, ("c",), [(core, 1 - core)])
 
     def all_blocks(value, own=None):
         own = value if own is None else own
         return [own] + [swap(value, ("dp",), k) for k in range(1, n_dp)]
 
     weights = 2 * width * units
-    shares = ((n_dp, 2, rows, chunk), BF16)
+    shares = ((n_dp, rows, chunk), BF16)
     wg, wu, hid_own, grads_own, gain, small_own = run(
         load_kernel, n_dp, ids,
         [w_gate[0], w_up[0], hidden_in, grad_out, norm_gain.reshape(1, width), route_ids.T, route_gates.T, context],
@@ -306,42 +307,43 @@
         [((all_rows, units), F32), ((all_rows, units), F32), ((all_rows, units), BF16), ((units, width), BF16)],
         [pltpu.VMEM((all_rows, width), BF16), pltpu.SemaphoreType.DMA], 2 * weights, "hidden", far=(n_dp + 3,),
     )
-    out_send, out_keep = run(
-        outward_kernel, n_dp, ids, smalls + grads + [act, wd], [shares, shares], [], weights, "outward"
-    )
-    out_other = swap(out_send, ("c",), 1)
-    grad_gate, grad_up, out_keep = run(
-        backward_kernel, n_dp, ids, grads + smalls + [pre_gate, pre_up, wd, out_keep],
-        [((all_rows, units), BF16), ((all_rows, units), BF16), shares],
+    (out_part,) = run(
+        outward_kernel, n_dp, ids, smalls + grads + [act, wd], [((n_dp, 2, rows, chunk), BF16)], [],
+        weights, "outward",
+    )
+    out_other = hand_over(out_part, 0)
+    grad_gate, grad_up, out_part = run(
+        backward_kernel, n_dp, ids, grads + smalls + [pre_gate, pre_up, wd, out_part],
+        [((all_rows, units), BF16), ((all_rows, units), BF16), ((n_dp, 2, rows, chunk), BF16)],
         [pltpu.VMEM((all_rows, width), BF16)], weights, "backward",
     )
-    out_half = add(out_keep, out_other)
-    out_blocks = [swap(out_half[k], ("dp",), k) for k in range(1, n_dp)]
-    in_send, out_block = run(
-        functools.partial(inward_kernel, 1), n_dp, ids, [grad_gate, grad_up, wg, wu, out_half[0]],
-        [shares, (shares[0][1:], BF16)], [], weights, "inward_send",
-    )
-    in_other = swap(in_send, ("c",), 1)
-    out_block = total_of([out_block] + out_blocks)
-    out_other = swap(out_block[1], ("y",), 1)
-    in_keep, out_share = run(
-        functools.partial(inward_kernel, 0), n_dp, ids, [grad_gate, grad_up, wg, wu, out_block[0]],
-        [shares, (shares[0][2:], BF16)], [], weights, "inward_keep",
-    )
-    out_total = add(out_share, out_other)
-    in_half = add(in_keep, in_other)
+    (in_part,) = run(
+        functools.partial(inward_kernel, 1), n_dp, ids, [grad_gate, grad_up, wg, wu], [shares], [],
+        weights, "inward_first",
+    )
+    in_other = hand_over(in_part, 1)
+    out_sum = add(out_part, out_other)
+    last_part, in_part = run(
+        inward_last_kernel, n_dp, ids, [grad_gate, grad_up, wg, wu, in_part, out_sum[0]], [shares, shares], [],
+        weights, "inward_last",
+    )
+    in_sums = [add(last_part, hand_over(last_part, 1)), add(in_part, in_other)]
     turns = [t for t in range(2 * n_dp - 1, 0, -1)]
-    in_share = total_of([in_half[0, 0]] + [swap(in_half[t // 2, t % 2], ("dp", "y"), t) for t in turns])
-    in_total = total_of([in_share] + [swap(in_share, ("hi",), t) for t in range(n_hi - 1, 0, -1)])
+    in_share = total_of(
+        [in_sums[0][0]] + [swap(in_sums[t % 2][t // 2], ("dp", "y"), t, 0) for t in turns]
+    )
+    in_total = total_of([in_share] + [swap(in_share, ("hi",), t, 0) for t in range(1, n_hi)])
+    out_block = total_of([out_sum[0]] + [swap(out_sum[k], ("dp",), k, 1) for k in range(1, n_dp)])
+    out_total = add(out_block[0], swap(out_block[1], ("y",), 1, 1))
     turn = 1
     while turn < n_hi:
-        out_total = add(out_total, swap(out_total, ("hi",), turn))
+        out_total = add(out_total, swap(out_total, ("hi",), turn, 1))
         turn = 2 * turn
-    spread = {t: swap(in_total, ("dp", "y"), t) for t in turns}
+    spread = {t: swap(in_total, ("dp", "y"), t, 0) for t in turns}
     back = [in_total] + [spread[t] for t in range(1, 2 * n_dp)]
-    moe = [out_total, swap(out_total, ("y",), 1)]
-    back = back + [swap(piece, ("c",), 1) for piece in back]
-    moe = moe + [swap(piece, ("c",), 1) for piece in moe]
+    moe = [out_total, swap(out_total, ("y",), 1, 1)]
+    back = back + [hand_over(piece, 0) for piece in back]
+    moe = moe + [hand_over(piece, 1) for piece in moe]
     return run(
         finish_kernel, n_dp, ids, hid + grads + smalls + back + moe + [gain, w_out],
         [((rows, width), BF16), ((rows, width), BF16), ((rows, heads), BF16), ((heads, width // n_dp), BF16)],

time: 56.5 us -> 82.1 us (1.45)
  starting transfers between devices: 25.5 us -> 50.4 us
    ppermute x0 -> x23, starting transfers between devices: none -> 45.3 us  [the longest x14 31.9 us: swap(): return lax.ppermute(value, axes + ('c',), pairs)]
    ppermute x25 -> x3, starting transfers between devices: 25.5 us -> 5.09 us  [swap(): return lax.ppermute(value, axes, [(i, i ^ turn) for i in range(count)])]
    ppermute x25 -> x3, waiting for transfers between devices: 9.24 us -> 0.01 us  [swap(): return lax.ppermute(value, axes, [(i, i ^ turn) for i in range(count)])]
    ppermute x0 -> x23, waiting for transfers between devices: none -> 8.77 us  [the longest x14 5.63 us: swap(): return lax.ppermute(value, axes + ('c',), pairs)]
  transfers between devices with their start and end apart: 25 -> 26, of which waited for: 7 -> 5; matrix products, arithmetic and copies ran while one was open for 0% -> 1% of each run, Pallas kernels for 29% -> 20%
where the time goes in v6:
time: 82.1 us; the launch traced here: 81.5 us
  starting transfers between devices  50.4 us (61%)
  Pallas kernels  20.6 us (25%)
  waiting for transfers between devices  8.78 us (11%)
  between operations  1.12 us (1%)
    ppermute x14, starting transfers between devices, swap(): return lax.ppermute(value, axes + ('c',), pairs)  31.9 us
    pallas_call x7, Pallas kernels, run(): pl.pallas_call(functools.partial(kernel, n_dp), out_shape=kinds, in_specs...  20.6 us
    ppermute x9, starting transfers between devices, hand_over(): return lax.ppermute(value, ('c',), [(core, 1 - core)])  13.4 us
    ppermute x14, waiting for transfers between devices, swap(): return lax.ppermute(value, axes + ('c',), pairs)  5.63 us
    ppermute x3, starting transfers between devices, swap(): return lax.ppermute(value, axes, [(i, i ^ turn) for i in range(count)])  5.09 us
    ppermute x9, waiting for transfers between devices, hand_over(): return lax.ppermute(value, ('c',), [(core, 1 - core)])  3.15 us
  transfers between devices with their start and end apart: 26, of which 5 were waited for; matrix products, arithmetic and copies ran while one was open for 1% of the time, Pallas kernels for 20%

profile of v6, /device:TPU:0, one launch (start us, length us, event | category | flops | bytes accessed | tf_op | source)
XLA Modules:
  0.0 81.5 jit_solution(3587571827140087173)
XLA Ops:
  0.6 3.0 %collective-permute-start = (bf16[24,4096]{1,0:T(8,128)(2,1)}, bf16[24,4096]{1,0:T(8,128)(2,1)S(1)}, u32[]{:S(2)}, u32[]{:S(2)}) collective-permute-start(bf16[24,4096]{1,0:T(8,128)(2,1)} %hid.1), channel_id=1, source_target_pairs={{0,16},{16,0},{1,17},{17,1},{2,18},{18,2},{3,19},{19,3},{4,20},{20... | collective-permute-start | bytes 589832 | tf_op jit(solution)/shard_map/ppermute | solution.py:270
  3.6 0.1 collective-permute-start.1
  3.7 0.1 pad_add_fusion.ids
  3.8 5.4 %load.1 = (bf16[4096,768]{1,0:T(8,128)(2,1)S(1)}, bf16[4096,768]{1,0:T(8,128)(2,1)S(1)}, bf16[24,4096]{1,0:T(8,128)(2,1)S(1)}, bf16[24,4096]{1,0:T(8,128)(2,1)S(...) custom-call(s32[4]{0:T(128)S(1)} %pad_add_fusion.ids, bf16[4096,768]{1,0:T(8,128)(2,1)} %bitcast.34, ...), custom_call_target="tpu_custom_call" | custom-call | bytes 12582912 | tf_op jit(solution)/shard_map/load/pallas_call | solution.py:241
  9.2 2.0 %collective-permute-start.2 = (f32[24,256]{1,0:T(8,128)S(1)}, f32[24,256]{1,0:T(8,128)S(1)}, u32[]{:S(2)}, u32[]{:S(2)}) collective-permute-start(f32[24,256]{1,0:T(8,128)S(1)} %get-tuple-element.21.refs_0_.refs_2_.refs_4_), channel_id=1, source_target_pairs={{0,16},{16,0},{1,17},{17,1},{2,18},{18,2},{3,19},{19,3},{4,20},{20... | collective-permute-start | bytes 73736 | tf_op jit(solution)/shard_map/ppermute | solution.py:270
  11.2 0.0 collective-permute-done.refs_1_
  11.2 3.3 %hidden.1 = (f32[48,768]{1,0:T(8,128)S(1)}, f32[48,768]{1,0:T(8,128)S(1)}, bf16[48,768]{1,0:T(8,128)(2,1)S(1)}, bf16[768,4096]{1,0:T(8,128)(2,1)S(1)}) custom-call(s32[4]{0:T(128)S(1)} %pad_add_fusion.ids, bf16[24,4096]{1,0:T(8,128)(2,1)S(1)} %get-tuple-element.19.refs_0_, bf16[24,4096]{1,0:T(8,128)(2,1)S(1)} %collective-permute-done.refs_1_, ...), custom_call_target="tpu_custom_call" | custom-call | bytes 12582912 | tf_op jit(solution)/shard_map/hidden/pallas_call | solution.py:241
  14.6 0.0 collective-permute-done.1.refs_3_.refs_1_
  14.6 1.8 %outward.1.refs_7_ = bf16[2,2,24,2048]{3,2,1,0:T(8,128)(2,1)S(1)} custom-call(s32[4]{0:T(128)S(1)} %pad_add_fusion.ids, f32[24,256]{1,0:T(8,128)S(1)} %get-tuple-element.21.refs_0_.refs_2_.refs_4_, f32[24,256]{1,0:T(8,128)S(1)} %collective-permute-done.2.refs_1_.refs_3_.refs_5_, bf16[24,4096]{1,0:T(8,128)(2,1)S(1)} %get-tuple-element.20.refs_2_.refs_0_, ...), custom_call_target="tpu_custom_call" | custom-call | bytes 6291456 | tf_op jit(solution)/shard_map/outward/pallas_call | solution.py:241
  16.4 1.3 %collective-permute-start.3 = (bf16[2,2,24,2048]{3,2,1,0:T(8,128)(2,1)S(1)}, bf16[2,2,24,2048]{3,2,1,0:T(8,128)(2,1)S(1)}, u32[]{:S(2)}, u32[]{:S(2)}) collective-permute-start(bf16[2,2,24,2048]{3,2,1,0:T(8,128)(2,1)S(1)} %outward.1.refs_7_), channel_id=1, source_target_pairs={{0,1},{2,3},{4,5},{6,7},{8,9},{10,11},{12,13},{14,15},{16,17},{18,... | collective-permute-start | bytes 1179656 | tf_op jit(solution)/shard_map/ppermute | solution.py:275
  17.7 2.6 %backward.1 = (bf16[48,768]{1,0:T(8,128)(2,1)S(1)}, bf16[48,768]{1,0:T(8,128)(2,1)S(1)}, bf16[2,2,24,2048]{3,2,1,0:T(8,128)(2,1)S(1)}) custom-call(s32[4]{0:T(128)S(1)} %pad_add_fusion.ids, bf16[24,4096]{1,0:T(8,128)(2,1)S(1)} %get-tuple-element.20.refs_2_.refs_0_, bf16[24,4096]{1,0:T(8,128)(2,1)S(1)} %collective-permute-done.1.refs_3_.refs_1_, ...), custom_call_target="tpu_custom_call" | custom-call | bytes 6291456 | tf_op jit(solution)/shard_map/backward/pallas_call | solution.py:241
  20.3 2.5 %inward_first.1.waiting = bf16[2,24,2048]{2,1,0:T(8,128)(2,1)S(1)} custom-call(s32[4]{0:T(128)S(1)} %pad_add_fusion.ids, bf16[48,768]{1,0:T(8,128)(2,1)S(1)} %get-tuple-element.29.grad_gate, bf16[48,768]{1,0:T(8,128)(2,1)S(1)} %get-tuple-element.30.grad_up, bf16[4096,768]{1,0:T(8,128)(2,1)S(1)} %get-tuple-element.23.refs_3_.w_gate, ...), custom_call_target="tpu_custom_call" | custom-call | bytes 6291456 | tf_op jit(solution)/shard_map/inward_first/pallas_call | solution.py:241
  22.9 1.3 %collective-permute-start.5 = (bf16[2,24,2048]{2,1,0:T(8,128)(2,1)S(1)}, bf16[2,24,2048]{2,1,0:T(8,128)(2,1)S(1)}, u32[]{:S(2)}, u32[]{:S(2)}) collective-permute-start(bf16[2,24,2048]{2,1,0:T(8,128)(2,1)S(1)} %inward_first.1.waiting), channel_id=1, source_target_pairs={{1,0},{3,2},{5,4},{7,6},{9,8},{11,10},{13,12},{15,14},{17,16},{19,... | collective-permute-start | bytes 589832 | tf_op jit(solution)/shard_map/ppermute | solution.py:275
  24.2 0.0 collective-permute-done.3
  24.2 0.1 add_convert_fusion
  24.3 0.0 copy-start
  24.3 2.5 %inward_last.1 = (bf16[2,24,2048]{2,1,0:T(8,128)(2,1)S(1)}, bf16[2,24,2048]{2,1,0:T(8,128)(2,1)S(1)}) custom-call(s32[4]{0:T(128)S(1)} %pad_add_fusion.ids, bf16[48,768]{1,0:T(8,128)(2,1)S(1)} %get-tuple-element.29.grad_gate, bf16[48,768]{1,0:T(8,128)(2,1)S(1)} %get-tuple-element.30.grad_up, bf16[4096,768]{1,0:T(8,128)(2,1)S(1)} %get-tuple-element.23.refs_3_.w_gate, ...), custom_call_target="tpu_custom_call" | custom-call | bytes 6291456 | tf_op jit(solution)/shard_map/inward_last/pallas_call | solution.py:241
  26.8 0.7 collective-permute-start.19
  27.6 3.5 %collective-permute-start.6 = (bf16[24,2048]{1,0:T(8,128)(2,1)S(1)}, bf16[24,2048]{1,0:T(8,128)(2,1)S(1)}, u32[]{:S(2)}, u32[]{:S(2)}) collective-permute-start(bf16[24,2048]{1,0:T(8,128)(2,1)S(1)} %get-tuple-element.36), channel_id=1, source_target_pairs={{0,18},{2,16},{16,2},{18,0},{4,22},{6,20},{20,6},{22,4},{8,26},{10... | collective-permute-start | bytes 294920 | tf_op jit(solution)/shard_map/ppermute | solution.py:272
  31.1 2.4 %collective-permute-start.8 = (bf16[24,2048]{1,0:T(8,128)(2,1)S(1)}, bf16[24,2048]{1,0:T(8,128)(2,1)S(1)}, u32[]{:S(2)}, u32[]{:S(2)}) collective-permute-start(bf16[24,2048]{1,0:T(8,128)(2,1)S(1)} %get-tuple-element.37), channel_id=1, source_target_pairs={{0,2},{2,0},{16,18},{18,16},{4,6},{6,4},{20,22},{22,20},{8,10},{10... | collective-permute-start | bytes 294920 | tf_op jit(solution)/shard_map/ppermute | solution.py:272
  33.5 1.3 %collective-permute-start.4 = (bf16[2,24,2048]{2,1,0:T(8,128)(2,1)S(1)}, bf16[2,24,2048]{2,1,0:T(8,128)(2,1)S(1)}, u32[]{:S(2)}, u32[]{:S(2)}) collective-permute-start(bf16[2,24,2048]{2,1,0:T(8,128)(2,1)S(1)} %get-tuple-element.32), channel_id=1, source_target_pairs={{1,0},{3,2},{5,4},{7,6},{9,8},{11,10},{13,12},{15,14},{17,16},{19,... | collective-permute-start | bytes 589832 | tf_op jit(solution)/shard_map/ppermute | solution.py:275
  34.9 0.7 collective-permute-start.20
  35.6 1.3 %collective-permute-done.4 = bf16[2,24,2048]{2,1,0:T(8,128)(2,1)S(1)} collective-permute-done((bf16[2,24,2048]{2,1,0:T(8,128)(2,1)S(1)}, bf16[2,24,2048]{2,1,0:T(8,128)(2,1)S(1)}, u32[]{:S(2)}, u32[]{:S(2)}) %collective-permute-start.4) | collective-permute-done | bytes 196640 | tf_op jit(solution)/shard_map/ppermute | solution.py:275
  36.9 3.3 %collective-permute-start.7 = (bf16[24,2048]{1,0:T(8,128)(2,1)S(1)}, bf16[24,2048]{1,0:T(8,128)(2,1)S(1)}, u32[]{:S(2)}, u32[]{:S(2)}) collective-permute-start(bf16[24,2048]{1,0:T(8,128)(2,1)S(1)} %slice_bitcast_fusion.5), channel_id=1, source_target_pairs={{0,16},{2,18},{16,0},{18,2},{4,20},{6,22},{20,4},{22,6},{8,24},{10... | collective-permute-start | bytes 294920 | tf_op jit(solution)/shard_map/ppermute | solution.py:272
  40.3 0.0 collective-permute-done.20
  40.3 0.7 collective-permute-start.21
  41.0 2.4 %collective-permute-done.7 = bf16[24,2048]{1,0:T(8,128)(2,1)S(1)} collective-permute-done((bf16[24,2048]{1,0:T(8,128)(2,1)S(1)}, bf16[24,2048]{1,0:T(8,128)(2,1)S(1)}, u32[]{:S(2)}, u32[]{:S(2)}) %collective-permute-start.7) | collective-permute-done | bytes 98336 | tf_op jit(solution)/shard_map/ppermute | solution.py:272
  43.4 0.1 fusion.3
  43.5 5.5 %collective-permute-start.11 = (bf16[24,2048]{1,0:T(8,128)(2,1)S(1)}, bf16[24,2048]{1,0:T(8,128)(2,1)S(1)}, u32[]{:S(2)}, u32[]{:S(2)}) collective-permute-start(bf16[24,2048]{1,0:T(8,128)(2,1)S(1)} %fusion.3), channel_id=1, source_target_pairs={{0,12},{4,8},{8,4},{12,0},{2,14},{6,10},{10,6},{14,2},{16,28},{20,... | collective-permute-start | bytes 294920 | tf_op jit(solution)/shard_map/ppermute | solution.py:272
  49.0 1.9 %collective-permute-start.10 = (bf16[24,2048]{1,0:T(8,128)(2,1)S(1)}, bf16[24,2048]{1,0:T(8,128)(2,1)S(1)}, u32[]{:S(2)}, u32[]{:S(2)}) collective-permute-start(bf16[24,2048]{1,0:T(8,128)(2,1)S(1)} %fusion.3), channel_id=1, source_target_pairs={{0,8},{4,12},{8,0},{12,4},{2,10},{6,14},{10,2},{14,6},{16,24},{20,... | collective-permute-start | bytes 294920 | tf_op jit(solution)/shard_map/ppermute | solution.py:272
  50.9 2.7 %collective-permute-start.9 = (bf16[24,2048]{1,0:T(8,128)(2,1)S(1)}, bf16[24,2048]{1,0:T(8,128)(2,1)S(1)}, u32[]{:S(2)}, u32[]{:S(2)}) collective-permute-start(bf16[24,2048]{1,0:T(8,128)(2,1)S(1)} %fusion.3), channel_id=1, source_target_pairs={{0,4},{4,0},{8,12},{12,8},{2,6},{6,2},{10,14},{14,10},{16,20},{20,... | collective-permute-start | bytes 294920 | tf_op jit(solution)/shard_map/ppermute | solution.py:272
  53.6 0.0 collective-permute-done.21
  53.7 0.7 collective-permute-start.22
  54.4 2.1 %collective-permute-done.10 = bf16[24,2048]{1,0:T(8,128)(2,1)S(1)} collective-permute-done((bf16[24,2048]{1,0:T(8,128)(2,1)S(1)}, bf16[24,2048]{1,0:T(8,128)(2,1)S(1)}, u32[]{:S(2)}, u32[]{:S(2)}) %collective-permute-start.10) | collective-permute-done | bytes 98336 | tf_op jit(solution)/shard_map/ppermute | solution.py:272
  56.5 1.0 %collective-permute-done.9 = bf16[24,2048]{1,0:T(8,128)(2,1)S(1)} collective-permute-done((bf16[24,2048]{1,0:T(8,128)(2,1)S(1)}, bf16[24,2048]{1,0:T(8,128)(2,1)S(1)}, u32[]{:S(2)}, u32[]{:S(2)}) %collective-permute-start.9) | collective-permute-done | bytes 98336 | tf_op jit(solution)/shard_map/ppermute | solution.py:272
  57.5 0.1 add_convert_fusion.6.refs_6_
  57.6 1.3 %collective-permute-start.15 = (bf16[24,2048]{1,0:T(8,128)(2,1)S(1)}, bf16[24,2048]{1,0:T(8,128)(2,1)S(1)}, u32[]{:S(2)}, u32[]{:S(2)}) collective-permute-start(bf16[24,2048]{1,0:T(8,128)(2,1)S(1)} %add_convert_fusion.6.refs_6_), channel_id=1, source_target_pairs={{0,1},{2,3},{4,5},{6,7},{8,9},{10,11},{12,13},{14,15},{16,17},{18,... | collective-permute-start | bytes 294920 | tf_op jit(solution)/shard_map/ppermute | solution.py:275
  58.9 4.3 %collective-permute-start.14 = (bf16[24,2048]{1,0:T(8,128)(2,1)S(1)}, bf16[24,2048]{1,0:T(8,128)(2,1)S(1)}, u32[]{:S(2)}, u32[]{:S(2)}) collective-permute-start(bf16[24,2048]{1,0:T(8,128)(2,1)S(1)} %add_convert_fusion.6.refs_6_), channel_id=1, source_target_pairs={{0,18},{2,16},{16,2},{18,0},{4,22},{6,20},{20,6},{22,4},{8,26},{10... | collective-permute-start | bytes 294920 | tf_op jit(solution)/shard_map/ppermute | solution.py:272
  63.2 2.5 %collective-permute-start.13 = (bf16[24,2048]{1,0:T(8,128)(2,1)S(1)}, bf16[24,2048]{1,0:T(8,128)(2,1)S(1)}, u32[]{:S(2)}, u32[]{:S(2)}) collective-permute-start(bf16[24,2048]{1,0:T(8,128)(2,1)S(1)} %add_convert_fusion.6.refs_6_), channel_id=1, source_target_pairs={{0,16},{2,18},{16,0},{18,2},{4,20},{6,22},{20,4},{22,6},{8,24},{10... | collective-permute-start | bytes 294920 | tf_op jit(solution)/shard_map/ppermute | solution.py:272
  65.7 2.4 %collective-permute-start.12 = (bf16[24,2048]{1,0:T(8,128)(2,1)S(1)}, bf16[24,2048]{1,0:T(8,128)(2,1)S(1)}, u32[]{:S(2)}, u32[]{:S(2)}) collective-permute-start(bf16[24,2048]{1,0:T(8,128)(2,1)S(1)} %add_convert_fusion.6.refs_6_), channel_id=1, source_target_pairs={{0,2},{2,0},{16,18},{18,16},{4,6},{6,4},{20,22},{22,20},{8,10},{10... | collective-permute-start | bytes 294920 | tf_op jit(solution)/shard_map/ppermute | solution.py:272
  68.2 0.7 collective-permute-start.23
  68.8 1.3 %collective-permute-start.24 = (bf16[24,2048]{1,0:T(8,128)(2,1)S(1)}, bf16[24,2048]{1,0:T(8,128)(2,1)S(1)}, u32[]{:S(2)}, u32[]{:S(2)}) collective-permute-start(bf16[24,2048]{1,0:T(8,128)(2,1)S(1)} %add_convert_fusion.4.refs_14_), channel_id=1, source_target_pairs={{1,0},{3,2},{5,4},{7,6},{9,8},{11,10},{13,12},{15,14},{17,16},{19,... | collective-permute-start | bytes 294920 | tf_op jit(solution)/shard_map/ppermute | solution.py:275
  70.2 3.0 %collective-permute-start.18 = (bf16[24,2048]{1,0:T(8,128)(2,1)S(1)}, bf16[24,2048]{1,0:T(8,128)(2,1)S(1)}, u32[]{:S(2)}, u32[]{:S(2)}) collective-permute-start(bf16[24,2048]{1,0:T(8,128)(2,1)S(1)} %collective-permute-done.14.refs_9_), channel_id=1, source_target_pairs={{0,1},{2,3},{4,5},{6,7},{8,9},{10,11},{12,13},{14,15},{16,17},{18,... | collective-permute-start | bytes 294920 | tf_op jit(solution)/shard_map/ppermute | solution.py:275
  73.2 1.3 %collective-permute-start.17 = (bf16[24,2048]{1,0:T(8,128)(2,1)S(1)}, bf16[24,2048]{1,0:T(8,128)(2,1)S(1)}, u32[]{:S(2)}, u32[]{:S(2)}) collective-permute-start(bf16[24,2048]{1,0:T(8,128)(2,1)S(1)} %collective-permute-done.13.refs_8_), channel_id=1, source_target_pairs={{0,1},{2,3},{4,5},{6,7},{8,9},{10,11},{12,13},{14,15},{16,17},{18,... | collective-permute-start | bytes 294920 | tf_op jit(solution)/shard_map/ppermute | solution.py:275
  74.5 1.3 %collective-permute-start.16 = (bf16[24,2048]{1,0:T(8,128)(2,1)S(1)}, bf16[24,2048]{1,0:T(8,128)(2,1)S(1)}, u32[]{:S(2)}, u32[]{:S(2)}) collective-permute-start(bf16[24,2048]{1,0:T(8,128)(2,1)S(1)} %collective-permute-done.12.refs_7_), channel_id=1, source_target_pairs={{0,1},{2,3},{4,5},{6,7},{8,9},{10,11},{12,13},{14,15},{16,17},{18,... | collective-permute-start | bytes 294920 | tf_op jit(solution)/shard_map/ppermute | solution.py:275
  75.8 1.3 %collective-permute-start.25 = (bf16[24,2048]{1,0:T(8,128)(2,1)S(1)}, bf16[24,2048]{1,0:T(8,128)(2,1)S(1)}, u32[]{:S(2)}, u32[]{:S(2)}) collective-permute-start(bf16[24,2048]{1,0:T(8,128)(2,1)S(1)} %collective-permute-done.23.refs_15_), channel_id=1, source_target_pairs={{1,0},{3,2},{5,4},{7,6},{9,8},{11,10},{13,12},{15,14},{17,16},{19,... | collective-permute-start | bytes 294920 | tf_op jit(solution)/shard_map/ppermute | solution.py:275
  77.2 1.9 %collective-permute-done.25.refs_17_ = bf16[24,2048]{1,0:T(8,128)(2,1)S(1)} collective-permute-done((bf16[24,2048]{1,0:T(8,128)(2,1)S(1)}, bf16[24,2048]{1,0:T(8,128)(2,1)S(1)}, u32[]{:S(2)}, u32[]{:S(2)}) %collective-permute-start.25) | collective-permute-done | bytes 98336 | tf_op jit(solution)/shard_map/ppermute | solution.py:275
  79.0 2.4 %finish.1 = (bf16[24,4096]{1,0:T(8,128)(2,1)}, bf16[24,4096]{1,0:T(8,128)(2,1)}, bf16[24,128]{1,0:T(8,128)(2,1)}, bf16[128,2048]{1,0:T(8,128)(2,1)}) custom-call(s32[4]{0:T(128)S(1)} %pad_add_fusion.ids, bf16[24,4096]{1,0:T(8,128)(2,1)S(1)} %get-tuple-element.19.refs_0_, bf16[24,4096]{1,0:T(8,128)(2,1)S(1)} %collective-permute-done.refs_1_, ...), custom_call_target="tpu_custom_call" | custom-call | bytes 6291456 | tf_op jit(solution)/shard_map/finish/pallas_call | solution.py:241
  (27 shorter events, 0.3 us)
Async XLA Ops:
  0.6 10.6 %collective-permute-start = (bf16[24,4096]{1,0:T(8,128)(2,1)}, bf16[24,4096]{1,0:T(8,128)(2,1)S(1)}, u32[]{:S(2)}, u32[]{:S(2)}) collective-permute-start(bf16[24,4096]{1,0:T(8,128)(2,1)} %hid.1), channel_id=1, source_target_pairs={{0,16},{16,0},{1,17},{17,1},{2,18},{18,2},{3,19},{19,3},{4,20},{20... | collective-permute-start | bytes 589832 | tf_op jit(solution)/shard_map/ppermute | solution.py:270
  3.6 11.0 %collective-permute-start.1 = (bf16[24,4096]{1,0:T(8,128)(2,1)}, bf16[24,4096]{1,0:T(8,128)(2,1)S(1)}, u32[]{:S(2)}, u32[]{:S(2)}) collective-permute-start(bf16[24,4096]{1,0:T(8,128)(2,1)} %grads.1), channel_id=1, source_target_pairs={{0,16},{16,0},{1,17},{17,1},{2,18},{18,2},{3,19},{19,3},{4,20},{20... | collective-permute-start | bytes 589832 | tf_op jit(solution)/shard_map/ppermute | solution.py:270
  9.2 5.4 %collective-permute-start.2 = (f32[24,256]{1,0:T(8,128)S(1)}, f32[24,256]{1,0:T(8,128)S(1)}, u32[]{:S(2)}, u32[]{:S(2)}) collective-permute-start(f32[24,256]{1,0:T(8,128)S(1)} %get-tuple-element.21.refs_0_.refs_2_.refs_4_), channel_id=1, source_target_pairs={{0,16},{16,0},{1,17},{17,1},{2,18},{18,2},{3,19},{19,3},{4,20},{20... | collective-permute-start | bytes 73736 | tf_op jit(solution)/shard_map/ppermute | solution.py:270
  16.4 7.7 %collective-permute-start.3 = (bf16[2,2,24,2048]{3,2,1,0:T(8,128)(2,1)S(1)}, bf16[2,2,24,2048]{3,2,1,0:T(8,128)(2,1)S(1)}, u32[]{:S(2)}, u32[]{:S(2)}) collective-permute-start(bf16[2,2,24,2048]{3,2,1,0:T(8,128)(2,1)S(1)} %outward.1.refs_7_), channel_id=1, source_target_pairs={{0,1},{2,3},{4,5},{6,7},{8,9},{10,11},{12,13},{14,15},{16,17},{18,... | collective-permute-start | bytes 1179656 | tf_op jit(solution)/shard_map/ppermute | solution.py:275
  22.9 4.7 %collective-permute-start.5 = (bf16[2,24,2048]{2,1,0:T(8,128)(2,1)S(1)}, bf16[2,24,2048]{2,1,0:T(8,128)(2,1)S(1)}, u32[]{:S(2)}, u32[]{:S(2)}) collective-permute-start(bf16[2,24,2048]{2,1,0:T(8,128)(2,1)S(1)} %inward_first.1.waiting), channel_id=1, source_target_pairs={{1,0},{3,2},{5,4},{7,6},{9,8},{11,10},{13,12},{15,14},{17,16},{19,... | collective-permute-start | bytes 589832 | tf_op jit(solution)/shard_map/ppermute | solution.py:275
  24.3 54.7 %copy-start = (bf16[128,4096]{1,0:T(8,128)(2,1)S(1)}, bf16[128,4096]{1,0:T(8,128)(2,1)}, u32[]{:S(2)}) copy-start(bf16[128,4096]{1,0:T(8,128)(2,1)} %refs_19_.1) | copy-start | bytes 3145732
  26.8 8.0 %collective-permute-start.19 = (bf16[2,24,2048]{2,1,0:T(8,128)(2,1)S(1)}, bf16[2,24,2048]{2,1,0:T(8,128)(2,1)S(1)}, u32[]{:S(2)}, u32[]{:S(2)}) collective-permute-start(bf16[2,24,2048]{2,1,0:T(8,128)(2,1)S(1)} %get-tuple-element.34), channel_id=1, source_target_pairs={{1,17},{17,1},{3,19},{19,3},{5,21},{21,5},{7,23},{23,7},{9,25},{25... | collective-permute-start | bytes 589832 | tf_op jit(solution)/shard_map/ppermute | solution.py:272
  27.6 13.4 %collective-permute-start.6 = (bf16[24,2048]{1,0:T(8,128)(2,1)S(1)}, bf16[24,2048]{1,0:T(8,128)(2,1)S(1)}, u32[]{:S(2)}, u32[]{:S(2)}) collective-permute-start(bf16[24,2048]{1,0:T(8,128)(2,1)S(1)} %get-tuple-element.36), channel_id=1, source_target_pairs={{0,18},{2,16},{16,2},{18,0},{4,22},{6,20},{20,6},{22,4},{8,26},{10... | collective-permute-start | bytes 294920 | tf_op jit(solution)/shard_map/ppermute | solution.py:272
  31.1 9.9 %collective-permute-start.8 = (bf16[24,2048]{1,0:T(8,128)(2,1)S(1)}, bf16[24,2048]{1,0:T(8,128)(2,1)S(1)}, u32[]{:S(2)}, u32[]{:S(2)}) collective-permute-start(bf16[24,2048]{1,0:T(8,128)(2,1)S(1)} %get-tuple-element.37), channel_id=1, source_target_pairs={{0,2},{2,0},{16,18},{18,16},{4,6},{6,4},{20,22},{22,20},{8,10},{10... | collective-permute-start | bytes 294920 | tf_op jit(solution)/shard_map/ppermute | solution.py:272
  33.5 3.3 %collective-permute-start.4 = (bf16[2,24,2048]{2,1,0:T(8,128)(2,1)S(1)}, bf16[2,24,2048]{2,1,0:T(8,128)(2,1)S(1)}, u32[]{:S(2)}, u32[]{:S(2)}) collective-permute-start(bf16[2,24,2048]{2,1,0:T(8,128)(2,1)S(1)} %get-tuple-element.32), channel_id=1, source_target_pairs={{1,0},{3,2},{5,4},{7,6},{9,8},{11,10},{13,12},{15,14},{17,16},{19,... | collective-permute-start | bytes 589832 | tf_op jit(solution)/shard_map/ppermute | solution.py:275
  34.9 5.3 %collective-permute-start.20 = (bf16[24,2048]{1,0:T(8,128)(2,1)S(1)}, bf16[24,2048]{1,0:T(8,128)(2,1)S(1)}, u32[]{:S(2)}, u32[]{:S(2)}) collective-permute-start(bf16[24,2048]{1,0:T(8,128)(2,1)S(1)} %slice_bitcast_fusion.2), channel_id=1, source_target_pairs={{1,3},{3,1},{5,7},{7,5},{9,11},{11,9},{13,15},{15,13},{17,19},{19,... | collective-permute-start | bytes 294920 | tf_op jit(solution)/shard_map/ppermute | solution.py:272
  36.9 6.5 %collective-permute-start.7 = (bf16[24,2048]{1,0:T(8,128)(2,1)S(1)}, bf16[24,2048]{1,0:T(8,128)(2,1)S(1)}, u32[]{:S(2)}, u32[]{:S(2)}) collective-permute-start(bf16[24,2048]{1,0:T(8,128)(2,1)S(1)} %slice_bitcast_fusion.5), channel_id=1, source_target_pairs={{0,16},{2,18},{16,0},{18,2},{4,20},{6,22},{20,4},{22,6},{8,24},{10... | collective-permute-start | bytes 294920 | tf_op jit(solution)/shard_map/ppermute | solution.py:272
  40.3 13.3 %collective-permute-start.21 = (bf16[24,2048]{1,0:T(8,128)(2,1)S(1)}, bf16[24,2048]{1,0:T(8,128)(2,1)S(1)}, u32[]{:S(2)}, u32[]{:S(2)}) collective-permute-start(bf16[24,2048]{1,0:T(8,128)(2,1)S(1)} %fusion), channel_id=1, source_target_pairs={{1,5},{5,1},{9,13},{13,9},{3,7},{7,3},{11,15},{15,11},{17,21},{21,... | collective-permute-start | bytes 294920 | tf_op jit(solution)/shard_map/ppermute | solution.py:272
  43.5 10.9 %collective-permute-start.11 = (bf16[24,2048]{1,0:T(8,128)(2,1)S(1)}, bf16[24,2048]{1,0:T(8,128)(2,1)S(1)}, u32[]{:S(2)}, u32[]{:S(2)}) collective-permute-start(bf16[24,2048]{1,0:T(8,128)(2,1)S(1)} %fusion.3), channel_id=1, source_target_pairs={{0,12},{4,8},{8,4},{12,0},{2,14},{6,10},{10,6},{14,2},{16,28},{20,... | collective-permute-start | bytes 294920 | tf_op jit(solution)/shard_map/ppermute | solution.py:272
  49.0 7.5 %collective-permute-start.10 = (bf16[24,2048]{1,0:T(8,128)(2,1)S(1)}, bf16[24,2048]{1,0:T(8,128)(2,1)S(1)}, u32[]{:S(2)}, u32[]{:S(2)}) collective-permute-start(bf16[24,2048]{1,0:T(8,128)(2,1)S(1)} %fusion.3), channel_id=1, source_target_pairs={{0,8},{4,12},{8,0},{12,4},{2,10},{6,14},{10,2},{14,6},{16,24},{20,... | collective-permute-start | bytes 294920 | tf_op jit(solution)/shard_map/ppermute | solution.py:272
  50.9 6.6 %collective-permute-start.9 = (bf16[24,2048]{1,0:T(8,128)(2,1)S(1)}, bf16[24,2048]{1,0:T(8,128)(2,1)S(1)}, u32[]{:S(2)}, u32[]{:S(2)}) collective-permute-start(bf16[24,2048]{1,0:T(8,128)(2,1)S(1)} %fusion.3), channel_id=1, source_target_pairs={{0,4},{4,0},{8,12},{12,8},{2,6},{6,2},{10,14},{14,10},{16,20},{20,... | collective-permute-start | bytes 294920 | tf_op jit(solution)/shard_map/ppermute | solution.py:272
  53.7 14.4 %collective-permute-start.22 = (bf16[24,2048]{1,0:T(8,128)(2,1)S(1)}, bf16[24,2048]{1,0:T(8,128)(2,1)S(1)}, u32[]{:S(2)}, u32[]{:S(2)}) collective-permute-start(bf16[24,2048]{1,0:T(8,128)(2,1)S(1)} %add_convert_fusion.5), channel_id=1, source_target_pairs={{1,9},{5,13},{9,1},{13,5},{3,11},{7,15},{11,3},{15,7},{17,25},{21,... | collective-permute-start | bytes 294920 | tf_op jit(solution)/shard_map/ppermute | solution.py:272
  57.6 11.3 %collective-permute-start.15 = (bf16[24,2048]{1,0:T(8,128)(2,1)S(1)}, bf16[24,2048]{1,0:T(8,128)(2,1)S(1)}, u32[]{:S(2)}, u32[]{:S(2)}) collective-permute-start(bf16[24,2048]{1,0:T(8,128)(2,1)S(1)} %add_convert_fusion.6.refs_6_), channel_id=1, source_target_pairs={{0,1},{2,3},{4,5},{6,7},{8,9},{10,11},{12,13},{14,15},{16,17},{18,... | collective-permute-start | bytes 294920 | tf_op jit(solution)/shard_map/ppermute | solution.py:275
  58.9 11.3 %collective-permute-start.14 = (bf16[24,2048]{1,0:T(8,128)(2,1)S(1)}, bf16[24,2048]{1,0:T(8,128)(2,1)S(1)}, u32[]{:S(2)}, u32[]{:S(2)}) collective-permute-start(bf16[24,2048]{1,0:T(8,128)(2,1)S(1)} %add_convert_fusion.6.refs_6_), channel_id=1, source_target_pairs={{0,18},{2,16},{16,2},{18,0},{4,22},{6,20},{20,6},{22,4},{8,26},{10... | collective-permute-start | bytes 294920 | tf_op jit(solution)/shard_map/ppermute | solution.py:272
  63.2 10.0 %collective-permute-start.13 = (bf16[24,2048]{1,0:T(8,128)(2,1)S(1)}, bf16[24,2048]{1,0:T(8,128)(2,1)S(1)}, u32[]{:S(2)}, u32[]{:S(2)}) collective-permute-start(bf16[24,2048]{1,0:T(8,128)(2,1)S(1)} %add_convert_fusion.6.refs_6_), channel_id=1, source_target_pairs={{0,16},{2,18},{16,0},{18,2},{4,20},{6,22},{20,4},{22,6},{8,24},{10... | collective-permute-start | bytes 294920 | tf_op jit(solution)/shard_map/ppermute | solution.py:272
  65.7 8.8 %collective-permute-start.12 = (bf16[24,2048]{1,0:T(8,128)(2,1)S(1)}, bf16[24,2048]{1,0:T(8,128)(2,1)S(1)}, u32[]{:S(2)}, u32[]{:S(2)}) collective-permute-start(bf16[24,2048]{1,0:T(8,128)(2,1)S(1)} %add_convert_fusion.6.refs_6_), channel_id=1, source_target_pairs={{0,2},{2,0},{16,18},{18,16},{4,6},{6,4},{20,22},{22,20},{8,10},{10... | collective-permute-start | bytes 294920 | tf_op jit(solution)/shard_map/ppermute | solution.py:272
  68.2 7.7 %collective-permute-start.23 = (bf16[24,2048]{1,0:T(8,128)(2,1)S(1)}, bf16[24,2048]{1,0:T(8,128)(2,1)S(1)}, u32[]{:S(2)}, u32[]{:S(2)}) collective-permute-start(bf16[24,2048]{1,0:T(8,128)(2,1)S(1)} %add_convert_fusion.4.refs_14_), channel_id=1, source_target_pairs={{1,3},{3,1},{5,7},{7,5},{9,11},{11,9},{13,15},{15,13},{17,19},{19,... | collective-permute-start | bytes 294920 | tf_op jit(solution)/shard_map/ppermute | solution.py:272
  68.8 8.3 %collective-permute-start.24 = (bf16[24,2048]{1,0:T(8,128)(2,1)S(1)}, bf16[24,2048]{1,0:T(8,128)(2,1)S(1)}, u32[]{:S(2)}, u32[]{:S(2)}) collective-permute-start(bf16[24,2048]{1,0:T(8,128)(2,1)S(1)} %add_convert_fusion.4.refs_14_), channel_id=1, source_target_pairs={{1,0},{3,2},{5,4},{7,6},{9,8},{11,10},{13,12},{15,14},{17,16},{19,... | collective-permute-start | bytes 294920 | tf_op jit(solution)/shard_map/ppermute | solution.py:275
  70.2 7.0 %collective-permute-start.18 = (bf16[24,2048]{1,0:T(8,128)(2,1)S(1)}, bf16[24,2048]{1,0:T(8,128)(2,1)S(1)}, u32[]{:S(2)}, u32[]{:S(2)}) collective-permute-start(bf16[24,2048]{1,0:T(8,128)(2,1)S(1)} %collective-permute-done.14.refs_9_), channel_id=1, source_target_pairs={{0,1},{2,3},{4,5},{6,7},{8,9},{10,11},{12,13},{14,15},{16,17},{18,... | collective-permute-start | bytes 294920 | tf_op jit(solution)/shard_map/ppermute | solution.py:275
  73.2 3.9 %collective-permute-start.17 = (bf16[24,2048]{1,0:T(8,128)(2,1)S(1)}, bf16[24,2048]{1,0:T(8,128)(2,1)S(1)}, u32[]{:S(2)}, u32[]{:S(2)}) collective-permute-start(bf16[24,2048]{1,0:T(8,128)(2,1)S(1)} %collective-permute-done.13.refs_8_), channel_id=1, source_target_pairs={{0,1},{2,3},{4,5},{6,7},{8,9},{10,11},{12,13},{14,15},{16,17},{18,... | collective-permute-start | bytes 294920 | tf_op jit(solution)/shard_map/ppermute | solution.py:275
  74.5 2.6 %collective-permute-start.16 = (bf16[24,2048]{1,0:T(8,128)(2,1)S(1)}, bf16[24,2048]{1,0:T(8,128)(2,1)S(1)}, u32[]{:S(2)}, u32[]{:S(2)}) collective-permute-start(bf16[24,2048]{1,0:T(8,128)(2,1)S(1)} %collective-permute-done.12.refs_7_), channel_id=1, source_target_pairs={{0,1},{2,3},{4,5},{6,7},{8,9},{10,11},{12,13},{14,15},{16,17},{18,... | collective-permute-start | bytes 294920 | tf_op jit(solution)/shard_map/ppermute | solution.py:275
  75.8 3.2 %collective-permute-start.25 = (bf16[24,2048]{1,0:T(8,128)(2,1)S(1)}, bf16[24,2048]{1,0:T(8,128)(2,1)S(1)}, u32[]{:S(2)}, u32[]{:S(2)}) collective-permute-start(bf16[24,2048]{1,0:T(8,128)(2,1)S(1)} %collective-permute-done.23.refs_15_), channel_id=1, source_target_pairs={{1,0},{3,2},{5,4},{7,6},{9,8},{11,10},{13,12},{15,14},{17,16},{19,... | collective-permute-start | bytes 294920 | tf_op jit(solution)/shard_map/ppermute | solution.py:275

commit v7 on v5

--- a/solution.py
+++ b/solution.py
@@ -39,41 +39,24 @@
         out_ref[k, j, :, columns] = value[k * rows : (k + 1) * rows].astype(BF16)
 
 
-def load_kernel(n_dp, ids, w_gate, w_up, hid, grads, gain, named, weights, context, *refs):
-    sources = (w_gate, w_up, hid, grads, gain)
-    targets, small, named_held, weights_held, context_held, sems = (
-        refs[:5], refs[5], refs[6], refs[7], refs[8], refs[9]
-    )
-    small_copies = [
+def gates_kernel(n_dp, ids, named, weights, context, w_gate, w_up, w_down, small, *held):
+    targets, sems = held[:3], held[3]
+    copies = [
         pltpu.make_async_copy(source, target, sems.at[n])
-        for n, (source, target) in enumerate(
-            ((named, named_held), (weights, weights_held), (context, context_held))
-        )
+        for n, (source, target) in enumerate(zip((named, weights, context), targets))
     ]
-    for copy in small_copies:
-        copy.start()
-    copies = []
-    for source, target in zip(sources, targets):
-        pieces = LOAD_PIECES if source.shape[0] % (LOAD_PIECES * 16) == 0 else 1
-        part = source.shape[0] // pieces
-        for p in range(pieces):
-            block = pl.ds(p * part, part)
-            where = (source.at[block], target.at[block]) if pieces > 1 else (source, target)
-            copies.append(pltpu.make_async_copy(*where, sems.at[len(copies) + 3]))
     for copy in copies:
         copy.start()
-    for copy in small_copies:
+    for copy in copies:
         copy.wait()
-    rows = context_held.shape[0]
+    named_held, weights_held, context_held = targets
+    rows, heads = context_held.shape
     row = jnp.sum(jnp.where(named_held[...] == ids[3], weights_held[...], 0.0), axis=0, keepdims=True)
     square = (rows, rows)
     diagonal = lax.broadcasted_iota(jnp.int32, square, 0) == lax.broadcasted_iota(jnp.int32, square, 1)
     gate = jnp.sum(jnp.where(diagonal, row, 0.0), axis=1, keepdims=True)
-    heads = context_held.shape[1]
     small[:, :heads] = context_held[...].astype(F32)
     small[:, heads:] = jnp.broadcast_to(gate, (rows, LANES))
-    for copy in copies:
-        copy.wait()
 
 
 def loop(count, body, unroll):
@@ -94,9 +77,7 @@
 
 def hidden_kernel(n_dp, ids, *refs):
     hid = refs[:n_dp]
-    gain, w_gate, w_up, down_source, pre_gate, pre_up, act, w_down, normed, sem = refs[n_dp:]
-    down_copy = pltpu.make_async_copy(down_source, w_down, sem)
-    down_copy.start()
+    gain, w_gate, w_up, pre_gate, pre_up, act, normed = refs[n_dp:]
     total = hid[0].shape[0] * n_dp
     width = hid[0].shape[1]
     few = total <= FEW_ROWS
@@ -121,25 +102,23 @@
         act[:, columns] = (gate_part * jax.nn.sigmoid(gate_part) * up_part).astype(BF16)
 
     loop(w_gate.shape[1] // STEP, hidden_units, few)
-    down_copy.wait()
-
-
-def outward_kernel(n_dp, ids, *refs):
+
+
+def outward_kernel(i, n_dp, ids, *refs):
     smalls = refs[:n_dp]
-    act, w_down, send, keep = refs[2 * n_dp :]
+    act, w_down, earlier, target = refs[2 * n_dp :]
     weight = gates_of(smalls)
-    chunk = send.shape[3]
+    chunk = target.shape[3]
     few = act.shape[0] <= FEW_ROWS
-    for i, target in ((1, send), (0, keep)):
-        for j in range(2):
-            first = own_columns(ids, i, j, chunk)
-
-            def outward(step):
-                columns = pl.ds(pl.multiple_of(first + step * STEP, STEP), STEP)
-                part = weight * dot(act[...], w_down[:, columns], ((1,), (0,)))
-                store_blocks(target, j, pl.ds(place(step, STEP), STEP), part, n_dp)
-
-            loop(chunk // STEP, outward, few)
+    for j in range(2):
+        first = own_columns(ids, i, j, chunk)
+
+        def outward(step):
+            columns = pl.ds(pl.multiple_of(first + step * STEP, STEP), STEP)
+            part = weight * dot(act[...], w_down[:, columns], ((1,), (0,)))
+            store_blocks(target, j, pl.ds(place(step, STEP), STEP), part, n_dp)
+
+        loop(chunk // STEP, outward, few)
 
 
 def inward_part(ids, i, n_dp, grad_gate, grad_up, w_gate, w_up, target):
@@ -273,24 +252,22 @@
             count *= size
         return lax.ppermute(value, axes, [(i, i ^ turn) for i in range(count)])
 
-    def all_blocks(value, own=None):
-        own = value if own is None else own
-        return [own] + [swap(value, ("dp",), k) for k in range(1, n_dp)]
+    def all_blocks(value):
+        return [value] + [swap(value, ("dp",), k) for k in range(1, n_dp)]
 
     weights = 2 * width * units
     shares = ((n_dp, 2, rows, chunk), BF16)
-    wg, wu, hid_own, grads_own, gain, small_own = run(
-        load_kernel, n_dp, ids,
-        [w_gate[0], w_up[0], hidden_in, grad_out, norm_gain.reshape(1, width), route_ids.T, route_gates.T, context],
-        [((width, units), BF16), ((width, units), BF16), ((rows, width), BF16), ((rows, width), BF16),
-         ((1, width), F32), ((rows, heads + LANES), F32)],
+    wg, wu, wd, gain = w_gate[0], w_up[0], w_down[0], norm_gain.reshape(1, width)
+    (small_own,) = run(
+        gates_kernel, n_dp, ids, [route_ids.T, route_gates.T, context, wg, wu, wd],
+        [((rows, heads + LANES), F32)],
         [pltpu.VMEM((top, rows), jnp.int32), pltpu.VMEM((top, rows), F32), pltpu.VMEM((rows, heads), BF16),
-         pltpu.SemaphoreType.DMA((2 * LOAD_PIECES + 6,))],
-        2 * weights, "load", far=range(8),
-    )
-    hid = all_blocks(hidden_in, hid_own)
+         pltpu.SemaphoreType.DMA((3,))],
+        4 * weights, "gates", far=range(6),
+    )
+    hid = all_blocks(hidden_in)
     smalls = all_blocks(small_own)
-    grads = all_blocks(grad_out, grads_own)
+    grads = all_blocks(grad_out)
 
     def add(one, other):
         return (one.astype(F32) + other.astype(F32)).astype(BF16)
@@ -301,25 +278,31 @@
             total = total + piece.astype(F32)
         return total.astype(BF16)
 
-    pre_gate, pre_up, act, wd = run(
-        hidden_kernel, n_dp, ids, hid + [gain, wg, wu, w_down[0]],
-        [((all_rows, units), F32), ((all_rows, units), F32), ((all_rows, units), BF16), ((units, width), BF16)],
-        [pltpu.VMEM((all_rows, width), BF16), pltpu.SemaphoreType.DMA], 2 * weights, "hidden", far=(n_dp + 3,),
-    )
-    out_send, out_keep = run(
-        outward_kernel, n_dp, ids, smalls + grads + [act, wd], [shares, shares], [], weights, "outward"
+    pre_gate, pre_up, act = run(
+        hidden_kernel, n_dp, ids, hid + [gain, wg, wu],
+        [((all_rows, units), F32), ((all_rows, units), F32), ((all_rows, units), BF16)],
+        [pltpu.VMEM((all_rows, width), BF16)], 2 * weights, "hidden",
+    )
+    (out_send,) = run(
+        functools.partial(outward_kernel, 1), n_dp, ids, smalls + grads + [act, wd, act], [shares], [],
+        weights // 2, "outward_send",
     )
     out_other = swap(out_send, ("c",), 1)
-    grad_gate, grad_up, out_keep = run(
-        backward_kernel, n_dp, ids, grads + smalls + [pre_gate, pre_up, wd, out_keep],
-        [((all_rows, units), BF16), ((all_rows, units), BF16), shares],
-        [pltpu.VMEM((all_rows, width), BF16)], weights, "backward",
+    (out_keep,) = run(
+        functools.partial(outward_kernel, 0), n_dp, ids, smalls + grads + [act, wd, out_send], [shares], [],
+        weights // 2, "outward_keep",
     )
     out_half = add(out_keep, out_other)
     out_blocks = [swap(out_half[k], ("dp",), k) for k in range(1, n_dp)]
+    block = (shares[0][1:], BF16)
+    grad_gate, grad_up, out_block = run(
+        backward_kernel, n_dp, ids, grads + smalls + [pre_gate, pre_up, wd, out_half[0]],
+        [((all_rows, units), BF16), ((all_rows, units), BF16), block],
+        [pltpu.VMEM((all_rows, width), BF16)], weights, "backward",
+    )
     in_send, out_block = run(
-        functools.partial(inward_kernel, 1), n_dp, ids, [grad_gate, grad_up, wg, wu, out_half[0]],
-        [shares, (shares[0][1:], BF16)], [], weights, "inward_send",
+        functools.partial(inward_kernel, 1), n_dp, ids, [grad_gate, grad_up, wg, wu, out_block],
+        [shares, block], [], weights, "inward_send",
     )
     in_other = swap(in_send, ("c",), 1)
     out_block = total_of([out_block] + out_blocks)

time: 56.5 us -> 55.2 us (0.977)
  Pallas kernels: 20.4 us -> 16.9 us
  starting transfers between devices: 25.5 us -> 26.6 us
  waiting for transfers between devices: 9.24 us -> 10.3 us
    pallas_call x7 -> x8, Pallas kernels: 20.4 us -> 16.9 us  [run(): pl.pallas_call(functools.partial(kernel, n_dp), out_shape=kinds, in_specs...]
    ppermute x25, starting transfers between devices: 25.5 us -> 26.6 us  [swap(): return lax.ppermute(value, axes, [(i, i ^ turn) for i in range(count)])]
    ppermute x25, waiting for transfers between devices: 9.24 us -> 10.3 us  [swap(): return lax.ppermute(value, axes, [(i, i ^ turn) for i in range(count)])]
  transfers between devices with their start and end apart: 25 -> 25, of which waited for: 7 -> 9; matrix products, arithmetic and copies ran while one was open for 0% -> 0% of each run, Pallas kernels for 29% -> 24%
where the time goes in v7:
time: 55.2 us; the launch traced here: 55.1 us
  starting transfers between devices  26.6 us (48%)
  Pallas kernels  16.9 us (31%)
  waiting for transfers between devices  10.3 us (19%)
  between operations  0.86 us (2%)
    ppermute x25, starting transfers between devices, swap(): return lax.ppermute(value, axes, [(i, i ^ turn) for i in range(count)])  26.6 us
    pallas_call x8, Pallas kernels, run(): pl.pallas_call(functools.partial(kernel, n_dp), out_shape=kinds, in_specs...  16.9 us
    ppermute x25, waiting for transfers between devices, swap(): return lax.ppermute(value, axes, [(i, i ^ turn) for i in range(count)])  10.3 us
  transfers between devices with their start and end apart: 25, of which 9 were waited for; matrix products, arithmetic and copies ran while one was open for 0% of the time, Pallas kernels for 24%

profile of v7, /device:TPU:0, one launch (start us, length us, event | category | flops | bytes accessed | tf_op | source)
XLA Modules:
  0.0 55.1 jit_solution(9818495459215673783)
XLA Ops:
  0.6 3.0 %collective-permute-start = (bf16[24,4096]{1,0:T(8,128)(2,1)}, bf16[24,4096]{1,0:T(8,128)(2,1)S(1)}, u32[]{:S(2)}, u32[]{:S(2)}) collective-permute-start(bf16[24,4096]{1,0:T(8,128)(2,1)} %refs_0_.5), channel_id=1, source_target_pairs={{0,16},{16,0},{1,17},{17,1},{2,18},{18,2},{3,19},{19,3},{4,20},{20... | collective-permute-start | bytes 589832 | tf_op jit(solution)/shard_map/ppermute | solution.py:253
  3.6 0.1 collective-permute-start.1
  3.7 0.1 pad_add_fusion.ids
  3.8 1.6 %gates.1.refs_0_.refs_2_.refs_4_ = f32[24,256]{1,0:T(8,128)S(1)} custom-call(s32[4]{0:T(128)S(1)} %pad_add_fusion.ids, s32[8,24]{1,0:T(8,128)} %bitcast.43, f32[8,24]{1,0:T(8,128)} %bitcast.44, bf16[24,128]{1,0:T(8,128)(2,1)} %context.1, bf16[4096,768]{1,0:T(8,128)(2,1)} %bitcast.33, bf16[4096,768]{1,0:T(8,128)(2,1)} %bitcast.37, bf16[768,4096]{1,0:T(8,128)(2,1)} %bitcast.29), custom_call_target="tpu_custom_call" | custom-call | bytes 25165824 | tf_op jit(solution)/shard_map/gates/pallas_call | solution.py:224
  5.4 2.0 %collective-permute-start.2 = (f32[24,256]{1,0:T(8,128)S(1)}, f32[24,256]{1,0:T(8,128)S(1)}, u32[]{:S(2)}, u32[]{:S(2)}) collective-permute-start(f32[24,256]{1,0:T(8,128)S(1)} %gates.1.refs_0_.refs_2_.refs_4_), channel_id=1, source_target_pairs={{0,16},{16,0},{1,17},{17,1},{2,18},{18,2},{3,19},{19,3},{4,20},{20... | collective-permute-start | bytes 73736 | tf_op jit(solution)/shard_map/ppermute | solution.py:253
  7.4 2.1 %collective-permute-done.refs_1_ = bf16[24,4096]{1,0:T(8,128)(2,1)S(1)} collective-permute-done((bf16[24,4096]{1,0:T(8,128)(2,1)}, bf16[24,4096]{1,0:T(8,128)(2,1)S(1)}, u32[]{:S(2)}, u32[]{:S(2)}) %collective-permute-start) | collective-permute-done | bytes 196640 | tf_op jit(solution)/shard_map/ppermute | solution.py:253
  9.6 0.0 copy-start
  9.6 0.0 copy-start.3
  9.6 3.0 %hidden.1 = (f32[48,768]{1,0:T(8,128)S(1)}, f32[48,768]{1,0:T(8,128)S(1)}, bf16[48,768]{1,0:T(8,128)(2,1)S(1)}) custom-call(s32[4]{0:T(128)S(1)} %pad_add_fusion.ids, bf16[24,4096]{1,0:T(8,128)(2,1)S(1)} %copy-done.5, bf16[24,4096]{1,0:T(8,128)(2,1)S(1)} %collective-permute-done.refs_1_, f32[1,4096]{1,0:T(1,128)S(1)} %bitcast.41, ...), custom_call_target="tpu_custom_call" | custom-call | bytes 12582912 | tf_op jit(solution)/shard_map/hidden/pallas_call | solution.py:224
  12.6 0.9 %collective-permute-done.2.refs_1_.refs_3_.refs_5_ = f32[24,256]{1,0:T(8,128)S(1)} collective-permute-done((f32[24,256]{1,0:T(8,128)S(1)}, f32[24,256]{1,0:T(8,128)S(1)}, u32[]{:S(2)}, u32[]{:S(2)}) %collective-permute-start.2) | collective-permute-done | bytes 24608 | tf_op jit(solution)/shard_map/ppermute | solution.py:253
  13.5 0.0 collective-permute-done.1.refs_3_.refs_1_
  13.5 1.2 %outward_send.1.refs_6_ = bf16[2,2,24,1024]{3,2,1,0:T(8,128)(2,1)S(1)} custom-call(s32[4]{0:T(128)S(1)} %pad_add_fusion.ids, f32[24,256]{1,0:T(8,128)S(1)} %gates.1.refs_0_.refs_2_.refs_4_, f32[24,256]{1,0:T(8,128)S(1)} %collective-permute-done.2.refs_1_.refs_3_.refs_5_, bf16[24,4096]{1,0:T(8,128)(2,1)S(1)} %copy-done.3, ...), custom_call_target="tpu_custom_call" | custom-call | bytes 3145728 | tf_op jit(solution)/shard_map/outward_send/pallas_call | solution.py:224
  14.7 0.1 collective-permute-start.3
  14.8 1.2 %outward_keep.1 = bf16[2,2,24,1024]{3,2,1,0:T(8,128)(2,1)S(1)} custom-call(s32[4]{0:T(128)S(1)} %pad_add_fusion.ids, f32[24,256]{1,0:T(8,128)S(1)} %gates.1.refs_0_.refs_2_.refs_4_, f32[24,256]{1,0:T(8,128)S(1)} %collective-permute-done.2.refs_1_.refs_3_.refs_5_, bf16[24,4096]{1,0:T(8,128)(2,1)S(1)} %copy-done.3, ...), custom_call_target="tpu_custom_call" | custom-call | bytes 3145728 | tf_op jit(solution)/shard_map/outward_keep/pallas_call | solution.py:224
  16.0 0.2 collective-permute-done.3
  16.3 1.8 %collective-permute-start.4 = (bf16[2,24,1024]{2,1,0:T(8,128)(2,1)S(1)}, bf16[2,24,1024]{2,1,0:T(8,128)(2,1)S(1)}, u32[]{:S(2)}, u32[]{:S(2)}) collective-permute-start(bf16[2,24,1024]{2,1,0:T(8,128)(2,1)S(1)} %get-tuple-element.27), channel_id=1, source_target_pairs={{0,16},{16,0},{1,17},{17,1},{2,18},{18,2},{3,19},{19,3},{4,20},{20... | collective-permute-start | bytes 294920 | tf_op jit(solution)/shard_map/ppermute | solution.py:253
  18.1 2.6 %backward.1 = (bf16[48,768]{1,0:T(8,128)(2,1)S(1)}, bf16[48,768]{1,0:T(8,128)(2,1)S(1)}, bf16[2,24,1024]{2,1,0:T(8,128)(2,1)S(1)}) custom-call(s32[4]{0:T(128)S(1)} %pad_add_fusion.ids, bf16[24,4096]{1,0:T(8,128)(2,1)S(1)} %copy-done.3, bf16[24,4096]{1,0:T(8,128)(2,1)S(1)} %collective-permute-done.1.refs_3_.refs_1_, ...), custom_call_target="tpu_custom_call" | custom-call | bytes 6291456 | tf_op jit(solution)/shard_map/backward/pallas_call | solution.py:224
  20.7 2.5 %inward_send.1 = (bf16[2,2,24,1024]{3,2,1,0:T(8,128)(2,1)S(1)}, bf16[2,24,1024]{2,1,0:T(8,128)(2,1)S(1)}) custom-call(s32[4]{0:T(128)S(1)} %pad_add_fusion.ids, bf16[48,768]{1,0:T(8,128)(2,1)S(1)} %get-tuple-element.17.grad_gate, bf16[48,768]{1,0:T(8,128)(2,1)S(1)} %get-tuple-element.18.grad_up, bf16[4096,768]{1,0:T(8,128)(2,1)S(1)} %bitcast.35, ...), custom_call_target="tpu_custom_call" | custom-call | bytes 6291456 | tf_op jit(solution)/shard_map/inward_send/pallas_call | solution.py:224
  23.2 0.0 collective-permute-done.4
  23.3 1.6 %collective-permute-start.19 = (bf16[24,1024]{1,0:T(8,128)(2,1)S(1)}, bf16[24,1024]{1,0:T(8,128)(2,1)S(1)}, u32[]{:S(2)}, u32[]{:S(2)}) collective-permute-start(bf16[24,1024]{1,0:T(8,128)(2,1)S(1)} %get-tuple-element.29), channel_id=1, source_target_pairs={{0,2},{2,0},{1,3},{3,1},{4,6},{6,4},{5,7},{7,5},{8,10},{10,8},{9,1... | collective-permute-start | bytes 147464 | tf_op jit(solution)/shard_map/ppermute | solution.py:253
  24.9 2.5 %inward_keep.1 = (bf16[2,2,24,1024]{3,2,1,0:T(8,128)(2,1)S(1)}, bf16[24,1024]{1,0:T(8,128)(2,1)S(1)}) custom-call(s32[4]{0:T(128)S(1)} %pad_add_fusion.ids, bf16[48,768]{1,0:T(8,128)(2,1)S(1)} %get-tuple-element.17.grad_gate, bf16[48,768]{1,0:T(8,128)(2,1)S(1)} %get-tuple-element.18.grad_up, bf16[4096,768]{1,0:T(8,128)(2,1)S(1)} %bitcast.36, ...), custom_call_target="tpu_custom_call" | custom-call | bytes 6291456 | tf_op jit(solution)/shard_map/inward_keep/pallas_call | solution.py:224
  27.4 0.0 collective-permute-done.19
  27.5 1.6 %collective-permute-start.20 = (bf16[24,1024]{1,0:T(8,128)(2,1)S(1)}, bf16[24,1024]{1,0:T(8,128)(2,1)S(1)}, u32[]{:S(2)}, u32[]{:S(2)}) collective-permute-start(bf16[24,1024]{1,0:T(8,128)(2,1)S(1)} %add_convert_fusion.5), channel_id=1, source_target_pairs={{0,4},{4,0},{8,12},{12,8},{1,5},{5,1},{9,13},{13,9},{2,6},{6,2},{1... | collective-permute-start | bytes 147464 | tf_op jit(solution)/shard_map/ppermute | solution.py:253
  29.1 0.0 collective-permute-done.5
  29.1 0.1 add_convert_fusion
  29.2 1.6 %collective-permute-start.6 = (bf16[24,1024]{1,0:T(8,128)(2,1)S(1)}, bf16[24,1024]{1,0:T(8,128)(2,1)S(1)}, u32[]{:S(2)}, u32[]{:S(2)}) collective-permute-start(bf16[24,1024]{1,0:T(8,128)(2,1)S(1)} %get-tuple-element.24), channel_id=1, source_target_pairs={{0,18},{2,16},{16,2},{18,0},{1,19},{3,17},{17,3},{19,1},{4,22},{6,... | collective-permute-start | bytes 147464 | tf_op jit(solution)/shard_map/ppermute | solution.py:253
  30.7 0.5 collective-permute-start.8
  31.3 1.5 %collective-permute-start.7 = (bf16[24,1024]{1,0:T(8,128)(2,1)S(1)}, bf16[24,1024]{1,0:T(8,128)(2,1)S(1)}, u32[]{:S(2)}, u32[]{:S(2)}) collective-permute-start(bf16[24,1024]{1,0:T(8,128)(2,1)S(1)} %get-tuple-element.26), channel_id=1, source_target_pairs={{0,16},{2,18},{16,0},{18,2},{1,17},{3,19},{17,1},{19,3},{4,20},{6,... | collective-permute-start | bytes 147464 | tf_op jit(solution)/shard_map/ppermute | solution.py:253
  32.8 2.7 %collective-permute-start.21 = (bf16[24,1024]{1,0:T(8,128)(2,1)S(1)}, bf16[24,1024]{1,0:T(8,128)(2,1)S(1)}, u32[]{:S(2)}, u32[]{:S(2)}) collective-permute-start(bf16[24,1024]{1,0:T(8,128)(2,1)S(1)} %add_convert_fusion.4), channel_id=1, source_target_pairs={{0,8},{4,12},{8,0},{12,4},{1,9},{5,13},{9,1},{13,5},{2,10},{6,14},... | collective-permute-start | bytes 147464 | tf_op jit(solution)/shard_map/ppermute | solution.py:253
  35.4 0.0 collective-permute-done.6
  35.4 0.0 collective-permute-done.8
  35.5 0.5 collective-permute-start.11
  36.0 2.5 %collective-permute-start.10 = (bf16[24,1024]{1,0:T(8,128)(2,1)S(1)}, bf16[24,1024]{1,0:T(8,128)(2,1)S(1)}, u32[]{:S(2)}, u32[]{:S(2)}) collective-permute-start(bf16[24,1024]{1,0:T(8,128)(2,1)S(1)} %fusion.2), channel_id=1, source_target_pairs={{0,8},{4,12},{8,0},{12,4},{1,9},{5,13},{9,1},{13,5},{2,10},{6,14},... | collective-permute-start | bytes 147464 | tf_op jit(solution)/shard_map/ppermute | solution.py:253
  38.5 1.4 %collective-permute-start.9 = (bf16[24,1024]{1,0:T(8,128)(2,1)S(1)}, bf16[24,1024]{1,0:T(8,128)(2,1)S(1)}, u32[]{:S(2)}, u32[]{:S(2)}) collective-permute-start(bf16[24,1024]{1,0:T(8,128)(2,1)S(1)} %fusion.2), channel_id=1, source_target_pairs={{0,12},{4,8},{8,4},{12,0},{1,13},{5,9},{9,5},{13,1},{2,14},{6,10},... | collective-permute-start | bytes 147464 | tf_op jit(solution)/shard_map/ppermute | solution.py:253
  39.9 0.1 collective-permute-start.23
  40.0 1.6 %collective-permute-start.22 = (bf16[24,1024]{1,0:T(8,128)(2,1)S(1)}, bf16[24,1024]{1,0:T(8,128)(2,1)S(1)}, u32[]{:S(2)}, u32[]{:S(2)}) collective-permute-start(bf16[24,1024]{1,0:T(8,128)(2,1)S(1)} %add_convert_fusion.3.refs_14_), channel_id=1, source_target_pairs={{0,2},{2,0},{1,3},{3,1},{4,6},{6,4},{5,7},{7,5},{8,10},{10,8},{9,1... | collective-permute-start | bytes 147464 | tf_op jit(solution)/shard_map/ppermute | solution.py:253
  41.6 2.8 %collective-permute-done.9 = bf16[24,1024]{1,0:T(8,128)(2,1)S(1)} collective-permute-done((bf16[24,1024]{1,0:T(8,128)(2,1)S(1)}, bf16[24,1024]{1,0:T(8,128)(2,1)S(1)}, u32[]{:S(2)}, u32[]{:S(2)}) %collective-permute-start.9) | collective-permute-done | bytes 49184 | tf_op jit(solution)/shard_map/ppermute | solution.py:253
  44.4 2.5 %collective-permute-start.14 = (bf16[24,1024]{1,0:T(8,128)(2,1)S(1)}, bf16[24,1024]{1,0:T(8,128)(2,1)S(1)}, u32[]{:S(2)}, u32[]{:S(2)}) collective-permute-start(bf16[24,1024]{1,0:T(8,128)(2,1)S(1)} %add_convert_fusion.6.refs_6_), channel_id=1, source_target_pairs={{0,18},{2,16},{16,2},{18,0},{1,19},{3,17},{17,3},{19,1},{4,22},{6,... | collective-permute-start | bytes 147464 | tf_op jit(solution)/shard_map/ppermute | solution.py:253
  46.9 0.5 collective-permute-start.13
  47.5 0.5 collective-permute-start.12
  48.0 0.0 collective-permute-done.23.refs_16_
  48.0 0.5 collective-permute-start.24
  48.5 1.0 %collective-permute-done.14.refs_9_ = bf16[24,1024]{1,0:T(8,128)(2,1)S(1)} collective-permute-done((bf16[24,1024]{1,0:T(8,128)(2,1)S(1)}, bf16[24,1024]{1,0:T(8,128)(2,1)S(1)}, u32[]{:S(2)}, u32[]{:S(2)}) %collective-permute-start.14) | collective-permute-done | bytes 49184 | tf_op jit(solution)/shard_map/ppermute | solution.py:253
  49.5 1.5 %collective-permute-done.13.refs_8_ = bf16[24,1024]{1,0:T(8,128)(2,1)S(1)} collective-permute-done((bf16[24,1024]{1,0:T(8,128)(2,1)S(1)}, bf16[24,1024]{1,0:T(8,128)(2,1)S(1)}, u32[]{:S(2)}, u32[]{:S(2)}) %collective-permute-start.13) | collective-permute-done | bytes 49184 | tf_op jit(solution)/shard_map/ppermute | solution.py:253
  51.0 0.5 collective-permute-done.12.refs_7_
  51.6 0.7 %collective-permute-done.17.refs_12_ = bf16[24,1024]{1,0:T(8,128)(2,1)S(1)} collective-permute-done((bf16[24,1024]{1,0:T(8,128)(2,1)S(1)}, bf16[24,1024]{1,0:T(8,128)(2,1)S(1)}, u32[]{:S(2)}, u32[]{:S(2)}) %collective-permute-start.17) | collective-permute-done | bytes 49184 | tf_op jit(solution)/shard_map/ppermute | solution.py:253
  52.2 0.5 collective-permute-done.16.refs_11_
  52.8 2.3 %finish.1 = (bf16[24,4096]{1,0:T(8,128)(2,1)}, bf16[24,4096]{1,0:T(8,128)(2,1)}, bf16[24,128]{1,0:T(8,128)(2,1)}, bf16[128,2048]{1,0:T(8,128)(2,1)}) custom-call(s32[4]{0:T(128)S(1)} %pad_add_fusion.ids, bf16[24,4096]{1,0:T(8,128)(2,1)S(1)} %copy-done.5, bf16[24,4096]{1,0:T(8,128)(2,1)S(1)} %collective-permute-done.refs_1_, bf16[24,4096]{1,0:T(8,128)(2,1)S(1)} %copy-done.3, ...), custom_call_target="tpu_custom_call" | custom-call | bytes 6291456 | tf_op jit(solution)/shard_map/finish/pallas_call | solution.py:224
  (36 shorter events, 0.3 us)
Async XLA Ops:
  0.6 8.9 %collective-permute-start = (bf16[24,4096]{1,0:T(8,128)(2,1)}, bf16[24,4096]{1,0:T(8,128)(2,1)S(1)}, u32[]{:S(2)}, u32[]{:S(2)}) collective-permute-start(bf16[24,4096]{1,0:T(8,128)(2,1)} %refs_0_.5), channel_id=1, source_target_pairs={{0,16},{16,0},{1,17},{17,1},{2,18},{18,2},{3,19},{19,3},{4,20},{20... | collective-permute-start | bytes 589832 | tf_op jit(solution)/shard_map/ppermute | solution.py:253
  3.6 9.9 %collective-permute-start.1 = (bf16[24,4096]{1,0:T(8,128)(2,1)}, bf16[24,4096]{1,0:T(8,128)(2,1)S(1)}, u32[]{:S(2)}, u32[]{:S(2)}) collective-permute-start(bf16[24,4096]{1,0:T(8,128)(2,1)} %refs_2_.5), channel_id=1, source_target_pairs={{0,16},{16,0},{1,17},{17,1},{2,18},{18,2},{3,19},{19,3},{4,20},{20... | collective-permute-start | bytes 589832 | tf_op jit(solution)/shard_map/ppermute | solution.py:253
  3.8 5.8 %copy-start.1 = (bf16[1,4096,768]{2,1,0:T(8,128)(2,1)S(1)}, bf16[1,4096,768]{2,1,0:T(8,128)(2,1)}, u32[]{:S(2)}) copy-start(bf16[1,4096,768]{2,1,0:T(8,128)(2,1)} %param.14) | copy-start | bytes 18874372
  3.8 5.8 %copy-start.2 = (bf16[1,4096,768]{2,1,0:T(8,128)(2,1)S(1)}, bf16[1,4096,768]{2,1,0:T(8,128)(2,1)}, u32[]{:S(2)}) copy-start(bf16[1,4096,768]{2,1,0:T(8,128)(2,1)} %param.15) | copy-start | bytes 18874372
  3.8 5.8 %copy-start.5 = (bf16[24,4096]{1,0:T(8,128)(2,1)S(1)}, bf16[24,4096]{1,0:T(8,128)(2,1)}, u32[]{:S(2)}) copy-start(bf16[24,4096]{1,0:T(8,128)(2,1)} %refs_0_.5) | copy-start | bytes 589828
  3.8 5.8 %copy-start.6 = (f32[4096]{0:T(1024)S(1)}, f32[4096]{0:T(1024)}, u32[]{:S(2)}) copy-start(f32[4096]{0:T(1024)} %param.11) | copy-start | bytes 49156
  5.4 8.1 %collective-permute-start.2 = (f32[24,256]{1,0:T(8,128)S(1)}, f32[24,256]{1,0:T(8,128)S(1)}, u32[]{:S(2)}, u32[]{:S(2)}) collective-permute-start(f32[24,256]{1,0:T(8,128)S(1)} %gates.1.refs_0_.refs_2_.refs_4_), channel_id=1, source_target_pairs={{0,16},{16,0},{1,17},{17,1},{2,18},{18,2},{3,19},{19,3},{4,20},{20... | collective-permute-start | bytes 73736 | tf_op jit(solution)/shard_map/ppermute | solution.py:253
  9.6 3.9 %copy-start = (bf16[1,768,4096]{2,1,0:T(8,128)(2,1)S(1)}, bf16[1,768,4096]{2,1,0:T(8,128)(2,1)}, u32[]{:S(2)}) copy-start(bf16[1,768,4096]{2,1,0:T(8,128)(2,1)} %param.16) | copy-start | bytes 18874372
  9.6 3.9 %copy-start.3 = (bf16[24,4096]{1,0:T(8,128)(2,1)S(1)}, bf16[24,4096]{1,0:T(8,128)(2,1)}, u32[]{:S(2)}) copy-start(bf16[24,4096]{1,0:T(8,128)(2,1)} %refs_2_.5) | copy-start | bytes 589828
  14.7 1.5 %collective-permute-start.3 = (bf16[2,2,24,1024]{3,2,1,0:T(8,128)(2,1)S(1)}, bf16[2,2,24,1024]{3,2,1,0:T(8,128)(2,1)S(1)}, u32[]{:S(2)}, u32[]{:S(2)}) collective-permute-start(bf16[2,2,24,1024]{3,2,1,0:T(8,128)(2,1)S(1)} %outward_send.1.refs_6_), channel_id=1, source_target_pairs={{0,1},{1,0},{2,3},{3,2},{4,5},{5,4},{6,7},{7,6},{8,9},{9,8},{10,11... | collective-permute-start | bytes 589832 | tf_op jit(solution)/shard_map/ppermute | solution.py:253
  16.3 6.9 %collective-permute-start.4 = (bf16[2,24,1024]{2,1,0:T(8,128)(2,1)S(1)}, bf16[2,24,1024]{2,1,0:T(8,128)(2,1)S(1)}, u32[]{:S(2)}, u32[]{:S(2)}) collective-permute-start(bf16[2,24,1024]{2,1,0:T(8,128)(2,1)S(1)} %get-tuple-element.27), channel_id=1, source_target_pairs={{0,16},{16,0},{1,17},{17,1},{2,18},{18,2},{3,19},{19,3},{4,20},{20... | collective-permute-start | bytes 294920 | tf_op jit(solution)/shard_map/ppermute | solution.py:253
  23.3 4.2 %collective-permute-start.19 = (bf16[24,1024]{1,0:T(8,128)(2,1)S(1)}, bf16[24,1024]{1,0:T(8,128)(2,1)S(1)}, u32[]{:S(2)}, u32[]{:S(2)}) collective-permute-start(bf16[24,1024]{1,0:T(8,128)(2,1)S(1)} %get-tuple-element.29), channel_id=1, source_target_pairs={{0,2},{2,0},{1,3},{3,1},{4,6},{6,4},{5,7},{7,5},{8,10},{10,8},{9,1... | collective-permute-start | bytes 147464 | tf_op jit(solution)/shard_map/ppermute | solution.py:253
  24.9 4.2 %collective-permute-start.5 = (bf16[2,2,24,1024]{3,2,1,0:T(8,128)(2,1)S(1)}, bf16[2,2,24,1024]{3,2,1,0:T(8,128)(2,1)S(1)}, u32[]{:S(2)}, u32[]{:S(2)}) collective-permute-start(bf16[2,2,24,1024]{3,2,1,0:T(8,128)(2,1)S(1)} %get-tuple-element.22), channel_id=1, source_target_pairs={{0,1},{1,0},{2,3},{3,2},{4,5},{5,4},{6,7},{7,6},{8,9},{9,8},{10,11... | collective-permute-start | bytes 589832 | tf_op jit(solution)/shard_map/ppermute | solution.py:253
  24.9 27.9 %copy-start.4 = (bf16[128,4096]{1,0:T(8,128)(2,1)S(1)}, bf16[128,4096]{1,0:T(8,128)(2,1)}, u32[]{:S(2)}) copy-start(bf16[128,4096]{1,0:T(8,128)(2,1)} %refs_19_.1) | copy-start | bytes 3145732
  27.5 5.3 %collective-permute-start.20 = (bf16[24,1024]{1,0:T(8,128)(2,1)S(1)}, bf16[24,1024]{1,0:T(8,128)(2,1)S(1)}, u32[]{:S(2)}, u32[]{:S(2)}) collective-permute-start(bf16[24,1024]{1,0:T(8,128)(2,1)S(1)} %add_convert_fusion.5), channel_id=1, source_target_pairs={{0,4},{4,0},{8,12},{12,8},{1,5},{5,1},{9,13},{13,9},{2,6},{6,2},{1... | collective-permute-start | bytes 147464 | tf_op jit(solution)/shard_map/ppermute | solution.py:253
  29.2 6.2 %collective-permute-start.6 = (bf16[24,1024]{1,0:T(8,128)(2,1)S(1)}, bf16[24,1024]{1,0:T(8,128)(2,1)S(1)}, u32[]{:S(2)}, u32[]{:S(2)}) collective-permute-start(bf16[24,1024]{1,0:T(8,128)(2,1)S(1)} %get-tuple-element.24), channel_id=1, source_target_pairs={{0,18},{2,16},{16,2},{18,0},{1,19},{3,17},{17,3},{19,1},{4,22},{6,... | collective-permute-start | bytes 147464 | tf_op jit(solution)/shard_map/ppermute | solution.py:253
  30.7 4.7 %collective-permute-start.8 = (bf16[24,1024]{1,0:T(8,128)(2,1)S(1)}, bf16[24,1024]{1,0:T(8,128)(2,1)S(1)}, u32[]{:S(2)}, u32[]{:S(2)}) collective-permute-start(bf16[24,1024]{1,0:T(8,128)(2,1)S(1)} %get-tuple-element.25), channel_id=1, source_target_pairs={{0,2},{2,0},{16,18},{18,16},{1,3},{3,1},{17,19},{19,17},{4,6},{6,4... | collective-permute-start | bytes 147464 | tf_op jit(solution)/shard_map/ppermute | solution.py:253
  31.3 4.2 %collective-permute-start.7 = (bf16[24,1024]{1,0:T(8,128)(2,1)S(1)}, bf16[24,1024]{1,0:T(8,128)(2,1)S(1)}, u32[]{:S(2)}, u32[]{:S(2)}) collective-permute-start(bf16[24,1024]{1,0:T(8,128)(2,1)S(1)} %get-tuple-element.26), channel_id=1, source_target_pairs={{0,16},{2,18},{16,0},{18,2},{1,17},{3,19},{17,1},{19,3},{4,20},{6,... | collective-permute-start | bytes 147464 | tf_op jit(solution)/shard_map/ppermute | solution.py:253
  32.8 7.2 %collective-permute-start.21 = (bf16[24,1024]{1,0:T(8,128)(2,1)S(1)}, bf16[24,1024]{1,0:T(8,128)(2,1)S(1)}, u32[]{:S(2)}, u32[]{:S(2)}) collective-permute-start(bf16[24,1024]{1,0:T(8,128)(2,1)S(1)} %add_convert_fusion.4), channel_id=1, source_target_pairs={{0,8},{4,12},{8,0},{12,4},{1,9},{5,13},{9,1},{13,5},{2,10},{6,14},... | collective-permute-start | bytes 147464 | tf_op jit(solution)/shard_map/ppermute | solution.py:253
  35.5 6.1 %collective-permute-start.11 = (bf16[24,1024]{1,0:T(8,128)(2,1)S(1)}, bf16[24,1024]{1,0:T(8,128)(2,1)S(1)}, u32[]{:S(2)}, u32[]{:S(2)}) collective-permute-start(bf16[24,1024]{1,0:T(8,128)(2,1)S(1)} %fusion.2), channel_id=1, source_target_pairs={{0,4},{4,0},{8,12},{12,8},{1,5},{5,1},{9,13},{13,9},{2,6},{6,2},{1... | collective-permute-start | bytes 147464 | tf_op jit(solution)/shard_map/ppermute | solution.py:253
  36.0 5.6 %collective-permute-start.10 = (bf16[24,1024]{1,0:T(8,128)(2,1)S(1)}, bf16[24,1024]{1,0:T(8,128)(2,1)S(1)}, u32[]{:S(2)}, u32[]{:S(2)}) collective-permute-start(bf16[24,1024]{1,0:T(8,128)(2,1)S(1)} %fusion.2), channel_id=1, source_target_pairs={{0,8},{4,12},{8,0},{12,4},{1,9},{5,13},{9,1},{13,5},{2,10},{6,14},... | collective-permute-start | bytes 147464 | tf_op jit(solution)/shard_map/ppermute | solution.py:253
  38.5 5.9 %collective-permute-start.9 = (bf16[24,1024]{1,0:T(8,128)(2,1)S(1)}, bf16[24,1024]{1,0:T(8,128)(2,1)S(1)}, u32[]{:S(2)}, u32[]{:S(2)}) collective-permute-start(bf16[24,1024]{1,0:T(8,128)(2,1)S(1)} %fusion.2), channel_id=1, source_target_pairs={{0,12},{4,8},{8,4},{12,0},{1,13},{5,9},{9,5},{13,1},{2,14},{6,10},... | collective-permute-start | bytes 147464 | tf_op jit(solution)/shard_map/ppermute | solution.py:253
  39.9 8.0 %collective-permute-start.23 = (bf16[24,1024]{1,0:T(8,128)(2,1)S(1)}, bf16[24,1024]{1,0:T(8,128)(2,1)S(1)}, u32[]{:S(2)}, u32[]{:S(2)}) collective-permute-start(bf16[24,1024]{1,0:T(8,128)(2,1)S(1)} %add_convert_fusion.3.refs_14_), channel_id=1, source_target_pairs={{0,1},{1,0},{2,3},{3,2},{4,5},{5,4},{6,7},{7,6},{8,9},{9,8},{10,11... | collective-permute-start | bytes 147464 | tf_op jit(solution)/shard_map/ppermute | solution.py:253
  40.0 7.9 %collective-permute-start.22 = (bf16[24,1024]{1,0:T(8,128)(2,1)S(1)}, bf16[24,1024]{1,0:T(8,128)(2,1)S(1)}, u32[]{:S(2)}, u32[]{:S(2)}) collective-permute-start(bf16[24,1024]{1,0:T(8,128)(2,1)S(1)} %add_convert_fusion.3.refs_14_), channel_id=1, source_target_pairs={{0,2},{2,0},{1,3},{3,1},{4,6},{6,4},{5,7},{7,5},{8,10},{10,8},{9,1... | collective-permute-start | bytes 147464 | tf_op jit(solution)/shard_map/ppermute | solution.py:253
  44.4 5.1 %collective-permute-start.14 = (bf16[24,1024]{1,0:T(8,128)(2,1)S(1)}, bf16[24,1024]{1,0:T(8,128)(2,1)S(1)}, u32[]{:S(2)}, u32[]{:S(2)}) collective-permute-start(bf16[24,1024]{1,0:T(8,128)(2,1)S(1)} %add_convert_fusion.6.refs_6_), channel_id=1, source_target_pairs={{0,18},{2,16},{16,2},{18,0},{1,19},{3,17},{17,3},{19,1},{4,22},{6,... | collective-permute-start | bytes 147464 | tf_op jit(solution)/shard_map/ppermute | solution.py:253
  46.9 4.1 %collective-permute-start.13 = (bf16[24,1024]{1,0:T(8,128)(2,1)S(1)}, bf16[24,1024]{1,0:T(8,128)(2,1)S(1)}, u32[]{:S(2)}, u32[]{:S(2)}) collective-permute-start(bf16[24,1024]{1,0:T(8,128)(2,1)S(1)} %add_convert_fusion.6.refs_6_), channel_id=1, source_target_pairs={{0,16},{2,18},{16,0},{18,2},{1,17},{3,19},{17,1},{19,3},{4,20},{6,... | collective-permute-start | bytes 147464 | tf_op jit(solution)/shard_map/ppermute | solution.py:253
  47.5 4.1 %collective-permute-start.12 = (bf16[24,1024]{1,0:T(8,128)(2,1)S(1)}, bf16[24,1024]{1,0:T(8,128)(2,1)S(1)}, u32[]{:S(2)}, u32[]{:S(2)}) collective-permute-start(bf16[24,1024]{1,0:T(8,128)(2,1)S(1)} %add_convert_fusion.6.refs_6_), channel_id=1, source_target_pairs={{0,2},{2,0},{16,18},{18,16},{1,3},{3,1},{17,19},{19,17},{4,6},{6,4... | collective-permute-start | bytes 147464 | tf_op jit(solution)/shard_map/ppermute | solution.py:253
  48.0 3.6 %collective-permute-start.15 = (bf16[24,1024]{1,0:T(8,128)(2,1)S(1)}, bf16[24,1024]{1,0:T(8,128)(2,1)S(1)}, u32[]{:S(2)}, u32[]{:S(2)}) collective-permute-start(bf16[24,1024]{1,0:T(8,128)(2,1)S(1)} %add_convert_fusion.6.refs_6_), channel_id=1, source_target_pairs={{0,1},{1,0},{2,3},{3,2},{4,5},{5,4},{6,7},{7,6},{8,9},{9,8},{10,11... | collective-permute-start | bytes 147464 | tf_op jit(solution)/shard_map/ppermute | solution.py:253
  48.0 3.6 %collective-permute-start.24 = (bf16[24,1024]{1,0:T(8,128)(2,1)S(1)}, bf16[24,1024]{1,0:T(8,128)(2,1)S(1)}, u32[]{:S(2)}, u32[]{:S(2)}) collective-permute-start(bf16[24,1024]{1,0:T(8,128)(2,1)S(1)} %collective-permute-done.22.refs_15_), channel_id=1, source_target_pairs={{0,1},{1,0},{2,3},{3,2},{4,5},{5,4},{6,7},{7,6},{8,9},{9,8},{10,11... | collective-permute-start | bytes 147464 | tf_op jit(solution)/shard_map/ppermute | solution.py:253
  49.5 2.1 %collective-permute-start.18 = (bf16[24,1024]{1,0:T(8,128)(2,1)S(1)}, bf16[24,1024]{1,0:T(8,128)(2,1)S(1)}, u32[]{:S(2)}, u32[]{:S(2)}) collective-permute-start(bf16[24,1024]{1,0:T(8,128)(2,1)S(1)} %collective-permute-done.14.refs_9_), channel_id=1, source_target_pairs={{0,1},{1,0},{2,3},{3,2},{4,5},{5,4},{6,7},{7,6},{8,9},{9,8},{10,11... | collective-permute-start | bytes 147464 | tf_op jit(solution)/shard_map/ppermute | solution.py:253
  51.0 1.2 %collective-permute-start.17 = (bf16[24,1024]{1,0:T(8,128)(2,1)S(1)}, bf16[24,1024]{1,0:T(8,128)(2,1)S(1)}, u32[]{:S(2)}, u32[]{:S(2)}) collective-permute-start(bf16[24,1024]{1,0:T(8,128)(2,1)S(1)} %collective-permute-done.13.refs_8_), channel_id=1, source_target_pairs={{0,1},{1,0},{2,3},{3,2},{4,5},{5,4},{6,7},{7,6},{8,9},{9,8},{10,11... | collective-permute-start | bytes 147464 | tf_op jit(solution)/shard_map/ppermute | solution.py:253
  51.5 1.2 %collective-permute-start.16 = (bf16[24,1024]{1,0:T(8,128)(2,1)S(1)}, bf16[24,1024]{1,0:T(8,128)(2,1)S(1)}, u32[]{:S(2)}, u32[]{:S(2)}) collective-permute-start(bf16[24,1024]{1,0:T(8,128)(2,1)S(1)} %collective-permute-done.12.refs_7_), channel_id=1, source_target_pairs={{0,1},{1,0},{2,3},{3,2},{4,5},{5,4},{6,7},{7,6},{8,9},{9,8},{10,11... | collective-permute-start | bytes 147464 | tf_op jit(solution)/shard_map/ppermute | solution.py:253

commit v8 on v7

--- a/solution.py
+++ b/solution.py
@@ -29,8 +29,8 @@
     return jnp.concatenate([ref[:, columns].astype(F32) for ref in refs], axis=0)
 
 
-def own_columns(ids, i, j, width):
-    return ((ids[1] ^ j) * 2 + (ids[2] ^ i)) * width
+def own_columns(i, j, width):
+    return ((lax.axis_index("y") ^ j) * 2 + (lax.axis_index("c") ^ i)) * width
 
 
 def store_blocks(out_ref, j, columns, value, count):
@@ -39,7 +39,7 @@
         out_ref[k, j, :, columns] = value[k * rows : (k + 1) * rows].astype(BF16)
 
 
-def gates_kernel(n_dp, ids, named, weights, context, w_gate, w_up, w_down, small, *held):
+def gates_kernel(n_dp, named, weights, context, w_gate, w_up, w_down, small, *held):
     targets, sems = held[:3], held[3]
     copies = [
         pltpu.make_async_copy(source, target, sems.at[n])
@@ -51,7 +51,8 @@
         copy.wait()
     named_held, weights_held, context_held = targets
     rows, heads = context_held.shape
-    row = jnp.sum(jnp.where(named_held[...] == ids[3], weights_held[...], 0.0), axis=0, keepdims=True)
+    expert = (lax.axis_index("hi") * 2 + lax.axis_index("y")) * 2 + lax.axis_index("c")
+    row = jnp.sum(jnp.where(named_held[...] == expert, weights_held[...], 0.0), axis=0, keepdims=True)
     square = (rows, rows)
     diagonal = lax.broadcasted_iota(jnp.int32, square, 0) == lax.broadcasted_iota(jnp.int32, square, 1)
     gate = jnp.sum(jnp.where(diagonal, row, 0.0), axis=1, keepdims=True)
@@ -75,7 +76,7 @@
     return jnp.concatenate([small[:, small.shape[1] - LANES : small.shape[1] - LANES + 1] for small in smalls], axis=0)
 
 
-def hidden_kernel(n_dp, ids, *refs):
+def hidden_kernel(n_dp, *refs):
     hid = refs[:n_dp]
     gain, w_gate, w_up, pre_gate, pre_up, act, normed = refs[n_dp:]
     total = hid[0].shape[0] * n_dp
@@ -104,14 +105,14 @@
     loop(w_gate.shape[1] // STEP, hidden_units, few)
 
 
-def outward_kernel(i, n_dp, ids, *refs):
+def outward_kernel(i, n_dp, *refs):
     smalls = refs[:n_dp]
-    act, w_down, earlier, target = refs[2 * n_dp :]
+    act, w_down, *_, target = refs[n_dp:]
     weight = gates_of(smalls)
     chunk = target.shape[3]
     few = act.shape[0] <= FEW_ROWS
     for j in range(2):
-        first = own_columns(ids, i, j, chunk)
+        first = own_columns(i, j, chunk)
 
         def outward(step):
             columns = pl.ds(pl.multiple_of(first + step * STEP, STEP), STEP)
@@ -121,11 +122,11 @@
         loop(chunk // STEP, outward, few)
 
 
-def inward_part(ids, i, n_dp, grad_gate, grad_up, w_gate, w_up, target):
+def inward_part(i, n_dp, grad_gate, grad_up, w_gate, w_up, target):
     chunk = target.shape[3]
     few = grad_gate.shape[0] <= FEW_ROWS
     for j in range(2):
-        first = own_columns(ids, i, j, chunk)
+        first = own_columns(i, j, chunk)
 
         def inward(step):
             columns = pl.ds(pl.multiple_of(first + step * STEP, STEP), STEP)
@@ -136,7 +137,7 @@
         loop(chunk // STEP, inward, few)
 
 
-def backward_kernel(n_dp, ids, *refs):
+def backward_kernel(n_dp, *refs):
     grads, smalls = refs[:n_dp], refs[n_dp : 2 * n_dp]
     pre_gate, pre_up, w_down, waiting, grad_gate, grad_up, passed, rows_grad = refs[2 * n_dp :]
     passed[...] = waiting[...]
@@ -160,25 +161,30 @@
     loop(w_down.shape[0] // STEP, hidden_units, few)
 
 
-def inward_kernel(i, n_dp, ids, grad_gate, grad_up, w_gate, w_up, waiting, target, passed):
+def inward_kernel(i, n_dp, grad_gate, grad_up, w_gate, w_up, waiting, target, passed):
     passed[...] = waiting[...]
-    inward_part(ids, i, n_dp, grad_gate, grad_up, w_gate, w_up, target)
-
-
-def finish_kernel(n_dp, ids, *refs):
+    inward_part(i, n_dp, grad_gate, grad_up, w_gate, w_up, target)
+
+
+def finish_kernel(n_dp, *refs):
     hid, grads, smalls = refs[:n_dp], refs[n_dp : 2 * n_dp], refs[2 * n_dp : 3 * n_dp]
     back, moe = refs[3 * n_dp : 7 * n_dp], refs[7 * n_dp : 7 * n_dp + 4]
-    gain, w_out, output, d_hidden, d_context, d_w_out, summed, d_all = refs[7 * n_dp + 4 :]
+    gain, w_out = refs[7 * n_dp + 4 : 7 * n_dp + 6]
+    targets, held = refs[7 * n_dp + 6 : 7 * n_dp + 10], refs[7 * n_dp + 10 : 7 * n_dp + 14]
+    summed, d_all, sems = refs[7 * n_dp + 14 :]
+    output, d_hidden, d_context, d_w_out = held
+    copies = [pltpu.make_async_copy(held[n], targets[n], sems.at[n]) for n in range(4)]
     rows, width = hid[0].shape
     chunk = moe[0].shape[1]
     for i in range(2):
         for j in range(2):
-            columns = pl.ds(pl.multiple_of(own_columns(ids, i, j, chunk), chunk), chunk)
+            columns = pl.ds(pl.multiple_of(own_columns(i, j, chunk), chunk), chunk)
             for k in range(n_dp):
                 piece = back[(i * n_dp + k) * 2 + j]
                 summed[k * rows : (k + 1) * rows, columns] = piece[...].astype(F32) * gain[:, columns]
             piece = moe[i * 2 + j]
             output[:, columns] = (hid[0][:, columns].astype(F32) + piece[...].astype(F32)).astype(BF16)
+    copies[0].start()
 
     few = rows * n_dp <= FEW_ROWS
     squares = jnp.zeros((rows * n_dp, 1), F32)
@@ -199,51 +205,49 @@
         d_hidden[:, columns] = value[:rows].astype(BF16)
 
     loop(width // 512, total, few)
+    copies[1].start()
     d_context[...] = dot(d_hidden[...], w_out[...], ((1,), (1,))).astype(BF16)
     part = width // n_dp
+    copies[2].start()
     heads = d_context.shape[1]
     turned = jnp.concatenate([small[:, :heads] for small in smalls], axis=0).T.astype(BF16)
     step_width = min(part, 512)
 
     def product(step):
-        columns = pl.ds(pl.multiple_of(ids[0] * part + step * step_width, step_width), step_width)
+        columns = pl.ds(pl.multiple_of(lax.axis_index("dp") * part + step * step_width, step_width), step_width)
         d_w_out[:, pl.ds(place(step, step_width), step_width)] = dot(
             turned, d_all[:, columns], ((1,), (0,))
         ).astype(BF16)
 
     loop(part // step_width, product, few)
-
-
-def run(kernel, n_dp, ids, operands, outs, scratch, cost, name, far=(), out_space=pltpu.VMEM):
+    copies[3].start()
+    for copy in copies:
+        copy.wait()
+
+
+def run(kernel, n_dp, operands, outs, scratch, cost, name, far=(), out_space=pltpu.VMEM):
     spaces = [pltpu.HBM if n in far else pltpu.VMEM for n in range(len(operands))]
     held = [pltpu.with_memory_space_constraint(value, space) for value, space in zip(operands, spaces)]
-    kinds = [
-        pltpu.VMEM(shape, kind) if out_space is pltpu.VMEM else jax.ShapeDtypeStruct(shape, kind)
-        for shape, kind in outs
-    ]
+    kinds = [out_space(shape, kind) for shape, kind in outs]
     return pl.pallas_call(
         functools.partial(kernel, n_dp),
         out_shape=kinds,
-        in_specs=[pl.BlockSpec(memory_space=pltpu.SMEM)]
-        + [pl.BlockSpec(memory_space=space) for space in spaces],
-        out_specs=[pl.BlockSpec(memory_space=pltpu.VMEM)] * len(outs),
+        in_specs=[pl.BlockSpec(memory_space=space) for space in spaces],
+        out_specs=[pl.BlockSpec(memory_space=out_space)] * len(outs),
         scratch_shapes=scratch,
         compiler_params=pltpu.CompilerParams(vmem_limit_bytes=VMEM_LIMIT),
         cost_estimate=pl.CostEstimate(flops=0, bytes_accessed=cost, transcendentals=0),
         name=name,
-    )(ids, *held)
+    )(*held)
 
 
 def per_device(
     hidden_in, norm_gain, route_ids, route_gates, w_gate, w_up, w_down, context, w_out, grad_out
 ):
     n_dp, n_hi = lax.axis_size("dp"), lax.axis_size("hi")
-    me, hi, y, c = (lax.axis_index(name) for name in ("dp", "hi", "y", "c"))
     rows, width = hidden_in.shape
     top, heads = route_ids.shape[1], context.shape[1]
     all_rows, units, chunk = n_dp * rows, w_gate.shape[2], width // 4
-    expert = (hi * 2 + y) * 2 + c
-    ids = jnp.stack([me, y, c, expert]).astype(jnp.int32)
 
     def swap(value, axes, turn):
         sizes = [lax.axis_size(name) for name in axes]
@@ -259,7 +263,7 @@
     shares = ((n_dp, 2, rows, chunk), BF16)
     wg, wu, wd, gain = w_gate[0], w_up[0], w_down[0], norm_gain.reshape(1, width)
     (small_own,) = run(
-        gates_kernel, n_dp, ids, [route_ids.T, route_gates.T, context, wg, wu, wd],
+        gates_kernel, n_dp, [route_ids.T, route_gates.T, context, wg, wu, wd],
         [((rows, heads + LANES), F32)],
         [pltpu.VMEM((top, rows), jnp.int32), pltpu.VMEM((top, rows), F32), pltpu.VMEM((rows, heads), BF16),
          pltpu.SemaphoreType.DMA((3,))],
@@ -279,57 +283,59 @@
         return total.astype(BF16)
 
     pre_gate, pre_up, act = run(
-        hidden_kernel, n_dp, ids, hid + [gain, wg, wu],
+        hidden_kernel, n_dp, hid + [gain, wg, wu],
         [((all_rows, units), F32), ((all_rows, units), F32), ((all_rows, units), BF16)],
         [pltpu.VMEM((all_rows, width), BF16)], 2 * weights, "hidden",
     )
     (out_send,) = run(
-        functools.partial(outward_kernel, 1), n_dp, ids, smalls + grads + [act, wd, act], [shares], [],
+        functools.partial(outward_kernel, 1), n_dp, smalls + [act, wd], [shares], [],
         weights // 2, "outward_send",
     )
     out_other = swap(out_send, ("c",), 1)
     (out_keep,) = run(
-        functools.partial(outward_kernel, 0), n_dp, ids, smalls + grads + [act, wd, out_send], [shares], [],
+        functools.partial(outward_kernel, 0), n_dp, smalls + [act, wd, out_send] + grads, [shares], [],
         weights // 2, "outward_keep",
     )
     out_half = add(out_keep, out_other)
     out_blocks = [swap(out_half[k], ("dp",), k) for k in range(1, n_dp)]
     block = (shares[0][1:], BF16)
     grad_gate, grad_up, out_block = run(
-        backward_kernel, n_dp, ids, grads + smalls + [pre_gate, pre_up, wd, out_half[0]],
+        backward_kernel, n_dp, grads + smalls + [pre_gate, pre_up, wd, out_half[0]],
         [((all_rows, units), BF16), ((all_rows, units), BF16), block],
         [pltpu.VMEM((all_rows, width), BF16)], weights, "backward",
     )
     in_send, out_block = run(
-        functools.partial(inward_kernel, 1), n_dp, ids, [grad_gate, grad_up, wg, wu, out_block],
+        functools.partial(inward_kernel, 1), n_dp, [grad_gate, grad_up, wg, wu, out_block],
         [shares, block], [], weights, "inward_send",
     )
     in_other = swap(in_send, ("c",), 1)
     out_block = total_of([out_block] + out_blocks)
     out_other = swap(out_block[1], ("y",), 1)
     in_keep, out_share = run(
-        functools.partial(inward_kernel, 0), n_dp, ids, [grad_gate, grad_up, wg, wu, out_block[0]],
+        functools.partial(inward_kernel, 0), n_dp, [grad_gate, grad_up, wg, wu, out_block[0]],
         [shares, (shares[0][2:], BF16)], [], weights, "inward_keep",
     )
     out_total = add(out_share, out_other)
     in_half = add(in_keep, in_other)
     turns = [t for t in range(2 * n_dp - 1, 0, -1)]
     in_share = total_of([in_half[0, 0]] + [swap(in_half[t // 2, t % 2], ("dp", "y"), t) for t in turns])
-    in_total = total_of([in_share] + [swap(in_share, ("hi",), t) for t in range(n_hi - 1, 0, -1)])
+    in_total = total_of([in_share] + [swap(in_share, ("hi",), t) for t in range(1, n_hi)])
     turn = 1
     while turn < n_hi:
         out_total = add(out_total, swap(out_total, ("hi",), turn))
         turn = 2 * turn
-    spread = {t: swap(in_total, ("dp", "y"), t) for t in turns}
+    order = [t for t in turns if t < 2] + [t for t in turns if t >= 2]
+    spread = {t: swap(in_total, ("dp", "y"), t) for t in order}
     back = [in_total] + [spread[t] for t in range(1, 2 * n_dp)]
     moe = [out_total, swap(out_total, ("y",), 1)]
     back = back + [swap(piece, ("c",), 1) for piece in back]
     moe = moe + [swap(piece, ("c",), 1) for piece in moe]
+    outs = [((rows, width), BF16), ((rows, width), BF16), ((rows, heads), BF16), ((heads, width // n_dp), BF16)]
     return run(
-        finish_kernel, n_dp, ids, hid + grads + smalls + back + moe + [gain, w_out],
-        [((rows, width), BF16), ((rows, width), BF16), ((rows, heads), BF16), ((heads, width // n_dp), BF16)],
-        [pltpu.VMEM((all_rows, width), F32), pltpu.VMEM((all_rows, width), BF16)],
-        weights, "finish", out_space=None,
+        finish_kernel, n_dp, hid + grads + smalls + back + moe + [gain, w_out], outs,
+        [pltpu.VMEM(*out) for out in outs]
+        + [pltpu.VMEM((all_rows, width), F32), pltpu.VMEM((all_rows, width), BF16), pltpu.SemaphoreType.DMA((4,))],
+        weights, "finish", out_space=pltpu.HBM,
     )
 
 

time: 55.2 us -> 51.5 us (0.933)
  Pallas kernels: 16.9 us -> 12.4 us
    pallas_call x8, Pallas kernels: 16.9 us -> 12.4 us  [run(): pl.pallas_call(functools.partial(kernel, n_dp), out_shape=kinds, in_specs...]
  transfers between devices with their start and end apart: 25 -> 25, of which waited for: 9 -> 12; matrix products, arithmetic and copies ran while one was open for 0% -> 0% of each run, Pallas kernels for 24% -> 21%
where the time goes in v8:
time: 51.5 us; the launch traced here: 51.4 us
  starting transfers between devices  26.9 us (52%)
  Pallas kernels  12.4 us (24%)
  waiting for transfers between devices  10.5 us (20%)
  between operations  0.86 us (2%)
    ppermute x25, starting transfers between devices, swap(): return lax.ppermute(value, axes, [(i, i ^ turn) for i in range(count)])  26.9 us
    pallas_call x8, Pallas kernels, run(): pl.pallas_call(functools.partial(kernel, n_dp), out_shape=kinds, in_specs...  12.4 us
    ppermute x25, waiting for transfers between devices, swap(): return lax.ppermute(value, axes, [(i, i ^ turn) for i in range(count)])  10.5 us
  transfers between devices with their start and end apart: 25, of which 12 were waited for; matrix products, arithmetic and copies ran while one was open for 0% of the time, Pallas kernels for 21%

profile of v8, /device:TPU:0, one launch (start us, length us, event | category | flops | bytes accessed | tf_op | source)
XLA Modules:
  0.0 51.4 jit_solution(12938280256047222498)
XLA Ops:
  0.6 3.0 %collective-permute-start = (bf16[24,4096]{1,0:T(8,128)(2,1)}, bf16[24,4096]{1,0:T(8,128)(2,1)S(1)}, u32[]{:S(2)}, u32[]{:S(2)}) collective-permute-start(bf16[24,4096]{1,0:T(8,128)(2,1)} %refs_0_.5), channel_id=1, source_target_pairs={{0,16},{16,0},{1,17},{17,1},{2,18},{18,2},{3,19},{19,3},{4,20},{20... | collective-permute-start | bytes 589832 | tf_op jit(solution)/shard_map/ppermute | solution.py:257
  3.7 1.0 %gates.1.refs_0_.refs_2_.refs_4_ = f32[24,256]{1,0:T(8,128)S(1)} custom-call(s32[8,24]{1,0:T(8,128)} %bitcast.39, f32[8,24]{1,0:T(8,128)} %bitcast.40, bf16[24,128]{1,0:T(8,128)(2,1)} %context.1, bf16[4096,768]{1,0:T(8,128)(2,1)} %bitcast.29, bf16[4096,768]{1,0:T(8,128)(2,1)} %bitcast.33, bf16[768,4096]{1,0:T(8,128)(2,1)} %bitcast.25), custom_call_target="tpu_custom_call" | custom-call | bytes 25165824 | tf_op jit(solution)/shard_map/gates/pallas_call | solution.py:232
  4.7 0.1 collective-permute-start.2
  4.8 2.0 %collective-permute-start.1 = (bf16[24,4096]{1,0:T(8,128)(2,1)S(1)}, bf16[24,4096]{1,0:T(8,128)(2,1)S(1)}, u32[]{:S(2)}, u32[]{:S(2)}) collective-permute-start(bf16[24,4096]{1,0:T(8,128)(2,1)S(1)} %copy-done.3), channel_id=1, source_target_pairs={{0,16},{16,0},{1,17},{17,1},{2,18},{18,2},{3,19},{19,3},{4,20},{20... | collective-permute-start | bytes 589832 | tf_op jit(solution)/shard_map/ppermute | solution.py:257
  6.8 2.8 %collective-permute-done.refs_1_ = bf16[24,4096]{1,0:T(8,128)(2,1)S(1)} collective-permute-done((bf16[24,4096]{1,0:T(8,128)(2,1)}, bf16[24,4096]{1,0:T(8,128)(2,1)S(1)}, u32[]{:S(2)}, u32[]{:S(2)}) %collective-permute-start) | collective-permute-done | bytes 196640 | tf_op jit(solution)/shard_map/ppermute | solution.py:257
  9.6 0.0 copy-start
  9.6 2.4 %hidden.1 = (f32[48,768]{1,0:T(8,128)S(1)}, f32[48,768]{1,0:T(8,128)S(1)}, bf16[48,768]{1,0:T(8,128)(2,1)S(1)}) custom-call(bf16[24,4096]{1,0:T(8,128)(2,1)S(1)} %copy-done.5, bf16[24,4096]{1,0:T(8,128)(2,1)S(1)} %collective-permute-done.refs_1_, f32[1,4096]{1,0:T(1,128)S(1)} %bitcast.37, bf16[4096,768]{1,0:T(8,128)(2,1)S(1)} %bitcast.30, ...), custom_call_target="tpu_custom_call" | custom-call | bytes 12582912 | tf_op jit(solution)/shard_map/hidden/pallas_call | solution.py:232
  12.0 0.0 collective-permute-done.2.refs_1_.refs_3_.refs_5_
  12.0 0.3 copy-done
  12.4 0.7 %outward_send.1.refs_4_ = bf16[2,2,24,1024]{3,2,1,0:T(8,128)(2,1)S(1)} custom-call(f32[24,256]{1,0:T(8,128)S(1)} %gates.1.refs_0_.refs_2_.refs_4_, f32[24,256]{1,0:T(8,128)S(1)} %collective-permute-done.2.refs_1_.refs_3_.refs_5_, bf16[48,768]{1,0:T(8,128)(2,1)S(1)} %get-tuple-element.16.refs_2_, bf16[768,4096]{1,0:T(8,128)(2,1)S(1)} %bitcast.26), custom_call_target="tpu_custom_call" | custom-call | bytes 3145728 | tf_op jit(solution)/shard_map/outward_send/pallas_call | solution.py:232
  13.1 0.1 collective-permute-start.3
  13.1 0.3 collective-permute-done.1.refs_6_.refs_1_.refs_3_
  13.5 0.7 %outward_keep.1 = bf16[2,2,24,1024]{3,2,1,0:T(8,128)(2,1)S(1)} custom-call(f32[24,256]{1,0:T(8,128)S(1)} %gates.1.refs_0_.refs_2_.refs_4_, f32[24,256]{1,0:T(8,128)S(1)} %collective-permute-done.2.refs_1_.refs_3_.refs_5_, bf16[48,768]{1,0:T(8,128)(2,1)S(1)} %get-tuple-element.16.refs_2_, bf16[768,4096]{1,0:T(8,128)(2,1)S(1)} %bitcast.27, ...), custom_call_target="tpu_custom_call" | custom-call | bytes 3145728 | tf_op jit(solution)/shard_map/outward_keep/pallas_call | solution.py:232
  14.2 0.4 collective-permute-done.3
  14.7 2.1 %collective-permute-start.4 = (bf16[2,24,1024]{2,1,0:T(8,128)(2,1)S(1)}, bf16[2,24,1024]{2,1,0:T(8,128)(2,1)S(1)}, u32[]{:S(2)}, u32[]{:S(2)}) collective-permute-start(bf16[2,24,1024]{2,1,0:T(8,128)(2,1)S(1)} %get-tuple-element.27), channel_id=1, source_target_pairs={{0,16},{16,0},{1,17},{17,1},{2,18},{18,2},{3,19},{19,3},{4,20},{20... | collective-permute-start | bytes 294920 | tf_op jit(solution)/shard_map/ppermute | solution.py:257
  16.8 2.0 %backward.1 = (bf16[48,768]{1,0:T(8,128)(2,1)S(1)}, bf16[48,768]{1,0:T(8,128)(2,1)S(1)}, bf16[2,24,1024]{2,1,0:T(8,128)(2,1)S(1)}) custom-call(bf16[24,4096]{1,0:T(8,128)(2,1)S(1)} %copy-done.3, bf16[24,4096]{1,0:T(8,128)(2,1)S(1)} %collective-permute-done.1.refs_6_.refs_1_.refs_3_, f32[24,256]{1,0:T(8,128)S(1)} %gates.1.refs_0_.refs_2_.refs_4_, ...), custom_call_target="tpu_custom_call" | custom-call | bytes 6291456 | tf_op jit(solution)/shard_map/backward/pallas_call | solution.py:232
  18.8 2.0 %inward_send.1 = (bf16[2,2,24,1024]{3,2,1,0:T(8,128)(2,1)S(1)}, bf16[2,24,1024]{2,1,0:T(8,128)(2,1)S(1)}) custom-call(bf16[48,768]{1,0:T(8,128)(2,1)S(1)} %get-tuple-element.17.grad_gate, bf16[48,768]{1,0:T(8,128)(2,1)S(1)} %get-tuple-element.18.grad_up, bf16[4096,768]{1,0:T(8,128)(2,1)S(1)} %bitcast.31, bf16[4096,768]{1,0:T(8,128)(2,1)S(1)} %bitcast.35, ...), custom_call_target="tpu_custom_call" | custom-call | bytes 6291456 | tf_op jit(solution)/shard_map/inward_send/pallas_call | solution.py:232
  20.8 0.0 collective-permute-done.4
  20.9 1.6 %collective-permute-start.19 = (bf16[24,1024]{1,0:T(8,128)(2,1)S(1)}, bf16[24,1024]{1,0:T(8,128)(2,1)S(1)}, u32[]{:S(2)}, u32[]{:S(2)}) collective-permute-start(bf16[24,1024]{1,0:T(8,128)(2,1)S(1)} %get-tuple-element.29), channel_id=1, source_target_pairs={{0,2},{2,0},{1,3},{3,1},{4,6},{6,4},{5,7},{7,5},{8,10},{10,8},{9,1... | collective-permute-start | bytes 147464 | tf_op jit(solution)/shard_map/ppermute | solution.py:257
  22.5 0.0 collective-permute-start.5
  22.5 2.0 %inward_keep.1 = (bf16[2,2,24,1024]{3,2,1,0:T(8,128)(2,1)S(1)}, bf16[24,1024]{1,0:T(8,128)(2,1)S(1)}) custom-call(bf16[48,768]{1,0:T(8,128)(2,1)S(1)} %get-tuple-element.17.grad_gate, bf16[48,768]{1,0:T(8,128)(2,1)S(1)} %get-tuple-element.18.grad_up, bf16[4096,768]{1,0:T(8,128)(2,1)S(1)} %bitcast.32, bf16[4096,768]{1,0:T(8,128)(2,1)S(1)} %bitcast.36, ...), custom_call_target="tpu_custom_call" | custom-call | bytes 6291456 | tf_op jit(solution)/shard_map/inward_keep/pallas_call | solution.py:232
  24.4 0.6 %collective-permute-done.19 = bf16[24,1024]{1,0:T(8,128)(2,1)S(1)} collective-permute-done((bf16[24,1024]{1,0:T(8,128)(2,1)S(1)}, bf16[24,1024]{1,0:T(8,128)(2,1)S(1)}, u32[]{:S(2)}, u32[]{:S(2)}) %collective-permute-start.19) | collective-permute-done | bytes 49184 | tf_op jit(solution)/shard_map/ppermute | solution.py:257
  25.0 1.6 %collective-permute-start.20 = (bf16[24,1024]{1,0:T(8,128)(2,1)S(1)}, bf16[24,1024]{1,0:T(8,128)(2,1)S(1)}, u32[]{:S(2)}, u32[]{:S(2)}) collective-permute-start(bf16[24,1024]{1,0:T(8,128)(2,1)S(1)} %add_convert_fusion.5), channel_id=1, source_target_pairs={{0,4},{4,0},{8,12},{12,8},{1,5},{5,1},{9,13},{13,9},{2,6},{6,2},{1... | collective-permute-start | bytes 147464 | tf_op jit(solution)/shard_map/ppermute | solution.py:257
  26.7 0.0 collective-permute-done.5
  26.8 1.8 %collective-permute-start.6 = (bf16[24,1024]{1,0:T(8,128)(2,1)S(1)}, bf16[24,1024]{1,0:T(8,128)(2,1)S(1)}, u32[]{:S(2)}, u32[]{:S(2)}) collective-permute-start(bf16[24,1024]{1,0:T(8,128)(2,1)S(1)} %get-tuple-element.24), channel_id=1, source_target_pairs={{0,18},{2,16},{16,2},{18,0},{1,19},{3,17},{17,3},{19,1},{4,22},{6,... | collective-permute-start | bytes 147464 | tf_op jit(solution)/shard_map/ppermute | solution.py:257
  28.6 0.5 collective-permute-start.8
  29.1 1.2 %collective-permute-start.7 = (bf16[24,1024]{1,0:T(8,128)(2,1)S(1)}, bf16[24,1024]{1,0:T(8,128)(2,1)S(1)}, u32[]{:S(2)}, u32[]{:S(2)}) collective-permute-start(bf16[24,1024]{1,0:T(8,128)(2,1)S(1)} %get-tuple-element.26), channel_id=1, source_target_pairs={{0,16},{2,18},{16,0},{18,2},{1,17},{3,19},{17,1},{19,3},{4,20},{6,... | collective-permute-start | bytes 147464 | tf_op jit(solution)/shard_map/ppermute | solution.py:257
  30.3 0.0 collective-permute-done.20
  30.3 2.7 %collective-permute-start.21 = (bf16[24,1024]{1,0:T(8,128)(2,1)S(1)}, bf16[24,1024]{1,0:T(8,128)(2,1)S(1)}, u32[]{:S(2)}, u32[]{:S(2)}) collective-permute-start(bf16[24,1024]{1,0:T(8,128)(2,1)S(1)} %add_convert_fusion.4), channel_id=1, source_target_pairs={{0,8},{4,12},{8,0},{12,4},{1,9},{5,13},{9,1},{13,5},{2,10},{6,14},... | collective-permute-start | bytes 147464 | tf_op jit(solution)/shard_map/ppermute | solution.py:257
  33.0 0.2 collective-permute-done.7
  33.2 2.5 %collective-permute-start.11 = (bf16[24,1024]{1,0:T(8,128)(2,1)S(1)}, bf16[24,1024]{1,0:T(8,128)(2,1)S(1)}, u32[]{:S(2)}, u32[]{:S(2)}) collective-permute-start(bf16[24,1024]{1,0:T(8,128)(2,1)S(1)} %fusion.2), channel_id=1, source_target_pairs={{0,12},{4,8},{8,4},{12,0},{1,13},{5,9},{9,5},{13,1},{2,14},{6,10},... | collective-permute-start | bytes 147464 | tf_op jit(solution)/shard_map/ppermute | solution.py:257
  35.8 0.2 collective-permute-start.10
  35.9 1.7 %collective-permute-start.9 = (bf16[24,1024]{1,0:T(8,128)(2,1)S(1)}, bf16[24,1024]{1,0:T(8,128)(2,1)S(1)}, u32[]{:S(2)}, u32[]{:S(2)}) collective-permute-start(bf16[24,1024]{1,0:T(8,128)(2,1)S(1)} %fusion.2), channel_id=1, source_target_pairs={{0,4},{4,0},{8,12},{12,8},{1,5},{5,1},{9,13},{13,9},{2,6},{6,2},{1... | collective-permute-start | bytes 147464 | tf_op jit(solution)/shard_map/ppermute | solution.py:257
  37.7 0.1 collective-permute-start.23
  37.8 1.6 %collective-permute-start.22 = (bf16[24,1024]{1,0:T(8,128)(2,1)S(1)}, bf16[24,1024]{1,0:T(8,128)(2,1)S(1)}, u32[]{:S(2)}, u32[]{:S(2)}) collective-permute-start(bf16[24,1024]{1,0:T(8,128)(2,1)S(1)} %add_convert_fusion.3.refs_14_), channel_id=1, source_target_pairs={{0,2},{2,0},{1,3},{3,1},{4,6},{6,4},{5,7},{7,5},{8,10},{10,8},{9,1... | collective-permute-start | bytes 147464 | tf_op jit(solution)/shard_map/ppermute | solution.py:257
  39.4 0.1 collective-permute-done.11
  39.4 1.8 %collective-permute-done.10 = bf16[24,1024]{1,0:T(8,128)(2,1)S(1)} collective-permute-done((bf16[24,1024]{1,0:T(8,128)(2,1)S(1)}, bf16[24,1024]{1,0:T(8,128)(2,1)S(1)}, u32[]{:S(2)}, u32[]{:S(2)}) %collective-permute-start.10) | collective-permute-done | bytes 49184 | tf_op jit(solution)/shard_map/ppermute | solution.py:257
  41.3 0.0 collective-permute-done.9
  41.3 2.3 %collective-permute-start.14 = (bf16[24,1024]{1,0:T(8,128)(2,1)S(1)}, bf16[24,1024]{1,0:T(8,128)(2,1)S(1)}, u32[]{:S(2)}, u32[]{:S(2)}) collective-permute-start(bf16[24,1024]{1,0:T(8,128)(2,1)S(1)} %add_convert_fusion.6.refs_6_), channel_id=1, source_target_pairs={{0,18},{2,16},{16,2},{18,0},{1,19},{3,17},{17,3},{19,1},{4,22},{6,... | collective-permute-start | bytes 147464 | tf_op jit(solution)/shard_map/ppermute | solution.py:257
  43.6 0.8 %collective-permute-start.13 = (bf16[24,1024]{1,0:T(8,128)(2,1)S(1)}, bf16[24,1024]{1,0:T(8,128)(2,1)S(1)}, u32[]{:S(2)}, u32[]{:S(2)}) collective-permute-start(bf16[24,1024]{1,0:T(8,128)(2,1)S(1)} %add_convert_fusion.6.refs_6_), channel_id=1, source_target_pairs={{0,16},{2,18},{16,0},{18,2},{1,17},{3,19},{17,1},{19,3},{4,20},{6,... | collective-permute-start | bytes 147464 | tf_op jit(solution)/shard_map/ppermute | solution.py:257
  44.4 0.5 collective-permute-start.12
  44.9 0.5 collective-permute-start.24
  45.4 1.0 %collective-permute-done.14.refs_9_ = bf16[24,1024]{1,0:T(8,128)(2,1)S(1)} collective-permute-done((bf16[24,1024]{1,0:T(8,128)(2,1)S(1)}, bf16[24,1024]{1,0:T(8,128)(2,1)S(1)}, u32[]{:S(2)}, u32[]{:S(2)}) %collective-permute-start.14) | collective-permute-done | bytes 49184 | tf_op jit(solution)/shard_map/ppermute | solution.py:257
  46.4 1.3 %collective-permute-done.13.refs_8_ = bf16[24,1024]{1,0:T(8,128)(2,1)S(1)} collective-permute-done((bf16[24,1024]{1,0:T(8,128)(2,1)S(1)}, bf16[24,1024]{1,0:T(8,128)(2,1)S(1)}, u32[]{:S(2)}, u32[]{:S(2)}) %collective-permute-start.13) | collective-permute-done | bytes 49184 | tf_op jit(solution)/shard_map/ppermute | solution.py:257
  47.7 0.8 %collective-permute-done.12.refs_7_ = bf16[24,1024]{1,0:T(8,128)(2,1)S(1)} collective-permute-done((bf16[24,1024]{1,0:T(8,128)(2,1)S(1)}, bf16[24,1024]{1,0:T(8,128)(2,1)S(1)}, u32[]{:S(2)}, u32[]{:S(2)}) %collective-permute-start.12) | collective-permute-done | bytes 49184 | tf_op jit(solution)/shard_map/ppermute | solution.py:257
  48.5 0.4 collective-permute-done.17.refs_12_
  48.9 0.8 %collective-permute-done.16.refs_11_ = bf16[24,1024]{1,0:T(8,128)(2,1)S(1)} collective-permute-done((bf16[24,1024]{1,0:T(8,128)(2,1)S(1)}, bf16[24,1024]{1,0:T(8,128)(2,1)S(1)}, u32[]{:S(2)}, u32[]{:S(2)}) %collective-permute-start.16) | collective-permute-done | bytes 49184 | tf_op jit(solution)/shard_map/ppermute | solution.py:257
  49.7 1.7 %finish.1 = (bf16[24,4096]{1,0:T(8,128)(2,1)}, bf16[24,4096]{1,0:T(8,128)(2,1)}, bf16[24,128]{1,0:T(8,128)(2,1)}, bf16[128,2048]{1,0:T(8,128)(2,1)}) custom-call(bf16[24,4096]{1,0:T(8,128)(2,1)S(1)} %copy-done.5, bf16[24,4096]{1,0:T(8,128)(2,1)S(1)} %collective-permute-done.refs_1_, bf16[24,4096]{1,0:T(8,128)(2,1)S(1)} %copy-done.3, ...), custom_call_target="tpu_custom_call" | custom-call | bytes 6291456 | tf_op jit(solution)/shard_map/finish/pallas_call | solution.py:232
  (35 shorter events, 0.3 us)
Async XLA Ops:
  0.6 8.9 %collective-permute-start = (bf16[24,4096]{1,0:T(8,128)(2,1)}, bf16[24,4096]{1,0:T(8,128)(2,1)S(1)}, u32[]{:S(2)}, u32[]{:S(2)}) collective-permute-start(bf16[24,4096]{1,0:T(8,128)(2,1)} %refs_0_.5), channel_id=1, source_target_pairs={{0,16},{16,0},{1,17},{17,1},{2,18},{18,2},{3,19},{19,3},{4,20},{20... | collective-permute-start | bytes 589832 | tf_op jit(solution)/shard_map/ppermute | solution.py:257
  3.6 1.1 %copy-start.3 = (bf16[24,4096]{1,0:T(8,128)(2,1)S(1)}, bf16[24,4096]{1,0:T(8,128)(2,1)}, u32[]{:S(2)}) copy-start(bf16[24,4096]{1,0:T(8,128)(2,1)} %refs_2_.1) | copy-start | bytes 589828
  3.6 5.9 %copy-start.1 = (bf16[1,4096,768]{2,1,0:T(8,128)(2,1)S(1)}, bf16[1,4096,768]{2,1,0:T(8,128)(2,1)}, u32[]{:S(2)}) copy-start(bf16[1,4096,768]{2,1,0:T(8,128)(2,1)} %param.14) | copy-start | bytes 18874372
  3.6 5.9 %copy-start.2 = (bf16[1,4096,768]{2,1,0:T(8,128)(2,1)S(1)}, bf16[1,4096,768]{2,1,0:T(8,128)(2,1)}, u32[]{:S(2)}) copy-start(bf16[1,4096,768]{2,1,0:T(8,128)(2,1)} %param.15) | copy-start | bytes 18874372
  3.6 5.9 %copy-start.5 = (bf16[24,4096]{1,0:T(8,128)(2,1)S(1)}, bf16[24,4096]{1,0:T(8,128)(2,1)}, u32[]{:S(2)}) copy-start(bf16[24,4096]{1,0:T(8,128)(2,1)} %refs_0_.5) | copy-start | bytes 589828
  3.6 5.9 %copy-start.6 = (f32[4096]{0:T(1024)S(1)}, f32[4096]{0:T(1024)}, u32[]{:S(2)}) copy-start(f32[4096]{0:T(1024)} %param.11) | copy-start | bytes 49156
  4.7 7.4 %collective-permute-start.2 = (f32[24,256]{1,0:T(8,128)S(1)}, f32[24,256]{1,0:T(8,128)S(1)}, u32[]{:S(2)}, u32[]{:S(2)}) collective-permute-start(f32[24,256]{1,0:T(8,128)S(1)} %gates.1.refs_0_.refs_2_.refs_4_), channel_id=1, source_target_pairs={{0,16},{16,0},{1,17},{17,1},{2,18},{18,2},{3,19},{19,3},{4,20},{20... | collective-permute-start | bytes 73736 | tf_op jit(solution)/shard_map/ppermute | solution.py:257
  4.8 8.7 %collective-permute-start.1 = (bf16[24,4096]{1,0:T(8,128)(2,1)S(1)}, bf16[24,4096]{1,0:T(8,128)(2,1)S(1)}, u32[]{:S(2)}, u32[]{:S(2)}) collective-permute-start(bf16[24,4096]{1,0:T(8,128)(2,1)S(1)} %copy-done.3), channel_id=1, source_target_pairs={{0,16},{16,0},{1,17},{17,1},{2,18},{18,2},{3,19},{19,3},{4,20},{20... | collective-permute-start | bytes 589832 | tf_op jit(solution)/shard_map/ppermute | solution.py:257
  9.6 2.8 %copy-start = (bf16[1,768,4096]{2,1,0:T(8,128)(2,1)S(1)}, bf16[1,768,4096]{2,1,0:T(8,128)(2,1)}, u32[]{:S(2)}) copy-start(bf16[1,768,4096]{2,1,0:T(8,128)(2,1)} %param.16) | copy-start | bytes 18874372
  13.1 1.5 %collective-permute-start.3 = (bf16[2,2,24,1024]{3,2,1,0:T(8,128)(2,1)S(1)}, bf16[2,2,24,1024]{3,2,1,0:T(8,128)(2,1)S(1)}, u32[]{:S(2)}, u32[]{:S(2)}) collective-permute-start(bf16[2,2,24,1024]{3,2,1,0:T(8,128)(2,1)S(1)} %outward_send.1.refs_4_), channel_id=1, source_target_pairs={{0,1},{1,0},{2,3},{3,2},{4,5},{5,4},{6,7},{7,6},{8,9},{9,8},{10,11... | collective-permute-start | bytes 589832 | tf_op jit(solution)/shard_map/ppermute | solution.py:257
  14.7 6.2 %collective-permute-start.4 = (bf16[2,24,1024]{2,1,0:T(8,128)(2,1)S(1)}, bf16[2,24,1024]{2,1,0:T(8,128)(2,1)S(1)}, u32[]{:S(2)}, u32[]{:S(2)}) collective-permute-start(bf16[2,24,1024]{2,1,0:T(8,128)(2,1)S(1)} %get-tuple-element.27), channel_id=1, source_target_pairs={{0,16},{16,0},{1,17},{17,1},{2,18},{18,2},{3,19},{19,3},{4,20},{20... | collective-permute-start | bytes 294920 | tf_op jit(solution)/shard_map/ppermute | solution.py:257
  20.9 4.2 %collective-permute-start.19 = (bf16[24,1024]{1,0:T(8,128)(2,1)S(1)}, bf16[24,1024]{1,0:T(8,128)(2,1)S(1)}, u32[]{:S(2)}, u32[]{:S(2)}) collective-permute-start(bf16[24,1024]{1,0:T(8,128)(2,1)S(1)} %get-tuple-element.29), channel_id=1, source_target_pairs={{0,2},{2,0},{1,3},{3,1},{4,6},{6,4},{5,7},{7,5},{8,10},{10,8},{9,1... | collective-permute-start | bytes 147464 | tf_op jit(solution)/shard_map/ppermute | solution.py:257
  22.5 4.2 %collective-permute-start.5 = (bf16[2,2,24,1024]{3,2,1,0:T(8,128)(2,1)S(1)}, bf16[2,2,24,1024]{3,2,1,0:T(8,128)(2,1)S(1)}, u32[]{:S(2)}, u32[]{:S(2)}) collective-permute-start(bf16[2,2,24,1024]{3,2,1,0:T(8,128)(2,1)S(1)} %get-tuple-element.22), channel_id=1, source_target_pairs={{0,1},{1,0},{2,3},{3,2},{4,5},{5,4},{6,7},{7,6},{8,9},{9,8},{10,11... | collective-permute-start | bytes 589832 | tf_op jit(solution)/shard_map/ppermute | solution.py:257
  22.5 27.2 %copy-start.4 = (bf16[128,4096]{1,0:T(8,128)(2,1)S(1)}, bf16[128,4096]{1,0:T(8,128)(2,1)}, u32[]{:S(2)}) copy-start(bf16[128,4096]{1,0:T(8,128)(2,1)} %refs_19_.1) | copy-start | bytes 3145732
  25.0 5.3 %collective-permute-start.20 = (bf16[24,1024]{1,0:T(8,128)(2,1)S(1)}, bf16[24,1024]{1,0:T(8,128)(2,1)S(1)}, u32[]{:S(2)}, u32[]{:S(2)}) collective-permute-start(bf16[24,1024]{1,0:T(8,128)(2,1)S(1)} %add_convert_fusion.5), channel_id=1, source_target_pairs={{0,4},{4,0},{8,12},{12,8},{1,5},{5,1},{9,13},{13,9},{2,6},{6,2},{1... | collective-permute-start | bytes 147464 | tf_op jit(solution)/shard_map/ppermute | solution.py:257
  26.8 6.2 %collective-permute-start.6 = (bf16[24,1024]{1,0:T(8,128)(2,1)S(1)}, bf16[24,1024]{1,0:T(8,128)(2,1)S(1)}, u32[]{:S(2)}, u32[]{:S(2)}) collective-permute-start(bf16[24,1024]{1,0:T(8,128)(2,1)S(1)} %get-tuple-element.24), channel_id=1, source_target_pairs={{0,18},{2,16},{16,2},{18,0},{1,19},{3,17},{17,3},{19,1},{4,22},{6,... | collective-permute-start | bytes 147464 | tf_op jit(solution)/shard_map/ppermute | solution.py:257
  28.6 4.4 %collective-permute-start.8 = (bf16[24,1024]{1,0:T(8,128)(2,1)S(1)}, bf16[24,1024]{1,0:T(8,128)(2,1)S(1)}, u32[]{:S(2)}, u32[]{:S(2)}) collective-permute-start(bf16[24,1024]{1,0:T(8,128)(2,1)S(1)} %get-tuple-element.25), channel_id=1, source_target_pairs={{0,2},{2,0},{16,18},{18,16},{1,3},{3,1},{17,19},{19,17},{4,6},{6,4... | collective-permute-start | bytes 147464 | tf_op jit(solution)/shard_map/ppermute | solution.py:257
  29.1 4.1 %collective-permute-start.7 = (bf16[24,1024]{1,0:T(8,128)(2,1)S(1)}, bf16[24,1024]{1,0:T(8,128)(2,1)S(1)}, u32[]{:S(2)}, u32[]{:S(2)}) collective-permute-start(bf16[24,1024]{1,0:T(8,128)(2,1)S(1)} %get-tuple-element.26), channel_id=1, source_target_pairs={{0,16},{2,18},{16,0},{18,2},{1,17},{3,19},{17,1},{19,3},{4,20},{6,... | collective-permute-start | bytes 147464 | tf_op jit(solution)/shard_map/ppermute | solution.py:257
  30.3 7.3 %collective-permute-start.21 = (bf16[24,1024]{1,0:T(8,128)(2,1)S(1)}, bf16[24,1024]{1,0:T(8,128)(2,1)S(1)}, u32[]{:S(2)}, u32[]{:S(2)}) collective-permute-start(bf16[24,1024]{1,0:T(8,128)(2,1)S(1)} %add_convert_fusion.4), channel_id=1, source_target_pairs={{0,8},{4,12},{8,0},{12,4},{1,9},{5,13},{9,1},{13,5},{2,10},{6,14},... | collective-permute-start | bytes 147464 | tf_op jit(solution)/shard_map/ppermute | solution.py:257
  33.2 6.2 %collective-permute-start.11 = (bf16[24,1024]{1,0:T(8,128)(2,1)S(1)}, bf16[24,1024]{1,0:T(8,128)(2,1)S(1)}, u32[]{:S(2)}, u32[]{:S(2)}) collective-permute-start(bf16[24,1024]{1,0:T(8,128)(2,1)S(1)} %fusion.2), channel_id=1, source_target_pairs={{0,12},{4,8},{8,4},{12,0},{1,13},{5,9},{9,5},{13,1},{2,14},{6,10},... | collective-permute-start | bytes 147464 | tf_op jit(solution)/shard_map/ppermute | solution.py:257
  35.8 5.5 %collective-permute-start.10 = (bf16[24,1024]{1,0:T(8,128)(2,1)S(1)}, bf16[24,1024]{1,0:T(8,128)(2,1)S(1)}, u32[]{:S(2)}, u32[]{:S(2)}) collective-permute-start(bf16[24,1024]{1,0:T(8,128)(2,1)S(1)} %fusion.2), channel_id=1, source_target_pairs={{0,8},{4,12},{8,0},{12,4},{1,9},{5,13},{9,1},{13,5},{2,10},{6,14},... | collective-permute-start | bytes 147464 | tf_op jit(solution)/shard_map/ppermute | solution.py:257
  35.9 5.3 %collective-permute-start.9 = (bf16[24,1024]{1,0:T(8,128)(2,1)S(1)}, bf16[24,1024]{1,0:T(8,128)(2,1)S(1)}, u32[]{:S(2)}, u32[]{:S(2)}) collective-permute-start(bf16[24,1024]{1,0:T(8,128)(2,1)S(1)} %fusion.2), channel_id=1, source_target_pairs={{0,4},{4,0},{8,12},{12,8},{1,5},{5,1},{9,13},{13,9},{2,6},{6,2},{1... | collective-permute-start | bytes 147464 | tf_op jit(solution)/shard_map/ppermute | solution.py:257
  37.7 7.2 %collective-permute-start.23 = (bf16[24,1024]{1,0:T(8,128)(2,1)S(1)}, bf16[24,1024]{1,0:T(8,128)(2,1)S(1)}, u32[]{:S(2)}, u32[]{:S(2)}) collective-permute-start(bf16[24,1024]{1,0:T(8,128)(2,1)S(1)} %add_convert_fusion.3.refs_14_), channel_id=1, source_target_pairs={{0,1},{1,0},{2,3},{3,2},{4,5},{5,4},{6,7},{7,6},{8,9},{9,8},{10,11... | collective-permute-start | bytes 147464 | tf_op jit(solution)/shard_map/ppermute | solution.py:257
  37.8 7.1 %collective-permute-start.22 = (bf16[24,1024]{1,0:T(8,128)(2,1)S(1)}, bf16[24,1024]{1,0:T(8,128)(2,1)S(1)}, u32[]{:S(2)}, u32[]{:S(2)}) collective-permute-start(bf16[24,1024]{1,0:T(8,128)(2,1)S(1)} %add_convert_fusion.3.refs_14_), channel_id=1, source_target_pairs={{0,2},{2,0},{1,3},{3,1},{4,6},{6,4},{5,7},{7,5},{8,10},{10,8},{9,1... | collective-permute-start | bytes 147464 | tf_op jit(solution)/shard_map/ppermute | solution.py:257
  41.3 5.1 %collective-permute-start.14 = (bf16[24,1024]{1,0:T(8,128)(2,1)S(1)}, bf16[24,1024]{1,0:T(8,128)(2,1)S(1)}, u32[]{:S(2)}, u32[]{:S(2)}) collective-permute-start(bf16[24,1024]{1,0:T(8,128)(2,1)S(1)} %add_convert_fusion.6.refs_6_), channel_id=1, source_target_pairs={{0,18},{2,16},{16,2},{18,0},{1,19},{3,17},{17,3},{19,1},{4,22},{6,... | collective-permute-start | bytes 147464 | tf_op jit(solution)/shard_map/ppermute | solution.py:257
  43.6 4.1 %collective-permute-start.13 = (bf16[24,1024]{1,0:T(8,128)(2,1)S(1)}, bf16[24,1024]{1,0:T(8,128)(2,1)S(1)}, u32[]{:S(2)}, u32[]{:S(2)}) collective-permute-start(bf16[24,1024]{1,0:T(8,128)(2,1)S(1)} %add_convert_fusion.6.refs_6_), channel_id=1, source_target_pairs={{0,16},{2,18},{16,0},{18,2},{1,17},{3,19},{17,1},{19,3},{4,20},{6,... | collective-permute-start | bytes 147464 | tf_op jit(solution)/shard_map/ppermute | solution.py:257
  44.4 4.1 %collective-permute-start.12 = (bf16[24,1024]{1,0:T(8,128)(2,1)S(1)}, bf16[24,1024]{1,0:T(8,128)(2,1)S(1)}, u32[]{:S(2)}, u32[]{:S(2)}) collective-permute-start(bf16[24,1024]{1,0:T(8,128)(2,1)S(1)} %add_convert_fusion.6.refs_6_), channel_id=1, source_target_pairs={{0,2},{2,0},{16,18},{18,16},{1,3},{3,1},{17,19},{19,17},{4,6},{6,4... | collective-permute-start | bytes 147464 | tf_op jit(solution)/shard_map/ppermute | solution.py:257
  44.9 3.6 %collective-permute-start.15 = (bf16[24,1024]{1,0:T(8,128)(2,1)S(1)}, bf16[24,1024]{1,0:T(8,128)(2,1)S(1)}, u32[]{:S(2)}, u32[]{:S(2)}) collective-permute-start(bf16[24,1024]{1,0:T(8,128)(2,1)S(1)} %add_convert_fusion.6.refs_6_), channel_id=1, source_target_pairs={{0,1},{1,0},{2,3},{3,2},{4,5},{5,4},{6,7},{7,6},{8,9},{9,8},{10,11... | collective-permute-start | bytes 147464 | tf_op jit(solution)/shard_map/ppermute | solution.py:257
  44.9 3.6 %collective-permute-start.24 = (bf16[24,1024]{1,0:T(8,128)(2,1)S(1)}, bf16[24,1024]{1,0:T(8,128)(2,1)S(1)}, u32[]{:S(2)}, u32[]{:S(2)}) collective-permute-start(bf16[24,1024]{1,0:T(8,128)(2,1)S(1)} %collective-permute-done.22.refs_15_), channel_id=1, source_target_pairs={{0,1},{1,0},{2,3},{3,2},{4,5},{5,4},{6,7},{7,6},{8,9},{9,8},{10,11... | collective-permute-start | bytes 147464 | tf_op jit(solution)/shard_map/ppermute | solution.py:257
  46.4 2.1 %collective-permute-start.18 = (bf16[24,1024]{1,0:T(8,128)(2,1)S(1)}, bf16[24,1024]{1,0:T(8,128)(2,1)S(1)}, u32[]{:S(2)}, u32[]{:S(2)}) collective-permute-start(bf16[24,1024]{1,0:T(8,128)(2,1)S(1)} %collective-permute-done.14.refs_9_), channel_id=1, source_target_pairs={{0,1},{1,0},{2,3},{3,2},{4,5},{5,4},{6,7},{7,6},{8,9},{9,8},{10,11... | collective-permute-start | bytes 147464 | tf_op jit(solution)/shard_map/ppermute | solution.py:257
  47.7 1.2 %collective-permute-start.17 = (bf16[24,1024]{1,0:T(8,128)(2,1)S(1)}, bf16[24,1024]{1,0:T(8,128)(2,1)S(1)}, u32[]{:S(2)}, u32[]{:S(2)}) collective-permute-start(bf16[24,1024]{1,0:T(8,128)(2,1)S(1)} %collective-permute-done.13.refs_8_), channel_id=1, source_target_pairs={{0,1},{1,0},{2,3},{3,2},{4,5},{5,4},{6,7},{7,6},{8,9},{9,8},{10,11... | collective-permute-start | bytes 147464 | tf_op jit(solution)/shard_map/ppermute | solution.py:257
  48.4 1.2 %collective-permute-start.16 = (bf16[24,1024]{1,0:T(8,128)(2,1)S(1)}, bf16[24,1024]{1,0:T(8,128)(2,1)S(1)}, u32[]{:S(2)}, u32[]{:S(2)}) collective-permute-start(bf16[24,1024]{1,0:T(8,128)(2,1)S(1)} %collective-permute-done.12.refs_7_), channel_id=1, source_target_pairs={{0,1},{1,0},{2,3},{3,2},{4,5},{5,4},{6,7},{7,6},{8,9},{9,8},{10,11... | collective-permute-start | bytes 147464 | tf_op jit(solution)/shard_map/ppermute | solution.py:257

commit v9 on v8

--- a/solution.py
+++ b/solution.py
@@ -166,6 +166,14 @@
     inward_part(i, n_dp, grad_gate, grad_up, w_gate, w_up, target)
 
 
+def join_kernel(n_dp, in_keep, in_other, out_block, *refs):
+    for t in range(2 * n_dp):
+        k, j = t // 2, t % 2
+        refs[t][...] = (in_keep[k, j].astype(F32) + in_other[k, j].astype(F32)).astype(BF16)
+    for j, target in enumerate(refs[-2:]):
+        target[...] = out_block[j]
+
+
 def finish_kernel(n_dp, *refs):
     hid, grads, smalls = refs[:n_dp], refs[n_dp : 2 * n_dp], refs[2 * n_dp : 3 * n_dp]
     back, moe = refs[3 * n_dp : 7 * n_dp], refs[7 * n_dp : 7 * n_dp + 4]
@@ -310,15 +318,17 @@
     )
     in_other = swap(in_send, ("c",), 1)
     out_block = total_of([out_block] + out_blocks)
-    out_other = swap(out_block[1], ("y",), 1)
-    in_keep, out_share = run(
-        functools.partial(inward_kernel, 0), n_dp, [grad_gate, grad_up, wg, wu, out_block[0]],
-        [shares, (shares[0][2:], BF16)], [], weights, "inward_keep",
-    )
-    out_total = add(out_share, out_other)
-    in_half = add(in_keep, in_other)
+    in_keep, out_block = run(
+        functools.partial(inward_kernel, 0), n_dp, [grad_gate, grad_up, wg, wu, out_block], [shares, block], [],
+        weights, "inward_keep",
+    )
+    *in_pieces, out_share, out_piece = run(
+        join_kernel, n_dp, [in_keep, in_other, out_block], [((rows, chunk), BF16)] * (2 * n_dp + 2), [],
+        rows * width, "join",
+    )
     turns = [t for t in range(2 * n_dp - 1, 0, -1)]
-    in_share = total_of([in_half[0, 0]] + [swap(in_half[t // 2, t % 2], ("dp", "y"), t) for t in turns])
+    in_share = total_of([in_pieces[0]] + [swap(in_pieces[t], ("dp", "y"), t) for t in turns])
+    out_total = add(out_share, swap(out_piece, ("y",), 1))
     in_total = total_of([in_share] + [swap(in_share, ("hi",), t) for t in range(1, n_hi)])
     turn = 1
     while turn < n_hi:

time: 51.5 us -> 50.8 us (0.986)
  starting transfers between devices: 26.9 us -> 25.8 us
    ppermute x25, starting transfers between devices: 26.9 us -> 25.8 us  [swap(): return lax.ppermute(value, axes, [(i, i ^ turn) for i in range(count)])]
    pallas_call x8 -> x9, Pallas kernels: 12.4 us -> 12.5 us  [run(): pl.pallas_call(functools.partial(kernel, n_dp), out_shape=kinds, in_specs...]
where the time goes in v9:
time: 50.8 us; the launch traced here: 50.6 us
  starting transfers between devices  25.8 us (51%)
  Pallas kernels  12.5 us (25%)
  waiting for transfers between devices  10.9 us (21%)
  between operations  0.85 us (2%)
    ppermute x25, starting transfers between devices, swap(): return lax.ppermute(value, axes, [(i, i ^ turn) for i in range(count)])  25.8 us
    pallas_call x9, Pallas kernels, run(): pl.pallas_call(functools.partial(kernel, n_dp), out_shape=kinds, in_specs...  12.5 us
    ppermute x25, waiting for transfers between devices, swap(): return lax.ppermute(value, axes, [(i, i ^ turn) for i in range(count)])  10.9 us
  transfers between devices with their start and end apart: 25, of which 12 were waited for; matrix products, arithmetic and copies ran while one was open for 0% of the time, Pallas kernels for 21%

profile of v9, /device:TPU:0, one launch (start us, length us, event | category | flops | bytes accessed | tf_op | source)
XLA Modules:
  0.0 50.6 jit_solution(7701701780001182512)
XLA Ops:
  0.6 3.0 %collective-permute-start = (bf16[24,4096]{1,0:T(8,128)(2,1)}, bf16[24,4096]{1,0:T(8,128)(2,1)S(1)}, u32[]{:S(2)}, u32[]{:S(2)}) collective-permute-start(bf16[24,4096]{1,0:T(8,128)(2,1)} %refs_0_.5), channel_id=1, source_target_pairs={{0,16},{16,0},{1,17},{17,1},{2,18},{18,2},{3,19},{19,3},{4,20},{20... | collective-permute-start | bytes 589832 | tf_op jit(solution)/shard_map/ppermute | solution.py:265
  3.7 1.0 %gates.1.refs_0_.refs_2_.refs_4_ = f32[24,256]{1,0:T(8,128)S(1)} custom-call(s32[8,24]{1,0:T(8,128)} %bitcast.24, f32[8,24]{1,0:T(8,128)} %bitcast.25, bf16[24,128]{1,0:T(8,128)(2,1)} %context.1, bf16[4096,768]{1,0:T(8,128)(2,1)} %bitcast.14, bf16[4096,768]{1,0:T(8,128)(2,1)} %bitcast.18, bf16[768,4096]{1,0:T(8,128)(2,1)} %bitcast.10), custom_call_target="tpu_custom_call" | custom-call | bytes 25165824 | tf_op jit(solution)/shard_map/gates/pallas_call | solution.py:240
  4.7 0.1 collective-permute-start.2
  4.8 2.0 %collective-permute-start.1 = (bf16[24,4096]{1,0:T(8,128)(2,1)S(1)}, bf16[24,4096]{1,0:T(8,128)(2,1)S(1)}, u32[]{:S(2)}, u32[]{:S(2)}) collective-permute-start(bf16[24,4096]{1,0:T(8,128)(2,1)S(1)} %copy-done.3), channel_id=1, source_target_pairs={{0,16},{16,0},{1,17},{17,1},{2,18},{18,2},{3,19},{19,3},{4,20},{20... | collective-permute-start | bytes 589832 | tf_op jit(solution)/shard_map/ppermute | solution.py:265
  6.8 2.8 %collective-permute-done.refs_1_ = bf16[24,4096]{1,0:T(8,128)(2,1)S(1)} collective-permute-done((bf16[24,4096]{1,0:T(8,128)(2,1)}, bf16[24,4096]{1,0:T(8,128)(2,1)S(1)}, u32[]{:S(2)}, u32[]{:S(2)}) %collective-permute-start) | collective-permute-done | bytes 196640 | tf_op jit(solution)/shard_map/ppermute | solution.py:265
  9.6 0.0 copy-start
  9.6 2.4 %hidden.1 = (f32[48,768]{1,0:T(8,128)S(1)}, f32[48,768]{1,0:T(8,128)S(1)}, bf16[48,768]{1,0:T(8,128)(2,1)S(1)}) custom-call(bf16[24,4096]{1,0:T(8,128)(2,1)S(1)} %copy-done.5, bf16[24,4096]{1,0:T(8,128)(2,1)S(1)} %collective-permute-done.refs_1_, f32[1,4096]{1,0:T(1,128)S(1)} %bitcast.22, bf16[4096,768]{1,0:T(8,128)(2,1)S(1)} %bitcast.15, ...), custom_call_target="tpu_custom_call" | custom-call | bytes 12582912 | tf_op jit(solution)/shard_map/hidden/pallas_call | solution.py:240
  12.0 0.0 collective-permute-done.2.refs_1_.refs_3_.refs_5_
  12.0 0.3 copy-done
  12.4 0.7 %outward_send.1.refs_4_ = bf16[2,2,24,1024]{3,2,1,0:T(8,128)(2,1)S(1)} custom-call(f32[24,256]{1,0:T(8,128)S(1)} %gates.1.refs_0_.refs_2_.refs_4_, f32[24,256]{1,0:T(8,128)S(1)} %collective-permute-done.2.refs_1_.refs_3_.refs_5_, bf16[48,768]{1,0:T(8,128)(2,1)S(1)} %get-tuple-element.22.refs_2_, bf16[768,4096]{1,0:T(8,128)(2,1)S(1)} %bitcast.11), custom_call_target="tpu_custom_call" | custom-call | bytes 3145728 | tf_op jit(solution)/shard_map/outward_send/pallas_call | solution.py:240
  13.1 0.1 collective-permute-start.3
  13.1 0.3 collective-permute-done.1.refs_6_.refs_1_.refs_3_
  13.5 0.7 %outward_keep.1 = bf16[2,2,24,1024]{3,2,1,0:T(8,128)(2,1)S(1)} custom-call(f32[24,256]{1,0:T(8,128)S(1)} %gates.1.refs_0_.refs_2_.refs_4_, f32[24,256]{1,0:T(8,128)S(1)} %collective-permute-done.2.refs_1_.refs_3_.refs_5_, bf16[48,768]{1,0:T(8,128)(2,1)S(1)} %get-tuple-element.22.refs_2_, bf16[768,4096]{1,0:T(8,128)(2,1)S(1)} %bitcast.12, ...), custom_call_target="tpu_custom_call" | custom-call | bytes 3145728 | tf_op jit(solution)/shard_map/outward_keep/pallas_call | solution.py:240
  14.2 0.4 collective-permute-done.3
  14.7 2.1 %collective-permute-start.4 = (bf16[2,24,1024]{2,1,0:T(8,128)(2,1)S(1)}, bf16[2,24,1024]{2,1,0:T(8,128)(2,1)S(1)}, u32[]{:S(2)}, u32[]{:S(2)}) collective-permute-start(bf16[2,24,1024]{2,1,0:T(8,128)(2,1)S(1)} %get-tuple-element.36), channel_id=1, source_target_pairs={{0,16},{16,0},{1,17},{17,1},{2,18},{18,2},{3,19},{19,3},{4,20},{20... | collective-permute-start | bytes 294920 | tf_op jit(solution)/shard_map/ppermute | solution.py:265
  16.8 2.0 %backward.1 = (bf16[48,768]{1,0:T(8,128)(2,1)S(1)}, bf16[48,768]{1,0:T(8,128)(2,1)S(1)}, bf16[2,24,1024]{2,1,0:T(8,128)(2,1)S(1)}) custom-call(bf16[24,4096]{1,0:T(8,128)(2,1)S(1)} %copy-done.3, bf16[24,4096]{1,0:T(8,128)(2,1)S(1)} %collective-permute-done.1.refs_6_.refs_1_.refs_3_, f32[24,256]{1,0:T(8,128)S(1)} %gates.1.refs_0_.refs_2_.refs_4_, ...), custom_call_target="tpu_custom_call" | custom-call | bytes 6291456 | tf_op jit(solution)/shard_map/backward/pallas_call | solution.py:240
  18.8 2.0 %inward_send.1 = (bf16[2,2,24,1024]{3,2,1,0:T(8,128)(2,1)S(1)}, bf16[2,24,1024]{2,1,0:T(8,128)(2,1)S(1)}) custom-call(bf16[48,768]{1,0:T(8,128)(2,1)S(1)} %get-tuple-element.23.grad_gate, bf16[48,768]{1,0:T(8,128)(2,1)S(1)} %get-tuple-element.24.grad_up, bf16[4096,768]{1,0:T(8,128)(2,1)S(1)} %bitcast.16, bf16[4096,768]{1,0:T(8,128)(2,1)S(1)} %bitcast.20, ...), custom_call_target="tpu_custom_call" | custom-call | bytes 6291456 | tf_op jit(solution)/shard_map/inward_send/pallas_call | solution.py:240
  20.8 0.1 collective-permute-start.5
  20.9 0.0 collective-permute-done.4
  20.9 0.0 copy-start.4
  20.9 2.0 %inward_keep.1 = (bf16[2,2,24,1024]{3,2,1,0:T(8,128)(2,1)S(1)}, bf16[2,24,1024]{2,1,0:T(8,128)(2,1)S(1)}) custom-call(bf16[48,768]{1,0:T(8,128)(2,1)S(1)} %get-tuple-element.23.grad_gate, bf16[48,768]{1,0:T(8,128)(2,1)S(1)} %get-tuple-element.24.grad_up, bf16[4096,768]{1,0:T(8,128)(2,1)S(1)} %bitcast.17, bf16[4096,768]{1,0:T(8,128)(2,1)S(1)} %bitcast.21, ...), custom_call_target="tpu_custom_call" | custom-call | bytes 6291456 | tf_op jit(solution)/shard_map/inward_keep/pallas_call | solution.py:240
  22.9 0.1 join.1
  23.0 1.6 %collective-permute-start.19 = (bf16[24,1024]{1,0:T(8,128)(2,1)S(1)}, bf16[24,1024]{1,0:T(8,128)(2,1)S(1)}, u32[]{:S(2)}, u32[]{:S(2)}) collective-permute-start(bf16[24,1024]{1,0:T(8,128)(2,1)S(1)} %get-tuple-element.35), channel_id=1, source_target_pairs={{0,2},{2,0},{1,3},{3,1},{4,6},{6,4},{5,7},{7,5},{8,10},{10,8},{9,1... | collective-permute-start | bytes 147464 | tf_op jit(solution)/shard_map/ppermute | solution.py:265
  24.6 0.7 %collective-permute-start.6 = (bf16[24,1024]{1,0:T(8,128)(2,1)S(1)}, bf16[24,1024]{1,0:T(8,128)(2,1)S(1)}, u32[]{:S(2)}, u32[]{:S(2)}) collective-permute-start(bf16[24,1024]{1,0:T(8,128)(2,1)S(1)} %get-tuple-element.31), channel_id=1, source_target_pairs={{0,18},{2,16},{16,2},{18,0},{1,19},{3,17},{17,3},{19,1},{4,22},{6,... | collective-permute-start | bytes 147464 | tf_op jit(solution)/shard_map/ppermute | solution.py:265
  25.2 1.3 %collective-permute-start.7 = (bf16[24,1024]{1,0:T(8,128)(2,1)S(1)}, bf16[24,1024]{1,0:T(8,128)(2,1)S(1)}, u32[]{:S(2)}, u32[]{:S(2)}) collective-permute-start(bf16[24,1024]{1,0:T(8,128)(2,1)S(1)} %get-tuple-element.32), channel_id=1, source_target_pairs={{0,16},{2,18},{16,0},{18,2},{1,17},{3,19},{17,1},{19,3},{4,20},{6,... | collective-permute-start | bytes 147464 | tf_op jit(solution)/shard_map/ppermute | solution.py:265
  26.6 1.5 %collective-permute-start.8 = (bf16[24,1024]{1,0:T(8,128)(2,1)S(1)}, bf16[24,1024]{1,0:T(8,128)(2,1)S(1)}, u32[]{:S(2)}, u32[]{:S(2)}) collective-permute-start(bf16[24,1024]{1,0:T(8,128)(2,1)S(1)} %get-tuple-element.33), channel_id=1, source_target_pairs={{0,2},{2,0},{16,18},{18,16},{1,3},{3,1},{17,19},{19,17},{4,6},{6,4... | collective-permute-start | bytes 147464 | tf_op jit(solution)/shard_map/ppermute | solution.py:265
  28.1 1.6 %collective-permute-start.20 = (bf16[24,1024]{1,0:T(8,128)(2,1)S(1)}, bf16[24,1024]{1,0:T(8,128)(2,1)S(1)}, u32[]{:S(2)}, u32[]{:S(2)}) collective-permute-start(bf16[24,1024]{1,0:T(8,128)(2,1)S(1)} %add_convert_fusion.4), channel_id=1, source_target_pairs={{0,4},{4,0},{8,12},{12,8},{1,5},{5,1},{9,13},{13,9},{2,6},{6,2},{1... | collective-permute-start | bytes 147464 | tf_op jit(solution)/shard_map/ppermute | solution.py:265
  29.7 0.1 collective-permute-done.6
  29.9 0.0 collective-permute-done.7
  29.9 0.8 %collective-permute-done.8 = bf16[24,1024]{1,0:T(8,128)(2,1)S(1)} collective-permute-done((bf16[24,1024]{1,0:T(8,128)(2,1)S(1)}, bf16[24,1024]{1,0:T(8,128)(2,1)S(1)}, u32[]{:S(2)}, u32[]{:S(2)}) %collective-permute-start.8) | collective-permute-done | bytes 49184 | tf_op jit(solution)/shard_map/ppermute | solution.py:265
  30.7 3.7 %collective-permute-start.11 = (bf16[24,1024]{1,0:T(8,128)(2,1)S(1)}, bf16[24,1024]{1,0:T(8,128)(2,1)S(1)}, u32[]{:S(2)}, u32[]{:S(2)}) collective-permute-start(bf16[24,1024]{1,0:T(8,128)(2,1)S(1)} %add_convert_fusion.6), channel_id=1, source_target_pairs={{0,12},{4,8},{8,4},{12,0},{1,13},{5,9},{9,5},{13,1},{2,14},{6,10},... | collective-permute-start | bytes 147464 | tf_op jit(solution)/shard_map/ppermute | solution.py:265
  34.3 0.8 %collective-permute-start.9 = (bf16[24,1024]{1,0:T(8,128)(2,1)S(1)}, bf16[24,1024]{1,0:T(8,128)(2,1)S(1)}, u32[]{:S(2)}, u32[]{:S(2)}) collective-permute-start(bf16[24,1024]{1,0:T(8,128)(2,1)S(1)} %add_convert_fusion.6), channel_id=1, source_target_pairs={{0,4},{4,0},{8,12},{12,8},{1,5},{5,1},{9,13},{13,9},{2,6},{6,2},{1... | collective-permute-start | bytes 147464 | tf_op jit(solution)/shard_map/ppermute | solution.py:265
  35.2 2.2 %collective-permute-start.21 = (bf16[24,1024]{1,0:T(8,128)(2,1)S(1)}, bf16[24,1024]{1,0:T(8,128)(2,1)S(1)}, u32[]{:S(2)}, u32[]{:S(2)}) collective-permute-start(bf16[24,1024]{1,0:T(8,128)(2,1)S(1)} %add_convert_fusion.3), channel_id=1, source_target_pairs={{0,8},{4,12},{8,0},{12,4},{1,9},{5,13},{9,1},{13,5},{2,10},{6,14},... | collective-permute-start | bytes 147464 | tf_op jit(solution)/shard_map/ppermute | solution.py:265
  37.4 2.5 %collective-permute-done.10 = bf16[24,1024]{1,0:T(8,128)(2,1)S(1)} collective-permute-done((bf16[24,1024]{1,0:T(8,128)(2,1)S(1)}, bf16[24,1024]{1,0:T(8,128)(2,1)S(1)}, u32[]{:S(2)}, u32[]{:S(2)}) %collective-permute-start.10) | collective-permute-done | bytes 49184 | tf_op jit(solution)/shard_map/ppermute | solution.py:265
  39.9 0.1 collective-permute-start.15
  40.0 1.2 %collective-permute-start.14 = (bf16[24,1024]{1,0:T(8,128)(2,1)S(1)}, bf16[24,1024]{1,0:T(8,128)(2,1)S(1)}, u32[]{:S(2)}, u32[]{:S(2)}) collective-permute-start(bf16[24,1024]{1,0:T(8,128)(2,1)S(1)} %add_convert_fusion.5.refs_6_), channel_id=1, source_target_pairs={{0,18},{2,16},{16,2},{18,0},{1,19},{3,17},{17,3},{19,1},{4,22},{6,... | collective-permute-start | bytes 147464 | tf_op jit(solution)/shard_map/ppermute | solution.py:265
  41.2 1.7 %collective-permute-start.13 = (bf16[24,1024]{1,0:T(8,128)(2,1)S(1)}, bf16[24,1024]{1,0:T(8,128)(2,1)S(1)}, u32[]{:S(2)}, u32[]{:S(2)}) collective-permute-start(bf16[24,1024]{1,0:T(8,128)(2,1)S(1)} %add_convert_fusion.5.refs_6_), channel_id=1, source_target_pairs={{0,16},{2,18},{16,0},{18,2},{1,17},{3,19},{17,1},{19,3},{4,20},{6,... | collective-permute-start | bytes 147464 | tf_op jit(solution)/shard_map/ppermute | solution.py:265
  42.9 0.7 %collective-permute-start.12 = (bf16[24,1024]{1,0:T(8,128)(2,1)S(1)}, bf16[24,1024]{1,0:T(8,128)(2,1)S(1)}, u32[]{:S(2)}, u32[]{:S(2)}) collective-permute-start(bf16[24,1024]{1,0:T(8,128)(2,1)S(1)} %add_convert_fusion.5.refs_6_), channel_id=1, source_target_pairs={{0,2},{2,0},{16,18},{18,16},{1,3},{3,1},{17,19},{19,17},{4,6},{6,4... | collective-permute-start | bytes 147464 | tf_op jit(solution)/shard_map/ppermute | solution.py:265
  43.6 1.4 %collective-permute-start.22 = (bf16[24,1024]{1,0:T(8,128)(2,1)S(1)}, bf16[24,1024]{1,0:T(8,128)(2,1)S(1)}, u32[]{:S(2)}, u32[]{:S(2)}) collective-permute-start(bf16[24,1024]{1,0:T(8,128)(2,1)S(1)} %add_convert_fusion.2.refs_14_), channel_id=1, source_target_pairs={{0,2},{2,0},{1,3},{3,1},{4,6},{6,4},{5,7},{7,5},{8,10},{10,8},{9,1... | collective-permute-start | bytes 147464 | tf_op jit(solution)/shard_map/ppermute | solution.py:265
  45.0 0.5 collective-permute-done.14.refs_9_
  45.5 0.0 collective-permute-start.18
  45.5 0.5 collective-permute-done.13.refs_8_
  46.0 0.0 collective-permute-start.17
  46.0 1.0 %collective-permute-done.12.refs_7_ = bf16[24,1024]{1,0:T(8,128)(2,1)S(1)} collective-permute-done((bf16[24,1024]{1,0:T(8,128)(2,1)S(1)}, bf16[24,1024]{1,0:T(8,128)(2,1)S(1)}, u32[]{:S(2)}, u32[]{:S(2)}) %collective-permute-start.12) | collective-permute-done | bytes 49184 | tf_op jit(solution)/shard_map/ppermute | solution.py:265
  47.0 0.7 %collective-permute-done.22.refs_15_ = bf16[24,1024]{1,0:T(8,128)(2,1)S(1)} collective-permute-done((bf16[24,1024]{1,0:T(8,128)(2,1)S(1)}, bf16[24,1024]{1,0:T(8,128)(2,1)S(1)}, u32[]{:S(2)}, u32[]{:S(2)}) %collective-permute-start.22) | collective-permute-done | bytes 49184 | tf_op jit(solution)/shard_map/ppermute | solution.py:265
  47.7 0.5 collective-permute-done.16.refs_11_
  48.2 0.7 %collective-permute-done.24.refs_17_ = bf16[24,1024]{1,0:T(8,128)(2,1)S(1)} collective-permute-done((bf16[24,1024]{1,0:T(8,128)(2,1)S(1)}, bf16[24,1024]{1,0:T(8,128)(2,1)S(1)}, u32[]{:S(2)}, u32[]{:S(2)}) %collective-permute-start.24) | collective-permute-done | bytes 49184 | tf_op jit(solution)/shard_map/ppermute | solution.py:265
  48.9 1.7 %finish.1 = (bf16[24,4096]{1,0:T(8,128)(2,1)}, bf16[24,4096]{1,0:T(8,128)(2,1)}, bf16[24,128]{1,0:T(8,128)(2,1)}, bf16[128,2048]{1,0:T(8,128)(2,1)}) custom-call(bf16[24,4096]{1,0:T(8,128)(2,1)S(1)} %copy-done.5, bf16[24,4096]{1,0:T(8,128)(2,1)S(1)} %collective-permute-done.refs_1_, bf16[24,4096]{1,0:T(8,128)(2,1)S(1)} %copy-done.3, ...), custom_call_target="tpu_custom_call" | custom-call | bytes 6291456 | tf_op jit(solution)/shard_map/finish/pallas_call | solution.py:240
  (33 shorter events, 0.3 us)
Async XLA Ops:
  0.6 8.9 %collective-permute-start = (bf16[24,4096]{1,0:T(8,128)(2,1)}, bf16[24,4096]{1,0:T(8,128)(2,1)S(1)}, u32[]{:S(2)}, u32[]{:S(2)}) collective-permute-start(bf16[24,4096]{1,0:T(8,128)(2,1)} %refs_0_.5), channel_id=1, source_target_pairs={{0,16},{16,0},{1,17},{17,1},{2,18},{18,2},{3,19},{19,3},{4,20},{20... | collective-permute-start | bytes 589832 | tf_op jit(solution)/shard_map/ppermute | solution.py:265
  3.6 1.1 %copy-start.3 = (bf16[24,4096]{1,0:T(8,128)(2,1)S(1)}, bf16[24,4096]{1,0:T(8,128)(2,1)}, u32[]{:S(2)}) copy-start(bf16[24,4096]{1,0:T(8,128)(2,1)} %refs_2_.1) | copy-start | bytes 589828
  3.6 5.9 %copy-start.1 = (bf16[1,4096,768]{2,1,0:T(8,128)(2,1)S(1)}, bf16[1,4096,768]{2,1,0:T(8,128)(2,1)}, u32[]{:S(2)}) copy-start(bf16[1,4096,768]{2,1,0:T(8,128)(2,1)} %param.14) | copy-start | bytes 18874372
  3.6 5.9 %copy-start.2 = (bf16[1,4096,768]{2,1,0:T(8,128)(2,1)S(1)}, bf16[1,4096,768]{2,1,0:T(8,128)(2,1)}, u32[]{:S(2)}) copy-start(bf16[1,4096,768]{2,1,0:T(8,128)(2,1)} %param.15) | copy-start | bytes 18874372
  3.6 5.9 %copy-start.5 = (bf16[24,4096]{1,0:T(8,128)(2,1)S(1)}, bf16[24,4096]{1,0:T(8,128)(2,1)}, u32[]{:S(2)}) copy-start(bf16[24,4096]{1,0:T(8,128)(2,1)} %refs_0_.5) | copy-start | bytes 589828
  3.6 5.9 %copy-start.6 = (f32[4096]{0:T(1024)S(1)}, f32[4096]{0:T(1024)}, u32[]{:S(2)}) copy-start(f32[4096]{0:T(1024)} %param.11) | copy-start | bytes 49156
  4.7 7.4 %collective-permute-start.2 = (f32[24,256]{1,0:T(8,128)S(1)}, f32[24,256]{1,0:T(8,128)S(1)}, u32[]{:S(2)}, u32[]{:S(2)}) collective-permute-start(f32[24,256]{1,0:T(8,128)S(1)} %gates.1.refs_0_.refs_2_.refs_4_), channel_id=1, source_target_pairs={{0,16},{16,0},{1,17},{17,1},{2,18},{18,2},{3,19},{19,3},{4,20},{20... | collective-permute-start | bytes 73736 | tf_op jit(solution)/shard_map/ppermute | solution.py:265
  4.8 8.7 %collective-permute-start.1 = (bf16[24,4096]{1,0:T(8,128)(2,1)S(1)}, bf16[24,4096]{1,0:T(8,128)(2,1)S(1)}, u32[]{:S(2)}, u32[]{:S(2)}) collective-permute-start(bf16[24,4096]{1,0:T(8,128)(2,1)S(1)} %copy-done.3), channel_id=1, source_target_pairs={{0,16},{16,0},{1,17},{17,1},{2,18},{18,2},{3,19},{19,3},{4,20},{20... | collective-permute-start | bytes 589832 | tf_op jit(solution)/shard_map/ppermute | solution.py:265
  9.6 2.8 %copy-start = (bf16[1,768,4096]{2,1,0:T(8,128)(2,1)S(1)}, bf16[1,768,4096]{2,1,0:T(8,128)(2,1)}, u32[]{:S(2)}) copy-start(bf16[1,768,4096]{2,1,0:T(8,128)(2,1)} %param.16) | copy-start | bytes 18874372
  13.1 1.5 %collective-permute-start.3 = (bf16[2,2,24,1024]{3,2,1,0:T(8,128)(2,1)S(1)}, bf16[2,2,24,1024]{3,2,1,0:T(8,128)(2,1)S(1)}, u32[]{:S(2)}, u32[]{:S(2)}) collective-permute-start(bf16[2,2,24,1024]{3,2,1,0:T(8,128)(2,1)S(1)} %outward_send.1.refs_4_), channel_id=1, source_target_pairs={{0,1},{1,0},{2,3},{3,2},{4,5},{5,4},{6,7},{7,6},{8,9},{9,8},{10,11... | collective-permute-start | bytes 589832 | tf_op jit(solution)/shard_map/ppermute | solution.py:265
  14.7 6.2 %collective-permute-start.4 = (bf16[2,24,1024]{2,1,0:T(8,128)(2,1)S(1)}, bf16[2,24,1024]{2,1,0:T(8,128)(2,1)S(1)}, u32[]{:S(2)}, u32[]{:S(2)}) collective-permute-start(bf16[2,24,1024]{2,1,0:T(8,128)(2,1)S(1)} %get-tuple-element.36), channel_id=1, source_target_pairs={{0,16},{16,0},{1,17},{17,1},{2,18},{18,2},{3,19},{19,3},{4,20},{20... | collective-permute-start | bytes 294920 | tf_op jit(solution)/shard_map/ppermute | solution.py:265
  20.8 2.1 %collective-permute-start.5 = (bf16[2,2,24,1024]{3,2,1,0:T(8,128)(2,1)S(1)}, bf16[2,2,24,1024]{3,2,1,0:T(8,128)(2,1)S(1)}, u32[]{:S(2)}, u32[]{:S(2)}) collective-permute-start(bf16[2,2,24,1024]{3,2,1,0:T(8,128)(2,1)S(1)} %get-tuple-element.28), channel_id=1, source_target_pairs={{0,1},{1,0},{2,3},{3,2},{4,5},{5,4},{6,7},{7,6},{8,9},{9,8},{10,11... | collective-permute-start | bytes 589832 | tf_op jit(solution)/shard_map/ppermute | solution.py:265
  20.9 28.0 %copy-start.4 = (bf16[128,4096]{1,0:T(8,128)(2,1)S(1)}, bf16[128,4096]{1,0:T(8,128)(2,1)}, u32[]{:S(2)}) copy-start(bf16[128,4096]{1,0:T(8,128)(2,1)} %refs_19_.1) | copy-start | bytes 3145732
  23.0 5.1 %collective-permute-start.19 = (bf16[24,1024]{1,0:T(8,128)(2,1)S(1)}, bf16[24,1024]{1,0:T(8,128)(2,1)S(1)}, u32[]{:S(2)}, u32[]{:S(2)}) collective-permute-start(bf16[24,1024]{1,0:T(8,128)(2,1)S(1)} %get-tuple-element.35), channel_id=1, source_target_pairs={{0,2},{2,0},{1,3},{3,1},{4,6},{6,4},{5,7},{7,5},{8,10},{10,8},{9,1... | collective-permute-start | bytes 147464 | tf_op jit(solution)/shard_map/ppermute | solution.py:265
  24.6 5.3 %collective-permute-start.6 = (bf16[24,1024]{1,0:T(8,128)(2,1)S(1)}, bf16[24,1024]{1,0:T(8,128)(2,1)S(1)}, u32[]{:S(2)}, u32[]{:S(2)}) collective-permute-start(bf16[24,1024]{1,0:T(8,128)(2,1)S(1)} %get-tuple-element.31), channel_id=1, source_target_pairs={{0,18},{2,16},{16,2},{18,0},{1,19},{3,17},{17,3},{19,1},{4,22},{6,... | collective-permute-start | bytes 147464 | tf_op jit(solution)/shard_map/ppermute | solution.py:265
  25.2 4.6 %collective-permute-start.7 = (bf16[24,1024]{1,0:T(8,128)(2,1)S(1)}, bf16[24,1024]{1,0:T(8,128)(2,1)S(1)}, u32[]{:S(2)}, u32[]{:S(2)}) collective-permute-start(bf16[24,1024]{1,0:T(8,128)(2,1)S(1)} %get-tuple-element.32), channel_id=1, source_target_pairs={{0,16},{2,18},{16,0},{18,2},{1,17},{3,19},{17,1},{19,3},{4,20},{6,... | collective-permute-start | bytes 147464 | tf_op jit(solution)/shard_map/ppermute | solution.py:265
  26.6 4.1 %collective-permute-start.8 = (bf16[24,1024]{1,0:T(8,128)(2,1)S(1)}, bf16[24,1024]{1,0:T(8,128)(2,1)S(1)}, u32[]{:S(2)}, u32[]{:S(2)}) collective-permute-start(bf16[24,1024]{1,0:T(8,128)(2,1)S(1)} %get-tuple-element.33), channel_id=1, source_target_pairs={{0,2},{2,0},{16,18},{18,16},{1,3},{3,1},{17,19},{19,17},{4,6},{6,4... | collective-permute-start | bytes 147464 | tf_op jit(solution)/shard_map/ppermute | solution.py:265
  28.1 7.0 %collective-permute-start.20 = (bf16[24,1024]{1,0:T(8,128)(2,1)S(1)}, bf16[24,1024]{1,0:T(8,128)(2,1)S(1)}, u32[]{:S(2)}, u32[]{:S(2)}) collective-permute-start(bf16[24,1024]{1,0:T(8,128)(2,1)S(1)} %add_convert_fusion.4), channel_id=1, source_target_pairs={{0,4},{4,0},{8,12},{12,8},{1,5},{5,1},{9,13},{13,9},{2,6},{6,2},{1... | collective-permute-start | bytes 147464 | tf_op jit(solution)/shard_map/ppermute | solution.py:265
  30.7 6.7 %collective-permute-start.11 = (bf16[24,1024]{1,0:T(8,128)(2,1)S(1)}, bf16[24,1024]{1,0:T(8,128)(2,1)S(1)}, u32[]{:S(2)}, u32[]{:S(2)}) collective-permute-start(bf16[24,1024]{1,0:T(8,128)(2,1)S(1)} %add_convert_fusion.6), channel_id=1, source_target_pairs={{0,12},{4,8},{8,4},{12,0},{1,13},{5,9},{9,5},{13,1},{2,14},{6,10},... | collective-permute-start | bytes 147464 | tf_op jit(solution)/shard_map/ppermute | solution.py:265
  34.3 5.5 %collective-permute-start.10 = (bf16[24,1024]{1,0:T(8,128)(2,1)S(1)}, bf16[24,1024]{1,0:T(8,128)(2,1)S(1)}, u32[]{:S(2)}, u32[]{:S(2)}) collective-permute-start(bf16[24,1024]{1,0:T(8,128)(2,1)S(1)} %add_convert_fusion.6), channel_id=1, source_target_pairs={{0,8},{4,12},{8,0},{12,4},{1,9},{5,13},{9,1},{13,5},{2,10},{6,14},... | collective-permute-start | bytes 147464 | tf_op jit(solution)/shard_map/ppermute | solution.py:265
  34.3 5.5 %collective-permute-start.9 = (bf16[24,1024]{1,0:T(8,128)(2,1)S(1)}, bf16[24,1024]{1,0:T(8,128)(2,1)S(1)}, u32[]{:S(2)}, u32[]{:S(2)}) collective-permute-start(bf16[24,1024]{1,0:T(8,128)(2,1)S(1)} %add_convert_fusion.6), channel_id=1, source_target_pairs={{0,4},{4,0},{8,12},{12,8},{1,5},{5,1},{9,13},{13,9},{2,6},{6,2},{1... | collective-permute-start | bytes 147464 | tf_op jit(solution)/shard_map/ppermute | solution.py:265
  35.2 8.4 %collective-permute-start.21 = (bf16[24,1024]{1,0:T(8,128)(2,1)S(1)}, bf16[24,1024]{1,0:T(8,128)(2,1)S(1)}, u32[]{:S(2)}, u32[]{:S(2)}) collective-permute-start(bf16[24,1024]{1,0:T(8,128)(2,1)S(1)} %add_convert_fusion.3), channel_id=1, source_target_pairs={{0,8},{4,12},{8,0},{12,4},{1,9},{5,13},{9,1},{13,5},{2,10},{6,14},... | collective-permute-start | bytes 147464 | tf_op jit(solution)/shard_map/ppermute | solution.py:265
  39.9 5.1 %collective-permute-start.15 = (bf16[24,1024]{1,0:T(8,128)(2,1)S(1)}, bf16[24,1024]{1,0:T(8,128)(2,1)S(1)}, u32[]{:S(2)}, u32[]{:S(2)}) collective-permute-start(bf16[24,1024]{1,0:T(8,128)(2,1)S(1)} %add_convert_fusion.5.refs_6_), channel_id=1, source_target_pairs={{0,1},{1,0},{2,3},{3,2},{4,5},{5,4},{6,7},{7,6},{8,9},{9,8},{10,11... | collective-permute-start | bytes 147464 | tf_op jit(solution)/shard_map/ppermute | solution.py:265
  40.0 5.5 %collective-permute-start.14 = (bf16[24,1024]{1,0:T(8,128)(2,1)S(1)}, bf16[24,1024]{1,0:T(8,128)(2,1)S(1)}, u32[]{:S(2)}, u32[]{:S(2)}) collective-permute-start(bf16[24,1024]{1,0:T(8,128)(2,1)S(1)} %add_convert_fusion.5.refs_6_), channel_id=1, source_target_pairs={{0,18},{2,16},{16,2},{18,0},{1,19},{3,17},{17,3},{19,1},{4,22},{6,... | collective-permute-start | bytes 147464 | tf_op jit(solution)/shard_map/ppermute | solution.py:265
  41.2 4.8 %collective-permute-start.13 = (bf16[24,1024]{1,0:T(8,128)(2,1)S(1)}, bf16[24,1024]{1,0:T(8,128)(2,1)S(1)}, u32[]{:S(2)}, u32[]{:S(2)}) collective-permute-start(bf16[24,1024]{1,0:T(8,128)(2,1)S(1)} %add_convert_fusion.5.refs_6_), channel_id=1, source_target_pairs={{0,16},{2,18},{16,0},{18,2},{1,17},{3,19},{17,1},{19,3},{4,20},{6,... | collective-permute-start | bytes 147464 | tf_op jit(solution)/shard_map/ppermute | solution.py:265
  42.9 4.1 %collective-permute-start.12 = (bf16[24,1024]{1,0:T(8,128)(2,1)S(1)}, bf16[24,1024]{1,0:T(8,128)(2,1)S(1)}, u32[]{:S(2)}, u32[]{:S(2)}) collective-permute-start(bf16[24,1024]{1,0:T(8,128)(2,1)S(1)} %add_convert_fusion.5.refs_6_), channel_id=1, source_target_pairs={{0,2},{2,0},{16,18},{18,16},{1,3},{3,1},{17,19},{19,17},{4,6},{6,4... | collective-permute-start | bytes 147464 | tf_op jit(solution)/shard_map/ppermute | solution.py:265
  43.6 4.2 %collective-permute-start.22 = (bf16[24,1024]{1,0:T(8,128)(2,1)S(1)}, bf16[24,1024]{1,0:T(8,128)(2,1)S(1)}, u32[]{:S(2)}, u32[]{:S(2)}) collective-permute-start(bf16[24,1024]{1,0:T(8,128)(2,1)S(1)} %add_convert_fusion.2.refs_14_), channel_id=1, source_target_pairs={{0,2},{2,0},{1,3},{3,1},{4,6},{6,4},{5,7},{7,5},{8,10},{10,8},{9,1... | collective-permute-start | bytes 147464 | tf_op jit(solution)/shard_map/ppermute | solution.py:265
  45.0 3.2 %collective-permute-start.23 = (bf16[24,1024]{1,0:T(8,128)(2,1)S(1)}, bf16[24,1024]{1,0:T(8,128)(2,1)S(1)}, u32[]{:S(2)}, u32[]{:S(2)}) collective-permute-start(bf16[24,1024]{1,0:T(8,128)(2,1)S(1)} %add_convert_fusion.2.refs_14_), channel_id=1, source_target_pairs={{0,1},{1,0},{2,3},{3,2},{4,5},{5,4},{6,7},{7,6},{8,9},{9,8},{10,11... | collective-permute-start | bytes 147464 | tf_op jit(solution)/shard_map/ppermute | solution.py:265
  45.5 2.2 %collective-permute-start.18 = (bf16[24,1024]{1,0:T(8,128)(2,1)S(1)}, bf16[24,1024]{1,0:T(8,128)(2,1)S(1)}, u32[]{:S(2)}, u32[]{:S(2)}) collective-permute-start(bf16[24,1024]{1,0:T(8,128)(2,1)S(1)} %collective-permute-done.14.refs_9_), channel_id=1, source_target_pairs={{0,1},{1,0},{2,3},{3,2},{4,5},{5,4},{6,7},{7,6},{8,9},{9,8},{10,11... | collective-permute-start | bytes 147464 | tf_op jit(solution)/shard_map/ppermute | solution.py:265
  46.0 1.7 %collective-permute-start.17 = (bf16[24,1024]{1,0:T(8,128)(2,1)S(1)}, bf16[24,1024]{1,0:T(8,128)(2,1)S(1)}, u32[]{:S(2)}, u32[]{:S(2)}) collective-permute-start(bf16[24,1024]{1,0:T(8,128)(2,1)S(1)} %collective-permute-done.13.refs_8_), channel_id=1, source_target_pairs={{0,1},{1,0},{2,3},{3,2},{4,5},{5,4},{6,7},{7,6},{8,9},{9,8},{10,11... | collective-permute-start | bytes 147464 | tf_op jit(solution)/shard_map/ppermute | solution.py:265
  47.0 1.2 %collective-permute-start.16 = (bf16[24,1024]{1,0:T(8,128)(2,1)S(1)}, bf16[24,1024]{1,0:T(8,128)(2,1)S(1)}, u32[]{:S(2)}, u32[]{:S(2)}) collective-permute-start(bf16[24,1024]{1,0:T(8,128)(2,1)S(1)} %collective-permute-done.12.refs_7_), channel_id=1, source_target_pairs={{0,1},{1,0},{2,3},{3,2},{4,5},{5,4},{6,7},{7,6},{8,9},{9,8},{10,11... | collective-permute-start | bytes 147464 | tf_op jit(solution)/shard_map/ppermute | solution.py:265
  47.7 1.2 %collective-permute-start.24 = (bf16[24,1024]{1,0:T(8,128)(2,1)S(1)}, bf16[24,1024]{1,0:T(8,128)(2,1)S(1)}, u32[]{:S(2)}, u32[]{:S(2)}) collective-permute-start(bf16[24,1024]{1,0:T(8,128)(2,1)S(1)} %collective-permute-done.22.refs_15_), channel_id=1, source_target_pairs={{0,1},{1,0},{2,3},{3,2},{4,5},{5,4},{6,7},{7,6},{8,9},{9,8},{10,11... | collective-permute-start | bytes 147464 | tf_op jit(solution)/shard_map/ppermute | solution.py:265

commit v10 on v9

--- a/solution.py
+++ b/solution.py
@@ -60,6 +60,10 @@
     small[:, heads:] = jnp.broadcast_to(gate, (rows, LANES))
 
 
+def unit_step(units):
+    return STEP if units % STEP == 0 else units
+
+
 def loop(count, body, unroll):
     if unroll:
         for step in range(count):
@@ -94,15 +98,17 @@
 
     loop(width // 512, norm, few)
 
+    size = unit_step(w_gate.shape[1])
+
     def hidden_units(step):
-        columns = pl.ds(place(step, STEP), STEP)
+        columns = pl.ds(place(step, size), size)
         gate_part = dot(normed[...], w_gate[:, columns], ((1,), (0,)))
         up_part = dot(normed[...], w_up[:, columns], ((1,), (0,)))
         pre_gate[:, columns] = gate_part
         pre_up[:, columns] = up_part
         act[:, columns] = (gate_part * jax.nn.sigmoid(gate_part) * up_part).astype(BF16)
 
-    loop(w_gate.shape[1] // STEP, hidden_units, few)
+    loop(w_gate.shape[1] // size, hidden_units, few)
 
 
 def outward_kernel(i, n_dp, *refs):
@@ -122,76 +128,91 @@
         loop(chunk // STEP, outward, few)
 
 
-def inward_part(i, n_dp, grad_gate, grad_up, w_gate, w_up, target):
+def inward_part(i, n_dp, grad_refs, w_gate, w_up, target):
     chunk = target.shape[3]
-    few = grad_gate.shape[0] <= FEW_ROWS
+    few = grad_refs[0].shape[0] <= FEW_ROWS
     for j in range(2):
         first = own_columns(i, j, chunk)
 
         def inward(step):
             columns = pl.ds(pl.multiple_of(first + step * STEP, STEP), STEP)
-            part = dot(grad_gate[...], w_gate[columns, :], ((1,), (1,)))
-            part = part + dot(grad_up[...], w_up[columns, :], ((1,), (1,)))
+            part = 0.0
+            for parity, weights in ((0, w_gate), (1, w_up)):
+                start = 0
+                for ref in grad_refs[parity::2]:
+                    part = part + dot(ref[...], weights[columns, start : start + ref.shape[1]], ((1,), (1,)))
+                    start += ref.shape[1]
             store_blocks(target, j, pl.ds(place(step, STEP), STEP), part, n_dp)
 
         loop(chunk // STEP, inward, few)
 
 
-def backward_kernel(n_dp, *refs):
-    grads, smalls = refs[:n_dp], refs[n_dp : 2 * n_dp]
-    pre_gate, pre_up, w_down, waiting, grad_gate, grad_up, passed, rows_grad = refs[2 * n_dp :]
-    passed[...] = waiting[...]
-    weight = gates_of(smalls)
-    few = rows_grad.shape[0] <= FEW_ROWS
-
-    def weigh(step):
-        columns = pl.ds(place(step, 512), 512)
-        rows_grad[:, columns] = (weight * rows_of(grads, columns)).astype(BF16)
-
-    loop(rows_grad.shape[1] // 512, weigh, few)
+def gradients(first, weighted, pre_gate, pre_up, w_down, grad_gate, grad_up, few):
+    size = unit_step(w_down.shape[0])
 
     def hidden_units(step):
-        columns = pl.ds(place(step, STEP), STEP)
-        back = dot(rows_grad[...], w_down[columns, :], ((1,), (1,)))
-        gate_part, up_part = pre_gate[:, columns], pre_up[:, columns]
+        columns = pl.ds(place(step, size), size)
+        units = pl.ds(first + step * size, size)
+        back = dot(weighted[...], w_down[units, :], ((1,), (1,)))
+        gate_part, up_part = pre_gate[:, units], pre_up[:, units]
         sig = jax.nn.sigmoid(gate_part)
         grad_gate[:, columns] = (back * up_part * sig * (1.0 + gate_part * (1.0 - sig))).astype(BF16)
         grad_up[:, columns] = (back * gate_part * sig).astype(BF16)
 
-    loop(w_down.shape[0] // STEP, hidden_units, few)
-
-
-def inward_kernel(i, n_dp, grad_gate, grad_up, w_gate, w_up, waiting, target, passed):
+    loop(grad_gate.shape[1] // size, hidden_units, few or grad_gate.shape[1] == size)
+
+
+def backward_first_kernel(n_dp, *refs):
+    grads, smalls = refs[:n_dp], refs[n_dp : 2 * n_dp]
+    pre_gate, pre_up, w_down, waiting, grad_gate, grad_up, weighted, passed = refs[2 * n_dp :]
     passed[...] = waiting[...]
-    inward_part(i, n_dp, grad_gate, grad_up, w_gate, w_up, target)
+    weight = gates_of(smalls)
+    few = weighted.shape[0] <= FEW_ROWS
+
+    def weigh(step):
+        columns = pl.ds(place(step, 512), 512)
+        weighted[:, columns] = (weight * rows_of(grads, columns)).astype(BF16)
+
+    loop(weighted.shape[1] // 512, weigh, few)
+    gradients(0, weighted, pre_gate, pre_up, w_down, grad_gate, grad_up, few)
+
+
+def backward_rest_kernel(n_dp, weighted, pre_gate, pre_up, w_down, waiting, grad_gate, grad_up, passed):
+    passed[...] = waiting[...]
+    first = pre_gate.shape[1] - grad_gate.shape[1]
+    gradients(first, weighted, pre_gate, pre_up, w_down, grad_gate, grad_up, True)
+
+
+def inward_kernel(i, n_dp, *refs):
+    w_gate, w_up, waiting, target, passed = refs[-5:]
+    passed[...] = waiting[...]
+    inward_part(i, n_dp, refs[:-5], w_gate, w_up, target)
 
 
 def join_kernel(n_dp, in_keep, in_other, out_block, *refs):
     for t in range(2 * n_dp):
         k, j = t // 2, t % 2
         refs[t][...] = (in_keep[k, j].astype(F32) + in_other[k, j].astype(F32)).astype(BF16)
-    for j, target in enumerate(refs[-2:]):
-        target[...] = out_block[j]
+    refs[-1][...] = out_block[...]
 
 
 def finish_kernel(n_dp, *refs):
     hid, grads, smalls = refs[:n_dp], refs[n_dp : 2 * n_dp], refs[2 * n_dp : 3 * n_dp]
-    back, moe = refs[3 * n_dp : 7 * n_dp], refs[7 * n_dp : 7 * n_dp + 4]
-    gain, w_out = refs[7 * n_dp + 4 : 7 * n_dp + 6]
-    targets, held = refs[7 * n_dp + 6 : 7 * n_dp + 10], refs[7 * n_dp + 10 : 7 * n_dp + 14]
-    summed, d_all, sems = refs[7 * n_dp + 14 :]
+    back, moe = refs[3 * n_dp : 7 * n_dp], refs[7 * n_dp : 7 * n_dp + 2]
+    gain, w_out = refs[7 * n_dp + 2 : 7 * n_dp + 4]
+    targets, held = refs[7 * n_dp + 4 : 7 * n_dp + 8], refs[7 * n_dp + 8 : 7 * n_dp + 12]
+    summed, d_all, sems = refs[7 * n_dp + 12 :]
     output, d_hidden, d_context, d_w_out = held
     copies = [pltpu.make_async_copy(held[n], targets[n], sems.at[n]) for n in range(4)]
     rows, width = hid[0].shape
-    chunk = moe[0].shape[1]
+    chunk = moe[0].shape[2]
     for i in range(2):
         for j in range(2):
             columns = pl.ds(pl.multiple_of(own_columns(i, j, chunk), chunk), chunk)
             for k in range(n_dp):
                 piece = back[(i * n_dp + k) * 2 + j]
                 summed[k * rows : (k + 1) * rows, columns] = piece[...].astype(F32) * gain[:, columns]
-            piece = moe[i * 2 + j]
-            output[:, columns] = (hid[0][:, columns].astype(F32) + piece[...].astype(F32)).astype(BF16)
+            output[:, columns] = (hid[0][:, columns].astype(F32) + moe[i][j].astype(F32)).astype(BF16)
     copies[0].start()
 
     few = rows * n_dp <= FEW_ROWS
@@ -304,31 +325,39 @@
         functools.partial(outward_kernel, 0), n_dp, smalls + [act, wd, out_send] + grads, [shares], [],
         weights // 2, "outward_keep",
     )
+    size = unit_step(units)
+    first_units, rest_units = ((all_rows, size), BF16), ((all_rows, units - size), BF16)
+    gate_first, up_first, weighted, out_keep = run(
+        backward_first_kernel, n_dp, grads + smalls + [pre_gate, pre_up, wd, out_keep],
+        [first_units, first_units, ((all_rows, width), BF16), shares], [], weights // 3, "backward_first",
+    )
+    back_grads = [gate_first, up_first]
     out_half = add(out_keep, out_other)
     out_blocks = [swap(out_half[k], ("dp",), k) for k in range(1, n_dp)]
-    block = (shares[0][1:], BF16)
-    grad_gate, grad_up, out_block = run(
-        backward_kernel, n_dp, grads + smalls + [pre_gate, pre_up, wd, out_half[0]],
-        [((all_rows, units), BF16), ((all_rows, units), BF16), block],
-        [pltpu.VMEM((all_rows, width), BF16)], weights, "backward",
-    )
+    block, out_block = (shares[0][1:], BF16), out_half[0]
+    if size < units:
+        gate_rest, up_rest, out_block = run(
+            backward_rest_kernel, n_dp, [weighted, pre_gate, pre_up, wd, out_block],
+            [rest_units, rest_units, block], [], weights * 2 // 3, "backward_rest",
+        )
+        back_grads = back_grads + [gate_rest, up_rest]
     in_send, out_block = run(
-        functools.partial(inward_kernel, 1), n_dp, [grad_gate, grad_up, wg, wu, out_block],
+        functools.partial(inward_kernel, 1), n_dp, back_grads + [wg, wu, out_block],
         [shares, block], [], weights, "inward_send",
     )
     in_other = swap(in_send, ("c",), 1)
     out_block = total_of([out_block] + out_blocks)
     in_keep, out_block = run(
-        functools.partial(inward_kernel, 0), n_dp, [grad_gate, grad_up, wg, wu, out_block], [shares, block], [],
+        functools.partial(inward_kernel, 0), n_dp, back_grads + [wg, wu, out_block], [shares, block], [],
         weights, "inward_keep",
     )
-    *in_pieces, out_share, out_piece = run(
-        join_kernel, n_dp, [in_keep, in_other, out_block], [((rows, chunk), BF16)] * (2 * n_dp + 2), [],
+    *in_pieces, out_block = run(
+        join_kernel, n_dp, [in_keep, in_other, out_block], [((rows, chunk), BF16)] * (2 * n_dp) + [block], [],
         rows * width, "join",
     )
     turns = [t for t in range(2 * n_dp - 1, 0, -1)]
     in_share = total_of([in_pieces[0]] + [swap(in_pieces[t], ("dp", "y"), t) for t in turns])
-    out_total = add(out_share, swap(out_piece, ("y",), 1))
+    out_total = add(out_block, swap(out_block, ("y",), 1)[::-1])
     in_total = total_of([in_share] + [swap(in_share, ("hi",), t) for t in range(1, n_hi)])
     turn = 1
     while turn < n_hi:
@@ -337,9 +366,8 @@
     order = [t for t in turns if t < 2] + [t for t in turns if t >= 2]
     spread = {t: swap(in_total, ("dp", "y"), t) for t in order}
     back = [in_total] + [spread[t] for t in range(1, 2 * n_dp)]
-    moe = [out_total, swap(out_total, ("y",), 1)]
     back = back + [swap(piece, ("c",), 1) for piece in back]
-    moe = moe + [swap(piece, ("c",), 1) for piece in moe]
+    moe = [out_total, swap(out_total, ("c",), 1)]
     outs = [((rows, width), BF16), ((rows, width), BF16), ((rows, heads), BF16), ((heads, width // n_dp), BF16)]
     return run(
         finish_kernel, n_dp, hid + grads + smalls + back + moe + [gain, w_out], outs,

time: 50.8 us -> 50.8 us (level)
  starting transfers between devices: 25.8 us -> 24.8 us
  waiting for transfers between devices: 10.9 us -> 11.7 us
    ppermute x25 -> x23, starting transfers between devices: 25.8 us -> 24.8 us  [swap(): return lax.ppermute(value, axes, [(i, i ^ turn) for i in range(count)])]
    ppermute x25 -> x23, waiting for transfers between devices: 10.9 us -> 11.7 us  [swap(): return lax.ppermute(value, axes, [(i, i ^ turn) for i in range(count)])]
    pallas_call x9 -> x10, Pallas kernels: 12.5 us -> 12.6 us  [run(): pl.pallas_call(functools.partial(kernel, n_dp), out_shape=kinds, in_specs...]
  transfers between devices with their start and end apart: 25 -> 23, of which waited for: 12 -> 11; matrix products, arithmetic and copies ran while one was open for 0% -> 0% of each run, Pallas kernels for 21% -> 22%
where the time goes in v10:
time: 50.8 us; the launch traced here: 50.6 us
  starting transfers between devices  24.8 us (49%)
  Pallas kernels  12.6 us (25%)
  waiting for transfers between devices  11.7 us (23%)
  between operations  0.85 us (2%)
    ppermute x23, starting transfers between devices, swap(): return lax.ppermute(value, axes, [(i, i ^ turn) for i in range(count)])  24.8 us
    pallas_call x10, Pallas kernels, run(): pl.pallas_call(functools.partial(kernel, n_dp), out_shape=kinds, in_specs...  12.6 us
    ppermute x23, waiting for transfers between devices, swap(): return lax.ppermute(value, axes, [(i, i ^ turn) for i in range(count)])  11.7 us
  transfers between devices with their start and end apart: 23, of which 11 were waited for; matrix products, arithmetic and copies ran while one was open for 0% of the time, Pallas kernels for 22%

profile of v10, /device:TPU:0, one launch (start us, length us, event | category | flops | bytes accessed | tf_op | source)
XLA Modules:
  0.0 50.6 jit_solution(15285591572118845250)
XLA Ops:
  0.6 3.0 %collective-permute-start = (bf16[24,4096]{1,0:T(8,128)(2,1)}, bf16[24,4096]{1,0:T(8,128)(2,1)S(1)}, u32[]{:S(2)}, u32[]{:S(2)}) collective-permute-start(bf16[24,4096]{1,0:T(8,128)(2,1)} %refs_0_.5), channel_id=1, source_target_pairs={{0,16},{16,0},{1,17},{17,1},{2,18},{18,2},{3,19},{19,3},{4,20},{20... | collective-permute-start | bytes 589832 | tf_op jit(solution)/shard_map/ppermute | solution.py:286
  3.7 1.0 %gates.1.refs_0_.refs_2_.refs_4_ = f32[24,256]{1,0:T(8,128)S(1)} custom-call(s32[8,24]{1,0:T(8,128)} %bitcast.25, f32[8,24]{1,0:T(8,128)} %bitcast.26, bf16[24,128]{1,0:T(8,128)(2,1)} %context.1, bf16[4096,768]{1,0:T(8,128)(2,1)} %bitcast.15, bf16[4096,768]{1,0:T(8,128)(2,1)} %bitcast.19, bf16[768,4096]{1,0:T(8,128)(2,1)} %bitcast.10), custom_call_target="tpu_custom_call" | custom-call | bytes 25165824 | tf_op jit(solution)/shard_map/gates/pallas_call | solution.py:261
  4.7 0.1 collective-permute-start.2
  4.8 2.0 %collective-permute-start.1 = (bf16[24,4096]{1,0:T(8,128)(2,1)S(1)}, bf16[24,4096]{1,0:T(8,128)(2,1)S(1)}, u32[]{:S(2)}, u32[]{:S(2)}) collective-permute-start(bf16[24,4096]{1,0:T(8,128)(2,1)S(1)} %copy-done.3), channel_id=1, source_target_pairs={{0,16},{16,0},{1,17},{17,1},{2,18},{18,2},{3,19},{19,3},{4,20},{20... | collective-permute-start | bytes 589832 | tf_op jit(solution)/shard_map/ppermute | solution.py:286
  6.8 2.8 %collective-permute-done.refs_1_ = bf16[24,4096]{1,0:T(8,128)(2,1)S(1)} collective-permute-done((bf16[24,4096]{1,0:T(8,128)(2,1)}, bf16[24,4096]{1,0:T(8,128)(2,1)S(1)}, u32[]{:S(2)}, u32[]{:S(2)}) %collective-permute-start) | collective-permute-done | bytes 196640 | tf_op jit(solution)/shard_map/ppermute | solution.py:286
  9.6 0.0 copy-start
  9.6 2.4 %hidden.1 = (f32[48,768]{1,0:T(8,128)S(1)}, f32[48,768]{1,0:T(8,128)S(1)}, bf16[48,768]{1,0:T(8,128)(2,1)S(1)}) custom-call(bf16[24,4096]{1,0:T(8,128)(2,1)S(1)} %copy-done.5, bf16[24,4096]{1,0:T(8,128)(2,1)S(1)} %collective-permute-done.refs_1_, f32[1,4096]{1,0:T(1,128)S(1)} %bitcast.23, bf16[4096,768]{1,0:T(8,128)(2,1)S(1)} %bitcast.16, ...), custom_call_target="tpu_custom_call" | custom-call | bytes 12582912 | tf_op jit(solution)/shard_map/hidden/pallas_call | solution.py:261
  12.0 0.0 collective-permute-done.2.refs_1_.refs_3_.refs_5_
  12.0 0.3 copy-done
  12.4 0.7 %outward_send.1.refs_4_ = bf16[2,2,24,1024]{3,2,1,0:T(8,128)(2,1)S(1)} custom-call(f32[24,256]{1,0:T(8,128)S(1)} %gates.1.refs_0_.refs_2_.refs_4_, f32[24,256]{1,0:T(8,128)S(1)} %collective-permute-done.2.refs_1_.refs_3_.refs_5_, bf16[48,768]{1,0:T(8,128)(2,1)S(1)} %get-tuple-element.25.refs_2_, bf16[768,4096]{1,0:T(8,128)(2,1)S(1)} %bitcast.11), custom_call_target="tpu_custom_call" | custom-call | bytes 3145728 | tf_op jit(solution)/shard_map/outward_send/pallas_call | solution.py:261
  13.1 0.1 collective-permute-start.3
  13.1 0.3 collective-permute-done.1.refs_6_.refs_1_.refs_3_
  13.5 0.7 %outward_keep.1.refs_7_ = bf16[2,2,24,1024]{3,2,1,0:T(8,128)(2,1)S(1)} custom-call(f32[24,256]{1,0:T(8,128)S(1)} %gates.1.refs_0_.refs_2_.refs_4_, f32[24,256]{1,0:T(8,128)S(1)} %collective-permute-done.2.refs_1_.refs_3_.refs_5_, bf16[48,768]{1,0:T(8,128)(2,1)S(1)} %get-tuple-element.25.refs_2_, bf16[768,4096]{1,0:T(8,128)(2,1)S(1)} %bitcast.12, ...), custom_call_target="tpu_custom_call" | custom-call | bytes 3145728 | tf_op jit(solution)/shard_map/outward_keep/pallas_call | solution.py:261
  14.2 0.8 %backward_first.1 = (bf16[48,256]{1,0:T(8,128)(2,1)S(1)}, bf16[48,256]{1,0:T(8,128)(2,1)S(1)}, bf16[48,4096]{1,0:T(8,128)(2,1)S(1)}, bf16[2,2,24,1024]{3,2,1,0:T(8,128)(2,1)S(1)}) custom-call(bf16[24,4096]{1,0:T(8,128)(2,1)S(1)} %copy-done.3, bf16[24,4096]{1,0:T(8,128)(2,1)S(1)} %collective-permute-done.1.refs_6_.refs_1_.refs_3_, ...), custom_call_target="tpu_custom_call" | custom-call | bytes 2097152 | tf_op jit(solution)/shard_map/backward_first/pallas_call | solution.py:261
  15.0 0.1 add_convert_fusion
  15.1 1.8 %collective-permute-start.4 = (bf16[2,24,1024]{2,1,0:T(8,128)(2,1)S(1)}, bf16[2,24,1024]{2,1,0:T(8,128)(2,1)S(1)}, u32[]{:S(2)}, u32[]{:S(2)}) collective-permute-start(bf16[2,24,1024]{2,1,0:T(8,128)(2,1)S(1)} %get-tuple-element.42), channel_id=1, source_target_pairs={{0,16},{16,0},{1,17},{17,1},{2,18},{18,2},{3,19},{19,3},{4,20},{20... | collective-permute-start | bytes 294920 | tf_op jit(solution)/shard_map/ppermute | solution.py:286
  16.9 1.4 %backward_rest.1 = (bf16[48,512]{1,0:T(8,128)(2,1)S(1)}, bf16[48,512]{1,0:T(8,128)(2,1)S(1)}, bf16[2,24,1024]{2,1,0:T(8,128)(2,1)S(1)}) custom-call(bf16[48,4096]{1,0:T(8,128)(2,1)S(1)} %get-tuple-element.28.weighted, f32[48,768]{1,0:T(8,128)S(1)} %get-tuple-element.23.refs_4_.pre_gate, f32[48,768]{1,0:T(8,128)S(1)} %get-tuple-element.24.refs_5_.pre_up, ...), custom_call_target="tpu_custom_call" | custom-call | bytes 4194304 | tf_op jit(solution)/shard_map/backward_rest/pallas_call | solution.py:261
  18.3 2.0 %inward_send.1 = (bf16[2,2,24,1024]{3,2,1,0:T(8,128)(2,1)S(1)}, bf16[2,24,1024]{2,1,0:T(8,128)(2,1)S(1)}) custom-call(bf16[48,256]{1,0:T(8,128)(2,1)S(1)} %get-tuple-element.26.refs_0_, bf16[48,256]{1,0:T(8,128)(2,1)S(1)} %get-tuple-element.27.refs_1_, bf16[48,512]{1,0:T(8,128)(2,1)S(1)} %get-tuple-element.30.refs_2_, ...), custom_call_target="tpu_custom_call" | custom-call | bytes 6291456 | tf_op jit(solution)/shard_map/inward_send/pallas_call | solution.py:261
  20.3 0.3 collective-permute-start.5
  20.6 0.0 copy-start.4
  20.6 2.0 %inward_keep.1 = (bf16[2,2,24,1024]{3,2,1,0:T(8,128)(2,1)S(1)}, bf16[2,24,1024]{2,1,0:T(8,128)(2,1)S(1)}) custom-call(bf16[48,256]{1,0:T(8,128)(2,1)S(1)} %get-tuple-element.26.refs_0_, bf16[48,256]{1,0:T(8,128)(2,1)S(1)} %get-tuple-element.27.refs_1_, bf16[48,512]{1,0:T(8,128)(2,1)S(1)} %get-tuple-element.30.refs_2_, ...), custom_call_target="tpu_custom_call" | custom-call | bytes 6291456 | tf_op jit(solution)/shard_map/inward_keep/pallas_call | solution.py:261
  22.6 0.0 collective-permute-done.5.in_other
  22.6 0.1 join.1
  22.6 1.6 %collective-permute-start.19 = (bf16[2,24,1024]{2,1,0:T(8,128)(2,1)S(1)}, bf16[2,24,1024]{2,1,0:T(8,128)(2,1)S(1)}, u32[]{:S(2)}, u32[]{:S(2)}) collective-permute-start(bf16[2,24,1024]{2,1,0:T(8,128)(2,1)S(1)} %get-tuple-element.41), channel_id=1, source_target_pairs={{0,2},{2,0},{1,3},{3,1},{4,6},{6,4},{5,7},{7,5},{8,10},{10,8},{9,1... | collective-permute-start | bytes 294920 | tf_op jit(solution)/shard_map/ppermute | solution.py:286
  24.2 1.4 %collective-permute-start.6 = (bf16[24,1024]{1,0:T(8,128)(2,1)S(1)}, bf16[24,1024]{1,0:T(8,128)(2,1)S(1)}, u32[]{:S(2)}, u32[]{:S(2)}) collective-permute-start(bf16[24,1024]{1,0:T(8,128)(2,1)S(1)} %get-tuple-element.38), channel_id=1, source_target_pairs={{0,18},{2,16},{16,2},{18,0},{1,19},{3,17},{17,3},{19,1},{4,22},{6,... | collective-permute-start | bytes 147464 | tf_op jit(solution)/shard_map/ppermute | solution.py:286
  25.7 0.5 collective-permute-start.7
  26.2 1.6 %collective-permute-start.8 = (bf16[24,1024]{1,0:T(8,128)(2,1)S(1)}, bf16[24,1024]{1,0:T(8,128)(2,1)S(1)}, u32[]{:S(2)}, u32[]{:S(2)}) collective-permute-start(bf16[24,1024]{1,0:T(8,128)(2,1)S(1)} %get-tuple-element.40), channel_id=1, source_target_pairs={{0,2},{2,0},{16,18},{18,16},{1,3},{3,1},{17,19},{19,17},{4,6},{6,4... | collective-permute-start | bytes 147464 | tf_op jit(solution)/shard_map/ppermute | solution.py:286
  27.7 0.2 collective-permute-done.19
  28.0 1.6 %collective-permute-start.20 = (bf16[2,24,1024]{2,1,0:T(8,128)(2,1)S(1)}, bf16[2,24,1024]{2,1,0:T(8,128)(2,1)S(1)}, u32[]{:S(2)}, u32[]{:S(2)}) collective-permute-start(bf16[2,24,1024]{2,1,0:T(8,128)(2,1)S(1)} %add_convert_fusion.3), channel_id=1, source_target_pairs={{0,4},{4,0},{8,12},{12,8},{1,5},{5,1},{9,13},{13,9},{2,6},{6,2},{1... | collective-permute-start | bytes 294920 | tf_op jit(solution)/shard_map/ppermute | solution.py:286
  29.6 0.0 collective-permute-done.6
  29.6 0.2 collective-permute-done.7
  29.8 0.5 collective-permute-done.8
  30.3 3.7 %collective-permute-start.11 = (bf16[24,1024]{1,0:T(8,128)(2,1)S(1)}, bf16[24,1024]{1,0:T(8,128)(2,1)S(1)}, u32[]{:S(2)}, u32[]{:S(2)}) collective-permute-start(bf16[24,1024]{1,0:T(8,128)(2,1)S(1)} %add_convert_fusion.6), channel_id=1, source_target_pairs={{0,12},{4,8},{8,4},{12,0},{1,13},{5,9},{9,5},{13,1},{2,14},{6,10},... | collective-permute-start | bytes 147464 | tf_op jit(solution)/shard_map/ppermute | solution.py:286
  34.0 0.0 collective-permute-start.10
  34.0 0.7 %collective-permute-start.9 = (bf16[24,1024]{1,0:T(8,128)(2,1)S(1)}, bf16[24,1024]{1,0:T(8,128)(2,1)S(1)}, u32[]{:S(2)}, u32[]{:S(2)}) collective-permute-start(bf16[24,1024]{1,0:T(8,128)(2,1)S(1)} %add_convert_fusion.6), channel_id=1, source_target_pairs={{0,4},{4,0},{8,12},{12,8},{1,5},{5,1},{9,13},{13,9},{2,6},{6,2},{1... | collective-permute-start | bytes 147464 | tf_op jit(solution)/shard_map/ppermute | solution.py:286
  34.8 2.2 %collective-permute-start.21 = (bf16[2,24,1024]{2,1,0:T(8,128)(2,1)S(1)}, bf16[2,24,1024]{2,1,0:T(8,128)(2,1)S(1)}, u32[]{:S(2)}, u32[]{:S(2)}) collective-permute-start(bf16[2,24,1024]{2,1,0:T(8,128)(2,1)S(1)} %add_convert_fusion.2), channel_id=1, source_target_pairs={{0,8},{4,12},{8,0},{12,4},{1,9},{5,13},{9,1},{13,5},{2,10},{6,14},... | collective-permute-start | bytes 294920 | tf_op jit(solution)/shard_map/ppermute | solution.py:286
  37.0 3.2 %collective-permute-done.10 = bf16[24,1024]{1,0:T(8,128)(2,1)S(1)} collective-permute-done((bf16[24,1024]{1,0:T(8,128)(2,1)S(1)}, bf16[24,1024]{1,0:T(8,128)(2,1)S(1)}, u32[]{:S(2)}, u32[]{:S(2)}) %collective-permute-start.10) | collective-permute-done | bytes 49184 | tf_op jit(solution)/shard_map/ppermute | solution.py:286
  40.3 2.5 %collective-permute-start.14 = (bf16[24,1024]{1,0:T(8,128)(2,1)S(1)}, bf16[24,1024]{1,0:T(8,128)(2,1)S(1)}, u32[]{:S(2)}, u32[]{:S(2)}) collective-permute-start(bf16[24,1024]{1,0:T(8,128)(2,1)S(1)} %add_convert_fusion.5.refs_6_), channel_id=1, source_target_pairs={{0,18},{2,16},{16,2},{18,0},{1,19},{3,17},{17,3},{19,1},{4,22},{6,... | collective-permute-start | bytes 147464 | tf_op jit(solution)/shard_map/ppermute | solution.py:286
  42.7 0.9 %collective-permute-start.13 = (bf16[24,1024]{1,0:T(8,128)(2,1)S(1)}, bf16[24,1024]{1,0:T(8,128)(2,1)S(1)}, u32[]{:S(2)}, u32[]{:S(2)}) collective-permute-start(bf16[24,1024]{1,0:T(8,128)(2,1)S(1)} %add_convert_fusion.5.refs_6_), channel_id=1, source_target_pairs={{0,16},{2,18},{16,0},{18,2},{1,17},{3,19},{17,1},{19,3},{4,20},{6,... | collective-permute-start | bytes 147464 | tf_op jit(solution)/shard_map/ppermute | solution.py:286
  43.6 0.2 collective-permute-start.12
  43.8 0.1 collective-permute-start.22
  43.9 0.5 collective-permute-start.15
  44.4 0.9 %collective-permute-done.14.refs_9_ = bf16[24,1024]{1,0:T(8,128)(2,1)S(1)} collective-permute-done((bf16[24,1024]{1,0:T(8,128)(2,1)S(1)}, bf16[24,1024]{1,0:T(8,128)(2,1)S(1)}, u32[]{:S(2)}, u32[]{:S(2)}) %collective-permute-start.14) | collective-permute-done | bytes 49184 | tf_op jit(solution)/shard_map/ppermute | solution.py:286
  45.3 1.5 %collective-permute-done.13.refs_8_ = bf16[24,1024]{1,0:T(8,128)(2,1)S(1)} collective-permute-done((bf16[24,1024]{1,0:T(8,128)(2,1)S(1)}, bf16[24,1024]{1,0:T(8,128)(2,1)S(1)}, u32[]{:S(2)}, u32[]{:S(2)}) %collective-permute-start.13) | collective-permute-done | bytes 49184 | tf_op jit(solution)/shard_map/ppermute | solution.py:286
  46.8 0.9 %collective-permute-done.12.refs_7_ = bf16[24,1024]{1,0:T(8,128)(2,1)S(1)} collective-permute-done((bf16[24,1024]{1,0:T(8,128)(2,1)S(1)}, bf16[24,1024]{1,0:T(8,128)(2,1)S(1)}, u32[]{:S(2)}, u32[]{:S(2)}) %collective-permute-start.12) | collective-permute-done | bytes 49184 | tf_op jit(solution)/shard_map/ppermute | solution.py:286
  47.7 0.3 collective-permute-done.17.refs_12_
  48.0 0.9 %collective-permute-done.16.refs_11_ = bf16[24,1024]{1,0:T(8,128)(2,1)S(1)} collective-permute-done((bf16[24,1024]{1,0:T(8,128)(2,1)S(1)}, bf16[24,1024]{1,0:T(8,128)(2,1)S(1)}, u32[]{:S(2)}, u32[]{:S(2)}) %collective-permute-start.16) | collective-permute-done | bytes 49184 | tf_op jit(solution)/shard_map/ppermute | solution.py:286
  48.9 1.7 %finish.1 = (bf16[24,4096]{1,0:T(8,128)(2,1)}, bf16[24,4096]{1,0:T(8,128)(2,1)}, bf16[24,128]{1,0:T(8,128)(2,1)}, bf16[128,2048]{1,0:T(8,128)(2,1)}) custom-call(bf16[24,4096]{1,0:T(8,128)(2,1)S(1)} %copy-done.5, bf16[24,4096]{1,0:T(8,128)(2,1)S(1)} %collective-permute-done.refs_1_, bf16[24,4096]{1,0:T(8,128)(2,1)S(1)} %copy-done.3, ...), custom_call_target="tpu_custom_call" | custom-call | bytes 6291456 | tf_op jit(solution)/shard_map/finish/pallas_call | solution.py:261
  (30 shorter events, 0.2 us)
Async XLA Ops:
  0.6 8.9 %collective-permute-start = (bf16[24,4096]{1,0:T(8,128)(2,1)}, bf16[24,4096]{1,0:T(8,128)(2,1)S(1)}, u32[]{:S(2)}, u32[]{:S(2)}) collective-permute-start(bf16[24,4096]{1,0:T(8,128)(2,1)} %refs_0_.5), channel_id=1, source_target_pairs={{0,16},{16,0},{1,17},{17,1},{2,18},{18,2},{3,19},{19,3},{4,20},{20... | collective-permute-start | bytes 589832 | tf_op jit(solution)/shard_map/ppermute | solution.py:286
  3.6 1.1 %copy-start.3 = (bf16[24,4096]{1,0:T(8,128)(2,1)S(1)}, bf16[24,4096]{1,0:T(8,128)(2,1)}, u32[]{:S(2)}) copy-start(bf16[24,4096]{1,0:T(8,128)(2,1)} %refs_2_.1) | copy-start | bytes 589828
  3.6 5.9 %copy-start.1 = (bf16[1,4096,768]{2,1,0:T(8,128)(2,1)S(1)}, bf16[1,4096,768]{2,1,0:T(8,128)(2,1)}, u32[]{:S(2)}) copy-start(bf16[1,4096,768]{2,1,0:T(8,128)(2,1)} %param.14) | copy-start | bytes 18874372
  3.6 5.9 %copy-start.2 = (bf16[1,4096,768]{2,1,0:T(8,128)(2,1)S(1)}, bf16[1,4096,768]{2,1,0:T(8,128)(2,1)}, u32[]{:S(2)}) copy-start(bf16[1,4096,768]{2,1,0:T(8,128)(2,1)} %param.15) | copy-start | bytes 18874372
  3.6 5.9 %copy-start.5 = (bf16[24,4096]{1,0:T(8,128)(2,1)S(1)}, bf16[24,4096]{1,0:T(8,128)(2,1)}, u32[]{:S(2)}) copy-start(bf16[24,4096]{1,0:T(8,128)(2,1)} %refs_0_.5) | copy-start | bytes 589828
  3.6 5.9 %copy-start.6 = (f32[4096]{0:T(1024)S(1)}, f32[4096]{0:T(1024)}, u32[]{:S(2)}) copy-start(f32[4096]{0:T(1024)} %param.11) | copy-start | bytes 49156
  4.7 7.4 %collective-permute-start.2 = (f32[24,256]{1,0:T(8,128)S(1)}, f32[24,256]{1,0:T(8,128)S(1)}, u32[]{:S(2)}, u32[]{:S(2)}) collective-permute-start(f32[24,256]{1,0:T(8,128)S(1)} %gates.1.refs_0_.refs_2_.refs_4_), channel_id=1, source_target_pairs={{0,16},{16,0},{1,17},{17,1},{2,18},{18,2},{3,19},{19,3},{4,20},{20... | collective-permute-start | bytes 73736 | tf_op jit(solution)/shard_map/ppermute | solution.py:286
  4.8 8.7 %collective-permute-start.1 = (bf16[24,4096]{1,0:T(8,128)(2,1)S(1)}, bf16[24,4096]{1,0:T(8,128)(2,1)S(1)}, u32[]{:S(2)}, u32[]{:S(2)}) collective-permute-start(bf16[24,4096]{1,0:T(8,128)(2,1)S(1)} %copy-done.3), channel_id=1, source_target_pairs={{0,16},{16,0},{1,17},{17,1},{2,18},{18,2},{3,19},{19,3},{4,20},{20... | collective-permute-start | bytes 589832 | tf_op jit(solution)/shard_map/ppermute | solution.py:286
  9.6 2.8 %copy-start = (bf16[1,768,4096]{2,1,0:T(8,128)(2,1)S(1)}, bf16[1,768,4096]{2,1,0:T(8,128)(2,1)}, u32[]{:S(2)}) copy-start(bf16[1,768,4096]{2,1,0:T(8,128)(2,1)} %param.16) | copy-start | bytes 18874372
  13.1 1.9 %collective-permute-start.3 = (bf16[2,2,24,1024]{3,2,1,0:T(8,128)(2,1)S(1)}, bf16[2,2,24,1024]{3,2,1,0:T(8,128)(2,1)S(1)}, u32[]{:S(2)}, u32[]{:S(2)}) collective-permute-start(bf16[2,2,24,1024]{3,2,1,0:T(8,128)(2,1)S(1)} %outward_send.1.refs_4_), channel_id=1, source_target_pairs={{0,1},{1,0},{2,3},{3,2},{4,5},{5,4},{6,7},{7,6},{8,9},{9,8},{10,11... | collective-permute-start | bytes 589832 | tf_op jit(solution)/shard_map/ppermute | solution.py:286
  15.1 5.5 %collective-permute-start.4 = (bf16[2,24,1024]{2,1,0:T(8,128)(2,1)S(1)}, bf16[2,24,1024]{2,1,0:T(8,128)(2,1)S(1)}, u32[]{:S(2)}, u32[]{:S(2)}) collective-permute-start(bf16[2,24,1024]{2,1,0:T(8,128)(2,1)S(1)} %get-tuple-element.42), channel_id=1, source_target_pairs={{0,16},{16,0},{1,17},{17,1},{2,18},{18,2},{3,19},{19,3},{4,20},{20... | collective-permute-start | bytes 294920 | tf_op jit(solution)/shard_map/ppermute | solution.py:286
  20.3 2.3 %collective-permute-start.5 = (bf16[2,2,24,1024]{3,2,1,0:T(8,128)(2,1)S(1)}, bf16[2,2,24,1024]{3,2,1,0:T(8,128)(2,1)S(1)}, u32[]{:S(2)}, u32[]{:S(2)}) collective-permute-start(bf16[2,2,24,1024]{3,2,1,0:T(8,128)(2,1)S(1)} %get-tuple-element.35), channel_id=1, source_target_pairs={{0,1},{1,0},{2,3},{3,2},{4,5},{5,4},{6,7},{7,6},{8,9},{9,8},{10,11... | collective-permute-start | bytes 589832 | tf_op jit(solution)/shard_map/ppermute | solution.py:286
  20.6 28.4 %copy-start.4 = (bf16[128,4096]{1,0:T(8,128)(2,1)S(1)}, bf16[128,4096]{1,0:T(8,128)(2,1)}, u32[]{:S(2)}) copy-start(bf16[128,4096]{1,0:T(8,128)(2,1)} %refs_17_.1) | copy-start | bytes 3145732
  22.6 5.3 %collective-permute-start.19 = (bf16[2,24,1024]{2,1,0:T(8,128)(2,1)S(1)}, bf16[2,24,1024]{2,1,0:T(8,128)(2,1)S(1)}, u32[]{:S(2)}, u32[]{:S(2)}) collective-permute-start(bf16[2,24,1024]{2,1,0:T(8,128)(2,1)S(1)} %get-tuple-element.41), channel_id=1, source_target_pairs={{0,2},{2,0},{1,3},{3,1},{4,6},{6,4},{5,7},{7,5},{8,10},{10,8},{9,1... | collective-permute-start | bytes 294920 | tf_op jit(solution)/shard_map/ppermute | solution.py:286
  24.2 5.4 %collective-permute-start.6 = (bf16[24,1024]{1,0:T(8,128)(2,1)S(1)}, bf16[24,1024]{1,0:T(8,128)(2,1)S(1)}, u32[]{:S(2)}, u32[]{:S(2)}) collective-permute-start(bf16[24,1024]{1,0:T(8,128)(2,1)S(1)} %get-tuple-element.38), channel_id=1, source_target_pairs={{0,18},{2,16},{16,2},{18,0},{1,19},{3,17},{17,3},{19,1},{4,22},{6,... | collective-permute-start | bytes 147464 | tf_op jit(solution)/shard_map/ppermute | solution.py:286
  25.7 4.1 %collective-permute-start.7 = (bf16[24,1024]{1,0:T(8,128)(2,1)S(1)}, bf16[24,1024]{1,0:T(8,128)(2,1)S(1)}, u32[]{:S(2)}, u32[]{:S(2)}) collective-permute-start(bf16[24,1024]{1,0:T(8,128)(2,1)S(1)} %get-tuple-element.39), channel_id=1, source_target_pairs={{0,16},{2,18},{16,0},{18,2},{1,17},{3,19},{17,1},{19,3},{4,20},{6,... | collective-permute-start | bytes 147464 | tf_op jit(solution)/shard_map/ppermute | solution.py:286
  26.2 4.1 %collective-permute-start.8 = (bf16[24,1024]{1,0:T(8,128)(2,1)S(1)}, bf16[24,1024]{1,0:T(8,128)(2,1)S(1)}, u32[]{:S(2)}, u32[]{:S(2)}) collective-permute-start(bf16[24,1024]{1,0:T(8,128)(2,1)S(1)} %get-tuple-element.40), channel_id=1, source_target_pairs={{0,2},{2,0},{16,18},{18,16},{1,3},{3,1},{17,19},{19,17},{4,6},{6,4... | collective-permute-start | bytes 147464 | tf_op jit(solution)/shard_map/ppermute | solution.py:286
  28.0 6.8 %collective-permute-start.20 = (bf16[2,24,1024]{2,1,0:T(8,128)(2,1)S(1)}, bf16[2,24,1024]{2,1,0:T(8,128)(2,1)S(1)}, u32[]{:S(2)}, u32[]{:S(2)}) collective-permute-start(bf16[2,24,1024]{2,1,0:T(8,128)(2,1)S(1)} %add_convert_fusion.3), channel_id=1, source_target_pairs={{0,4},{4,0},{8,12},{12,8},{1,5},{5,1},{9,13},{13,9},{2,6},{6,2},{1... | collective-permute-start | bytes 294920 | tf_op jit(solution)/shard_map/ppermute | solution.py:286
  30.3 6.7 %collective-permute-start.11 = (bf16[24,1024]{1,0:T(8,128)(2,1)S(1)}, bf16[24,1024]{1,0:T(8,128)(2,1)S(1)}, u32[]{:S(2)}, u32[]{:S(2)}) collective-permute-start(bf16[24,1024]{1,0:T(8,128)(2,1)S(1)} %add_convert_fusion.6), channel_id=1, source_target_pairs={{0,12},{4,8},{8,4},{12,0},{1,13},{5,9},{9,5},{13,1},{2,14},{6,10},... | collective-permute-start | bytes 147464 | tf_op jit(solution)/shard_map/ppermute | solution.py:286
  34.0 6.2 %collective-permute-start.10 = (bf16[24,1024]{1,0:T(8,128)(2,1)S(1)}, bf16[24,1024]{1,0:T(8,128)(2,1)S(1)}, u32[]{:S(2)}, u32[]{:S(2)}) collective-permute-start(bf16[24,1024]{1,0:T(8,128)(2,1)S(1)} %add_convert_fusion.6), channel_id=1, source_target_pairs={{0,8},{4,12},{8,0},{12,4},{1,9},{5,13},{9,1},{13,5},{2,10},{6,14},... | collective-permute-start | bytes 147464 | tf_op jit(solution)/shard_map/ppermute | solution.py:286
  34.0 6.2 %collective-permute-start.9 = (bf16[24,1024]{1,0:T(8,128)(2,1)S(1)}, bf16[24,1024]{1,0:T(8,128)(2,1)S(1)}, u32[]{:S(2)}, u32[]{:S(2)}) collective-permute-start(bf16[24,1024]{1,0:T(8,128)(2,1)S(1)} %add_convert_fusion.6), channel_id=1, source_target_pairs={{0,4},{4,0},{8,12},{12,8},{1,5},{5,1},{9,13},{13,9},{2,6},{6,2},{1... | collective-permute-start | bytes 147464 | tf_op jit(solution)/shard_map/ppermute | solution.py:286
  34.8 9.0 %collective-permute-start.21 = (bf16[2,24,1024]{2,1,0:T(8,128)(2,1)S(1)}, bf16[2,24,1024]{2,1,0:T(8,128)(2,1)S(1)}, u32[]{:S(2)}, u32[]{:S(2)}) collective-permute-start(bf16[2,24,1024]{2,1,0:T(8,128)(2,1)S(1)} %add_convert_fusion.2), channel_id=1, source_target_pairs={{0,8},{4,12},{8,0},{12,4},{1,9},{5,13},{9,1},{13,5},{2,10},{6,14},... | collective-permute-start | bytes 294920 | tf_op jit(solution)/shard_map/ppermute | solution.py:286
  40.3 5.1 %collective-permute-start.14 = (bf16[24,1024]{1,0:T(8,128)(2,1)S(1)}, bf16[24,1024]{1,0:T(8,128)(2,1)S(1)}, u32[]{:S(2)}, u32[]{:S(2)}) collective-permute-start(bf16[24,1024]{1,0:T(8,128)(2,1)S(1)} %add_convert_fusion.5.refs_6_), channel_id=1, source_target_pairs={{0,18},{2,16},{16,2},{18,0},{1,19},{3,17},{17,3},{19,1},{4,22},{6,... | collective-permute-start | bytes 147464 | tf_op jit(solution)/shard_map/ppermute | solution.py:286
  42.7 4.1 %collective-permute-start.13 = (bf16[24,1024]{1,0:T(8,128)(2,1)S(1)}, bf16[24,1024]{1,0:T(8,128)(2,1)S(1)}, u32[]{:S(2)}, u32[]{:S(2)}) collective-permute-start(bf16[24,1024]{1,0:T(8,128)(2,1)S(1)} %add_convert_fusion.5.refs_6_), channel_id=1, source_target_pairs={{0,16},{2,18},{16,0},{18,2},{1,17},{3,19},{17,1},{19,3},{4,20},{6,... | collective-permute-start | bytes 147464 | tf_op jit(solution)/shard_map/ppermute | solution.py:286
  43.6 4.1 %collective-permute-start.12 = (bf16[24,1024]{1,0:T(8,128)(2,1)S(1)}, bf16[24,1024]{1,0:T(8,128)(2,1)S(1)}, u32[]{:S(2)}, u32[]{:S(2)}) collective-permute-start(bf16[24,1024]{1,0:T(8,128)(2,1)S(1)} %add_convert_fusion.5.refs_6_), channel_id=1, source_target_pairs={{0,2},{2,0},{16,18},{18,16},{1,3},{3,1},{17,19},{19,17},{4,6},{6,4... | collective-permute-start | bytes 147464 | tf_op jit(solution)/shard_map/ppermute | solution.py:286
  43.8 5.1 %collective-permute-start.22 = (bf16[2,24,1024]{2,1,0:T(8,128)(2,1)S(1)}, bf16[2,24,1024]{2,1,0:T(8,128)(2,1)S(1)}, u32[]{:S(2)}, u32[]{:S(2)}) collective-permute-start(bf16[2,24,1024]{2,1,0:T(8,128)(2,1)S(1)} %add_convert_fusion.1.refs_14_), channel_id=1, source_target_pairs={{0,1},{1,0},{2,3},{3,2},{4,5},{5,4},{6,7},{7,6},{8,9},{9,8},{10,11... | collective-permute-start | bytes 294920 | tf_op jit(solution)/shard_map/ppermute | solution.py:286
  43.9 3.8 %collective-permute-start.15 = (bf16[24,1024]{1,0:T(8,128)(2,1)S(1)}, bf16[24,1024]{1,0:T(8,128)(2,1)S(1)}, u32[]{:S(2)}, u32[]{:S(2)}) collective-permute-start(bf16[24,1024]{1,0:T(8,128)(2,1)S(1)} %add_convert_fusion.5.refs_6_), channel_id=1, source_target_pairs={{0,1},{1,0},{2,3},{3,2},{4,5},{5,4},{6,7},{7,6},{8,9},{9,8},{10,11... | collective-permute-start | bytes 147464 | tf_op jit(solution)/shard_map/ppermute | solution.py:286
  45.3 2.4 %collective-permute-start.18 = (bf16[24,1024]{1,0:T(8,128)(2,1)S(1)}, bf16[24,1024]{1,0:T(8,128)(2,1)S(1)}, u32[]{:S(2)}, u32[]{:S(2)}) collective-permute-start(bf16[24,1024]{1,0:T(8,128)(2,1)S(1)} %collective-permute-done.14.refs_9_), channel_id=1, source_target_pairs={{0,1},{1,0},{2,3},{3,2},{4,5},{5,4},{6,7},{7,6},{8,9},{9,8},{10,11... | collective-permute-start | bytes 147464 | tf_op jit(solution)/shard_map/ppermute | solution.py:286
  46.8 1.2 %collective-permute-start.17 = (bf16[24,1024]{1,0:T(8,128)(2,1)S(1)}, bf16[24,1024]{1,0:T(8,128)(2,1)S(1)}, u32[]{:S(2)}, u32[]{:S(2)}) collective-permute-start(bf16[24,1024]{1,0:T(8,128)(2,1)S(1)} %collective-permute-done.13.refs_8_), channel_id=1, source_target_pairs={{0,1},{1,0},{2,3},{3,2},{4,5},{5,4},{6,7},{7,6},{8,9},{9,8},{10,11... | collective-permute-start | bytes 147464 | tf_op jit(solution)/shard_map/ppermute | solution.py:286
  47.7 1.2 %collective-permute-start.16 = (bf16[24,1024]{1,0:T(8,128)(2,1)S(1)}, bf16[24,1024]{1,0:T(8,128)(2,1)S(1)}, u32[]{:S(2)}, u32[]{:S(2)}) collective-permute-start(bf16[24,1024]{1,0:T(8,128)(2,1)S(1)} %collective-permute-done.12.refs_7_), channel_id=1, source_target_pairs={{0,1},{1,0},{2,3},{3,2},{4,5},{5,4},{6,7},{7,6},{8,9},{9,8},{10,11... | collective-permute-start | bytes 147464 | tf_op jit(solution)/shard_map/ppermute | solution.py:286

commit v11 on v10

--- a/solution.py
+++ b/solution.py
@@ -15,6 +15,7 @@
 LOAD_PIECES = 8
 FEW_ROWS = 64
 VMEM_LIMIT = 12 * 1024 * 1024
+VMEM_LIMIT_MANY = 24 * 1024 * 1024
 
 
 def dot(a, b, dims):
@@ -25,12 +26,36 @@
     return pl.multiple_of(step * count, count)
 
 
-def rows_of(refs, columns):
-    return jnp.concatenate([ref[:, columns].astype(F32) for ref in refs], axis=0)
+def parity(number):
+    shift = 1
+    while shift < 32:
+        number = number ^ (number >> shift)
+        shift = 2 * shift
+    return number & 1
+
+
+def own_half():
+    chip = lax.axis_index("dp") ^ lax.axis_index("y") ^ lax.axis_index("hi")
+    return lax.axis_index("c") ^ parity(chip)
 
 
 def own_columns(i, j, width):
-    return ((lax.axis_index("y") ^ j) * 2 + (lax.axis_index("c") ^ i)) * width
+    return ((lax.axis_index("y") ^ j) * 2 + (own_half() ^ i)) * width
+
+
+def both_halves(refs, width, body):
+    core, half = lax.axis_index("c"), width // 2
+    size = 512 if len(refs[0]) <= 3 else 128
+    for h in range(2):
+        for step in range(half // size):
+            columns = pl.ds(pl.multiple_of((core ^ h) * half + step * size, size), size)
+
+            def rows_at(group):
+                first = group[0][:, columns].astype(F32)
+                others = [ref[:, step * size : (step + 1) * size].astype(F32) for ref in group[1 + h :: 2]]
+                return jnp.concatenate([first] + others, axis=0)
+
+            body(columns, *[rows_at(group) for group in refs])
 
 
 def store_blocks(out_ref, j, columns, value, count):
@@ -81,23 +106,22 @@
 
 
 def hidden_kernel(n_dp, *refs):
-    hid = refs[:n_dp]
-    gain, w_gate, w_up, pre_gate, pre_up, act, normed = refs[n_dp:]
-    total = hid[0].shape[0] * n_dp
-    width = hid[0].shape[1]
+    hid = refs[: 2 * n_dp - 1]
+    gain, w_gate, w_up, pre_gate, pre_up, act, normed = refs[2 * n_dp - 1 :]
+    total, width = hid[0].shape[0] * n_dp, hid[0].shape[1]
     few = total <= FEW_ROWS
-    sums = jnp.zeros((total, 1), F32)
-    for step in range(width // 512):
-        value = rows_of(hid, pl.ds(step * 512, 512))
-        sums = sums + jnp.sum(value * value, axis=1, keepdims=True)
-    scale = lax.rsqrt(sums / width + EPSILON)
-
-    def norm(step):
-        columns = pl.ds(place(step, 512), 512)
-        normed[:, columns] = (rows_of(hid, columns) * scale * gain[:, columns]).astype(BF16)
-
-    loop(width // 512, norm, few)
-
+    sums = [jnp.zeros((total, 1), F32)]
+
+    def square(columns, value):
+        sums[0] = sums[0] + jnp.sum(value * value, axis=1, keepdims=True)
+
+    both_halves([hid], width, square)
+    scale = lax.rsqrt(sums[0] / width + EPSILON)
+
+    def norm(columns, value):
+        normed[:, columns] = (value * scale * gain[:, columns]).astype(BF16)
+
+    both_halves([hid], width, norm)
     size = unit_step(w_gate.shape[1])
 
     def hidden_units(step):
@@ -163,17 +187,16 @@
 
 
 def backward_first_kernel(n_dp, *refs):
-    grads, smalls = refs[:n_dp], refs[n_dp : 2 * n_dp]
-    pre_gate, pre_up, w_down, waiting, grad_gate, grad_up, weighted, passed = refs[2 * n_dp :]
+    grads, smalls = refs[: 2 * n_dp - 1], refs[2 * n_dp - 1 : 3 * n_dp - 1]
+    pre_gate, pre_up, w_down, waiting, grad_gate, grad_up, weighted, passed = refs[3 * n_dp - 1 :]
     passed[...] = waiting[...]
     weight = gates_of(smalls)
     few = weighted.shape[0] <= FEW_ROWS
 
-    def weigh(step):
-        columns = pl.ds(place(step, 512), 512)
-        weighted[:, columns] = (weight * rows_of(grads, columns)).astype(BF16)
-
-    loop(weighted.shape[1] // 512, weigh, few)
+    def weigh(columns, value):
+        weighted[:, columns] = (weight * value).astype(BF16)
+
+    both_halves([grads], weighted.shape[1], weigh)
     gradients(0, weighted, pre_gate, pre_up, w_down, grad_gate, grad_up, few)
 
 
@@ -197,11 +220,13 @@
 
 
 def finish_kernel(n_dp, *refs):
-    hid, grads, smalls = refs[:n_dp], refs[n_dp : 2 * n_dp], refs[2 * n_dp : 3 * n_dp]
-    back, moe = refs[3 * n_dp : 7 * n_dp], refs[7 * n_dp : 7 * n_dp + 2]
-    gain, w_out = refs[7 * n_dp + 2 : 7 * n_dp + 4]
-    targets, held = refs[7 * n_dp + 4 : 7 * n_dp + 8], refs[7 * n_dp + 8 : 7 * n_dp + 12]
-    summed, d_all, sems = refs[7 * n_dp + 12 :]
+    count = 2 * n_dp - 1
+    hid, grads, smalls = refs[:count], refs[count : 2 * count], refs[2 * count : 2 * count + n_dp]
+    refs = refs[2 * count + n_dp :]
+    back, moe = refs[: 4 * n_dp], refs[4 * n_dp : 4 * n_dp + 2]
+    refs = refs[4 * n_dp + 2 :]
+    gain, w_out, targets, held = refs[0], refs[1], refs[2:6], refs[6:10]
+    summed, d_all, sems = refs[10:]
     output, d_hidden, d_context, d_w_out = held
     copies = [pltpu.make_async_copy(held[n], targets[n], sems.at[n]) for n in range(4)]
     rows, width = hid[0].shape
@@ -216,24 +241,22 @@
     copies[0].start()
 
     few = rows * n_dp <= FEW_ROWS
-    squares = jnp.zeros((rows * n_dp, 1), F32)
-    products = squares
-    for step in range(width // 512):
-        columns = pl.ds(step * 512, 512)
-        value = rows_of(hid, columns)
-        squares = squares + jnp.sum(value * value, axis=1, keepdims=True)
-        products = products + jnp.sum(value * summed[:, columns], axis=1, keepdims=True)
-    scale = lax.rsqrt(squares / width + EPSILON)
-    centre = scale * products / width
-
-    def total(step):
-        columns = pl.ds(place(step, 512), 512)
-        unit_rows = rows_of(hid, columns) * scale
-        value = rows_of(grads, columns) + scale * (summed[:, columns] - unit_rows * centre)
-        d_all[:, columns] = value.astype(BF16)
-        d_hidden[:, columns] = value[:rows].astype(BF16)
-
-    loop(width // 512, total, few)
+    sums = [jnp.zeros((rows * n_dp, 1), F32)] * 2
+
+    def products(columns, value):
+        sums[0] = sums[0] + jnp.sum(value * value, axis=1, keepdims=True)
+        sums[1] = sums[1] + jnp.sum(value * summed[:, columns], axis=1, keepdims=True)
+
+    both_halves([hid], width, products)
+    scale = lax.rsqrt(sums[0] / width + EPSILON)
+    centre = scale * sums[1] / width
+
+    def total(columns, value, grad):
+        result = grad + scale * (summed[:, columns] - value * scale * centre)
+        d_all[:, columns] = result.astype(BF16)
+        d_hidden[:, columns] = result[:rows].astype(BF16)
+
+    both_halves([hid, grads], width, total)
     copies[1].start()
     d_context[...] = dot(d_hidden[...], w_out[...], ((1,), (1,))).astype(BF16)
     part = width // n_dp
@@ -264,7 +287,7 @@
         in_specs=[pl.BlockSpec(memory_space=space) for space in spaces],
         out_specs=[pl.BlockSpec(memory_space=out_space)] * len(outs),
         scratch_shapes=scratch,
-        compiler_params=pltpu.CompilerParams(vmem_limit_bytes=VMEM_LIMIT),
+        compiler_params=pltpu.CompilerParams(vmem_limit_bytes=VMEM_LIMIT if n_dp <= 2 else VMEM_LIMIT_MANY),
         cost_estimate=pl.CostEstimate(flops=0, bytes_accessed=cost, transcendentals=0),
         name=name,
     )(*held)
@@ -278,15 +301,20 @@
     top, heads = route_ids.shape[1], context.shape[1]
     all_rows, units, chunk = n_dp * rows, w_gate.shape[2], width // 4
 
-    def swap(value, axes, turn):
-        sizes = [lax.axis_size(name) for name in axes]
-        count = 1
-        for size in sizes:
-            count *= size
-        return lax.ppermute(value, axes, [(i, i ^ turn) for i in range(count)])
+    def swap(value, axes, turn, cross=True):
+        count = 2
+        for name in axes:
+            count *= lax.axis_size(name)
+        turn = 2 * turn + (parity(turn) if cross else 0)
+        return lax.ppermute(value, axes + ("c",), [(i, i ^ turn) for i in range(count)])
+
+    def other_core(value):
+        return lax.ppermute(value, ("c",), [(0, 1), (1, 0)])
 
     def all_blocks(value):
-        return [value] + [swap(value, ("dp",), k) for k in range(1, n_dp)]
+        half = lax.dynamic_slice_in_dim(value, lax.axis_index("c") * (width // 2), width // 2, 1)
+        here = [swap(half, ("dp",), k, False) for k in range(1, n_dp)]
+        return [value] + [piece for one in here for piece in (one, other_core(one))]
 
     weights = 2 * width * units
     shares = ((n_dp, 2, rows, chunk), BF16)
@@ -299,7 +327,7 @@
         4 * weights, "gates", far=range(6),
     )
     hid = all_blocks(hidden_in)
-    smalls = all_blocks(small_own)
+    smalls = [small_own] + [swap(small_own, ("dp",), k, False) for k in range(1, n_dp)]
     grads = all_blocks(grad_out)
 
     def add(one, other):
@@ -320,7 +348,7 @@
         functools.partial(outward_kernel, 1), n_dp, smalls + [act, wd], [shares], [],
         weights // 2, "outward_send",
     )
-    out_other = swap(out_send, ("c",), 1)
+    out_other = other_core(out_send)
     (out_keep,) = run(
         functools.partial(outward_kernel, 0), n_dp, smalls + [act, wd, out_send] + grads, [shares], [],
         weights // 2, "outward_keep",
@@ -345,7 +373,7 @@
         functools.partial(inward_kernel, 1), n_dp, back_grads + [wg, wu, out_block],
         [shares, block], [], weights, "inward_send",
     )
-    in_other = swap(in_send, ("c",), 1)
+    in_other = other_core(in_send)
     out_block = total_of([out_block] + out_blocks)
     in_keep, out_block = run(
         functools.partial(inward_kernel, 0), n_dp, back_grads + [wg, wu, out_block], [shares, block], [],
@@ -366,8 +394,8 @@
     order = [t for t in turns if t < 2] + [t for t in turns if t >= 2]
     spread = {t: swap(in_total, ("dp", "y"), t) for t in order}
     back = [in_total] + [spread[t] for t in range(1, 2 * n_dp)]
-    back = back + [swap(piece, ("c",), 1) for piece in back]
-    moe = [out_total, swap(out_total, ("c",), 1)]
+    back = back + [other_core(piece) for piece in back]
+    moe = [out_total, other_core(out_total)]
     outs = [((rows, width), BF16), ((rows, width), BF16), ((rows, heads), BF16), ((heads, width // n_dp), BF16)]
     return run(
         finish_kernel, n_dp, hid + grads + smalls + back + moe + [gain, w_out], outs,

time: 50.8 us -> 50.1 us (0.986)
  waiting for transfers between devices: 11.7 us -> 10.3 us
  local copies, waits for them, and re-layouts: 0.38 us -> 1.32 us
  starting transfers between devices: 24.8 us -> 24.1 us
    ppermute x23 -> x25, waiting for transfers between devices: 11.7 us -> 10.3 us  [the longest x16 8.38 us: swap(): lax.ppermute(value, axes + ('c',), [(i, i ^ turn) for i in range(count)])]
    dynamic_slice x0 -> x2, local copies, waits for them, and re-layouts: none -> 1.07 us  [all_blocks(): lax.dynamic_slice_in_dim(value, lax.axis_index('c') * (width // 2), width...]
    ppermute x23 -> x25, starting transfers between devices: 24.8 us -> 24.1 us  [the longest x16 22 us: swap(): lax.ppermute(value, axes + ('c',), [(i, i ^ turn) for i in range(count)])]
  transfers between devices with their start and end apart: 23 -> 25, of which waited for: 11 -> 12; matrix products, arithmetic and copies ran while one was open for 0% -> 0% of each run, Pallas kernels for 22% -> 22%
where the time goes in v11:
time: 50.1 us; the launch traced here: 49.9 us
  starting transfers between devices  24.1 us (48%)
  Pallas kernels  13 us (26%)
  waiting for transfers between devices  10.3 us (21%)
  local copies, waits for them, and re-layouts  1.32 us (3%)
  between operations  0.89 us (2%)
    ppermute x16, starting transfers between devices, swap(): lax.ppermute(value, axes + ('c',), [(i, i ^ turn) for i in range(count)])  22 us
    pallas_call x10, Pallas kernels, run(): pl.pallas_call(functools.partial(kernel, n_dp), out_shape=kinds, in_specs...  13 us
    ppermute x16, waiting for transfers between devices, swap(): lax.ppermute(value, axes + ('c',), [(i, i ^ turn) for i in range(count)])  8.38 us
    ppermute x9, starting transfers between devices, other_core(): return lax.ppermute(value, ('c',), [(0, 1), (1, 0)])  2.09 us
    ppermute x9, waiting for transfers between devices, other_core(): return lax.ppermute(value, ('c',), [(0, 1), (1, 0)])  1.96 us
    dynamic_slice x2, local copies, waits for them, and re-layouts, all_blocks(): lax.dynamic_slice_in_dim(value, lax.axis_index('c') * (width // 2), width...  1.07 us
  transfers between devices with their start and end apart: 25, of which 12 were waited for; matrix products, arithmetic and copies ran while one was open for 0% of the time, Pallas kernels for 22%

profile of v11, /device:TPU:0, one launch (start us, length us, event | category | flops | bytes accessed | tf_op | source)
XLA Modules:
  0.0 49.9 jit_solution(9061926417404135659)
XLA Ops:
  0.6 0.0 slice-start.2
  0.7 1.1 %constant_dynamic-slice_fusion.1 = bf16[24,2048]{1,0:T(8,128)(2,1)S(1)} fusion(bf16[24,4096]{1,0:T(8,128)(2,1)} %refs_0_.5, s32[]{:T(128)S(6)} %select_n.4), kind=kLoop, calls=%fused_computation.10 | loop fusion | bytes 196612 | tf_op jit(solution)/shard_map/dynamic_slice | solution.py:315
  1.7 2.9 %collective-permute-start = (bf16[24,2048]{1,0:T(8,128)(2,1)S(1)}, bf16[24,2048]{1,0:T(8,128)(2,1)S(1)}, u32[]{:S(2)}, u32[]{:S(2)}) collective-permute-start(bf16[24,2048]{1,0:T(8,128)(2,1)S(1)} %constant_dynamic-slice_fusion.1), channel_id=1, source_target_pairs={{0,16},{1,17},{16,0},{17,1},{2,18},{3,19},{18,2},{19,3},{4,20},{5,... | collective-permute-start | bytes 294920 | tf_op jit(solution)/shard_map/ppermute | solution.py:309
  4.7 1.0 %gates.1.refs_0_.refs_3_.refs_6_ = f32[24,256]{1,0:T(8,128)S(1)} custom-call(s32[8,24]{1,0:T(8,128)} %bitcast.29, f32[8,24]{1,0:T(8,128)} %bitcast.30, bf16[24,128]{1,0:T(8,128)(2,1)} %context.1, bf16[4096,768]{1,0:T(8,128)(2,1)} %bitcast.15, bf16[4096,768]{1,0:T(8,128)(2,1)} %bitcast.21, bf16[768,4096]{1,0:T(8,128)(2,1)} %bitcast.10), custom_call_target="tpu_custom_call" | custom-call | bytes 25165824 | tf_op jit(solution)/shard_map/gates/pallas_call | solution.py:284
  5.7 0.5 collective-permute-start.4
  6.2 1.3 %collective-permute-done.refs_1_ = bf16[24,2048]{1,0:T(8,128)(2,1)S(1)} collective-permute-done((bf16[24,2048]{1,0:T(8,128)(2,1)S(1)}, bf16[24,2048]{1,0:T(8,128)(2,1)S(1)}, u32[]{:S(2)}, u32[]{:S(2)}) %collective-permute-start) | collective-permute-done | bytes 98336 | tf_op jit(solution)/shard_map/ppermute | solution.py:309
  7.5 2.2 %collective-permute-start.2 = (bf16[24,2048]{1,0:T(8,128)(2,1)S(1)}, bf16[24,2048]{1,0:T(8,128)(2,1)S(1)}, u32[]{:S(2)}, u32[]{:S(2)}) collective-permute-start(bf16[24,2048]{1,0:T(8,128)(2,1)S(1)} %constant_dynamic-slice_fusion), channel_id=1, source_target_pairs={{0,16},{1,17},{16,0},{17,1},{2,18},{3,19},{18,2},{19,3},{4,20},{5,... | collective-permute-start | bytes 294920 | tf_op jit(solution)/shard_map/ppermute | solution.py:309
  9.7 2.6 %hidden.1 = (f32[48,768]{1,0:T(8,128)S(1)}, f32[48,768]{1,0:T(8,128)S(1)}, bf16[48,768]{1,0:T(8,128)(2,1)S(1)}) custom-call(bf16[24,4096]{1,0:T(8,128)(2,1)S(1)} %copy-done.2, bf16[24,2048]{1,0:T(8,128)(2,1)S(1)} %collective-permute-done.refs_1_, bf16[24,2048]{1,0:T(8,128)(2,1)S(1)} %collective-permute-done.1.refs_2_, f32[1,4096]{1,0:T(1,128)S(1)} %bitcast.27, ...), custom_call_target="tpu_custom_call" | custom-call | bytes 12582912 | tf_op jit(solution)/shard_map/hidden/pallas_call | solution.py:284
  12.3 0.2 copy-done
  12.5 0.7 %outward_send.1.refs_4_ = bf16[2,2,24,1024]{3,2,1,0:T(8,128)(2,1)S(1)} custom-call(f32[24,256]{1,0:T(8,128)S(1)} %gates.1.refs_0_.refs_3_.refs_6_, f32[24,256]{1,0:T(8,128)S(1)} %collective-permute-done.4.refs_1_.refs_4_.refs_7_, bf16[48,768]{1,0:T(8,128)(2,1)S(1)} %get-tuple-element.25.refs_2_, bf16[768,4096]{1,0:T(8,128)(2,1)S(1)} %bitcast.11), custom_call_target="tpu_custom_call" | custom-call | bytes 3145728 | tf_op jit(solution)/shard_map/outward_send/pallas_call | solution.py:284
  13.2 0.3 collective-permute-start.5
  13.5 0.3 collective-permute-start.3
  13.7 1.1 %collective-permute-done.3.refs_7_.refs_2_.refs_5_ = bf16[24,2048]{1,0:T(8,128)(2,1)S(1)} collective-permute-done((bf16[24,2048]{1,0:T(8,128)(2,1)S(1)}, bf16[24,2048]{1,0:T(8,128)(2,1)S(1)}, u32[]{:S(2)}, u32[]{:S(2)}) %collective-permute-start.3) | collective-permute-done | bytes 98336 | tf_op jit(solution)/shard_map/ppermute | solution.py:312
  14.8 0.7 %outward_keep.1.refs_8_ = bf16[2,2,24,1024]{3,2,1,0:T(8,128)(2,1)S(1)} custom-call(f32[24,256]{1,0:T(8,128)S(1)} %gates.1.refs_0_.refs_3_.refs_6_, f32[24,256]{1,0:T(8,128)S(1)} %collective-permute-done.4.refs_1_.refs_4_.refs_7_, bf16[48,768]{1,0:T(8,128)(2,1)S(1)} %get-tuple-element.25.refs_2_, bf16[768,4096]{1,0:T(8,128)(2,1)S(1)} %bitcast.12, ...), custom_call_target="tpu_custom_call" | custom-call | bytes 3145728 | tf_op jit(solution)/shard_map/outward_keep/pallas_call | solution.py:284
  15.5 0.8 %backward_first.1 = (bf16[48,256]{1,0:T(8,128)(2,1)S(1)}, bf16[48,256]{1,0:T(8,128)(2,1)S(1)}, bf16[48,4096]{1,0:T(8,128)(2,1)S(1)}, bf16[2,2,24,1024]{3,2,1,0:T(8,128)(2,1)S(1)}) custom-call(bf16[24,4096]{1,0:T(8,128)(2,1)S(1)} %copy-done.1, bf16[24,2048]{1,0:T(8,128)(2,1)S(1)} %collective-permute-done.2.refs_6_.refs_1_.refs_4_, ...), custom_call_target="tpu_custom_call" | custom-call | bytes 2097152 | tf_op jit(solution)/shard_map/backward_first/pallas_call | solution.py:284
  16.3 0.1 add_convert_fusion
  16.4 1.1 %collective-permute-start.6 = (bf16[2,24,1024]{2,1,0:T(8,128)(2,1)S(1)}, bf16[2,24,1024]{2,1,0:T(8,128)(2,1)S(1)}, u32[]{:S(2)}, u32[]{:S(2)}) collective-permute-start(bf16[2,24,1024]{2,1,0:T(8,128)(2,1)S(1)} %get-tuple-element.42), channel_id=1, source_target_pairs={{0,17},{1,16},{16,1},{17,0},{2,19},{3,18},{18,3},{19,2},{4,21},{5,... | collective-permute-start | bytes 294920 | tf_op jit(solution)/shard_map/ppermute | solution.py:309
  17.6 1.4 %backward_rest.1 = (bf16[48,512]{1,0:T(8,128)(2,1)S(1)}, bf16[48,512]{1,0:T(8,128)(2,1)S(1)}, bf16[2,24,1024]{2,1,0:T(8,128)(2,1)S(1)}) custom-call(bf16[48,4096]{1,0:T(8,128)(2,1)S(1)} %get-tuple-element.28.weighted, f32[48,768]{1,0:T(8,128)S(1)} %get-tuple-element.23.refs_5_.pre_gate, f32[48,768]{1,0:T(8,128)S(1)} %get-tuple-element.24.refs_6_.pre_up, ...), custom_call_target="tpu_custom_call" | custom-call | bytes 4194304 | tf_op jit(solution)/shard_map/backward_rest/pallas_call | solution.py:284
  19.0 2.0 %inward_send.1 = (bf16[2,2,24,1024]{3,2,1,0:T(8,128)(2,1)S(1)}, bf16[2,24,1024]{2,1,0:T(8,128)(2,1)S(1)}) custom-call(bf16[48,256]{1,0:T(8,128)(2,1)S(1)} %get-tuple-element.26.refs_0_, bf16[48,256]{1,0:T(8,128)(2,1)S(1)} %get-tuple-element.27.refs_1_, bf16[48,512]{1,0:T(8,128)(2,1)S(1)} %get-tuple-element.30.refs_2_, ...), custom_call_target="tpu_custom_call" | custom-call | bytes 6291456 | tf_op jit(solution)/shard_map/inward_send/pallas_call | solution.py:284
  21.0 0.4 collective-permute-start.7
  21.4 2.0 %inward_keep.1 = (bf16[2,2,24,1024]{3,2,1,0:T(8,128)(2,1)S(1)}, bf16[2,24,1024]{2,1,0:T(8,128)(2,1)S(1)}) custom-call(bf16[48,256]{1,0:T(8,128)(2,1)S(1)} %get-tuple-element.26.refs_0_, bf16[48,256]{1,0:T(8,128)(2,1)S(1)} %get-tuple-element.27.refs_1_, bf16[48,512]{1,0:T(8,128)(2,1)S(1)} %get-tuple-element.30.refs_2_, ...), custom_call_target="tpu_custom_call" | custom-call | bytes 6291456 | tf_op jit(solution)/shard_map/inward_keep/pallas_call | solution.py:284
  23.4 0.1 join.1
  23.5 1.3 %collective-permute-start.21 = (bf16[2,24,1024]{2,1,0:T(8,128)(2,1)S(1)}, bf16[2,24,1024]{2,1,0:T(8,128)(2,1)S(1)}, u32[]{:S(2)}, u32[]{:S(2)}) collective-permute-start(bf16[2,24,1024]{2,1,0:T(8,128)(2,1)S(1)} %get-tuple-element.41), channel_id=1, source_target_pairs={{0,3},{1,2},{2,1},{3,0},{4,7},{5,6},{6,5},{7,4},{8,11},{9,10},{10,... | collective-permute-start | bytes 294920 | tf_op jit(solution)/shard_map/ppermute | solution.py:309
  24.8 1.1 %collective-permute-start.8 = (bf16[24,1024]{1,0:T(8,128)(2,1)S(1)}, bf16[24,1024]{1,0:T(8,128)(2,1)S(1)}, u32[]{:S(2)}, u32[]{:S(2)}) collective-permute-start(bf16[24,1024]{1,0:T(8,128)(2,1)S(1)} %get-tuple-element.38), channel_id=1, source_target_pairs={{0,18},{1,19},{2,16},{3,17},{16,2},{17,3},{18,0},{19,1},{4,22},{5,... | collective-permute-start | bytes 147464 | tf_op jit(solution)/shard_map/ppermute | solution.py:309
  26.0 0.5 %collective-permute-start.9 = (bf16[24,1024]{1,0:T(8,128)(2,1)S(1)}, bf16[24,1024]{1,0:T(8,128)(2,1)S(1)}, u32[]{:S(2)}, u32[]{:S(2)}) collective-permute-start(bf16[24,1024]{1,0:T(8,128)(2,1)S(1)} %get-tuple-element.39), channel_id=1, source_target_pairs={{0,17},{1,16},{2,19},{3,18},{16,1},{17,0},{18,3},{19,2},{4,21},{5,... | collective-permute-start | bytes 147464 | tf_op jit(solution)/shard_map/ppermute | solution.py:309
  26.5 1.6 %collective-permute-start.10 = (bf16[24,1024]{1,0:T(8,128)(2,1)S(1)}, bf16[24,1024]{1,0:T(8,128)(2,1)S(1)}, u32[]{:S(2)}, u32[]{:S(2)}) collective-permute-start(bf16[24,1024]{1,0:T(8,128)(2,1)S(1)} %get-tuple-element.40), channel_id=1, source_target_pairs={{0,3},{1,2},{2,1},{3,0},{16,19},{17,18},{18,17},{19,16},{4,7},{5,6... | collective-permute-start | bytes 147464 | tf_op jit(solution)/shard_map/ppermute | solution.py:309
  28.1 0.9 %collective-permute-done.21 = bf16[2,24,1024]{2,1,0:T(8,128)(2,1)S(1)} collective-permute-done((bf16[2,24,1024]{2,1,0:T(8,128)(2,1)S(1)}, bf16[2,24,1024]{2,1,0:T(8,128)(2,1)S(1)}, u32[]{:S(2)}, u32[]{:S(2)}) %collective-permute-start.21) | collective-permute-done | bytes 98336 | tf_op jit(solution)/shard_map/ppermute | solution.py:309
  28.9 0.8 %collective-permute-start.22 = (bf16[2,24,1024]{2,1,0:T(8,128)(2,1)S(1)}, bf16[2,24,1024]{2,1,0:T(8,128)(2,1)S(1)}, u32[]{:S(2)}, u32[]{:S(2)}) collective-permute-start(bf16[2,24,1024]{2,1,0:T(8,128)(2,1)S(1)} %add_convert_fusion.3), channel_id=1, source_target_pairs={{0,5},{1,4},{4,1},{5,0},{8,13},{9,12},{12,9},{13,8},{2,7},{3,6},{6... | collective-permute-start | bytes 294920 | tf_op jit(solution)/shard_map/ppermute | solution.py:309
  29.8 0.1 collective-permute-done.8
  29.9 0.7 %collective-permute-done.10 = bf16[24,1024]{1,0:T(8,128)(2,1)S(1)} collective-permute-done((bf16[24,1024]{1,0:T(8,128)(2,1)S(1)}, bf16[24,1024]{1,0:T(8,128)(2,1)S(1)}, u32[]{:S(2)}, u32[]{:S(2)}) %collective-permute-start.10) | collective-permute-done | bytes 49184 | tf_op jit(solution)/shard_map/ppermute | solution.py:309
  30.6 3.7 %collective-permute-start.13 = (bf16[24,1024]{1,0:T(8,128)(2,1)S(1)}, bf16[24,1024]{1,0:T(8,128)(2,1)S(1)}, u32[]{:S(2)}, u32[]{:S(2)}) collective-permute-start(bf16[24,1024]{1,0:T(8,128)(2,1)S(1)} %add_convert_fusion.6), channel_id=1, source_target_pairs={{0,12},{1,13},{4,8},{5,9},{8,4},{9,5},{12,0},{13,1},{2,14},{3,15},... | collective-permute-start | bytes 147464 | tf_op jit(solution)/shard_map/ppermute | solution.py:309
  34.3 0.5 collective-permute-start.11
  34.9 2.2 %collective-permute-start.23 = (bf16[2,24,1024]{2,1,0:T(8,128)(2,1)S(1)}, bf16[2,24,1024]{2,1,0:T(8,128)(2,1)S(1)}, u32[]{:S(2)}, u32[]{:S(2)}) collective-permute-start(bf16[2,24,1024]{2,1,0:T(8,128)(2,1)S(1)} %add_convert_fusion.2), channel_id=1, source_target_pairs={{0,9},{1,8},{4,13},{5,12},{8,1},{9,0},{12,5},{13,4},{2,11},{3,10},... | collective-permute-start | bytes 294920 | tf_op jit(solution)/shard_map/ppermute | solution.py:309
  37.1 0.1 collective-permute-done.13
  37.2 2.2 %collective-permute-done.12 = bf16[24,1024]{1,0:T(8,128)(2,1)S(1)} collective-permute-done((bf16[24,1024]{1,0:T(8,128)(2,1)S(1)}, bf16[24,1024]{1,0:T(8,128)(2,1)S(1)}, u32[]{:S(2)}, u32[]{:S(2)}) %collective-permute-start.12) | collective-permute-done | bytes 49184 | tf_op jit(solution)/shard_map/ppermute | solution.py:309
  39.5 3.2 %collective-permute-start.16 = (bf16[24,1024]{1,0:T(8,128)(2,1)S(1)}, bf16[24,1024]{1,0:T(8,128)(2,1)S(1)}, u32[]{:S(2)}, u32[]{:S(2)}) collective-permute-start(bf16[24,1024]{1,0:T(8,128)(2,1)S(1)} %add_convert_fusion.5.refs_8_), channel_id=1, source_target_pairs={{0,18},{1,19},{2,16},{3,17},{16,2},{17,3},{18,0},{19,1},{4,22},{5,... | collective-permute-start | bytes 147464 | tf_op jit(solution)/shard_map/ppermute | solution.py:309
  42.6 0.3 collective-permute-start.15
  42.9 0.1 collective-permute-start.14
  43.0 0.6 %collective-permute-done.23 = bf16[2,24,1024]{2,1,0:T(8,128)(2,1)S(1)} collective-permute-done((bf16[2,24,1024]{2,1,0:T(8,128)(2,1)S(1)}, bf16[2,24,1024]{2,1,0:T(8,128)(2,1)S(1)}, u32[]{:S(2)}, u32[]{:S(2)}) %collective-permute-start.23) | collective-permute-done | bytes 98336 | tf_op jit(solution)/shard_map/ppermute | solution.py:309
  43.6 0.2 collective-permute-start.24
  43.8 0.4 collective-permute-start.17
  44.2 0.7 %collective-permute-done.16.refs_11_ = bf16[24,1024]{1,0:T(8,128)(2,1)S(1)} collective-permute-done((bf16[24,1024]{1,0:T(8,128)(2,1)S(1)}, bf16[24,1024]{1,0:T(8,128)(2,1)S(1)}, u32[]{:S(2)}, u32[]{:S(2)}) %collective-permute-start.16) | collective-permute-done | bytes 49184 | tf_op jit(solution)/shard_map/ppermute | solution.py:309
  44.9 1.8 %collective-permute-done.15.refs_10_ = bf16[24,1024]{1,0:T(8,128)(2,1)S(1)} collective-permute-done((bf16[24,1024]{1,0:T(8,128)(2,1)S(1)}, bf16[24,1024]{1,0:T(8,128)(2,1)S(1)}, u32[]{:S(2)}, u32[]{:S(2)}) %collective-permute-start.15) | collective-permute-done | bytes 49184 | tf_op jit(solution)/shard_map/ppermute | solution.py:309
  46.7 0.1 collective-permute-start.19
  46.8 0.4 collective-permute-start.18
  47.2 0.7 %collective-permute-done.19.refs_14_ = bf16[24,1024]{1,0:T(8,128)(2,1)S(1)} collective-permute-done((bf16[24,1024]{1,0:T(8,128)(2,1)S(1)}, bf16[24,1024]{1,0:T(8,128)(2,1)S(1)}, u32[]{:S(2)}, u32[]{:S(2)}) %collective-permute-start.19) | collective-permute-done | bytes 49184 | tf_op jit(solution)/shard_map/ppermute | solution.py:312
  47.9 0.2 collective-permute-done.18.refs_13_
  48.1 1.9 %finish.1 = (bf16[24,4096]{1,0:T(8,128)(2,1)}, bf16[24,4096]{1,0:T(8,128)(2,1)}, bf16[24,128]{1,0:T(8,128)(2,1)}, bf16[128,2048]{1,0:T(8,128)(2,1)}) custom-call(bf16[24,4096]{1,0:T(8,128)(2,1)S(1)} %copy-done.2, bf16[24,2048]{1,0:T(8,128)(2,1)S(1)} %collective-permute-done.refs_1_, bf16[24,2048]{1,0:T(8,128)(2,1)S(1)} %collective-permute-done.1.refs_2_, ...), custom_call_target="tpu_custom_call" | custom-call | bytes 6291456 | tf_op jit(solution)/shard_map/finish/pallas_call | solution.py:284
  (42 shorter events, 0.3 us)
Async XLA Ops:
  0.6 9.0 %slice-start = ((s8[6291456]{0:T(1024)(128)(4,1)}), s8[4194304]{0:T(1024)(128)(4,1)S(1)}, s32[]{:S(2)}) async-start(s8[6291456]{0:T(1024)(128)(4,1)} %bitcast.16), calls=%async_computation | async-start | bytes 8388608
  0.6 9.0 %slice-start.2 = ((s8[6291456]{0:T(1024)(128)(4,1)}), s8[4194304]{0:T(1024)(128)(4,1)S(1)}, s32[]{:S(2)}) async-start(s8[6291456]{0:T(1024)(128)(4,1)} %bitcast.22), calls=%async_computation.2 | async-start | bytes 8388608
  1.7 5.7 %collective-permute-start = (bf16[24,2048]{1,0:T(8,128)(2,1)S(1)}, bf16[24,2048]{1,0:T(8,128)(2,1)S(1)}, u32[]{:S(2)}, u32[]{:S(2)}) collective-permute-start(bf16[24,2048]{1,0:T(8,128)(2,1)S(1)} %constant_dynamic-slice_fusion.1), channel_id=1, source_target_pairs={{0,16},{1,17},{16,0},{17,1},{2,18},{3,19},{18,2},{19,3},{4,20},{5,... | collective-permute-start | bytes 294920 | tf_op jit(solution)/shard_map/ppermute | solution.py:309
  4.7 2.8 %copy-start.1 = (bf16[24,4096]{1,0:T(8,128)(2,1)S(1)}, bf16[24,4096]{1,0:T(8,128)(2,1)}, u32[]{:S(2)}) copy-start(bf16[24,4096]{1,0:T(8,128)(2,1)} %refs_3_.1) | copy-start | bytes 589828
  4.7 5.0 %slice-start.1 = ((s8[6291456]{0:T(1024)(128)(4,1)}), s8[2097152]{0:T(1024)(128)(4,1)S(1)}, s32[]{:S(2)}) async-start(s8[6291456]{0:T(1024)(128)(4,1)} %bitcast.16), calls=%async_computation.1 | async-start | bytes 4194304
  4.7 5.0 %slice-start.3 = ((s8[6291456]{0:T(1024)(128)(4,1)}), s8[2097152]{0:T(1024)(128)(4,1)S(1)}, s32[]{:S(2)}) async-start(s8[6291456]{0:T(1024)(128)(4,1)} %bitcast.22), calls=%async_computation.3 | async-start | bytes 4194304
  4.7 5.0 %copy-start.2 = (bf16[24,4096]{1,0:T(8,128)(2,1)S(1)}, bf16[24,4096]{1,0:T(8,128)(2,1)}, u32[]{:S(2)}) copy-start(bf16[24,4096]{1,0:T(8,128)(2,1)} %refs_0_.5) | copy-start | bytes 589828
  4.7 5.0 %copy-start.4 = (f32[4096]{0:T(1024)S(1)}, f32[4096]{0:T(1024)}, u32[]{:S(2)}) copy-start(f32[4096]{0:T(1024)} %param.11) | copy-start | bytes 49156
  5.7 6.6 %collective-permute-start.4 = (f32[24,256]{1,0:T(8,128)S(1)}, f32[24,256]{1,0:T(8,128)S(1)}, u32[]{:S(2)}, u32[]{:S(2)}) collective-permute-start(f32[24,256]{1,0:T(8,128)S(1)} %gates.1.refs_0_.refs_3_.refs_6_), channel_id=1, source_target_pairs={{0,16},{1,17},{16,0},{17,1},{2,18},{3,19},{18,2},{19,3},{4,20},{5,... | collective-permute-start | bytes 73736 | tf_op jit(solution)/shard_map/ppermute | solution.py:309
  7.4 2.2 %collective-permute-start.1 = (bf16[24,2048]{1,0:T(8,128)(2,1)S(1)}, bf16[24,2048]{1,0:T(8,128)(2,1)S(1)}, u32[]{:S(2)}, u32[]{:S(2)}) collective-permute-start(bf16[24,2048]{1,0:T(8,128)(2,1)S(1)} %collective-permute-done.refs_1_), channel_id=1, source_target_pairs={{0,1},{1,0},{2,3},{3,2},{4,5},{5,4},{6,7},{7,6},{8,9},{9,8},{10,11... | collective-permute-start | bytes 294920 | tf_op jit(solution)/shard_map/ppermute | solution.py:312
  7.5 6.0 %collective-permute-start.2 = (bf16[24,2048]{1,0:T(8,128)(2,1)S(1)}, bf16[24,2048]{1,0:T(8,128)(2,1)S(1)}, u32[]{:S(2)}, u32[]{:S(2)}) collective-permute-start(bf16[24,2048]{1,0:T(8,128)(2,1)S(1)} %constant_dynamic-slice_fusion), channel_id=1, source_target_pairs={{0,16},{1,17},{16,0},{17,1},{2,18},{3,19},{18,2},{19,3},{4,20},{5,... | collective-permute-start | bytes 294920 | tf_op jit(solution)/shard_map/ppermute | solution.py:309
  9.7 2.8 %copy-start = (bf16[1,768,4096]{2,1,0:T(8,128)(2,1)S(1)}, bf16[1,768,4096]{2,1,0:T(8,128)(2,1)}, u32[]{:S(2)}) copy-start(bf16[1,768,4096]{2,1,0:T(8,128)(2,1)} %param.16) | copy-start | bytes 18874372
  13.2 3.2 %collective-permute-start.5 = (bf16[2,2,24,1024]{3,2,1,0:T(8,128)(2,1)S(1)}, bf16[2,2,24,1024]{3,2,1,0:T(8,128)(2,1)S(1)}, u32[]{:S(2)}, u32[]{:S(2)}) collective-permute-start(bf16[2,2,24,1024]{3,2,1,0:T(8,128)(2,1)S(1)} %outward_send.1.refs_4_), channel_id=1, source_target_pairs={{0,1},{1,0},{2,3},{3,2},{4,5},{5,4},{6,7},{7,6},{8,9},{9,8},{10,11... | collective-permute-start | bytes 589832 | tf_op jit(solution)/shard_map/ppermute | solution.py:312
  13.5 1.4 %collective-permute-start.3 = (bf16[24,2048]{1,0:T(8,128)(2,1)S(1)}, bf16[24,2048]{1,0:T(8,128)(2,1)S(1)}, u32[]{:S(2)}, u32[]{:S(2)}) collective-permute-start(bf16[24,2048]{1,0:T(8,128)(2,1)S(1)} %collective-permute-done.2.refs_6_.refs_1_.refs_4_), channel_id=1, source_target_pairs={{0,1},{1,0},{2,3},{3,2},{4,5},{5,4},{6,7},{7,6},{8,9},{9,8},{10,11... | collective-permute-start | bytes 294920 | tf_op jit(solution)/shard_map/ppermute | solution.py:312
  16.4 5.0 %collective-permute-start.6 = (bf16[2,24,1024]{2,1,0:T(8,128)(2,1)S(1)}, bf16[2,24,1024]{2,1,0:T(8,128)(2,1)S(1)}, u32[]{:S(2)}, u32[]{:S(2)}) collective-permute-start(bf16[2,24,1024]{2,1,0:T(8,128)(2,1)S(1)} %get-tuple-element.42), channel_id=1, source_target_pairs={{0,17},{1,16},{16,1},{17,0},{2,19},{3,18},{18,3},{19,2},{4,21},{5,... | collective-permute-start | bytes 294920 | tf_op jit(solution)/shard_map/ppermute | solution.py:309
  21.0 2.5 %collective-permute-start.7 = (bf16[2,2,24,1024]{3,2,1,0:T(8,128)(2,1)S(1)}, bf16[2,2,24,1024]{3,2,1,0:T(8,128)(2,1)S(1)}, u32[]{:S(2)}, u32[]{:S(2)}) collective-permute-start(bf16[2,2,24,1024]{3,2,1,0:T(8,128)(2,1)S(1)} %get-tuple-element.35), channel_id=1, source_target_pairs={{0,1},{1,0},{2,3},{3,2},{4,5},{5,4},{6,7},{7,6},{8,9},{9,8},{10,11... | collective-permute-start | bytes 589832 | tf_op jit(solution)/shard_map/ppermute | solution.py:312
  21.4 26.6 %copy-start.3 = (bf16[128,4096]{1,0:T(8,128)(2,1)S(1)}, bf16[128,4096]{1,0:T(8,128)(2,1)}, u32[]{:S(2)}) copy-start(bf16[128,4096]{1,0:T(8,128)(2,1)} %refs_19_.1) | copy-start | bytes 3145732
  23.5 5.4 %collective-permute-start.21 = (bf16[2,24,1024]{2,1,0:T(8,128)(2,1)S(1)}, bf16[2,24,1024]{2,1,0:T(8,128)(2,1)S(1)}, u32[]{:S(2)}, u32[]{:S(2)}) collective-permute-start(bf16[2,24,1024]{2,1,0:T(8,128)(2,1)S(1)} %get-tuple-element.41), channel_id=1, source_target_pairs={{0,3},{1,2},{2,1},{3,0},{4,7},{5,6},{6,5},{7,4},{8,11},{9,10},{10,... | collective-permute-start | bytes 294920 | tf_op jit(solution)/shard_map/ppermute | solution.py:309
  24.8 5.0 %collective-permute-start.8 = (bf16[24,1024]{1,0:T(8,128)(2,1)S(1)}, bf16[24,1024]{1,0:T(8,128)(2,1)S(1)}, u32[]{:S(2)}, u32[]{:S(2)}) collective-permute-start(bf16[24,1024]{1,0:T(8,128)(2,1)S(1)} %get-tuple-element.38), channel_id=1, source_target_pairs={{0,18},{1,19},{2,16},{3,17},{16,2},{17,3},{18,0},{19,1},{4,22},{5,... | collective-permute-start | bytes 147464 | tf_op jit(solution)/shard_map/ppermute | solution.py:309
  26.0 3.9 %collective-permute-start.9 = (bf16[24,1024]{1,0:T(8,128)(2,1)S(1)}, bf16[24,1024]{1,0:T(8,128)(2,1)S(1)}, u32[]{:S(2)}, u32[]{:S(2)}) collective-permute-start(bf16[24,1024]{1,0:T(8,128)(2,1)S(1)} %get-tuple-element.39), channel_id=1, source_target_pairs={{0,17},{1,16},{2,19},{3,18},{16,1},{17,0},{18,3},{19,2},{4,21},{5,... | collective-permute-start | bytes 147464 | tf_op jit(solution)/shard_map/ppermute | solution.py:309
  26.5 4.1 %collective-permute-start.10 = (bf16[24,1024]{1,0:T(8,128)(2,1)S(1)}, bf16[24,1024]{1,0:T(8,128)(2,1)S(1)}, u32[]{:S(2)}, u32[]{:S(2)}) collective-permute-start(bf16[24,1024]{1,0:T(8,128)(2,1)S(1)} %get-tuple-element.40), channel_id=1, source_target_pairs={{0,3},{1,2},{2,1},{3,0},{16,19},{17,18},{18,17},{19,16},{4,7},{5,6... | collective-permute-start | bytes 147464 | tf_op jit(solution)/shard_map/ppermute | solution.py:309
  28.9 5.9 %collective-permute-start.22 = (bf16[2,24,1024]{2,1,0:T(8,128)(2,1)S(1)}, bf16[2,24,1024]{2,1,0:T(8,128)(2,1)S(1)}, u32[]{:S(2)}, u32[]{:S(2)}) collective-permute-start(bf16[2,24,1024]{2,1,0:T(8,128)(2,1)S(1)} %add_convert_fusion.3), channel_id=1, source_target_pairs={{0,5},{1,4},{4,1},{5,0},{8,13},{9,12},{12,9},{13,8},{2,7},{3,6},{6... | collective-permute-start | bytes 294920 | tf_op jit(solution)/shard_map/ppermute | solution.py:309
  30.6 6.5 %collective-permute-start.13 = (bf16[24,1024]{1,0:T(8,128)(2,1)S(1)}, bf16[24,1024]{1,0:T(8,128)(2,1)S(1)}, u32[]{:S(2)}, u32[]{:S(2)}) collective-permute-start(bf16[24,1024]{1,0:T(8,128)(2,1)S(1)} %add_convert_fusion.6), channel_id=1, source_target_pairs={{0,12},{1,13},{4,8},{5,9},{8,4},{9,5},{12,0},{13,1},{2,14},{3,15},... | collective-permute-start | bytes 147464 | tf_op jit(solution)/shard_map/ppermute | solution.py:309
  34.3 5.1 %collective-permute-start.12 = (bf16[24,1024]{1,0:T(8,128)(2,1)S(1)}, bf16[24,1024]{1,0:T(8,128)(2,1)S(1)}, u32[]{:S(2)}, u32[]{:S(2)}) collective-permute-start(bf16[24,1024]{1,0:T(8,128)(2,1)S(1)} %add_convert_fusion.6), channel_id=1, source_target_pairs={{0,9},{1,8},{4,13},{5,12},{8,1},{9,0},{12,5},{13,4},{2,11},{3,10},... | collective-permute-start | bytes 147464 | tf_op jit(solution)/shard_map/ppermute | solution.py:309
  34.3 5.1 %collective-permute-start.11 = (bf16[24,1024]{1,0:T(8,128)(2,1)S(1)}, bf16[24,1024]{1,0:T(8,128)(2,1)S(1)}, u32[]{:S(2)}, u32[]{:S(2)}) collective-permute-start(bf16[24,1024]{1,0:T(8,128)(2,1)S(1)} %add_convert_fusion.6), channel_id=1, source_target_pairs={{0,5},{1,4},{4,1},{5,0},{8,13},{9,12},{12,9},{13,8},{2,7},{3,6},{6... | collective-permute-start | bytes 147464 | tf_op jit(solution)/shard_map/ppermute | solution.py:309
  34.9 8.7 %collective-permute-start.23 = (bf16[2,24,1024]{2,1,0:T(8,128)(2,1)S(1)}, bf16[2,24,1024]{2,1,0:T(8,128)(2,1)S(1)}, u32[]{:S(2)}, u32[]{:S(2)}) collective-permute-start(bf16[2,24,1024]{2,1,0:T(8,128)(2,1)S(1)} %add_convert_fusion.2), channel_id=1, source_target_pairs={{0,9},{1,8},{4,13},{5,12},{8,1},{9,0},{12,5},{13,4},{2,11},{3,10},... | collective-permute-start | bytes 294920 | tf_op jit(solution)/shard_map/ppermute | solution.py:309
  39.5 5.4 %collective-permute-start.16 = (bf16[24,1024]{1,0:T(8,128)(2,1)S(1)}, bf16[24,1024]{1,0:T(8,128)(2,1)S(1)}, u32[]{:S(2)}, u32[]{:S(2)}) collective-permute-start(bf16[24,1024]{1,0:T(8,128)(2,1)S(1)} %add_convert_fusion.5.refs_8_), channel_id=1, source_target_pairs={{0,18},{1,19},{2,16},{3,17},{16,2},{17,3},{18,0},{19,1},{4,22},{5,... | collective-permute-start | bytes 147464 | tf_op jit(solution)/shard_map/ppermute | solution.py:309
  42.6 4.0 %collective-permute-start.15 = (bf16[24,1024]{1,0:T(8,128)(2,1)S(1)}, bf16[24,1024]{1,0:T(8,128)(2,1)S(1)}, u32[]{:S(2)}, u32[]{:S(2)}) collective-permute-start(bf16[24,1024]{1,0:T(8,128)(2,1)S(1)} %add_convert_fusion.5.refs_8_), channel_id=1, source_target_pairs={{0,17},{1,16},{2,19},{3,18},{16,1},{17,0},{18,3},{19,2},{4,21},{5,... | collective-permute-start | bytes 147464 | tf_op jit(solution)/shard_map/ppermute | solution.py:309
  42.9 3.9 %collective-permute-start.14 = (bf16[24,1024]{1,0:T(8,128)(2,1)S(1)}, bf16[24,1024]{1,0:T(8,128)(2,1)S(1)}, u32[]{:S(2)}, u32[]{:S(2)}) collective-permute-start(bf16[24,1024]{1,0:T(8,128)(2,1)S(1)} %add_convert_fusion.5.refs_8_), channel_id=1, source_target_pairs={{0,3},{1,2},{2,1},{3,0},{16,19},{17,18},{18,17},{19,16},{4,7},{5,6... | collective-permute-start | bytes 147464 | tf_op jit(solution)/shard_map/ppermute | solution.py:309
  43.6 4.5 %collective-permute-start.24 = (bf16[2,24,1024]{2,1,0:T(8,128)(2,1)S(1)}, bf16[2,24,1024]{2,1,0:T(8,128)(2,1)S(1)}, u32[]{:S(2)}, u32[]{:S(2)}) collective-permute-start(bf16[2,24,1024]{2,1,0:T(8,128)(2,1)S(1)} %add_convert_fusion.1.refs_16_), channel_id=1, source_target_pairs={{0,1},{1,0},{2,3},{3,2},{4,5},{5,4},{6,7},{7,6},{8,9},{9,8},{10,11... | collective-permute-start | bytes 294920 | tf_op jit(solution)/shard_map/ppermute | solution.py:312
  43.8 3.4 %collective-permute-start.17 = (bf16[24,1024]{1,0:T(8,128)(2,1)S(1)}, bf16[24,1024]{1,0:T(8,128)(2,1)S(1)}, u32[]{:S(2)}, u32[]{:S(2)}) collective-permute-start(bf16[24,1024]{1,0:T(8,128)(2,1)S(1)} %add_convert_fusion.5.refs_8_), channel_id=1, source_target_pairs={{0,1},{1,0},{2,3},{3,2},{4,5},{5,4},{6,7},{7,6},{8,9},{9,8},{10,11... | collective-permute-start | bytes 147464 | tf_op jit(solution)/shard_map/ppermute | solution.py:312
  44.9 2.3 %collective-permute-start.20 = (bf16[24,1024]{1,0:T(8,128)(2,1)S(1)}, bf16[24,1024]{1,0:T(8,128)(2,1)S(1)}, u32[]{:S(2)}, u32[]{:S(2)}) collective-permute-start(bf16[24,1024]{1,0:T(8,128)(2,1)S(1)} %collective-permute-done.16.refs_11_), channel_id=1, source_target_pairs={{0,1},{1,0},{2,3},{3,2},{4,5},{5,4},{6,7},{7,6},{8,9},{9,8},{10,11... | collective-permute-start | bytes 147464 | tf_op jit(solution)/shard_map/ppermute | solution.py:312
  46.7 1.2 %collective-permute-start.19 = (bf16[24,1024]{1,0:T(8,128)(2,1)S(1)}, bf16[24,1024]{1,0:T(8,128)(2,1)S(1)}, u32[]{:S(2)}, u32[]{:S(2)}) collective-permute-start(bf16[24,1024]{1,0:T(8,128)(2,1)S(1)} %collective-permute-done.15.refs_10_), channel_id=1, source_target_pairs={{0,1},{1,0},{2,3},{3,2},{4,5},{5,4},{6,7},{7,6},{8,9},{9,8},{10,11... | collective-permute-start | bytes 147464 | tf_op jit(solution)/shard_map/ppermute | solution.py:312
  46.8 1.3 %collective-permute-start.18 = (bf16[24,1024]{1,0:T(8,128)(2,1)S(1)}, bf16[24,1024]{1,0:T(8,128)(2,1)S(1)}, u32[]{:S(2)}, u32[]{:S(2)}) collective-permute-start(bf16[24,1024]{1,0:T(8,128)(2,1)S(1)} %collective-permute-done.14.refs_9_), channel_id=1, source_target_pairs={{0,1},{1,0},{2,3},{3,2},{4,5},{5,4},{6,7},{7,6},{8,9},{9,8},{10,11... | collective-permute-start | bytes 147464 | tf_op jit(solution)/shard_map/ppermute | solution.py:312

commit v12 on v11

--- a/solution.py
+++ b/solution.py
@@ -12,6 +12,7 @@
 BF16 = jnp.bfloat16
 STEP = 256
 LANES = 128
+TERMS = 3
 LOAD_PIECES = 8
 FEW_ROWS = 64
 VMEM_LIMIT = 12 * 1024 * 1024
@@ -43,6 +44,10 @@
     return ((lax.axis_index("y") ^ j) * 2 + (own_half() ^ i)) * width
 
 
+def folded(value):
+    return sum(value[:, start : start + LANES] for start in range(0, value.shape[1], LANES))
+
+
 def both_halves(refs, width, body):
     core, half = lax.axis_index("c"), width // 2
     size = 512 if len(refs[0]) <= 3 else 128
@@ -64,25 +69,41 @@
         out_ref[k, j, :, columns] = value[k * rows : (k + 1) * rows].astype(BF16)
 
 
-def gates_kernel(n_dp, named, weights, context, w_gate, w_up, w_down, small, *held):
-    targets, sems = held[:3], held[3]
-    copies = [
-        pltpu.make_async_copy(source, target, sems.at[n])
-        for n, (source, target) in enumerate(zip((named, weights, context), targets))
+def cut_kernel(n_dp, source, target, sem):
+    width = target.shape[1]
+    columns = pl.ds(pl.multiple_of(lax.axis_index("c") * width, width), width)
+    copy = pltpu.make_async_copy(source.at[:, columns], target, sem)
+    copy.start()
+    copy.wait()
+
+
+def gates_kernel(n_dp, named, weights, context, grads, w_gate, w_up, w_down, packed, named_held, weights_held, sems):
+    width, heads = grads.shape[1] // 2, context.shape[1]
+    columns = pl.ds(pl.multiple_of(lax.axis_index("c") * width, width), width)
+    pairs = [
+        (named, named_held), (weights, weights_held), (context, packed.at[:, pl.ds(width, heads)]),
+        (grads.at[:, columns], packed.at[:, pl.ds(0, width)]),
     ]
+    copies = [pltpu.make_async_copy(*pair, sems.at[n]) for n, pair in enumerate(pairs)]
     for copy in copies:
         copy.start()
-    for copy in copies:
-        copy.wait()
-    named_held, weights_held, context_held = targets
-    rows, heads = context_held.shape
+    copies[0].wait()
+    copies[1].wait()
+    rows = context.shape[0]
     expert = (lax.axis_index("hi") * 2 + lax.axis_index("y")) * 2 + lax.axis_index("c")
     row = jnp.sum(jnp.where(named_held[...] == expert, weights_held[...], 0.0), axis=0, keepdims=True)
     square = (rows, rows)
     diagonal = lax.broadcasted_iota(jnp.int32, square, 0) == lax.broadcasted_iota(jnp.int32, square, 1)
     gate = jnp.sum(jnp.where(diagonal, row, 0.0), axis=1, keepdims=True)
-    small[:, :heads] = context_held[...].astype(F32)
-    small[:, heads:] = jnp.broadcast_to(gate, (rows, LANES))
+    lane = lax.broadcasted_iota(jnp.int32, (rows, LANES), 1)
+    rest, block = jnp.broadcast_to(gate, (rows, LANES)), jnp.zeros((rows, LANES), F32)
+    for term in range(TERMS):
+        rounded = rest.astype(BF16).astype(F32)
+        block = jnp.where(lane == term, rounded, block)
+        rest = rest - rounded
+    packed[:, width + heads :] = block.astype(BF16)
+    copies[2].wait()
+    copies[3].wait()
 
 
 def unit_step(units):
@@ -101,8 +122,11 @@
         lax.fori_loop(0, count, carried, 0)
 
 
-def gates_of(smalls):
-    return jnp.concatenate([small[:, small.shape[1] - LANES : small.shape[1] - LANES + 1] for small in smalls], axis=0)
+def gates_of(packs):
+    first = packs[0].shape[1] - LANES
+    blocks = [pack[:, first : first + LANES].astype(F32) for pack in packs]
+    gates = jnp.concatenate(blocks, axis=0)
+    return gates[:, 0:1] + gates[:, 1:2] + gates[:, 2:3]
 
 
 def hidden_kernel(n_dp, *refs):
@@ -110,13 +134,13 @@
     gain, w_gate, w_up, pre_gate, pre_up, act, normed = refs[2 * n_dp - 1 :]
     total, width = hid[0].shape[0] * n_dp, hid[0].shape[1]
     few = total <= FEW_ROWS
-    sums = [jnp.zeros((total, 1), F32)]
+    sums = [0.0]
 
     def square(columns, value):
-        sums[0] = sums[0] + jnp.sum(value * value, axis=1, keepdims=True)
+        sums[0] = sums[0] + folded(value * value)
 
     both_halves([hid], width, square)
-    scale = lax.rsqrt(sums[0] / width + EPSILON)
+    scale = lax.rsqrt(jnp.sum(sums[0], axis=1, keepdims=True) / width + EPSILON)
 
     def norm(columns, value):
         normed[:, columns] = (value * scale * gain[:, columns]).astype(BF16)
@@ -241,15 +265,15 @@
     copies[0].start()
 
     few = rows * n_dp <= FEW_ROWS
-    sums = [jnp.zeros((rows * n_dp, 1), F32)] * 2
+    sums = [0.0, 0.0]
 
     def products(columns, value):
-        sums[0] = sums[0] + jnp.sum(value * value, axis=1, keepdims=True)
-        sums[1] = sums[1] + jnp.sum(value * summed[:, columns], axis=1, keepdims=True)
+        sums[0] = sums[0] + folded(value * value)
+        sums[1] = sums[1] + folded(value * summed[:, columns])
 
     both_halves([hid], width, products)
-    scale = lax.rsqrt(sums[0] / width + EPSILON)
-    centre = scale * sums[1] / width
+    scale = lax.rsqrt(jnp.sum(sums[0], axis=1, keepdims=True) / width + EPSILON)
+    centre = scale * jnp.sum(sums[1], axis=1, keepdims=True) / width
 
     def total(columns, value, grad):
         result = grad + scale * (summed[:, columns] - value * scale * centre)
@@ -262,7 +286,8 @@
     part = width // n_dp
     copies[2].start()
     heads = d_context.shape[1]
-    turned = jnp.concatenate([small[:, :heads] for small in smalls], axis=0).T.astype(BF16)
+    lanes = slice(width // 2, width // 2 + heads)
+    turned = jnp.concatenate([small[:, lanes].astype(F32) for small in smalls], axis=0).T.astype(BF16)
     step_width = min(part, 512)
 
     def product(step):
@@ -311,24 +336,27 @@
     def other_core(value):
         return lax.ppermute(value, ("c",), [(0, 1), (1, 0)])
 
-    def all_blocks(value):
-        half = lax.dynamic_slice_in_dim(value, lax.axis_index("c") * (width // 2), width // 2, 1)
-        here = [swap(half, ("dp",), k, False) for k in range(1, n_dp)]
-        return [value] + [piece for one in here for piece in (one, other_core(one))]
-
     weights = 2 * width * units
     shares = ((n_dp, 2, rows, chunk), BF16)
     wg, wu, wd, gain = w_gate[0], w_up[0], w_down[0], norm_gain.reshape(1, width)
-    (small_own,) = run(
-        gates_kernel, n_dp, [route_ids.T, route_gates.T, context, wg, wu, wd],
-        [((rows, heads + LANES), F32)],
-        [pltpu.VMEM((top, rows), jnp.int32), pltpu.VMEM((top, rows), F32), pltpu.VMEM((rows, heads), BF16),
-         pltpu.SemaphoreType.DMA((3,))],
-        4 * weights, "gates", far=range(6),
-    )
-    hid = all_blocks(hidden_in)
-    smalls = [small_own] + [swap(small_own, ("dp",), k, False) for k in range(1, n_dp)]
-    grads = all_blocks(grad_out)
+    half = width // 2
+    (hid_half,) = run(
+        cut_kernel, n_dp, [hidden_in], [((rows, half), BF16)], [pltpu.SemaphoreType.DMA], rows * width, "cut", far=(0,)
+    )
+    (packed,) = run(
+        gates_kernel, n_dp, [route_ids.T, route_gates.T, context, grad_out, wg, wu, wd],
+        [((rows, half + heads + LANES), BF16)],
+        [pltpu.VMEM((top, rows), jnp.int32), pltpu.VMEM((top, rows), F32), pltpu.SemaphoreType.DMA((4,))],
+        4 * weights, "gates", far=range(7),
+    )
+
+    def others(value):
+        here = [swap(value, ("dp",), k, False) for k in range(1, n_dp)]
+        return here, [piece for one in here for piece in (one, other_core(one))]
+
+    hid = [hidden_in] + others(hid_half)[1]
+    packs, blocks = others(packed)
+    smalls, grads = [packed] + packs, [grad_out] + blocks
 
     def add(one, other):
         return (one.astype(F32) + other.astype(F32)).astype(BF16)
@@ -350,7 +378,7 @@
     )
     out_other = other_core(out_send)
     (out_keep,) = run(
-        functools.partial(outward_kernel, 0), n_dp, smalls + [act, wd, out_send] + grads, [shares], [],
+        functools.partial(outward_kernel, 0), n_dp, smalls + [act, wd, out_send], [shares], [],
         weights // 2, "outward_keep",
     )
     size = unit_step(units)

time: 50.1 us -> 49.4 us (0.986)
  Pallas kernels: 13 us -> 14.3 us
  starting transfers between devices: 24.1 us -> 23 us
  local copies, waits for them, and re-layouts: 1.32 us -> 0.27 us
    pallas_call x10 -> x11, Pallas kernels: 13 us -> 14.3 us  [run(): pl.pallas_call(functools.partial(kernel, n_dp), out_shape=kinds, in_specs...]
    ppermute x16 -> x15, starting transfers between devices: 22 us -> 20.9 us  [swap(): lax.ppermute(value, axes + ('c',), [(i, i ^ turn) for i in range(count)])]
    dynamic_slice x2 -> x0, local copies, waits for them, and re-layouts: 1.07 us -> none  [all_blocks(): lax.dynamic_slice_in_dim(value, lax.axis_index('c') * (width // 2), width...]
    ppermute x9, waiting for transfers between devices: 1.96 us -> 2.59 us  [other_core(): return lax.ppermute(value, ('c',), [(0, 1), (1, 0)])]
    ppermute x16 -> x15, waiting for transfers between devices: 8.38 us -> 8.06 us  [swap(): lax.ppermute(value, axes + ('c',), [(i, i ^ turn) for i in range(count)])]
  transfers between devices with their start and end apart: 25 -> 24, of which waited for: 12 -> 13; matrix products, arithmetic and copies ran while one was open for 0% -> 0% of each run, Pallas kernels for 22% -> 22%
where the time goes in v12:
time: 49.4 us; the launch traced here: 49.3 us
  starting transfers between devices  23 us (47%)
  Pallas kernels  14.3 us (29%)
  waiting for transfers between devices  10.7 us (22%)
  between operations  0.87 us (2%)
    ppermute x15, starting transfers between devices, swap(): lax.ppermute(value, axes + ('c',), [(i, i ^ turn) for i in range(count)])  20.9 us
    pallas_call x11, Pallas kernels, run(): pl.pallas_call(functools.partial(kernel, n_dp), out_shape=kinds, in_specs...  14.3 us
    ppermute x15, waiting for transfers between devices, swap(): lax.ppermute(value, axes + ('c',), [(i, i ^ turn) for i in range(count)])  8.06 us
    ppermute x9, waiting for transfers between devices, other_core(): return lax.ppermute(value, ('c',), [(0, 1), (1, 0)])  2.59 us
    ppermute x9, starting transfers between devices, other_core(): return lax.ppermute(value, ('c',), [(0, 1), (1, 0)])  2.01 us
  transfers between devices with their start and end apart: 24, of which 13 were waited for; matrix products, arithmetic and copies ran while one was open for 0% of the time, Pallas kernels for 22%

profile of v12, /device:TPU:0, one launch (start us, length us, event | category | flops | bytes accessed | tf_op | source)
XLA Modules:
  0.0 49.3 jit_solution(6950613277841419123)
XLA Ops:
  0.7 1.1 %cut.1 = bf16[24,2048]{1,0:T(8,128)(2,1)S(1)} custom-call(bf16[24,4096]{1,0:T(8,128)(2,1)} %refs_0_.5), custom_call_target="tpu_custom_call" | custom-call | bytes 98304 | tf_op jit(solution)/shard_map/cut/pallas_call | solution.py:309
  1.7 3.0 %collective-permute-start = (bf16[24,2048]{1,0:T(8,128)(2,1)S(1)}, bf16[24,2048]{1,0:T(8,128)(2,1)S(1)}, u32[]{:S(2)}, u32[]{:S(2)}) collective-permute-start(bf16[24,2048]{1,0:T(8,128)(2,1)S(1)} %cut.1), channel_id=1, source_target_pairs={{0,16},{1,17},{16,0},{17,1},{2,18},{3,19},{18,2},{19,3},{4,20},{5,... | collective-permute-start | bytes 294920 | tf_op jit(solution)/shard_map/ppermute | solution.py:334
  4.7 1.1 %gates.1.refs_0_.refs_3_.refs_6_ = bf16[24,2304]{1,0:T(8,128)(2,1)S(1)} custom-call(s32[8,24]{1,0:T(8,128)} %bitcast.29, f32[8,24]{1,0:T(8,128)} %bitcast.30, bf16[24,128]{1,0:T(8,128)(2,1)} %context.1, bf16[24,4096]{1,0:T(8,128)(2,1)} %refs_3_.1, bf16[4096,768]{1,0:T(8,128)(2,1)} %bitcast.15, bf16[4096,768]{1,0:T(8,128)(2,1)} %bitcast.21, ...), custom_call_target="tpu_custom_call" | custom-call | bytes 25165824 | tf_op jit(solution)/shard_map/gates/pallas_call | solution.py:309
  5.9 0.6 %collective-permute-start.2 = (bf16[24,2304]{1,0:T(8,128)(2,1)S(1)}, bf16[24,2304]{1,0:T(8,128)(2,1)S(1)}, u32[]{:S(2)}, u32[]{:S(2)}) collective-permute-start(bf16[24,2304]{1,0:T(8,128)(2,1)S(1)} %gates.1.refs_0_.refs_3_.refs_6_), channel_id=1, source_target_pairs={{0,16},{1,17},{16,0},{17,1},{2,18},{3,19},{18,2},{19,3},{4,20},{5,... | collective-permute-start | bytes 331784 | tf_op jit(solution)/shard_map/ppermute | solution.py:334
  6.4 1.1 %collective-permute-done.refs_1_ = bf16[24,2048]{1,0:T(8,128)(2,1)S(1)} collective-permute-done((bf16[24,2048]{1,0:T(8,128)(2,1)S(1)}, bf16[24,2048]{1,0:T(8,128)(2,1)S(1)}, u32[]{:S(2)}, u32[]{:S(2)}) %collective-permute-start) | collective-permute-done | bytes 98336 | tf_op jit(solution)/shard_map/ppermute | solution.py:334
  7.5 1.3 %collective-permute-done.1.refs_2_ = bf16[24,2048]{1,0:T(8,128)(2,1)S(1)} collective-permute-done((bf16[24,2048]{1,0:T(8,128)(2,1)S(1)}, bf16[24,2048]{1,0:T(8,128)(2,1)S(1)}, u32[]{:S(2)}, u32[]{:S(2)}) %collective-permute-start.1) | collective-permute-done | bytes 98336 | tf_op jit(solution)/shard_map/ppermute | solution.py:337
  8.9 2.5 %hidden.1 = (f32[48,768]{1,0:T(8,128)S(1)}, f32[48,768]{1,0:T(8,128)S(1)}, bf16[48,768]{1,0:T(8,128)(2,1)S(1)}) custom-call(bf16[24,4096]{1,0:T(8,128)(2,1)S(1)} %copy-done.2, bf16[24,2048]{1,0:T(8,128)(2,1)S(1)} %collective-permute-done.refs_1_, bf16[24,2048]{1,0:T(8,128)(2,1)S(1)} %collective-permute-done.1.refs_2_, f32[1,4096]{1,0:T(1,128)S(1)} %bitcast.27, ...), custom_call_target="tpu_custom_call" | custom-call | bytes 12582912 | tf_op jit(solution)/shard_map/hidden/pallas_call | solution.py:309
  11.5 0.2 copy-done
  11.7 0.7 %outward_send.1.refs_4_ = bf16[2,2,24,1024]{3,2,1,0:T(8,128)(2,1)S(1)} custom-call(bf16[24,2304]{1,0:T(8,128)(2,1)S(1)} %gates.1.refs_0_.refs_3_.refs_6_, bf16[24,2304]{1,0:T(8,128)(2,1)S(1)} %collective-permute-done.2.refs_1_.refs_4_.refs_7_, bf16[48,768]{1,0:T(8,128)(2,1)S(1)} %get-tuple-element.25.refs_2_, bf16[768,4096]{1,0:T(8,128)(2,1)S(1)} %bitcast.11), custom_call_target="tpu_custom_call" | custom-call | bytes 3145728 | tf_op jit(solution)/shard_map/outward_send/pallas_call | solution.py:309
  12.4 0.2 collective-permute-start.4
  12.6 0.4 collective-permute-start.3
  12.9 0.7 %outward_keep.1.refs_8_ = bf16[2,2,24,1024]{3,2,1,0:T(8,128)(2,1)S(1)} custom-call(bf16[24,2304]{1,0:T(8,128)(2,1)S(1)} %gates.1.refs_0_.refs_3_.refs_6_, bf16[24,2304]{1,0:T(8,128)(2,1)S(1)} %collective-permute-done.2.refs_1_.refs_4_.refs_7_, bf16[48,768]{1,0:T(8,128)(2,1)S(1)} %get-tuple-element.25.refs_2_, bf16[768,4096]{1,0:T(8,128)(2,1)S(1)} %bitcast.12, ...), custom_call_target="tpu_custom_call" | custom-call | bytes 3145728 | tf_op jit(solution)/shard_map/outward_keep/pallas_call | solution.py:309
  13.6 0.4 collective-permute-done.3.refs_2_.refs_5_
  14.0 0.9 %backward_first.1 = (bf16[48,256]{1,0:T(8,128)(2,1)S(1)}, bf16[48,256]{1,0:T(8,128)(2,1)S(1)}, bf16[48,4096]{1,0:T(8,128)(2,1)S(1)}, bf16[2,2,24,1024]{3,2,1,0:T(8,128)(2,1)S(1)}) custom-call(bf16[24,4096]{1,0:T(8,128)(2,1)S(1)} %copy-done.1, bf16[24,2304]{1,0:T(8,128)(2,1)S(1)} %collective-permute-done.2.refs_1_.refs_4_.refs_7_, ...), custom_call_target="tpu_custom_call" | custom-call | bytes 2097152 | tf_op jit(solution)/shard_map/backward_first/pallas_call | solution.py:309
  14.9 0.1 add_convert_fusion
  15.0 2.3 %collective-permute-start.5 = (bf16[2,24,1024]{2,1,0:T(8,128)(2,1)S(1)}, bf16[2,24,1024]{2,1,0:T(8,128)(2,1)S(1)}, u32[]{:S(2)}, u32[]{:S(2)}) collective-permute-start(bf16[2,24,1024]{2,1,0:T(8,128)(2,1)S(1)} %get-tuple-element.42), channel_id=1, source_target_pairs={{0,17},{1,16},{16,1},{17,0},{2,19},{3,18},{18,3},{19,2},{4,21},{5,... | collective-permute-start | bytes 294920 | tf_op jit(solution)/shard_map/ppermute | solution.py:334
  17.3 1.4 %backward_rest.1 = (bf16[48,512]{1,0:T(8,128)(2,1)S(1)}, bf16[48,512]{1,0:T(8,128)(2,1)S(1)}, bf16[2,24,1024]{2,1,0:T(8,128)(2,1)S(1)}) custom-call(bf16[48,4096]{1,0:T(8,128)(2,1)S(1)} %get-tuple-element.28.weighted, f32[48,768]{1,0:T(8,128)S(1)} %get-tuple-element.23.refs_5_.pre_gate, f32[48,768]{1,0:T(8,128)S(1)} %get-tuple-element.24.refs_6_.pre_up, ...), custom_call_target="tpu_custom_call" | custom-call | bytes 4194304 | tf_op jit(solution)/shard_map/backward_rest/pallas_call | solution.py:309
  18.7 2.0 %inward_send.1 = (bf16[2,2,24,1024]{3,2,1,0:T(8,128)(2,1)S(1)}, bf16[2,24,1024]{2,1,0:T(8,128)(2,1)S(1)}) custom-call(bf16[48,256]{1,0:T(8,128)(2,1)S(1)} %get-tuple-element.26.refs_0_, bf16[48,256]{1,0:T(8,128)(2,1)S(1)} %get-tuple-element.27.refs_1_, bf16[48,512]{1,0:T(8,128)(2,1)S(1)} %get-tuple-element.30.refs_2_, ...), custom_call_target="tpu_custom_call" | custom-call | bytes 6291456 | tf_op jit(solution)/shard_map/inward_send/pallas_call | solution.py:309
  20.7 0.3 collective-permute-start.6
  21.1 2.0 %inward_keep.1 = (bf16[2,2,24,1024]{3,2,1,0:T(8,128)(2,1)S(1)}, bf16[2,24,1024]{2,1,0:T(8,128)(2,1)S(1)}) custom-call(bf16[48,256]{1,0:T(8,128)(2,1)S(1)} %get-tuple-element.26.refs_0_, bf16[48,256]{1,0:T(8,128)(2,1)S(1)} %get-tuple-element.27.refs_1_, bf16[48,512]{1,0:T(8,128)(2,1)S(1)} %get-tuple-element.30.refs_2_, ...), custom_call_target="tpu_custom_call" | custom-call | bytes 6291456 | tf_op jit(solution)/shard_map/inward_keep/pallas_call | solution.py:309
  23.1 0.1 join.1
  23.1 1.1 %collective-permute-start.20 = (bf16[2,24,1024]{2,1,0:T(8,128)(2,1)S(1)}, bf16[2,24,1024]{2,1,0:T(8,128)(2,1)S(1)}, u32[]{:S(2)}, u32[]{:S(2)}) collective-permute-start(bf16[2,24,1024]{2,1,0:T(8,128)(2,1)S(1)} %get-tuple-element.41), channel_id=1, source_target_pairs={{0,3},{1,2},{2,1},{3,0},{4,7},{5,6},{6,5},{7,4},{8,11},{9,10},{10,... | collective-permute-start | bytes 294920 | tf_op jit(solution)/shard_map/ppermute | solution.py:334
  24.2 1.4 %collective-permute-start.7 = (bf16[24,1024]{1,0:T(8,128)(2,1)S(1)}, bf16[24,1024]{1,0:T(8,128)(2,1)S(1)}, u32[]{:S(2)}, u32[]{:S(2)}) collective-permute-start(bf16[24,1024]{1,0:T(8,128)(2,1)S(1)} %get-tuple-element.38), channel_id=1, source_target_pairs={{0,18},{1,19},{2,16},{3,17},{16,2},{17,3},{18,0},{19,1},{4,22},{5,... | collective-permute-start | bytes 147464 | tf_op jit(solution)/shard_map/ppermute | solution.py:334
  25.6 0.5 %collective-permute-start.8 = (bf16[24,1024]{1,0:T(8,128)(2,1)S(1)}, bf16[24,1024]{1,0:T(8,128)(2,1)S(1)}, u32[]{:S(2)}, u32[]{:S(2)}) collective-permute-start(bf16[24,1024]{1,0:T(8,128)(2,1)S(1)} %get-tuple-element.39), channel_id=1, source_target_pairs={{0,17},{1,16},{2,19},{3,18},{16,1},{17,0},{18,3},{19,2},{4,21},{5,... | collective-permute-start | bytes 147464 | tf_op jit(solution)/shard_map/ppermute | solution.py:334
  26.1 1.3 %collective-permute-start.9 = (bf16[24,1024]{1,0:T(8,128)(2,1)S(1)}, bf16[24,1024]{1,0:T(8,128)(2,1)S(1)}, u32[]{:S(2)}, u32[]{:S(2)}) collective-permute-start(bf16[24,1024]{1,0:T(8,128)(2,1)S(1)} %get-tuple-element.40), channel_id=1, source_target_pairs={{0,3},{1,2},{2,1},{3,0},{16,19},{17,18},{18,17},{19,16},{4,7},{5,6... | collective-permute-start | bytes 147464 | tf_op jit(solution)/shard_map/ppermute | solution.py:334
  27.4 0.7 %collective-permute-done.20 = bf16[2,24,1024]{2,1,0:T(8,128)(2,1)S(1)} collective-permute-done((bf16[2,24,1024]{2,1,0:T(8,128)(2,1)S(1)}, bf16[2,24,1024]{2,1,0:T(8,128)(2,1)S(1)}, u32[]{:S(2)}, u32[]{:S(2)}) %collective-permute-start.20) | collective-permute-done | bytes 98336 | tf_op jit(solution)/shard_map/ppermute | solution.py:334
  28.1 0.9 %collective-permute-start.21 = (bf16[2,24,1024]{2,1,0:T(8,128)(2,1)S(1)}, bf16[2,24,1024]{2,1,0:T(8,128)(2,1)S(1)}, u32[]{:S(2)}, u32[]{:S(2)}) collective-permute-start(bf16[2,24,1024]{2,1,0:T(8,128)(2,1)S(1)} %add_convert_fusion.3), channel_id=1, source_target_pairs={{0,5},{1,4},{4,1},{5,0},{8,13},{9,12},{12,9},{13,8},{2,7},{3,6},{6... | collective-permute-start | bytes 294920 | tf_op jit(solution)/shard_map/ppermute | solution.py:334
  29.1 0.2 collective-permute-done.7
  29.3 0.1 collective-permute-done.8
  29.4 0.6 %collective-permute-done.9 = bf16[24,1024]{1,0:T(8,128)(2,1)S(1)} collective-permute-done((bf16[24,1024]{1,0:T(8,128)(2,1)S(1)}, bf16[24,1024]{1,0:T(8,128)(2,1)S(1)}, u32[]{:S(2)}, u32[]{:S(2)}) %collective-permute-start.9) | collective-permute-done | bytes 49184 | tf_op jit(solution)/shard_map/ppermute | solution.py:334
  30.0 3.7 %collective-permute-start.12 = (bf16[24,1024]{1,0:T(8,128)(2,1)S(1)}, bf16[24,1024]{1,0:T(8,128)(2,1)S(1)}, u32[]{:S(2)}, u32[]{:S(2)}) collective-permute-start(bf16[24,1024]{1,0:T(8,128)(2,1)S(1)} %add_convert_fusion.6), channel_id=1, source_target_pairs={{0,12},{1,13},{4,8},{5,9},{8,4},{9,5},{12,0},{13,1},{2,14},{3,15},... | collective-permute-start | bytes 147464 | tf_op jit(solution)/shard_map/ppermute | solution.py:334
  33.7 0.5 %collective-permute-start.10 = (bf16[24,1024]{1,0:T(8,128)(2,1)S(1)}, bf16[24,1024]{1,0:T(8,128)(2,1)S(1)}, u32[]{:S(2)}, u32[]{:S(2)}) collective-permute-start(bf16[24,1024]{1,0:T(8,128)(2,1)S(1)} %add_convert_fusion.6), channel_id=1, source_target_pairs={{0,5},{1,4},{4,1},{5,0},{8,13},{9,12},{12,9},{13,8},{2,7},{3,6},{6... | collective-permute-start | bytes 147464 | tf_op jit(solution)/shard_map/ppermute | solution.py:334
  34.2 2.2 %collective-permute-start.22 = (bf16[2,24,1024]{2,1,0:T(8,128)(2,1)S(1)}, bf16[2,24,1024]{2,1,0:T(8,128)(2,1)S(1)}, u32[]{:S(2)}, u32[]{:S(2)}) collective-permute-start(bf16[2,24,1024]{2,1,0:T(8,128)(2,1)S(1)} %add_convert_fusion.2), channel_id=1, source_target_pairs={{0,9},{1,8},{4,13},{5,12},{8,1},{9,0},{12,5},{13,4},{2,11},{3,10},... | collective-permute-start | bytes 294920 | tf_op jit(solution)/shard_map/ppermute | solution.py:334
  36.4 0.0 collective-permute-done.12
  36.5 2.3 %collective-permute-done.11 = bf16[24,1024]{1,0:T(8,128)(2,1)S(1)} collective-permute-done((bf16[24,1024]{1,0:T(8,128)(2,1)S(1)}, bf16[24,1024]{1,0:T(8,128)(2,1)S(1)}, u32[]{:S(2)}, u32[]{:S(2)}) %collective-permute-start.11) | collective-permute-done | bytes 49184 | tf_op jit(solution)/shard_map/ppermute | solution.py:334
  38.8 3.1 %collective-permute-start.15 = (bf16[24,1024]{1,0:T(8,128)(2,1)S(1)}, bf16[24,1024]{1,0:T(8,128)(2,1)S(1)}, u32[]{:S(2)}, u32[]{:S(2)}) collective-permute-start(bf16[24,1024]{1,0:T(8,128)(2,1)S(1)} %add_convert_fusion.5.refs_8_), channel_id=1, source_target_pairs={{0,18},{1,19},{2,16},{3,17},{16,2},{17,3},{18,0},{19,1},{4,22},{5,... | collective-permute-start | bytes 147464 | tf_op jit(solution)/shard_map/ppermute | solution.py:334
  41.9 0.2 collective-permute-start.14
  42.1 0.2 collective-permute-start.13
  42.3 0.6 %collective-permute-done.22 = bf16[2,24,1024]{2,1,0:T(8,128)(2,1)S(1)} collective-permute-done((bf16[2,24,1024]{2,1,0:T(8,128)(2,1)S(1)}, bf16[2,24,1024]{2,1,0:T(8,128)(2,1)S(1)}, u32[]{:S(2)}, u32[]{:S(2)}) %collective-permute-start.22) | collective-permute-done | bytes 98336 | tf_op jit(solution)/shard_map/ppermute | solution.py:334
  43.0 0.2 collective-permute-start.23
  43.1 0.4 collective-permute-start.16
  43.5 0.7 %collective-permute-done.15.refs_11_ = bf16[24,1024]{1,0:T(8,128)(2,1)S(1)} collective-permute-done((bf16[24,1024]{1,0:T(8,128)(2,1)S(1)}, bf16[24,1024]{1,0:T(8,128)(2,1)S(1)}, u32[]{:S(2)}, u32[]{:S(2)}) %collective-permute-start.15) | collective-permute-done | bytes 49184 | tf_op jit(solution)/shard_map/ppermute | solution.py:334
  44.2 1.8 %collective-permute-done.14.refs_10_ = bf16[24,1024]{1,0:T(8,128)(2,1)S(1)} collective-permute-done((bf16[24,1024]{1,0:T(8,128)(2,1)S(1)}, bf16[24,1024]{1,0:T(8,128)(2,1)S(1)}, u32[]{:S(2)}, u32[]{:S(2)}) %collective-permute-start.14) | collective-permute-done | bytes 49184 | tf_op jit(solution)/shard_map/ppermute | solution.py:334
  46.0 0.1 collective-permute-start.18
  46.1 0.4 collective-permute-start.17
  46.5 0.7 %collective-permute-done.18.refs_14_ = bf16[24,1024]{1,0:T(8,128)(2,1)S(1)} collective-permute-done((bf16[24,1024]{1,0:T(8,128)(2,1)S(1)}, bf16[24,1024]{1,0:T(8,128)(2,1)S(1)}, u32[]{:S(2)}, u32[]{:S(2)}) %collective-permute-start.18) | collective-permute-done | bytes 49184 | tf_op jit(solution)/shard_map/ppermute | solution.py:337
  47.2 0.2 collective-permute-done.17.refs_13_
  47.4 1.9 %finish.1 = (bf16[24,4096]{1,0:T(8,128)(2,1)}, bf16[24,4096]{1,0:T(8,128)(2,1)}, bf16[24,128]{1,0:T(8,128)(2,1)}, bf16[128,2048]{1,0:T(8,128)(2,1)}) custom-call(bf16[24,4096]{1,0:T(8,128)(2,1)S(1)} %copy-done.2, bf16[24,2048]{1,0:T(8,128)(2,1)S(1)} %collective-permute-done.refs_1_, bf16[24,2048]{1,0:T(8,128)(2,1)S(1)} %collective-permute-done.1.refs_2_, ...), custom_call_target="tpu_custom_call" | custom-call | bytes 6291456 | tf_op jit(solution)/shard_map/finish/pallas_call | solution.py:309
  (39 shorter events, 0.3 us)
Async XLA Ops:
  0.6 8.2 %slice-start = ((s8[6291456]{0:T(1024)(128)(4,1)}), s8[4194304]{0:T(1024)(128)(4,1)S(1)}, s32[]{:S(2)}) async-start(s8[6291456]{0:T(1024)(128)(4,1)} %bitcast.16), calls=%async_computation | async-start | bytes 8388608
  0.6 8.2 %slice-start.2 = ((s8[6291456]{0:T(1024)(128)(4,1)}), s8[4194304]{0:T(1024)(128)(4,1)S(1)}, s32[]{:S(2)}) async-start(s8[6291456]{0:T(1024)(128)(4,1)} %bitcast.22), calls=%async_computation.2 | async-start | bytes 8388608
  1.7 5.8 %collective-permute-start = (bf16[24,2048]{1,0:T(8,128)(2,1)S(1)}, bf16[24,2048]{1,0:T(8,128)(2,1)S(1)}, u32[]{:S(2)}, u32[]{:S(2)}) collective-permute-start(bf16[24,2048]{1,0:T(8,128)(2,1)S(1)} %cut.1), channel_id=1, source_target_pairs={{0,16},{1,17},{16,0},{17,1},{2,18},{3,19},{18,2},{19,3},{4,20},{5,... | collective-permute-start | bytes 294920 | tf_op jit(solution)/shard_map/ppermute | solution.py:334
  4.7 4.1 %slice-start.1 = ((s8[6291456]{0:T(1024)(128)(4,1)}), s8[2097152]{0:T(1024)(128)(4,1)S(1)}, s32[]{:S(2)}) async-start(s8[6291456]{0:T(1024)(128)(4,1)} %bitcast.16), calls=%async_computation.1 | async-start | bytes 4194304
  4.7 4.1 %slice-start.3 = ((s8[6291456]{0:T(1024)(128)(4,1)}), s8[2097152]{0:T(1024)(128)(4,1)S(1)}, s32[]{:S(2)}) async-start(s8[6291456]{0:T(1024)(128)(4,1)} %bitcast.22), calls=%async_computation.3 | async-start | bytes 4194304
  4.7 4.1 %copy-start.2 = (bf16[24,4096]{1,0:T(8,128)(2,1)S(1)}, bf16[24,4096]{1,0:T(8,128)(2,1)}, u32[]{:S(2)}) copy-start(bf16[24,4096]{1,0:T(8,128)(2,1)} %refs_0_.5) | copy-start | bytes 589828
  4.7 4.1 %copy-start.4 = (f32[4096]{0:T(1024)S(1)}, f32[4096]{0:T(1024)}, u32[]{:S(2)}) copy-start(f32[4096]{0:T(1024)} %param.11) | copy-start | bytes 49156
  5.9 5.6 %collective-permute-start.2 = (bf16[24,2304]{1,0:T(8,128)(2,1)S(1)}, bf16[24,2304]{1,0:T(8,128)(2,1)S(1)}, u32[]{:S(2)}, u32[]{:S(2)}) collective-permute-start(bf16[24,2304]{1,0:T(8,128)(2,1)S(1)} %gates.1.refs_0_.refs_3_.refs_6_), channel_id=1, source_target_pairs={{0,16},{1,17},{16,0},{17,1},{2,18},{3,19},{18,2},{19,3},{4,20},{5,... | collective-permute-start | bytes 331784 | tf_op jit(solution)/shard_map/ppermute | solution.py:334
  7.5 1.3 %collective-permute-start.1 = (bf16[24,2048]{1,0:T(8,128)(2,1)S(1)}, bf16[24,2048]{1,0:T(8,128)(2,1)S(1)}, u32[]{:S(2)}, u32[]{:S(2)}) collective-permute-start(bf16[24,2048]{1,0:T(8,128)(2,1)S(1)} %collective-permute-done.refs_1_), channel_id=1, source_target_pairs={{0,1},{1,0},{2,3},{3,2},{4,5},{5,4},{6,7},{7,6},{8,9},{9,8},{10,11... | collective-permute-start | bytes 294920 | tf_op jit(solution)/shard_map/ppermute | solution.py:337
  8.9 2.8 %copy-start = (bf16[1,768,4096]{2,1,0:T(8,128)(2,1)S(1)}, bf16[1,768,4096]{2,1,0:T(8,128)(2,1)}, u32[]{:S(2)}) copy-start(bf16[1,768,4096]{2,1,0:T(8,128)(2,1)} %param.16) | copy-start | bytes 18874372
  11.7 2.4 %copy-start.1 = (bf16[24,4096]{1,0:T(8,128)(2,1)S(1)}, bf16[24,4096]{1,0:T(8,128)(2,1)}, u32[]{:S(2)}) copy-start(bf16[24,4096]{1,0:T(8,128)(2,1)} %refs_3_.1) | copy-start | bytes 589828
  12.4 2.6 %collective-permute-start.4 = (bf16[2,2,24,1024]{3,2,1,0:T(8,128)(2,1)S(1)}, bf16[2,2,24,1024]{3,2,1,0:T(8,128)(2,1)S(1)}, u32[]{:S(2)}, u32[]{:S(2)}) collective-permute-start(bf16[2,2,24,1024]{3,2,1,0:T(8,128)(2,1)S(1)} %outward_send.1.refs_4_), channel_id=1, source_target_pairs={{0,1},{1,0},{2,3},{3,2},{4,5},{5,4},{6,7},{7,6},{8,9},{9,8},{10,11... | collective-permute-start | bytes 589832 | tf_op jit(solution)/shard_map/ppermute | solution.py:337
  12.6 1.5 %collective-permute-start.3 = (bf16[24,2304]{1,0:T(8,128)(2,1)S(1)}, bf16[24,2304]{1,0:T(8,128)(2,1)S(1)}, u32[]{:S(2)}, u32[]{:S(2)}) collective-permute-start(bf16[24,2304]{1,0:T(8,128)(2,1)S(1)} %collective-permute-done.2.refs_1_.refs_4_.refs_7_), channel_id=1, source_target_pairs={{0,1},{1,0},{2,3},{3,2},{4,5},{5,4},{6,7},{7,6},{8,9},{9,8},{10,11... | collective-permute-start | bytes 331784 | tf_op jit(solution)/shard_map/ppermute | solution.py:337
  15.0 6.0 %collective-permute-start.5 = (bf16[2,24,1024]{2,1,0:T(8,128)(2,1)S(1)}, bf16[2,24,1024]{2,1,0:T(8,128)(2,1)S(1)}, u32[]{:S(2)}, u32[]{:S(2)}) collective-permute-start(bf16[2,24,1024]{2,1,0:T(8,128)(2,1)S(1)} %get-tuple-element.42), channel_id=1, source_target_pairs={{0,17},{1,16},{16,1},{17,0},{2,19},{3,18},{18,3},{19,2},{4,21},{5,... | collective-permute-start | bytes 294920 | tf_op jit(solution)/shard_map/ppermute | solution.py:334
  20.7 2.4 %collective-permute-start.6 = (bf16[2,2,24,1024]{3,2,1,0:T(8,128)(2,1)S(1)}, bf16[2,2,24,1024]{3,2,1,0:T(8,128)(2,1)S(1)}, u32[]{:S(2)}, u32[]{:S(2)}) collective-permute-start(bf16[2,2,24,1024]{3,2,1,0:T(8,128)(2,1)S(1)} %get-tuple-element.35), channel_id=1, source_target_pairs={{0,1},{1,0},{2,3},{3,2},{4,5},{5,4},{6,7},{7,6},{8,9},{9,8},{10,11... | collective-permute-start | bytes 589832 | tf_op jit(solution)/shard_map/ppermute | solution.py:337
  21.1 26.3 %copy-start.3 = (bf16[128,4096]{1,0:T(8,128)(2,1)S(1)}, bf16[128,4096]{1,0:T(8,128)(2,1)}, u32[]{:S(2)}) copy-start(bf16[128,4096]{1,0:T(8,128)(2,1)} %refs_19_.1) | copy-start | bytes 3145732
  23.1 5.0 %collective-permute-start.20 = (bf16[2,24,1024]{2,1,0:T(8,128)(2,1)S(1)}, bf16[2,24,1024]{2,1,0:T(8,128)(2,1)S(1)}, u32[]{:S(2)}, u32[]{:S(2)}) collective-permute-start(bf16[2,24,1024]{2,1,0:T(8,128)(2,1)S(1)} %get-tuple-element.41), channel_id=1, source_target_pairs={{0,3},{1,2},{2,1},{3,0},{4,7},{5,6},{6,5},{7,4},{8,11},{9,10},{10,... | collective-permute-start | bytes 294920 | tf_op jit(solution)/shard_map/ppermute | solution.py:334
  24.2 5.0 %collective-permute-start.7 = (bf16[24,1024]{1,0:T(8,128)(2,1)S(1)}, bf16[24,1024]{1,0:T(8,128)(2,1)S(1)}, u32[]{:S(2)}, u32[]{:S(2)}) collective-permute-start(bf16[24,1024]{1,0:T(8,128)(2,1)S(1)} %get-tuple-element.38), channel_id=1, source_target_pairs={{0,18},{1,19},{2,16},{3,17},{16,2},{17,3},{18,0},{19,1},{4,22},{5,... | collective-permute-start | bytes 147464 | tf_op jit(solution)/shard_map/ppermute | solution.py:334
  25.6 3.8 %collective-permute-start.8 = (bf16[24,1024]{1,0:T(8,128)(2,1)S(1)}, bf16[24,1024]{1,0:T(8,128)(2,1)S(1)}, u32[]{:S(2)}, u32[]{:S(2)}) collective-permute-start(bf16[24,1024]{1,0:T(8,128)(2,1)S(1)} %get-tuple-element.39), channel_id=1, source_target_pairs={{0,17},{1,16},{2,19},{3,18},{16,1},{17,0},{18,3},{19,2},{4,21},{5,... | collective-permute-start | bytes 147464 | tf_op jit(solution)/shard_map/ppermute | solution.py:334
  26.1 3.9 %collective-permute-start.9 = (bf16[24,1024]{1,0:T(8,128)(2,1)S(1)}, bf16[24,1024]{1,0:T(8,128)(2,1)S(1)}, u32[]{:S(2)}, u32[]{:S(2)}) collective-permute-start(bf16[24,1024]{1,0:T(8,128)(2,1)S(1)} %get-tuple-element.40), channel_id=1, source_target_pairs={{0,3},{1,2},{2,1},{3,0},{16,19},{17,18},{18,17},{19,16},{4,7},{5,6... | collective-permute-start | bytes 147464 | tf_op jit(solution)/shard_map/ppermute | solution.py:334
  28.1 6.1 %collective-permute-start.21 = (bf16[2,24,1024]{2,1,0:T(8,128)(2,1)S(1)}, bf16[2,24,1024]{2,1,0:T(8,128)(2,1)S(1)}, u32[]{:S(2)}, u32[]{:S(2)}) collective-permute-start(bf16[2,24,1024]{2,1,0:T(8,128)(2,1)S(1)} %add_convert_fusion.3), channel_id=1, source_target_pairs={{0,5},{1,4},{4,1},{5,0},{8,13},{9,12},{12,9},{13,8},{2,7},{3,6},{6... | collective-permute-start | bytes 294920 | tf_op jit(solution)/shard_map/ppermute | solution.py:334
  30.0 6.5 %collective-permute-start.12 = (bf16[24,1024]{1,0:T(8,128)(2,1)S(1)}, bf16[24,1024]{1,0:T(8,128)(2,1)S(1)}, u32[]{:S(2)}, u32[]{:S(2)}) collective-permute-start(bf16[24,1024]{1,0:T(8,128)(2,1)S(1)} %add_convert_fusion.6), channel_id=1, source_target_pairs={{0,12},{1,13},{4,8},{5,9},{8,4},{9,5},{12,0},{13,1},{2,14},{3,15},... | collective-permute-start | bytes 147464 | tf_op jit(solution)/shard_map/ppermute | solution.py:334
  33.7 5.1 %collective-permute-start.11 = (bf16[24,1024]{1,0:T(8,128)(2,1)S(1)}, bf16[24,1024]{1,0:T(8,128)(2,1)S(1)}, u32[]{:S(2)}, u32[]{:S(2)}) collective-permute-start(bf16[24,1024]{1,0:T(8,128)(2,1)S(1)} %add_convert_fusion.6), channel_id=1, source_target_pairs={{0,9},{1,8},{4,13},{5,12},{8,1},{9,0},{12,5},{13,4},{2,11},{3,10},... | collective-permute-start | bytes 147464 | tf_op jit(solution)/shard_map/ppermute | solution.py:334
  33.7 5.1 %collective-permute-start.10 = (bf16[24,1024]{1,0:T(8,128)(2,1)S(1)}, bf16[24,1024]{1,0:T(8,128)(2,1)S(1)}, u32[]{:S(2)}, u32[]{:S(2)}) collective-permute-start(bf16[24,1024]{1,0:T(8,128)(2,1)S(1)} %add_convert_fusion.6), channel_id=1, source_target_pairs={{0,5},{1,4},{4,1},{5,0},{8,13},{9,12},{12,9},{13,8},{2,7},{3,6},{6... | collective-permute-start | bytes 147464 | tf_op jit(solution)/shard_map/ppermute | solution.py:334
  34.2 8.7 %collective-permute-start.22 = (bf16[2,24,1024]{2,1,0:T(8,128)(2,1)S(1)}, bf16[2,24,1024]{2,1,0:T(8,128)(2,1)S(1)}, u32[]{:S(2)}, u32[]{:S(2)}) collective-permute-start(bf16[2,24,1024]{2,1,0:T(8,128)(2,1)S(1)} %add_convert_fusion.2), channel_id=1, source_target_pairs={{0,9},{1,8},{4,13},{5,12},{8,1},{9,0},{12,5},{13,4},{2,11},{3,10},... | collective-permute-start | bytes 294920 | tf_op jit(solution)/shard_map/ppermute | solution.py:334
  38.8 5.4 %collective-permute-start.15 = (bf16[24,1024]{1,0:T(8,128)(2,1)S(1)}, bf16[24,1024]{1,0:T(8,128)(2,1)S(1)}, u32[]{:S(2)}, u32[]{:S(2)}) collective-permute-start(bf16[24,1024]{1,0:T(8,128)(2,1)S(1)} %add_convert_fusion.5.refs_8_), channel_id=1, source_target_pairs={{0,18},{1,19},{2,16},{3,17},{16,2},{17,3},{18,0},{19,1},{4,22},{5,... | collective-permute-start | bytes 147464 | tf_op jit(solution)/shard_map/ppermute | solution.py:334
  41.9 4.0 %collective-permute-start.14 = (bf16[24,1024]{1,0:T(8,128)(2,1)S(1)}, bf16[24,1024]{1,0:T(8,128)(2,1)S(1)}, u32[]{:S(2)}, u32[]{:S(2)}) collective-permute-start(bf16[24,1024]{1,0:T(8,128)(2,1)S(1)} %add_convert_fusion.5.refs_8_), channel_id=1, source_target_pairs={{0,17},{1,16},{2,19},{3,18},{16,1},{17,0},{18,3},{19,2},{4,21},{5,... | collective-permute-start | bytes 147464 | tf_op jit(solution)/shard_map/ppermute | solution.py:334
  42.1 4.0 %collective-permute-start.13 = (bf16[24,1024]{1,0:T(8,128)(2,1)S(1)}, bf16[24,1024]{1,0:T(8,128)(2,1)S(1)}, u32[]{:S(2)}, u32[]{:S(2)}) collective-permute-start(bf16[24,1024]{1,0:T(8,128)(2,1)S(1)} %add_convert_fusion.5.refs_8_), channel_id=1, source_target_pairs={{0,3},{1,2},{2,1},{3,0},{16,19},{17,18},{18,17},{19,16},{4,7},{5,6... | collective-permute-start | bytes 147464 | tf_op jit(solution)/shard_map/ppermute | solution.py:334
  43.0 4.4 %collective-permute-start.23 = (bf16[2,24,1024]{2,1,0:T(8,128)(2,1)S(1)}, bf16[2,24,1024]{2,1,0:T(8,128)(2,1)S(1)}, u32[]{:S(2)}, u32[]{:S(2)}) collective-permute-start(bf16[2,24,1024]{2,1,0:T(8,128)(2,1)S(1)} %add_convert_fusion.1.refs_16_), channel_id=1, source_target_pairs={{0,1},{1,0},{2,3},{3,2},{4,5},{5,4},{6,7},{7,6},{8,9},{9,8},{10,11... | collective-permute-start | bytes 294920 | tf_op jit(solution)/shard_map/ppermute | solution.py:337
  43.1 3.4 %collective-permute-start.16 = (bf16[24,1024]{1,0:T(8,128)(2,1)S(1)}, bf16[24,1024]{1,0:T(8,128)(2,1)S(1)}, u32[]{:S(2)}, u32[]{:S(2)}) collective-permute-start(bf16[24,1024]{1,0:T(8,128)(2,1)S(1)} %add_convert_fusion.5.refs_8_), channel_id=1, source_target_pairs={{0,1},{1,0},{2,3},{3,2},{4,5},{5,4},{6,7},{7,6},{8,9},{9,8},{10,11... | collective-permute-start | bytes 147464 | tf_op jit(solution)/shard_map/ppermute | solution.py:337
  44.2 2.3 %collective-permute-start.19 = (bf16[24,1024]{1,0:T(8,128)(2,1)S(1)}, bf16[24,1024]{1,0:T(8,128)(2,1)S(1)}, u32[]{:S(2)}, u32[]{:S(2)}) collective-permute-start(bf16[24,1024]{1,0:T(8,128)(2,1)S(1)} %collective-permute-done.15.refs_11_), channel_id=1, source_target_pairs={{0,1},{1,0},{2,3},{3,2},{4,5},{5,4},{6,7},{7,6},{8,9},{9,8},{10,11... | collective-permute-start | bytes 147464 | tf_op jit(solution)/shard_map/ppermute | solution.py:337
  46.0 1.2 %collective-permute-start.18 = (bf16[24,1024]{1,0:T(8,128)(2,1)S(1)}, bf16[24,1024]{1,0:T(8,128)(2,1)S(1)}, u32[]{:S(2)}, u32[]{:S(2)}) collective-permute-start(bf16[24,1024]{1,0:T(8,128)(2,1)S(1)} %collective-permute-done.14.refs_10_), channel_id=1, source_target_pairs={{0,1},{1,0},{2,3},{3,2},{4,5},{5,4},{6,7},{7,6},{8,9},{9,8},{10,11... | collective-permute-start | bytes 147464 | tf_op jit(solution)/shard_map/ppermute | solution.py:337
  46.1 1.3 %collective-permute-start.17 = (bf16[24,1024]{1,0:T(8,128)(2,1)S(1)}, bf16[24,1024]{1,0:T(8,128)(2,1)S(1)}, u32[]{:S(2)}, u32[]{:S(2)}) collective-permute-start(bf16[24,1024]{1,0:T(8,128)(2,1)S(1)} %collective-permute-done.13.refs_9_), channel_id=1, source_target_pairs={{0,1},{1,0},{2,3},{3,2},{4,5},{5,4},{6,7},{7,6},{8,9},{9,8},{10,11... | collective-permute-start | bytes 147464 | tf_op jit(solution)/shard_map/ppermute | solution.py:337

commit v13 on v12

--- a/solution.py
+++ b/solution.py
@@ -13,6 +13,7 @@
 STEP = 256
 LANES = 128
 TERMS = 3
+PIECES = 2
 LOAD_PIECES = 8
 FEW_ROWS = 64
 VMEM_LIMIT = 12 * 1024 * 1024
@@ -129,34 +130,56 @@
     return gates[:, 0:1] + gates[:, 1:2] + gates[:, 2:3]
 
 
-def hidden_kernel(n_dp, *refs):
-    hid = refs[: 2 * n_dp - 1]
-    gain, w_gate, w_up, pre_gate, pre_up, act, normed = refs[2 * n_dp - 1 :]
-    total, width = hid[0].shape[0] * n_dp, hid[0].shape[1]
-    few = total <= FEW_ROWS
-    sums = [0.0]
-
-    def square(columns, value):
-        sums[0] = sums[0] + folded(value * value)
-
-    both_halves([hid], width, square)
-    scale = lax.rsqrt(jnp.sum(sums[0], axis=1, keepdims=True) / width + EPSILON)
-
-    def norm(columns, value):
-        normed[:, columns] = (value * scale * gain[:, columns]).astype(BF16)
-
-    both_halves([hid], width, norm)
-    size = unit_step(w_gate.shape[1])
+def half_columns(h, half):
+    return pl.multiple_of((lax.axis_index("c") ^ h) * half, half)
+
+
+def scaled_half(h, own, others, gain, scaled):
+    half = scaled.shape[1]
+    first, size = half_columns(h, half), 512 if len(others) < 2 else 128
+    squares = 0.0
+    for start in range(0, half, size):
+        columns = pl.ds(pl.multiple_of(first + start, size), size)
+        rows = [own[:, columns]] + [other[:, start : start + size] for other in others]
+        value = jnp.concatenate([row.astype(F32) for row in rows], axis=0)
+        squares = squares + folded(value * value)
+        scaled[:, start : start + size] = (value * gain[:, columns]).astype(BF16)
+    return squares
+
+
+def hidden_first_kernel(n_dp, own, *refs):
+    others = refs[: n_dp - 1]
+    gain, w_gate, w_up, gate_sum, up_sum, square_sum, scaled = refs[n_dp - 1 :]
+    half = scaled.shape[1]
+    square_sum[...] = scaled_half(0, own, others, gain, scaled)
+    size, rows = unit_step(w_gate.shape[1]), pl.ds(half_columns(0, half), half)
 
     def hidden_units(step):
         columns = pl.ds(place(step, size), size)
-        gate_part = dot(normed[...], w_gate[:, columns], ((1,), (0,)))
-        up_part = dot(normed[...], w_up[:, columns], ((1,), (0,)))
+        gate_sum[:, columns] = dot(scaled[...], w_gate[rows, columns], ((1,), (0,)))
+        up_sum[:, columns] = dot(scaled[...], w_up[rows, columns], ((1,), (0,)))
+
+    loop(w_gate.shape[1] // size, hidden_units, scaled.shape[0] <= FEW_ROWS)
+
+
+def hidden_rest_kernel(n_dp, own, *refs):
+    others = refs[: n_dp - 1]
+    gain, w_gate, w_up, gate_sum, up_sum, square_sum, pre_gate, pre_up, act, scales, scaled = refs[n_dp - 1 :]
+    half = scaled.shape[1]
+    squares = square_sum[...] + scaled_half(1, own, others, gain, scaled)
+    scale = lax.rsqrt(jnp.sum(squares, axis=1, keepdims=True) / (2 * half) + EPSILON)
+    scales[...] = jnp.broadcast_to(scale, scales.shape)
+    size, rows = unit_step(w_gate.shape[1]), pl.ds(half_columns(1, half), half)
+
+    def hidden_units(step):
+        columns = pl.ds(place(step, size), size)
+        gate_part = scale * (gate_sum[:, columns] + dot(scaled[...], w_gate[rows, columns], ((1,), (0,))))
+        up_part = scale * (up_sum[:, columns] + dot(scaled[...], w_up[rows, columns], ((1,), (0,))))
         pre_gate[:, columns] = gate_part
         pre_up[:, columns] = up_part
         act[:, columns] = (gate_part * jax.nn.sigmoid(gate_part) * up_part).astype(BF16)
 
-    loop(w_gate.shape[1] // size, hidden_units, few)
+    loop(w_gate.shape[1] // size, hidden_units, scaled.shape[0] <= FEW_ROWS)
 
 
 def outward_kernel(i, n_dp, *refs):
@@ -249,10 +272,14 @@
     refs = refs[2 * count + n_dp :]
     back, moe = refs[: 4 * n_dp], refs[4 * n_dp : 4 * n_dp + 2]
     refs = refs[4 * n_dp + 2 :]
-    gain, w_out, targets, held = refs[0], refs[1], refs[2:6], refs[6:10]
-    summed, d_all, sems = refs[10:]
+    gain, scales, w_out, targets, held = refs[0], refs[1], refs[2], refs[3:7], refs[7:11]
+    summed, d_all, sems = refs[11:]
     output, d_hidden, d_context, d_w_out = held
-    copies = [pltpu.make_async_copy(held[n], targets[n], sems.at[n]) for n in range(4)]
+    copies = [pltpu.make_async_copy(held[n], targets[n], sems.at[n]) for n in range(3)]
+    size = d_w_out.shape[1] // PIECES
+    for piece in range(PIECES):
+        block = (slice(None), pl.ds(piece * size, size))
+        copies.append(pltpu.make_async_copy(d_w_out.at[block], targets[3].at[block], sems.at[3 + piece]))
     rows, width = hid[0].shape
     chunk = moe[0].shape[2]
     for i in range(2):
@@ -265,15 +292,14 @@
     copies[0].start()
 
     few = rows * n_dp <= FEW_ROWS
-    sums = [0.0, 0.0]
+    sums = [0.0]
 
     def products(columns, value):
-        sums[0] = sums[0] + folded(value * value)
-        sums[1] = sums[1] + folded(value * summed[:, columns])
+        sums[0] = sums[0] + folded(value * summed[:, columns])
 
     both_halves([hid], width, products)
-    scale = lax.rsqrt(jnp.sum(sums[0], axis=1, keepdims=True) / width + EPSILON)
-    centre = scale * jnp.sum(sums[1], axis=1, keepdims=True) / width
+    scale = scales[:, :1]
+    centre = scale * jnp.sum(sums[0], axis=1, keepdims=True) / width
 
     def total(columns, value, grad):
         result = grad + scale * (summed[:, columns] - value * scale * centre)
@@ -282,22 +308,18 @@
 
     both_halves([hid, grads], width, total)
     copies[1].start()
-    d_context[...] = dot(d_hidden[...], w_out[...], ((1,), (1,))).astype(BF16)
+    heads = d_context.shape[1]
     part = width // n_dp
-    copies[2].start()
-    heads = d_context.shape[1]
     lanes = slice(width // 2, width // 2 + heads)
     turned = jnp.concatenate([small[:, lanes].astype(F32) for small in smalls], axis=0).T.astype(BF16)
-    step_width = min(part, 512)
-
-    def product(step):
-        columns = pl.ds(pl.multiple_of(lax.axis_index("dp") * part + step * step_width, step_width), step_width)
-        d_w_out[:, pl.ds(place(step, step_width), step_width)] = dot(
-            turned, d_all[:, columns], ((1,), (0,))
-        ).astype(BF16)
-
-    loop(part // step_width, product, few)
-    copies[3].start()
+    size = part // PIECES
+    for piece in range(PIECES):
+        columns = pl.ds(pl.multiple_of(lax.axis_index("dp") * part + piece * size, LANES), size)
+        block = pl.ds(piece * size, size)
+        d_w_out[:, block] = dot(turned, d_all[:, columns], ((1,), (0,))).astype(BF16)
+        copies[3 + piece].start()
+    d_context[...] = dot(d_hidden[...], w_out[...], ((1,), (1,))).astype(BF16)
+    copies[2].start()
     for copy in copies:
         copy.wait()
 
@@ -367,10 +389,15 @@
             total = total + piece.astype(F32)
         return total.astype(BF16)
 
-    pre_gate, pre_up, act = run(
-        hidden_kernel, n_dp, hid + [gain, wg, wu],
-        [((all_rows, units), F32), ((all_rows, units), F32), ((all_rows, units), BF16)],
-        [pltpu.VMEM((all_rows, width), BF16)], 2 * weights, "hidden",
+    hidden_units, row_block = ((all_rows, units), F32), ((all_rows, LANES), F32)
+    scaled = pltpu.VMEM((all_rows, half), BF16)
+    gate_sum, up_sum, square_sum = run(
+        hidden_first_kernel, n_dp, [hidden_in] + hid[1::2] + [gain, wg, wu],
+        [hidden_units, hidden_units, row_block], [scaled], weights, "hidden_first",
+    )
+    pre_gate, pre_up, act, scales = run(
+        hidden_rest_kernel, n_dp, [hidden_in] + hid[2::2] + [gain, wg, wu, gate_sum, up_sum, square_sum],
+        [hidden_units, hidden_units, ((all_rows, units), BF16), row_block], [scaled], weights, "hidden_rest",
     )
     (out_send,) = run(
         functools.partial(outward_kernel, 1), n_dp, smalls + [act, wd], [shares], [],
@@ -426,9 +453,9 @@
     moe = [out_total, other_core(out_total)]
     outs = [((rows, width), BF16), ((rows, width), BF16), ((rows, heads), BF16), ((heads, width // n_dp), BF16)]
     return run(
-        finish_kernel, n_dp, hid + grads + smalls + back + moe + [gain, w_out], outs,
+        finish_kernel, n_dp, hid + grads + smalls + back + moe + [gain, scales, w_out], outs,
         [pltpu.VMEM(*out) for out in outs]
-        + [pltpu.VMEM((all_rows, width), F32), pltpu.VMEM((all_rows, width), BF16), pltpu.SemaphoreType.DMA((4,))],
+        + [pltpu.VMEM((all_rows, width), F32), pltpu.VMEM((all_rows, width), BF16), pltpu.SemaphoreType.DMA((3 + PIECES,))],
         weights, "finish", out_space=pltpu.HBM,
     )
 

time: 49.4 us -> 48.4 us (0.980)
  waiting for transfers between devices: 10.7 us -> 9.99 us
    ppermute x9, waiting for transfers between devices: 2.59 us -> 1.44 us  [other_core(): return lax.ppermute(value, ('c',), [(0, 1), (1, 0)])]
    pallas_call x11 -> x12, Pallas kernels: 14.3 us -> 14.1 us  [run(): pl.pallas_call(functools.partial(kernel, n_dp), out_shape=kinds, in_specs...]
where the time goes in v13:
time: 48.4 us; the launch traced here: 48.2 us
  starting transfers between devices  23 us (48%)
  Pallas kernels  14.1 us (29%)
  waiting for transfers between devices  9.99 us (21%)
  between operations  0.9 us (2%)
    ppermute x15, starting transfers between devices, swap(): lax.ppermute(value, axes + ('c',), [(i, i ^ turn) for i in range(count)])  21 us
    pallas_call x12, Pallas kernels, run(): pl.pallas_call(functools.partial(kernel, n_dp), out_shape=kinds, in_specs...  14.1 us
    ppermute x15, waiting for transfers between devices, swap(): lax.ppermute(value, axes + ('c',), [(i, i ^ turn) for i in range(count)])  8.55 us
    ppermute x9, starting transfers between devices, other_core(): return lax.ppermute(value, ('c',), [(0, 1), (1, 0)])  1.98 us
    ppermute x9, waiting for transfers between devices, other_core(): return lax.ppermute(value, ('c',), [(0, 1), (1, 0)])  1.44 us
  transfers between devices with their start and end apart: 24, of which 13 were waited for; matrix products, arithmetic and copies ran while one was open for 0% of the time, Pallas kernels for 22%

profile of v13, /device:TPU:0, one launch (start us, length us, event | category | flops | bytes accessed | tf_op | source)
XLA Modules:
  0.0 48.2 jit_solution(3065756699079983077)
XLA Ops:
  0.7 1.1 %cut.1 = bf16[24,2048]{1,0:T(8,128)(2,1)S(1)} custom-call(bf16[24,4096]{1,0:T(8,128)(2,1)} %refs_0_.3), custom_call_target="tpu_custom_call" | custom-call | bytes 98304 | tf_op jit(solution)/shard_map/cut/pallas_call | solution.py:331
  1.7 3.0 %collective-permute-start = (bf16[24,2048]{1,0:T(8,128)(2,1)S(1)}, bf16[24,2048]{1,0:T(8,128)(2,1)S(1)}, u32[]{:S(2)}, u32[]{:S(2)}) collective-permute-start(bf16[24,2048]{1,0:T(8,128)(2,1)S(1)} %cut.1), channel_id=1, source_target_pairs={{0,16},{1,17},{16,0},{17,1},{2,18},{3,19},{18,2},{19,3},{4,20},{5,... | collective-permute-start | bytes 294920 | tf_op jit(solution)/shard_map/ppermute | solution.py:356
  4.7 1.1 %gates.1.refs_0_.refs_3_.refs_6_ = bf16[24,2304]{1,0:T(8,128)(2,1)S(1)} custom-call(s32[8,24]{1,0:T(8,128)} %bitcast.34, f32[8,24]{1,0:T(8,128)} %bitcast.35, bf16[24,128]{1,0:T(8,128)(2,1)} %context.1, bf16[24,4096]{1,0:T(8,128)(2,1)} %refs_3_.1, bf16[4096,768]{1,0:T(8,128)(2,1)} %bitcast.17, bf16[4096,768]{1,0:T(8,128)(2,1)} %bitcast.24, ...), custom_call_target="tpu_custom_call" | custom-call | bytes 25165824 | tf_op jit(solution)/shard_map/gates/pallas_call | solution.py:331
  5.9 0.6 %collective-permute-start.2 = (bf16[24,2304]{1,0:T(8,128)(2,1)S(1)}, bf16[24,2304]{1,0:T(8,128)(2,1)S(1)}, u32[]{:S(2)}, u32[]{:S(2)}) collective-permute-start(bf16[24,2304]{1,0:T(8,128)(2,1)S(1)} %gates.1.refs_0_.refs_3_.refs_6_), channel_id=1, source_target_pairs={{0,16},{1,17},{16,0},{17,1},{2,18},{3,19},{18,2},{19,3},{4,20},{5,... | collective-permute-start | bytes 331784 | tf_op jit(solution)/shard_map/ppermute | solution.py:356
  6.4 1.1 %collective-permute-done.refs_0_.refs_1_ = bf16[24,2048]{1,0:T(8,128)(2,1)S(1)} collective-permute-done((bf16[24,2048]{1,0:T(8,128)(2,1)S(1)}, bf16[24,2048]{1,0:T(8,128)(2,1)S(1)}, u32[]{:S(2)}, u32[]{:S(2)}) %collective-permute-start) | collective-permute-done | bytes 98336 | tf_op jit(solution)/shard_map/ppermute | solution.py:356
  7.6 1.2 %hidden_first.1 = (f32[48,768]{1,0:T(8,128)S(1)}, f32[48,768]{1,0:T(8,128)S(1)}, f32[48,128]{1,0:T(8,128)S(1)}) custom-call(bf16[24,4096]{1,0:T(8,128)(2,1)S(1)} %copy-done, bf16[24,2048]{1,0:T(8,128)(2,1)S(1)} %collective-permute-done.refs_0_.refs_1_, f32[1,4096]{1,0:T(1,128)S(1)} %bitcast.31, bf16[4096,768]{1,0:T(8,128)(2,1)S(1)} %bitcast.20, ...), custom_call_target="tpu_custom_call" | custom-call | bytes 6291456 | tf_op jit(solution)/shard_map/hidden_first/pallas_call | solution.py:331
  8.8 0.0 slice-start.1
  8.8 1.2 %hidden_rest.1 = (f32[48,768]{1,0:T(8,128)S(1)}, f32[48,768]{1,0:T(8,128)S(1)}, bf16[48,768]{1,0:T(8,128)(2,1)S(1)}, f32[48,128]{1,0:T(8,128)S(1)}) custom-call(bf16[24,4096]{1,0:T(8,128)(2,1)S(1)} %copy-done, bf16[24,2048]{1,0:T(8,128)(2,1)S(1)} %collective-permute-done.1.refs_0_.refs_2_, f32[1,4096]{1,0:T(1,128)S(1)} %bitcast.32, ...), custom_call_target="tpu_custom_call" | custom-call | bytes 6291456 | tf_op jit(solution)/shard_map/hidden_rest/pallas_call | solution.py:331
  10.1 0.6 %collective-permute-done.2.refs_1_.refs_4_.refs_7_ = bf16[24,2304]{1,0:T(8,128)(2,1)S(1)} collective-permute-done((bf16[24,2304]{1,0:T(8,128)(2,1)S(1)}, bf16[24,2304]{1,0:T(8,128)(2,1)S(1)}, u32[]{:S(2)}, u32[]{:S(2)}) %collective-permute-start.2) | collective-permute-done | bytes 110624 | tf_op jit(solution)/shard_map/ppermute | solution.py:356
  10.7 0.7 %outward_send.1.refs_4_ = bf16[2,2,24,1024]{3,2,1,0:T(8,128)(2,1)S(1)} custom-call(bf16[24,2304]{1,0:T(8,128)(2,1)S(1)} %gates.1.refs_0_.refs_3_.refs_6_, bf16[24,2304]{1,0:T(8,128)(2,1)S(1)} %collective-permute-done.2.refs_1_.refs_4_.refs_7_, bf16[48,768]{1,0:T(8,128)(2,1)S(1)} %get-tuple-element.32.refs_2_, bf16[768,4096]{1,0:T(8,128)(2,1)S(1)} %bitcast.13), custom_call_target="tpu_custom_call" | custom-call | bytes 3145728 | tf_op jit(solution)/shard_map/outward_send/pallas_call | solution.py:331
  11.4 0.5 %collective-permute-start.4 = (bf16[2,2,24,1024]{3,2,1,0:T(8,128)(2,1)S(1)}, bf16[2,2,24,1024]{3,2,1,0:T(8,128)(2,1)S(1)}, u32[]{:S(2)}, u32[]{:S(2)}) collective-permute-start(bf16[2,2,24,1024]{3,2,1,0:T(8,128)(2,1)S(1)} %outward_send.1.refs_4_), channel_id=1, source_target_pairs={{0,1},{1,0},{2,3},{3,2},{4,5},{5,4},{6,7},{7,6},{8,9},{9,8},{10,11... | collective-permute-start | bytes 589832 | tf_op jit(solution)/shard_map/ppermute | solution.py:359
  11.9 0.1 collective-permute-start.3
  12.0 0.7 %outward_keep.1.refs_8_ = bf16[2,2,24,1024]{3,2,1,0:T(8,128)(2,1)S(1)} custom-call(bf16[24,2304]{1,0:T(8,128)(2,1)S(1)} %gates.1.refs_0_.refs_3_.refs_6_, bf16[24,2304]{1,0:T(8,128)(2,1)S(1)} %collective-permute-done.2.refs_1_.refs_4_.refs_7_, bf16[48,768]{1,0:T(8,128)(2,1)S(1)} %get-tuple-element.32.refs_2_, bf16[768,4096]{1,0:T(8,128)(2,1)S(1)} %bitcast.14, ...), custom_call_target="tpu_custom_call" | custom-call | bytes 3145728 | tf_op jit(solution)/shard_map/outward_keep/pallas_call | solution.py:331
  12.7 0.6 %collective-permute-done.3.refs_2_.refs_5_ = bf16[24,2304]{1,0:T(8,128)(2,1)S(1)} collective-permute-done((bf16[24,2304]{1,0:T(8,128)(2,1)S(1)}, bf16[24,2304]{1,0:T(8,128)(2,1)S(1)}, u32[]{:S(2)}, u32[]{:S(2)}) %collective-permute-start.3) | collective-permute-done | bytes 110624 | tf_op jit(solution)/shard_map/ppermute | solution.py:359
  13.3 0.9 %backward_first.1 = (bf16[48,256]{1,0:T(8,128)(2,1)S(1)}, bf16[48,256]{1,0:T(8,128)(2,1)S(1)}, bf16[48,4096]{1,0:T(8,128)(2,1)S(1)}, bf16[2,2,24,1024]{3,2,1,0:T(8,128)(2,1)S(1)}) custom-call(bf16[24,4096]{1,0:T(8,128)(2,1)S(1)} %copy-done.1, bf16[24,2304]{1,0:T(8,128)(2,1)S(1)} %collective-permute-done.2.refs_1_.refs_4_.refs_7_, ...), custom_call_target="tpu_custom_call" | custom-call | bytes 2097152 | tf_op jit(solution)/shard_map/backward_first/pallas_call | solution.py:331
  14.2 0.1 add_convert_fusion
  14.2 2.3 %collective-permute-start.5 = (bf16[2,24,1024]{2,1,0:T(8,128)(2,1)S(1)}, bf16[2,24,1024]{2,1,0:T(8,128)(2,1)S(1)}, u32[]{:S(2)}, u32[]{:S(2)}) collective-permute-start(bf16[2,24,1024]{2,1,0:T(8,128)(2,1)S(1)} %get-tuple-element.50), channel_id=1, source_target_pairs={{0,17},{1,16},{16,1},{17,0},{2,19},{3,18},{18,3},{19,2},{4,21},{5,... | collective-permute-start | bytes 294920 | tf_op jit(solution)/shard_map/ppermute | solution.py:356
  16.6 1.4 %backward_rest.1 = (bf16[48,512]{1,0:T(8,128)(2,1)S(1)}, bf16[48,512]{1,0:T(8,128)(2,1)S(1)}, bf16[2,24,1024]{2,1,0:T(8,128)(2,1)S(1)}) custom-call(bf16[48,4096]{1,0:T(8,128)(2,1)S(1)} %get-tuple-element.35.weighted, f32[48,768]{1,0:T(8,128)S(1)} %get-tuple-element.30.refs_5_.pre_gate, f32[48,768]{1,0:T(8,128)S(1)} %get-tuple-element.31.refs_6_.pre_up, ...), custom_call_target="tpu_custom_call" | custom-call | bytes 4194304 | tf_op jit(solution)/shard_map/backward_rest/pallas_call | solution.py:331
  18.0 2.0 %inward_send.1 = (bf16[2,2,24,1024]{3,2,1,0:T(8,128)(2,1)S(1)}, bf16[2,24,1024]{2,1,0:T(8,128)(2,1)S(1)}) custom-call(bf16[48,256]{1,0:T(8,128)(2,1)S(1)} %get-tuple-element.33.refs_0_, bf16[48,256]{1,0:T(8,128)(2,1)S(1)} %get-tuple-element.34.refs_1_, bf16[48,512]{1,0:T(8,128)(2,1)S(1)} %get-tuple-element.37.refs_2_, ...), custom_call_target="tpu_custom_call" | custom-call | bytes 6291456 | tf_op jit(solution)/shard_map/inward_send/pallas_call | solution.py:331
  20.0 0.3 collective-permute-start.6
  20.3 2.0 %inward_keep.1 = (bf16[2,2,24,1024]{3,2,1,0:T(8,128)(2,1)S(1)}, bf16[2,24,1024]{2,1,0:T(8,128)(2,1)S(1)}) custom-call(bf16[48,256]{1,0:T(8,128)(2,1)S(1)} %get-tuple-element.33.refs_0_, bf16[48,256]{1,0:T(8,128)(2,1)S(1)} %get-tuple-element.34.refs_1_, bf16[48,512]{1,0:T(8,128)(2,1)S(1)} %get-tuple-element.37.refs_2_, ...), custom_call_target="tpu_custom_call" | custom-call | bytes 6291456 | tf_op jit(solution)/shard_map/inward_keep/pallas_call | solution.py:331
  22.3 0.1 join.1
  22.4 1.1 %collective-permute-start.20 = (bf16[2,24,1024]{2,1,0:T(8,128)(2,1)S(1)}, bf16[2,24,1024]{2,1,0:T(8,128)(2,1)S(1)}, u32[]{:S(2)}, u32[]{:S(2)}) collective-permute-start(bf16[2,24,1024]{2,1,0:T(8,128)(2,1)S(1)} %get-tuple-element.48), channel_id=1, source_target_pairs={{0,3},{1,2},{2,1},{3,0},{4,7},{5,6},{6,5},{7,4},{8,11},{9,10},{10,... | collective-permute-start | bytes 294920 | tf_op jit(solution)/shard_map/ppermute | solution.py:356
  23.5 1.3 %collective-permute-start.7 = (bf16[24,1024]{1,0:T(8,128)(2,1)S(1)}, bf16[24,1024]{1,0:T(8,128)(2,1)S(1)}, u32[]{:S(2)}, u32[]{:S(2)}) collective-permute-start(bf16[24,1024]{1,0:T(8,128)(2,1)S(1)} %get-tuple-element.45), channel_id=1, source_target_pairs={{0,18},{1,19},{2,16},{3,17},{16,2},{17,3},{18,0},{19,1},{4,22},{5,... | collective-permute-start | bytes 147464 | tf_op jit(solution)/shard_map/ppermute | solution.py:356
  24.8 0.5 %collective-permute-start.8 = (bf16[24,1024]{1,0:T(8,128)(2,1)S(1)}, bf16[24,1024]{1,0:T(8,128)(2,1)S(1)}, u32[]{:S(2)}, u32[]{:S(2)}) collective-permute-start(bf16[24,1024]{1,0:T(8,128)(2,1)S(1)} %get-tuple-element.46), channel_id=1, source_target_pairs={{0,17},{1,16},{2,19},{3,18},{16,1},{17,0},{18,3},{19,2},{4,21},{5,... | collective-permute-start | bytes 147464 | tf_op jit(solution)/shard_map/ppermute | solution.py:356
  25.4 1.3 %collective-permute-start.9 = (bf16[24,1024]{1,0:T(8,128)(2,1)S(1)}, bf16[24,1024]{1,0:T(8,128)(2,1)S(1)}, u32[]{:S(2)}, u32[]{:S(2)}) collective-permute-start(bf16[24,1024]{1,0:T(8,128)(2,1)S(1)} %get-tuple-element.47), channel_id=1, source_target_pairs={{0,3},{1,2},{2,1},{3,0},{16,19},{17,18},{18,17},{19,16},{4,7},{5,6... | collective-permute-start | bytes 147464 | tf_op jit(solution)/shard_map/ppermute | solution.py:356
  26.7 0.6 %collective-permute-done.20 = bf16[2,24,1024]{2,1,0:T(8,128)(2,1)S(1)} collective-permute-done((bf16[2,24,1024]{2,1,0:T(8,128)(2,1)S(1)}, bf16[2,24,1024]{2,1,0:T(8,128)(2,1)S(1)}, u32[]{:S(2)}, u32[]{:S(2)}) %collective-permute-start.20) | collective-permute-done | bytes 98336 | tf_op jit(solution)/shard_map/ppermute | solution.py:356
  27.4 0.9 %collective-permute-start.21 = (bf16[2,24,1024]{2,1,0:T(8,128)(2,1)S(1)}, bf16[2,24,1024]{2,1,0:T(8,128)(2,1)S(1)}, u32[]{:S(2)}, u32[]{:S(2)}) collective-permute-start(bf16[2,24,1024]{2,1,0:T(8,128)(2,1)S(1)} %add_convert_fusion.3), channel_id=1, source_target_pairs={{0,5},{1,4},{4,1},{5,0},{8,13},{9,12},{12,9},{13,8},{2,7},{3,6},{6... | collective-permute-start | bytes 294920 | tf_op jit(solution)/shard_map/ppermute | solution.py:356
  28.3 0.3 collective-permute-done.7
  28.6 0.1 collective-permute-done.8
  28.8 0.4 collective-permute-done.9
  29.2 3.8 %collective-permute-start.12 = (bf16[24,1024]{1,0:T(8,128)(2,1)S(1)}, bf16[24,1024]{1,0:T(8,128)(2,1)S(1)}, u32[]{:S(2)}, u32[]{:S(2)}) collective-permute-start(bf16[24,1024]{1,0:T(8,128)(2,1)S(1)} %add_convert_fusion.6), channel_id=1, source_target_pairs={{0,12},{1,13},{4,8},{5,9},{8,4},{9,5},{12,0},{13,1},{2,14},{3,15},... | collective-permute-start | bytes 147464 | tf_op jit(solution)/shard_map/ppermute | solution.py:356
  33.0 0.4 collective-permute-start.10
  33.4 2.3 %collective-permute-start.22 = (bf16[2,24,1024]{2,1,0:T(8,128)(2,1)S(1)}, bf16[2,24,1024]{2,1,0:T(8,128)(2,1)S(1)}, u32[]{:S(2)}, u32[]{:S(2)}) collective-permute-start(bf16[2,24,1024]{2,1,0:T(8,128)(2,1)S(1)} %add_convert_fusion.2), channel_id=1, source_target_pairs={{0,9},{1,8},{4,13},{5,12},{8,1},{9,0},{12,5},{13,4},{2,11},{3,10},... | collective-permute-start | bytes 294920 | tf_op jit(solution)/shard_map/ppermute | solution.py:356
  35.7 2.3 %collective-permute-done.11 = bf16[24,1024]{1,0:T(8,128)(2,1)S(1)} collective-permute-done((bf16[24,1024]{1,0:T(8,128)(2,1)S(1)}, bf16[24,1024]{1,0:T(8,128)(2,1)S(1)}, u32[]{:S(2)}, u32[]{:S(2)}) %collective-permute-start.11) | collective-permute-done | bytes 49184 | tf_op jit(solution)/shard_map/ppermute | solution.py:356
  38.1 2.9 %collective-permute-start.15 = (bf16[24,1024]{1,0:T(8,128)(2,1)S(1)}, bf16[24,1024]{1,0:T(8,128)(2,1)S(1)}, u32[]{:S(2)}, u32[]{:S(2)}) collective-permute-start(bf16[24,1024]{1,0:T(8,128)(2,1)S(1)} %add_convert_fusion.5.refs_8_), channel_id=1, source_target_pairs={{0,18},{1,19},{2,16},{3,17},{16,2},{17,3},{18,0},{19,1},{4,22},{5,... | collective-permute-start | bytes 147464 | tf_op jit(solution)/shard_map/ppermute | solution.py:356
  41.0 0.3 collective-permute-start.14
  41.3 0.1 collective-permute-start.13
  41.4 0.8 %collective-permute-done.22 = bf16[2,24,1024]{2,1,0:T(8,128)(2,1)S(1)} collective-permute-done((bf16[2,24,1024]{2,1,0:T(8,128)(2,1)S(1)}, bf16[2,24,1024]{2,1,0:T(8,128)(2,1)S(1)}, u32[]{:S(2)}, u32[]{:S(2)}) %collective-permute-start.22) | collective-permute-done | bytes 98336 | tf_op jit(solution)/shard_map/ppermute | solution.py:356
  42.3 0.2 collective-permute-start.23
  42.4 0.4 collective-permute-start.16
  42.8 0.5 collective-permute-done.15.refs_11_
  43.3 1.8 %collective-permute-done.14.refs_10_ = bf16[24,1024]{1,0:T(8,128)(2,1)S(1)} collective-permute-done((bf16[24,1024]{1,0:T(8,128)(2,1)S(1)}, bf16[24,1024]{1,0:T(8,128)(2,1)S(1)}, u32[]{:S(2)}, u32[]{:S(2)}) %collective-permute-start.14) | collective-permute-done | bytes 49184 | tf_op jit(solution)/shard_map/ppermute | solution.py:356
  45.1 0.1 collective-permute-start.18
  45.2 0.4 collective-permute-start.17
  45.6 0.7 %collective-permute-done.18.refs_14_ = bf16[24,1024]{1,0:T(8,128)(2,1)S(1)} collective-permute-done((bf16[24,1024]{1,0:T(8,128)(2,1)S(1)}, bf16[24,1024]{1,0:T(8,128)(2,1)S(1)}, u32[]{:S(2)}, u32[]{:S(2)}) %collective-permute-start.18) | collective-permute-done | bytes 49184 | tf_op jit(solution)/shard_map/ppermute | solution.py:359
  46.3 0.2 collective-permute-done.17.refs_13_
  46.5 1.7 %finish.1 = (bf16[24,4096]{1,0:T(8,128)(2,1)}, bf16[24,4096]{1,0:T(8,128)(2,1)}, bf16[24,128]{1,0:T(8,128)(2,1)}, bf16[128,2048]{1,0:T(8,128)(2,1)}) custom-call(bf16[24,4096]{1,0:T(8,128)(2,1)S(1)} %copy-done, bf16[24,2048]{1,0:T(8,128)(2,1)S(1)} %collective-permute-done.refs_0_.refs_1_, bf16[24,2048]{1,0:T(8,128)(2,1)S(1)} %collective-permute-done.1.refs_0_.refs_2_, ...), custom_call_target="tpu_custom_call" | custom-call | bytes 6291456 | tf_op jit(solution)/shard_map/finish/pallas_call | solution.py:331
  (43 shorter events, 0.3 us)
Async XLA Ops:
  0.6 6.9 %slice-start.2 = ((s8[6291456]{0:T(1024)(128)(4,1)}), s8[4194304]{0:T(1024)(128)(4,1)S(1)}, s32[]{:S(2)}) async-start(s8[6291456]{0:T(1024)(128)(4,1)} %bitcast.18), calls=%async_computation.2 | async-start | bytes 8388608
  0.6 6.9 %slice-start.4 = ((s8[6291456]{0:T(1024)(128)(4,1)}), s8[4194304]{0:T(1024)(128)(4,1)S(1)}, s32[]{:S(2)}) async-start(s8[6291456]{0:T(1024)(128)(4,1)} %bitcast.25), calls=%async_computation.4 | async-start | bytes 8388608
  1.7 5.8 %collective-permute-start = (bf16[24,2048]{1,0:T(8,128)(2,1)S(1)}, bf16[24,2048]{1,0:T(8,128)(2,1)S(1)}, u32[]{:S(2)}, u32[]{:S(2)}) collective-permute-start(bf16[24,2048]{1,0:T(8,128)(2,1)S(1)} %cut.1), channel_id=1, source_target_pairs={{0,16},{1,17},{16,0},{17,1},{2,18},{3,19},{18,2},{19,3},{4,20},{5,... | collective-permute-start | bytes 294920 | tf_op jit(solution)/shard_map/ppermute | solution.py:356
  4.7 2.8 %slice-start.3 = ((s8[6291456]{0:T(1024)(128)(4,1)}), s8[2097152]{0:T(1024)(128)(4,1)S(1)}, s32[]{:S(2)}) async-start(s8[6291456]{0:T(1024)(128)(4,1)} %bitcast.18), calls=%async_computation.3 | async-start | bytes 4194304
  4.7 2.8 %slice-start.5 = ((s8[6291456]{0:T(1024)(128)(4,1)}), s8[2097152]{0:T(1024)(128)(4,1)S(1)}, s32[]{:S(2)}) async-start(s8[6291456]{0:T(1024)(128)(4,1)} %bitcast.25), calls=%async_computation.5 | async-start | bytes 4194304
  4.7 2.8 %copy-start = (bf16[24,4096]{1,0:T(8,128)(2,1)S(1)}, bf16[24,4096]{1,0:T(8,128)(2,1)}, u32[]{:S(2)}) copy-start(bf16[24,4096]{1,0:T(8,128)(2,1)} %refs_0_.3) | copy-start | bytes 589828
  4.7 2.8 %copy-start.3 = (f32[4096]{0:T(1024)S(1)}, f32[4096]{0:T(1024)}, u32[]{:S(2)}) copy-start(f32[4096]{0:T(1024)} %param.11) | copy-start | bytes 49156
  5.9 4.8 %collective-permute-start.2 = (bf16[24,2304]{1,0:T(8,128)(2,1)S(1)}, bf16[24,2304]{1,0:T(8,128)(2,1)S(1)}, u32[]{:S(2)}, u32[]{:S(2)}) collective-permute-start(bf16[24,2304]{1,0:T(8,128)(2,1)S(1)} %gates.1.refs_0_.refs_3_.refs_6_), channel_id=1, source_target_pairs={{0,16},{1,17},{16,0},{17,1},{2,18},{3,19},{18,2},{19,3},{4,20},{5,... | collective-permute-start | bytes 331784 | tf_op jit(solution)/shard_map/ppermute | solution.py:356
  7.5 1.3 %collective-permute-start.1 = (bf16[24,2048]{1,0:T(8,128)(2,1)S(1)}, bf16[24,2048]{1,0:T(8,128)(2,1)S(1)}, u32[]{:S(2)}, u32[]{:S(2)}) collective-permute-start(bf16[24,2048]{1,0:T(8,128)(2,1)S(1)} %collective-permute-done.refs_0_.refs_1_), channel_id=1, source_target_pairs={{0,1},{1,0},{2,3},{3,2},{4,5},{5,4},{6,7},{7,6},{8,9},{9,8},{10,11... | collective-permute-start | bytes 294920 | tf_op jit(solution)/shard_map/ppermute | solution.py:359
  7.6 3.1 %slice-start = ((s8[6291456]{0:T(1024)(128)(4,1)}), s8[4194304]{0:T(1024)(128)(4,1)S(1)}, s32[]{:S(2)}) async-start(s8[6291456]{0:T(1024)(128)(4,1)} %bitcast.11), calls=%async_computation | async-start | bytes 8388608
  8.8 1.9 %slice-start.1 = ((s8[6291456]{0:T(1024)(128)(4,1)}), s8[2097152]{0:T(1024)(128)(4,1)S(1)}, s32[]{:S(2)}) async-start(s8[6291456]{0:T(1024)(128)(4,1)} %bitcast.11), calls=%async_computation.1 | async-start | bytes 4194304
  10.7 2.6 %copy-start.1 = (bf16[24,4096]{1,0:T(8,128)(2,1)S(1)}, bf16[24,4096]{1,0:T(8,128)(2,1)}, u32[]{:S(2)}) copy-start(bf16[24,4096]{1,0:T(8,128)(2,1)} %refs_3_.1) | copy-start | bytes 589828
  11.4 2.7 %collective-permute-start.4 = (bf16[2,2,24,1024]{3,2,1,0:T(8,128)(2,1)S(1)}, bf16[2,2,24,1024]{3,2,1,0:T(8,128)(2,1)S(1)}, u32[]{:S(2)}, u32[]{:S(2)}) collective-permute-start(bf16[2,2,24,1024]{3,2,1,0:T(8,128)(2,1)S(1)} %outward_send.1.refs_4_), channel_id=1, source_target_pairs={{0,1},{1,0},{2,3},{3,2},{4,5},{5,4},{6,7},{7,6},{8,9},{9,8},{10,11... | collective-permute-start | bytes 589832 | tf_op jit(solution)/shard_map/ppermute | solution.py:359
  11.9 1.3 %collective-permute-start.3 = (bf16[24,2304]{1,0:T(8,128)(2,1)S(1)}, bf16[24,2304]{1,0:T(8,128)(2,1)S(1)}, u32[]{:S(2)}, u32[]{:S(2)}) collective-permute-start(bf16[24,2304]{1,0:T(8,128)(2,1)S(1)} %collective-permute-done.2.refs_1_.refs_4_.refs_7_), channel_id=1, source_target_pairs={{0,1},{1,0},{2,3},{3,2},{4,5},{5,4},{6,7},{7,6},{8,9},{9,8},{10,11... | collective-permute-start | bytes 331784 | tf_op jit(solution)/shard_map/ppermute | solution.py:359
  14.2 6.0 %collective-permute-start.5 = (bf16[2,24,1024]{2,1,0:T(8,128)(2,1)S(1)}, bf16[2,24,1024]{2,1,0:T(8,128)(2,1)S(1)}, u32[]{:S(2)}, u32[]{:S(2)}) collective-permute-start(bf16[2,24,1024]{2,1,0:T(8,128)(2,1)S(1)} %get-tuple-element.50), channel_id=1, source_target_pairs={{0,17},{1,16},{16,1},{17,0},{2,19},{3,18},{18,3},{19,2},{4,21},{5,... | collective-permute-start | bytes 294920 | tf_op jit(solution)/shard_map/ppermute | solution.py:356
  20.0 2.3 %collective-permute-start.6 = (bf16[2,2,24,1024]{3,2,1,0:T(8,128)(2,1)S(1)}, bf16[2,2,24,1024]{3,2,1,0:T(8,128)(2,1)S(1)}, u32[]{:S(2)}, u32[]{:S(2)}) collective-permute-start(bf16[2,2,24,1024]{3,2,1,0:T(8,128)(2,1)S(1)} %get-tuple-element.42), channel_id=1, source_target_pairs={{0,1},{1,0},{2,3},{3,2},{4,5},{5,4},{6,7},{7,6},{8,9},{9,8},{10,11... | collective-permute-start | bytes 589832 | tf_op jit(solution)/shard_map/ppermute | solution.py:359
  20.3 26.2 %copy-start.2 = (bf16[128,4096]{1,0:T(8,128)(2,1)S(1)}, bf16[128,4096]{1,0:T(8,128)(2,1)}, u32[]{:S(2)}) copy-start(bf16[128,4096]{1,0:T(8,128)(2,1)} %refs_20_.1) | copy-start | bytes 3145732
  22.4 5.0 %collective-permute-start.20 = (bf16[2,24,1024]{2,1,0:T(8,128)(2,1)S(1)}, bf16[2,24,1024]{2,1,0:T(8,128)(2,1)S(1)}, u32[]{:S(2)}, u32[]{:S(2)}) collective-permute-start(bf16[2,24,1024]{2,1,0:T(8,128)(2,1)S(1)} %get-tuple-element.48), channel_id=1, source_target_pairs={{0,3},{1,2},{2,1},{3,0},{4,7},{5,6},{6,5},{7,4},{8,11},{9,10},{10,... | collective-permute-start | bytes 294920 | tf_op jit(solution)/shard_map/ppermute | solution.py:356
  23.5 5.1 %collective-permute-start.7 = (bf16[24,1024]{1,0:T(8,128)(2,1)S(1)}, bf16[24,1024]{1,0:T(8,128)(2,1)S(1)}, u32[]{:S(2)}, u32[]{:S(2)}) collective-permute-start(bf16[24,1024]{1,0:T(8,128)(2,1)S(1)} %get-tuple-element.45), channel_id=1, source_target_pairs={{0,18},{1,19},{2,16},{3,17},{16,2},{17,3},{18,0},{19,1},{4,22},{5,... | collective-permute-start | bytes 147464 | tf_op jit(solution)/shard_map/ppermute | solution.py:356
  24.8 3.9 %collective-permute-start.8 = (bf16[24,1024]{1,0:T(8,128)(2,1)S(1)}, bf16[24,1024]{1,0:T(8,128)(2,1)S(1)}, u32[]{:S(2)}, u32[]{:S(2)}) collective-permute-start(bf16[24,1024]{1,0:T(8,128)(2,1)S(1)} %get-tuple-element.46), channel_id=1, source_target_pairs={{0,17},{1,16},{2,19},{3,18},{16,1},{17,0},{18,3},{19,2},{4,21},{5,... | collective-permute-start | bytes 147464 | tf_op jit(solution)/shard_map/ppermute | solution.py:356
  25.4 3.8 %collective-permute-start.9 = (bf16[24,1024]{1,0:T(8,128)(2,1)S(1)}, bf16[24,1024]{1,0:T(8,128)(2,1)S(1)}, u32[]{:S(2)}, u32[]{:S(2)}) collective-permute-start(bf16[24,1024]{1,0:T(8,128)(2,1)S(1)} %get-tuple-element.47), channel_id=1, source_target_pairs={{0,3},{1,2},{2,1},{3,0},{16,19},{17,18},{18,17},{19,16},{4,7},{5,6... | collective-permute-start | bytes 147464 | tf_op jit(solution)/shard_map/ppermute | solution.py:356
  27.4 6.0 %collective-permute-start.21 = (bf16[2,24,1024]{2,1,0:T(8,128)(2,1)S(1)}, bf16[2,24,1024]{2,1,0:T(8,128)(2,1)S(1)}, u32[]{:S(2)}, u32[]{:S(2)}) collective-permute-start(bf16[2,24,1024]{2,1,0:T(8,128)(2,1)S(1)} %add_convert_fusion.3), channel_id=1, source_target_pairs={{0,5},{1,4},{4,1},{5,0},{8,13},{9,12},{12,9},{13,8},{2,7},{3,6},{6... | collective-permute-start | bytes 294920 | tf_op jit(solution)/shard_map/ppermute | solution.py:356
  29.2 6.5 %collective-permute-start.12 = (bf16[24,1024]{1,0:T(8,128)(2,1)S(1)}, bf16[24,1024]{1,0:T(8,128)(2,1)S(1)}, u32[]{:S(2)}, u32[]{:S(2)}) collective-permute-start(bf16[24,1024]{1,0:T(8,128)(2,1)S(1)} %add_convert_fusion.6), channel_id=1, source_target_pairs={{0,12},{1,13},{4,8},{5,9},{8,4},{9,5},{12,0},{13,1},{2,14},{3,15},... | collective-permute-start | bytes 147464 | tf_op jit(solution)/shard_map/ppermute | solution.py:356
  33.0 5.1 %collective-permute-start.11 = (bf16[24,1024]{1,0:T(8,128)(2,1)S(1)}, bf16[24,1024]{1,0:T(8,128)(2,1)S(1)}, u32[]{:S(2)}, u32[]{:S(2)}) collective-permute-start(bf16[24,1024]{1,0:T(8,128)(2,1)S(1)} %add_convert_fusion.6), channel_id=1, source_target_pairs={{0,9},{1,8},{4,13},{5,12},{8,1},{9,0},{12,5},{13,4},{2,11},{3,10},... | collective-permute-start | bytes 147464 | tf_op jit(solution)/shard_map/ppermute | solution.py:356
  33.0 5.1 %collective-permute-start.10 = (bf16[24,1024]{1,0:T(8,128)(2,1)S(1)}, bf16[24,1024]{1,0:T(8,128)(2,1)S(1)}, u32[]{:S(2)}, u32[]{:S(2)}) collective-permute-start(bf16[24,1024]{1,0:T(8,128)(2,1)S(1)} %add_convert_fusion.6), channel_id=1, source_target_pairs={{0,5},{1,4},{4,1},{5,0},{8,13},{9,12},{12,9},{13,8},{2,7},{3,6},{6... | collective-permute-start | bytes 147464 | tf_op jit(solution)/shard_map/ppermute | solution.py:356
  33.4 8.8 %collective-permute-start.22 = (bf16[2,24,1024]{2,1,0:T(8,128)(2,1)S(1)}, bf16[2,24,1024]{2,1,0:T(8,128)(2,1)S(1)}, u32[]{:S(2)}, u32[]{:S(2)}) collective-permute-start(bf16[2,24,1024]{2,1,0:T(8,128)(2,1)S(1)} %add_convert_fusion.2), channel_id=1, source_target_pairs={{0,9},{1,8},{4,13},{5,12},{8,1},{9,0},{12,5},{13,4},{2,11},{3,10},... | collective-permute-start | bytes 294920 | tf_op jit(solution)/shard_map/ppermute | solution.py:356
  38.1 5.2 %collective-permute-start.15 = (bf16[24,1024]{1,0:T(8,128)(2,1)S(1)}, bf16[24,1024]{1,0:T(8,128)(2,1)S(1)}, u32[]{:S(2)}, u32[]{:S(2)}) collective-permute-start(bf16[24,1024]{1,0:T(8,128)(2,1)S(1)} %add_convert_fusion.5.refs_8_), channel_id=1, source_target_pairs={{0,18},{1,19},{2,16},{3,17},{16,2},{17,3},{18,0},{19,1},{4,22},{5,... | collective-permute-start | bytes 147464 | tf_op jit(solution)/shard_map/ppermute | solution.py:356
  41.0 4.0 %collective-permute-start.14 = (bf16[24,1024]{1,0:T(8,128)(2,1)S(1)}, bf16[24,1024]{1,0:T(8,128)(2,1)S(1)}, u32[]{:S(2)}, u32[]{:S(2)}) collective-permute-start(bf16[24,1024]{1,0:T(8,128)(2,1)S(1)} %add_convert_fusion.5.refs_8_), channel_id=1, source_target_pairs={{0,17},{1,16},{2,19},{3,18},{16,1},{17,0},{18,3},{19,2},{4,21},{5,... | collective-permute-start | bytes 147464 | tf_op jit(solution)/shard_map/ppermute | solution.py:356
  41.3 3.9 %collective-permute-start.13 = (bf16[24,1024]{1,0:T(8,128)(2,1)S(1)}, bf16[24,1024]{1,0:T(8,128)(2,1)S(1)}, u32[]{:S(2)}, u32[]{:S(2)}) collective-permute-start(bf16[24,1024]{1,0:T(8,128)(2,1)S(1)} %add_convert_fusion.5.refs_8_), channel_id=1, source_target_pairs={{0,3},{1,2},{2,1},{3,0},{16,19},{17,18},{18,17},{19,16},{4,7},{5,6... | collective-permute-start | bytes 147464 | tf_op jit(solution)/shard_map/ppermute | solution.py:356
  42.3 4.2 %collective-permute-start.23 = (bf16[2,24,1024]{2,1,0:T(8,128)(2,1)S(1)}, bf16[2,24,1024]{2,1,0:T(8,128)(2,1)S(1)}, u32[]{:S(2)}, u32[]{:S(2)}) collective-permute-start(bf16[2,24,1024]{2,1,0:T(8,128)(2,1)S(1)} %add_convert_fusion.1.refs_16_), channel_id=1, source_target_pairs={{0,1},{1,0},{2,3},{3,2},{4,5},{5,4},{6,7},{7,6},{8,9},{9,8},{10,11... | collective-permute-start | bytes 294920 | tf_op jit(solution)/shard_map/ppermute | solution.py:359
  42.4 3.2 %collective-permute-start.16 = (bf16[24,1024]{1,0:T(8,128)(2,1)S(1)}, bf16[24,1024]{1,0:T(8,128)(2,1)S(1)}, u32[]{:S(2)}, u32[]{:S(2)}) collective-permute-start(bf16[24,1024]{1,0:T(8,128)(2,1)S(1)} %add_convert_fusion.5.refs_8_), channel_id=1, source_target_pairs={{0,1},{1,0},{2,3},{3,2},{4,5},{5,4},{6,7},{7,6},{8,9},{9,8},{10,11... | collective-permute-start | bytes 147464 | tf_op jit(solution)/shard_map/ppermute | solution.py:359
  43.3 2.3 %collective-permute-start.19 = (bf16[24,1024]{1,0:T(8,128)(2,1)S(1)}, bf16[24,1024]{1,0:T(8,128)(2,1)S(1)}, u32[]{:S(2)}, u32[]{:S(2)}) collective-permute-start(bf16[24,1024]{1,0:T(8,128)(2,1)S(1)} %collective-permute-done.15.refs_11_), channel_id=1, source_target_pairs={{0,1},{1,0},{2,3},{3,2},{4,5},{5,4},{6,7},{7,6},{8,9},{9,8},{10,11... | collective-permute-start | bytes 147464 | tf_op jit(solution)/shard_map/ppermute | solution.py:359
  45.1 1.2 %collective-permute-start.18 = (bf16[24,1024]{1,0:T(8,128)(2,1)S(1)}, bf16[24,1024]{1,0:T(8,128)(2,1)S(1)}, u32[]{:S(2)}, u32[]{:S(2)}) collective-permute-start(bf16[24,1024]{1,0:T(8,128)(2,1)S(1)} %collective-permute-done.14.refs_10_), channel_id=1, source_target_pairs={{0,1},{1,0},{2,3},{3,2},{4,5},{5,4},{6,7},{7,6},{8,9},{9,8},{10,11... | collective-permute-start | bytes 147464 | tf_op jit(solution)/shard_map/ppermute | solution.py:359
  45.2 1.3 %collective-permute-start.17 = (bf16[24,1024]{1,0:T(8,128)(2,1)S(1)}, bf16[24,1024]{1,0:T(8,128)(2,1)S(1)}, u32[]{:S(2)}, u32[]{:S(2)}) collective-permute-start(bf16[24,1024]{1,0:T(8,128)(2,1)S(1)} %collective-permute-done.13.refs_9_), channel_id=1, source_target_pairs={{0,1},{1,0},{2,3},{3,2},{4,5},{5,4},{6,7},{7,6},{8,9},{9,8},{10,11... | collective-permute-start | bytes 147464 | tf_op jit(solution)/shard_map/ppermute | solution.py:359

commit v14 on v13

--- a/solution.py
+++ b/solution.py
@@ -262,8 +262,19 @@
 def join_kernel(n_dp, in_keep, in_other, out_block, *refs):
     for t in range(2 * n_dp):
         k, j = t // 2, t % 2
-        refs[t][...] = (in_keep[k, j].astype(F32) + in_other[k, j].astype(F32)).astype(BF16)
+        total = (in_keep[k, j].astype(F32) + in_other[k, j].astype(F32)).astype(BF16)
+        if t == 1:
+            refs[t][0] = total
+        else:
+            refs[t][...] = total
+    for j in range(2):
+        refs[1][1 + j] = out_block[j]
     refs[-1][...] = out_block[...]
+
+
+def flip_add_kernel(n_dp, own, arrived, target):
+    for j in range(2):
+        target[j] = (own[j].astype(F32) + arrived[2 - j].astype(F32)).astype(BF16)
 
 
 def finish_kernel(n_dp, *refs):
@@ -434,13 +445,15 @@
         functools.partial(inward_kernel, 0), n_dp, back_grads + [wg, wu, out_block], [shares, block], [],
         weights, "inward_keep",
     )
+    piece, three = ((rows, chunk), BF16), ((3, rows, chunk), BF16)
     *in_pieces, out_block = run(
-        join_kernel, n_dp, [in_keep, in_other, out_block], [((rows, chunk), BF16)] * (2 * n_dp) + [block], [],
-        rows * width, "join",
+        join_kernel, n_dp, [in_keep, in_other, out_block],
+        [three if t == 1 else piece for t in range(2 * n_dp)] + [block], [], rows * width, "join",
     )
     turns = [t for t in range(2 * n_dp - 1, 0, -1)]
-    in_share = total_of([in_pieces[0]] + [swap(in_pieces[t], ("dp", "y"), t) for t in turns])
-    out_total = add(out_block, swap(out_block, ("y",), 1)[::-1])
+    arrived = {t: swap(in_pieces[t], ("dp", "y"), t) for t in turns[::-1]}
+    (out_total,) = run(flip_add_kernel, n_dp, [out_block, arrived[1]], [block], [], rows * width, "flip_add")
+    in_share = total_of([in_pieces[0], arrived[1][0]] + [arrived[t] for t in turns[:-1]])
     in_total = total_of([in_share] + [swap(in_share, ("hi",), t) for t in range(1, n_hi)])
     turn = 1
     while turn < n_hi:

time: 48.4 us -> 49.2 us (1.017)
  waiting for transfers between devices: 9.99 us -> 12.2 us
  starting transfers between devices: 23 us -> 21.6 us
    ppermute x15 -> x14, waiting for transfers between devices: 8.55 us -> 10.7 us  [swap(): lax.ppermute(value, axes + ('c',), [(i, i ^ turn) for i in range(count)])]
    ppermute x15 -> x14, starting transfers between devices: 21 us -> 19.6 us  [swap(): lax.ppermute(value, axes + ('c',), [(i, i ^ turn) for i in range(count)])]
    pallas_call x12 -> x13, Pallas kernels: 14.1 us -> 14.1 us  [run(): pl.pallas_call(functools.partial(kernel, n_dp), out_shape=kinds, in_specs...]
  transfers between devices with their start and end apart: 24 -> 23, of which waited for: 13 -> 11; matrix products, arithmetic and copies ran while one was open for 0% -> 0% of each run, Pallas kernels for 22% -> 21%
where the time goes in v14:
time: 49.2 us; the launch traced here: 49.1 us
  starting transfers between devices  21.6 us (44%)
  Pallas kernels  14.1 us (29%)
  waiting for transfers between devices  12.2 us (25%)
  between operations  0.89 us (2%)
    ppermute x14, starting transfers between devices, swap(): lax.ppermute(value, axes + ('c',), [(i, i ^ turn) for i in range(count)])  19.6 us
    pallas_call x13, Pallas kernels, run(): pl.pallas_call(functools.partial(kernel, n_dp), out_shape=kinds, in_specs...  14.1 us
    ppermute x14, waiting for transfers between devices, swap(): lax.ppermute(value, axes + ('c',), [(i, i ^ turn) for i in range(count)])  10.7 us
    ppermute x9, starting transfers between devices, other_core(): return lax.ppermute(value, ('c',), [(0, 1), (1, 0)])  2.03 us
    ppermute x9, waiting for transfers between devices, other_core(): return lax.ppermute(value, ('c',), [(0, 1), (1, 0)])  1.45 us
  transfers between devices with their start and end apart: 23, of which 11 were waited for; matrix products, arithmetic and copies ran while one was open for 0% of the time, Pallas kernels for 21%

profile of v14, /device:TPU:0, one launch (start us, length us, event | category | flops | bytes accessed | tf_op | source)
XLA Modules:
  0.0 49.1 jit_solution(9388220991937486486)
XLA Ops:
  0.6 0.0 slice-start.2
  0.7 1.1 %cut.1 = bf16[24,2048]{1,0:T(8,128)(2,1)S(1)} custom-call(bf16[24,4096]{1,0:T(8,128)(2,1)} %refs_0_.3), custom_call_target="tpu_custom_call" | custom-call | bytes 98304 | tf_op jit(solution)/shard_map/cut/pallas_call | solution.py:342
  1.7 3.0 %collective-permute-start = (bf16[24,2048]{1,0:T(8,128)(2,1)S(1)}, bf16[24,2048]{1,0:T(8,128)(2,1)S(1)}, u32[]{:S(2)}, u32[]{:S(2)}) collective-permute-start(bf16[24,2048]{1,0:T(8,128)(2,1)S(1)} %cut.1), channel_id=1, source_target_pairs={{0,16},{1,17},{16,0},{17,1},{2,18},{3,19},{18,2},{19,3},{4,20},{5,... | collective-permute-start | bytes 294920 | tf_op jit(solution)/shard_map/ppermute | solution.py:367
  4.7 1.1 %gates.1.refs_0_.refs_3_.refs_6_ = bf16[24,2304]{1,0:T(8,128)(2,1)S(1)} custom-call(s32[8,24]{1,0:T(8,128)} %bitcast.39, f32[8,24]{1,0:T(8,128)} %bitcast.40, bf16[24,128]{1,0:T(8,128)(2,1)} %context.1, bf16[24,4096]{1,0:T(8,128)(2,1)} %refs_3_.1, bf16[4096,768]{1,0:T(8,128)(2,1)} %bitcast.22, bf16[4096,768]{1,0:T(8,128)(2,1)} %bitcast.29, ...), custom_call_target="tpu_custom_call" | custom-call | bytes 25165824 | tf_op jit(solution)/shard_map/gates/pallas_call | solution.py:342
  5.9 0.6 %collective-permute-start.2 = (bf16[24,2304]{1,0:T(8,128)(2,1)S(1)}, bf16[24,2304]{1,0:T(8,128)(2,1)S(1)}, u32[]{:S(2)}, u32[]{:S(2)}) collective-permute-start(bf16[24,2304]{1,0:T(8,128)(2,1)S(1)} %gates.1.refs_0_.refs_3_.refs_6_), channel_id=1, source_target_pairs={{0,16},{1,17},{16,0},{17,1},{2,18},{3,19},{18,2},{19,3},{4,20},{5,... | collective-permute-start | bytes 331784 | tf_op jit(solution)/shard_map/ppermute | solution.py:367
  6.4 1.1 %collective-permute-done.refs_0_.refs_1_ = bf16[24,2048]{1,0:T(8,128)(2,1)S(1)} collective-permute-done((bf16[24,2048]{1,0:T(8,128)(2,1)S(1)}, bf16[24,2048]{1,0:T(8,128)(2,1)S(1)}, u32[]{:S(2)}, u32[]{:S(2)}) %collective-permute-start) | collective-permute-done | bytes 98336 | tf_op jit(solution)/shard_map/ppermute | solution.py:367
  7.6 1.2 %hidden_first.1 = (f32[48,768]{1,0:T(8,128)S(1)}, f32[48,768]{1,0:T(8,128)S(1)}, f32[48,128]{1,0:T(8,128)S(1)}) custom-call(bf16[24,4096]{1,0:T(8,128)(2,1)S(1)} %copy-done, bf16[24,2048]{1,0:T(8,128)(2,1)S(1)} %collective-permute-done.refs_0_.refs_1_, f32[1,4096]{1,0:T(1,128)S(1)} %bitcast.36, bf16[4096,768]{1,0:T(8,128)(2,1)S(1)} %bitcast.25, ...), custom_call_target="tpu_custom_call" | custom-call | bytes 6291456 | tf_op jit(solution)/shard_map/hidden_first/pallas_call | solution.py:342
  8.8 0.0 collective-permute-done.1.refs_0_.refs_2_
  8.8 0.0 slice-start.1
  8.8 1.2 %hidden_rest.1 = (f32[48,768]{1,0:T(8,128)S(1)}, f32[48,768]{1,0:T(8,128)S(1)}, bf16[48,768]{1,0:T(8,128)(2,1)S(1)}, f32[48,128]{1,0:T(8,128)S(1)}) custom-call(bf16[24,4096]{1,0:T(8,128)(2,1)S(1)} %copy-done, bf16[24,2048]{1,0:T(8,128)(2,1)S(1)} %collective-permute-done.1.refs_0_.refs_2_, f32[1,4096]{1,0:T(1,128)S(1)} %bitcast.37, ...), custom_call_target="tpu_custom_call" | custom-call | bytes 6291456 | tf_op jit(solution)/shard_map/hidden_rest/pallas_call | solution.py:342
  10.1 0.6 %collective-permute-done.2.refs_1_.refs_4_.refs_7_ = bf16[24,2304]{1,0:T(8,128)(2,1)S(1)} collective-permute-done((bf16[24,2304]{1,0:T(8,128)(2,1)S(1)}, bf16[24,2304]{1,0:T(8,128)(2,1)S(1)}, u32[]{:S(2)}, u32[]{:S(2)}) %collective-permute-start.2) | collective-permute-done | bytes 110624 | tf_op jit(solution)/shard_map/ppermute | solution.py:367
  10.7 0.7 %outward_send.1.refs_4_ = bf16[2,2,24,1024]{3,2,1,0:T(8,128)(2,1)S(1)} custom-call(bf16[24,2304]{1,0:T(8,128)(2,1)S(1)} %gates.1.refs_0_.refs_3_.refs_6_, bf16[24,2304]{1,0:T(8,128)(2,1)S(1)} %collective-permute-done.2.refs_1_.refs_4_.refs_7_, bf16[48,768]{1,0:T(8,128)(2,1)S(1)} %get-tuple-element.32.refs_2_, bf16[768,4096]{1,0:T(8,128)(2,1)S(1)} %bitcast.18), custom_call_target="tpu_custom_call" | custom-call | bytes 3145728 | tf_op jit(solution)/shard_map/outward_send/pallas_call | solution.py:342
  11.4 0.5 %collective-permute-start.4 = (bf16[2,2,24,1024]{3,2,1,0:T(8,128)(2,1)S(1)}, bf16[2,2,24,1024]{3,2,1,0:T(8,128)(2,1)S(1)}, u32[]{:S(2)}, u32[]{:S(2)}) collective-permute-start(bf16[2,2,24,1024]{3,2,1,0:T(8,128)(2,1)S(1)} %outward_send.1.refs_4_), channel_id=1, source_target_pairs={{0,1},{1,0},{2,3},{3,2},{4,5},{5,4},{6,7},{7,6},{8,9},{9,8},{10,11... | collective-permute-start | bytes 589832 | tf_op jit(solution)/shard_map/ppermute | solution.py:370
  11.9 0.1 collective-permute-start.3
  12.0 0.7 %outward_keep.1.refs_8_ = bf16[2,2,24,1024]{3,2,1,0:T(8,128)(2,1)S(1)} custom-call(bf16[24,2304]{1,0:T(8,128)(2,1)S(1)} %gates.1.refs_0_.refs_3_.refs_6_, bf16[24,2304]{1,0:T(8,128)(2,1)S(1)} %collective-permute-done.2.refs_1_.refs_4_.refs_7_, bf16[48,768]{1,0:T(8,128)(2,1)S(1)} %get-tuple-element.32.refs_2_, bf16[768,4096]{1,0:T(8,128)(2,1)S(1)} %bitcast.19, ...), custom_call_target="tpu_custom_call" | custom-call | bytes 3145728 | tf_op jit(solution)/shard_map/outward_keep/pallas_call | solution.py:342
  12.7 0.6 %collective-permute-done.3.refs_2_.refs_5_ = bf16[24,2304]{1,0:T(8,128)(2,1)S(1)} collective-permute-done((bf16[24,2304]{1,0:T(8,128)(2,1)S(1)}, bf16[24,2304]{1,0:T(8,128)(2,1)S(1)}, u32[]{:S(2)}, u32[]{:S(2)}) %collective-permute-start.3) | collective-permute-done | bytes 110624 | tf_op jit(solution)/shard_map/ppermute | solution.py:370
  13.3 0.9 %backward_first.1 = (bf16[48,256]{1,0:T(8,128)(2,1)S(1)}, bf16[48,256]{1,0:T(8,128)(2,1)S(1)}, bf16[48,4096]{1,0:T(8,128)(2,1)S(1)}, bf16[2,2,24,1024]{3,2,1,0:T(8,128)(2,1)S(1)}) custom-call(bf16[24,4096]{1,0:T(8,128)(2,1)S(1)} %copy-done.1, bf16[24,2304]{1,0:T(8,128)(2,1)S(1)} %collective-permute-done.2.refs_1_.refs_4_.refs_7_, ...), custom_call_target="tpu_custom_call" | custom-call | bytes 2097152 | tf_op jit(solution)/shard_map/backward_first/pallas_call | solution.py:342
  14.2 0.1 add_convert_fusion
  14.3 2.3 %collective-permute-start.5 = (bf16[2,24,1024]{2,1,0:T(8,128)(2,1)S(1)}, bf16[2,24,1024]{2,1,0:T(8,128)(2,1)S(1)}, u32[]{:S(2)}, u32[]{:S(2)}) collective-permute-start(bf16[2,24,1024]{2,1,0:T(8,128)(2,1)S(1)} %get-tuple-element.50), channel_id=1, source_target_pairs={{0,17},{1,16},{16,1},{17,0},{2,19},{3,18},{18,3},{19,2},{4,21},{5,... | collective-permute-start | bytes 294920 | tf_op jit(solution)/shard_map/ppermute | solution.py:367
  16.6 1.4 %backward_rest.1 = (bf16[48,512]{1,0:T(8,128)(2,1)S(1)}, bf16[48,512]{1,0:T(8,128)(2,1)S(1)}, bf16[2,24,1024]{2,1,0:T(8,128)(2,1)S(1)}) custom-call(bf16[48,4096]{1,0:T(8,128)(2,1)S(1)} %get-tuple-element.35.weighted, f32[48,768]{1,0:T(8,128)S(1)} %get-tuple-element.30.refs_5_.pre_gate, f32[48,768]{1,0:T(8,128)S(1)} %get-tuple-element.31.refs_6_.pre_up, ...), custom_call_target="tpu_custom_call" | custom-call | bytes 4194304 | tf_op jit(solution)/shard_map/backward_rest/pallas_call | solution.py:342
  18.0 2.0 %inward_send.1 = (bf16[2,2,24,1024]{3,2,1,0:T(8,128)(2,1)S(1)}, bf16[2,24,1024]{2,1,0:T(8,128)(2,1)S(1)}) custom-call(bf16[48,256]{1,0:T(8,128)(2,1)S(1)} %get-tuple-element.33.refs_0_, bf16[48,256]{1,0:T(8,128)(2,1)S(1)} %get-tuple-element.34.refs_1_, bf16[48,512]{1,0:T(8,128)(2,1)S(1)} %get-tuple-element.37.refs_2_, ...), custom_call_target="tpu_custom_call" | custom-call | bytes 6291456 | tf_op jit(solution)/shard_map/inward_send/pallas_call | solution.py:342
  20.0 0.3 collective-permute-start.6
  20.3 2.0 %inward_keep.1 = (bf16[2,2,24,1024]{3,2,1,0:T(8,128)(2,1)S(1)}, bf16[2,24,1024]{2,1,0:T(8,128)(2,1)S(1)}) custom-call(bf16[48,256]{1,0:T(8,128)(2,1)S(1)} %get-tuple-element.33.refs_0_, bf16[48,256]{1,0:T(8,128)(2,1)S(1)} %get-tuple-element.34.refs_1_, bf16[48,512]{1,0:T(8,128)(2,1)S(1)} %get-tuple-element.37.refs_2_, ...), custom_call_target="tpu_custom_call" | custom-call | bytes 6291456 | tf_op jit(solution)/shard_map/inward_keep/pallas_call | solution.py:342
  22.3 0.1 join.1
  22.4 1.1 %collective-permute-start.7 = (bf16[3,24,1024]{2,1,0:T(8,128)(2,1)S(1)}, bf16[3,24,1024]{2,1,0:T(8,128)(2,1)S(1)}, u32[]{:S(2)}, u32[]{:S(2)}) collective-permute-start(bf16[3,24,1024]{2,1,0:T(8,128)(2,1)S(1)} %get-tuple-element.45), channel_id=1, source_target_pairs={{0,3},{1,2},{2,1},{3,0},{16,19},{17,18},{18,17},{19,16},{4,7},{5,6... | collective-permute-start | bytes 442376 | tf_op jit(solution)/shard_map/ppermute | solution.py:367
  23.5 1.3 %collective-permute-start.8 = (bf16[24,1024]{1,0:T(8,128)(2,1)S(1)}, bf16[24,1024]{1,0:T(8,128)(2,1)S(1)}, u32[]{:S(2)}, u32[]{:S(2)}) collective-permute-start(bf16[24,1024]{1,0:T(8,128)(2,1)S(1)} %get-tuple-element.46), channel_id=1, source_target_pairs={{0,18},{1,19},{2,16},{3,17},{16,2},{17,3},{18,0},{19,1},{4,22},{5,... | collective-permute-start | bytes 147464 | tf_op jit(solution)/shard_map/ppermute | solution.py:367
  24.8 0.5 %collective-permute-start.9 = (bf16[24,1024]{1,0:T(8,128)(2,1)S(1)}, bf16[24,1024]{1,0:T(8,128)(2,1)S(1)}, u32[]{:S(2)}, u32[]{:S(2)}) collective-permute-start(bf16[24,1024]{1,0:T(8,128)(2,1)S(1)} %get-tuple-element.47), channel_id=1, source_target_pairs={{0,17},{1,16},{2,19},{3,18},{16,1},{17,0},{18,3},{19,2},{4,21},{5,... | collective-permute-start | bytes 147464 | tf_op jit(solution)/shard_map/ppermute | solution.py:367
  25.4 3.9 %collective-permute-done.7.arrived = bf16[3,24,1024]{2,1,0:T(8,128)(2,1)S(1)} collective-permute-done((bf16[3,24,1024]{2,1,0:T(8,128)(2,1)S(1)}, bf16[3,24,1024]{2,1,0:T(8,128)(2,1)S(1)}, u32[]{:S(2)}, u32[]{:S(2)}) %collective-permute-start.7) | collective-permute-done | bytes 147488 | tf_op jit(solution)/shard_map/ppermute | solution.py:367
  29.3 1.1 %collective-permute-start.20 = (bf16[2,24,1024]{2,1,0:T(8,128)(2,1)S(1)}, bf16[2,24,1024]{2,1,0:T(8,128)(2,1)S(1)}, u32[]{:S(2)}, u32[]{:S(2)}) collective-permute-start(bf16[2,24,1024]{2,1,0:T(8,128)(2,1)S(1)} %flip_add.1), channel_id=1, source_target_pairs={{0,5},{1,4},{4,1},{5,0},{8,13},{9,12},{12,9},{13,8},{2,7},{3,6},{6... | collective-permute-start | bytes 294920 | tf_op jit(solution)/shard_map/ppermute | solution.py:367
  30.4 2.5 %collective-permute-start.12 = (bf16[24,1024]{1,0:T(8,128)(2,1)S(1)}, bf16[24,1024]{1,0:T(8,128)(2,1)S(1)}, u32[]{:S(2)}, u32[]{:S(2)}) collective-permute-start(bf16[24,1024]{1,0:T(8,128)(2,1)S(1)} %fusion.2), channel_id=1, source_target_pairs={{0,12},{1,13},{4,8},{5,9},{8,4},{9,5},{12,0},{13,1},{2,14},{3,15},... | collective-permute-start | bytes 147464 | tf_op jit(solution)/shard_map/ppermute | solution.py:367
  33.0 0.1 collective-permute-start.11
  33.1 1.5 %collective-permute-start.10 = (bf16[24,1024]{1,0:T(8,128)(2,1)S(1)}, bf16[24,1024]{1,0:T(8,128)(2,1)S(1)}, u32[]{:S(2)}, u32[]{:S(2)}) collective-permute-start(bf16[24,1024]{1,0:T(8,128)(2,1)S(1)} %fusion.2), channel_id=1, source_target_pairs={{0,5},{1,4},{4,1},{5,0},{8,13},{9,12},{12,9},{13,8},{2,7},{3,6},{6... | collective-permute-start | bytes 147464 | tf_op jit(solution)/shard_map/ppermute | solution.py:367
  34.6 2.2 %collective-permute-start.21 = (bf16[2,24,1024]{2,1,0:T(8,128)(2,1)S(1)}, bf16[2,24,1024]{2,1,0:T(8,128)(2,1)S(1)}, u32[]{:S(2)}, u32[]{:S(2)}) collective-permute-start(bf16[2,24,1024]{2,1,0:T(8,128)(2,1)S(1)} %add_convert_fusion.2), channel_id=1, source_target_pairs={{0,9},{1,8},{4,13},{5,12},{8,1},{9,0},{12,5},{13,4},{2,11},{3,10},... | collective-permute-start | bytes 294920 | tf_op jit(solution)/shard_map/ppermute | solution.py:367
  36.8 0.6 %collective-permute-done.12 = bf16[24,1024]{1,0:T(8,128)(2,1)S(1)} collective-permute-done((bf16[24,1024]{1,0:T(8,128)(2,1)S(1)}, bf16[24,1024]{1,0:T(8,128)(2,1)S(1)}, u32[]{:S(2)}, u32[]{:S(2)}) %collective-permute-start.12) | collective-permute-done | bytes 49184 | tf_op jit(solution)/shard_map/ppermute | solution.py:367
  37.4 2.3 %collective-permute-done.11 = bf16[24,1024]{1,0:T(8,128)(2,1)S(1)} collective-permute-done((bf16[24,1024]{1,0:T(8,128)(2,1)S(1)}, bf16[24,1024]{1,0:T(8,128)(2,1)S(1)}, u32[]{:S(2)}, u32[]{:S(2)}) %collective-permute-start.11) | collective-permute-done | bytes 49184 | tf_op jit(solution)/shard_map/ppermute | solution.py:367
  39.8 2.2 %collective-permute-start.15 = (bf16[24,1024]{1,0:T(8,128)(2,1)S(1)}, bf16[24,1024]{1,0:T(8,128)(2,1)S(1)}, u32[]{:S(2)}, u32[]{:S(2)}) collective-permute-start(bf16[24,1024]{1,0:T(8,128)(2,1)S(1)} %add_convert_fusion.4.refs_8_), channel_id=1, source_target_pairs={{0,18},{1,19},{2,16},{3,17},{16,2},{17,3},{18,0},{19,1},{4,22},{5,... | collective-permute-start | bytes 147464 | tf_op jit(solution)/shard_map/ppermute | solution.py:367
  41.9 0.4 collective-permute-start.14
  42.3 0.7 %collective-permute-start.13 = (bf16[24,1024]{1,0:T(8,128)(2,1)S(1)}, bf16[24,1024]{1,0:T(8,128)(2,1)S(1)}, u32[]{:S(2)}, u32[]{:S(2)}) collective-permute-start(bf16[24,1024]{1,0:T(8,128)(2,1)S(1)} %add_convert_fusion.4.refs_8_), channel_id=1, source_target_pairs={{0,3},{1,2},{2,1},{3,0},{16,19},{17,18},{18,17},{19,16},{4,7},{5,6... | collective-permute-start | bytes 147464 | tf_op jit(solution)/shard_map/ppermute | solution.py:367
  43.0 0.5 collective-permute-done.21
  43.5 0.2 collective-permute-start.22
  43.7 0.4 collective-permute-start.16
  44.1 0.7 %collective-permute-done.15.refs_11_ = bf16[24,1024]{1,0:T(8,128)(2,1)S(1)} collective-permute-done((bf16[24,1024]{1,0:T(8,128)(2,1)S(1)}, bf16[24,1024]{1,0:T(8,128)(2,1)S(1)}, u32[]{:S(2)}, u32[]{:S(2)}) %collective-permute-start.15) | collective-permute-done | bytes 49184 | tf_op jit(solution)/shard_map/ppermute | solution.py:367
  44.8 1.1 %collective-permute-done.14.refs_10_ = bf16[24,1024]{1,0:T(8,128)(2,1)S(1)} collective-permute-done((bf16[24,1024]{1,0:T(8,128)(2,1)S(1)}, bf16[24,1024]{1,0:T(8,128)(2,1)S(1)}, u32[]{:S(2)}, u32[]{:S(2)}) %collective-permute-start.14) | collective-permute-done | bytes 49184 | tf_op jit(solution)/shard_map/ppermute | solution.py:367
  45.9 0.1 collective-permute-start.18
  46.0 0.4 collective-permute-start.17
  46.4 0.7 %collective-permute-done.18.refs_14_ = bf16[24,1024]{1,0:T(8,128)(2,1)S(1)} collective-permute-done((bf16[24,1024]{1,0:T(8,128)(2,1)S(1)}, bf16[24,1024]{1,0:T(8,128)(2,1)S(1)}, u32[]{:S(2)}, u32[]{:S(2)}) %collective-permute-start.18) | collective-permute-done | bytes 49184 | tf_op jit(solution)/shard_map/ppermute | solution.py:370
  47.1 0.2 collective-permute-done.17.refs_13_
  47.3 1.7 %finish.1 = (bf16[24,4096]{1,0:T(8,128)(2,1)}, bf16[24,4096]{1,0:T(8,128)(2,1)}, bf16[24,128]{1,0:T(8,128)(2,1)}, bf16[128,2048]{1,0:T(8,128)(2,1)}) custom-call(bf16[24,4096]{1,0:T(8,128)(2,1)S(1)} %copy-done, bf16[24,2048]{1,0:T(8,128)(2,1)S(1)} %collective-permute-done.refs_0_.refs_1_, bf16[24,2048]{1,0:T(8,128)(2,1)S(1)} %collective-permute-done.1.refs_0_.refs_2_, ...), custom_call_target="tpu_custom_call" | custom-call | bytes 6291456 | tf_op jit(solution)/shard_map/finish/pallas_call | solution.py:342
  (41 shorter events, 0.3 us)
Async XLA Ops:
  0.6 6.9 %slice-start.2 = ((s8[6291456]{0:T(1024)(128)(4,1)}), s8[4194304]{0:T(1024)(128)(4,1)S(1)}, s32[]{:S(2)}) async-start(s8[6291456]{0:T(1024)(128)(4,1)} %bitcast.23), calls=%async_computation.2 | async-start | bytes 8388608
  0.6 6.9 %slice-start.4 = ((s8[6291456]{0:T(1024)(128)(4,1)}), s8[4194304]{0:T(1024)(128)(4,1)S(1)}, s32[]{:S(2)}) async-start(s8[6291456]{0:T(1024)(128)(4,1)} %bitcast.30), calls=%async_computation.4 | async-start | bytes 8388608
  1.7 5.8 %collective-permute-start = (bf16[24,2048]{1,0:T(8,128)(2,1)S(1)}, bf16[24,2048]{1,0:T(8,128)(2,1)S(1)}, u32[]{:S(2)}, u32[]{:S(2)}) collective-permute-start(bf16[24,2048]{1,0:T(8,128)(2,1)S(1)} %cut.1), channel_id=1, source_target_pairs={{0,16},{1,17},{16,0},{17,1},{2,18},{3,19},{18,2},{19,3},{4,20},{5,... | collective-permute-start | bytes 294920 | tf_op jit(solution)/shard_map/ppermute | solution.py:367
  4.7 2.8 %slice-start.3 = ((s8[6291456]{0:T(1024)(128)(4,1)}), s8[2097152]{0:T(1024)(128)(4,1)S(1)}, s32[]{:S(2)}) async-start(s8[6291456]{0:T(1024)(128)(4,1)} %bitcast.23), calls=%async_computation.3 | async-start | bytes 4194304
  4.7 2.8 %slice-start.5 = ((s8[6291456]{0:T(1024)(128)(4,1)}), s8[2097152]{0:T(1024)(128)(4,1)S(1)}, s32[]{:S(2)}) async-start(s8[6291456]{0:T(1024)(128)(4,1)} %bitcast.30), calls=%async_computation.5 | async-start | bytes 4194304
  4.7 2.8 %copy-start = (bf16[24,4096]{1,0:T(8,128)(2,1)S(1)}, bf16[24,4096]{1,0:T(8,128)(2,1)}, u32[]{:S(2)}) copy-start(bf16[24,4096]{1,0:T(8,128)(2,1)} %refs_0_.3) | copy-start | bytes 589828
  4.7 2.8 %copy-start.3 = (f32[4096]{0:T(1024)S(1)}, f32[4096]{0:T(1024)}, u32[]{:S(2)}) copy-start(f32[4096]{0:T(1024)} %param.11) | copy-start | bytes 49156
  5.9 4.8 %collective-permute-start.2 = (bf16[24,2304]{1,0:T(8,128)(2,1)S(1)}, bf16[24,2304]{1,0:T(8,128)(2,1)S(1)}, u32[]{:S(2)}, u32[]{:S(2)}) collective-permute-start(bf16[24,2304]{1,0:T(8,128)(2,1)S(1)} %gates.1.refs_0_.refs_3_.refs_6_), channel_id=1, source_target_pairs={{0,16},{1,17},{16,0},{17,1},{2,18},{3,19},{18,2},{19,3},{4,20},{5,... | collective-permute-start | bytes 331784 | tf_op jit(solution)/shard_map/ppermute | solution.py:367
  7.5 1.3 %collective-permute-start.1 = (bf16[24,2048]{1,0:T(8,128)(2,1)S(1)}, bf16[24,2048]{1,0:T(8,128)(2,1)S(1)}, u32[]{:S(2)}, u32[]{:S(2)}) collective-permute-start(bf16[24,2048]{1,0:T(8,128)(2,1)S(1)} %collective-permute-done.refs_0_.refs_1_), channel_id=1, source_target_pairs={{0,1},{1,0},{2,3},{3,2},{4,5},{5,4},{6,7},{7,6},{8,9},{9,8},{10,11... | collective-permute-start | bytes 294920 | tf_op jit(solution)/shard_map/ppermute | solution.py:370
  7.6 3.1 %slice-start = ((s8[6291456]{0:T(1024)(128)(4,1)}), s8[4194304]{0:T(1024)(128)(4,1)S(1)}, s32[]{:S(2)}) async-start(s8[6291456]{0:T(1024)(128)(4,1)} %bitcast.16), calls=%async_computation | async-start | bytes 8388608
  8.8 1.9 %slice-start.1 = ((s8[6291456]{0:T(1024)(128)(4,1)}), s8[2097152]{0:T(1024)(128)(4,1)S(1)}, s32[]{:S(2)}) async-start(s8[6291456]{0:T(1024)(128)(4,1)} %bitcast.16), calls=%async_computation.1 | async-start | bytes 4194304
  10.7 2.6 %copy-start.1 = (bf16[24,4096]{1,0:T(8,128)(2,1)S(1)}, bf16[24,4096]{1,0:T(8,128)(2,1)}, u32[]{:S(2)}) copy-start(bf16[24,4096]{1,0:T(8,128)(2,1)} %refs_3_.1) | copy-start | bytes 589828
  11.4 2.7 %collective-permute-start.4 = (bf16[2,2,24,1024]{3,2,1,0:T(8,128)(2,1)S(1)}, bf16[2,2,24,1024]{3,2,1,0:T(8,128)(2,1)S(1)}, u32[]{:S(2)}, u32[]{:S(2)}) collective-permute-start(bf16[2,2,24,1024]{3,2,1,0:T(8,128)(2,1)S(1)} %outward_send.1.refs_4_), channel_id=1, source_target_pairs={{0,1},{1,0},{2,3},{3,2},{4,5},{5,4},{6,7},{7,6},{8,9},{9,8},{10,11... | collective-permute-start | bytes 589832 | tf_op jit(solution)/shard_map/ppermute | solution.py:370
  11.9 1.3 %collective-permute-start.3 = (bf16[24,2304]{1,0:T(8,128)(2,1)S(1)}, bf16[24,2304]{1,0:T(8,128)(2,1)S(1)}, u32[]{:S(2)}, u32[]{:S(2)}) collective-permute-start(bf16[24,2304]{1,0:T(8,128)(2,1)S(1)} %collective-permute-done.2.refs_1_.refs_4_.refs_7_), channel_id=1, source_target_pairs={{0,1},{1,0},{2,3},{3,2},{4,5},{5,4},{6,7},{7,6},{8,9},{9,8},{10,11... | collective-permute-start | bytes 331784 | tf_op jit(solution)/shard_map/ppermute | solution.py:370
  14.3 6.0 %collective-permute-start.5 = (bf16[2,24,1024]{2,1,0:T(8,128)(2,1)S(1)}, bf16[2,24,1024]{2,1,0:T(8,128)(2,1)S(1)}, u32[]{:S(2)}, u32[]{:S(2)}) collective-permute-start(bf16[2,24,1024]{2,1,0:T(8,128)(2,1)S(1)} %get-tuple-element.50), channel_id=1, source_target_pairs={{0,17},{1,16},{16,1},{17,0},{2,19},{3,18},{18,3},{19,2},{4,21},{5,... | collective-permute-start | bytes 294920 | tf_op jit(solution)/shard_map/ppermute | solution.py:367
  20.0 2.3 %collective-permute-start.6 = (bf16[2,2,24,1024]{3,2,1,0:T(8,128)(2,1)S(1)}, bf16[2,2,24,1024]{3,2,1,0:T(8,128)(2,1)S(1)}, u32[]{:S(2)}, u32[]{:S(2)}) collective-permute-start(bf16[2,2,24,1024]{3,2,1,0:T(8,128)(2,1)S(1)} %get-tuple-element.42), channel_id=1, source_target_pairs={{0,1},{1,0},{2,3},{3,2},{4,5},{5,4},{6,7},{7,6},{8,9},{9,8},{10,11... | collective-permute-start | bytes 589832 | tf_op jit(solution)/shard_map/ppermute | solution.py:370
  20.3 27.0 %copy-start.2 = (bf16[128,4096]{1,0:T(8,128)(2,1)S(1)}, bf16[128,4096]{1,0:T(8,128)(2,1)}, u32[]{:S(2)}) copy-start(bf16[128,4096]{1,0:T(8,128)(2,1)} %refs_20_.1) | copy-start | bytes 3145732
  22.4 6.9 %collective-permute-start.7 = (bf16[3,24,1024]{2,1,0:T(8,128)(2,1)S(1)}, bf16[3,24,1024]{2,1,0:T(8,128)(2,1)S(1)}, u32[]{:S(2)}, u32[]{:S(2)}) collective-permute-start(bf16[3,24,1024]{2,1,0:T(8,128)(2,1)S(1)} %get-tuple-element.45), channel_id=1, source_target_pairs={{0,3},{1,2},{2,1},{3,0},{16,19},{17,18},{18,17},{19,16},{4,7},{5,6... | collective-permute-start | bytes 442376 | tf_op jit(solution)/shard_map/ppermute | solution.py:367
  23.5 6.9 %collective-permute-start.8 = (bf16[24,1024]{1,0:T(8,128)(2,1)S(1)}, bf16[24,1024]{1,0:T(8,128)(2,1)S(1)}, u32[]{:S(2)}, u32[]{:S(2)}) collective-permute-start(bf16[24,1024]{1,0:T(8,128)(2,1)S(1)} %get-tuple-element.46), channel_id=1, source_target_pairs={{0,18},{1,19},{2,16},{3,17},{16,2},{17,3},{18,0},{19,1},{4,22},{5,... | collective-permute-start | bytes 147464 | tf_op jit(solution)/shard_map/ppermute | solution.py:367
  24.8 5.6 %collective-permute-start.9 = (bf16[24,1024]{1,0:T(8,128)(2,1)S(1)}, bf16[24,1024]{1,0:T(8,128)(2,1)S(1)}, u32[]{:S(2)}, u32[]{:S(2)}) collective-permute-start(bf16[24,1024]{1,0:T(8,128)(2,1)S(1)} %get-tuple-element.47), channel_id=1, source_target_pairs={{0,17},{1,16},{2,19},{3,18},{16,1},{17,0},{18,3},{19,2},{4,21},{5,... | collective-permute-start | bytes 147464 | tf_op jit(solution)/shard_map/ppermute | solution.py:367
  29.3 5.3 %collective-permute-start.20 = (bf16[2,24,1024]{2,1,0:T(8,128)(2,1)S(1)}, bf16[2,24,1024]{2,1,0:T(8,128)(2,1)S(1)}, u32[]{:S(2)}, u32[]{:S(2)}) collective-permute-start(bf16[2,24,1024]{2,1,0:T(8,128)(2,1)S(1)} %flip_add.1), channel_id=1, source_target_pairs={{0,5},{1,4},{4,1},{5,0},{8,13},{9,12},{12,9},{13,8},{2,7},{3,6},{6... | collective-permute-start | bytes 294920 | tf_op jit(solution)/shard_map/ppermute | solution.py:367
  30.4 6.9 %collective-permute-start.12 = (bf16[24,1024]{1,0:T(8,128)(2,1)S(1)}, bf16[24,1024]{1,0:T(8,128)(2,1)S(1)}, u32[]{:S(2)}, u32[]{:S(2)}) collective-permute-start(bf16[24,1024]{1,0:T(8,128)(2,1)S(1)} %fusion.2), channel_id=1, source_target_pairs={{0,12},{1,13},{4,8},{5,9},{8,4},{9,5},{12,0},{13,1},{2,14},{3,15},... | collective-permute-start | bytes 147464 | tf_op jit(solution)/shard_map/ppermute | solution.py:367
  33.0 6.7 %collective-permute-start.11 = (bf16[24,1024]{1,0:T(8,128)(2,1)S(1)}, bf16[24,1024]{1,0:T(8,128)(2,1)S(1)}, u32[]{:S(2)}, u32[]{:S(2)}) collective-permute-start(bf16[24,1024]{1,0:T(8,128)(2,1)S(1)} %fusion.2), channel_id=1, source_target_pairs={{0,9},{1,8},{4,13},{5,12},{8,1},{9,0},{12,5},{13,4},{2,11},{3,10},... | collective-permute-start | bytes 147464 | tf_op jit(solution)/shard_map/ppermute | solution.py:367
  33.1 6.6 %collective-permute-start.10 = (bf16[24,1024]{1,0:T(8,128)(2,1)S(1)}, bf16[24,1024]{1,0:T(8,128)(2,1)S(1)}, u32[]{:S(2)}, u32[]{:S(2)}) collective-permute-start(bf16[24,1024]{1,0:T(8,128)(2,1)S(1)} %fusion.2), channel_id=1, source_target_pairs={{0,5},{1,4},{4,1},{5,0},{8,13},{9,12},{12,9},{13,8},{2,7},{3,6},{6... | collective-permute-start | bytes 147464 | tf_op jit(solution)/shard_map/ppermute | solution.py:367
  34.6 8.8 %collective-permute-start.21 = (bf16[2,24,1024]{2,1,0:T(8,128)(2,1)S(1)}, bf16[2,24,1024]{2,1,0:T(8,128)(2,1)S(1)}, u32[]{:S(2)}, u32[]{:S(2)}) collective-permute-start(bf16[2,24,1024]{2,1,0:T(8,128)(2,1)S(1)} %add_convert_fusion.2), channel_id=1, source_target_pairs={{0,9},{1,8},{4,13},{5,12},{8,1},{9,0},{12,5},{13,4},{2,11},{3,10},... | collective-permute-start | bytes 294920 | tf_op jit(solution)/shard_map/ppermute | solution.py:367
  39.8 5.1 %collective-permute-start.15 = (bf16[24,1024]{1,0:T(8,128)(2,1)S(1)}, bf16[24,1024]{1,0:T(8,128)(2,1)S(1)}, u32[]{:S(2)}, u32[]{:S(2)}) collective-permute-start(bf16[24,1024]{1,0:T(8,128)(2,1)S(1)} %add_convert_fusion.4.refs_8_), channel_id=1, source_target_pairs={{0,18},{1,19},{2,16},{3,17},{16,2},{17,3},{18,0},{19,1},{4,22},{5,... | collective-permute-start | bytes 147464 | tf_op jit(solution)/shard_map/ppermute | solution.py:367
  41.9 4.0 %collective-permute-start.14 = (bf16[24,1024]{1,0:T(8,128)(2,1)S(1)}, bf16[24,1024]{1,0:T(8,128)(2,1)S(1)}, u32[]{:S(2)}, u32[]{:S(2)}) collective-permute-start(bf16[24,1024]{1,0:T(8,128)(2,1)S(1)} %add_convert_fusion.4.refs_8_), channel_id=1, source_target_pairs={{0,17},{1,16},{2,19},{3,18},{16,1},{17,0},{18,3},{19,2},{4,21},{5,... | collective-permute-start | bytes 147464 | tf_op jit(solution)/shard_map/ppermute | solution.py:367
  42.3 3.7 %collective-permute-start.13 = (bf16[24,1024]{1,0:T(8,128)(2,1)S(1)}, bf16[24,1024]{1,0:T(8,128)(2,1)S(1)}, u32[]{:S(2)}, u32[]{:S(2)}) collective-permute-start(bf16[24,1024]{1,0:T(8,128)(2,1)S(1)} %add_convert_fusion.4.refs_8_), channel_id=1, source_target_pairs={{0,3},{1,2},{2,1},{3,0},{16,19},{17,18},{18,17},{19,16},{4,7},{5,6... | collective-permute-start | bytes 147464 | tf_op jit(solution)/shard_map/ppermute | solution.py:367
  43.5 3.8 %collective-permute-start.22 = (bf16[2,24,1024]{2,1,0:T(8,128)(2,1)S(1)}, bf16[2,24,1024]{2,1,0:T(8,128)(2,1)S(1)}, u32[]{:S(2)}, u32[]{:S(2)}) collective-permute-start(bf16[2,24,1024]{2,1,0:T(8,128)(2,1)S(1)} %add_convert_fusion.1.refs_16_), channel_id=1, source_target_pairs={{0,1},{1,0},{2,3},{3,2},{4,5},{5,4},{6,7},{7,6},{8,9},{9,8},{10,11... | collective-permute-start | bytes 294920 | tf_op jit(solution)/shard_map/ppermute | solution.py:370
  43.7 2.7 %collective-permute-start.16 = (bf16[24,1024]{1,0:T(8,128)(2,1)S(1)}, bf16[24,1024]{1,0:T(8,128)(2,1)S(1)}, u32[]{:S(2)}, u32[]{:S(2)}) collective-permute-start(bf16[24,1024]{1,0:T(8,128)(2,1)S(1)} %add_convert_fusion.4.refs_8_), channel_id=1, source_target_pairs={{0,1},{1,0},{2,3},{3,2},{4,5},{5,4},{6,7},{7,6},{8,9},{9,8},{10,11... | collective-permute-start | bytes 147464 | tf_op jit(solution)/shard_map/ppermute | solution.py:370
  44.8 1.6 %collective-permute-start.19 = (bf16[24,1024]{1,0:T(8,128)(2,1)S(1)}, bf16[24,1024]{1,0:T(8,128)(2,1)S(1)}, u32[]{:S(2)}, u32[]{:S(2)}) collective-permute-start(bf16[24,1024]{1,0:T(8,128)(2,1)S(1)} %collective-permute-done.15.refs_11_), channel_id=1, source_target_pairs={{0,1},{1,0},{2,3},{3,2},{4,5},{5,4},{6,7},{7,6},{8,9},{9,8},{10,11... | collective-permute-start | bytes 147464 | tf_op jit(solution)/shard_map/ppermute | solution.py:370
  45.9 1.2 %collective-permute-start.18 = (bf16[24,1024]{1,0:T(8,128)(2,1)S(1)}, bf16[24,1024]{1,0:T(8,128)(2,1)S(1)}, u32[]{:S(2)}, u32[]{:S(2)}) collective-permute-start(bf16[24,1024]{1,0:T(8,128)(2,1)S(1)} %collective-permute-done.14.refs_10_), channel_id=1, source_target_pairs={{0,1},{1,0},{2,3},{3,2},{4,5},{5,4},{6,7},{7,6},{8,9},{9,8},{10,11... | collective-permute-start | bytes 147464 | tf_op jit(solution)/shard_map/ppermute | solution.py:370
  46.0 1.3 %collective-permute-start.17 = (bf16[24,1024]{1,0:T(8,128)(2,1)S(1)}, bf16[24,1024]{1,0:T(8,128)(2,1)S(1)}, u32[]{:S(2)}, u32[]{:S(2)}) collective-permute-start(bf16[24,1024]{1,0:T(8,128)(2,1)S(1)} %collective-permute-done.13.refs_9_), channel_id=1, source_target_pairs={{0,1},{1,0},{2,3},{3,2},{4,5},{5,4},{6,7},{7,6},{8,9},{9,8},{10,11... | collective-permute-start | bytes 147464 | tf_op jit(solution)/shard_map/ppermute | solution.py:370

commit v15 on v13

--- a/solution.py
+++ b/solution.py
@@ -266,60 +266,94 @@
     refs[-1][...] = out_block[...]
 
 
-def finish_kernel(n_dp, *refs):
-    count = 2 * n_dp - 1
-    hid, grads, smalls = refs[:count], refs[count : 2 * count], refs[2 * count : 2 * count + n_dp]
-    refs = refs[2 * count + n_dp :]
-    back, moe = refs[: 4 * n_dp], refs[4 * n_dp : 4 * n_dp + 2]
-    refs = refs[4 * n_dp + 2 :]
-    gain, scales, w_out, targets, held = refs[0], refs[1], refs[2], refs[3:7], refs[7:11]
-    summed, d_all, sems = refs[11:]
-    output, d_hidden, d_context, d_w_out = held
-    copies = [pltpu.make_async_copy(held[n], targets[n], sems.at[n]) for n in range(3)]
-    size = d_w_out.shape[1] // PIECES
-    for piece in range(PIECES):
-        block = (slice(None), pl.ds(piece * size, size))
-        copies.append(pltpu.make_async_copy(d_w_out.at[block], targets[3].at[block], sems.at[3 + piece]))
-    rows, width = hid[0].shape
-    chunk = moe[0].shape[2]
+def own_rows_kernel(n_dp, hid, grads, *refs):
+    back, gain, scales, w_out = refs[:4], refs[4], refs[5], refs[6]
+    targets, d_half, held, summed, sems = refs[7:9], refs[9], refs[10:12], refs[12], refs[13]
+    d_hidden, d_context = held
+    copies = [pltpu.make_async_copy(held[n], targets[n], sems.at[n]) for n in range(2)]
+    rows, width = hid.shape
+    chunk = back[0].shape[1]
+    products = 0.0
     for i in range(2):
         for j in range(2):
             columns = pl.ds(pl.multiple_of(own_columns(i, j, chunk), chunk), chunk)
-            for k in range(n_dp):
-                piece = back[(i * n_dp + k) * 2 + j]
-                summed[k * rows : (k + 1) * rows, columns] = piece[...].astype(F32) * gain[:, columns]
-            output[:, columns] = (hid[0][:, columns].astype(F32) + moe[i][j].astype(F32)).astype(BF16)
+            value = hid[:, columns].astype(F32)
+            total = back[i * 2 + j][...].astype(F32) * gain[:, columns]
+            summed[:, columns] = total
+            products = products + folded(value * total)
+    scale = scales[:rows, :1]
+    centre = scale * jnp.sum(products, axis=1, keepdims=True) / width
+    for start in range(0, width, 512):
+        columns = slice(start, start + 512)
+        value = summed[:, columns] - hid[:, columns].astype(F32) * scale * centre
+        d_hidden[:, columns] = (grads[:, columns].astype(F32) + scale * value).astype(BF16)
     copies[0].start()
-
-    few = rows * n_dp <= FEW_ROWS
+    part = width // n_dp
+    d_half[...] = d_hidden[:, pl.ds(pl.multiple_of(lax.axis_index("dp") * part, part), part)]
+    d_context[...] = dot(d_hidden[...], w_out[...], ((1,), (1,))).astype(BF16)
+    copies[1].start()
+    for copy in copies:
+        copy.wait()
+
+
+def far_rows_kernel(n_dp, *refs):
+    count, far = 2 * (n_dp - 1), n_dp - 1
+    hid, grads, packs = refs[:count], refs[count : 2 * count], refs[2 * count : 2 * count + n_dp]
+    refs = refs[2 * count + n_dp :]
+    back, refs = refs[: 4 * far], refs[4 * far :]
+    own, moe, refs = refs[0], refs[1:3], refs[3:]
+    d_half, gain, scales, out_target, target, output, held, summed, d_far, sems = refs
+    rows, chunk = back[0].shape
+    width = summed.shape[1]
+    size = width // n_dp // PIECES
+    copies = []
+    for piece in range(PIECES):
+        block = (slice(None), pl.ds(piece * size, size))
+        copies.append(pltpu.make_async_copy(held.at[block], target.at[block], sems.at[piece]))
+    copies.append(pltpu.make_async_copy(output, out_target, sems.at[PIECES]))
+    for i in range(2):
+        for j in range(2):
+            columns = pl.ds(pl.multiple_of(own_columns(i, j, chunk), chunk), chunk)
+            output[:, columns] = (own[:, columns].astype(F32) + moe[i][j].astype(F32)).astype(BF16)
+            for k in range(far):
+                piece = back[(i * far + k) * 2 + j][...].astype(F32)
+                summed[k * rows : (k + 1) * rows, columns] = piece * gain[:, columns]
+    copies[PIECES].start()
+    half, step = width // 2, 512 if n_dp <= 2 else 128
+
+    def over_halves(body):
+        for h in range(2):
+            for start in range(0, half, step):
+                columns = pl.ds(pl.multiple_of(half_columns(h, half) + start, step), step)
+                value, grad = [
+                    jnp.concatenate([ref[:, start : start + step].astype(F32) for ref in group[h::2]], axis=0)
+                    for group in (hid, grads)
+                ]
+                body(columns, value, grad)
+
     sums = [0.0]
 
-    def products(columns, value):
+    def products(columns, value, grad):
         sums[0] = sums[0] + folded(value * summed[:, columns])
 
-    both_halves([hid], width, products)
-    scale = scales[:, :1]
+    over_halves(products)
+    scale = scales[rows:, :1]
     centre = scale * jnp.sum(sums[0], axis=1, keepdims=True) / width
 
     def total(columns, value, grad):
-        result = grad + scale * (summed[:, columns] - value * scale * centre)
-        d_all[:, columns] = result.astype(BF16)
-        d_hidden[:, columns] = result[:rows].astype(BF16)
-
-    both_halves([hid, grads], width, total)
-    copies[1].start()
-    heads = d_context.shape[1]
-    part = width // n_dp
-    lanes = slice(width // 2, width // 2 + heads)
-    turned = jnp.concatenate([small[:, lanes].astype(F32) for small in smalls], axis=0).T.astype(BF16)
-    size = part // PIECES
+        d_far[:, columns] = grad + scale * (summed[:, columns] - value * scale * centre)
+
+    over_halves(total)
+    heads = held.shape[0]
+    lanes = slice(half, half + heads)
+    turned = jnp.concatenate([pack[:, lanes].astype(F32) for pack in packs], axis=0).T.astype(BF16)
     for piece in range(PIECES):
-        columns = pl.ds(pl.multiple_of(lax.axis_index("dp") * part + piece * size, LANES), size)
-        block = pl.ds(piece * size, size)
-        d_w_out[:, block] = dot(turned, d_all[:, columns], ((1,), (0,))).astype(BF16)
-        copies[3 + piece].start()
-    d_context[...] = dot(d_hidden[...], w_out[...], ((1,), (1,))).astype(BF16)
-    copies[2].start()
+        first = lax.axis_index("dp") * (width // n_dp) + piece * size
+        block = slice(piece * size, (piece + 1) * size)
+        columns = pl.ds(pl.multiple_of(first, LANES), size)
+        both = jnp.concatenate([d_half[:, block].astype(F32), d_far[:, columns]], axis=0).astype(BF16)
+        held[:, block] = dot(turned, both, ((1,), (0,))).astype(BF16)
+        copies[piece].start()
     for copy in copies:
         copy.wait()
 
@@ -327,12 +361,13 @@
 def run(kernel, n_dp, operands, outs, scratch, cost, name, far=(), out_space=pltpu.VMEM):
     spaces = [pltpu.HBM if n in far else pltpu.VMEM for n in range(len(operands))]
     held = [pltpu.with_memory_space_constraint(value, space) for value, space in zip(operands, spaces)]
-    kinds = [out_space(shape, kind) for shape, kind in outs]
+    places = out_space if isinstance(out_space, list) else [out_space] * len(outs)
+    kinds = [place_of(shape, kind) for place_of, (shape, kind) in zip(places, outs)]
     return pl.pallas_call(
         functools.partial(kernel, n_dp),
         out_shape=kinds,
         in_specs=[pl.BlockSpec(memory_space=space) for space in spaces],
-        out_specs=[pl.BlockSpec(memory_space=out_space)] * len(outs),
+        out_specs=[pl.BlockSpec(memory_space=space) for space in places],
         scratch_shapes=scratch,
         compiler_params=pltpu.CompilerParams(vmem_limit_bytes=VMEM_LIMIT if n_dp <= 2 else VMEM_LIMIT_MANY),
         cost_estimate=pl.CostEstimate(flops=0, bytes_accessed=cost, transcendentals=0),
@@ -446,18 +481,27 @@
     while turn < n_hi:
         out_total = add(out_total, swap(out_total, ("hi",), turn))
         turn = 2 * turn
-    order = [t for t in turns if t < 2] + [t for t in turns if t >= 2]
-    spread = {t: swap(in_total, ("dp", "y"), t) for t in order}
+    spread = {t: swap(in_total, ("dp", "y"), t) for t in turns}
     back = [in_total] + [spread[t] for t in range(1, 2 * n_dp)]
-    back = back + [other_core(piece) for piece in back]
+    crossed = [other_core(one) for one in back]
     moe = [out_total, other_core(out_total)]
-    outs = [((rows, width), BF16), ((rows, width), BF16), ((rows, heads), BF16), ((heads, width // n_dp), BF16)]
-    return run(
-        finish_kernel, n_dp, hid + grads + smalls + back + moe + [gain, scales, w_out], outs,
-        [pltpu.VMEM(*out) for out in outs]
-        + [pltpu.VMEM((all_rows, width), F32), pltpu.VMEM((all_rows, width), BF16), pltpu.SemaphoreType.DMA((3 + PIECES,))],
-        weights, "finish", out_space=pltpu.HBM,
-    )
+    part, far_rows = width // n_dp, all_rows - rows
+    whole, context_out, weight_out = ((rows, width), BF16), ((rows, heads), BF16), ((heads, part), BF16)
+    d_hidden, d_context, d_half = run(
+        own_rows_kernel, n_dp, [hidden_in, grad_out] + back[:2] + crossed[:2] + [gain, scales, w_out],
+        [whole, context_out, ((rows, part), BF16)],
+        [pltpu.VMEM(*whole), pltpu.VMEM(*context_out), pltpu.VMEM((rows, width), F32), pltpu.SemaphoreType.DMA((2,))],
+        weights // 2, "own_rows", out_space=[pltpu.HBM] * 2 + [pltpu.VMEM],
+    )
+    output, d_w_out = run(
+        far_rows_kernel, n_dp,
+        hid[1:] + grads[1:] + smalls + back[2:] + crossed[2:] + [hidden_in] + moe + [d_half, gain, scales],
+        [whole, weight_out],
+        [pltpu.VMEM(*whole), pltpu.VMEM(*weight_out), pltpu.VMEM((far_rows, width), F32),
+         pltpu.VMEM((far_rows, width), F32), pltpu.SemaphoreType.DMA((PIECES + 1,))],
+        weights // 2, "far_rows", out_space=pltpu.HBM,
+    )
+    return output, d_hidden, d_context, d_w_out
 
 
 def solution(mesh):

time: 48.4 us -> 48.5 us (level)
  Pallas kernels: 14.1 us -> 15 us
  waiting for transfers between devices: 9.99 us -> 9.14 us
    pallas_call x12 -> x13, Pallas kernels: 14.1 us -> 15 us  [run(): pl.pallas_call(functools.partial(kernel, n_dp), out_shape=kinds, in_specs...]
    ppermute x9, waiting for transfers between devices: 1.44 us -> 0.58 us  [other_core(): return lax.ppermute(value, ('c',), [(0, 1), (1, 0)])]
  transfers between devices with their start and end apart: 24 -> 24, of which waited for: 13 -> 10; matrix products, arithmetic and copies ran while one was open for 0% -> 0% of each run, Pallas kernels for 22% -> 24%
where the time goes in v15:
time: 48.5 us; the launch traced here: 48.4 us
  starting transfers between devices  23 us (47%)
  Pallas kernels  15 us (31%)
  waiting for transfers between devices  9.14 us (19%)
  between operations  0.92 us (2%)
    ppermute x15, starting transfers between devices, swap(): lax.ppermute(value, axes + ('c',), [(i, i ^ turn) for i in range(count)])  20.9 us
    pallas_call x13, Pallas kernels, run(): pl.pallas_call(functools.partial(kernel, n_dp), out_shape=kinds, in_specs...  15 us
    ppermute x15, waiting for transfers between devices, swap(): lax.ppermute(value, axes + ('c',), [(i, i ^ turn) for i in range(count)])  8.56 us
    ppermute x9, starting transfers between devices, other_core(): return lax.ppermute(value, ('c',), [(0, 1), (1, 0)])  2.07 us
  transfers between devices with their start and end apart: 24, of which 10 were waited for; matrix products, arithmetic and copies ran while one was open for 0% of the time, Pallas kernels for 24%

profile of v15, /device:TPU:0, one launch (start us, length us, event | category | flops | bytes accessed | tf_op | source)
XLA Modules:
  0.0 48.4 jit_solution(5911309509453485972)
XLA Ops:
  0.6 0.0 slice-start.4
  0.7 1.1 %cut.1 = bf16[24,2048]{1,0:T(8,128)(2,1)S(1)} custom-call(bf16[24,4096]{1,0:T(8,128)(2,1)} %refs_10_.1), custom_call_target="tpu_custom_call" | custom-call | bytes 98304 | tf_op jit(solution)/shard_map/cut/pallas_call | solution.py:366
  1.7 3.0 %collective-permute-start = (bf16[24,2048]{1,0:T(8,128)(2,1)S(1)}, bf16[24,2048]{1,0:T(8,128)(2,1)S(1)}, u32[]{:S(2)}, u32[]{:S(2)}) collective-permute-start(bf16[24,2048]{1,0:T(8,128)(2,1)S(1)} %cut.1), channel_id=1, source_target_pairs={{0,16},{1,17},{16,0},{17,1},{2,18},{3,19},{18,2},{19,3},{4,20},{5,... | collective-permute-start | bytes 294920 | tf_op jit(solution)/shard_map/ppermute | solution.py:391
  4.7 1.1 %gates.1.refs_0_.refs_3_.refs_4_ = bf16[24,2304]{1,0:T(8,128)(2,1)S(1)} custom-call(s32[8,24]{1,0:T(8,128)} %bitcast.35, f32[8,24]{1,0:T(8,128)} %bitcast.36, bf16[24,128]{1,0:T(8,128)(2,1)} %context.1, bf16[24,4096]{1,0:T(8,128)(2,1)} %grads.3, bf16[4096,768]{1,0:T(8,128)(2,1)} %bitcast.17, bf16[4096,768]{1,0:T(8,128)(2,1)} %bitcast.24, ...), custom_call_target="tpu_custom_call" | custom-call | bytes 25165824 | tf_op jit(solution)/shard_map/gates/pallas_call | solution.py:366
  5.9 0.6 %collective-permute-start.2 = (bf16[24,2304]{1,0:T(8,128)(2,1)S(1)}, bf16[24,2304]{1,0:T(8,128)(2,1)S(1)}, u32[]{:S(2)}, u32[]{:S(2)}) collective-permute-start(bf16[24,2304]{1,0:T(8,128)(2,1)S(1)} %gates.1.refs_0_.refs_3_.refs_4_), channel_id=1, source_target_pairs={{0,16},{1,17},{16,0},{17,1},{2,18},{3,19},{18,2},{19,3},{4,20},{5,... | collective-permute-start | bytes 331784 | tf_op jit(solution)/shard_map/ppermute | solution.py:391
  6.4 1.1 %collective-permute-done.refs_0_ = bf16[24,2048]{1,0:T(8,128)(2,1)S(1)} collective-permute-done((bf16[24,2048]{1,0:T(8,128)(2,1)S(1)}, bf16[24,2048]{1,0:T(8,128)(2,1)S(1)}, u32[]{:S(2)}, u32[]{:S(2)}) %collective-permute-start) | collective-permute-done | bytes 98336 | tf_op jit(solution)/shard_map/ppermute | solution.py:391
  7.6 1.2 %hidden_first.1 = (f32[48,768]{1,0:T(8,128)S(1)}, f32[48,768]{1,0:T(8,128)S(1)}, f32[48,128]{1,0:T(8,128)S(1)}) custom-call(bf16[24,4096]{1,0:T(8,128)(2,1)S(1)} %copy-done, bf16[24,2048]{1,0:T(8,128)(2,1)S(1)} %collective-permute-done.refs_0_, f32[1,4096]{1,0:T(1,128)S(1)} %bitcast.31, bf16[4096,768]{1,0:T(8,128)(2,1)S(1)} %bitcast.20, ...), custom_call_target="tpu_custom_call" | custom-call | bytes 6291456 | tf_op jit(solution)/shard_map/hidden_first/pallas_call | solution.py:366
  8.8 0.0 collective-permute-done.1.refs_0_.refs_1_
  8.8 1.2 %hidden_rest.1 = (f32[48,768]{1,0:T(8,128)S(1)}, f32[48,768]{1,0:T(8,128)S(1)}, bf16[48,768]{1,0:T(8,128)(2,1)S(1)}, f32[48,128]{1,0:T(8,128)S(1)}) custom-call(bf16[24,4096]{1,0:T(8,128)(2,1)S(1)} %copy-done, bf16[24,2048]{1,0:T(8,128)(2,1)S(1)} %collective-permute-done.1.refs_0_.refs_1_, f32[1,4096]{1,0:T(1,128)S(1)} %bitcast.32, ...), custom_call_target="tpu_custom_call" | custom-call | bytes 6291456 | tf_op jit(solution)/shard_map/hidden_rest/pallas_call | solution.py:366
  10.1 0.6 %collective-permute-done.2.refs_1_.refs_4_.refs_2_.refs_5_ = bf16[24,2304]{1,0:T(8,128)(2,1)S(1)} collective-permute-done((bf16[24,2304]{1,0:T(8,128)(2,1)S(1)}, bf16[24,2304]{1,0:T(8,128)(2,1)S(1)}, u32[]{:S(2)}, u32[]{:S(2)}) %collective-permute-start.2) | collective-permute-done | bytes 110624 | tf_op jit(solution)/shard_map/ppermute | solution.py:391
  10.7 0.7 %outward_send.1.refs_4_ = bf16[2,2,24,1024]{3,2,1,0:T(8,128)(2,1)S(1)} custom-call(bf16[24,2304]{1,0:T(8,128)(2,1)S(1)} %gates.1.refs_0_.refs_3_.refs_4_, bf16[24,2304]{1,0:T(8,128)(2,1)S(1)} %collective-permute-done.2.refs_1_.refs_4_.refs_2_.refs_5_, bf16[48,768]{1,0:T(8,128)(2,1)S(1)} %get-tuple-element.37.refs_2_, bf16[768,4096]{1,0:T(8,128)(2,1)S(1)} %bitcast.13), custom_call_target="tpu_custom_call" | custom-call | bytes 3145728 | tf_op jit(solution)/shard_map/outward_send/pallas_call | solution.py:366
  11.4 0.5 %collective-permute-start.4 = (bf16[2,2,24,1024]{3,2,1,0:T(8,128)(2,1)S(1)}, bf16[2,2,24,1024]{3,2,1,0:T(8,128)(2,1)S(1)}, u32[]{:S(2)}, u32[]{:S(2)}) collective-permute-start(bf16[2,2,24,1024]{3,2,1,0:T(8,128)(2,1)S(1)} %outward_send.1.refs_4_), channel_id=1, source_target_pairs={{0,1},{1,0},{2,3},{3,2},{4,5},{5,4},{6,7},{7,6},{8,9},{9,8},{10,11... | collective-permute-start | bytes 589832 | tf_op jit(solution)/shard_map/ppermute | solution.py:394
  11.9 0.1 collective-permute-start.3
  12.0 0.7 %outward_keep.1.refs_8_ = bf16[2,2,24,1024]{3,2,1,0:T(8,128)(2,1)S(1)} custom-call(bf16[24,2304]{1,0:T(8,128)(2,1)S(1)} %gates.1.refs_0_.refs_3_.refs_4_, bf16[24,2304]{1,0:T(8,128)(2,1)S(1)} %collective-permute-done.2.refs_1_.refs_4_.refs_2_.refs_5_, bf16[48,768]{1,0:T(8,128)(2,1)S(1)} %get-tuple-element.37.refs_2_, bf16[768,4096]{1,0:T(8,128)(2,1)S(1)} %bitcast.14, ...), custom_call_target="tpu_custom_call" | custom-call | bytes 3145728 | tf_op jit(solution)/shard_map/outward_keep/pallas_call | solution.py:366
  12.7 0.6 %collective-permute-done.3.refs_2_.refs_3_ = bf16[24,2304]{1,0:T(8,128)(2,1)S(1)} collective-permute-done((bf16[24,2304]{1,0:T(8,128)(2,1)S(1)}, bf16[24,2304]{1,0:T(8,128)(2,1)S(1)}, u32[]{:S(2)}, u32[]{:S(2)}) %collective-permute-start.3) | collective-permute-done | bytes 110624 | tf_op jit(solution)/shard_map/ppermute | solution.py:394
  13.3 0.9 %backward_first.1 = (bf16[48,256]{1,0:T(8,128)(2,1)S(1)}, bf16[48,256]{1,0:T(8,128)(2,1)S(1)}, bf16[48,4096]{1,0:T(8,128)(2,1)S(1)}, bf16[2,2,24,1024]{3,2,1,0:T(8,128)(2,1)S(1)}) custom-call(bf16[24,4096]{1,0:T(8,128)(2,1)S(1)} %copy-done.1, bf16[24,2304]{1,0:T(8,128)(2,1)S(1)} %collective-permute-done.2.refs_1_.refs_4_.refs_2_.refs_5_, ...), custom_call_target="tpu_custom_call" | custom-call | bytes 2097152 | tf_op jit(solution)/shard_map/backward_first/pallas_call | solution.py:366
  14.2 0.1 add_convert_fusion
  14.3 2.3 %collective-permute-start.5 = (bf16[2,24,1024]{2,1,0:T(8,128)(2,1)S(1)}, bf16[2,24,1024]{2,1,0:T(8,128)(2,1)S(1)}, u32[]{:S(2)}, u32[]{:S(2)}) collective-permute-start(bf16[2,24,1024]{2,1,0:T(8,128)(2,1)S(1)} %get-tuple-element.60), channel_id=1, source_target_pairs={{0,17},{1,16},{16,1},{17,0},{2,19},{3,18},{18,3},{19,2},{4,21},{5,... | collective-permute-start | bytes 294920 | tf_op jit(solution)/shard_map/ppermute | solution.py:391
  16.6 1.4 %backward_rest.1 = (bf16[48,512]{1,0:T(8,128)(2,1)S(1)}, bf16[48,512]{1,0:T(8,128)(2,1)S(1)}, bf16[2,24,1024]{2,1,0:T(8,128)(2,1)S(1)}) custom-call(bf16[48,4096]{1,0:T(8,128)(2,1)S(1)} %get-tuple-element.40.weighted, f32[48,768]{1,0:T(8,128)S(1)} %get-tuple-element.35.refs_5_.pre_gate, f32[48,768]{1,0:T(8,128)S(1)} %get-tuple-element.36.refs_6_.pre_up, ...), custom_call_target="tpu_custom_call" | custom-call | bytes 4194304 | tf_op jit(solution)/shard_map/backward_rest/pallas_call | solution.py:366
  18.0 2.0 %inward_send.1 = (bf16[2,2,24,1024]{3,2,1,0:T(8,128)(2,1)S(1)}, bf16[2,24,1024]{2,1,0:T(8,128)(2,1)S(1)}) custom-call(bf16[48,256]{1,0:T(8,128)(2,1)S(1)} %get-tuple-element.38.refs_0_, bf16[48,256]{1,0:T(8,128)(2,1)S(1)} %get-tuple-element.39.refs_1_, bf16[48,512]{1,0:T(8,128)(2,1)S(1)} %get-tuple-element.42.refs_2_, ...), custom_call_target="tpu_custom_call" | custom-call | bytes 6291456 | tf_op jit(solution)/shard_map/inward_send/pallas_call | solution.py:366
  20.0 0.3 collective-permute-start.6
  20.3 2.0 %inward_keep.1 = (bf16[2,2,24,1024]{3,2,1,0:T(8,128)(2,1)S(1)}, bf16[2,24,1024]{2,1,0:T(8,128)(2,1)S(1)}) custom-call(bf16[48,256]{1,0:T(8,128)(2,1)S(1)} %get-tuple-element.38.refs_0_, bf16[48,256]{1,0:T(8,128)(2,1)S(1)} %get-tuple-element.39.refs_1_, bf16[48,512]{1,0:T(8,128)(2,1)S(1)} %get-tuple-element.42.refs_2_, ...), custom_call_target="tpu_custom_call" | custom-call | bytes 6291456 | tf_op jit(solution)/shard_map/inward_keep/pallas_call | solution.py:366
  22.3 0.1 join.1
  22.4 1.1 %collective-permute-start.17 = (bf16[2,24,1024]{2,1,0:T(8,128)(2,1)S(1)}, bf16[2,24,1024]{2,1,0:T(8,128)(2,1)S(1)}, u32[]{:S(2)}, u32[]{:S(2)}) collective-permute-start(bf16[2,24,1024]{2,1,0:T(8,128)(2,1)S(1)} %get-tuple-element.53), channel_id=1, source_target_pairs={{0,3},{1,2},{2,1},{3,0},{4,7},{5,6},{6,5},{7,4},{8,11},{9,10},{10,... | collective-permute-start | bytes 294920 | tf_op jit(solution)/shard_map/ppermute | solution.py:391
  23.5 1.3 %collective-permute-start.7 = (bf16[24,1024]{1,0:T(8,128)(2,1)S(1)}, bf16[24,1024]{1,0:T(8,128)(2,1)S(1)}, u32[]{:S(2)}, u32[]{:S(2)}) collective-permute-start(bf16[24,1024]{1,0:T(8,128)(2,1)S(1)} %get-tuple-element.50), channel_id=1, source_target_pairs={{0,18},{1,19},{2,16},{3,17},{16,2},{17,3},{18,0},{19,1},{4,22},{5,... | collective-permute-start | bytes 147464 | tf_op jit(solution)/shard_map/ppermute | solution.py:391
  24.8 0.5 %collective-permute-start.8 = (bf16[24,1024]{1,0:T(8,128)(2,1)S(1)}, bf16[24,1024]{1,0:T(8,128)(2,1)S(1)}, u32[]{:S(2)}, u32[]{:S(2)}) collective-permute-start(bf16[24,1024]{1,0:T(8,128)(2,1)S(1)} %get-tuple-element.51), channel_id=1, source_target_pairs={{0,17},{1,16},{2,19},{3,18},{16,1},{17,0},{18,3},{19,2},{4,21},{5,... | collective-permute-start | bytes 147464 | tf_op jit(solution)/shard_map/ppermute | solution.py:391
  25.4 1.3 %collective-permute-start.9 = (bf16[24,1024]{1,0:T(8,128)(2,1)S(1)}, bf16[24,1024]{1,0:T(8,128)(2,1)S(1)}, u32[]{:S(2)}, u32[]{:S(2)}) collective-permute-start(bf16[24,1024]{1,0:T(8,128)(2,1)S(1)} %get-tuple-element.52), channel_id=1, source_target_pairs={{0,3},{1,2},{2,1},{3,0},{16,19},{17,18},{18,17},{19,16},{4,7},{5,6... | collective-permute-start | bytes 147464 | tf_op jit(solution)/shard_map/ppermute | solution.py:391
  26.7 0.6 %collective-permute-done.17 = bf16[2,24,1024]{2,1,0:T(8,128)(2,1)S(1)} collective-permute-done((bf16[2,24,1024]{2,1,0:T(8,128)(2,1)S(1)}, bf16[2,24,1024]{2,1,0:T(8,128)(2,1)S(1)}, u32[]{:S(2)}, u32[]{:S(2)}) %collective-permute-start.17) | collective-permute-done | bytes 98336 | tf_op jit(solution)/shard_map/ppermute | solution.py:391
  27.4 0.9 %collective-permute-start.18 = (bf16[2,24,1024]{2,1,0:T(8,128)(2,1)S(1)}, bf16[2,24,1024]{2,1,0:T(8,128)(2,1)S(1)}, u32[]{:S(2)}, u32[]{:S(2)}) collective-permute-start(bf16[2,24,1024]{2,1,0:T(8,128)(2,1)S(1)} %add_convert_fusion.3), channel_id=1, source_target_pairs={{0,5},{1,4},{4,1},{5,0},{8,13},{9,12},{12,9},{13,8},{2,7},{3,6},{6... | collective-permute-start | bytes 294920 | tf_op jit(solution)/shard_map/ppermute | solution.py:391
  28.3 0.3 collective-permute-done.7
  28.6 0.2 collective-permute-done.8
  28.8 0.4 collective-permute-done.9
  29.2 3.8 %collective-permute-start.12 = (bf16[24,1024]{1,0:T(8,128)(2,1)S(1)}, bf16[24,1024]{1,0:T(8,128)(2,1)S(1)}, u32[]{:S(2)}, u32[]{:S(2)}) collective-permute-start(bf16[24,1024]{1,0:T(8,128)(2,1)S(1)} %add_convert_fusion.6), channel_id=1, source_target_pairs={{0,12},{1,13},{4,8},{5,9},{8,4},{9,5},{12,0},{13,1},{2,14},{3,15},... | collective-permute-start | bytes 147464 | tf_op jit(solution)/shard_map/ppermute | solution.py:391
  33.0 0.4 collective-permute-start.10
  33.4 2.3 %collective-permute-start.19 = (bf16[2,24,1024]{2,1,0:T(8,128)(2,1)S(1)}, bf16[2,24,1024]{2,1,0:T(8,128)(2,1)S(1)}, u32[]{:S(2)}, u32[]{:S(2)}) collective-permute-start(bf16[2,24,1024]{2,1,0:T(8,128)(2,1)S(1)} %add_convert_fusion.2), channel_id=1, source_target_pairs={{0,9},{1,8},{4,13},{5,12},{8,1},{9,0},{12,5},{13,4},{2,11},{3,10},... | collective-permute-start | bytes 294920 | tf_op jit(solution)/shard_map/ppermute | solution.py:391
  35.7 2.3 %collective-permute-done.11 = bf16[24,1024]{1,0:T(8,128)(2,1)S(1)} collective-permute-done((bf16[24,1024]{1,0:T(8,128)(2,1)S(1)}, bf16[24,1024]{1,0:T(8,128)(2,1)S(1)}, u32[]{:S(2)}, u32[]{:S(2)}) %collective-permute-start.11) | collective-permute-done | bytes 49184 | tf_op jit(solution)/shard_map/ppermute | solution.py:391
  38.1 2.0 %collective-permute-start.21 = (bf16[24,1024]{1,0:T(8,128)(2,1)S(1)}, bf16[24,1024]{1,0:T(8,128)(2,1)S(1)}, u32[]{:S(2)}, u32[]{:S(2)}) collective-permute-start(bf16[24,1024]{1,0:T(8,128)(2,1)S(1)} %add_convert_fusion.5.refs_0_), channel_id=1, source_target_pairs={{0,3},{1,2},{2,1},{3,0},{16,19},{17,18},{18,17},{19,16},{4,7},{5,6... | collective-permute-start | bytes 147464 | tf_op jit(solution)/shard_map/ppermute | solution.py:391
  40.1 1.0 %collective-permute-start.14 = (bf16[24,1024]{1,0:T(8,128)(2,1)S(1)}, bf16[24,1024]{1,0:T(8,128)(2,1)S(1)}, u32[]{:S(2)}, u32[]{:S(2)}) collective-permute-start(bf16[24,1024]{1,0:T(8,128)(2,1)S(1)} %add_convert_fusion.5.refs_0_), channel_id=1, source_target_pairs={{0,18},{1,19},{2,16},{3,17},{16,2},{17,3},{18,0},{19,1},{4,22},{5,... | collective-permute-start | bytes 147464 | tf_op jit(solution)/shard_map/ppermute | solution.py:391
  41.1 0.3 collective-permute-start.13
  41.4 0.8 %collective-permute-done.19 = bf16[2,24,1024]{2,1,0:T(8,128)(2,1)S(1)} collective-permute-done((bf16[2,24,1024]{2,1,0:T(8,128)(2,1)S(1)}, bf16[2,24,1024]{2,1,0:T(8,128)(2,1)S(1)}, u32[]{:S(2)}, u32[]{:S(2)}) %collective-permute-start.19) | collective-permute-done | bytes 98336 | tf_op jit(solution)/shard_map/ppermute | solution.py:391
  42.3 0.2 collective-permute-start.20
  42.4 0.4 collective-permute-start.22
  42.8 0.1 collective-permute-start.23
  42.9 2.2 %collective-permute-done.14.refs_7_ = bf16[24,1024]{1,0:T(8,128)(2,1)S(1)} collective-permute-done((bf16[24,1024]{1,0:T(8,128)(2,1)S(1)}, bf16[24,1024]{1,0:T(8,128)(2,1)S(1)}, u32[]{:S(2)}, u32[]{:S(2)}) %collective-permute-start.14) | collective-permute-done | bytes 49184 | tf_op jit(solution)/shard_map/ppermute | solution.py:391
  45.1 0.0 collective-permute-done.13.refs_6_
  45.1 0.5 collective-permute-start.15
  45.6 1.3 %own_rows.1 = (bf16[24,4096]{1,0:T(8,128)(2,1)}, bf16[24,128]{1,0:T(8,128)(2,1)}, bf16[24,2048]{1,0:T(8,128)(2,1)S(1)}) custom-call(bf16[24,4096]{1,0:T(8,128)(2,1)S(1)} %copy-done, bf16[24,4096]{1,0:T(8,128)(2,1)S(1)} %copy-done.1, bf16[24,1024]{1,0:T(8,128)(2,1)S(1)} %add_convert_fusion.5.refs_0_, bf16[24,1024]{1,0:T(8,128)(2,1)S(1)} %collective-permute-done.21.refs_1_, ...), custom_call_target="tpu_custom_call" | custom-call | bytes 3145728 | tf_op jit(solution)/shard_map/own_rows/pallas_call | solution.py:366
  47.0 1.4 %far_rows.1 = (bf16[24,4096]{1,0:T(8,128)(2,1)}, bf16[128,2048]{1,0:T(8,128)(2,1)}) custom-call(bf16[24,2048]{1,0:T(8,128)(2,1)S(1)} %collective-permute-done.refs_0_, bf16[24,2048]{1,0:T(8,128)(2,1)S(1)} %collective-permute-done.1.refs_0_.refs_1_, bf16[24,2304]{1,0:T(8,128)(2,1)S(1)} %collective-permute-done.2.refs_1_.refs_4_.refs_2_.refs_5_, ...), custom_call_target="tpu_custom_call" | custom-call | bytes 3145728 | tf_op jit(solution)/shard_map/far_rows/pallas_call | solution.py:366
  (44 shorter events, 0.3 us)
Async XLA Ops:
  0.6 6.9 %slice-start.2 = ((s8[6291456]{0:T(1024)(128)(4,1)}), s8[4194304]{0:T(1024)(128)(4,1)S(1)}, s32[]{:S(2)}) async-start(s8[6291456]{0:T(1024)(128)(4,1)} %bitcast.18), calls=%async_computation.2 | async-start | bytes 8388608
  0.6 6.9 %slice-start.4 = ((s8[6291456]{0:T(1024)(128)(4,1)}), s8[4194304]{0:T(1024)(128)(4,1)S(1)}, s32[]{:S(2)}) async-start(s8[6291456]{0:T(1024)(128)(4,1)} %bitcast.25), calls=%async_computation.4 | async-start | bytes 8388608
  1.7 5.8 %collective-permute-start = (bf16[24,2048]{1,0:T(8,128)(2,1)S(1)}, bf16[24,2048]{1,0:T(8,128)(2,1)S(1)}, u32[]{:S(2)}, u32[]{:S(2)}) collective-permute-start(bf16[24,2048]{1,0:T(8,128)(2,1)S(1)} %cut.1), channel_id=1, source_target_pairs={{0,16},{1,17},{16,0},{17,1},{2,18},{3,19},{18,2},{19,3},{4,20},{5,... | collective-permute-start | bytes 294920 | tf_op jit(solution)/shard_map/ppermute | solution.py:391
  4.7 2.8 %slice-start.3 = ((s8[6291456]{0:T(1024)(128)(4,1)}), s8[2097152]{0:T(1024)(128)(4,1)S(1)}, s32[]{:S(2)}) async-start(s8[6291456]{0:T(1024)(128)(4,1)} %bitcast.18), calls=%async_computation.3 | async-start | bytes 4194304
  4.7 2.8 %slice-start.5 = ((s8[6291456]{0:T(1024)(128)(4,1)}), s8[2097152]{0:T(1024)(128)(4,1)S(1)}, s32[]{:S(2)}) async-start(s8[6291456]{0:T(1024)(128)(4,1)} %bitcast.25), calls=%async_computation.5 | async-start | bytes 4194304
  4.7 2.8 %copy-start = (bf16[24,4096]{1,0:T(8,128)(2,1)S(1)}, bf16[24,4096]{1,0:T(8,128)(2,1)}, u32[]{:S(2)}) copy-start(bf16[24,4096]{1,0:T(8,128)(2,1)} %refs_10_.1) | copy-start | bytes 589828
  4.7 2.8 %copy-start.3 = (f32[4096]{0:T(1024)S(1)}, f32[4096]{0:T(1024)}, u32[]{:S(2)}) copy-start(f32[4096]{0:T(1024)} %param.11) | copy-start | bytes 49156
  5.9 4.8 %collective-permute-start.2 = (bf16[24,2304]{1,0:T(8,128)(2,1)S(1)}, bf16[24,2304]{1,0:T(8,128)(2,1)S(1)}, u32[]{:S(2)}, u32[]{:S(2)}) collective-permute-start(bf16[24,2304]{1,0:T(8,128)(2,1)S(1)} %gates.1.refs_0_.refs_3_.refs_4_), channel_id=1, source_target_pairs={{0,16},{1,17},{16,0},{17,1},{2,18},{3,19},{18,2},{19,3},{4,20},{5,... | collective-permute-start | bytes 331784 | tf_op jit(solution)/shard_map/ppermute | solution.py:391
  7.5 1.3 %collective-permute-start.1 = (bf16[24,2048]{1,0:T(8,128)(2,1)S(1)}, bf16[24,2048]{1,0:T(8,128)(2,1)S(1)}, u32[]{:S(2)}, u32[]{:S(2)}) collective-permute-start(bf16[24,2048]{1,0:T(8,128)(2,1)S(1)} %collective-permute-done.refs_0_), channel_id=1, source_target_pairs={{0,1},{1,0},{2,3},{3,2},{4,5},{5,4},{6,7},{7,6},{8,9},{9,8},{10,11... | collective-permute-start | bytes 294920 | tf_op jit(solution)/shard_map/ppermute | solution.py:394
  7.6 3.1 %slice-start = ((s8[6291456]{0:T(1024)(128)(4,1)}), s8[4194304]{0:T(1024)(128)(4,1)S(1)}, s32[]{:S(2)}) async-start(s8[6291456]{0:T(1024)(128)(4,1)} %bitcast.11), calls=%async_computation | async-start | bytes 8388608
  8.8 1.9 %slice-start.1 = ((s8[6291456]{0:T(1024)(128)(4,1)}), s8[2097152]{0:T(1024)(128)(4,1)S(1)}, s32[]{:S(2)}) async-start(s8[6291456]{0:T(1024)(128)(4,1)} %bitcast.11), calls=%async_computation.1 | async-start | bytes 4194304
  10.7 2.6 %copy-start.1 = (bf16[24,4096]{1,0:T(8,128)(2,1)S(1)}, bf16[24,4096]{1,0:T(8,128)(2,1)}, u32[]{:S(2)}) copy-start(bf16[24,4096]{1,0:T(8,128)(2,1)} %grads.3) | copy-start | bytes 589828
  11.4 2.7 %collective-permute-start.4 = (bf16[2,2,24,1024]{3,2,1,0:T(8,128)(2,1)S(1)}, bf16[2,2,24,1024]{3,2,1,0:T(8,128)(2,1)S(1)}, u32[]{:S(2)}, u32[]{:S(2)}) collective-permute-start(bf16[2,2,24,1024]{3,2,1,0:T(8,128)(2,1)S(1)} %outward_send.1.refs_4_), channel_id=1, source_target_pairs={{0,1},{1,0},{2,3},{3,2},{4,5},{5,4},{6,7},{7,6},{8,9},{9,8},{10,11... | collective-permute-start | bytes 589832 | tf_op jit(solution)/shard_map/ppermute | solution.py:394
  11.9 1.3 %collective-permute-start.3 = (bf16[24,2304]{1,0:T(8,128)(2,1)S(1)}, bf16[24,2304]{1,0:T(8,128)(2,1)S(1)}, u32[]{:S(2)}, u32[]{:S(2)}) collective-permute-start(bf16[24,2304]{1,0:T(8,128)(2,1)S(1)} %collective-permute-done.2.refs_1_.refs_4_.refs_2_.refs_5_), channel_id=1, source_target_pairs={{0,1},{1,0},{2,3},{3,2},{4,5},{5,4},{6,7},{7,6},{8,9},{9,8},{10,11... | collective-permute-start | bytes 331784 | tf_op jit(solution)/shard_map/ppermute | solution.py:394
  14.3 6.0 %collective-permute-start.5 = (bf16[2,24,1024]{2,1,0:T(8,128)(2,1)S(1)}, bf16[2,24,1024]{2,1,0:T(8,128)(2,1)S(1)}, u32[]{:S(2)}, u32[]{:S(2)}) collective-permute-start(bf16[2,24,1024]{2,1,0:T(8,128)(2,1)S(1)} %get-tuple-element.60), channel_id=1, source_target_pairs={{0,17},{1,16},{16,1},{17,0},{2,19},{3,18},{18,3},{19,2},{4,21},{5,... | collective-permute-start | bytes 294920 | tf_op jit(solution)/shard_map/ppermute | solution.py:391
  20.0 2.3 %collective-permute-start.6 = (bf16[2,2,24,1024]{3,2,1,0:T(8,128)(2,1)S(1)}, bf16[2,2,24,1024]{3,2,1,0:T(8,128)(2,1)S(1)}, u32[]{:S(2)}, u32[]{:S(2)}) collective-permute-start(bf16[2,2,24,1024]{3,2,1,0:T(8,128)(2,1)S(1)} %get-tuple-element.47), channel_id=1, source_target_pairs={{0,1},{1,0},{2,3},{3,2},{4,5},{5,4},{6,7},{7,6},{8,9},{9,8},{10,11... | collective-permute-start | bytes 589832 | tf_op jit(solution)/shard_map/ppermute | solution.py:394
  20.3 25.3 %copy-start.2 = (bf16[128,4096]{1,0:T(8,128)(2,1)S(1)}, bf16[128,4096]{1,0:T(8,128)(2,1)}, u32[]{:S(2)}) copy-start(bf16[128,4096]{1,0:T(8,128)(2,1)} %refs_6_.1) | copy-start | bytes 3145732
  22.4 4.9 %collective-permute-start.17 = (bf16[2,24,1024]{2,1,0:T(8,128)(2,1)S(1)}, bf16[2,24,1024]{2,1,0:T(8,128)(2,1)S(1)}, u32[]{:S(2)}, u32[]{:S(2)}) collective-permute-start(bf16[2,24,1024]{2,1,0:T(8,128)(2,1)S(1)} %get-tuple-element.53), channel_id=1, source_target_pairs={{0,3},{1,2},{2,1},{3,0},{4,7},{5,6},{6,5},{7,4},{8,11},{9,10},{10,... | collective-permute-start | bytes 294920 | tf_op jit(solution)/shard_map/ppermute | solution.py:391
  23.5 5.1 %collective-permute-start.7 = (bf16[24,1024]{1,0:T(8,128)(2,1)S(1)}, bf16[24,1024]{1,0:T(8,128)(2,1)S(1)}, u32[]{:S(2)}, u32[]{:S(2)}) collective-permute-start(bf16[24,1024]{1,0:T(8,128)(2,1)S(1)} %get-tuple-element.50), channel_id=1, source_target_pairs={{0,18},{1,19},{2,16},{3,17},{16,2},{17,3},{18,0},{19,1},{4,22},{5,... | collective-permute-start | bytes 147464 | tf_op jit(solution)/shard_map/ppermute | solution.py:391
  24.8 3.9 %collective-permute-start.8 = (bf16[24,1024]{1,0:T(8,128)(2,1)S(1)}, bf16[24,1024]{1,0:T(8,128)(2,1)S(1)}, u32[]{:S(2)}, u32[]{:S(2)}) collective-permute-start(bf16[24,1024]{1,0:T(8,128)(2,1)S(1)} %get-tuple-element.51), channel_id=1, source_target_pairs={{0,17},{1,16},{2,19},{3,18},{16,1},{17,0},{18,3},{19,2},{4,21},{5,... | collective-permute-start | bytes 147464 | tf_op jit(solution)/shard_map/ppermute | solution.py:391
  25.4 3.8 %collective-permute-start.9 = (bf16[24,1024]{1,0:T(8,128)(2,1)S(1)}, bf16[24,1024]{1,0:T(8,128)(2,1)S(1)}, u32[]{:S(2)}, u32[]{:S(2)}) collective-permute-start(bf16[24,1024]{1,0:T(8,128)(2,1)S(1)} %get-tuple-element.52), channel_id=1, source_target_pairs={{0,3},{1,2},{2,1},{3,0},{16,19},{17,18},{18,17},{19,16},{4,7},{5,6... | collective-permute-start | bytes 147464 | tf_op jit(solution)/shard_map/ppermute | solution.py:391
  27.4 6.0 %collective-permute-start.18 = (bf16[2,24,1024]{2,1,0:T(8,128)(2,1)S(1)}, bf16[2,24,1024]{2,1,0:T(8,128)(2,1)S(1)}, u32[]{:S(2)}, u32[]{:S(2)}) collective-permute-start(bf16[2,24,1024]{2,1,0:T(8,128)(2,1)S(1)} %add_convert_fusion.3), channel_id=1, source_target_pairs={{0,5},{1,4},{4,1},{5,0},{8,13},{9,12},{12,9},{13,8},{2,7},{3,6},{6... | collective-permute-start | bytes 294920 | tf_op jit(solution)/shard_map/ppermute | solution.py:391
  29.2 6.5 %collective-permute-start.12 = (bf16[24,1024]{1,0:T(8,128)(2,1)S(1)}, bf16[24,1024]{1,0:T(8,128)(2,1)S(1)}, u32[]{:S(2)}, u32[]{:S(2)}) collective-permute-start(bf16[24,1024]{1,0:T(8,128)(2,1)S(1)} %add_convert_fusion.6), channel_id=1, source_target_pairs={{0,12},{1,13},{4,8},{5,9},{8,4},{9,5},{12,0},{13,1},{2,14},{3,15},... | collective-permute-start | bytes 147464 | tf_op jit(solution)/shard_map/ppermute | solution.py:391
  33.0 5.1 %collective-permute-start.11 = (bf16[24,1024]{1,0:T(8,128)(2,1)S(1)}, bf16[24,1024]{1,0:T(8,128)(2,1)S(1)}, u32[]{:S(2)}, u32[]{:S(2)}) collective-permute-start(bf16[24,1024]{1,0:T(8,128)(2,1)S(1)} %add_convert_fusion.6), channel_id=1, source_target_pairs={{0,9},{1,8},{4,13},{5,12},{8,1},{9,0},{12,5},{13,4},{2,11},{3,10},... | collective-permute-start | bytes 147464 | tf_op jit(solution)/shard_map/ppermute | solution.py:391
  33.0 5.1 %collective-permute-start.10 = (bf16[24,1024]{1,0:T(8,128)(2,1)S(1)}, bf16[24,1024]{1,0:T(8,128)(2,1)S(1)}, u32[]{:S(2)}, u32[]{:S(2)}) collective-permute-start(bf16[24,1024]{1,0:T(8,128)(2,1)S(1)} %add_convert_fusion.6), channel_id=1, source_target_pairs={{0,5},{1,4},{4,1},{5,0},{8,13},{9,12},{12,9},{13,8},{2,7},{3,6},{6... | collective-permute-start | bytes 147464 | tf_op jit(solution)/shard_map/ppermute | solution.py:391
  33.4 8.8 %collective-permute-start.19 = (bf16[2,24,1024]{2,1,0:T(8,128)(2,1)S(1)}, bf16[2,24,1024]{2,1,0:T(8,128)(2,1)S(1)}, u32[]{:S(2)}, u32[]{:S(2)}) collective-permute-start(bf16[2,24,1024]{2,1,0:T(8,128)(2,1)S(1)} %add_convert_fusion.2), channel_id=1, source_target_pairs={{0,9},{1,8},{4,13},{5,12},{8,1},{9,0},{12,5},{13,4},{2,11},{3,10},... | collective-permute-start | bytes 294920 | tf_op jit(solution)/shard_map/ppermute | solution.py:391
  38.1 4.7 %collective-permute-start.21 = (bf16[24,1024]{1,0:T(8,128)(2,1)S(1)}, bf16[24,1024]{1,0:T(8,128)(2,1)S(1)}, u32[]{:S(2)}, u32[]{:S(2)}) collective-permute-start(bf16[24,1024]{1,0:T(8,128)(2,1)S(1)} %add_convert_fusion.5.refs_0_), channel_id=1, source_target_pairs={{0,3},{1,2},{2,1},{3,0},{16,19},{17,18},{18,17},{19,16},{4,7},{5,6... | collective-permute-start | bytes 147464 | tf_op jit(solution)/shard_map/ppermute | solution.py:391
  40.1 5.0 %collective-permute-start.14 = (bf16[24,1024]{1,0:T(8,128)(2,1)S(1)}, bf16[24,1024]{1,0:T(8,128)(2,1)S(1)}, u32[]{:S(2)}, u32[]{:S(2)}) collective-permute-start(bf16[24,1024]{1,0:T(8,128)(2,1)S(1)} %add_convert_fusion.5.refs_0_), channel_id=1, source_target_pairs={{0,18},{1,19},{2,16},{3,17},{16,2},{17,3},{18,0},{19,1},{4,22},{5,... | collective-permute-start | bytes 147464 | tf_op jit(solution)/shard_map/ppermute | solution.py:391
  41.1 4.0 %collective-permute-start.13 = (bf16[24,1024]{1,0:T(8,128)(2,1)S(1)}, bf16[24,1024]{1,0:T(8,128)(2,1)S(1)}, u32[]{:S(2)}, u32[]{:S(2)}) collective-permute-start(bf16[24,1024]{1,0:T(8,128)(2,1)S(1)} %add_convert_fusion.5.refs_0_), channel_id=1, source_target_pairs={{0,17},{1,16},{2,19},{3,18},{16,1},{17,0},{18,3},{19,2},{4,21},{5,... | collective-permute-start | bytes 147464 | tf_op jit(solution)/shard_map/ppermute | solution.py:391
  42.3 4.7 %collective-permute-start.20 = (bf16[2,24,1024]{2,1,0:T(8,128)(2,1)S(1)}, bf16[2,24,1024]{2,1,0:T(8,128)(2,1)S(1)}, u32[]{:S(2)}, u32[]{:S(2)}) collective-permute-start(bf16[2,24,1024]{2,1,0:T(8,128)(2,1)S(1)} %add_convert_fusion.1.refs_11_), channel_id=1, source_target_pairs={{0,1},{1,0},{2,3},{3,2},{4,5},{5,4},{6,7},{7,6},{8,9},{9,8},{10,11... | collective-permute-start | bytes 294920 | tf_op jit(solution)/shard_map/ppermute | solution.py:394
  42.4 3.2 %collective-permute-start.22 = (bf16[24,1024]{1,0:T(8,128)(2,1)S(1)}, bf16[24,1024]{1,0:T(8,128)(2,1)S(1)}, u32[]{:S(2)}, u32[]{:S(2)}) collective-permute-start(bf16[24,1024]{1,0:T(8,128)(2,1)S(1)} %add_convert_fusion.5.refs_0_), channel_id=1, source_target_pairs={{0,1},{1,0},{2,3},{3,2},{4,5},{5,4},{6,7},{7,6},{8,9},{9,8},{10,11... | collective-permute-start | bytes 147464 | tf_op jit(solution)/shard_map/ppermute | solution.py:394
  42.8 2.8 %collective-permute-start.23 = (bf16[24,1024]{1,0:T(8,128)(2,1)S(1)}, bf16[24,1024]{1,0:T(8,128)(2,1)S(1)}, u32[]{:S(2)}, u32[]{:S(2)}) collective-permute-start(bf16[24,1024]{1,0:T(8,128)(2,1)S(1)} %collective-permute-done.21.refs_1_), channel_id=1, source_target_pairs={{0,1},{1,0},{2,3},{3,2},{4,5},{5,4},{6,7},{7,6},{8,9},{9,8},{10,11... | collective-permute-start | bytes 147464 | tf_op jit(solution)/shard_map/ppermute | solution.py:394
  45.1 1.8 %collective-permute-start.16 = (bf16[24,1024]{1,0:T(8,128)(2,1)S(1)}, bf16[24,1024]{1,0:T(8,128)(2,1)S(1)}, u32[]{:S(2)}, u32[]{:S(2)}) collective-permute-start(bf16[24,1024]{1,0:T(8,128)(2,1)S(1)} %collective-permute-done.14.refs_7_), channel_id=1, source_target_pairs={{0,1},{1,0},{2,3},{3,2},{4,5},{5,4},{6,7},{7,6},{8,9},{9,8},{10,11... | collective-permute-start | bytes 147464 | tf_op jit(solution)/shard_map/ppermute | solution.py:394
  45.1 1.8 %collective-permute-start.15 = (bf16[24,1024]{1,0:T(8,128)(2,1)S(1)}, bf16[24,1024]{1,0:T(8,128)(2,1)S(1)}, u32[]{:S(2)}, u32[]{:S(2)}) collective-permute-start(bf16[24,1024]{1,0:T(8,128)(2,1)S(1)} %collective-permute-done.13.refs_6_), channel_id=1, source_target_pairs={{0,1},{1,0},{2,3},{3,2},{4,5},{5,4},{6,7},{7,6},{8,9},{9,8},{10,11... | collective-permute-start | bytes 147464 | tf_op jit(solution)/shard_map/ppermute | solution.py:394

commit v16 on v15

--- a/solution.py
+++ b/solution.py
@@ -475,12 +475,13 @@
     )
     turns = [t for t in range(2 * n_dp - 1, 0, -1)]
     in_share = total_of([in_pieces[0]] + [swap(in_pieces[t], ("dp", "y"), t) for t in turns])
-    out_total = add(out_block, swap(out_block, ("y",), 1)[::-1])
+    out_total = out_block
     in_total = total_of([in_share] + [swap(in_share, ("hi",), t) for t in range(1, n_hi)])
     turn = 1
     while turn < n_hi:
         out_total = add(out_total, swap(out_total, ("hi",), turn))
         turn = 2 * turn
+    out_total = add(out_total, swap(out_total, ("y",), 1)[::-1])
     spread = {t: swap(in_total, ("dp", "y"), t) for t in turns}
     back = [in_total] + [spread[t] for t in range(1, 2 * n_dp)]
     crossed = [other_core(one) for one in back]

time: 48.5 us -> 48.7 us (level)
  starting transfers between devices: 23 us -> 23.8 us
  waiting for transfers between devices: 9.14 us -> 8.55 us
    ppermute x15, starting transfers between devices: 20.9 us -> 21.8 us  [swap(): lax.ppermute(value, axes + ('c',), [(i, i ^ turn) for i in range(count)])]
    ppermute x15, waiting for transfers between devices: 8.56 us -> 7.96 us  [swap(): lax.ppermute(value, axes + ('c',), [(i, i ^ turn) for i in range(count)])]
  transfers between devices with their start and end apart: 24 -> 24, of which waited for: 10 -> 11; matrix products, arithmetic and copies ran while one was open for 0% -> 0% of each run, Pallas kernels for 24% -> 24%
where the time goes in v16:
time: 48.7 us; the launch traced here: 48.5 us
  starting transfers between devices  23.8 us (49%)
  Pallas kernels  15 us (31%)
  waiting for transfers between devices  8.55 us (18%)
  between operations  0.92 us (2%)
    ppermute x15, starting transfers between devices, swap(): lax.ppermute(value, axes + ('c',), [(i, i ^ turn) for i in range(count)])  21.8 us
    pallas_call x13, Pallas kernels, run(): pl.pallas_call(functools.partial(kernel, n_dp), out_shape=kinds, in_specs...  15 us
    ppermute x15, waiting for transfers between devices, swap(): lax.ppermute(value, axes + ('c',), [(i, i ^ turn) for i in range(count)])  7.96 us
    ppermute x9, starting transfers between devices, other_core(): return lax.ppermute(value, ('c',), [(0, 1), (1, 0)])  1.94 us
  transfers between devices with their start and end apart: 24, of which 11 were waited for; matrix products, arithmetic and copies ran while one was open for 0% of the time, Pallas kernels for 24%

profile of v16, /device:TPU:0, one launch (start us, length us, event | category | flops | bytes accessed | tf_op | source)
XLA Modules:
  0.0 48.5 jit_solution(4169770341221525866)
XLA Ops:
  0.7 1.1 %cut.1 = bf16[24,2048]{1,0:T(8,128)(2,1)S(1)} custom-call(bf16[24,4096]{1,0:T(8,128)(2,1)} %refs_10_.1), custom_call_target="tpu_custom_call" | custom-call | bytes 98304 | tf_op jit(solution)/shard_map/cut/pallas_call | solution.py:366
  1.7 3.0 %collective-permute-start = (bf16[24,2048]{1,0:T(8,128)(2,1)S(1)}, bf16[24,2048]{1,0:T(8,128)(2,1)S(1)}, u32[]{:S(2)}, u32[]{:S(2)}) collective-permute-start(bf16[24,2048]{1,0:T(8,128)(2,1)S(1)} %cut.1), channel_id=1, source_target_pairs={{0,16},{1,17},{16,0},{17,1},{2,18},{3,19},{18,2},{19,3},{4,20},{5,... | collective-permute-start | bytes 294920 | tf_op jit(solution)/shard_map/ppermute | solution.py:391
  4.7 1.1 %gates.1.refs_0_.refs_3_.refs_4_ = bf16[24,2304]{1,0:T(8,128)(2,1)S(1)} custom-call(s32[8,24]{1,0:T(8,128)} %bitcast.35, f32[8,24]{1,0:T(8,128)} %bitcast.36, bf16[24,128]{1,0:T(8,128)(2,1)} %context.1, bf16[24,4096]{1,0:T(8,128)(2,1)} %grads.3, bf16[4096,768]{1,0:T(8,128)(2,1)} %bitcast.17, bf16[4096,768]{1,0:T(8,128)(2,1)} %bitcast.24, ...), custom_call_target="tpu_custom_call" | custom-call | bytes 25165824 | tf_op jit(solution)/shard_map/gates/pallas_call | solution.py:366
  5.9 0.6 %collective-permute-start.2 = (bf16[24,2304]{1,0:T(8,128)(2,1)S(1)}, bf16[24,2304]{1,0:T(8,128)(2,1)S(1)}, u32[]{:S(2)}, u32[]{:S(2)}) collective-permute-start(bf16[24,2304]{1,0:T(8,128)(2,1)S(1)} %gates.1.refs_0_.refs_3_.refs_4_), channel_id=1, source_target_pairs={{0,16},{1,17},{16,0},{17,1},{2,18},{3,19},{18,2},{19,3},{4,20},{5,... | collective-permute-start | bytes 331784 | tf_op jit(solution)/shard_map/ppermute | solution.py:391
  6.4 1.1 %collective-permute-done.refs_0_ = bf16[24,2048]{1,0:T(8,128)(2,1)S(1)} collective-permute-done((bf16[24,2048]{1,0:T(8,128)(2,1)S(1)}, bf16[24,2048]{1,0:T(8,128)(2,1)S(1)}, u32[]{:S(2)}, u32[]{:S(2)}) %collective-permute-start) | collective-permute-done | bytes 98336 | tf_op jit(solution)/shard_map/ppermute | solution.py:391
  7.6 1.2 %hidden_first.1 = (f32[48,768]{1,0:T(8,128)S(1)}, f32[48,768]{1,0:T(8,128)S(1)}, f32[48,128]{1,0:T(8,128)S(1)}) custom-call(bf16[24,4096]{1,0:T(8,128)(2,1)S(1)} %copy-done, bf16[24,2048]{1,0:T(8,128)(2,1)S(1)} %collective-permute-done.refs_0_, f32[1,4096]{1,0:T(1,128)S(1)} %bitcast.31, bf16[4096,768]{1,0:T(8,128)(2,1)S(1)} %bitcast.20, ...), custom_call_target="tpu_custom_call" | custom-call | bytes 6291456 | tf_op jit(solution)/shard_map/hidden_first/pallas_call | solution.py:366
  8.8 0.0 collective-permute-done.1.refs_0_.refs_1_
  8.8 1.2 %hidden_rest.1 = (f32[48,768]{1,0:T(8,128)S(1)}, f32[48,768]{1,0:T(8,128)S(1)}, bf16[48,768]{1,0:T(8,128)(2,1)S(1)}, f32[48,128]{1,0:T(8,128)S(1)}) custom-call(bf16[24,4096]{1,0:T(8,128)(2,1)S(1)} %copy-done, bf16[24,2048]{1,0:T(8,128)(2,1)S(1)} %collective-permute-done.1.refs_0_.refs_1_, f32[1,4096]{1,0:T(1,128)S(1)} %bitcast.32, ...), custom_call_target="tpu_custom_call" | custom-call | bytes 6291456 | tf_op jit(solution)/shard_map/hidden_rest/pallas_call | solution.py:366
  10.1 0.6 %collective-permute-done.2.refs_1_.refs_4_.refs_2_.refs_5_ = bf16[24,2304]{1,0:T(8,128)(2,1)S(1)} collective-permute-done((bf16[24,2304]{1,0:T(8,128)(2,1)S(1)}, bf16[24,2304]{1,0:T(8,128)(2,1)S(1)}, u32[]{:S(2)}, u32[]{:S(2)}) %collective-permute-start.2) | collective-permute-done | bytes 110624 | tf_op jit(solution)/shard_map/ppermute | solution.py:391
  10.7 0.7 %outward_send.1.refs_4_ = bf16[2,2,24,1024]{3,2,1,0:T(8,128)(2,1)S(1)} custom-call(bf16[24,2304]{1,0:T(8,128)(2,1)S(1)} %gates.1.refs_0_.refs_3_.refs_4_, bf16[24,2304]{1,0:T(8,128)(2,1)S(1)} %collective-permute-done.2.refs_1_.refs_4_.refs_2_.refs_5_, bf16[48,768]{1,0:T(8,128)(2,1)S(1)} %get-tuple-element.37.refs_2_, bf16[768,4096]{1,0:T(8,128)(2,1)S(1)} %bitcast.13), custom_call_target="tpu_custom_call" | custom-call | bytes 3145728 | tf_op jit(solution)/shard_map/outward_send/pallas_call | solution.py:366
  11.4 0.5 %collective-permute-start.4 = (bf16[2,2,24,1024]{3,2,1,0:T(8,128)(2,1)S(1)}, bf16[2,2,24,1024]{3,2,1,0:T(8,128)(2,1)S(1)}, u32[]{:S(2)}, u32[]{:S(2)}) collective-permute-start(bf16[2,2,24,1024]{3,2,1,0:T(8,128)(2,1)S(1)} %outward_send.1.refs_4_), channel_id=1, source_target_pairs={{0,1},{1,0},{2,3},{3,2},{4,5},{5,4},{6,7},{7,6},{8,9},{9,8},{10,11... | collective-permute-start | bytes 589832 | tf_op jit(solution)/shard_map/ppermute | solution.py:394
  11.9 0.1 collective-permute-start.3
  12.0 0.7 %outward_keep.1.refs_8_ = bf16[2,2,24,1024]{3,2,1,0:T(8,128)(2,1)S(1)} custom-call(bf16[24,2304]{1,0:T(8,128)(2,1)S(1)} %gates.1.refs_0_.refs_3_.refs_4_, bf16[24,2304]{1,0:T(8,128)(2,1)S(1)} %collective-permute-done.2.refs_1_.refs_4_.refs_2_.refs_5_, bf16[48,768]{1,0:T(8,128)(2,1)S(1)} %get-tuple-element.37.refs_2_, bf16[768,4096]{1,0:T(8,128)(2,1)S(1)} %bitcast.14, ...), custom_call_target="tpu_custom_call" | custom-call | bytes 3145728 | tf_op jit(solution)/shard_map/outward_keep/pallas_call | solution.py:366
  12.7 0.6 %collective-permute-done.3.refs_2_.refs_3_ = bf16[24,2304]{1,0:T(8,128)(2,1)S(1)} collective-permute-done((bf16[24,2304]{1,0:T(8,128)(2,1)S(1)}, bf16[24,2304]{1,0:T(8,128)(2,1)S(1)}, u32[]{:S(2)}, u32[]{:S(2)}) %collective-permute-start.3) | collective-permute-done | bytes 110624 | tf_op jit(solution)/shard_map/ppermute | solution.py:394
  13.3 0.9 %backward_first.1 = (bf16[48,256]{1,0:T(8,128)(2,1)S(1)}, bf16[48,256]{1,0:T(8,128)(2,1)S(1)}, bf16[48,4096]{1,0:T(8,128)(2,1)S(1)}, bf16[2,2,24,1024]{3,2,1,0:T(8,128)(2,1)S(1)}) custom-call(bf16[24,4096]{1,0:T(8,128)(2,1)S(1)} %copy-done.1, bf16[24,2304]{1,0:T(8,128)(2,1)S(1)} %collective-permute-done.2.refs_1_.refs_4_.refs_2_.refs_5_, ...), custom_call_target="tpu_custom_call" | custom-call | bytes 2097152 | tf_op jit(solution)/shard_map/backward_first/pallas_call | solution.py:366
  14.2 0.1 add_convert_fusion
  14.3 2.3 %collective-permute-start.5 = (bf16[2,24,1024]{2,1,0:T(8,128)(2,1)S(1)}, bf16[2,24,1024]{2,1,0:T(8,128)(2,1)S(1)}, u32[]{:S(2)}, u32[]{:S(2)}) collective-permute-start(bf16[2,24,1024]{2,1,0:T(8,128)(2,1)S(1)} %get-tuple-element.60), channel_id=1, source_target_pairs={{0,17},{1,16},{16,1},{17,0},{2,19},{3,18},{18,3},{19,2},{4,21},{5,... | collective-permute-start | bytes 294920 | tf_op jit(solution)/shard_map/ppermute | solution.py:391
  16.6 1.4 %backward_rest.1 = (bf16[48,512]{1,0:T(8,128)(2,1)S(1)}, bf16[48,512]{1,0:T(8,128)(2,1)S(1)}, bf16[2,24,1024]{2,1,0:T(8,128)(2,1)S(1)}) custom-call(bf16[48,4096]{1,0:T(8,128)(2,1)S(1)} %get-tuple-element.40.weighted, f32[48,768]{1,0:T(8,128)S(1)} %get-tuple-element.35.refs_5_.pre_gate, f32[48,768]{1,0:T(8,128)S(1)} %get-tuple-element.36.refs_6_.pre_up, ...), custom_call_target="tpu_custom_call" | custom-call | bytes 4194304 | tf_op jit(solution)/shard_map/backward_rest/pallas_call | solution.py:366
  18.0 2.0 %inward_send.1 = (bf16[2,2,24,1024]{3,2,1,0:T(8,128)(2,1)S(1)}, bf16[2,24,1024]{2,1,0:T(8,128)(2,1)S(1)}) custom-call(bf16[48,256]{1,0:T(8,128)(2,1)S(1)} %get-tuple-element.38.refs_0_, bf16[48,256]{1,0:T(8,128)(2,1)S(1)} %get-tuple-element.39.refs_1_, bf16[48,512]{1,0:T(8,128)(2,1)S(1)} %get-tuple-element.42.refs_2_, ...), custom_call_target="tpu_custom_call" | custom-call | bytes 6291456 | tf_op jit(solution)/shard_map/inward_send/pallas_call | solution.py:366
  20.0 0.3 collective-permute-start.6
  20.3 2.0 %inward_keep.1 = (bf16[2,2,24,1024]{3,2,1,0:T(8,128)(2,1)S(1)}, bf16[2,24,1024]{2,1,0:T(8,128)(2,1)S(1)}) custom-call(bf16[48,256]{1,0:T(8,128)(2,1)S(1)} %get-tuple-element.38.refs_0_, bf16[48,256]{1,0:T(8,128)(2,1)S(1)} %get-tuple-element.39.refs_1_, bf16[48,512]{1,0:T(8,128)(2,1)S(1)} %get-tuple-element.42.refs_2_, ...), custom_call_target="tpu_custom_call" | custom-call | bytes 6291456 | tf_op jit(solution)/shard_map/inward_keep/pallas_call | solution.py:366
  22.3 0.1 join.1
  22.4 1.2 %collective-permute-start.17 = (bf16[2,24,1024]{2,1,0:T(8,128)(2,1)S(1)}, bf16[2,24,1024]{2,1,0:T(8,128)(2,1)S(1)}, u32[]{:S(2)}, u32[]{:S(2)}) collective-permute-start(bf16[2,24,1024]{2,1,0:T(8,128)(2,1)S(1)} %get-tuple-element.53), channel_id=1, source_target_pairs={{0,5},{1,4},{4,1},{5,0},{8,13},{9,12},{12,9},{13,8},{2,7},{3,6},{6... | collective-permute-start | bytes 294920 | tf_op jit(solution)/shard_map/ppermute | solution.py:391
  23.6 2.0 %collective-permute-start.7 = (bf16[24,1024]{1,0:T(8,128)(2,1)S(1)}, bf16[24,1024]{1,0:T(8,128)(2,1)S(1)}, u32[]{:S(2)}, u32[]{:S(2)}) collective-permute-start(bf16[24,1024]{1,0:T(8,128)(2,1)S(1)} %get-tuple-element.50), channel_id=1, source_target_pairs={{0,18},{1,19},{2,16},{3,17},{16,2},{17,3},{18,0},{19,1},{4,22},{5,... | collective-permute-start | bytes 147464 | tf_op jit(solution)/shard_map/ppermute | solution.py:391
  25.6 0.5 %collective-permute-start.8 = (bf16[24,1024]{1,0:T(8,128)(2,1)S(1)}, bf16[24,1024]{1,0:T(8,128)(2,1)S(1)}, u32[]{:S(2)}, u32[]{:S(2)}) collective-permute-start(bf16[24,1024]{1,0:T(8,128)(2,1)S(1)} %get-tuple-element.51), channel_id=1, source_target_pairs={{0,17},{1,16},{2,19},{3,18},{16,1},{17,0},{18,3},{19,2},{4,21},{5,... | collective-permute-start | bytes 147464 | tf_op jit(solution)/shard_map/ppermute | solution.py:391
  26.1 0.7 %collective-permute-start.9 = (bf16[24,1024]{1,0:T(8,128)(2,1)S(1)}, bf16[24,1024]{1,0:T(8,128)(2,1)S(1)}, u32[]{:S(2)}, u32[]{:S(2)}) collective-permute-start(bf16[24,1024]{1,0:T(8,128)(2,1)S(1)} %get-tuple-element.52), channel_id=1, source_target_pairs={{0,3},{1,2},{2,1},{3,0},{16,19},{17,18},{18,17},{19,16},{4,7},{5,6... | collective-permute-start | bytes 147464 | tf_op jit(solution)/shard_map/ppermute | solution.py:391
  26.8 0.4 collective-permute-done.17
  27.2 2.1 %collective-permute-start.18 = (bf16[2,24,1024]{2,1,0:T(8,128)(2,1)S(1)}, bf16[2,24,1024]{2,1,0:T(8,128)(2,1)S(1)}, u32[]{:S(2)}, u32[]{:S(2)}) collective-permute-start(bf16[2,24,1024]{2,1,0:T(8,128)(2,1)S(1)} %add_convert_fusion.3), channel_id=1, source_target_pairs={{0,9},{1,8},{4,13},{5,12},{8,1},{9,0},{12,5},{13,4},{2,11},{3,10},... | collective-permute-start | bytes 294920 | tf_op jit(solution)/shard_map/ppermute | solution.py:391
  29.3 0.2 collective-permute-done.8
  29.5 0.1 collective-permute-done.9
  29.7 2.5 %collective-permute-start.12 = (bf16[24,1024]{1,0:T(8,128)(2,1)S(1)}, bf16[24,1024]{1,0:T(8,128)(2,1)S(1)}, u32[]{:S(2)}, u32[]{:S(2)}) collective-permute-start(bf16[24,1024]{1,0:T(8,128)(2,1)S(1)} %add_convert_fusion.6), channel_id=1, source_target_pairs={{0,12},{1,13},{4,8},{5,9},{8,4},{9,5},{12,0},{13,1},{2,14},{3,15},... | collective-permute-start | bytes 147464 | tf_op jit(solution)/shard_map/ppermute | solution.py:391
  32.2 0.4 collective-permute-start.11
  32.5 1.3 %collective-permute-start.10 = (bf16[24,1024]{1,0:T(8,128)(2,1)S(1)}, bf16[24,1024]{1,0:T(8,128)(2,1)S(1)}, u32[]{:S(2)}, u32[]{:S(2)}) collective-permute-start(bf16[24,1024]{1,0:T(8,128)(2,1)S(1)} %add_convert_fusion.6), channel_id=1, source_target_pairs={{0,5},{1,4},{4,1},{5,0},{8,13},{9,12},{12,9},{13,8},{2,7},{3,6},{6... | collective-permute-start | bytes 147464 | tf_op jit(solution)/shard_map/ppermute | solution.py:391
  33.8 2.3 %collective-permute-done.18 = bf16[2,24,1024]{2,1,0:T(8,128)(2,1)S(1)} collective-permute-done((bf16[2,24,1024]{2,1,0:T(8,128)(2,1)S(1)}, bf16[2,24,1024]{2,1,0:T(8,128)(2,1)S(1)}, u32[]{:S(2)}, u32[]{:S(2)}) %collective-permute-start.18) | collective-permute-done | bytes 98336 | tf_op jit(solution)/shard_map/ppermute | solution.py:391
  36.2 2.3 %collective-permute-start.19 = (bf16[2,24,1024]{2,1,0:T(8,128)(2,1)S(1)}, bf16[2,24,1024]{2,1,0:T(8,128)(2,1)S(1)}, u32[]{:S(2)}, u32[]{:S(2)}) collective-permute-start(bf16[2,24,1024]{2,1,0:T(8,128)(2,1)S(1)} %add_convert_fusion.2), channel_id=1, source_target_pairs={{0,3},{1,2},{2,1},{3,0},{4,7},{5,6},{6,5},{7,4},{8,11},{9,10},{10,... | collective-permute-start | bytes 294920 | tf_op jit(solution)/shard_map/ppermute | solution.py:391
  38.5 0.8 %collective-permute-done.11 = bf16[24,1024]{1,0:T(8,128)(2,1)S(1)} collective-permute-done((bf16[24,1024]{1,0:T(8,128)(2,1)S(1)}, bf16[24,1024]{1,0:T(8,128)(2,1)S(1)}, u32[]{:S(2)}, u32[]{:S(2)}) %collective-permute-start.11) | collective-permute-done | bytes 49184 | tf_op jit(solution)/shard_map/ppermute | solution.py:391
  39.3 1.0 %collective-permute-start.21 = (bf16[24,1024]{1,0:T(8,128)(2,1)S(1)}, bf16[24,1024]{1,0:T(8,128)(2,1)S(1)}, u32[]{:S(2)}, u32[]{:S(2)}) collective-permute-start(bf16[24,1024]{1,0:T(8,128)(2,1)S(1)} %add_convert_fusion.5.refs_0_), channel_id=1, source_target_pairs={{0,3},{1,2},{2,1},{3,0},{16,19},{17,18},{18,17},{19,16},{4,7},{5,6... | collective-permute-start | bytes 147464 | tf_op jit(solution)/shard_map/ppermute | solution.py:391
  40.3 1.5 %collective-permute-start.14 = (bf16[24,1024]{1,0:T(8,128)(2,1)S(1)}, bf16[24,1024]{1,0:T(8,128)(2,1)S(1)}, u32[]{:S(2)}, u32[]{:S(2)}) collective-permute-start(bf16[24,1024]{1,0:T(8,128)(2,1)S(1)} %add_convert_fusion.5.refs_0_), channel_id=1, source_target_pairs={{0,18},{1,19},{2,16},{3,17},{16,2},{17,3},{18,0},{19,1},{4,22},{5,... | collective-permute-start | bytes 147464 | tf_op jit(solution)/shard_map/ppermute | solution.py:391
  41.8 0.5 %collective-permute-start.13 = (bf16[24,1024]{1,0:T(8,128)(2,1)S(1)}, bf16[24,1024]{1,0:T(8,128)(2,1)S(1)}, u32[]{:S(2)}, u32[]{:S(2)}) collective-permute-start(bf16[24,1024]{1,0:T(8,128)(2,1)S(1)} %add_convert_fusion.5.refs_0_), channel_id=1, source_target_pairs={{0,17},{1,16},{2,19},{3,18},{16,1},{17,0},{18,3},{19,2},{4,21},{5,... | collective-permute-start | bytes 147464 | tf_op jit(solution)/shard_map/ppermute | solution.py:391
  42.3 0.5 %collective-permute-start.20 = (bf16[2,24,1024]{2,1,0:T(8,128)(2,1)S(1)}, bf16[2,24,1024]{2,1,0:T(8,128)(2,1)S(1)}, u32[]{:S(2)}, u32[]{:S(2)}) collective-permute-start(bf16[2,24,1024]{2,1,0:T(8,128)(2,1)S(1)} %add_convert_fusion.1.refs_11_), channel_id=1, source_target_pairs={{0,1},{1,0},{2,3},{3,2},{4,5},{5,4},{6,7},{7,6},{8,9},{9,8},{10,11... | collective-permute-start | bytes 294920 | tf_op jit(solution)/shard_map/ppermute | solution.py:394
  42.8 0.1 collective-permute-start.22
  42.9 0.2 collective-permute-done.21.refs_1_
  43.1 0.2 collective-permute-start.23
  43.3 2.0 %collective-permute-done.14.refs_7_ = bf16[24,1024]{1,0:T(8,128)(2,1)S(1)} collective-permute-done((bf16[24,1024]{1,0:T(8,128)(2,1)S(1)}, bf16[24,1024]{1,0:T(8,128)(2,1)S(1)}, u32[]{:S(2)}, u32[]{:S(2)}) %collective-permute-start.14) | collective-permute-done | bytes 49184 | tf_op jit(solution)/shard_map/ppermute | solution.py:391
  45.3 0.3 collective-permute-done.13.refs_6_
  45.6 0.2 collective-permute-start.15
  45.8 1.3 %own_rows.1 = (bf16[24,4096]{1,0:T(8,128)(2,1)}, bf16[24,128]{1,0:T(8,128)(2,1)}, bf16[24,2048]{1,0:T(8,128)(2,1)S(1)}) custom-call(bf16[24,4096]{1,0:T(8,128)(2,1)S(1)} %copy-done, bf16[24,4096]{1,0:T(8,128)(2,1)S(1)} %copy-done.1, bf16[24,1024]{1,0:T(8,128)(2,1)S(1)} %add_convert_fusion.5.refs_0_, bf16[24,1024]{1,0:T(8,128)(2,1)S(1)} %collective-permute-done.21.refs_1_, ...), custom_call_target="tpu_custom_call" | custom-call | bytes 3145728 | tf_op jit(solution)/shard_map/own_rows/pallas_call | solution.py:366
  47.1 1.4 %far_rows.1 = (bf16[24,4096]{1,0:T(8,128)(2,1)}, bf16[128,2048]{1,0:T(8,128)(2,1)}) custom-call(bf16[24,2048]{1,0:T(8,128)(2,1)S(1)} %collective-permute-done.refs_0_, bf16[24,2048]{1,0:T(8,128)(2,1)S(1)} %collective-permute-done.1.refs_0_.refs_1_, bf16[24,2304]{1,0:T(8,128)(2,1)S(1)} %collective-permute-done.2.refs_1_.refs_4_.refs_2_.refs_5_, ...), custom_call_target="tpu_custom_call" | custom-call | bytes 3145728 | tf_op jit(solution)/shard_map/far_rows/pallas_call | solution.py:366
  (44 shorter events, 0.3 us)
Async XLA Ops:
  0.6 6.9 %slice-start.2 = ((s8[6291456]{0:T(1024)(128)(4,1)}), s8[4194304]{0:T(1024)(128)(4,1)S(1)}, s32[]{:S(2)}) async-start(s8[6291456]{0:T(1024)(128)(4,1)} %bitcast.18), calls=%async_computation.2 | async-start | bytes 8388608
  0.6 6.9 %slice-start.4 = ((s8[6291456]{0:T(1024)(128)(4,1)}), s8[4194304]{0:T(1024)(128)(4,1)S(1)}, s32[]{:S(2)}) async-start(s8[6291456]{0:T(1024)(128)(4,1)} %bitcast.25), calls=%async_computation.4 | async-start | bytes 8388608
  1.7 5.8 %collective-permute-start = (bf16[24,2048]{1,0:T(8,128)(2,1)S(1)}, bf16[24,2048]{1,0:T(8,128)(2,1)S(1)}, u32[]{:S(2)}, u32[]{:S(2)}) collective-permute-start(bf16[24,2048]{1,0:T(8,128)(2,1)S(1)} %cut.1), channel_id=1, source_target_pairs={{0,16},{1,17},{16,0},{17,1},{2,18},{3,19},{18,2},{19,3},{4,20},{5,... | collective-permute-start | bytes 294920 | tf_op jit(solution)/shard_map/ppermute | solution.py:391
  4.7 2.8 %slice-start.3 = ((s8[6291456]{0:T(1024)(128)(4,1)}), s8[2097152]{0:T(1024)(128)(4,1)S(1)}, s32[]{:S(2)}) async-start(s8[6291456]{0:T(1024)(128)(4,1)} %bitcast.18), calls=%async_computation.3 | async-start | bytes 4194304
  4.7 2.8 %slice-start.5 = ((s8[6291456]{0:T(1024)(128)(4,1)}), s8[2097152]{0:T(1024)(128)(4,1)S(1)}, s32[]{:S(2)}) async-start(s8[6291456]{0:T(1024)(128)(4,1)} %bitcast.25), calls=%async_computation.5 | async-start | bytes 4194304
  4.7 2.8 %copy-start = (bf16[24,4096]{1,0:T(8,128)(2,1)S(1)}, bf16[24,4096]{1,0:T(8,128)(2,1)}, u32[]{:S(2)}) copy-start(bf16[24,4096]{1,0:T(8,128)(2,1)} %refs_10_.1) | copy-start | bytes 589828
  4.7 2.8 %copy-start.3 = (f32[4096]{0:T(1024)S(1)}, f32[4096]{0:T(1024)}, u32[]{:S(2)}) copy-start(f32[4096]{0:T(1024)} %param.11) | copy-start | bytes 49156
  5.9 4.8 %collective-permute-start.2 = (bf16[24,2304]{1,0:T(8,128)(2,1)S(1)}, bf16[24,2304]{1,0:T(8,128)(2,1)S(1)}, u32[]{:S(2)}, u32[]{:S(2)}) collective-permute-start(bf16[24,2304]{1,0:T(8,128)(2,1)S(1)} %gates.1.refs_0_.refs_3_.refs_4_), channel_id=1, source_target_pairs={{0,16},{1,17},{16,0},{17,1},{2,18},{3,19},{18,2},{19,3},{4,20},{5,... | collective-permute-start | bytes 331784 | tf_op jit(solution)/shard_map/ppermute | solution.py:391
  7.5 1.3 %collective-permute-start.1 = (bf16[24,2048]{1,0:T(8,128)(2,1)S(1)}, bf16[24,2048]{1,0:T(8,128)(2,1)S(1)}, u32[]{:S(2)}, u32[]{:S(2)}) collective-permute-start(bf16[24,2048]{1,0:T(8,128)(2,1)S(1)} %collective-permute-done.refs_0_), channel_id=1, source_target_pairs={{0,1},{1,0},{2,3},{3,2},{4,5},{5,4},{6,7},{7,6},{8,9},{9,8},{10,11... | collective-permute-start | bytes 294920 | tf_op jit(solution)/shard_map/ppermute | solution.py:394
  7.6 3.1 %slice-start = ((s8[6291456]{0:T(1024)(128)(4,1)}), s8[4194304]{0:T(1024)(128)(4,1)S(1)}, s32[]{:S(2)}) async-start(s8[6291456]{0:T(1024)(128)(4,1)} %bitcast.11), calls=%async_computation | async-start | bytes 8388608
  8.8 1.9 %slice-start.1 = ((s8[6291456]{0:T(1024)(128)(4,1)}), s8[2097152]{0:T(1024)(128)(4,1)S(1)}, s32[]{:S(2)}) async-start(s8[6291456]{0:T(1024)(128)(4,1)} %bitcast.11), calls=%async_computation.1 | async-start | bytes 4194304
  10.7 2.6 %copy-start.1 = (bf16[24,4096]{1,0:T(8,128)(2,1)S(1)}, bf16[24,4096]{1,0:T(8,128)(2,1)}, u32[]{:S(2)}) copy-start(bf16[24,4096]{1,0:T(8,128)(2,1)} %grads.3) | copy-start | bytes 589828
  11.4 2.7 %collective-permute-start.4 = (bf16[2,2,24,1024]{3,2,1,0:T(8,128)(2,1)S(1)}, bf16[2,2,24,1024]{3,2,1,0:T(8,128)(2,1)S(1)}, u32[]{:S(2)}, u32[]{:S(2)}) collective-permute-start(bf16[2,2,24,1024]{3,2,1,0:T(8,128)(2,1)S(1)} %outward_send.1.refs_4_), channel_id=1, source_target_pairs={{0,1},{1,0},{2,3},{3,2},{4,5},{5,4},{6,7},{7,6},{8,9},{9,8},{10,11... | collective-permute-start | bytes 589832 | tf_op jit(solution)/shard_map/ppermute | solution.py:394
  11.9 1.3 %collective-permute-start.3 = (bf16[24,2304]{1,0:T(8,128)(2,1)S(1)}, bf16[24,2304]{1,0:T(8,128)(2,1)S(1)}, u32[]{:S(2)}, u32[]{:S(2)}) collective-permute-start(bf16[24,2304]{1,0:T(8,128)(2,1)S(1)} %collective-permute-done.2.refs_1_.refs_4_.refs_2_.refs_5_), channel_id=1, source_target_pairs={{0,1},{1,0},{2,3},{3,2},{4,5},{5,4},{6,7},{7,6},{8,9},{9,8},{10,11... | collective-permute-start | bytes 331784 | tf_op jit(solution)/shard_map/ppermute | solution.py:394
  14.3 6.0 %collective-permute-start.5 = (bf16[2,24,1024]{2,1,0:T(8,128)(2,1)S(1)}, bf16[2,24,1024]{2,1,0:T(8,128)(2,1)S(1)}, u32[]{:S(2)}, u32[]{:S(2)}) collective-permute-start(bf16[2,24,1024]{2,1,0:T(8,128)(2,1)S(1)} %get-tuple-element.60), channel_id=1, source_target_pairs={{0,17},{1,16},{16,1},{17,0},{2,19},{3,18},{18,3},{19,2},{4,21},{5,... | collective-permute-start | bytes 294920 | tf_op jit(solution)/shard_map/ppermute | solution.py:391
  20.0 2.3 %collective-permute-start.6 = (bf16[2,2,24,1024]{3,2,1,0:T(8,128)(2,1)S(1)}, bf16[2,2,24,1024]{3,2,1,0:T(8,128)(2,1)S(1)}, u32[]{:S(2)}, u32[]{:S(2)}) collective-permute-start(bf16[2,2,24,1024]{3,2,1,0:T(8,128)(2,1)S(1)} %get-tuple-element.47), channel_id=1, source_target_pairs={{0,1},{1,0},{2,3},{3,2},{4,5},{5,4},{6,7},{7,6},{8,9},{9,8},{10,11... | collective-permute-start | bytes 589832 | tf_op jit(solution)/shard_map/ppermute | solution.py:394
  20.3 25.5 %copy-start.2 = (bf16[128,4096]{1,0:T(8,128)(2,1)S(1)}, bf16[128,4096]{1,0:T(8,128)(2,1)}, u32[]{:S(2)}) copy-start(bf16[128,4096]{1,0:T(8,128)(2,1)} %refs_6_.1) | copy-start | bytes 3145732
  22.4 4.8 %collective-permute-start.17 = (bf16[2,24,1024]{2,1,0:T(8,128)(2,1)S(1)}, bf16[2,24,1024]{2,1,0:T(8,128)(2,1)S(1)}, u32[]{:S(2)}, u32[]{:S(2)}) collective-permute-start(bf16[2,24,1024]{2,1,0:T(8,128)(2,1)S(1)} %get-tuple-element.53), channel_id=1, source_target_pairs={{0,5},{1,4},{4,1},{5,0},{8,13},{9,12},{12,9},{13,8},{2,7},{3,6},{6... | collective-permute-start | bytes 294920 | tf_op jit(solution)/shard_map/ppermute | solution.py:391
  23.6 5.7 %collective-permute-start.7 = (bf16[24,1024]{1,0:T(8,128)(2,1)S(1)}, bf16[24,1024]{1,0:T(8,128)(2,1)S(1)}, u32[]{:S(2)}, u32[]{:S(2)}) collective-permute-start(bf16[24,1024]{1,0:T(8,128)(2,1)S(1)} %get-tuple-element.50), channel_id=1, source_target_pairs={{0,18},{1,19},{2,16},{3,17},{16,2},{17,3},{18,0},{19,1},{4,22},{5,... | collective-permute-start | bytes 147464 | tf_op jit(solution)/shard_map/ppermute | solution.py:391
  25.6 3.9 %collective-permute-start.8 = (bf16[24,1024]{1,0:T(8,128)(2,1)S(1)}, bf16[24,1024]{1,0:T(8,128)(2,1)S(1)}, u32[]{:S(2)}, u32[]{:S(2)}) collective-permute-start(bf16[24,1024]{1,0:T(8,128)(2,1)S(1)} %get-tuple-element.51), channel_id=1, source_target_pairs={{0,17},{1,16},{2,19},{3,18},{16,1},{17,0},{18,3},{19,2},{4,21},{5,... | collective-permute-start | bytes 147464 | tf_op jit(solution)/shard_map/ppermute | solution.py:391
  26.1 3.5 %collective-permute-start.9 = (bf16[24,1024]{1,0:T(8,128)(2,1)S(1)}, bf16[24,1024]{1,0:T(8,128)(2,1)S(1)}, u32[]{:S(2)}, u32[]{:S(2)}) collective-permute-start(bf16[24,1024]{1,0:T(8,128)(2,1)S(1)} %get-tuple-element.52), channel_id=1, source_target_pairs={{0,3},{1,2},{2,1},{3,0},{16,19},{17,18},{18,17},{19,16},{4,7},{5,6... | collective-permute-start | bytes 147464 | tf_op jit(solution)/shard_map/ppermute | solution.py:391
  27.2 9.0 %collective-permute-start.18 = (bf16[2,24,1024]{2,1,0:T(8,128)(2,1)S(1)}, bf16[2,24,1024]{2,1,0:T(8,128)(2,1)S(1)}, u32[]{:S(2)}, u32[]{:S(2)}) collective-permute-start(bf16[2,24,1024]{2,1,0:T(8,128)(2,1)S(1)} %add_convert_fusion.3), channel_id=1, source_target_pairs={{0,9},{1,8},{4,13},{5,12},{8,1},{9,0},{12,5},{13,4},{2,11},{3,10},... | collective-permute-start | bytes 294920 | tf_op jit(solution)/shard_map/ppermute | solution.py:391
  29.7 8.8 %collective-permute-start.12 = (bf16[24,1024]{1,0:T(8,128)(2,1)S(1)}, bf16[24,1024]{1,0:T(8,128)(2,1)S(1)}, u32[]{:S(2)}, u32[]{:S(2)}) collective-permute-start(bf16[24,1024]{1,0:T(8,128)(2,1)S(1)} %add_convert_fusion.6), channel_id=1, source_target_pairs={{0,12},{1,13},{4,8},{5,9},{8,4},{9,5},{12,0},{13,1},{2,14},{3,15},... | collective-permute-start | bytes 147464 | tf_op jit(solution)/shard_map/ppermute | solution.py:391
  32.2 7.1 %collective-permute-start.11 = (bf16[24,1024]{1,0:T(8,128)(2,1)S(1)}, bf16[24,1024]{1,0:T(8,128)(2,1)S(1)}, u32[]{:S(2)}, u32[]{:S(2)}) collective-permute-start(bf16[24,1024]{1,0:T(8,128)(2,1)S(1)} %add_convert_fusion.6), channel_id=1, source_target_pairs={{0,9},{1,8},{4,13},{5,12},{8,1},{9,0},{12,5},{13,4},{2,11},{3,10},... | collective-permute-start | bytes 147464 | tf_op jit(solution)/shard_map/ppermute | solution.py:391
  32.5 6.7 %collective-permute-start.10 = (bf16[24,1024]{1,0:T(8,128)(2,1)S(1)}, bf16[24,1024]{1,0:T(8,128)(2,1)S(1)}, u32[]{:S(2)}, u32[]{:S(2)}) collective-permute-start(bf16[24,1024]{1,0:T(8,128)(2,1)S(1)} %add_convert_fusion.6), channel_id=1, source_target_pairs={{0,5},{1,4},{4,1},{5,0},{8,13},{9,12},{12,9},{13,8},{2,7},{3,6},{6... | collective-permute-start | bytes 147464 | tf_op jit(solution)/shard_map/ppermute | solution.py:391
  36.2 6.1 %collective-permute-start.19 = (bf16[2,24,1024]{2,1,0:T(8,128)(2,1)S(1)}, bf16[2,24,1024]{2,1,0:T(8,128)(2,1)S(1)}, u32[]{:S(2)}, u32[]{:S(2)}) collective-permute-start(bf16[2,24,1024]{2,1,0:T(8,128)(2,1)S(1)} %add_convert_fusion.2), channel_id=1, source_target_pairs={{0,3},{1,2},{2,1},{3,0},{4,7},{5,6},{6,5},{7,4},{8,11},{9,10},{10,... | collective-permute-start | bytes 294920 | tf_op jit(solution)/shard_map/ppermute | solution.py:391
  39.3 3.8 %collective-permute-start.21 = (bf16[24,1024]{1,0:T(8,128)(2,1)S(1)}, bf16[24,1024]{1,0:T(8,128)(2,1)S(1)}, u32[]{:S(2)}, u32[]{:S(2)}) collective-permute-start(bf16[24,1024]{1,0:T(8,128)(2,1)S(1)} %add_convert_fusion.5.refs_0_), channel_id=1, source_target_pairs={{0,3},{1,2},{2,1},{3,0},{16,19},{17,18},{18,17},{19,16},{4,7},{5,6... | collective-permute-start | bytes 147464 | tf_op jit(solution)/shard_map/ppermute | solution.py:391
  40.3 5.0 %collective-permute-start.14 = (bf16[24,1024]{1,0:T(8,128)(2,1)S(1)}, bf16[24,1024]{1,0:T(8,128)(2,1)S(1)}, u32[]{:S(2)}, u32[]{:S(2)}) collective-permute-start(bf16[24,1024]{1,0:T(8,128)(2,1)S(1)} %add_convert_fusion.5.refs_0_), channel_id=1, source_target_pairs={{0,18},{1,19},{2,16},{3,17},{16,2},{17,3},{18,0},{19,1},{4,22},{5,... | collective-permute-start | bytes 147464 | tf_op jit(solution)/shard_map/ppermute | solution.py:391
  41.8 3.8 %collective-permute-start.13 = (bf16[24,1024]{1,0:T(8,128)(2,1)S(1)}, bf16[24,1024]{1,0:T(8,128)(2,1)S(1)}, u32[]{:S(2)}, u32[]{:S(2)}) collective-permute-start(bf16[24,1024]{1,0:T(8,128)(2,1)S(1)} %add_convert_fusion.5.refs_0_), channel_id=1, source_target_pairs={{0,17},{1,16},{2,19},{3,18},{16,1},{17,0},{18,3},{19,2},{4,21},{5,... | collective-permute-start | bytes 147464 | tf_op jit(solution)/shard_map/ppermute | solution.py:391
  42.3 4.8 %collective-permute-start.20 = (bf16[2,24,1024]{2,1,0:T(8,128)(2,1)S(1)}, bf16[2,24,1024]{2,1,0:T(8,128)(2,1)S(1)}, u32[]{:S(2)}, u32[]{:S(2)}) collective-permute-start(bf16[2,24,1024]{2,1,0:T(8,128)(2,1)S(1)} %add_convert_fusion.1.refs_11_), channel_id=1, source_target_pairs={{0,1},{1,0},{2,3},{3,2},{4,5},{5,4},{6,7},{7,6},{8,9},{9,8},{10,11... | collective-permute-start | bytes 294920 | tf_op jit(solution)/shard_map/ppermute | solution.py:394
  42.8 3.0 %collective-permute-start.22 = (bf16[24,1024]{1,0:T(8,128)(2,1)S(1)}, bf16[24,1024]{1,0:T(8,128)(2,1)S(1)}, u32[]{:S(2)}, u32[]{:S(2)}) collective-permute-start(bf16[24,1024]{1,0:T(8,128)(2,1)S(1)} %add_convert_fusion.5.refs_0_), channel_id=1, source_target_pairs={{0,1},{1,0},{2,3},{3,2},{4,5},{5,4},{6,7},{7,6},{8,9},{9,8},{10,11... | collective-permute-start | bytes 147464 | tf_op jit(solution)/shard_map/ppermute | solution.py:394
  43.1 2.7 %collective-permute-start.23 = (bf16[24,1024]{1,0:T(8,128)(2,1)S(1)}, bf16[24,1024]{1,0:T(8,128)(2,1)S(1)}, u32[]{:S(2)}, u32[]{:S(2)}) collective-permute-start(bf16[24,1024]{1,0:T(8,128)(2,1)S(1)} %collective-permute-done.21.refs_1_), channel_id=1, source_target_pairs={{0,1},{1,0},{2,3},{3,2},{4,5},{5,4},{6,7},{7,6},{8,9},{9,8},{10,11... | collective-permute-start | bytes 147464 | tf_op jit(solution)/shard_map/ppermute | solution.py:394
  45.3 1.8 %collective-permute-start.16 = (bf16[24,1024]{1,0:T(8,128)(2,1)S(1)}, bf16[24,1024]{1,0:T(8,128)(2,1)S(1)}, u32[]{:S(2)}, u32[]{:S(2)}) collective-permute-start(bf16[24,1024]{1,0:T(8,128)(2,1)S(1)} %collective-permute-done.14.refs_7_), channel_id=1, source_target_pairs={{0,1},{1,0},{2,3},{3,2},{4,5},{5,4},{6,7},{7,6},{8,9},{9,8},{10,11... | collective-permute-start | bytes 147464 | tf_op jit(solution)/shard_map/ppermute | solution.py:394
  45.6 1.6 %collective-permute-start.15 = (bf16[24,1024]{1,0:T(8,128)(2,1)S(1)}, bf16[24,1024]{1,0:T(8,128)(2,1)S(1)}, u32[]{:S(2)}, u32[]{:S(2)}) collective-permute-start(bf16[24,1024]{1,0:T(8,128)(2,1)S(1)} %collective-permute-done.13.refs_6_), channel_id=1, source_target_pairs={{0,1},{1,0},{2,3},{3,2},{4,5},{5,4},{6,7},{7,6},{8,9},{9,8},{10,11... | collective-permute-start | bytes 147464 | tf_op jit(solution)/shard_map/ppermute | solution.py:394

commit v17 on v16

--- a/solution.py
+++ b/solution.py
@@ -480,8 +480,9 @@
     turn = 1
     while turn < n_hi:
         out_total = add(out_total, swap(out_total, ("hi",), turn))
+        if turn == 1:
+            out_total = add(out_total, swap(out_total, ("y",), 1)[::-1])
         turn = 2 * turn
-    out_total = add(out_total, swap(out_total, ("y",), 1)[::-1])
     spread = {t: swap(in_total, ("dp", "y"), t) for t in turns}
     back = [in_total] + [spread[t] for t in range(1, 2 * n_dp)]
     crossed = [other_core(one) for one in back]

time: 48.7 us -> 48.2 us (0.990)
  starting transfers between devices: 23.8 us -> 23.1 us
    ppermute x15, starting transfers between devices: 21.8 us -> 20.9 us  [swap(): lax.ppermute(value, axes + ('c',), [(i, i ^ turn) for i in range(count)])]
  transfers between devices with their start and end apart: 24 -> 24, of which waited for: 11 -> 11; matrix products, arithmetic and copies ran while one was open for 0% -> 0% of each run, Pallas kernels for 24% -> 25%
where the time goes in v17:
time: 48.2 us; the launch traced here: 48.1 us
  starting transfers between devices  23.1 us (48%)
  Pallas kernels  15 us (31%)
  waiting for transfers between devices  8.78 us (18%)
  between operations  0.92 us (2%)
    ppermute x15, starting transfers between devices, swap(): lax.ppermute(value, axes + ('c',), [(i, i ^ turn) for i in range(count)])  20.9 us
    pallas_call x13, Pallas kernels, run(): pl.pallas_call(functools.partial(kernel, n_dp), out_shape=kinds, in_specs...  15 us
    ppermute x15, waiting for transfers between devices, swap(): lax.ppermute(value, axes + ('c',), [(i, i ^ turn) for i in range(count)])  8.2 us
    ppermute x9, starting transfers between devices, other_core(): return lax.ppermute(value, ('c',), [(0, 1), (1, 0)])  2.18 us
  transfers between devices with their start and end apart: 24, of which 11 were waited for; matrix products, arithmetic and copies ran while one was open for 0% of the time, Pallas kernels for 25%

profile of v17, /device:TPU:0, one launch (start us, length us, event | category | flops | bytes accessed | tf_op | source)
XLA Modules:
  0.0 48.1 jit_solution(10353519070437650031)
XLA Ops:
  0.7 1.1 %cut.1 = bf16[24,2048]{1,0:T(8,128)(2,1)S(1)} custom-call(bf16[24,4096]{1,0:T(8,128)(2,1)} %refs_10_.1), custom_call_target="tpu_custom_call" | custom-call | bytes 98304 | tf_op jit(solution)/shard_map/cut/pallas_call | solution.py:366
  1.7 3.0 %collective-permute-start = (bf16[24,2048]{1,0:T(8,128)(2,1)S(1)}, bf16[24,2048]{1,0:T(8,128)(2,1)S(1)}, u32[]{:S(2)}, u32[]{:S(2)}) collective-permute-start(bf16[24,2048]{1,0:T(8,128)(2,1)S(1)} %cut.1), channel_id=1, source_target_pairs={{0,16},{1,17},{16,0},{17,1},{2,18},{3,19},{18,2},{19,3},{4,20},{5,... | collective-permute-start | bytes 294920 | tf_op jit(solution)/shard_map/ppermute | solution.py:391
  4.7 1.1 %gates.1.refs_0_.refs_3_.refs_4_ = bf16[24,2304]{1,0:T(8,128)(2,1)S(1)} custom-call(s32[8,24]{1,0:T(8,128)} %bitcast.35, f32[8,24]{1,0:T(8,128)} %bitcast.36, bf16[24,128]{1,0:T(8,128)(2,1)} %context.1, bf16[24,4096]{1,0:T(8,128)(2,1)} %grads.3, bf16[4096,768]{1,0:T(8,128)(2,1)} %bitcast.17, bf16[4096,768]{1,0:T(8,128)(2,1)} %bitcast.24, ...), custom_call_target="tpu_custom_call" | custom-call | bytes 25165824 | tf_op jit(solution)/shard_map/gates/pallas_call | solution.py:366
  5.9 0.6 %collective-permute-start.2 = (bf16[24,2304]{1,0:T(8,128)(2,1)S(1)}, bf16[24,2304]{1,0:T(8,128)(2,1)S(1)}, u32[]{:S(2)}, u32[]{:S(2)}) collective-permute-start(bf16[24,2304]{1,0:T(8,128)(2,1)S(1)} %gates.1.refs_0_.refs_3_.refs_4_), channel_id=1, source_target_pairs={{0,16},{1,17},{16,0},{17,1},{2,18},{3,19},{18,2},{19,3},{4,20},{5,... | collective-permute-start | bytes 331784 | tf_op jit(solution)/shard_map/ppermute | solution.py:391
  6.4 1.1 %collective-permute-done.refs_0_ = bf16[24,2048]{1,0:T(8,128)(2,1)S(1)} collective-permute-done((bf16[24,2048]{1,0:T(8,128)(2,1)S(1)}, bf16[24,2048]{1,0:T(8,128)(2,1)S(1)}, u32[]{:S(2)}, u32[]{:S(2)}) %collective-permute-start) | collective-permute-done | bytes 98336 | tf_op jit(solution)/shard_map/ppermute | solution.py:391
  7.6 1.2 %hidden_first.1 = (f32[48,768]{1,0:T(8,128)S(1)}, f32[48,768]{1,0:T(8,128)S(1)}, f32[48,128]{1,0:T(8,128)S(1)}) custom-call(bf16[24,4096]{1,0:T(8,128)(2,1)S(1)} %copy-done, bf16[24,2048]{1,0:T(8,128)(2,1)S(1)} %collective-permute-done.refs_0_, f32[1,4096]{1,0:T(1,128)S(1)} %bitcast.31, bf16[4096,768]{1,0:T(8,128)(2,1)S(1)} %bitcast.20, ...), custom_call_target="tpu_custom_call" | custom-call | bytes 6291456 | tf_op jit(solution)/shard_map/hidden_first/pallas_call | solution.py:366
  8.8 0.0 collective-permute-done.1.refs_0_.refs_1_
  8.8 1.2 %hidden_rest.1 = (f32[48,768]{1,0:T(8,128)S(1)}, f32[48,768]{1,0:T(8,128)S(1)}, bf16[48,768]{1,0:T(8,128)(2,1)S(1)}, f32[48,128]{1,0:T(8,128)S(1)}) custom-call(bf16[24,4096]{1,0:T(8,128)(2,1)S(1)} %copy-done, bf16[24,2048]{1,0:T(8,128)(2,1)S(1)} %collective-permute-done.1.refs_0_.refs_1_, f32[1,4096]{1,0:T(1,128)S(1)} %bitcast.32, ...), custom_call_target="tpu_custom_call" | custom-call | bytes 6291456 | tf_op jit(solution)/shard_map/hidden_rest/pallas_call | solution.py:366
  10.1 0.6 %collective-permute-done.2.refs_1_.refs_4_.refs_2_.refs_5_ = bf16[24,2304]{1,0:T(8,128)(2,1)S(1)} collective-permute-done((bf16[24,2304]{1,0:T(8,128)(2,1)S(1)}, bf16[24,2304]{1,0:T(8,128)(2,1)S(1)}, u32[]{:S(2)}, u32[]{:S(2)}) %collective-permute-start.2) | collective-permute-done | bytes 110624 | tf_op jit(solution)/shard_map/ppermute | solution.py:391
  10.7 0.7 %outward_send.1.refs_4_ = bf16[2,2,24,1024]{3,2,1,0:T(8,128)(2,1)S(1)} custom-call(bf16[24,2304]{1,0:T(8,128)(2,1)S(1)} %gates.1.refs_0_.refs_3_.refs_4_, bf16[24,2304]{1,0:T(8,128)(2,1)S(1)} %collective-permute-done.2.refs_1_.refs_4_.refs_2_.refs_5_, bf16[48,768]{1,0:T(8,128)(2,1)S(1)} %get-tuple-element.37.refs_2_, bf16[768,4096]{1,0:T(8,128)(2,1)S(1)} %bitcast.13), custom_call_target="tpu_custom_call" | custom-call | bytes 3145728 | tf_op jit(solution)/shard_map/outward_send/pallas_call | solution.py:366
  11.4 0.5 %collective-permute-start.4 = (bf16[2,2,24,1024]{3,2,1,0:T(8,128)(2,1)S(1)}, bf16[2,2,24,1024]{3,2,1,0:T(8,128)(2,1)S(1)}, u32[]{:S(2)}, u32[]{:S(2)}) collective-permute-start(bf16[2,2,24,1024]{3,2,1,0:T(8,128)(2,1)S(1)} %outward_send.1.refs_4_), channel_id=1, source_target_pairs={{0,1},{1,0},{2,3},{3,2},{4,5},{5,4},{6,7},{7,6},{8,9},{9,8},{10,11... | collective-permute-start | bytes 589832 | tf_op jit(solution)/shard_map/ppermute | solution.py:394
  11.9 0.1 collective-permute-start.3
  12.0 0.7 %outward_keep.1.refs_8_ = bf16[2,2,24,1024]{3,2,1,0:T(8,128)(2,1)S(1)} custom-call(bf16[24,2304]{1,0:T(8,128)(2,1)S(1)} %gates.1.refs_0_.refs_3_.refs_4_, bf16[24,2304]{1,0:T(8,128)(2,1)S(1)} %collective-permute-done.2.refs_1_.refs_4_.refs_2_.refs_5_, bf16[48,768]{1,0:T(8,128)(2,1)S(1)} %get-tuple-element.37.refs_2_, bf16[768,4096]{1,0:T(8,128)(2,1)S(1)} %bitcast.14, ...), custom_call_target="tpu_custom_call" | custom-call | bytes 3145728 | tf_op jit(solution)/shard_map/outward_keep/pallas_call | solution.py:366
  12.7 0.6 %collective-permute-done.3.refs_2_.refs_3_ = bf16[24,2304]{1,0:T(8,128)(2,1)S(1)} collective-permute-done((bf16[24,2304]{1,0:T(8,128)(2,1)S(1)}, bf16[24,2304]{1,0:T(8,128)(2,1)S(1)}, u32[]{:S(2)}, u32[]{:S(2)}) %collective-permute-start.3) | collective-permute-done | bytes 110624 | tf_op jit(solution)/shard_map/ppermute | solution.py:394
  13.3 0.9 %backward_first.1 = (bf16[48,256]{1,0:T(8,128)(2,1)S(1)}, bf16[48,256]{1,0:T(8,128)(2,1)S(1)}, bf16[48,4096]{1,0:T(8,128)(2,1)S(1)}, bf16[2,2,24,1024]{3,2,1,0:T(8,128)(2,1)S(1)}) custom-call(bf16[24,4096]{1,0:T(8,128)(2,1)S(1)} %copy-done.1, bf16[24,2304]{1,0:T(8,128)(2,1)S(1)} %collective-permute-done.2.refs_1_.refs_4_.refs_2_.refs_5_, ...), custom_call_target="tpu_custom_call" | custom-call | bytes 2097152 | tf_op jit(solution)/shard_map/backward_first/pallas_call | solution.py:366
  14.2 0.1 add_convert_fusion
  14.3 2.3 %collective-permute-start.5 = (bf16[2,24,1024]{2,1,0:T(8,128)(2,1)S(1)}, bf16[2,24,1024]{2,1,0:T(8,128)(2,1)S(1)}, u32[]{:S(2)}, u32[]{:S(2)}) collective-permute-start(bf16[2,24,1024]{2,1,0:T(8,128)(2,1)S(1)} %get-tuple-element.60), channel_id=1, source_target_pairs={{0,17},{1,16},{16,1},{17,0},{2,19},{3,18},{18,3},{19,2},{4,21},{5,... | collective-permute-start | bytes 294920 | tf_op jit(solution)/shard_map/ppermute | solution.py:391
  16.6 1.4 %backward_rest.1 = (bf16[48,512]{1,0:T(8,128)(2,1)S(1)}, bf16[48,512]{1,0:T(8,128)(2,1)S(1)}, bf16[2,24,1024]{2,1,0:T(8,128)(2,1)S(1)}) custom-call(bf16[48,4096]{1,0:T(8,128)(2,1)S(1)} %get-tuple-element.40.weighted, f32[48,768]{1,0:T(8,128)S(1)} %get-tuple-element.35.refs_5_.pre_gate, f32[48,768]{1,0:T(8,128)S(1)} %get-tuple-element.36.refs_6_.pre_up, ...), custom_call_target="tpu_custom_call" | custom-call | bytes 4194304 | tf_op jit(solution)/shard_map/backward_rest/pallas_call | solution.py:366
  18.0 2.0 %inward_send.1 = (bf16[2,2,24,1024]{3,2,1,0:T(8,128)(2,1)S(1)}, bf16[2,24,1024]{2,1,0:T(8,128)(2,1)S(1)}) custom-call(bf16[48,256]{1,0:T(8,128)(2,1)S(1)} %get-tuple-element.38.refs_0_, bf16[48,256]{1,0:T(8,128)(2,1)S(1)} %get-tuple-element.39.refs_1_, bf16[48,512]{1,0:T(8,128)(2,1)S(1)} %get-tuple-element.42.refs_2_, ...), custom_call_target="tpu_custom_call" | custom-call | bytes 6291456 | tf_op jit(solution)/shard_map/inward_send/pallas_call | solution.py:366
  20.0 0.3 collective-permute-start.6
  20.3 2.0 %inward_keep.1 = (bf16[2,2,24,1024]{3,2,1,0:T(8,128)(2,1)S(1)}, bf16[2,24,1024]{2,1,0:T(8,128)(2,1)S(1)}) custom-call(bf16[48,256]{1,0:T(8,128)(2,1)S(1)} %get-tuple-element.38.refs_0_, bf16[48,256]{1,0:T(8,128)(2,1)S(1)} %get-tuple-element.39.refs_1_, bf16[48,512]{1,0:T(8,128)(2,1)S(1)} %get-tuple-element.42.refs_2_, ...), custom_call_target="tpu_custom_call" | custom-call | bytes 6291456 | tf_op jit(solution)/shard_map/inward_keep/pallas_call | solution.py:366
  22.3 0.1 join.1
  22.4 1.2 %collective-permute-start.17 = (bf16[2,24,1024]{2,1,0:T(8,128)(2,1)S(1)}, bf16[2,24,1024]{2,1,0:T(8,128)(2,1)S(1)}, u32[]{:S(2)}, u32[]{:S(2)}) collective-permute-start(bf16[2,24,1024]{2,1,0:T(8,128)(2,1)S(1)} %get-tuple-element.53), channel_id=1, source_target_pairs={{0,5},{1,4},{4,1},{5,0},{8,13},{9,12},{12,9},{13,8},{2,7},{3,6},{6... | collective-permute-start | bytes 294920 | tf_op jit(solution)/shard_map/ppermute | solution.py:391
  23.6 2.0 %collective-permute-start.7 = (bf16[24,1024]{1,0:T(8,128)(2,1)S(1)}, bf16[24,1024]{1,0:T(8,128)(2,1)S(1)}, u32[]{:S(2)}, u32[]{:S(2)}) collective-permute-start(bf16[24,1024]{1,0:T(8,128)(2,1)S(1)} %get-tuple-element.50), channel_id=1, source_target_pairs={{0,18},{1,19},{2,16},{3,17},{16,2},{17,3},{18,0},{19,1},{4,22},{5,... | collective-permute-start | bytes 147464 | tf_op jit(solution)/shard_map/ppermute | solution.py:391
  25.6 0.5 %collective-permute-start.8 = (bf16[24,1024]{1,0:T(8,128)(2,1)S(1)}, bf16[24,1024]{1,0:T(8,128)(2,1)S(1)}, u32[]{:S(2)}, u32[]{:S(2)}) collective-permute-start(bf16[24,1024]{1,0:T(8,128)(2,1)S(1)} %get-tuple-element.51), channel_id=1, source_target_pairs={{0,17},{1,16},{2,19},{3,18},{16,1},{17,0},{18,3},{19,2},{4,21},{5,... | collective-permute-start | bytes 147464 | tf_op jit(solution)/shard_map/ppermute | solution.py:391
  26.1 0.7 %collective-permute-start.9 = (bf16[24,1024]{1,0:T(8,128)(2,1)S(1)}, bf16[24,1024]{1,0:T(8,128)(2,1)S(1)}, u32[]{:S(2)}, u32[]{:S(2)}) collective-permute-start(bf16[24,1024]{1,0:T(8,128)(2,1)S(1)} %get-tuple-element.52), channel_id=1, source_target_pairs={{0,3},{1,2},{2,1},{3,0},{16,19},{17,18},{18,17},{19,16},{4,7},{5,6... | collective-permute-start | bytes 147464 | tf_op jit(solution)/shard_map/ppermute | solution.py:391
  26.8 0.4 collective-permute-done.17
  27.2 1.1 %collective-permute-start.18 = (bf16[2,24,1024]{2,1,0:T(8,128)(2,1)S(1)}, bf16[2,24,1024]{2,1,0:T(8,128)(2,1)S(1)}, u32[]{:S(2)}, u32[]{:S(2)}) collective-permute-start(bf16[2,24,1024]{2,1,0:T(8,128)(2,1)S(1)} %add_convert_fusion.3), channel_id=1, source_target_pairs={{0,3},{1,2},{2,1},{3,0},{4,7},{5,6},{6,5},{7,4},{8,11},{9,10},{10,... | collective-permute-start | bytes 294920 | tf_op jit(solution)/shard_map/ppermute | solution.py:391
  28.2 0.4 collective-permute-done.7
  28.7 0.8 %collective-permute-done.8 = bf16[24,1024]{1,0:T(8,128)(2,1)S(1)} collective-permute-done((bf16[24,1024]{1,0:T(8,128)(2,1)S(1)}, bf16[24,1024]{1,0:T(8,128)(2,1)S(1)}, u32[]{:S(2)}, u32[]{:S(2)}) %collective-permute-start.8) | collective-permute-done | bytes 49184 | tf_op jit(solution)/shard_map/ppermute | solution.py:391
  29.5 0.1 collective-permute-done.9
  29.7 2.6 %collective-permute-start.12 = (bf16[24,1024]{1,0:T(8,128)(2,1)S(1)}, bf16[24,1024]{1,0:T(8,128)(2,1)S(1)}, u32[]{:S(2)}, u32[]{:S(2)}) collective-permute-start(bf16[24,1024]{1,0:T(8,128)(2,1)S(1)} %add_convert_fusion.6), channel_id=1, source_target_pairs={{0,12},{1,13},{4,8},{5,9},{8,4},{9,5},{12,0},{13,1},{2,14},{3,15},... | collective-permute-start | bytes 147464 | tf_op jit(solution)/shard_map/ppermute | solution.py:391
  32.3 1.0 %collective-permute-start.11 = (bf16[24,1024]{1,0:T(8,128)(2,1)S(1)}, bf16[24,1024]{1,0:T(8,128)(2,1)S(1)}, u32[]{:S(2)}, u32[]{:S(2)}) collective-permute-start(bf16[24,1024]{1,0:T(8,128)(2,1)S(1)} %add_convert_fusion.6), channel_id=1, source_target_pairs={{0,9},{1,8},{4,13},{5,12},{8,1},{9,0},{12,5},{13,4},{2,11},{3,10},... | collective-permute-start | bytes 147464 | tf_op jit(solution)/shard_map/ppermute | solution.py:391
  33.3 0.5 %collective-permute-start.10 = (bf16[24,1024]{1,0:T(8,128)(2,1)S(1)}, bf16[24,1024]{1,0:T(8,128)(2,1)S(1)}, u32[]{:S(2)}, u32[]{:S(2)}) collective-permute-start(bf16[24,1024]{1,0:T(8,128)(2,1)S(1)} %add_convert_fusion.6), channel_id=1, source_target_pairs={{0,5},{1,4},{4,1},{5,0},{8,13},{9,12},{12,9},{13,8},{2,7},{3,6},{6... | collective-permute-start | bytes 147464 | tf_op jit(solution)/shard_map/ppermute | solution.py:391
  33.9 2.4 %collective-permute-start.19 = (bf16[2,24,1024]{2,1,0:T(8,128)(2,1)S(1)}, bf16[2,24,1024]{2,1,0:T(8,128)(2,1)S(1)}, u32[]{:S(2)}, u32[]{:S(2)}) collective-permute-start(bf16[2,24,1024]{2,1,0:T(8,128)(2,1)S(1)} %add_convert_fusion.2), channel_id=1, source_target_pairs={{0,9},{1,8},{4,13},{5,12},{8,1},{9,0},{12,5},{13,4},{2,11},{3,10},... | collective-permute-start | bytes 294920 | tf_op jit(solution)/shard_map/ppermute | solution.py:391
  36.3 1.5 %collective-permute-done.11 = bf16[24,1024]{1,0:T(8,128)(2,1)S(1)} collective-permute-done((bf16[24,1024]{1,0:T(8,128)(2,1)S(1)}, bf16[24,1024]{1,0:T(8,128)(2,1)S(1)}, u32[]{:S(2)}, u32[]{:S(2)}) %collective-permute-start.11) | collective-permute-done | bytes 49184 | tf_op jit(solution)/shard_map/ppermute | solution.py:391
  37.7 0.7 %collective-permute-done.10 = bf16[24,1024]{1,0:T(8,128)(2,1)S(1)} collective-permute-done((bf16[24,1024]{1,0:T(8,128)(2,1)S(1)}, bf16[24,1024]{1,0:T(8,128)(2,1)S(1)}, u32[]{:S(2)}, u32[]{:S(2)}) %collective-permute-start.10) | collective-permute-done | bytes 49184 | tf_op jit(solution)/shard_map/ppermute | solution.py:391
  38.4 1.3 %collective-permute-start.21 = (bf16[24,1024]{1,0:T(8,128)(2,1)S(1)}, bf16[24,1024]{1,0:T(8,128)(2,1)S(1)}, u32[]{:S(2)}, u32[]{:S(2)}) collective-permute-start(bf16[24,1024]{1,0:T(8,128)(2,1)S(1)} %add_convert_fusion.5.refs_0_), channel_id=1, source_target_pairs={{0,3},{1,2},{2,1},{3,0},{16,19},{17,18},{18,17},{19,16},{4,7},{5,6... | collective-permute-start | bytes 147464 | tf_op jit(solution)/shard_map/ppermute | solution.py:391
  39.7 1.0 %collective-permute-start.14 = (bf16[24,1024]{1,0:T(8,128)(2,1)S(1)}, bf16[24,1024]{1,0:T(8,128)(2,1)S(1)}, u32[]{:S(2)}, u32[]{:S(2)}) collective-permute-start(bf16[24,1024]{1,0:T(8,128)(2,1)S(1)} %add_convert_fusion.5.refs_0_), channel_id=1, source_target_pairs={{0,18},{1,19},{2,16},{3,17},{16,2},{17,3},{18,0},{19,1},{4,22},{5,... | collective-permute-start | bytes 147464 | tf_op jit(solution)/shard_map/ppermute | solution.py:391
  40.7 0.7 %collective-permute-start.13 = (bf16[24,1024]{1,0:T(8,128)(2,1)S(1)}, bf16[24,1024]{1,0:T(8,128)(2,1)S(1)}, u32[]{:S(2)}, u32[]{:S(2)}) collective-permute-start(bf16[24,1024]{1,0:T(8,128)(2,1)S(1)} %add_convert_fusion.5.refs_0_), channel_id=1, source_target_pairs={{0,17},{1,16},{2,19},{3,18},{16,1},{17,0},{18,3},{19,2},{4,21},{5,... | collective-permute-start | bytes 147464 | tf_op jit(solution)/shard_map/ppermute | solution.py:391
  41.4 0.6 %collective-permute-done.19 = bf16[2,24,1024]{2,1,0:T(8,128)(2,1)S(1)} collective-permute-done((bf16[2,24,1024]{2,1,0:T(8,128)(2,1)S(1)}, bf16[2,24,1024]{2,1,0:T(8,128)(2,1)S(1)}, u32[]{:S(2)}, u32[]{:S(2)}) %collective-permute-start.19) | collective-permute-done | bytes 98336 | tf_op jit(solution)/shard_map/ppermute | solution.py:391
  42.1 0.3 collective-permute-start.20
  42.4 0.3 collective-permute-start.22
  42.7 0.2 collective-permute-start.23
  42.9 1.9 %collective-permute-done.14.refs_7_ = bf16[24,1024]{1,0:T(8,128)(2,1)S(1)} collective-permute-done((bf16[24,1024]{1,0:T(8,128)(2,1)S(1)}, bf16[24,1024]{1,0:T(8,128)(2,1)S(1)}, u32[]{:S(2)}, u32[]{:S(2)}) %collective-permute-start.14) | collective-permute-done | bytes 49184 | tf_op jit(solution)/shard_map/ppermute | solution.py:391
  44.8 0.5 %collective-permute-start.15 = (bf16[24,1024]{1,0:T(8,128)(2,1)S(1)}, bf16[24,1024]{1,0:T(8,128)(2,1)S(1)}, u32[]{:S(2)}, u32[]{:S(2)}) collective-permute-start(bf16[24,1024]{1,0:T(8,128)(2,1)S(1)} %collective-permute-done.13.refs_6_), channel_id=1, source_target_pairs={{0,1},{1,0},{2,3},{3,2},{4,5},{5,4},{6,7},{7,6},{8,9},{9,8},{10,11... | collective-permute-start | bytes 147464 | tf_op jit(solution)/shard_map/ppermute | solution.py:394
  45.3 1.3 %own_rows.1 = (bf16[24,4096]{1,0:T(8,128)(2,1)}, bf16[24,128]{1,0:T(8,128)(2,1)}, bf16[24,2048]{1,0:T(8,128)(2,1)S(1)}) custom-call(bf16[24,4096]{1,0:T(8,128)(2,1)S(1)} %copy-done, bf16[24,4096]{1,0:T(8,128)(2,1)S(1)} %copy-done.1, bf16[24,1024]{1,0:T(8,128)(2,1)S(1)} %add_convert_fusion.5.refs_0_, bf16[24,1024]{1,0:T(8,128)(2,1)S(1)} %collective-permute-done.21.refs_1_, ...), custom_call_target="tpu_custom_call" | custom-call | bytes 3145728 | tf_op jit(solution)/shard_map/own_rows/pallas_call | solution.py:366
  46.7 1.4 %far_rows.1 = (bf16[24,4096]{1,0:T(8,128)(2,1)}, bf16[128,2048]{1,0:T(8,128)(2,1)}) custom-call(bf16[24,2048]{1,0:T(8,128)(2,1)S(1)} %collective-permute-done.refs_0_, bf16[24,2048]{1,0:T(8,128)(2,1)S(1)} %collective-permute-done.1.refs_0_.refs_1_, bf16[24,2304]{1,0:T(8,128)(2,1)S(1)} %collective-permute-done.2.refs_1_.refs_4_.refs_2_.refs_5_, ...), custom_call_target="tpu_custom_call" | custom-call | bytes 3145728 | tf_op jit(solution)/shard_map/far_rows/pallas_call | solution.py:366
  (44 shorter events, 0.3 us)
Async XLA Ops:
  0.6 6.9 %slice-start.2 = ((s8[6291456]{0:T(1024)(128)(4,1)}), s8[4194304]{0:T(1024)(128)(4,1)S(1)}, s32[]{:S(2)}) async-start(s8[6291456]{0:T(1024)(128)(4,1)} %bitcast.18), calls=%async_computation.2 | async-start | bytes 8388608
  0.6 6.9 %slice-start.4 = ((s8[6291456]{0:T(1024)(128)(4,1)}), s8[4194304]{0:T(1024)(128)(4,1)S(1)}, s32[]{:S(2)}) async-start(s8[6291456]{0:T(1024)(128)(4,1)} %bitcast.25), calls=%async_computation.4 | async-start | bytes 8388608
  1.7 5.8 %collective-permute-start = (bf16[24,2048]{1,0:T(8,128)(2,1)S(1)}, bf16[24,2048]{1,0:T(8,128)(2,1)S(1)}, u32[]{:S(2)}, u32[]{:S(2)}) collective-permute-start(bf16[24,2048]{1,0:T(8,128)(2,1)S(1)} %cut.1), channel_id=1, source_target_pairs={{0,16},{1,17},{16,0},{17,1},{2,18},{3,19},{18,2},{19,3},{4,20},{5,... | collective-permute-start | bytes 294920 | tf_op jit(solution)/shard_map/ppermute | solution.py:391
  4.7 2.8 %slice-start.3 = ((s8[6291456]{0:T(1024)(128)(4,1)}), s8[2097152]{0:T(1024)(128)(4,1)S(1)}, s32[]{:S(2)}) async-start(s8[6291456]{0:T(1024)(128)(4,1)} %bitcast.18), calls=%async_computation.3 | async-start | bytes 4194304
  4.7 2.8 %slice-start.5 = ((s8[6291456]{0:T(1024)(128)(4,1)}), s8[2097152]{0:T(1024)(128)(4,1)S(1)}, s32[]{:S(2)}) async-start(s8[6291456]{0:T(1024)(128)(4,1)} %bitcast.25), calls=%async_computation.5 | async-start | bytes 4194304
  4.7 2.8 %copy-start = (bf16[24,4096]{1,0:T(8,128)(2,1)S(1)}, bf16[24,4096]{1,0:T(8,128)(2,1)}, u32[]{:S(2)}) copy-start(bf16[24,4096]{1,0:T(8,128)(2,1)} %refs_10_.1) | copy-start | bytes 589828
  4.7 2.8 %copy-start.3 = (f32[4096]{0:T(1024)S(1)}, f32[4096]{0:T(1024)}, u32[]{:S(2)}) copy-start(f32[4096]{0:T(1024)} %param.11) | copy-start | bytes 49156
  5.9 4.8 %collective-permute-start.2 = (bf16[24,2304]{1,0:T(8,128)(2,1)S(1)}, bf16[24,2304]{1,0:T(8,128)(2,1)S(1)}, u32[]{:S(2)}, u32[]{:S(2)}) collective-permute-start(bf16[24,2304]{1,0:T(8,128)(2,1)S(1)} %gates.1.refs_0_.refs_3_.refs_4_), channel_id=1, source_target_pairs={{0,16},{1,17},{16,0},{17,1},{2,18},{3,19},{18,2},{19,3},{4,20},{5,... | collective-permute-start | bytes 331784 | tf_op jit(solution)/shard_map/ppermute | solution.py:391
  7.5 1.3 %collective-permute-start.1 = (bf16[24,2048]{1,0:T(8,128)(2,1)S(1)}, bf16[24,2048]{1,0:T(8,128)(2,1)S(1)}, u32[]{:S(2)}, u32[]{:S(2)}) collective-permute-start(bf16[24,2048]{1,0:T(8,128)(2,1)S(1)} %collective-permute-done.refs_0_), channel_id=1, source_target_pairs={{0,1},{1,0},{2,3},{3,2},{4,5},{5,4},{6,7},{7,6},{8,9},{9,8},{10,11... | collective-permute-start | bytes 294920 | tf_op jit(solution)/shard_map/ppermute | solution.py:394
  7.6 3.1 %slice-start = ((s8[6291456]{0:T(1024)(128)(4,1)}), s8[4194304]{0:T(1024)(128)(4,1)S(1)}, s32[]{:S(2)}) async-start(s8[6291456]{0:T(1024)(128)(4,1)} %bitcast.11), calls=%async_computation | async-start | bytes 8388608
  8.8 1.9 %slice-start.1 = ((s8[6291456]{0:T(1024)(128)(4,1)}), s8[2097152]{0:T(1024)(128)(4,1)S(1)}, s32[]{:S(2)}) async-start(s8[6291456]{0:T(1024)(128)(4,1)} %bitcast.11), calls=%async_computation.1 | async-start | bytes 4194304
  10.7 2.6 %copy-start.1 = (bf16[24,4096]{1,0:T(8,128)(2,1)S(1)}, bf16[24,4096]{1,0:T(8,128)(2,1)}, u32[]{:S(2)}) copy-start(bf16[24,4096]{1,0:T(8,128)(2,1)} %grads.3) | copy-start | bytes 589828
  11.4 2.7 %collective-permute-start.4 = (bf16[2,2,24,1024]{3,2,1,0:T(8,128)(2,1)S(1)}, bf16[2,2,24,1024]{3,2,1,0:T(8,128)(2,1)S(1)}, u32[]{:S(2)}, u32[]{:S(2)}) collective-permute-start(bf16[2,2,24,1024]{3,2,1,0:T(8,128)(2,1)S(1)} %outward_send.1.refs_4_), channel_id=1, source_target_pairs={{0,1},{1,0},{2,3},{3,2},{4,5},{5,4},{6,7},{7,6},{8,9},{9,8},{10,11... | collective-permute-start | bytes 589832 | tf_op jit(solution)/shard_map/ppermute | solution.py:394
  11.9 1.3 %collective-permute-start.3 = (bf16[24,2304]{1,0:T(8,128)(2,1)S(1)}, bf16[24,2304]{1,0:T(8,128)(2,1)S(1)}, u32[]{:S(2)}, u32[]{:S(2)}) collective-permute-start(bf16[24,2304]{1,0:T(8,128)(2,1)S(1)} %collective-permute-done.2.refs_1_.refs_4_.refs_2_.refs_5_), channel_id=1, source_target_pairs={{0,1},{1,0},{2,3},{3,2},{4,5},{5,4},{6,7},{7,6},{8,9},{9,8},{10,11... | collective-permute-start | bytes 331784 | tf_op jit(solution)/shard_map/ppermute | solution.py:394
  14.3 6.0 %collective-permute-start.5 = (bf16[2,24,1024]{2,1,0:T(8,128)(2,1)S(1)}, bf16[2,24,1024]{2,1,0:T(8,128)(2,1)S(1)}, u32[]{:S(2)}, u32[]{:S(2)}) collective-permute-start(bf16[2,24,1024]{2,1,0:T(8,128)(2,1)S(1)} %get-tuple-element.60), channel_id=1, source_target_pairs={{0,17},{1,16},{16,1},{17,0},{2,19},{3,18},{18,3},{19,2},{4,21},{5,... | collective-permute-start | bytes 294920 | tf_op jit(solution)/shard_map/ppermute | solution.py:391
  20.0 2.3 %collective-permute-start.6 = (bf16[2,2,24,1024]{3,2,1,0:T(8,128)(2,1)S(1)}, bf16[2,2,24,1024]{3,2,1,0:T(8,128)(2,1)S(1)}, u32[]{:S(2)}, u32[]{:S(2)}) collective-permute-start(bf16[2,2,24,1024]{3,2,1,0:T(8,128)(2,1)S(1)} %get-tuple-element.47), channel_id=1, source_target_pairs={{0,1},{1,0},{2,3},{3,2},{4,5},{5,4},{6,7},{7,6},{8,9},{9,8},{10,11... | collective-permute-start | bytes 589832 | tf_op jit(solution)/shard_map/ppermute | solution.py:394
  20.3 25.0 %copy-start.2 = (bf16[128,4096]{1,0:T(8,128)(2,1)S(1)}, bf16[128,4096]{1,0:T(8,128)(2,1)}, u32[]{:S(2)}) copy-start(bf16[128,4096]{1,0:T(8,128)(2,1)} %refs_6_.1) | copy-start | bytes 3145732
  22.4 4.8 %collective-permute-start.17 = (bf16[2,24,1024]{2,1,0:T(8,128)(2,1)S(1)}, bf16[2,24,1024]{2,1,0:T(8,128)(2,1)S(1)}, u32[]{:S(2)}, u32[]{:S(2)}) collective-permute-start(bf16[2,24,1024]{2,1,0:T(8,128)(2,1)S(1)} %get-tuple-element.53), channel_id=1, source_target_pairs={{0,5},{1,4},{4,1},{5,0},{8,13},{9,12},{12,9},{13,8},{2,7},{3,6},{6... | collective-permute-start | bytes 294920 | tf_op jit(solution)/shard_map/ppermute | solution.py:391
  23.6 5.1 %collective-permute-start.7 = (bf16[24,1024]{1,0:T(8,128)(2,1)S(1)}, bf16[24,1024]{1,0:T(8,128)(2,1)S(1)}, u32[]{:S(2)}, u32[]{:S(2)}) collective-permute-start(bf16[24,1024]{1,0:T(8,128)(2,1)S(1)} %get-tuple-element.50), channel_id=1, source_target_pairs={{0,18},{1,19},{2,16},{3,17},{16,2},{17,3},{18,0},{19,1},{4,22},{5,... | collective-permute-start | bytes 147464 | tf_op jit(solution)/shard_map/ppermute | solution.py:391
  25.6 3.9 %collective-permute-start.8 = (bf16[24,1024]{1,0:T(8,128)(2,1)S(1)}, bf16[24,1024]{1,0:T(8,128)(2,1)S(1)}, u32[]{:S(2)}, u32[]{:S(2)}) collective-permute-start(bf16[24,1024]{1,0:T(8,128)(2,1)S(1)} %get-tuple-element.51), channel_id=1, source_target_pairs={{0,17},{1,16},{2,19},{3,18},{16,1},{17,0},{18,3},{19,2},{4,21},{5,... | collective-permute-start | bytes 147464 | tf_op jit(solution)/shard_map/ppermute | solution.py:391
  26.1 3.5 %collective-permute-start.9 = (bf16[24,1024]{1,0:T(8,128)(2,1)S(1)}, bf16[24,1024]{1,0:T(8,128)(2,1)S(1)}, u32[]{:S(2)}, u32[]{:S(2)}) collective-permute-start(bf16[24,1024]{1,0:T(8,128)(2,1)S(1)} %get-tuple-element.52), channel_id=1, source_target_pairs={{0,3},{1,2},{2,1},{3,0},{16,19},{17,18},{18,17},{19,16},{4,7},{5,6... | collective-permute-start | bytes 147464 | tf_op jit(solution)/shard_map/ppermute | solution.py:391
  27.2 6.6 %collective-permute-start.18 = (bf16[2,24,1024]{2,1,0:T(8,128)(2,1)S(1)}, bf16[2,24,1024]{2,1,0:T(8,128)(2,1)S(1)}, u32[]{:S(2)}, u32[]{:S(2)}) collective-permute-start(bf16[2,24,1024]{2,1,0:T(8,128)(2,1)S(1)} %add_convert_fusion.3), channel_id=1, source_target_pairs={{0,3},{1,2},{2,1},{3,0},{4,7},{5,6},{6,5},{7,4},{8,11},{9,10},{10,... | collective-permute-start | bytes 294920 | tf_op jit(solution)/shard_map/ppermute | solution.py:391
  29.7 6.6 %collective-permute-start.12 = (bf16[24,1024]{1,0:T(8,128)(2,1)S(1)}, bf16[24,1024]{1,0:T(8,128)(2,1)S(1)}, u32[]{:S(2)}, u32[]{:S(2)}) collective-permute-start(bf16[24,1024]{1,0:T(8,128)(2,1)S(1)} %add_convert_fusion.6), channel_id=1, source_target_pairs={{0,12},{1,13},{4,8},{5,9},{8,4},{9,5},{12,0},{13,1},{2,14},{3,15},... | collective-permute-start | bytes 147464 | tf_op jit(solution)/shard_map/ppermute | solution.py:391
  32.3 5.5 %collective-permute-start.11 = (bf16[24,1024]{1,0:T(8,128)(2,1)S(1)}, bf16[24,1024]{1,0:T(8,128)(2,1)S(1)}, u32[]{:S(2)}, u32[]{:S(2)}) collective-permute-start(bf16[24,1024]{1,0:T(8,128)(2,1)S(1)} %add_convert_fusion.6), channel_id=1, source_target_pairs={{0,9},{1,8},{4,13},{5,12},{8,1},{9,0},{12,5},{13,4},{2,11},{3,10},... | collective-permute-start | bytes 147464 | tf_op jit(solution)/shard_map/ppermute | solution.py:391
  33.3 5.1 %collective-permute-start.10 = (bf16[24,1024]{1,0:T(8,128)(2,1)S(1)}, bf16[24,1024]{1,0:T(8,128)(2,1)S(1)}, u32[]{:S(2)}, u32[]{:S(2)}) collective-permute-start(bf16[24,1024]{1,0:T(8,128)(2,1)S(1)} %add_convert_fusion.6), channel_id=1, source_target_pairs={{0,5},{1,4},{4,1},{5,0},{8,13},{9,12},{12,9},{13,8},{2,7},{3,6},{6... | collective-permute-start | bytes 147464 | tf_op jit(solution)/shard_map/ppermute | solution.py:391
  33.9 8.2 %collective-permute-start.19 = (bf16[2,24,1024]{2,1,0:T(8,128)(2,1)S(1)}, bf16[2,24,1024]{2,1,0:T(8,128)(2,1)S(1)}, u32[]{:S(2)}, u32[]{:S(2)}) collective-permute-start(bf16[2,24,1024]{2,1,0:T(8,128)(2,1)S(1)} %add_convert_fusion.2), channel_id=1, source_target_pairs={{0,9},{1,8},{4,13},{5,12},{8,1},{9,0},{12,5},{13,4},{2,11},{3,10},... | collective-permute-start | bytes 294920 | tf_op jit(solution)/shard_map/ppermute | solution.py:391
  38.4 4.2 %collective-permute-start.21 = (bf16[24,1024]{1,0:T(8,128)(2,1)S(1)}, bf16[24,1024]{1,0:T(8,128)(2,1)S(1)}, u32[]{:S(2)}, u32[]{:S(2)}) collective-permute-start(bf16[24,1024]{1,0:T(8,128)(2,1)S(1)} %add_convert_fusion.5.refs_0_), channel_id=1, source_target_pairs={{0,3},{1,2},{2,1},{3,0},{16,19},{17,18},{18,17},{19,16},{4,7},{5,6... | collective-permute-start | bytes 147464 | tf_op jit(solution)/shard_map/ppermute | solution.py:391
  39.7 5.1 %collective-permute-start.14 = (bf16[24,1024]{1,0:T(8,128)(2,1)S(1)}, bf16[24,1024]{1,0:T(8,128)(2,1)S(1)}, u32[]{:S(2)}, u32[]{:S(2)}) collective-permute-start(bf16[24,1024]{1,0:T(8,128)(2,1)S(1)} %add_convert_fusion.5.refs_0_), channel_id=1, source_target_pairs={{0,18},{1,19},{2,16},{3,17},{16,2},{17,3},{18,0},{19,1},{4,22},{5,... | collective-permute-start | bytes 147464 | tf_op jit(solution)/shard_map/ppermute | solution.py:391
  40.7 4.1 %collective-permute-start.13 = (bf16[24,1024]{1,0:T(8,128)(2,1)S(1)}, bf16[24,1024]{1,0:T(8,128)(2,1)S(1)}, u32[]{:S(2)}, u32[]{:S(2)}) collective-permute-start(bf16[24,1024]{1,0:T(8,128)(2,1)S(1)} %add_convert_fusion.5.refs_0_), channel_id=1, source_target_pairs={{0,17},{1,16},{2,19},{3,18},{16,1},{17,0},{18,3},{19,2},{4,21},{5,... | collective-permute-start | bytes 147464 | tf_op jit(solution)/shard_map/ppermute | solution.py:391
  42.1 4.5 %collective-permute-start.20 = (bf16[2,24,1024]{2,1,0:T(8,128)(2,1)S(1)}, bf16[2,24,1024]{2,1,0:T(8,128)(2,1)S(1)}, u32[]{:S(2)}, u32[]{:S(2)}) collective-permute-start(bf16[2,24,1024]{2,1,0:T(8,128)(2,1)S(1)} %add_convert_fusion.1.refs_11_), channel_id=1, source_target_pairs={{0,1},{1,0},{2,3},{3,2},{4,5},{5,4},{6,7},{7,6},{8,9},{9,8},{10,11... | collective-permute-start | bytes 294920 | tf_op jit(solution)/shard_map/ppermute | solution.py:394
  42.4 3.0 %collective-permute-start.22 = (bf16[24,1024]{1,0:T(8,128)(2,1)S(1)}, bf16[24,1024]{1,0:T(8,128)(2,1)S(1)}, u32[]{:S(2)}, u32[]{:S(2)}) collective-permute-start(bf16[24,1024]{1,0:T(8,128)(2,1)S(1)} %add_convert_fusion.5.refs_0_), channel_id=1, source_target_pairs={{0,1},{1,0},{2,3},{3,2},{4,5},{5,4},{6,7},{7,6},{8,9},{9,8},{10,11... | collective-permute-start | bytes 147464 | tf_op jit(solution)/shard_map/ppermute | solution.py:394
  42.7 2.6 %collective-permute-start.23 = (bf16[24,1024]{1,0:T(8,128)(2,1)S(1)}, bf16[24,1024]{1,0:T(8,128)(2,1)S(1)}, u32[]{:S(2)}, u32[]{:S(2)}) collective-permute-start(bf16[24,1024]{1,0:T(8,128)(2,1)S(1)} %collective-permute-done.21.refs_1_), channel_id=1, source_target_pairs={{0,1},{1,0},{2,3},{3,2},{4,5},{5,4},{6,7},{7,6},{8,9},{9,8},{10,11... | collective-permute-start | bytes 147464 | tf_op jit(solution)/shard_map/ppermute | solution.py:394
  44.8 1.8 %collective-permute-start.16 = (bf16[24,1024]{1,0:T(8,128)(2,1)S(1)}, bf16[24,1024]{1,0:T(8,128)(2,1)S(1)}, u32[]{:S(2)}, u32[]{:S(2)}) collective-permute-start(bf16[24,1024]{1,0:T(8,128)(2,1)S(1)} %collective-permute-done.14.refs_7_), channel_id=1, source_target_pairs={{0,1},{1,0},{2,3},{3,2},{4,5},{5,4},{6,7},{7,6},{8,9},{9,8},{10,11... | collective-permute-start | bytes 147464 | tf_op jit(solution)/shard_map/ppermute | solution.py:394
  44.8 1.8 %collective-permute-start.15 = (bf16[24,1024]{1,0:T(8,128)(2,1)S(1)}, bf16[24,1024]{1,0:T(8,128)(2,1)S(1)}, u32[]{:S(2)}, u32[]{:S(2)}) collective-permute-start(bf16[24,1024]{1,0:T(8,128)(2,1)S(1)} %collective-permute-done.13.refs_6_), channel_id=1, source_target_pairs={{0,1},{1,0},{2,3},{3,2},{4,5},{5,4},{6,7},{7,6},{8,9},{9,8},{10,11... | collective-permute-start | bytes 147464 | tf_op jit(solution)/shard_map/ppermute | solution.py:394

commit v18 on v13

--- a/solution.py
+++ b/solution.py
@@ -440,11 +440,13 @@
     )
     turns = [t for t in range(2 * n_dp - 1, 0, -1)]
     in_share = total_of([in_pieces[0]] + [swap(in_pieces[t], ("dp", "y"), t) for t in turns])
-    out_total = add(out_block, swap(out_block, ("y",), 1)[::-1])
+    out_total = out_block
     in_total = total_of([in_share] + [swap(in_share, ("hi",), t) for t in range(1, n_hi)])
     turn = 1
     while turn < n_hi:
         out_total = add(out_total, swap(out_total, ("hi",), turn))
+        if turn == 1:
+            out_total = add(out_total, swap(out_total, ("y",), 1)[::-1])
         turn = 2 * turn
     order = [t for t in turns if t < 2] + [t for t in turns if t >= 2]
     spread = {t: swap(in_total, ("dp", "y"), t) for t in order}

time: 48.4 us -> 47.8 us (0.988)
  waiting for transfers between devices: 9.99 us -> 9.15 us
    ppermute x15, waiting for transfers between devices: 8.55 us -> 7.71 us  [swap(): lax.ppermute(value, axes + ('c',), [(i, i ^ turn) for i in range(count)])]
  transfers between devices with their start and end apart: 24 -> 24, of which waited for: 13 -> 14; matrix products, arithmetic and copies ran while one was open for 0% -> 0% of each run, Pallas kernels for 22% -> 22%
where the time goes in v18:
time: 47.8 us; the launch traced here: 47.7 us
  starting transfers between devices  23.3 us (49%)
  Pallas kernels  14.1 us (29%)
  waiting for transfers between devices  9.15 us (19%)
  between operations  0.9 us (2%)
    ppermute x15, starting transfers between devices, swap(): lax.ppermute(value, axes + ('c',), [(i, i ^ turn) for i in range(count)])  21.2 us
    pallas_call x12, Pallas kernels, run(): pl.pallas_call(functools.partial(kernel, n_dp), out_shape=kinds, in_specs...  14.1 us
    ppermute x15, waiting for transfers between devices, swap(): lax.ppermute(value, axes + ('c',), [(i, i ^ turn) for i in range(count)])  7.71 us
    ppermute x9, starting transfers between devices, other_core(): return lax.ppermute(value, ('c',), [(0, 1), (1, 0)])  2.11 us
    ppermute x9, waiting for transfers between devices, other_core(): return lax.ppermute(value, ('c',), [(0, 1), (1, 0)])  1.44 us
  transfers between devices with their start and end apart: 24, of which 14 were waited for; matrix products, arithmetic and copies ran while one was open for 0% of the time, Pallas kernels for 22%

profile of v18, /device:TPU:0, one launch (start us, length us, event | category | flops | bytes accessed | tf_op | source)
XLA Modules:
  0.0 47.7 jit_solution(9593397063497202086)
XLA Ops:
  0.7 1.1 %cut.1 = bf16[24,2048]{1,0:T(8,128)(2,1)S(1)} custom-call(bf16[24,4096]{1,0:T(8,128)(2,1)} %refs_0_.3), custom_call_target="tpu_custom_call" | custom-call | bytes 98304 | tf_op jit(solution)/shard_map/cut/pallas_call | solution.py:331
  1.7 3.0 %collective-permute-start = (bf16[24,2048]{1,0:T(8,128)(2,1)S(1)}, bf16[24,2048]{1,0:T(8,128)(2,1)S(1)}, u32[]{:S(2)}, u32[]{:S(2)}) collective-permute-start(bf16[24,2048]{1,0:T(8,128)(2,1)S(1)} %cut.1), channel_id=1, source_target_pairs={{0,16},{1,17},{16,0},{17,1},{2,18},{3,19},{18,2},{19,3},{4,20},{5,... | collective-permute-start | bytes 294920 | tf_op jit(solution)/shard_map/ppermute | solution.py:356
  4.7 1.1 %gates.1.refs_0_.refs_3_.refs_6_ = bf16[24,2304]{1,0:T(8,128)(2,1)S(1)} custom-call(s32[8,24]{1,0:T(8,128)} %bitcast.34, f32[8,24]{1,0:T(8,128)} %bitcast.35, bf16[24,128]{1,0:T(8,128)(2,1)} %context.1, bf16[24,4096]{1,0:T(8,128)(2,1)} %refs_3_.1, bf16[4096,768]{1,0:T(8,128)(2,1)} %bitcast.17, bf16[4096,768]{1,0:T(8,128)(2,1)} %bitcast.24, ...), custom_call_target="tpu_custom_call" | custom-call | bytes 25165824 | tf_op jit(solution)/shard_map/gates/pallas_call | solution.py:331
  5.9 0.6 %collective-permute-start.2 = (bf16[24,2304]{1,0:T(8,128)(2,1)S(1)}, bf16[24,2304]{1,0:T(8,128)(2,1)S(1)}, u32[]{:S(2)}, u32[]{:S(2)}) collective-permute-start(bf16[24,2304]{1,0:T(8,128)(2,1)S(1)} %gates.1.refs_0_.refs_3_.refs_6_), channel_id=1, source_target_pairs={{0,16},{1,17},{16,0},{17,1},{2,18},{3,19},{18,2},{19,3},{4,20},{5,... | collective-permute-start | bytes 331784 | tf_op jit(solution)/shard_map/ppermute | solution.py:356
  6.4 1.1 %collective-permute-done.refs_0_.refs_1_ = bf16[24,2048]{1,0:T(8,128)(2,1)S(1)} collective-permute-done((bf16[24,2048]{1,0:T(8,128)(2,1)S(1)}, bf16[24,2048]{1,0:T(8,128)(2,1)S(1)}, u32[]{:S(2)}, u32[]{:S(2)}) %collective-permute-start) | collective-permute-done | bytes 98336 | tf_op jit(solution)/shard_map/ppermute | solution.py:356
  7.6 1.2 %hidden_first.1 = (f32[48,768]{1,0:T(8,128)S(1)}, f32[48,768]{1,0:T(8,128)S(1)}, f32[48,128]{1,0:T(8,128)S(1)}) custom-call(bf16[24,4096]{1,0:T(8,128)(2,1)S(1)} %copy-done, bf16[24,2048]{1,0:T(8,128)(2,1)S(1)} %collective-permute-done.refs_0_.refs_1_, f32[1,4096]{1,0:T(1,128)S(1)} %bitcast.31, bf16[4096,768]{1,0:T(8,128)(2,1)S(1)} %bitcast.20, ...), custom_call_target="tpu_custom_call" | custom-call | bytes 6291456 | tf_op jit(solution)/shard_map/hidden_first/pallas_call | solution.py:331
  8.8 1.2 %hidden_rest.1 = (f32[48,768]{1,0:T(8,128)S(1)}, f32[48,768]{1,0:T(8,128)S(1)}, bf16[48,768]{1,0:T(8,128)(2,1)S(1)}, f32[48,128]{1,0:T(8,128)S(1)}) custom-call(bf16[24,4096]{1,0:T(8,128)(2,1)S(1)} %copy-done, bf16[24,2048]{1,0:T(8,128)(2,1)S(1)} %collective-permute-done.1.refs_0_.refs_2_, f32[1,4096]{1,0:T(1,128)S(1)} %bitcast.32, ...), custom_call_target="tpu_custom_call" | custom-call | bytes 6291456 | tf_op jit(solution)/shard_map/hidden_rest/pallas_call | solution.py:331
  10.1 0.6 %collective-permute-done.2.refs_1_.refs_4_.refs_7_ = bf16[24,2304]{1,0:T(8,128)(2,1)S(1)} collective-permute-done((bf16[24,2304]{1,0:T(8,128)(2,1)S(1)}, bf16[24,2304]{1,0:T(8,128)(2,1)S(1)}, u32[]{:S(2)}, u32[]{:S(2)}) %collective-permute-start.2) | collective-permute-done | bytes 110624 | tf_op jit(solution)/shard_map/ppermute | solution.py:356
  10.7 0.7 %outward_send.1.refs_4_ = bf16[2,2,24,1024]{3,2,1,0:T(8,128)(2,1)S(1)} custom-call(bf16[24,2304]{1,0:T(8,128)(2,1)S(1)} %gates.1.refs_0_.refs_3_.refs_6_, bf16[24,2304]{1,0:T(8,128)(2,1)S(1)} %collective-permute-done.2.refs_1_.refs_4_.refs_7_, bf16[48,768]{1,0:T(8,128)(2,1)S(1)} %get-tuple-element.32.refs_2_, bf16[768,4096]{1,0:T(8,128)(2,1)S(1)} %bitcast.13), custom_call_target="tpu_custom_call" | custom-call | bytes 3145728 | tf_op jit(solution)/shard_map/outward_send/pallas_call | solution.py:331
  11.4 0.5 %collective-permute-start.4 = (bf16[2,2,24,1024]{3,2,1,0:T(8,128)(2,1)S(1)}, bf16[2,2,24,1024]{3,2,1,0:T(8,128)(2,1)S(1)}, u32[]{:S(2)}, u32[]{:S(2)}) collective-permute-start(bf16[2,2,24,1024]{3,2,1,0:T(8,128)(2,1)S(1)} %outward_send.1.refs_4_), channel_id=1, source_target_pairs={{0,1},{1,0},{2,3},{3,2},{4,5},{5,4},{6,7},{7,6},{8,9},{9,8},{10,11... | collective-permute-start | bytes 589832 | tf_op jit(solution)/shard_map/ppermute | solution.py:359
  11.9 0.1 collective-permute-start.3
  12.0 0.7 %outward_keep.1.refs_8_ = bf16[2,2,24,1024]{3,2,1,0:T(8,128)(2,1)S(1)} custom-call(bf16[24,2304]{1,0:T(8,128)(2,1)S(1)} %gates.1.refs_0_.refs_3_.refs_6_, bf16[24,2304]{1,0:T(8,128)(2,1)S(1)} %collective-permute-done.2.refs_1_.refs_4_.refs_7_, bf16[48,768]{1,0:T(8,128)(2,1)S(1)} %get-tuple-element.32.refs_2_, bf16[768,4096]{1,0:T(8,128)(2,1)S(1)} %bitcast.14, ...), custom_call_target="tpu_custom_call" | custom-call | bytes 3145728 | tf_op jit(solution)/shard_map/outward_keep/pallas_call | solution.py:331
  12.7 0.6 %collective-permute-done.3.refs_2_.refs_5_ = bf16[24,2304]{1,0:T(8,128)(2,1)S(1)} collective-permute-done((bf16[24,2304]{1,0:T(8,128)(2,1)S(1)}, bf16[24,2304]{1,0:T(8,128)(2,1)S(1)}, u32[]{:S(2)}, u32[]{:S(2)}) %collective-permute-start.3) | collective-permute-done | bytes 110624 | tf_op jit(solution)/shard_map/ppermute | solution.py:359
  13.3 0.9 %backward_first.1 = (bf16[48,256]{1,0:T(8,128)(2,1)S(1)}, bf16[48,256]{1,0:T(8,128)(2,1)S(1)}, bf16[48,4096]{1,0:T(8,128)(2,1)S(1)}, bf16[2,2,24,1024]{3,2,1,0:T(8,128)(2,1)S(1)}) custom-call(bf16[24,4096]{1,0:T(8,128)(2,1)S(1)} %copy-done.1, bf16[24,2304]{1,0:T(8,128)(2,1)S(1)} %collective-permute-done.2.refs_1_.refs_4_.refs_7_, ...), custom_call_target="tpu_custom_call" | custom-call | bytes 2097152 | tf_op jit(solution)/shard_map/backward_first/pallas_call | solution.py:331
  14.2 0.1 add_convert_fusion
  14.2 2.3 %collective-permute-start.5 = (bf16[2,24,1024]{2,1,0:T(8,128)(2,1)S(1)}, bf16[2,24,1024]{2,1,0:T(8,128)(2,1)S(1)}, u32[]{:S(2)}, u32[]{:S(2)}) collective-permute-start(bf16[2,24,1024]{2,1,0:T(8,128)(2,1)S(1)} %get-tuple-element.50), channel_id=1, source_target_pairs={{0,17},{1,16},{16,1},{17,0},{2,19},{3,18},{18,3},{19,2},{4,21},{5,... | collective-permute-start | bytes 294920 | tf_op jit(solution)/shard_map/ppermute | solution.py:356
  16.6 1.4 %backward_rest.1 = (bf16[48,512]{1,0:T(8,128)(2,1)S(1)}, bf16[48,512]{1,0:T(8,128)(2,1)S(1)}, bf16[2,24,1024]{2,1,0:T(8,128)(2,1)S(1)}) custom-call(bf16[48,4096]{1,0:T(8,128)(2,1)S(1)} %get-tuple-element.35.weighted, f32[48,768]{1,0:T(8,128)S(1)} %get-tuple-element.30.refs_5_.pre_gate, f32[48,768]{1,0:T(8,128)S(1)} %get-tuple-element.31.refs_6_.pre_up, ...), custom_call_target="tpu_custom_call" | custom-call | bytes 4194304 | tf_op jit(solution)/shard_map/backward_rest/pallas_call | solution.py:331
  18.0 2.0 %inward_send.1 = (bf16[2,2,24,1024]{3,2,1,0:T(8,128)(2,1)S(1)}, bf16[2,24,1024]{2,1,0:T(8,128)(2,1)S(1)}) custom-call(bf16[48,256]{1,0:T(8,128)(2,1)S(1)} %get-tuple-element.33.refs_0_, bf16[48,256]{1,0:T(8,128)(2,1)S(1)} %get-tuple-element.34.refs_1_, bf16[48,512]{1,0:T(8,128)(2,1)S(1)} %get-tuple-element.37.refs_2_, ...), custom_call_target="tpu_custom_call" | custom-call | bytes 6291456 | tf_op jit(solution)/shard_map/inward_send/pallas_call | solution.py:331
  20.0 0.3 collective-permute-start.6
  20.3 2.0 %inward_keep.1 = (bf16[2,2,24,1024]{3,2,1,0:T(8,128)(2,1)S(1)}, bf16[2,24,1024]{2,1,0:T(8,128)(2,1)S(1)}) custom-call(bf16[48,256]{1,0:T(8,128)(2,1)S(1)} %get-tuple-element.33.refs_0_, bf16[48,256]{1,0:T(8,128)(2,1)S(1)} %get-tuple-element.34.refs_1_, bf16[48,512]{1,0:T(8,128)(2,1)S(1)} %get-tuple-element.37.refs_2_, ...), custom_call_target="tpu_custom_call" | custom-call | bytes 6291456 | tf_op jit(solution)/shard_map/inward_keep/pallas_call | solution.py:331
  22.4 1.2 %collective-permute-start.20 = (bf16[2,24,1024]{2,1,0:T(8,128)(2,1)S(1)}, bf16[2,24,1024]{2,1,0:T(8,128)(2,1)S(1)}, u32[]{:S(2)}, u32[]{:S(2)}) collective-permute-start(bf16[2,24,1024]{2,1,0:T(8,128)(2,1)S(1)} %get-tuple-element.48), channel_id=1, source_target_pairs={{0,5},{1,4},{4,1},{5,0},{8,13},{9,12},{12,9},{13,8},{2,7},{3,6},{6... | collective-permute-start | bytes 294920 | tf_op jit(solution)/shard_map/ppermute | solution.py:356
  23.6 2.0 %collective-permute-start.7 = (bf16[24,1024]{1,0:T(8,128)(2,1)S(1)}, bf16[24,1024]{1,0:T(8,128)(2,1)S(1)}, u32[]{:S(2)}, u32[]{:S(2)}) collective-permute-start(bf16[24,1024]{1,0:T(8,128)(2,1)S(1)} %get-tuple-element.45), channel_id=1, source_target_pairs={{0,18},{1,19},{2,16},{3,17},{16,2},{17,3},{18,0},{19,1},{4,22},{5,... | collective-permute-start | bytes 147464 | tf_op jit(solution)/shard_map/ppermute | solution.py:356
  25.6 0.5 %collective-permute-start.8 = (bf16[24,1024]{1,0:T(8,128)(2,1)S(1)}, bf16[24,1024]{1,0:T(8,128)(2,1)S(1)}, u32[]{:S(2)}, u32[]{:S(2)}) collective-permute-start(bf16[24,1024]{1,0:T(8,128)(2,1)S(1)} %get-tuple-element.46), channel_id=1, source_target_pairs={{0,17},{1,16},{2,19},{3,18},{16,1},{17,0},{18,3},{19,2},{4,21},{5,... | collective-permute-start | bytes 147464 | tf_op jit(solution)/shard_map/ppermute | solution.py:356
  26.1 0.7 %collective-permute-start.9 = (bf16[24,1024]{1,0:T(8,128)(2,1)S(1)}, bf16[24,1024]{1,0:T(8,128)(2,1)S(1)}, u32[]{:S(2)}, u32[]{:S(2)}) collective-permute-start(bf16[24,1024]{1,0:T(8,128)(2,1)S(1)} %get-tuple-element.47), channel_id=1, source_target_pairs={{0,3},{1,2},{2,1},{3,0},{16,19},{17,18},{18,17},{19,16},{4,7},{5,6... | collective-permute-start | bytes 147464 | tf_op jit(solution)/shard_map/ppermute | solution.py:356
  26.8 0.4 collective-permute-done.20
  27.2 1.1 %collective-permute-start.21 = (bf16[2,24,1024]{2,1,0:T(8,128)(2,1)S(1)}, bf16[2,24,1024]{2,1,0:T(8,128)(2,1)S(1)}, u32[]{:S(2)}, u32[]{:S(2)}) collective-permute-start(bf16[2,24,1024]{2,1,0:T(8,128)(2,1)S(1)} %add_convert_fusion.3), channel_id=1, source_target_pairs={{0,3},{1,2},{2,1},{3,0},{4,7},{5,6},{6,5},{7,4},{8,11},{9,10},{10,... | collective-permute-start | bytes 294920 | tf_op jit(solution)/shard_map/ppermute | solution.py:356
  28.2 0.4 collective-permute-done.7
  28.7 0.8 %collective-permute-done.8 = bf16[24,1024]{1,0:T(8,128)(2,1)S(1)} collective-permute-done((bf16[24,1024]{1,0:T(8,128)(2,1)S(1)}, bf16[24,1024]{1,0:T(8,128)(2,1)S(1)}, u32[]{:S(2)}, u32[]{:S(2)}) %collective-permute-start.8) | collective-permute-done | bytes 49184 | tf_op jit(solution)/shard_map/ppermute | solution.py:356
  29.5 0.1 collective-permute-done.9
  29.6 2.6 %collective-permute-start.12 = (bf16[24,1024]{1,0:T(8,128)(2,1)S(1)}, bf16[24,1024]{1,0:T(8,128)(2,1)S(1)}, u32[]{:S(2)}, u32[]{:S(2)}) collective-permute-start(bf16[24,1024]{1,0:T(8,128)(2,1)S(1)} %add_convert_fusion.6), channel_id=1, source_target_pairs={{0,12},{1,13},{4,8},{5,9},{8,4},{9,5},{12,0},{13,1},{2,14},{3,15},... | collective-permute-start | bytes 147464 | tf_op jit(solution)/shard_map/ppermute | solution.py:356
  32.2 1.0 %collective-permute-start.11 = (bf16[24,1024]{1,0:T(8,128)(2,1)S(1)}, bf16[24,1024]{1,0:T(8,128)(2,1)S(1)}, u32[]{:S(2)}, u32[]{:S(2)}) collective-permute-start(bf16[24,1024]{1,0:T(8,128)(2,1)S(1)} %add_convert_fusion.6), channel_id=1, source_target_pairs={{0,9},{1,8},{4,13},{5,12},{8,1},{9,0},{12,5},{13,4},{2,11},{3,10},... | collective-permute-start | bytes 147464 | tf_op jit(solution)/shard_map/ppermute | solution.py:356
  33.3 0.5 %collective-permute-start.10 = (bf16[24,1024]{1,0:T(8,128)(2,1)S(1)}, bf16[24,1024]{1,0:T(8,128)(2,1)S(1)}, u32[]{:S(2)}, u32[]{:S(2)}) collective-permute-start(bf16[24,1024]{1,0:T(8,128)(2,1)S(1)} %add_convert_fusion.6), channel_id=1, source_target_pairs={{0,5},{1,4},{4,1},{5,0},{8,13},{9,12},{12,9},{13,8},{2,7},{3,6},{6... | collective-permute-start | bytes 147464 | tf_op jit(solution)/shard_map/ppermute | solution.py:356
  33.9 2.4 %collective-permute-start.22 = (bf16[2,24,1024]{2,1,0:T(8,128)(2,1)S(1)}, bf16[2,24,1024]{2,1,0:T(8,128)(2,1)S(1)}, u32[]{:S(2)}, u32[]{:S(2)}) collective-permute-start(bf16[2,24,1024]{2,1,0:T(8,128)(2,1)S(1)} %add_convert_fusion.2), channel_id=1, source_target_pairs={{0,9},{1,8},{4,13},{5,12},{8,1},{9,0},{12,5},{13,4},{2,11},{3,10},... | collective-permute-start | bytes 294920 | tf_op jit(solution)/shard_map/ppermute | solution.py:356
  36.2 1.5 %collective-permute-done.11 = bf16[24,1024]{1,0:T(8,128)(2,1)S(1)} collective-permute-done((bf16[24,1024]{1,0:T(8,128)(2,1)S(1)}, bf16[24,1024]{1,0:T(8,128)(2,1)S(1)}, u32[]{:S(2)}, u32[]{:S(2)}) %collective-permute-start.11) | collective-permute-done | bytes 49184 | tf_op jit(solution)/shard_map/ppermute | solution.py:356
  37.7 0.7 %collective-permute-done.10 = bf16[24,1024]{1,0:T(8,128)(2,1)S(1)} collective-permute-done((bf16[24,1024]{1,0:T(8,128)(2,1)S(1)}, bf16[24,1024]{1,0:T(8,128)(2,1)S(1)}, u32[]{:S(2)}, u32[]{:S(2)}) %collective-permute-start.10) | collective-permute-done | bytes 49184 | tf_op jit(solution)/shard_map/ppermute | solution.py:356
  38.4 2.0 %collective-permute-start.15 = (bf16[24,1024]{1,0:T(8,128)(2,1)S(1)}, bf16[24,1024]{1,0:T(8,128)(2,1)S(1)}, u32[]{:S(2)}, u32[]{:S(2)}) collective-permute-start(bf16[24,1024]{1,0:T(8,128)(2,1)S(1)} %add_convert_fusion.5.refs_8_), channel_id=1, source_target_pairs={{0,18},{1,19},{2,16},{3,17},{16,2},{17,3},{18,0},{19,1},{4,22},{5,... | collective-permute-start | bytes 147464 | tf_op jit(solution)/shard_map/ppermute | solution.py:356
  40.5 0.5 collective-permute-start.14
  40.9 0.8 %collective-permute-start.13 = (bf16[24,1024]{1,0:T(8,128)(2,1)S(1)}, bf16[24,1024]{1,0:T(8,128)(2,1)S(1)}, u32[]{:S(2)}, u32[]{:S(2)}) collective-permute-start(bf16[24,1024]{1,0:T(8,128)(2,1)S(1)} %add_convert_fusion.5.refs_8_), channel_id=1, source_target_pairs={{0,3},{1,2},{2,1},{3,0},{16,19},{17,18},{18,17},{19,16},{4,7},{5,6... | collective-permute-start | bytes 147464 | tf_op jit(solution)/shard_map/ppermute | solution.py:356
  41.7 0.4 collective-permute-done.22
  42.1 0.3 collective-permute-start.23
  42.4 0.3 collective-permute-start.16
  42.7 1.1 %collective-permute-done.15.refs_11_ = bf16[24,1024]{1,0:T(8,128)(2,1)S(1)} collective-permute-done((bf16[24,1024]{1,0:T(8,128)(2,1)S(1)}, bf16[24,1024]{1,0:T(8,128)(2,1)S(1)}, u32[]{:S(2)}, u32[]{:S(2)}) %collective-permute-start.15) | collective-permute-done | bytes 49184 | tf_op jit(solution)/shard_map/ppermute | solution.py:356
  43.7 0.7 %collective-permute-done.14.refs_10_ = bf16[24,1024]{1,0:T(8,128)(2,1)S(1)} collective-permute-done((bf16[24,1024]{1,0:T(8,128)(2,1)S(1)}, bf16[24,1024]{1,0:T(8,128)(2,1)S(1)}, u32[]{:S(2)}, u32[]{:S(2)}) %collective-permute-start.14) | collective-permute-done | bytes 49184 | tf_op jit(solution)/shard_map/ppermute | solution.py:356
  44.4 0.1 collective-permute-start.18
  44.6 0.5 %collective-permute-start.17 = (bf16[24,1024]{1,0:T(8,128)(2,1)S(1)}, bf16[24,1024]{1,0:T(8,128)(2,1)S(1)}, u32[]{:S(2)}, u32[]{:S(2)}) collective-permute-start(bf16[24,1024]{1,0:T(8,128)(2,1)S(1)} %collective-permute-done.13.refs_9_), channel_id=1, source_target_pairs={{0,1},{1,0},{2,3},{3,2},{4,5},{5,4},{6,7},{7,6},{8,9},{9,8},{10,11... | collective-permute-start | bytes 147464 | tf_op jit(solution)/shard_map/ppermute | solution.py:359
  45.1 0.6 %collective-permute-done.18.refs_14_ = bf16[24,1024]{1,0:T(8,128)(2,1)S(1)} collective-permute-done((bf16[24,1024]{1,0:T(8,128)(2,1)S(1)}, bf16[24,1024]{1,0:T(8,128)(2,1)S(1)}, u32[]{:S(2)}, u32[]{:S(2)}) %collective-permute-start.18) | collective-permute-done | bytes 49184 | tf_op jit(solution)/shard_map/ppermute | solution.py:359
  45.6 0.3 collective-permute-done.17.refs_13_
  45.9 1.7 %finish.1 = (bf16[24,4096]{1,0:T(8,128)(2,1)}, bf16[24,4096]{1,0:T(8,128)(2,1)}, bf16[24,128]{1,0:T(8,128)(2,1)}, bf16[128,2048]{1,0:T(8,128)(2,1)}) custom-call(bf16[24,4096]{1,0:T(8,128)(2,1)S(1)} %copy-done, bf16[24,2048]{1,0:T(8,128)(2,1)S(1)} %collective-permute-done.refs_0_.refs_1_, bf16[24,2048]{1,0:T(8,128)(2,1)S(1)} %collective-permute-done.1.refs_0_.refs_2_, ...), custom_call_target="tpu_custom_call" | custom-call | bytes 6291456 | tf_op jit(solution)/shard_map/finish/pallas_call | solution.py:331
  (43 shorter events, 0.3 us)
Async XLA Ops:
  0.6 6.9 %slice-start.2 = ((s8[6291456]{0:T(1024)(128)(4,1)}), s8[4194304]{0:T(1024)(128)(4,1)S(1)}, s32[]{:S(2)}) async-start(s8[6291456]{0:T(1024)(128)(4,1)} %bitcast.18), calls=%async_computation.2 | async-start | bytes 8388608
  0.6 6.9 %slice-start.4 = ((s8[6291456]{0:T(1024)(128)(4,1)}), s8[4194304]{0:T(1024)(128)(4,1)S(1)}, s32[]{:S(2)}) async-start(s8[6291456]{0:T(1024)(128)(4,1)} %bitcast.25), calls=%async_computation.4 | async-start | bytes 8388608
  1.7 5.8 %collective-permute-start = (bf16[24,2048]{1,0:T(8,128)(2,1)S(1)}, bf16[24,2048]{1,0:T(8,128)(2,1)S(1)}, u32[]{:S(2)}, u32[]{:S(2)}) collective-permute-start(bf16[24,2048]{1,0:T(8,128)(2,1)S(1)} %cut.1), channel_id=1, source_target_pairs={{0,16},{1,17},{16,0},{17,1},{2,18},{3,19},{18,2},{19,3},{4,20},{5,... | collective-permute-start | bytes 294920 | tf_op jit(solution)/shard_map/ppermute | solution.py:356
  4.7 2.8 %slice-start.3 = ((s8[6291456]{0:T(1024)(128)(4,1)}), s8[2097152]{0:T(1024)(128)(4,1)S(1)}, s32[]{:S(2)}) async-start(s8[6291456]{0:T(1024)(128)(4,1)} %bitcast.18), calls=%async_computation.3 | async-start | bytes 4194304
  4.7 2.8 %slice-start.5 = ((s8[6291456]{0:T(1024)(128)(4,1)}), s8[2097152]{0:T(1024)(128)(4,1)S(1)}, s32[]{:S(2)}) async-start(s8[6291456]{0:T(1024)(128)(4,1)} %bitcast.25), calls=%async_computation.5 | async-start | bytes 4194304
  4.7 2.8 %copy-start = (bf16[24,4096]{1,0:T(8,128)(2,1)S(1)}, bf16[24,4096]{1,0:T(8,128)(2,1)}, u32[]{:S(2)}) copy-start(bf16[24,4096]{1,0:T(8,128)(2,1)} %refs_0_.3) | copy-start | bytes 589828
  4.7 2.8 %copy-start.3 = (f32[4096]{0:T(1024)S(1)}, f32[4096]{0:T(1024)}, u32[]{:S(2)}) copy-start(f32[4096]{0:T(1024)} %param.11) | copy-start | bytes 49156
  5.9 4.8 %collective-permute-start.2 = (bf16[24,2304]{1,0:T(8,128)(2,1)S(1)}, bf16[24,2304]{1,0:T(8,128)(2,1)S(1)}, u32[]{:S(2)}, u32[]{:S(2)}) collective-permute-start(bf16[24,2304]{1,0:T(8,128)(2,1)S(1)} %gates.1.refs_0_.refs_3_.refs_6_), channel_id=1, source_target_pairs={{0,16},{1,17},{16,0},{17,1},{2,18},{3,19},{18,2},{19,3},{4,20},{5,... | collective-permute-start | bytes 331784 | tf_op jit(solution)/shard_map/ppermute | solution.py:356
  7.5 1.3 %collective-permute-start.1 = (bf16[24,2048]{1,0:T(8,128)(2,1)S(1)}, bf16[24,2048]{1,0:T(8,128)(2,1)S(1)}, u32[]{:S(2)}, u32[]{:S(2)}) collective-permute-start(bf16[24,2048]{1,0:T(8,128)(2,1)S(1)} %collective-permute-done.refs_0_.refs_1_), channel_id=1, source_target_pairs={{0,1},{1,0},{2,3},{3,2},{4,5},{5,4},{6,7},{7,6},{8,9},{9,8},{10,11... | collective-permute-start | bytes 294920 | tf_op jit(solution)/shard_map/ppermute | solution.py:359
  7.6 3.1 %slice-start = ((s8[6291456]{0:T(1024)(128)(4,1)}), s8[4194304]{0:T(1024)(128)(4,1)S(1)}, s32[]{:S(2)}) async-start(s8[6291456]{0:T(1024)(128)(4,1)} %bitcast.11), calls=%async_computation | async-start | bytes 8388608
  8.8 1.9 %slice-start.1 = ((s8[6291456]{0:T(1024)(128)(4,1)}), s8[2097152]{0:T(1024)(128)(4,1)S(1)}, s32[]{:S(2)}) async-start(s8[6291456]{0:T(1024)(128)(4,1)} %bitcast.11), calls=%async_computation.1 | async-start | bytes 4194304
  10.7 2.6 %copy-start.1 = (bf16[24,4096]{1,0:T(8,128)(2,1)S(1)}, bf16[24,4096]{1,0:T(8,128)(2,1)}, u32[]{:S(2)}) copy-start(bf16[24,4096]{1,0:T(8,128)(2,1)} %refs_3_.1) | copy-start | bytes 589828
  11.4 2.7 %collective-permute-start.4 = (bf16[2,2,24,1024]{3,2,1,0:T(8,128)(2,1)S(1)}, bf16[2,2,24,1024]{3,2,1,0:T(8,128)(2,1)S(1)}, u32[]{:S(2)}, u32[]{:S(2)}) collective-permute-start(bf16[2,2,24,1024]{3,2,1,0:T(8,128)(2,1)S(1)} %outward_send.1.refs_4_), channel_id=1, source_target_pairs={{0,1},{1,0},{2,3},{3,2},{4,5},{5,4},{6,7},{7,6},{8,9},{9,8},{10,11... | collective-permute-start | bytes 589832 | tf_op jit(solution)/shard_map/ppermute | solution.py:359
  11.9 1.3 %collective-permute-start.3 = (bf16[24,2304]{1,0:T(8,128)(2,1)S(1)}, bf16[24,2304]{1,0:T(8,128)(2,1)S(1)}, u32[]{:S(2)}, u32[]{:S(2)}) collective-permute-start(bf16[24,2304]{1,0:T(8,128)(2,1)S(1)} %collective-permute-done.2.refs_1_.refs_4_.refs_7_), channel_id=1, source_target_pairs={{0,1},{1,0},{2,3},{3,2},{4,5},{5,4},{6,7},{7,6},{8,9},{9,8},{10,11... | collective-permute-start | bytes 331784 | tf_op jit(solution)/shard_map/ppermute | solution.py:359
  14.2 6.0 %collective-permute-start.5 = (bf16[2,24,1024]{2,1,0:T(8,128)(2,1)S(1)}, bf16[2,24,1024]{2,1,0:T(8,128)(2,1)S(1)}, u32[]{:S(2)}, u32[]{:S(2)}) collective-permute-start(bf16[2,24,1024]{2,1,0:T(8,128)(2,1)S(1)} %get-tuple-element.50), channel_id=1, source_target_pairs={{0,17},{1,16},{16,1},{17,0},{2,19},{3,18},{18,3},{19,2},{4,21},{5,... | collective-permute-start | bytes 294920 | tf_op jit(solution)/shard_map/ppermute | solution.py:356
  20.0 2.3 %collective-permute-start.6 = (bf16[2,2,24,1024]{3,2,1,0:T(8,128)(2,1)S(1)}, bf16[2,2,24,1024]{3,2,1,0:T(8,128)(2,1)S(1)}, u32[]{:S(2)}, u32[]{:S(2)}) collective-permute-start(bf16[2,2,24,1024]{3,2,1,0:T(8,128)(2,1)S(1)} %get-tuple-element.42), channel_id=1, source_target_pairs={{0,1},{1,0},{2,3},{3,2},{4,5},{5,4},{6,7},{7,6},{8,9},{9,8},{10,11... | collective-permute-start | bytes 589832 | tf_op jit(solution)/shard_map/ppermute | solution.py:359
  20.3 25.6 %copy-start.2 = (bf16[128,4096]{1,0:T(8,128)(2,1)S(1)}, bf16[128,4096]{1,0:T(8,128)(2,1)}, u32[]{:S(2)}) copy-start(bf16[128,4096]{1,0:T(8,128)(2,1)} %refs_20_.1) | copy-start | bytes 3145732
  22.4 4.8 %collective-permute-start.20 = (bf16[2,24,1024]{2,1,0:T(8,128)(2,1)S(1)}, bf16[2,24,1024]{2,1,0:T(8,128)(2,1)S(1)}, u32[]{:S(2)}, u32[]{:S(2)}) collective-permute-start(bf16[2,24,1024]{2,1,0:T(8,128)(2,1)S(1)} %get-tuple-element.48), channel_id=1, source_target_pairs={{0,5},{1,4},{4,1},{5,0},{8,13},{9,12},{12,9},{13,8},{2,7},{3,6},{6... | collective-permute-start | bytes 294920 | tf_op jit(solution)/shard_map/ppermute | solution.py:356
  23.6 5.1 %collective-permute-start.7 = (bf16[24,1024]{1,0:T(8,128)(2,1)S(1)}, bf16[24,1024]{1,0:T(8,128)(2,1)S(1)}, u32[]{:S(2)}, u32[]{:S(2)}) collective-permute-start(bf16[24,1024]{1,0:T(8,128)(2,1)S(1)} %get-tuple-element.45), channel_id=1, source_target_pairs={{0,18},{1,19},{2,16},{3,17},{16,2},{17,3},{18,0},{19,1},{4,22},{5,... | collective-permute-start | bytes 147464 | tf_op jit(solution)/shard_map/ppermute | solution.py:356
  25.6 3.9 %collective-permute-start.8 = (bf16[24,1024]{1,0:T(8,128)(2,1)S(1)}, bf16[24,1024]{1,0:T(8,128)(2,1)S(1)}, u32[]{:S(2)}, u32[]{:S(2)}) collective-permute-start(bf16[24,1024]{1,0:T(8,128)(2,1)S(1)} %get-tuple-element.46), channel_id=1, source_target_pairs={{0,17},{1,16},{2,19},{3,18},{16,1},{17,0},{18,3},{19,2},{4,21},{5,... | collective-permute-start | bytes 147464 | tf_op jit(solution)/shard_map/ppermute | solution.py:356
  26.1 3.5 %collective-permute-start.9 = (bf16[24,1024]{1,0:T(8,128)(2,1)S(1)}, bf16[24,1024]{1,0:T(8,128)(2,1)S(1)}, u32[]{:S(2)}, u32[]{:S(2)}) collective-permute-start(bf16[24,1024]{1,0:T(8,128)(2,1)S(1)} %get-tuple-element.47), channel_id=1, source_target_pairs={{0,3},{1,2},{2,1},{3,0},{16,19},{17,18},{18,17},{19,16},{4,7},{5,6... | collective-permute-start | bytes 147464 | tf_op jit(solution)/shard_map/ppermute | solution.py:356
  27.2 6.6 %collective-permute-start.21 = (bf16[2,24,1024]{2,1,0:T(8,128)(2,1)S(1)}, bf16[2,24,1024]{2,1,0:T(8,128)(2,1)S(1)}, u32[]{:S(2)}, u32[]{:S(2)}) collective-permute-start(bf16[2,24,1024]{2,1,0:T(8,128)(2,1)S(1)} %add_convert_fusion.3), channel_id=1, source_target_pairs={{0,3},{1,2},{2,1},{3,0},{4,7},{5,6},{6,5},{7,4},{8,11},{9,10},{10,... | collective-permute-start | bytes 294920 | tf_op jit(solution)/shard_map/ppermute | solution.py:356
  29.6 6.6 %collective-permute-start.12 = (bf16[24,1024]{1,0:T(8,128)(2,1)S(1)}, bf16[24,1024]{1,0:T(8,128)(2,1)S(1)}, u32[]{:S(2)}, u32[]{:S(2)}) collective-permute-start(bf16[24,1024]{1,0:T(8,128)(2,1)S(1)} %add_convert_fusion.6), channel_id=1, source_target_pairs={{0,12},{1,13},{4,8},{5,9},{8,4},{9,5},{12,0},{13,1},{2,14},{3,15},... | collective-permute-start | bytes 147464 | tf_op jit(solution)/shard_map/ppermute | solution.py:356
  32.2 5.5 %collective-permute-start.11 = (bf16[24,1024]{1,0:T(8,128)(2,1)S(1)}, bf16[24,1024]{1,0:T(8,128)(2,1)S(1)}, u32[]{:S(2)}, u32[]{:S(2)}) collective-permute-start(bf16[24,1024]{1,0:T(8,128)(2,1)S(1)} %add_convert_fusion.6), channel_id=1, source_target_pairs={{0,9},{1,8},{4,13},{5,12},{8,1},{9,0},{12,5},{13,4},{2,11},{3,10},... | collective-permute-start | bytes 147464 | tf_op jit(solution)/shard_map/ppermute | solution.py:356
  33.3 5.1 %collective-permute-start.10 = (bf16[24,1024]{1,0:T(8,128)(2,1)S(1)}, bf16[24,1024]{1,0:T(8,128)(2,1)S(1)}, u32[]{:S(2)}, u32[]{:S(2)}) collective-permute-start(bf16[24,1024]{1,0:T(8,128)(2,1)S(1)} %add_convert_fusion.6), channel_id=1, source_target_pairs={{0,5},{1,4},{4,1},{5,0},{8,13},{9,12},{12,9},{13,8},{2,7},{3,6},{6... | collective-permute-start | bytes 147464 | tf_op jit(solution)/shard_map/ppermute | solution.py:356
  33.9 8.2 %collective-permute-start.22 = (bf16[2,24,1024]{2,1,0:T(8,128)(2,1)S(1)}, bf16[2,24,1024]{2,1,0:T(8,128)(2,1)S(1)}, u32[]{:S(2)}, u32[]{:S(2)}) collective-permute-start(bf16[2,24,1024]{2,1,0:T(8,128)(2,1)S(1)} %add_convert_fusion.2), channel_id=1, source_target_pairs={{0,9},{1,8},{4,13},{5,12},{8,1},{9,0},{12,5},{13,4},{2,11},{3,10},... | collective-permute-start | bytes 294920 | tf_op jit(solution)/shard_map/ppermute | solution.py:356
  38.4 5.3 %collective-permute-start.15 = (bf16[24,1024]{1,0:T(8,128)(2,1)S(1)}, bf16[24,1024]{1,0:T(8,128)(2,1)S(1)}, u32[]{:S(2)}, u32[]{:S(2)}) collective-permute-start(bf16[24,1024]{1,0:T(8,128)(2,1)S(1)} %add_convert_fusion.5.refs_8_), channel_id=1, source_target_pairs={{0,18},{1,19},{2,16},{3,17},{16,2},{17,3},{18,0},{19,1},{4,22},{5,... | collective-permute-start | bytes 147464 | tf_op jit(solution)/shard_map/ppermute | solution.py:356
  40.5 4.0 %collective-permute-start.14 = (bf16[24,1024]{1,0:T(8,128)(2,1)S(1)}, bf16[24,1024]{1,0:T(8,128)(2,1)S(1)}, u32[]{:S(2)}, u32[]{:S(2)}) collective-permute-start(bf16[24,1024]{1,0:T(8,128)(2,1)S(1)} %add_convert_fusion.5.refs_8_), channel_id=1, source_target_pairs={{0,17},{1,16},{2,19},{3,18},{16,1},{17,0},{18,3},{19,2},{4,21},{5,... | collective-permute-start | bytes 147464 | tf_op jit(solution)/shard_map/ppermute | solution.py:356
  40.9 3.6 %collective-permute-start.13 = (bf16[24,1024]{1,0:T(8,128)(2,1)S(1)}, bf16[24,1024]{1,0:T(8,128)(2,1)S(1)}, u32[]{:S(2)}, u32[]{:S(2)}) collective-permute-start(bf16[24,1024]{1,0:T(8,128)(2,1)S(1)} %add_convert_fusion.5.refs_8_), channel_id=1, source_target_pairs={{0,3},{1,2},{2,1},{3,0},{16,19},{17,18},{18,17},{19,16},{4,7},{5,6... | collective-permute-start | bytes 147464 | tf_op jit(solution)/shard_map/ppermute | solution.py:356
  42.1 3.8 %collective-permute-start.23 = (bf16[2,24,1024]{2,1,0:T(8,128)(2,1)S(1)}, bf16[2,24,1024]{2,1,0:T(8,128)(2,1)S(1)}, u32[]{:S(2)}, u32[]{:S(2)}) collective-permute-start(bf16[2,24,1024]{2,1,0:T(8,128)(2,1)S(1)} %add_convert_fusion.1.refs_16_), channel_id=1, source_target_pairs={{0,1},{1,0},{2,3},{3,2},{4,5},{5,4},{6,7},{7,6},{8,9},{9,8},{10,11... | collective-permute-start | bytes 294920 | tf_op jit(solution)/shard_map/ppermute | solution.py:359
  42.4 2.7 %collective-permute-start.16 = (bf16[24,1024]{1,0:T(8,128)(2,1)S(1)}, bf16[24,1024]{1,0:T(8,128)(2,1)S(1)}, u32[]{:S(2)}, u32[]{:S(2)}) collective-permute-start(bf16[24,1024]{1,0:T(8,128)(2,1)S(1)} %add_convert_fusion.5.refs_8_), channel_id=1, source_target_pairs={{0,1},{1,0},{2,3},{3,2},{4,5},{5,4},{6,7},{7,6},{8,9},{9,8},{10,11... | collective-permute-start | bytes 147464 | tf_op jit(solution)/shard_map/ppermute | solution.py:359
  43.7 1.3 %collective-permute-start.19 = (bf16[24,1024]{1,0:T(8,128)(2,1)S(1)}, bf16[24,1024]{1,0:T(8,128)(2,1)S(1)}, u32[]{:S(2)}, u32[]{:S(2)}) collective-permute-start(bf16[24,1024]{1,0:T(8,128)(2,1)S(1)} %collective-permute-done.15.refs_11_), channel_id=1, source_target_pairs={{0,1},{1,0},{2,3},{3,2},{4,5},{5,4},{6,7},{7,6},{8,9},{9,8},{10,11... | collective-permute-start | bytes 147464 | tf_op jit(solution)/shard_map/ppermute | solution.py:359
  44.4 1.2 %collective-permute-start.18 = (bf16[24,1024]{1,0:T(8,128)(2,1)S(1)}, bf16[24,1024]{1,0:T(8,128)(2,1)S(1)}, u32[]{:S(2)}, u32[]{:S(2)}) collective-permute-start(bf16[24,1024]{1,0:T(8,128)(2,1)S(1)} %collective-permute-done.14.refs_10_), channel_id=1, source_target_pairs={{0,1},{1,0},{2,3},{3,2},{4,5},{5,4},{6,7},{7,6},{8,9},{9,8},{10,11... | collective-permute-start | bytes 147464 | tf_op jit(solution)/shard_map/ppermute | solution.py:359
  44.6 1.4 %collective-permute-start.17 = (bf16[24,1024]{1,0:T(8,128)(2,1)S(1)}, bf16[24,1024]{1,0:T(8,128)(2,1)S(1)}, u32[]{:S(2)}, u32[]{:S(2)}) collective-permute-start(bf16[24,1024]{1,0:T(8,128)(2,1)S(1)} %collective-permute-done.13.refs_9_), channel_id=1, source_target_pairs={{0,1},{1,0},{2,3},{3,2},{4,5},{5,4},{6,7},{7,6},{8,9},{9,8},{10,11... | collective-permute-start | bytes 147464 | tf_op jit(solution)/shard_map/ppermute | solution.py:359
